TPU v7x, 32 devices: a whole 2x2x4 slice. The times are simulated.
32 devices in a mesh: space: 8 (over y, x, core), vel: 4 (over z).
Axes of the slice: x: 2, y: 2, z: 4, core: 2. Of those that a mesh axis runs over, the one named last changes fastest.
Arguments:
- particle_profile: float32 [64, 262144], P('space', 'vel'), as said below
- neighbors: int32 [6, 64], P(None, 'space'), may hold values from -1 to 63, as said below
- face_vectors: float32 [3, 6, 64], P(None, None, 'space'), may hold values from -0.8 to 0.8, as said below
- volumes: float32 [64], P('space'), may hold values from 2 to 4
- wall_temp: float32 [64], P('space'), may hold values from 0.5 to 1.5
Outputs:
- evolved: float32 [64, 262144], P('space', 'vel')
- macro_quantities: float32 [8, 64], P(None, 'space')
Inputs may be any that keep to these rules, and one draw needn't show every extreme that they name: neighbors[k, g] is -1 or a cell other than g at most 3 cells away from g in cell order; face 0 of an even cell points 3 cells ahead and of an odd cell 3 cells behind, or is -1 where that leaves the mesh. `face_vectors`: every component has a magnitude between 0.3 and 0.8. `particle_profile`: positive.
All inputs are finite; a program needn't handle non-finite values.
Results may differ from a plain program's by a relative error of at most 0.00015.
Values sent between devices are 32-bit elements; how exact they have to be, the bound alone decides.
No kernel may reach another device: no remote copies, remote signals or barrier semaphores. Data moves between devices by JAX's collectives and lax.ppermute only.
A program may use at most 64 MiB of HBM per device.

v0:
```python
import math

import jax
import jax.numpy as jnp
from jax import lax
from jax.experimental import pallas as pl
from jax.experimental.pallas import tpu as pltpu
from jax.sharding import PartitionSpec as P

NV = 64
FACES = 6
REACH = 3
STEPS = 2
LANES = 128
SUB = 8

TIME_STEP = 0.015
SHEAR = 0.1
POWER = 0.81
SPEED_LIMIT = 6.0
H = 2.0 * SPEED_LIMIT / NV
WEIGHT = H**3 * (2.0 * math.pi) ** (-1.5)

CHUNKS = NV * NV // LANES
TILES = CHUNKS // SUB

FV, VOL, WT, WALL = 0, 18, 19, 20
GEO = 26
EMIT, ABSORB = 13, 19
SUMS = 25

F32 = jnp.float32
VMEM_LIMIT = 40 * 1024 * 1024


def lane_iota():
    return lax.broadcasted_iota(jnp.int32, (SUB, LANES), 1)


def sub_iota():
    return lax.broadcasted_iota(jnp.int32, (SUB, LANES), 0)


def half_of(lane):
    return (lane >= NV).astype(F32)


def third_component(lane):
    c = jnp.where(lane >= NV, lane - NV, lane).astype(F32)
    return -SPEED_LIMIT + (c + 0.5) * H


def tile_nodes(t):
    lane = lane_iota()
    b = (2 * SUB * t + 2 * sub_iota()).astype(F32) + half_of(lane)
    return -SPEED_LIMIT + (b + 0.5) * H, third_component(lane)


def plane_node(first_plane, a):
    return -SPEED_LIMIT + ((first_plane + a).astype(F32) + 0.5) * H


def column(tile, p):
    return jnp.broadcast_to(tile[:, p : p + 1], (SUB, LANES))


def splat(ref, i, g):
    return jnp.broadcast_to(ref[i, pl.ds(g, 1), :], (SUB, LANES))


def total(tile):
    return jnp.broadcast_to(jnp.sum(tile, axis=1, keepdims=True), (SUB, LANES))


def polynomial_sums(native_ref, planes, first_plane):
    half = CHUNKS // 2

    def plane(a, acc):
        xa = plane_node(first_plane, a)
        base = a * CHUNKS
        b0 = b1 = b2 = b3 = None
        for i in range(half):
            y = (2 * i + 1) * H
            hi = native_ref[pl.ds(pl.multiple_of((base + half + i) * SUB, SUB), SUB), :]
            lo = native_ref[pl.ds(pl.multiple_of((base + half - 1 - i) * SUB, SUB), SUB), :]
            s, d = hi + lo, hi - lo
            terms = (s, y * d, (y * y) * s, (y * y * y) * d)
            if i == 0:
                b0, b1, b2, b3 = terms
            else:
                b0, b1, b2, b3 = b0 + terms[0], b1 + terms[1], b2 + terms[2], b3 + terms[3]
        a0, a1, a2 = xa * b0, xa * b1, xa * b2
        aa0, aa1 = xa * a0, xa * a1
        new = (b0, b1, b2, b3, a0, a1, a2, aa0, aa1, xa * aa0)
        return tuple(x + y for x, y in zip(acc, new))

    zero = jnp.zeros((SUB, LANES), F32)
    g00, g01, g02, g03, g10, g11, g12, g20, g21, g30 = lax.fori_loop(0, planes, plane, (zero,) * 10)
    lane = lane_iota()
    e = (half_of(lane) - 0.5) * H
    c = third_component(lane)
    h00, h10, h20, h30 = g00, g10, g20, g30
    h01 = g01 + e * g00
    h11 = g11 + e * g10
    h21 = g21 + e * g20
    h02 = g02 + e * (2.0 * g01 + e * g00)
    h12 = g12 + e * (2.0 * g11 + e * g10)
    h03 = g03 + e * (3.0 * g02 + e * (3.0 * g01 + e * g00))
    return (
        h00,
        h10,
        h01,
        c * h00,
        h20,
        h02,
        c * c * h00,
        h11,
        c * h10,
        c * h01,
        h30 + h12 + c * c * h10,
        h21 + h03 + c * c * h01,
        c * (h20 + h02 + c * c * h00),
    )


def pack_sums(arrays, start):
    lane = lane_iota()
    out = jnp.zeros((SUB, LANES), F32)
    for p, x in enumerate(arrays):
        out = jnp.where(lane == start + p, total(x), out)
    return out


def face_sums(ref, k):
    out = ref[k, pl.ds(0, SUB, stride=SUB), :]
    for s in range(1, SUB):
        out = out + ref[k, pl.ds(s, SUB, stride=SUB), :]
    return out


def wall_tiles(wall_temp):
    rt = 1.0 / wall_temp
    scale = rt * jnp.sqrt(rt)
    out = []
    for t in range(TILES):
        xb, xc = tile_nodes(t)
        out.append(scale * jnp.exp(-0.5 * (xb * xb + xc * xc) * rt))
    return out


def emitted_sums(f_ref, first_row, planes, first_plane, nbr_ref, geo_ref, sums_ref, with_absorbed):
    sums_ref[...] = jnp.zeros_like(sums_ref)

    def cell(g, _):
        for k in range(FACES):

            @pl.when(nbr_ref[k, g] < 0)
            def _():
                v0, v1, v2 = [splat(geo_ref, FV + FACES * i + k, g) for i in range(3)]
                base = []
                for t in range(TILES):
                    xb, xc = tile_nodes(t)
                    base.append(v1 * xb + v2 * xc)
                if with_absorbed:
                    wt = splat(geo_ref, WT, g)
                    shape = wall_tiles(wt)

                def plane(a, acc):
                    out, back = acc
                    xa = plane_node(first_plane, a)
                    sa = v0 * xa
                    if with_absorbed:
                        wa = jnp.exp(-0.5 * xa * xa / wt)
                    for t in range(TILES):
                        s = sa + base[t]
                        f = f_ref[first_row + g, pl.ds(pl.multiple_of((a * TILES + t) * SUB, SUB), SUB), :]
                        out = out + jnp.maximum(s, 0.0) * f
                        if with_absorbed:
                            back = back + jnp.maximum(-s, 0.0) * (wa * shape[t])
                    return out, back

                zero = jnp.zeros((SUB, LANES), F32)
                out, back = lax.fori_loop(0, planes, plane, (zero, zero))
                at = pl.ds(pl.multiple_of(g * SUB, SUB), SUB)
                sums_ref[k, at, :] = out
                if with_absorbed:
                    sums_ref[FACES + k, at, :] = back

        return 0

    lax.fori_loop(0, SUB, cell, 0)


def unpack_geo(geo_in, geo_ref):
    tile = geo_in[...]
    for p in range(GEO):
        geo_ref[p] = column(tile, p)


def split_kernel(native_ref, f_ref, up_ref, down_ref):
    groups = native_ref.shape[0] // (SUB * SUB)

    def group(j, _):
        for g in range(SUB):
            x = native_ref[pl.ds(j * SUB * SUB + g, SUB, stride=SUB), :]
            at = pl.ds(pl.multiple_of(j * SUB, SUB), SUB)
            f_ref[g, at, :] = x
            if g < REACH:
                down_ref[g, at, :] = x
            if g >= SUB - REACH:
                up_ref[g - (SUB - REACH), at, :] = x
        return 0

    lax.fori_loop(0, groups, group, 0, unroll=2)


def split_profile(native):
    rows = native.shape[0] // SUB
    block = rows // 8
    spec = lambda n: pl.BlockSpec((n, block, LANES), lambda i: (0, i, 0))
    return pl.pallas_call(
        split_kernel,
        grid=(8,),
        in_specs=[pl.BlockSpec((block * SUB, LANES), lambda i: (i, 0))],
        out_specs=[spec(SUB), spec(REACH), spec(REACH)],
        out_shape=[
            jax.ShapeDtypeStruct((SUB, rows, LANES), F32),
            jax.ShapeDtypeStruct((REACH, rows, LANES), F32),
            jax.ShapeDtypeStruct((REACH, rows, LANES), F32),
        ],
        compiler_params=pltpu.CompilerParams(vmem_limit_bytes=VMEM_LIMIT),
        name="split_profile",
    )(native)


def first_sums_kernel(meta_ref, nbr_ref, geo_in, native_ref, f_ref, sums_out, out_ref, geo_ref, face_ref):
    rows = f_ref.shape[1]
    planes = rows // CHUNKS
    first_plane = meta_ref[1]
    unpack_geo(geo_in, geo_ref)
    packed = pack_sums(polynomial_sums(native_ref, planes, first_plane), 0)
    emitted_sums(f_ref, 0, planes, first_plane, nbr_ref, geo_ref, face_ref, True)
    packed = packed + pack_sums([face_sums(face_ref, k) for k in range(2 * FACES)], EMIT)
    sums_out[...] = packed

    def cell(g, _):
        scale = TIME_STEP / splat(geo_ref, VOL, g)
        v0, v1, v2 = [[scale * splat(geo_ref, FV + FACES * i + k, g) for k in range(FACES)] for i in range(3)]
        for t in range(TILES):
            xb, xc = tile_nodes(t)
            base = [v1[k] * xb + v2[k] * xc for k in range(FACES)]

            def plane(a, _):
                xa = plane_node(first_plane, a)
                acc = None
                for k in range(FACES):
                    term = jnp.maximum(v0[k] * xa + base[k], 0.0)
                    acc = term if acc is None else acc + term
                out_ref[g, pl.ds(pl.multiple_of((a * TILES + t) * SUB, SUB), SUB), :] = acc
                return 0

            lax.fori_loop(0, planes, plane, 0, unroll=4)
        return 0

    lax.fori_loop(0, SUB, cell, 0)


def first_sums(meta, nbr, geo, native, f):
    rows = f.shape[1]
    return pl.pallas_call(
        first_sums_kernel,
        in_specs=[
            pl.BlockSpec(memory_space=pltpu.SMEM),
            pl.BlockSpec(memory_space=pltpu.SMEM),
            pl.BlockSpec(memory_space=pltpu.VMEM),
            pl.BlockSpec(memory_space=pltpu.VMEM),
            pl.BlockSpec(memory_space=pltpu.VMEM),
        ],
        out_specs=[pl.BlockSpec(memory_space=pltpu.VMEM)] * 2,
        out_shape=[
            jax.ShapeDtypeStruct((SUB, LANES), F32),
            jax.ShapeDtypeStruct((SUB, rows, LANES), F32),
        ],
        scratch_shapes=[
            pltpu.VMEM((GEO, SUB, LANES), F32),
            pltpu.VMEM((2 * FACES, SUB * SUB, LANES), F32),
        ],
        compiler_params=pltpu.CompilerParams(vmem_limit_bytes=VMEM_LIMIT),
        name="first_sums",
    )(meta, nbr, geo, native, f)


def quantities(tile):
    m = [WEIGHT * column(tile, p) for p in range(13)]
    n = m[0]
    rn = 1.0 / n
    u = [m[1 + i] * rn for i in range(3)]
    uu = u[0] * u[0] + u[1] * u[1] + u[2] * u[2]
    trace = m[4] + m[5] + m[6]
    width = trace - n * uu
    temperature = width * rn * (1.0 / 3.0)
    second = [[m[4], m[7], m[8]], [m[7], m[5], m[9]], [m[8], m[9], m[6]]]
    q = []
    for i in range(3):
        across = u[0] * second[i][0] + u[1] * second[i][1] + u[2] * second[i][2]
        q.append(0.5 * (m[10 + i] - 2.0 * across - u[i] * trace + 2.0 * uu * m[1 + i]))
    return n, u, temperature, q


def macro_kernel(sums_ref, out_ref):
    n, u, temperature, q = quantities(sums_ref[...])
    lane, sub = lane_iota(), sub_iota()
    for i, x in enumerate((n, *u, temperature, *q)):
        row = jnp.sum(jnp.where(lane == sub, x, 0.0), axis=0, keepdims=True)
        out_ref[pl.ds(i, 1), :] = row[:, :SUB]


def macro(sums):
    return pl.pallas_call(
        macro_kernel,
        in_specs=[pl.BlockSpec(memory_space=pltpu.VMEM)],
        out_specs=pl.BlockSpec(memory_space=pltpu.VMEM),
        out_shape=jax.ShapeDtypeStruct((8, SUB), F32),
        name="macro",
    )(sums)


def step_kernel(
    last,
    meta_ref,
    nbr_ref,
    geo_in,
    sums_in,
    absorbed_in,
    f_any,
    before_any,
    after_any,
    out_any,
    *refs,
):
    if last:
        native_ref, sums_out, ext, outflow, geo_ref, ta, coef, sems = refs
    else:
        f_out, up_out, down_out, sums_out, native_ref, ext, outflow, face_ref, geo_ref, ta, coef, sems = refs
    rows = ext.shape[1]
    planes = rows // CHUNKS
    first_plane = meta_ref[1]
    copies = [
        pltpu.make_async_copy(before_any, ext.at[pl.ds(0, REACH)], sems.at[0]),
        pltpu.make_async_copy(f_any, ext.at[pl.ds(REACH, SUB)], sems.at[1]),
        pltpu.make_async_copy(after_any, ext.at[pl.ds(REACH + SUB, REACH)], sems.at[2]),
        pltpu.make_async_copy(out_any, outflow, sems.at[3]),
    ]
    for c in copies:
        c.start()

    unpack_geo(geo_in, geo_ref)
    sums = sums_in[...]
    absorbed = absorbed_in[...]
    n, u, temperature, q = quantities(sums)
    rt = 1.0 / temperature
    rate = TIME_STEP * n * temperature / (SHEAR * jnp.exp(POWER * jnp.log(temperature)))
    height = rate * n * rt * jnp.sqrt(rt)
    slope = (1.0 / 3.0) / (5.0 * n * temperature * temperature)
    scale = -TIME_STEP / geo_ref[VOL]
    coef[0] = rate
    coef[1] = rt
    coef[2], coef[3] = u[1], u[2]
    coef[4], coef[5] = slope * q[1], slope * q[2]
    for k in range(FACES):
        wall = geo_ref[WALL + k] > 0.5
        ratio = jnp.where(
            wall, column(sums, EMIT + k) / jnp.where(wall, column(absorbed, ABSORB + k), 1.0), 1.0
        )
        for i in range(3):
            coef[6 + FACES * i + k] = scale * ratio * geo_ref[FV + FACES * i + k]

    def plane_table(a, _):
        ca = plane_node(first_plane, a) - u[0]
        za = ca * ca * rt
        ta[0, a] = height * jnp.exp(-0.5 * za)
        ta[1, a] = slope * q[0] * ca
        ta[2, a] = za - 5.0
        return 0

    lax.fori_loop(0, planes, plane_table, 0)

    def wall_row(g, _):
        walls = nbr_ref[0, g] < 0
        for k in range(1, FACES):
            walls = jnp.logical_or(walls, nbr_ref[k, g] < 0)

        @pl.when(walls)
        def _():
            wt = splat(geo_ref, WT, g)
            shape = wall_tiles(wt)

            def plane(a, _):
                xa = plane_node(first_plane, a)
                wa = jnp.exp(-0.5 * xa * xa / wt)
                for t in range(TILES):
                    at = pl.ds(pl.multiple_of((a * TILES + t) * SUB, SUB), SUB)
                    ext[2 * REACH + SUB + g, at, :] = wa * shape[t]
                return 0

            lax.fori_loop(0, planes, plane, 0)

        return 0

    lax.fori_loop(0, SUB, wall_row, 0)
    for c in copies:
        c.wait()

    def cell(g, _):
        base_row = meta_ref[0]
        source = []
        for k in range(FACES):
            j = nbr_ref[k, g]
            source.append(jnp.where(j < 0, 2 * REACH + SUB + g, j - base_row))
        keep = 1.0 - splat(coef, 0, g)
        rtg = splat(coef, 1, g)
        ub, uc = splat(coef, 2, g), splat(coef, 3, g)
        qb, qc = splat(coef, 4, g), splat(coef, 5, g)
        v0 = [splat(coef, 6 + k, g) for k in range(FACES)]
        for pair in range(TILES // 2):
            base, bell, heat, zz = [], [], [], []
            for t in (2 * pair, 2 * pair + 1):
                xb, xc = tile_nodes(t)
                cb, cc = xb - ub, xc - uc
                z = (cb * cb + cc * cc) * rtg
                bell.append(jnp.exp(-0.5 * z))
                heat.append(cb * qb + cc * qc)
                zz.append(z)
                base.append(
                    [splat(coef, 12 + k, g) * xb + splat(coef, 18 + k, g) * xc for k in range(FACES)]
                )

            def plane(a, _):
                xa = plane_node(first_plane, a)
                height_a = jnp.broadcast_to(ta[0, a, pl.ds(g, 1), :], (SUB, LANES))
                heat_a = jnp.broadcast_to(ta[1, a, pl.ds(g, 1), :], (SUB, LANES))
                z_a = jnp.broadcast_to(ta[2, a, pl.ds(g, 1), :], (SUB, LANES))
                sa = [v0[k] * xa for k in range(FACES)]
                for i in range(2):
                    tile = a * TILES + 2 * pair + i
                    at = pl.ds(pl.multiple_of(tile * SUB, SUB), SUB)
                    f = ext[REACH + g, at, :]
                    acc = f * (keep - outflow[g, at, :])
                    for k in range(FACES):
                        acc = acc + jnp.maximum(sa[k] + base[i][k], 0.0) * ext[source[k], at, :]
                    target = (height_a * bell[i]) * (1.0 + (heat_a + heat[i]) * (z_a + zz[i]))
                    new = acc + target
                    native_ref[pl.ds(tile * SUB * SUB + g, SUB, stride=SUB), :] = new
                    if not last:
                        f_out[g, at, :] = new
                return 0

            lax.fori_loop(0, planes, plane, 0, unroll=2)
        return 0

    lax.fori_loop(0, SUB, cell, 0)

    if not last:

        def spread(j, _):
            at = pl.ds(pl.multiple_of(j * SUB, SUB), SUB)
            for i in range(REACH):
                down_out[i, at, :] = f_out[i, at, :]
                up_out[i, at, :] = f_out[SUB - REACH + i, at, :]
            return 0

        lax.fori_loop(0, rows // SUB, spread, 0, unroll=4)

    packed = pack_sums(polynomial_sums(native_ref, planes, first_plane), 0)
    if not last:
        emitted_sums(f_out, 0, planes, first_plane, nbr_ref, geo_ref, face_ref, False)
        packed = packed + pack_sums([face_sums(face_ref, k) for k in range(FACES)], EMIT)
    sums_out[...] = packed


def step(last, meta, nbr, geo, sums, absorbed, f, before, after, outflow):
    rows = f.shape[1]
    planes = rows // CHUNKS
    vmem, smem, anywhere = (
        pl.BlockSpec(memory_space=pltpu.VMEM),
        pl.BlockSpec(memory_space=pltpu.SMEM),
        pl.BlockSpec(memory_space=pl.ANY),
    )
    array = lambda *shape: jax.ShapeDtypeStruct(shape, F32)
    native = (SUB * rows, LANES)
    if last:
        out_shape = [array(*native), array(SUB, LANES)]
        scratch = []
    else:
        out_shape = [array(SUB, rows, LANES), array(REACH, rows, LANES), array(REACH, rows, LANES), array(SUB, LANES)]
        scratch = [pltpu.VMEM(native, F32)]
    scratch += [
        pltpu.VMEM((2 * REACH + 2 * SUB, rows, LANES), F32),
        pltpu.VMEM((SUB, rows, LANES), F32),
    ]
    if not last:
        scratch.append(pltpu.VMEM((FACES, SUB * SUB, LANES), F32))
    scratch += [
        pltpu.VMEM((GEO, SUB, LANES), F32),
        pltpu.VMEM((3, planes, SUB, LANES), F32),
        pltpu.VMEM((6 + 3 * FACES, SUB, LANES), F32),
        pltpu.SemaphoreType.DMA((4,)),
    ]

    def kernel(*refs):
        step_kernel(last, *refs)

    return pl.pallas_call(
        kernel,
        in_specs=[smem, smem, vmem, vmem, vmem, anywhere, anywhere, anywhere, anywhere],
        out_specs=[vmem] * len(out_shape),
        out_shape=out_shape,
        scratch_shapes=scratch,
        compiler_params=pltpu.CompilerParams(vmem_limit_bytes=VMEM_LIMIT),
        name="last_step" if last else "step",
    )(meta, nbr, geo, sums, absorbed, f, before, after, outflow)


def exchange(up, down):
    size = lax.axis_size("space")
    forward = [(i, i + 1) for i in range(size - 1)]
    backward = [(i + 1, i) for i in range(size - 1)]
    return lax.ppermute(up, "space", forward), lax.ppermute(down, "space", backward)


def per_device(particle_profile, neighbors, face_vectors, volumes, wall_temp):
    cells, points = particle_profile.shape
    rows = points // LANES
    plane_count = NV // lax.axis_size("vel")
    native = particle_profile.reshape(cells, rows, LANES).transpose(1, 0, 2).reshape(cells * rows, LANES)
    meta = jnp.stack([lax.axis_index("space") * cells - REACH, lax.axis_index("vel") * plane_count])
    geo = jnp.concatenate(
        [face_vectors.reshape(3 * FACES, cells), volumes[None], wall_temp[None], (neighbors < 0).astype(F32)]
    )
    geo = jnp.pad(geo.T, ((0, 0), (0, LANES - GEO)))
    f, up, down = split_profile(native)
    before, after = exchange(up, down)
    sums0, outflow = first_sums(meta, neighbors, geo, native, f)
    sums0 = lax.psum(sums0, "vel")
    f, up, down, sums1 = step(False, meta, neighbors, geo, sums0, sums0, f, before, after, outflow)
    before, after = exchange(up, down)
    sums1 = lax.psum(sums1, "vel")
    native, sums2 = step(True, meta, neighbors, geo, sums1, sums0, f, before, after, outflow)
    macro_quantities = macro(lax.psum(sums2, "vel"))
    evolved = native.reshape(rows, cells, LANES).transpose(1, 0, 2).reshape(cells, points)
    return evolved, macro_quantities


def solution(mesh):
    return jax.shard_map(
        per_device,
        mesh=mesh,
        in_specs=(
            P("space", "vel"),
            P(None, "space"),
            P(None, None, "space"),
            P("space"),
            P("space"),
        ),
        out_specs=(P("space", "vel"), P(None, "space")),
        check_vma=False,
    )
```

profile of v0, /device:TPU:4, one launch (start us, length us, event | category | flops | bytes accessed | tf_op | source)
XLA Modules:
  0.0 87.4 jit_solution(2807655846856604918)
XLA Ops:
  0.6 0.0 copy-start.9
  0.6 0.0 copy-start.10
  0.7 0.0 copy-start.3
  0.7 1.6 %copy-done.3 = f32[8,65536]{1,0:T(8,128)S(1)} copy-done((f32[8,65536]{1,0:T(8,128)S(1)}, f32[8,65536]{1,0:T(8,128)}, u32[]{:S(2)}) %copy-start.3) | copy-done | bytes 2097176
  2.3 0.0 copy-start.7
  2.3 0.0 copy-start.8
  2.3 3.3 %split_profile.1 = (f32[8,512,128]{2,1,0:T(8,128)S(1)}, f32[3,512,128]{2,1,0:T(8,128)}, f32[3,512,128]{2,1,0:T(8,128)}) custom-call(f32[4096,128]{1,0:T(8,128)S(1)} %bitcast.16), custom_call_target="tpu_custom_call" | custom-call | tf_op jit(solution)/shard_map/split_profile/pallas_call | solution.py:221
  5.5 0.0 copy-start
  5.5 1.3 %copy-done = f32[8,512,128]{2,1,0:T(8,128)} copy-done((f32[8,512,128]{2,1,0:T(8,128)}, f32[8,512,128]{2,1,0:T(8,128)S(1)}, u32[]{:S(2)}) %copy-start) | copy-done | bytes 2097176
  6.8 1.9 %collective-permute-start = (f32[3,512,128]{2,1,0:T(8,128)}, f32[3,512,128]{2,1,0:T(8,128)S(1)}, u32[]{:S(2)}, u32[]{:S(2)}) collective-permute-start(f32[3,512,128]{2,1,0:T(8,128)} %get-tuple-element.15), channel_id=1, source_target_pairs={{0,4},{4,8},{8,12},{12,16},{16,20},{20,24},{24,28},{1,5},{5,9},{9,... | collective-permute-start | bytes 2359304 | tf_op jit(solution)/shard_map/ppermute | solution.py:528
  8.8 4.5 %collective-permute-start.1 = (f32[3,512,128]{2,1,0:T(8,128)}, f32[3,512,128]{2,1,0:T(8,128)}, u32[]{:S(2)}, u32[]{:S(2)}) collective-permute-start(f32[3,512,128]{2,1,0:T(8,128)} %get-tuple-element.16), channel_id=1, source_target_pairs={{4,0},{8,4},{12,8},{16,12},{20,16},{24,20},{28,24},{5,1},{9,5},{13... | collective-permute-start | bytes 2359304 | tf_op jit(solution)/shard_map/ppermute | solution.py:528
  13.3 0.0 copy-done.9
  13.3 0.1 copy.13
  13.4 0.0 copy-done.10
  13.4 0.1 copy.14
  13.5 0.0 copy-done.7
  13.5 0.1 copy.12
  13.6 0.0 copy-done.8
  13.6 0.1 copy.15
  13.7 0.1 maximum_bitcast_fusion
  13.8 0.1 pad_add_fusion.meta_ref.refs_0_
  13.8 0.0 copy-start.1
  13.8 1.6 %copy-done.1 = f32[8,512,128]{2,1,0:T(8,128)S(1)} copy-done((f32[8,512,128]{2,1,0:T(8,128)S(1)}, f32[8,512,128]{2,1,0:T(8,128)}, u32[]{:S(2)}) %copy-start.1) | copy-done | bytes 2097176
  15.4 0.0 copy-start.4
  15.4 1.6 %copy-done.4 = f32[8,65536]{1,0:T(8,128)S(1)} copy-done((f32[8,65536]{1,0:T(8,128)S(1)}, f32[8,65536]{1,0:T(8,128)}, u32[]{:S(2)}) %copy-start.4) | copy-done | bytes 2097176
  17.0 6.0 %first_sums.1 = (f32[8,128]{1,0:T(8,128)S(1)}, f32[8,512,128]{2,1,0:T(8,128)S(1)}) custom-call(s32[2]{0:T(128)S(1)} %pad_add_fusion.meta_ref.refs_0_, s32[6,8]{1,0:T(8,128)S(1)} %copy-done.7, f32[8,128]{1,0:T(8,128)S(1)} %pad.4.geo_in.refs_2_, f32[4096,128]{1,0:T(8,128)S(1)} %bitcast.17, f32[8,512,128]{2,1,0:T(8,128)S(1)} %copy-done.1), custom_call_target="tpu_custom_call" | custom-call | tf_op jit(solution)/shard_map/first_sums/pallas_call | solution.py:270
  23.0 12.0 %psum.21.refs_3_.refs_4_ = f32[8,128]{1,0:T(8,128)S(1)} all-reduce(f32[8,128]{1,0:T(8,128)S(1)} %get-tuple-element.14), channel_id=1, replica_groups=mesh['space'=8,'vel'=4] {'vel'}, use_global_device_ids=true, to_apply=%region_0.1 | all-reduce | flops 1024 | bytes 8192 | tf_op jit(solution)/shard_map/psum | solution.py:544
  35.0 0.0 collective-permute-done.refs_6_
  35.0 0.0 collective-permute-done.1.refs_7_
  35.0 0.0 copy-start.2
  35.0 1.6 %copy-done.2 = f32[8,512,128]{2,1,0:T(8,128)S(1)} copy-done((f32[8,512,128]{2,1,0:T(8,128)S(1)}, f32[8,512,128]{2,1,0:T(8,128)}, u32[]{:S(2)}) %copy-start.2) | copy-done | bytes 2097176
  36.6 8.9 %step.1 = (f32[8,512,128]{2,1,0:T(8,128)S(1)}, f32[3,512,128]{2,1,0:T(8,128)}, f32[3,512,128]{2,1,0:T(8,128)}, f32[8,128]{1,0:T(8,128)S(1)}) custom-call(s32[2]{0:T(128)S(1)} %pad_add_fusion.meta_ref.refs_0_, s32[6,8]{1,0:T(8,128)S(1)} %copy-done.7, f32[8,128]{1,0:T(8,128)S(1)} %pad.4.geo_in.refs_2_, f32[8,128]{1,0:T(8,128)S(1)} %psum.21.refs_3_.refs_4_, ...), custom_call_target="tpu_custom_call" | custom-call | tf_op jit(solution)/shard_map/step/pallas_call | solution.py:513
  45.5 0.0 copy-start.5
  45.5 1.3 %copy-done.5 = f32[8,512,128]{2,1,0:T(8,128)} copy-done((f32[8,512,128]{2,1,0:T(8,128)}, f32[8,512,128]{2,1,0:T(8,128)S(1)}, u32[]{:S(2)}) %copy-start.5) | copy-done | bytes 2097176
  46.8 1.9 %collective-permute-start.2 = (f32[3,512,128]{2,1,0:T(8,128)}, f32[3,512,128]{2,1,0:T(8,128)S(1)}, u32[]{:S(2)}, u32[]{:S(2)}) collective-permute-start(f32[3,512,128]{2,1,0:T(8,128)} %get-tuple-element.20), channel_id=1, source_target_pairs={{0,4},{4,8},{8,12},{12,16},{16,20},{20,24},{24,28},{1,5},{5,9},{9,... | collective-permute-start | bytes 2359304 | tf_op jit(solution)/shard_map/ppermute | solution.py:528
  48.7 4.5 %collective-permute-start.3 = (f32[3,512,128]{2,1,0:T(8,128)}, f32[3,512,128]{2,1,0:T(8,128)}, u32[]{:S(2)}, u32[]{:S(2)}) collective-permute-start(f32[3,512,128]{2,1,0:T(8,128)} %get-tuple-element.21), channel_id=1, source_target_pairs={{4,0},{8,4},{12,8},{16,12},{20,16},{24,20},{28,24},{5,1},{9,5},{13... | collective-permute-start | bytes 2359304 | tf_op jit(solution)/shard_map/ppermute | solution.py:528
  53.3 8.4 %psum.22.refs_3_ = f32[8,128]{1,0:T(8,128)S(1)} all-reduce(f32[8,128]{1,0:T(8,128)S(1)} %get-tuple-element.18), channel_id=1, replica_groups=mesh['space'=8,'vel'=4] {'vel'}, use_global_device_ids=true, to_apply=%region_1.2 | all-reduce | flops 1024 | bytes 8192 | tf_op jit(solution)/shard_map/psum | solution.py:547
  61.7 3.3 %collective-permute-done.2.refs_6_ = f32[3,512,128]{2,1,0:T(8,128)S(1)} collective-permute-done((f32[3,512,128]{2,1,0:T(8,128)}, f32[3,512,128]{2,1,0:T(8,128)S(1)}, u32[]{:S(2)}, u32[]{:S(2)}) %collective-permute-start.2) | collective-permute-done | bytes 786464 | tf_op jit(solution)/shard_map/ppermute | solution.py:528
  64.9 2.9 %collective-permute-done.3.refs_7_ = f32[3,512,128]{2,1,0:T(8,128)} collective-permute-done((f32[3,512,128]{2,1,0:T(8,128)}, f32[3,512,128]{2,1,0:T(8,128)}, u32[]{:S(2)}, u32[]{:S(2)}) %collective-permute-start.3) | collective-permute-done | bytes 786464 | tf_op jit(solution)/shard_map/ppermute | solution.py:528
  67.8 0.0 copy-start.6
  67.8 1.6 %copy-done.6 = f32[8,512,128]{2,1,0:T(8,128)S(1)} copy-done((f32[8,512,128]{2,1,0:T(8,128)S(1)}, f32[8,512,128]{2,1,0:T(8,128)}, u32[]{:S(2)}) %copy-start.6) | copy-done | bytes 2097176
  69.4 7.6 %last_step.1 = (f32[4096,128]{1,0:T(8,128)}, f32[8,128]{1,0:T(8,128)S(1)}) custom-call(s32[2]{0:T(128)S(1)} %pad_add_fusion.meta_ref.refs_0_, s32[6,8]{1,0:T(8,128)S(1)} %copy-done.7, f32[8,128]{1,0:T(8,128)S(1)} %pad.4.geo_in.refs_2_, f32[8,128]{1,0:T(8,128)S(1)} %psum.22.refs_3_, f32[8,128]{1,0:T(8,128)S(1)} %psum.21.refs_3_.refs_4_, ...), custom_call_target="tpu_custom_call" | custom-call | tf_op jit(solution)/shard_map/last_step/pallas_call | solution.py:513
  77.1 9.0 %psum.23.sums_ref = f32[8,128]{1,0:T(8,128)} all-reduce(f32[8,128]{1,0:T(8,128)S(1)} %get-tuple-element.23), channel_id=1, replica_groups=mesh['space'=8,'vel'=4] {'vel'}, use_global_device_ids=true, to_apply=%region_2.3 | all-reduce | flops 1024 | bytes 8192 | tf_op jit(solution)/shard_map/psum | solution.py:549
  86.0 1.4 %macro.1 = f32[8,8]{1,0:T(8,128)} custom-call(f32[8,128]{1,0:T(8,128)} %psum.23.sums_ref), custom_call_target="tpu_custom_call" | custom-call | tf_op jit(solution)/shard_map/macro/pallas_call | solution.py:319
  (3 shorter events, 0.0 us)
Async XLA Ops:
  0.6 12.7 %copy-start.9 = (f32[8]{0:T(128)S(1)}, f32[8]{0:T(128)}, u32[]{:S(2)}) copy-start(f32[8]{0:T(128)} %param.8) | copy-start | bytes 100
  0.6 12.8 %copy-start.10 = (f32[8]{0:T(128)S(1)}, f32[8]{0:T(128)}, u32[]{:S(2)}) copy-start(f32[8]{0:T(128)} %param.9) | copy-start | bytes 100
  0.7 1.6 %copy-start.3 = (f32[8,65536]{1,0:T(8,128)S(1)}, f32[8,65536]{1,0:T(8,128)}, u32[]{:S(2)}) copy-start(f32[8,65536]{1,0:T(8,128)} %param.5) | copy-start | bytes 6291460
  2.3 11.2 %copy-start.7 = (s32[6,8]{1,0:T(8,128)S(1)}, s32[6,8]{1,0:T(8,128)}, u32[]{:S(2)}) copy-start(s32[6,8]{1,0:T(8,128)} %refs_1_.3) | copy-start | bytes 580
  2.3 11.3 %copy-start.8 = (f32[3,6,8]{2,1,0:T(8,128)S(1)}, f32[3,6,8]{2,1,0:T(8,128)}, u32[]{:S(2)}) copy-start(f32[3,6,8]{2,1,0:T(8,128)} %param.7) | copy-start | bytes 1732
  5.5 1.3 %copy-start = (f32[8,512,128]{2,1,0:T(8,128)}, f32[8,512,128]{2,1,0:T(8,128)S(1)}, u32[]{:S(2)}) copy-start(f32[8,512,128]{2,1,0:T(8,128)S(1)} %get-tuple-element.13.f_ref.refs_5_) | copy-start | bytes 6291460
  6.8 28.1 %collective-permute-start = (f32[3,512,128]{2,1,0:T(8,128)}, f32[3,512,128]{2,1,0:T(8,128)S(1)}, u32[]{:S(2)}, u32[]{:S(2)}) collective-permute-start(f32[3,512,128]{2,1,0:T(8,128)} %get-tuple-element.15), channel_id=1, source_target_pairs={{0,4},{4,8},{8,12},{12,16},{16,20},{20,24},{24,28},{1,5},{5,9},{9,... | collective-permute-start | bytes 2359304 | tf_op jit(solution)/shard_map/ppermute | solution.py:528
  8.8 26.2 %collective-permute-start.1 = (f32[3,512,128]{2,1,0:T(8,128)}, f32[3,512,128]{2,1,0:T(8,128)}, u32[]{:S(2)}, u32[]{:S(2)}) collective-permute-start(f32[3,512,128]{2,1,0:T(8,128)} %get-tuple-element.16), channel_id=1, source_target_pairs={{4,0},{8,4},{12,8},{16,12},{20,16},{24,20},{28,24},{5,1},{9,5},{13... | collective-permute-start | bytes 2359304 | tf_op jit(solution)/shard_map/ppermute | solution.py:528
  13.8 1.6 %copy-start.1 = (f32[8,512,128]{2,1,0:T(8,128)S(1)}, f32[8,512,128]{2,1,0:T(8,128)}, u32[]{:S(2)}) copy-start(f32[8,512,128]{2,1,0:T(8,128)} %copy-done) | copy-start | bytes 6291460
  15.4 1.6 %copy-start.4 = (f32[8,65536]{1,0:T(8,128)S(1)}, f32[8,65536]{1,0:T(8,128)}, u32[]{:S(2)}) copy-start(f32[8,65536]{1,0:T(8,128)} %param.5) | copy-start | bytes 6291460
  35.0 1.6 %copy-start.2 = (f32[8,512,128]{2,1,0:T(8,128)S(1)}, f32[8,512,128]{2,1,0:T(8,128)}, u32[]{:S(2)}) copy-start(f32[8,512,128]{2,1,0:T(8,128)} %copy-done) | copy-start | bytes 6291460
  45.5 1.3 %copy-start.5 = (f32[8,512,128]{2,1,0:T(8,128)}, f32[8,512,128]{2,1,0:T(8,128)S(1)}, u32[]{:S(2)}) copy-start(f32[8,512,128]{2,1,0:T(8,128)S(1)} %get-tuple-element.19.refs_5_) | copy-start | bytes 6291460
  46.8 18.1 %collective-permute-start.2 = (f32[3,512,128]{2,1,0:T(8,128)}, f32[3,512,128]{2,1,0:T(8,128)S(1)}, u32[]{:S(2)}, u32[]{:S(2)}) collective-permute-start(f32[3,512,128]{2,1,0:T(8,128)} %get-tuple-element.20), channel_id=1, source_target_pairs={{0,4},{4,8},{8,12},{12,16},{16,20},{20,24},{24,28},{1,5},{5,9},{9,... | collective-permute-start | bytes 2359304 | tf_op jit(solution)/shard_map/ppermute | solution.py:528
  48.7 19.1 %collective-permute-start.3 = (f32[3,512,128]{2,1,0:T(8,128)}, f32[3,512,128]{2,1,0:T(8,128)}, u32[]{:S(2)}, u32[]{:S(2)}) collective-permute-start(f32[3,512,128]{2,1,0:T(8,128)} %get-tuple-element.21), channel_id=1, source_target_pairs={{4,0},{8,4},{12,8},{16,12},{20,16},{24,20},{28,24},{5,1},{9,5},{13... | collective-permute-start | bytes 2359304 | tf_op jit(solution)/shard_map/ppermute | solution.py:528
  67.8 1.6 %copy-start.6 = (f32[8,512,128]{2,1,0:T(8,128)S(1)}, f32[8,512,128]{2,1,0:T(8,128)}, u32[]{:S(2)}) copy-start(f32[8,512,128]{2,1,0:T(8,128)} %copy-done.5) | copy-start | bytes 6291460
where the time goes:
time: 89.1 us; the launch traced here: 87.4 us
  blocking collectives  29.3 us (33%)
  Pallas kernels  27.2 us (31%)
  starting transfers between devices  12.9 us (14%)
  local copies, waits for them, and re-layouts  10.9 us (12%)
  waiting for transfers between devices  6.18 us (7%)
    pallas_call x2, Pallas kernels, step(): pl.pallas_call(kernel, in_specs=[smem, smem, vmem, vmem, vmem, anywhere,...  16.5 us
    psum x1, blocking collectives, per_device(): sums0 = lax.psum(sums0, 'vel')  12 us
    unnamed x23, local copies, waits for them, and re-layouts  10.7 us
    ppermute x2, starting transfers between devices, exchange(): lax.ppermute(down, 'space', backward)  9.08 us
    psum x1, blocking collectives, per_device(): macro_quantities = macro(lax.psum(sums2, 'vel'))  8.96 us
    psum x1, blocking collectives, per_device(): sums1 = lax.psum(sums1, 'vel')  8.38 us
    pallas_call x1, Pallas kernels, first_sums(): pl.pallas_call(first_sums_kernel, in_specs=[pl.BlockSpec(memory_space=plt...  5.99 us
    ppermute x2, starting transfers between devices, exchange(): lax.ppermute(up, 'space', forward)  3.82 us
  transfers between devices with their start and end apart: 4, of which 2 were waited for; matrix products, arithmetic and copies ran while one was open for 1% of the time, Pallas kernels for 7%

commit v1 on v0

v1 whole, which is shorter than its diff:
```python
import functools
import math

import jax
import jax.numpy as jnp
from jax import lax
from jax.experimental import pallas as pl
from jax.experimental.pallas import tpu as pltpu
from jax.sharding import PartitionSpec as P

NV = 64
FACES = 6
REACH = 3
STEPS = 2
LANES = 128
SUB = 8

TIME_STEP = 0.015
SHEAR = 0.1
POWER = 0.81
SPEED_LIMIT = 6.0
H = 2.0 * SPEED_LIMIT / NV
WEIGHT = H**3 * (2.0 * math.pi) ** (-1.5)

CHUNKS = NV * NV // LANES
TILES = CHUNKS // SUB

FV, VOL, WT, WALL, LOCAL, FIRST = 0, 18, 19, 20, 26, 32
GEO = 33
WALL_LINK = -64
BEFORE_PAIRS = tuple((g, r) for g in range(REACH) for r in range(g, REACH))
EMIT, ABSORB = 13, 19
SUMS = 25

F32 = jnp.float32
VMEM_LIMIT = 16 * 1024 * 1024


def lane_iota():
    return lax.broadcasted_iota(jnp.int32, (SUB, LANES), 1)


def sub_iota():
    return lax.broadcasted_iota(jnp.int32, (SUB, LANES), 0)


def half_of(lane):
    return (lane >= NV).astype(F32)


def third_component(lane):
    c = jnp.where(lane >= NV, lane - NV, lane).astype(F32)
    return -SPEED_LIMIT + (c + 0.5) * H


def tile_nodes(t):
    lane = lane_iota()
    b = (2 * SUB * t + 2 * sub_iota()).astype(F32) + half_of(lane)
    return -SPEED_LIMIT + (b + 0.5) * H, third_component(lane)


def column(tile, p):
    return jnp.broadcast_to(tile[:, p : p + 1], (SUB, LANES))


def splat(ref, i, g):
    return jnp.broadcast_to(ref[i, pl.ds(g, 1), :], (SUB, LANES))


def total(tile):
    return jnp.broadcast_to(jnp.sum(tile, axis=1, keepdims=True), (SUB, LANES))


def face_coefficients(geo_ref, k, g):
    return [splat(geo_ref, FV + FACES * i + k, g) for i in range(3)]


def at_rows(start, size=SUB):
    return pl.ds(pl.multiple_of(start, SUB), size)


def wall_tiles(wall_temp):
    rt = 1.0 / wall_temp
    scale = rt * jnp.sqrt(rt)
    out = []
    for t in range(TILES):
        xb, xc = tile_nodes(t)
        out.append(scale * jnp.exp(-0.5 * (xb * xb + xc * xc) * rt))
    return out


def unpack_geo(geo_in, geo_ref):
    tile = geo_in[...]
    for p in range(GEO):
        geo_ref[p] = column(tile, p)


def pack_sums(arrays, start):
    lane = lane_iota()
    out = jnp.zeros((SUB, LANES), F32)
    for p, x in enumerate(arrays):
        out = jnp.where(lane == start + p, total(x), out)
    return out


def over_sublanes(ref, k):
    out = ref[k, pl.ds(0, SUB, stride=SUB), :]
    for s in range(1, SUB):
        out = out + ref[k, pl.ds(s, SUB, stride=SUB), :]
    return out


def finish_polynomials(y, first, planes):
    y0, y1, y2, y3, by0, by1, by2, bby0, bby1, bbby0 = y
    m = first + 0.5 * (planes - 1) * H
    c = third_component(lane_iota())
    cc = c * c
    a = y1 + m * y0
    aa = y2 + m * (2.0 * y1 + m * y0)
    aaa = y3 + m * (3.0 * y2 + m * (3.0 * y1 + m * y0))
    ab = by1 + m * by0
    aab = by2 + m * (2.0 * by1 + m * by0)
    abb = bby1 + m * bby0
    return (
        y0,
        a,
        by0,
        c * y0,
        aa,
        bby0,
        cc * y0,
        ab,
        c * a,
        c * by0,
        aaa + abb + cc * a,
        aab + bbby0 + cc * by0,
        c * (aa + bby0 + cc * y0),
    )


def polynomial_sums(f_ref, planes, parts_ref):
    half = planes // 2

    def cell(g, _):
        out = [None] * 10
        for t in range(TILES):
            y0 = y1 = y2 = y3 = None
            for i in range(half):
                d = (i + 0.5) * H
                hi = f_ref[g, pl.ds(((half + i) * TILES + t) * SUB, SUB), :]
                lo = f_ref[g, pl.ds(((half - 1 - i) * TILES + t) * SUB, SUB), :]
                s, r = hi + lo, hi - lo
                if i == 0:
                    y0, y1, y2, y3 = s, d * r, (d * d) * s, (d * d * d) * r
                else:
                    y0, y1, y2, y3 = y0 + s, y1 + d * r, y2 + (d * d) * s, y3 + (d * d * d) * r
            b, _c = tile_nodes(t)
            bb = b * b
            terms = (y0, y1, y2, y3, b * y0, b * y1, b * y2, bb * y0, bb * y1, bb * (b * y0))
            out = [x if o is None else o + x for o, x in zip(out, terms)]
        for p in range(10):
            parts_ref[p, at_rows(g * SUB), :] = out[p]
        return 0

    lax.fori_loop(0, SUB, cell, 0)
    return [over_sublanes(parts_ref, p) for p in range(10)]


def native_polynomial_sums(native_ref, planes):
    half, side = planes // 2, CHUNKS // 2
    zero = jnp.zeros((SUB, LANES), F32)
    acc = [zero] * 10

    def plane(a, acc):
        xa = (a.astype(F32) - 0.5 * (planes - 1)) * H
        b0 = b1 = b2 = b3 = None
        for i in range(side):
            y = (2 * i + 1) * H
            hi = native_ref[at_rows((a * CHUNKS + side + i) * SUB), :]
            lo = native_ref[at_rows((a * CHUNKS + side - 1 - i) * SUB), :]
            s, d = hi + lo, hi - lo
            terms = (s, y * d, (y * y) * s, (y * y * y) * d)
            if i == 0:
                b0, b1, b2, b3 = terms
            else:
                b0, b1, b2, b3 = b0 + terms[0], b1 + terms[1], b2 + terms[2], b3 + terms[3]
        a0, a1, a2 = xa * b0, xa * b1, xa * b2
        aa0 = xa * a0
        new = (b0, a0, aa0, xa * aa0, b1, a1, xa * a1, b2, a2, b3)
        return tuple(x + z for x, z in zip(acc, new))

    g0, a0, aa0, aaa0, g1, a1, aa1, g2, a2, g3 = lax.fori_loop(0, planes, plane, tuple(acc))
    e = (half_of(lane_iota()) - 0.5) * H
    return [
        g0,
        a0,
        aa0,
        aaa0,
        g1 + e * g0,
        a1 + e * a0,
        aa1 + e * aa0,
        g2 + e * (2.0 * g1 + e * g0),
        a2 + e * (2.0 * a1 + e * a0),
        g3 + e * (3.0 * g2 + e * (3.0 * g1 + e * g0)),
    ]


def wall_sums(f_ref, planes, links_ref, geo_ref, sums_ref, with_absorbed):
    sums_ref[...] = jnp.zeros_like(sums_ref)

    def cell(g, _):
        for k in range(FACES):

            @pl.when(links_ref[k, g] == WALL_LINK)
            def _():
                v0, v1, v2 = face_coefficients(geo_ref, k, g)
                first = splat(geo_ref, FIRST, g)
                base = []
                for t in range(TILES):
                    xb, xc = tile_nodes(t)
                    base.append(v1 * xb + v2 * xc)
                if with_absorbed:
                    wt = splat(geo_ref, WT, g)
                    shape = wall_tiles(wt)

                def plane(a, acc):
                    out, back = acc
                    xa = first + a.astype(F32) * H
                    sa = v0 * xa
                    if with_absorbed:
                        wa = jnp.exp(-0.5 * xa * xa / wt)
                    for t in range(TILES):
                        s = sa + base[t]
                        f = f_ref[g, at_rows((a * TILES + t) * SUB), :]
                        out = out + jnp.maximum(s, 0.0) * f
                        if with_absorbed:
                            back = back + jnp.maximum(-s, 0.0) * (wa * shape[t])
                    return out, back

                zero = jnp.zeros((SUB, LANES), F32)
                out, back = lax.fori_loop(0, planes, plane, (zero, zero), unroll=2)
                at = at_rows(g * SUB)
                sums_ref[k, at, :] = out
                if with_absorbed:
                    sums_ref[FACES + k, at, :] = back

        return 0

    lax.fori_loop(0, SUB, cell, 0)


def sums_kernel(with_absorbed, links_ref, geo_in, f_ref, sums_out, geo_ref, parts_ref, face_ref):
    planes = f_ref.shape[1] // CHUNKS
    unpack_geo(geo_in, geo_ref)
    first = geo_ref[FIRST]
    y = polynomial_sums(f_ref, planes, parts_ref)
    packed = pack_sums(finish_polynomials(y, first, planes), 0)
    wall_sums(f_ref, planes, links_ref, geo_ref, face_ref, with_absorbed)
    faces = 2 * FACES if with_absorbed else FACES
    sums_out[...] = packed + pack_sums([over_sublanes(face_ref, k) for k in range(faces)], EMIT)


def spec(space):
    return pl.BlockSpec(memory_space=space)


def array(*shape):
    return jax.ShapeDtypeStruct(shape, F32)


def params():
    return pltpu.CompilerParams(vmem_limit_bytes=VMEM_LIMIT)


def local_sums(with_absorbed, links, geo, f):
    return pl.pallas_call(
        functools.partial(sums_kernel, with_absorbed),
        in_specs=[spec(pltpu.SMEM), spec(pltpu.VMEM), spec(pltpu.VMEM)],
        out_specs=spec(pltpu.VMEM),
        out_shape=array(SUB, LANES),
        scratch_shapes=[
            pltpu.VMEM((GEO, SUB, LANES), F32),
            pltpu.VMEM((10, SUB * SUB, LANES), F32),
            pltpu.VMEM(((2 if with_absorbed else 1) * FACES, SUB * SUB, LANES), F32),
        ],
        compiler_params=params(),
        name="local_sums",
    )(links, geo, f)


SPLIT_PARTS = 4


def split_kernel(native_hbm, f_ref, up_ref, down_ref, native_ref, sems):
    rows = native_ref.shape[0]
    part = rows // SPLIT_PARTS
    copies = [
        pltpu.make_async_copy(
            native_hbm.at[pl.ds(i * part, part)], native_ref.at[pl.ds(i * part, part)], sems.at[i]
        )
        for i in range(SPLIT_PARTS)
    ]
    for c in copies:
        c.start()
    groups = part // (SUB * SUB)

    for i, c in enumerate(copies):
        c.wait()

        def group(j, _):
            for g in range(SUB):
                x = native_ref[pl.ds(j * SUB * SUB + g, SUB, stride=SUB), :]
                at = at_rows(j * SUB)
                f_ref[g, at, :] = x
                if g < REACH:
                    down_ref[g, at, :] = x
                if g >= SUB - REACH:
                    up_ref[g - (SUB - REACH), at, :] = x
            return 0

        lax.fori_loop(i * groups, (i + 1) * groups, group, 0, unroll=2)


def split_profile(native):
    rows = native.shape[0] // SUB
    return pl.pallas_call(
        split_kernel,
        in_specs=[spec(pltpu.HBM)],
        out_specs=[spec(pltpu.VMEM)] * 3,
        out_shape=[array(SUB, rows, LANES), array(REACH, rows, LANES), array(REACH, rows, LANES)],
        scratch_shapes=[pltpu.VMEM((SUB * rows, LANES), F32), pltpu.SemaphoreType.DMA((SPLIT_PARTS,))],
        compiler_params=params(),
        name="split_profile",
    )(native)


def geometry_kernel(links_ref, geo_in, outflow_ref, pairs_ref, geo_ref):
    rows = outflow_ref.shape[1]
    planes = rows // CHUNKS
    unpack_geo(geo_in, geo_ref)
    first = splat(geo_ref, FIRST, 0)

    def clear(j, _):
        for p in range(pairs_ref.shape[0]):
            pairs_ref[p, at_rows(j * SUB), :] = jnp.zeros((SUB, LANES), F32)
        return 0

    lax.fori_loop(0, rows // SUB, clear, 0)

    def cell(g, _):
        scale = TIME_STEP / splat(geo_ref, VOL, g)
        v = [[scale * x for x in face_coefficients(geo_ref, k, g)] for k in range(FACES)]
        for t in range(TILES):
            xb, xc = tile_nodes(t)
            base = [v[k][1] * xb + v[k][2] * xc for k in range(FACES)]

            def plane(a, _):
                xa = first + a.astype(F32) * H
                acc = None
                for k in range(FACES):
                    term = jnp.maximum(v[k][0] * xa + base[k], 0.0)
                    acc = term if acc is None else acc + term
                outflow_ref[g, at_rows((a * TILES + t) * SUB), :] = acc
                return 0

            lax.fori_loop(0, planes, plane, 0, unroll=4)

        edge = g - (SUB - REACH)
        for k in range(FACES):
            j = links_ref[k, g]
            is_before = jnp.logical_and(j < 0, j != WALL_LINK)

            @pl.when(jnp.logical_or(is_before, j >= SUB))
            def _():
                r = j + REACH
                before = g * REACH - g * (g - 1) // 2 + r - g
                after = len(BEFORE_PAIRS) + edge * (edge + 1) // 2 + j - SUB
                at_pair = jnp.where(is_before, before, after)
                for t in range(TILES):
                    xb, xc = tile_nodes(t)
                    base = v[k][1] * xb + v[k][2] * xc

                    def plane(a, _):
                        xa = first + a.astype(F32) * H
                        at = at_rows((a * TILES + t) * SUB)
                        weight = jnp.maximum(-(v[k][0] * xa + base), 0.0)
                        pairs_ref[at_pair, at, :] = pairs_ref[at_pair, at, :] + weight
                        return 0

                    lax.fori_loop(0, planes, plane, 0, unroll=4)

        return 0

    lax.fori_loop(0, SUB, cell, 0)


def geometry(links, geo, rows):
    return pl.pallas_call(
        geometry_kernel,
        in_specs=[spec(pltpu.SMEM), spec(pltpu.VMEM)],
        out_specs=[spec(pltpu.VMEM)] * 2,
        out_shape=[array(SUB, rows, LANES), array(2 * len(BEFORE_PAIRS), rows, LANES)],
        scratch_shapes=[pltpu.VMEM((GEO, SUB, LANES), F32)],
        compiler_params=params(),
        name="geometry",
    )(links, geo)


def gather_sums(tile):
    size = lax.axis_size("vel")
    if size not in (2, 4):
        return [lax.psum(tile, "vel")]
    others = [lax.ppermute(tile, "vel", [(i, i ^ s) for i in range(size)]) for s in range(1, size)]
    return [tile, *others]


def add_tiles(refs):
    tiles = [r[...] for r in refs]
    while len(tiles) > 1:
        tiles = [tiles[i] + tiles[i + 1] for i in range(0, len(tiles), 2)]
    return tiles[0]


def quantities(tile):
    m = [WEIGHT * column(tile, p) for p in range(13)]
    n = m[0]
    rn = 1.0 / n
    u = [m[1 + i] * rn for i in range(3)]
    uu = u[0] * u[0] + u[1] * u[1] + u[2] * u[2]
    trace = m[4] + m[5] + m[6]
    width = trace - n * uu
    temperature = width * rn * (1.0 / 3.0)
    second = [[m[4], m[7], m[8]], [m[7], m[5], m[9]], [m[8], m[9], m[6]]]
    q = []
    for i in range(3):
        across = u[0] * second[i][0] + u[1] * second[i][1] + u[2] * second[i][2]
        q.append(0.5 * (m[10 + i] - 2.0 * across - u[i] * trace + 2.0 * uu * m[1 + i]))
    return n, u, temperature, q


def macro_kernel(*refs):
    out_ref = refs[-1]
    n, u, temperature, q = quantities(add_tiles(refs[:-1]))
    lane, sub = lane_iota(), sub_iota()
    for i, x in enumerate((n, *u, temperature, *q)):
        row = jnp.sum(jnp.where(lane == sub, x, 0.0), axis=0, keepdims=True)
        out_ref[pl.ds(i, 1), :] = row[:, :SUB]


def macro(tiles):
    return pl.pallas_call(
        macro_kernel,
        in_specs=[spec(pltpu.VMEM)] * len(tiles),
        out_specs=spec(pltpu.VMEM),
        out_shape=array(8, SUB),
        name="macro",
    )(*tiles)


def inner_kernel(last, count, links_ref, geo_in, absorbed_in, *refs):
    sums_refs, (f_ref, outflow_ref, out_ref, sum_out, geo_ref, ta, coef) = refs[:count], refs[count:]
    planes = f_ref.shape[1] // CHUNKS
    unpack_geo(geo_in, geo_ref)
    sums = add_tiles(sums_refs)
    sum_out[...] = sums
    absorbed = sums if absorbed_in is None else absorbed_in[...]
    n, u, temperature, q = quantities(sums)
    rt = 1.0 / temperature
    rate = TIME_STEP * n * temperature / (SHEAR * jnp.exp(POWER * jnp.log(temperature)))
    height = rate * n * rt * jnp.sqrt(rt)
    slope = (1.0 / 3.0) / (5.0 * n * temperature * temperature)
    scale = -TIME_STEP / geo_ref[VOL]
    coef[0] = rate
    coef[1] = rt
    coef[2], coef[3] = u[1], u[2]
    coef[4], coef[5] = slope * q[1], slope * q[2]
    for k in range(FACES):
        wall = geo_ref[WALL + k] > 0.5
        ratio = column(sums, EMIT + k) / jnp.where(wall, column(absorbed, ABSORB + k), 1.0)
        factor = scale * jnp.where(wall, ratio, geo_ref[LOCAL + k])
        for i in range(3):
            coef[6 + FACES * i + k] = factor * geo_ref[FV + FACES * i + k]

    first = geo_ref[FIRST]

    def plane_table(a, _):
        ca = first + a.astype(F32) * H - u[0]
        za = ca * ca * rt
        ta[0, a] = height * jnp.exp(-0.5 * za)
        ta[1, a] = slope * q[0] * ca
        ta[2, a] = za - 5.0
        return 0

    lax.fori_loop(0, planes, plane_table, 0)

    def place(g, tile):
        if last:
            return (pl.ds(tile * SUB * SUB + g, SUB, stride=SUB), slice(None))
        return (g, at_rows(tile * SUB), slice(None))

    def cell(g, _):
        source, weight = [], []
        for k in range(FACES):
            j = links_ref[k, g]
            own = jnp.logical_and(j >= 0, j < SUB)
            source.append(jnp.where(own, j, g))
            weight.append([splat(coef, 6 + FACES * i + k, g) * splat(geo_ref, LOCAL + k, g) for i in range(3)])
        keep = 1.0 - splat(coef, 0, g)
        rtg = splat(coef, 1, g)
        ub, uc = splat(coef, 2, g), splat(coef, 3, g)
        qb, qc = splat(coef, 4, g), splat(coef, 5, g)
        x0 = splat(geo_ref, FIRST, g)
        for pair in range(TILES // 2):
            base, bell, heat, zz = [], [], [], []
            for t in (2 * pair, 2 * pair + 1):
                xb, xc = tile_nodes(t)
                cb, cc = xb - ub, xc - uc
                z = (cb * cb + cc * cc) * rtg
                bell.append(jnp.exp(-0.5 * z))
                heat.append(cb * qb + cc * qc)
                zz.append(z)
                base.append([weight[k][1] * xb + weight[k][2] * xc for k in range(FACES)])

            def plane(a, _):
                xa = x0 + a.astype(F32) * H
                height_a, heat_a, z_a = [
                    jnp.broadcast_to(ta[i, a, pl.ds(g, 1), :], (SUB, LANES)) for i in range(3)
                ]
                sa = [weight[k][0] * xa for k in range(FACES)]
                for i in range(2):
                    tile = a * TILES + 2 * pair + i
                    at = at_rows(tile * SUB)
                    acc = f_ref[g, at, :] * (keep - outflow_ref[g, at, :])
                    for k in range(FACES):
                        acc = acc + jnp.maximum(sa[k] + base[i][k], 0.0) * f_ref[source[k], at, :]
                    target = (height_a * bell[i]) * (1.0 + (heat_a + heat[i]) * (z_a + zz[i]))
                    out_ref[place(g, tile)] = acc + target
                return 0

            lax.fori_loop(0, planes, plane, 0, unroll=2)

        for k in range(FACES):

            @pl.when(links_ref[k, g] == WALL_LINK)
            def _():
                wt = splat(geo_ref, WT, g)
                shape = wall_tiles(wt)
                v0, v1, v2 = [splat(coef, 6 + FACES * i + k, g) for i in range(3)]
                base = []
                for t in range(TILES):
                    xb, xc = tile_nodes(t)
                    base.append(v1 * xb + v2 * xc)

                def plane(a, _):
                    xa = x0 + a.astype(F32) * H
                    wa = jnp.exp(-0.5 * xa * xa / wt)
                    sa = v0 * xa
                    for t in range(TILES):
                        where = place(g, a * TILES + t)
                        out_ref[where] = out_ref[where] + jnp.maximum(sa + base[t], 0.0) * (wa * shape[t])
                    return 0

                lax.fori_loop(0, planes, plane, 0, unroll=2)

        return 0

    lax.fori_loop(0, SUB, cell, 0)


def inner(last, links, geo, absorbed, tiles, f, outflow):
    rows = f.shape[1]
    vmem = spec(pltpu.VMEM)
    given = [links, geo] + ([] if absorbed is None else [absorbed]) + list(tiles) + [f, outflow]

    def kernel(links_ref, geo_in, *refs):
        if absorbed is None:
            inner_kernel(last, len(tiles), links_ref, geo_in, None, *refs)
        else:
            inner_kernel(last, len(tiles), links_ref, geo_in, *refs)

    return pl.pallas_call(
        kernel,
        in_specs=[spec(pltpu.SMEM)] + [vmem] * (len(given) - 1),
        out_specs=[vmem] * 2,
        out_shape=[
            array(SUB * rows, LANES) if last else array(SUB, rows, LANES),
            array(SUB, LANES),
        ],
        scratch_shapes=[
            pltpu.VMEM((GEO, SUB, LANES), F32),
            pltpu.VMEM((3, rows // CHUNKS, SUB, LANES), F32),
            pltpu.VMEM((6 + 3 * FACES, SUB, LANES), F32),
        ],
        compiler_params=params(),
        name="inner",
    )(*given)


def halo_terms(pairs_ref, before_ref, after_ref, at):
    count = len(BEFORE_PAIRS)
    low, high = [None] * REACH, [None] * REACH
    rows = [before_ref[r, at, :] for r in range(REACH)]
    for p, (g, r) in enumerate(BEFORE_PAIRS):
        term = pairs_ref[p, at, :] * rows[r]
        low[g] = term if low[g] is None else low[g] + term
    rows = [after_ref[r, at, :] for r in range(REACH)]
    p = count
    for e in range(REACH):
        for r in range(e + 1):
            term = pairs_ref[p, at, :] * rows[r]
            high[e] = term if high[e] is None else high[e] + term
            p += 1
    return low, high


def edge_kernel(pairs_ref, before_ref, after_ref, part_ref, f_ref, up_ref, down_ref):
    def group(j, _):
        at = at_rows(j * SUB)
        low, high = halo_terms(pairs_ref, before_ref, after_ref, at)
        for g in range(SUB):
            x = part_ref[g, at, :]
            if g < REACH:
                x = x + low[g]
                down_ref[g, at, :] = x
            e = g - (SUB - REACH)
            if e >= 0:
                x = x + high[e]
                up_ref[e, at, :] = x
            f_ref[g, at, :] = x
        return 0

    lax.fori_loop(0, part_ref.shape[1] // SUB, group, 0)


def edge(pairs, before, after, part):
    rows = part.shape[1]
    return pl.pallas_call(
        edge_kernel,
        in_specs=[spec(pltpu.VMEM)] * 4,
        out_specs=[spec(pltpu.VMEM)] * 3,
        out_shape=[array(SUB, rows, LANES), array(REACH, rows, LANES), array(REACH, rows, LANES)],
        compiler_params=params(),
        name="edge",
    )(pairs, before, after, part)


def last_edge_kernel(geo_in, pairs_ref, before_ref, after_ref, part_ref, out_hbm, sums_out, native_ref, sems):
    rows = part_ref.shape[0] // SUB
    planes = rows // CHUNKS
    tiles = rows // SUB
    part = tiles // LAST_PARTS
    copies = []
    for i in range(LAST_PARTS):

        def group(j, _):
            at = at_rows(j * SUB)
            low, high = halo_terms(pairs_ref, before_ref, after_ref, at)
            terms = low + [None] * (SUB - 2 * REACH) + high
            for g in range(SUB):
                where = (pl.ds(j * SUB * SUB + g, SUB, stride=SUB), slice(None))
                x = part_ref[where]
                native_ref[where] = x if terms[g] is None else x + terms[g]
            return 0

        lax.fori_loop(i * part, (i + 1) * part, group, 0)
        at = pl.ds(i * part * SUB * SUB, part * SUB * SUB)
        copies.append(pltpu.make_async_copy(native_ref.at[at], out_hbm.at[at], sems.at[i]))
        copies[-1].start()
    y = native_polynomial_sums(native_ref, planes)
    sums_out[...] = pack_sums(finish_polynomials(y, column(geo_in[...], FIRST), planes), 0)
    for c in copies:
        c.wait()


LAST_PARTS = 4


def last_edge(geo, pairs, before, after, part):
    return pl.pallas_call(
        last_edge_kernel,
        in_specs=[spec(pltpu.VMEM)] * 5,
        out_specs=[spec(pltpu.HBM), spec(pltpu.VMEM)],
        out_shape=[array(*part.shape), array(SUB, LANES)],
        scratch_shapes=[pltpu.VMEM(part.shape, F32), pltpu.SemaphoreType.DMA((LAST_PARTS,))],
        compiler_params=params(),
        name="last_edge",
    )(geo, pairs, before, after, part)


def exchange(up, down):
    size = lax.axis_size("space")
    forward = [(i, i + 1) for i in range(size - 1)]
    backward = [(i + 1, i) for i in range(size - 1)]
    return lax.ppermute(up, "space", forward), lax.ppermute(down, "space", backward)


def per_device(particle_profile, neighbors, face_vectors, volumes, wall_temp):
    cells, points = particle_profile.shape
    rows = points // LANES
    plane_count = NV // lax.axis_size("vel")
    native = particle_profile.reshape(cells, rows, LANES).transpose(1, 0, 2).reshape(cells * rows, LANES)
    wall = neighbors < 0
    links = jnp.where(wall, WALL_LINK, neighbors - lax.axis_index("space") * cells)
    own = (links >= 0) & (links < cells)
    first = -SPEED_LIMIT + ((lax.axis_index("vel") * plane_count).astype(F32) + 0.5) * H
    geo = jnp.concatenate(
        [
            face_vectors.reshape(3 * FACES, cells),
            volumes[None],
            wall_temp[None],
            wall.astype(F32),
            own.astype(F32),
            jnp.full((1, cells), first, F32),
        ]
    )
    geo = jnp.pad(geo.T, ((0, 0), (0, LANES - GEO)))
    f, up, down = split_profile(pltpu.with_memory_space_constraint(native, pltpu.HBM))
    before, after = exchange(up, down)
    tiles = gather_sums(local_sums(True, links, geo, f))
    outflow, pairs = geometry(links, geo, rows)
    part, absorbed = inner(False, links, geo, None, tiles, f, outflow)
    f, up, down = edge(pairs, before, after, part)
    before, after = exchange(up, down)
    tiles = gather_sums(local_sums(False, links, geo, f))
    part, _ = inner(True, links, geo, absorbed, tiles, f, outflow)
    native, sums = last_edge(geo, pairs, before, after, part)
    macro_quantities = macro(gather_sums(sums))
    evolved = native.reshape(rows, cells, LANES).transpose(1, 0, 2).reshape(cells, points)
    return evolved, macro_quantities


def solution(mesh):
    return jax.shard_map(
        per_device,
        mesh=mesh,
        in_specs=(
            P("space", "vel"),
            P(None, "space"),
            P(None, None, "space"),
            P("space"),
            P("space"),
        ),
        out_specs=(P("space", "vel"), P(None, "space")),
        check_vma=False,
    )
```

time: 89.1 us -> 69 us (0.77); the launches traced: 87.4 us -> 68.4 us
  blocking collectives: 29.3 us -> 0 us
  starting transfers between devices: 12.9 us -> 26.2 us
  local copies, waits for them, and re-layouts: 10.9 us -> 1.66 us
  Pallas kernels: 27.2 us -> 34.3 us
    psum x3 -> x0, blocking collectives: 29.3 us -> none  [the longest x1 12 us: per_device(): sums0 = lax.psum(sums0, 'vel')]
    ppermute x0 -> x9, starting transfers between devices: none -> 13.3 us  [gather_sums(): lax.ppermute(tile, 'vel', [(i, i ^ s) for i in range(size)])]
    unnamed x23 -> x17, local copies, waits for them, and re-layouts: 10.7 us -> 1.24 us
    pallas_call x5 -> x9, Pallas kernels: 27.2 us -> 34.3 us  [the longest x2 13.1 us: inner(): pl.pallas_call(kernel, in_specs=[spec(pltpu.SMEM)] + [vmem] * (len(given)...]
    ppermute x0 -> x9, waiting for transfers between devices: none -> 5.35 us  [gather_sums(): lax.ppermute(tile, 'vel', [(i, i ^ s) for i in range(size)])]
    ppermute x2, waiting for transfers between devices: 3.28 us -> 0.01 us  [exchange(): lax.ppermute(up, 'space', forward)]
    ppermute x2, waiting for transfers between devices: 2.9 us -> 0.01 us  [exchange(): lax.ppermute(down, 'space', backward)]
  transfers between devices with their start and end apart: 4 -> 13, of which waited for: 2 -> 4; matrix products, arithmetic and copies ran while one was open for 1% -> 1% of each run, Pallas kernels for 7% -> 38%
where the time goes in v1:
time: 69 us; the launch traced here: 68.4 us
  Pallas kernels  34.3 us (50%)
  starting transfers between devices  26.2 us (38%)
  waiting for transfers between devices  5.36 us (8%)
  local copies, waits for them, and re-layouts  1.66 us (2%)
  between operations  0.82 us (1%)
    ppermute x9, starting transfers between devices, gather_sums(): lax.ppermute(tile, 'vel', [(i, i ^ s) for i in range(size)])  13.3 us
    pallas_call x2, Pallas kernels, inner(): pl.pallas_call(kernel, in_specs=[spec(pltpu.SMEM)] + [vmem] * (len(given)...  13.1 us
    ppermute x2, starting transfers between devices, exchange(): lax.ppermute(down, 'space', backward)  9.08 us
    pallas_call x1, Pallas kernels, geometry(): pl.pallas_call(geometry_kernel, in_specs=[spec(pltpu.SMEM), spec(pltpu.VM...  7.57 us
    ppermute x9, waiting for transfers between devices, gather_sums(): lax.ppermute(tile, 'vel', [(i, i ^ s) for i in range(size)])  5.35 us
    pallas_call x2, Pallas kernels, local_sums(): pl.pallas_call(functools.partial(sums_kernel, with_absorbed), in_specs=[s...  4.99 us
    ppermute x2, starting transfers between devices, exchange(): lax.ppermute(up, 'space', forward)  3.84 us
    pallas_call x1, Pallas kernels, split_profile(): pl.pallas_call(split_kernel, in_specs=[spec(pltpu.HBM)], out_specs=[spec(...  2.84 us
  transfers between devices with their start and end apart: 13, of which 4 were waited for; matrix products, arithmetic and copies ran while one was open for 1% of the time, Pallas kernels for 38%

profile of v1, /device:TPU:4, one launch (start us, length us, event | category | flops | bytes accessed | tf_op | source)
XLA Modules:
  0.0 68.4 jit_solution(12664340837775751598)
XLA Ops:
  0.6 0.0 copy-start.5
  0.6 0.0 copy-start.6
  0.7 0.0 copy-start.7
  0.7 0.0 copy-start.1
  0.7 2.8 %split_profile.1 = (f32[8,512,128]{2,1,0:T(8,128)S(1)}, f32[3,512,128]{2,1,0:T(8,128)}, f32[3,512,128]{2,1,0:T(8,128)}) custom-call(f32[4096,128]{1,0:T(8,128)} %bitcast.13), custom_call_target="tpu_custom_call" | custom-call | tf_op jit(solution)/shard_map/split_profile/pallas_call | solution.py:326
  3.5 1.9 %collective-permute-start = (f32[3,512,128]{2,1,0:T(8,128)}, f32[3,512,128]{2,1,0:T(8,128)S(1)}, u32[]{:S(2)}, u32[]{:S(2)}) collective-permute-start(f32[3,512,128]{2,1,0:T(8,128)} %get-tuple-element.16), channel_id=1, source_target_pairs={{0,4},{4,8},{8,12},{12,16},{16,20},{20,24},{24,28},{1,5},{5,9},{9,... | collective-permute-start | bytes 2359304 | tf_op jit(solution)/shard_map/ppermute | solution.py:694
  5.4 4.5 %collective-permute-start.1 = (f32[3,512,128]{2,1,0:T(8,128)}, f32[3,512,128]{2,1,0:T(8,128)}, u32[]{:S(2)}, u32[]{:S(2)}) collective-permute-start(f32[3,512,128]{2,1,0:T(8,128)} %get-tuple-element.17), channel_id=1, source_target_pairs={{4,0},{8,4},{12,8},{16,12},{20,16},{24,20},{28,24},{5,1},{9,5},{13... | collective-permute-start | bytes 2359304 | tf_op jit(solution)/shard_map/ppermute | solution.py:694
  10.0 0.1 copy.18
  10.1 0.1 copy.20
  10.2 0.1 copy.21
  10.3 0.1 copy.22.links_ref
  10.4 0.1 copy.27
  10.4 0.1 concatenate.3
  10.5 2.6 %local_sums.2.refs_0_ = f32[8,128]{1,0:T(8,128)S(1)} custom-call(s32[6,8]{1,0:T(8,128)S(1)} %copy.22.links_ref, f32[8,128]{1,0:T(8,128)S(1)} %pad.4.geo_in, f32[8,512,128]{2,1,0:T(8,128)S(1)} %get-tuple-element.18.f_ref.refs_4_), custom_call_target="tpu_custom_call" | custom-call | tf_op jit(solution)/shard_map/local_sums/pallas_call | solution.py:276
  13.2 3.7 %collective-permute-start.4 = (f32[8,128]{1,0:T(8,128)S(1)}, f32[8,128]{1,0:T(8,128)S(1)}, u32[]{:S(2)}, u32[]{:S(2)}) collective-permute-start(f32[8,128]{1,0:T(8,128)S(1)} %local_sums.2.refs_0_), channel_id=1, source_target_pairs={{0,3},{1,2},{2,1},{3,0},{4,7},{5,6},{6,5},{7,4},{8,11},{9,10},{10,... | collective-permute-start | bytes 12296 | tf_op jit(solution)/shard_map/ppermute | solution.py:413
  16.8 0.0 collective-permute-start.3
  16.8 0.8 %collective-permute-start.2 = (f32[8,128]{1,0:T(8,128)S(1)}, f32[8,128]{1,0:T(8,128)S(1)}, u32[]{:S(2)}, u32[]{:S(2)}) collective-permute-start(f32[8,128]{1,0:T(8,128)S(1)} %local_sums.2.refs_0_), channel_id=1, source_target_pairs={{0,1},{1,0},{2,3},{3,2},{4,5},{5,4},{6,7},{7,6},{8,9},{9,8},{10,11... | collective-permute-start | bytes 12296 | tf_op jit(solution)/shard_map/ppermute | solution.py:413
  17.6 7.6 %geometry.1 = (f32[8,512,128]{2,1,0:T(8,128)S(1)}, f32[12,512,128]{2,1,0:T(8,128)S(1)}) custom-call(s32[6,8]{1,0:T(8,128)S(1)} %copy.22.links_ref, f32[8,128]{1,0:T(8,128)S(1)} %pad.4.geo_in), custom_call_target="tpu_custom_call" | custom-call | tf_op jit(solution)/shard_map/geometry/pallas_call | solution.py:398
  25.2 0.0 collective-permute-done.4.refs_3_
  25.2 0.0 collective-permute-done.3.refs_2_
  25.2 0.0 collective-permute-done.2.refs_1_
  25.2 6.2 %inner.2 = (f32[8,512,128]{2,1,0:T(8,128)S(1)}, f32[8,128]{1,0:T(8,128)S(1)}) custom-call(s32[6,8]{1,0:T(8,128)S(1)} %copy.22.links_ref, f32[8,128]{1,0:T(8,128)S(1)} %pad.4.geo_in, f32[8,128]{1,0:T(8,128)S(1)} %local_sums.2.refs_0_, f32[8,128]{1,0:T(8,128)S(1)} %collective-permute-done.2.refs_1_, f32[8,128]{1,0:T(8,128)S(1)} %collective-permute-done.3.refs_2_, ...), custom_call_target="tpu_custom_call" | custom-call | tf_op jit(solution)/shard_map/inner/pallas_call | solution.py:581
  31.4 0.0 collective-permute-done.before_ref
  31.4 0.0 collective-permute-done.1.after_ref
  31.4 2.3 %edge.1 = (f32[8,512,128]{2,1,0:T(8,128)S(1)}, f32[3,512,128]{2,1,0:T(8,128)S(1)}, f32[3,512,128]{2,1,0:T(8,128)S(1)}) custom-call(f32[12,512,128]{2,1,0:T(8,128)S(1)} %get-tuple-element.15.pairs_ref, f32[3,512,128]{2,1,0:T(8,128)S(1)} %collective-permute-done.before_ref, f32[3,512,128]{2,1,0:T(8,128)} %collective-permute-done.1.after_ref, ...), custom_call_target="tpu_custom_call" | custom-call | tf_op jit(solution)/shard_map/edge/pallas_call | solution.py:637
  33.7 1.9 %collective-permute-start.5 = (f32[3,512,128]{2,1,0:T(8,128)S(1)}, f32[3,512,128]{2,1,0:T(8,128)S(1)}, u32[]{:S(2)}, u32[]{:S(2)}) collective-permute-start(f32[3,512,128]{2,1,0:T(8,128)S(1)} %get-tuple-element.21), channel_id=1, source_target_pairs={{0,4},{4,8},{8,12},{12,16},{16,20},{20,24},{24,28},{1,5},{5,9},{9,... | collective-permute-start | bytes 2359304 | tf_op jit(solution)/shard_map/ppermute | solution.py:694
  35.7 4.5 %collective-permute-start.6 = (f32[3,512,128]{2,1,0:T(8,128)S(1)}, f32[3,512,128]{2,1,0:T(8,128)S(1)}, u32[]{:S(2)}, u32[]{:S(2)}) collective-permute-start(f32[3,512,128]{2,1,0:T(8,128)S(1)} %get-tuple-element.22), channel_id=1, source_target_pairs={{4,0},{8,4},{12,8},{16,12},{20,16},{24,20},{28,24},{5,1},{9,5},{13... | collective-permute-start | bytes 2359304 | tf_op jit(solution)/shard_map/ppermute | solution.py:694
  40.2 2.3 %local_sums.3.refs_1_ = f32[8,128]{1,0:T(8,128)S(1)} custom-call(s32[6,8]{1,0:T(8,128)S(1)} %copy.22.links_ref, f32[8,128]{1,0:T(8,128)S(1)} %pad.4.geo_in, f32[8,512,128]{2,1,0:T(8,128)S(1)} %get-tuple-element.24.f_ref.refs_5_), custom_call_target="tpu_custom_call" | custom-call | tf_op jit(solution)/shard_map/local_sums/pallas_call | solution.py:276
  42.6 3.6 %collective-permute-start.9 = (f32[8,128]{1,0:T(8,128)S(1)}, f32[8,128]{1,0:T(8,128)S(1)}, u32[]{:S(2)}, u32[]{:S(2)}) collective-permute-start(f32[8,128]{1,0:T(8,128)S(1)} %local_sums.3.refs_1_), channel_id=1, source_target_pairs={{0,3},{1,2},{2,1},{3,0},{4,7},{5,6},{6,5},{7,4},{8,11},{9,10},{10,... | collective-permute-start | bytes 12296 | tf_op jit(solution)/shard_map/ppermute | solution.py:413
  46.2 0.0 collective-permute-start.8
  46.2 0.8 %collective-permute-start.7 = (f32[8,128]{1,0:T(8,128)S(1)}, f32[8,128]{1,0:T(8,128)S(1)}, u32[]{:S(2)}, u32[]{:S(2)}) collective-permute-start(f32[8,128]{1,0:T(8,128)S(1)} %local_sums.3.refs_1_), channel_id=1, source_target_pairs={{0,1},{1,0},{2,3},{3,2},{4,5},{5,4},{6,7},{7,6},{8,9},{9,8},{10,11... | collective-permute-start | bytes 12296 | tf_op jit(solution)/shard_map/ppermute | solution.py:413
  47.0 1.0 %collective-permute-done.9.refs_4_ = f32[8,128]{1,0:T(8,128)S(1)} collective-permute-done((f32[8,128]{1,0:T(8,128)S(1)}, f32[8,128]{1,0:T(8,128)S(1)}, u32[]{:S(2)}, u32[]{:S(2)}) %collective-permute-start.9) | collective-permute-done | bytes 4128 | tf_op jit(solution)/shard_map/ppermute | solution.py:413
  48.0 2.7 %collective-permute-done.8.refs_3_ = f32[8,128]{1,0:T(8,128)S(1)} collective-permute-done((f32[8,128]{1,0:T(8,128)S(1)}, f32[8,128]{1,0:T(8,128)S(1)}, u32[]{:S(2)}, u32[]{:S(2)}) %collective-permute-start.8) | collective-permute-done | bytes 4128 | tf_op jit(solution)/shard_map/ppermute | solution.py:413
  50.7 0.0 collective-permute-done.7.refs_2_
  50.7 6.9 %inner.3 = (f32[4096,128]{1,0:T(8,128)S(1)}, f32[8,128]{1,0:T(8,128)}) custom-call(s32[6,8]{1,0:T(8,128)S(1)} %copy.22.links_ref, f32[8,128]{1,0:T(8,128)S(1)} %pad.4.geo_in, f32[8,128]{1,0:T(8,128)S(1)} %get-tuple-element.23.refs_0_, f32[8,128]{1,0:T(8,128)S(1)} %local_sums.3.refs_1_, f32[8,128]{1,0:T(8,128)S(1)} %collective-permute-done.7.refs_2_, ...), custom_call_target="tpu_custom_call" | custom-call | tf_op jit(solution)/shard_map/inner/pallas_call | solution.py:581
  57.6 0.0 collective-permute-done.5.before_ref
  57.6 0.0 collective-permute-done.6.after_ref
  57.6 2.1 %last_edge.1 = (f32[4096,128]{1,0:T(8,128)}, f32[8,128]{1,0:T(8,128)S(1)}) custom-call(f32[8,128]{1,0:T(8,128)S(1)} %pad.4.geo_in, f32[12,512,128]{2,1,0:T(8,128)S(1)} %get-tuple-element.15.pairs_ref, f32[3,512,128]{2,1,0:T(8,128)S(1)} %collective-permute-done.5.before_ref, f32[3,512,128]{2,1,0:T(8,128)S(1)} %collective-permute-done.6.after_ref, ...), custom_call_target="tpu_custom_call" | custom-call | tf_op jit(solution)/shard_map/last_edge/pallas_call | solution.py:679
  59.8 1.5 %collective-permute-start.12 = (f32[8,128]{1,0:T(8,128)S(1)}, f32[8,128]{1,0:T(8,128)S(1)}, u32[]{:S(2)}, u32[]{:S(2)}) collective-permute-start(f32[8,128]{1,0:T(8,128)S(1)} %get-tuple-element.27.refs_0_), channel_id=1, source_target_pairs={{0,3},{1,2},{2,1},{3,0},{4,7},{5,6},{6,5},{7,4},{8,11},{9,10},{10,... | collective-permute-start | bytes 12296 | tf_op jit(solution)/shard_map/ppermute | solution.py:413
  61.3 0.6 collective-permute-start.11
  62.0 2.3 %collective-permute-start.10 = (f32[8,128]{1,0:T(8,128)S(1)}, f32[8,128]{1,0:T(8,128)S(1)}, u32[]{:S(2)}, u32[]{:S(2)}) collective-permute-start(f32[8,128]{1,0:T(8,128)S(1)} %get-tuple-element.27.refs_0_), channel_id=1, source_target_pairs={{0,1},{1,0},{2,3},{3,2},{4,5},{5,4},{6,7},{7,6},{8,9},{9,8},{10,11... | collective-permute-start | bytes 12296 | tf_op jit(solution)/shard_map/ppermute | solution.py:413
  64.2 1.0 %collective-permute-done.12.refs_3_ = f32[8,128]{1,0:T(8,128)S(1)} collective-permute-done((f32[8,128]{1,0:T(8,128)S(1)}, f32[8,128]{1,0:T(8,128)S(1)}, u32[]{:S(2)}, u32[]{:S(2)}) %collective-permute-start.12) | collective-permute-done | bytes 4128 | tf_op jit(solution)/shard_map/ppermute | solution.py:413
  65.3 0.6 collective-permute-done.11.refs_2_
  65.8 0.0 collective-permute-done.10.refs_1_
  65.9 0.0 copy-done
  65.9 0.5 copy-done.3
  66.4 0.6 copy-done.4
  67.0 1.4 %macro.1 = f32[8,8]{1,0:T(8,128)} custom-call(f32[8,128]{1,0:T(8,128)} %copy-done, f32[8,128]{1,0:T(8,128)} %copy-done.4, f32[8,128]{1,0:T(8,128)} %copy-done.3, f32[8,128]{1,0:T(8,128)} %copy-done.2), custom_call_target="tpu_custom_call" | custom-call | tf_op jit(solution)/shard_map/macro/pallas_call | solution.py:451
  (13 shorter events, 0.0 us)
Async XLA Ops:
  0.6 9.4 %copy-start.5 = (s32[6,8]{1,0:T(8,128)S(1)}, s32[6,8]{1,0:T(8,128)}, u32[]{:S(2)}) copy-start(s32[6,8]{1,0:T(8,128)} %param.6) | copy-start | bytes 580
  0.6 9.5 %copy-start.6 = (f32[8]{0:T(128)S(1)}, f32[8]{0:T(128)}, u32[]{:S(2)}) copy-start(f32[8]{0:T(128)} %param.8) | copy-start | bytes 100
  0.7 9.5 %copy-start.7 = (f32[8]{0:T(128)S(1)}, f32[8]{0:T(128)}, u32[]{:S(2)}) copy-start(f32[8]{0:T(128)} %param.9) | copy-start | bytes 100
  0.7 9.7 %copy-start.1 = (f32[3,6,8]{2,1,0:T(8,128)S(1)}, f32[3,6,8]{2,1,0:T(8,128)}, u32[]{:S(2)}) copy-start(f32[3,6,8]{2,1,0:T(8,128)} %param.7) | copy-start | bytes 1732
  3.5 27.9 %collective-permute-start = (f32[3,512,128]{2,1,0:T(8,128)}, f32[3,512,128]{2,1,0:T(8,128)S(1)}, u32[]{:S(2)}, u32[]{:S(2)}) collective-permute-start(f32[3,512,128]{2,1,0:T(8,128)} %get-tuple-element.16), channel_id=1, source_target_pairs={{0,4},{4,8},{8,12},{12,16},{16,20},{20,24},{24,28},{1,5},{5,9},{9,... | collective-permute-start | bytes 2359304 | tf_op jit(solution)/shard_map/ppermute | solution.py:694
  5.4 26.0 %collective-permute-start.1 = (f32[3,512,128]{2,1,0:T(8,128)}, f32[3,512,128]{2,1,0:T(8,128)}, u32[]{:S(2)}, u32[]{:S(2)}) collective-permute-start(f32[3,512,128]{2,1,0:T(8,128)} %get-tuple-element.17), channel_id=1, source_target_pairs={{4,0},{8,4},{12,8},{16,12},{20,16},{24,20},{28,24},{5,1},{9,5},{13... | collective-permute-start | bytes 2359304 | tf_op jit(solution)/shard_map/ppermute | solution.py:694
  13.2 12.0 %collective-permute-start.4 = (f32[8,128]{1,0:T(8,128)S(1)}, f32[8,128]{1,0:T(8,128)S(1)}, u32[]{:S(2)}, u32[]{:S(2)}) collective-permute-start(f32[8,128]{1,0:T(8,128)S(1)} %local_sums.2.refs_0_), channel_id=1, source_target_pairs={{0,3},{1,2},{2,1},{3,0},{4,7},{5,6},{6,5},{7,4},{8,11},{9,10},{10,... | collective-permute-start | bytes 12296 | tf_op jit(solution)/shard_map/ppermute | solution.py:413
  16.8 8.4 %collective-permute-start.3 = (f32[8,128]{1,0:T(8,128)S(1)}, f32[8,128]{1,0:T(8,128)S(1)}, u32[]{:S(2)}, u32[]{:S(2)}) collective-permute-start(f32[8,128]{1,0:T(8,128)S(1)} %local_sums.2.refs_0_), channel_id=1, source_target_pairs={{0,2},{1,3},{2,0},{3,1},{4,6},{5,7},{6,4},{7,5},{8,10},{9,11},{10,... | collective-permute-start | bytes 12296 | tf_op jit(solution)/shard_map/ppermute | solution.py:413
  16.8 8.4 %collective-permute-start.2 = (f32[8,128]{1,0:T(8,128)S(1)}, f32[8,128]{1,0:T(8,128)S(1)}, u32[]{:S(2)}, u32[]{:S(2)}) collective-permute-start(f32[8,128]{1,0:T(8,128)S(1)} %local_sums.2.refs_0_), channel_id=1, source_target_pairs={{0,1},{1,0},{2,3},{3,2},{4,5},{5,4},{6,7},{7,6},{8,9},{9,8},{10,11... | collective-permute-start | bytes 12296 | tf_op jit(solution)/shard_map/ppermute | solution.py:413
  33.7 23.9 %collective-permute-start.5 = (f32[3,512,128]{2,1,0:T(8,128)S(1)}, f32[3,512,128]{2,1,0:T(8,128)S(1)}, u32[]{:S(2)}, u32[]{:S(2)}) collective-permute-start(f32[3,512,128]{2,1,0:T(8,128)S(1)} %get-tuple-element.21), channel_id=1, source_target_pairs={{0,4},{4,8},{8,12},{12,16},{16,20},{20,24},{24,28},{1,5},{5,9},{9,... | collective-permute-start | bytes 2359304 | tf_op jit(solution)/shard_map/ppermute | solution.py:694
  35.7 22.0 %collective-permute-start.6 = (f32[3,512,128]{2,1,0:T(8,128)S(1)}, f32[3,512,128]{2,1,0:T(8,128)S(1)}, u32[]{:S(2)}, u32[]{:S(2)}) collective-permute-start(f32[3,512,128]{2,1,0:T(8,128)S(1)} %get-tuple-element.22), channel_id=1, source_target_pairs={{4,0},{8,4},{12,8},{16,12},{20,16},{24,20},{28,24},{5,1},{9,5},{13... | collective-permute-start | bytes 2359304 | tf_op jit(solution)/shard_map/ppermute | solution.py:694
  42.6 5.4 %collective-permute-start.9 = (f32[8,128]{1,0:T(8,128)S(1)}, f32[8,128]{1,0:T(8,128)S(1)}, u32[]{:S(2)}, u32[]{:S(2)}) collective-permute-start(f32[8,128]{1,0:T(8,128)S(1)} %local_sums.3.refs_1_), channel_id=1, source_target_pairs={{0,3},{1,2},{2,1},{3,0},{4,7},{5,6},{6,5},{7,4},{8,11},{9,10},{10,... | collective-permute-start | bytes 12296 | tf_op jit(solution)/shard_map/ppermute | solution.py:413
  46.2 4.5 %collective-permute-start.8 = (f32[8,128]{1,0:T(8,128)S(1)}, f32[8,128]{1,0:T(8,128)S(1)}, u32[]{:S(2)}, u32[]{:S(2)}) collective-permute-start(f32[8,128]{1,0:T(8,128)S(1)} %local_sums.3.refs_1_), channel_id=1, source_target_pairs={{0,2},{1,3},{2,0},{3,1},{4,6},{5,7},{6,4},{7,5},{8,10},{9,11},{10,... | collective-permute-start | bytes 12296 | tf_op jit(solution)/shard_map/ppermute | solution.py:413
  46.2 4.5 %collective-permute-start.7 = (f32[8,128]{1,0:T(8,128)S(1)}, f32[8,128]{1,0:T(8,128)S(1)}, u32[]{:S(2)}, u32[]{:S(2)}) collective-permute-start(f32[8,128]{1,0:T(8,128)S(1)} %local_sums.3.refs_1_), channel_id=1, source_target_pairs={{0,1},{1,0},{2,3},{3,2},{4,5},{5,4},{6,7},{7,6},{8,9},{9,8},{10,11... | collective-permute-start | bytes 12296 | tf_op jit(solution)/shard_map/ppermute | solution.py:413
  59.8 6.1 %copy-start = (f32[8,128]{1,0:T(8,128)}, f32[8,128]{1,0:T(8,128)S(1)}, u32[]{:S(2)}) copy-start(f32[8,128]{1,0:T(8,128)S(1)} %get-tuple-element.27.refs_0_) | copy-start | bytes 12292
  59.8 5.5 %collective-permute-start.12 = (f32[8,128]{1,0:T(8,128)S(1)}, f32[8,128]{1,0:T(8,128)S(1)}, u32[]{:S(2)}, u32[]{:S(2)}) collective-permute-start(f32[8,128]{1,0:T(8,128)S(1)} %get-tuple-element.27.refs_0_), channel_id=1, source_target_pairs={{0,3},{1,2},{2,1},{3,0},{4,7},{5,6},{6,5},{7,4},{8,11},{9,10},{10,... | collective-permute-start | bytes 12296 | tf_op jit(solution)/shard_map/ppermute | solution.py:413
  61.3 4.5 %collective-permute-start.11 = (f32[8,128]{1,0:T(8,128)S(1)}, f32[8,128]{1,0:T(8,128)S(1)}, u32[]{:S(2)}, u32[]{:S(2)}) collective-permute-start(f32[8,128]{1,0:T(8,128)S(1)} %get-tuple-element.27.refs_0_), channel_id=1, source_target_pairs={{0,2},{1,3},{2,0},{3,1},{4,6},{5,7},{6,4},{7,5},{8,10},{9,11},{10,... | collective-permute-start | bytes 12296 | tf_op jit(solution)/shard_map/ppermute | solution.py:413
  62.0 3.9 %collective-permute-start.10 = (f32[8,128]{1,0:T(8,128)S(1)}, f32[8,128]{1,0:T(8,128)S(1)}, u32[]{:S(2)}, u32[]{:S(2)}) collective-permute-start(f32[8,128]{1,0:T(8,128)S(1)} %get-tuple-element.27.refs_0_), channel_id=1, source_target_pairs={{0,1},{1,0},{2,3},{3,2},{4,5},{5,4},{6,7},{7,6},{8,9},{9,8},{10,11... | collective-permute-start | bytes 12296 | tf_op jit(solution)/shard_map/ppermute | solution.py:413
  65.3 0.6 copy-start.2
  65.8 0.6 copy-start.3
  66.4 0.6 copy-start.4

commit v2 on v1

--- a/solution.py
+++ b/solution.py
@@ -334,8 +334,8 @@
     )(native)
 
 
-def geometry_kernel(links_ref, geo_in, outflow_ref, pairs_ref, geo_ref):
-    rows = outflow_ref.shape[1]
+def geometry_kernel(links_ref, geo_in, pairs_ref, geo_ref):
+    rows = pairs_ref.shape[1]
     planes = rows // CHUNKS
     unpack_geo(geo_in, geo_ref)
     first = splat(geo_ref, FIRST, 0)
@@ -345,26 +345,9 @@
             pairs_ref[p, at_rows(j * SUB), :] = jnp.zeros((SUB, LANES), F32)
         return 0
 
-    lax.fori_loop(0, rows // SUB, clear, 0)
+    lax.fori_loop(0, rows // SUB, clear, 0, unroll=2)
 
     def cell(g, _):
-        scale = TIME_STEP / splat(geo_ref, VOL, g)
-        v = [[scale * x for x in face_coefficients(geo_ref, k, g)] for k in range(FACES)]
-        for t in range(TILES):
-            xb, xc = tile_nodes(t)
-            base = [v[k][1] * xb + v[k][2] * xc for k in range(FACES)]
-
-            def plane(a, _):
-                xa = first + a.astype(F32) * H
-                acc = None
-                for k in range(FACES):
-                    term = jnp.maximum(v[k][0] * xa + base[k], 0.0)
-                    acc = term if acc is None else acc + term
-                outflow_ref[g, at_rows((a * TILES + t) * SUB), :] = acc
-                return 0
-
-            lax.fori_loop(0, planes, plane, 0, unroll=4)
-
         edge = g - (SUB - REACH)
         for k in range(FACES):
             j = links_ref[k, g]
@@ -372,22 +355,24 @@
 
             @pl.when(jnp.logical_or(is_before, j >= SUB))
             def _():
-                r = j + REACH
-                before = g * REACH - g * (g - 1) // 2 + r - g
+                before = g * REACH - g * (g - 1) // 2 + (j + REACH) - g
                 after = len(BEFORE_PAIRS) + edge * (edge + 1) // 2 + j - SUB
                 at_pair = jnp.where(is_before, before, after)
+                scale = -TIME_STEP / splat(geo_ref, VOL, g)
+                v0, v1, v2 = [scale * x for x in face_coefficients(geo_ref, k, g)]
+                base = []
                 for t in range(TILES):
                     xb, xc = tile_nodes(t)
-                    base = v[k][1] * xb + v[k][2] * xc
-
-                    def plane(a, _):
-                        xa = first + a.astype(F32) * H
+                    base.append(v1 * xb + v2 * xc)
+
+                def plane(a, _):
+                    sa = v0 * (first + a.astype(F32) * H)
+                    for t in range(TILES):
                         at = at_rows((a * TILES + t) * SUB)
-                        weight = jnp.maximum(-(v[k][0] * xa + base), 0.0)
-                        pairs_ref[at_pair, at, :] = pairs_ref[at_pair, at, :] + weight
-                        return 0
-
-                    lax.fori_loop(0, planes, plane, 0, unroll=4)
+                        pairs_ref[at_pair, at, :] = pairs_ref[at_pair, at, :] + jnp.maximum(sa + base[t], 0.0)
+                    return 0
+
+                lax.fori_loop(0, planes, plane, 0, unroll=4)
 
         return 0
 
@@ -398,8 +383,8 @@
     return pl.pallas_call(
         geometry_kernel,
         in_specs=[spec(pltpu.SMEM), spec(pltpu.VMEM)],
-        out_specs=[spec(pltpu.VMEM)] * 2,
-        out_shape=[array(SUB, rows, LANES), array(2 * len(BEFORE_PAIRS), rows, LANES)],
+        out_specs=spec(pltpu.VMEM),
+        out_shape=array(2 * len(BEFORE_PAIRS), rows, LANES),
         scratch_shapes=[pltpu.VMEM((GEO, SUB, LANES), F32)],
         compiler_params=params(),
         name="geometry",
@@ -458,7 +443,7 @@
 
 
 def inner_kernel(last, count, links_ref, geo_in, absorbed_in, *refs):
-    sums_refs, (f_ref, outflow_ref, out_ref, sum_out, geo_ref, ta, coef) = refs[:count], refs[count:]
+    sums_refs, (f_ref, out_ref, sum_out, geo_ref, ta, coef) = refs[:count], refs[count:]
     planes = f_ref.shape[1] // CHUNKS
     unpack_geo(geo_in, geo_ref)
     sums = add_tiles(sums_refs)
@@ -470,16 +455,20 @@
     height = rate * n * rt * jnp.sqrt(rt)
     slope = (1.0 / 3.0) / (5.0 * n * temperature * temperature)
     scale = -TIME_STEP / geo_ref[VOL]
-    coef[0] = rate
+    coef[0] = 1.0 - rate
     coef[1] = rt
     coef[2], coef[3] = u[1], u[2]
     coef[4], coef[5] = slope * q[1], slope * q[2]
+    for i in range(3):
+        whole = None
+        for k in range(FACES):
+            x = scale * geo_ref[FV + FACES * i + k]
+            coef[6 + FACES * i + k] = x
+            whole = x if whole is None else whole + x
+        coef[24 + i] = whole
     for k in range(FACES):
         wall = geo_ref[WALL + k] > 0.5
-        ratio = column(sums, EMIT + k) / jnp.where(wall, column(absorbed, ABSORB + k), 1.0)
-        factor = scale * jnp.where(wall, ratio, geo_ref[LOCAL + k])
-        for i in range(3):
-            coef[6 + FACES * i + k] = factor * geo_ref[FV + FACES * i + k]
+        coef[27 + k] = column(sums, EMIT + k) / jnp.where(wall, column(absorbed, ABSORB + k), 1.0)
 
     first = geo_ref[FIRST]
 
@@ -491,7 +480,7 @@
         ta[2, a] = za - 5.0
         return 0
 
-    lax.fori_loop(0, planes, plane_table, 0)
+    lax.fori_loop(0, planes, plane_table, 0, unroll=4)
 
     def place(g, tile):
         if last:
@@ -505,13 +494,13 @@
             own = jnp.logical_and(j >= 0, j < SUB)
             source.append(jnp.where(own, j, g))
             weight.append([splat(coef, 6 + FACES * i + k, g) * splat(geo_ref, LOCAL + k, g) for i in range(3)])
-        keep = 1.0 - splat(coef, 0, g)
-        rtg = splat(coef, 1, g)
+        keep, rtg = splat(coef, 0, g), splat(coef, 1, g)
         ub, uc = splat(coef, 2, g), splat(coef, 3, g)
         qb, qc = splat(coef, 4, g), splat(coef, 5, g)
+        whole = [splat(coef, 24 + i, g) for i in range(3)]
         x0 = splat(geo_ref, FIRST, g)
         for pair in range(TILES // 2):
-            base, bell, heat, zz = [], [], [], []
+            base, bell, heat, zz, stay = [], [], [], [], []
             for t in (2 * pair, 2 * pair + 1):
                 xb, xc = tile_nodes(t)
                 cb, cc = xb - ub, xc - uc
@@ -520,6 +509,7 @@
                 heat.append(cb * qb + cc * qc)
                 zz.append(z)
                 base.append([weight[k][1] * xb + weight[k][2] * xc for k in range(FACES)])
+                stay.append(keep + whole[1] * xb + whole[2] * xc)
 
             def plane(a, _):
                 xa = x0 + a.astype(F32) * H
@@ -527,24 +517,29 @@
                     jnp.broadcast_to(ta[i, a, pl.ds(g, 1), :], (SUB, LANES)) for i in range(3)
                 ]
                 sa = [weight[k][0] * xa for k in range(FACES)]
+                stay_a = whole[0] * xa
                 for i in range(2):
                     tile = a * TILES + 2 * pair + i
                     at = at_rows(tile * SUB)
-                    acc = f_ref[g, at, :] * (keep - outflow_ref[g, at, :])
-                    for k in range(FACES):
-                        acc = acc + jnp.maximum(sa[k] + base[i][k], 0.0) * f_ref[source[k], at, :]
+                    f = f_ref[g, at, :]
+                    terms = [
+                        jnp.maximum(sa[k] + base[i][k], 0.0) * (f_ref[source[k], at, :] - f)
+                        for k in range(FACES)
+                    ]
                     target = (height_a * bell[i]) * (1.0 + (heat_a + heat[i]) * (z_a + zz[i]))
-                    out_ref[place(g, tile)] = acc + target
+                    inflow = (terms[0] + terms[1]) + (terms[2] + terms[3]) + (terms[4] + terms[5])
+                    out_ref[place(g, tile)] = (f * (stay_a + stay[i]) + target) + inflow
                 return 0
 
-            lax.fori_loop(0, planes, plane, 0, unroll=2)
+            lax.fori_loop(0, planes, plane, 0, unroll=4)
 
         for k in range(FACES):
 
             @pl.when(links_ref[k, g] == WALL_LINK)
             def _():
                 wt = splat(geo_ref, WT, g)
-                shape = wall_tiles(wt)
+                ratio = splat(coef, 27 + k, g)
+                shape = [ratio * x for x in wall_tiles(wt)]
                 v0, v1, v2 = [splat(coef, 6 + FACES * i + k, g) for i in range(3)]
                 base = []
                 for t in range(TILES):
@@ -556,21 +551,23 @@
                     wa = jnp.exp(-0.5 * xa * xa / wt)
                     sa = v0 * xa
                     for t in range(TILES):
-                        where = place(g, a * TILES + t)
-                        out_ref[where] = out_ref[where] + jnp.maximum(sa + base[t], 0.0) * (wa * shape[t])
+                        tile = a * TILES + t
+                        where = place(g, tile)
+                        f = f_ref[g, at_rows(tile * SUB), :]
+                        out_ref[where] = out_ref[where] + jnp.maximum(sa + base[t], 0.0) * (wa * shape[t] - f)
                     return 0
 
-                lax.fori_loop(0, planes, plane, 0, unroll=2)
+                lax.fori_loop(0, planes, plane, 0, unroll=4)
 
         return 0
 
     lax.fori_loop(0, SUB, cell, 0)
 
 
-def inner(last, links, geo, absorbed, tiles, f, outflow):
+def inner(last, links, geo, absorbed, tiles, f):
     rows = f.shape[1]
     vmem = spec(pltpu.VMEM)
-    given = [links, geo] + ([] if absorbed is None else [absorbed]) + list(tiles) + [f, outflow]
+    given = [links, geo] + ([] if absorbed is None else [absorbed]) + list(tiles) + [f]
 
     def kernel(links_ref, geo_in, *refs):
         if absorbed is None:
@@ -589,62 +586,64 @@
         scratch_shapes=[
             pltpu.VMEM((GEO, SUB, LANES), F32),
             pltpu.VMEM((3, rows // CHUNKS, SUB, LANES), F32),
-            pltpu.VMEM((6 + 3 * FACES, SUB, LANES), F32),
+            pltpu.VMEM((27 + FACES, SUB, LANES), F32),
         ],
         compiler_params=params(),
         name="inner",
     )(*given)
 
 
-def halo_terms(pairs_ref, before_ref, after_ref, at):
-    count = len(BEFORE_PAIRS)
+def halo_terms(pairs_ref, before_ref, after_ref, f_ref, at):
     low, high = [None] * REACH, [None] * REACH
     rows = [before_ref[r, at, :] for r in range(REACH)]
+    own = [f_ref[g, at, :] for g in range(REACH)]
     for p, (g, r) in enumerate(BEFORE_PAIRS):
-        term = pairs_ref[p, at, :] * rows[r]
+        term = pairs_ref[p, at, :] * (rows[r] - own[g])
         low[g] = term if low[g] is None else low[g] + term
     rows = [after_ref[r, at, :] for r in range(REACH)]
-    p = count
+    own = [f_ref[SUB - REACH + e, at, :] for e in range(REACH)]
+    p = len(BEFORE_PAIRS)
     for e in range(REACH):
         for r in range(e + 1):
-            term = pairs_ref[p, at, :] * rows[r]
+            term = pairs_ref[p, at, :] * (rows[r] - own[e])
             high[e] = term if high[e] is None else high[e] + term
             p += 1
     return low, high
 
 
-def edge_kernel(pairs_ref, before_ref, after_ref, part_ref, f_ref, up_ref, down_ref):
+def edge_kernel(pairs_ref, before_ref, after_ref, old_ref, part_ref, f_ref, up_ref, down_ref):
     def group(j, _):
         at = at_rows(j * SUB)
-        low, high = halo_terms(pairs_ref, before_ref, after_ref, at)
-        for g in range(SUB):
-            x = part_ref[g, at, :]
-            if g < REACH:
-                x = x + low[g]
-                down_ref[g, at, :] = x
-            e = g - (SUB - REACH)
-            if e >= 0:
-                x = x + high[e]
-                up_ref[e, at, :] = x
+        low, high = halo_terms(pairs_ref, before_ref, after_ref, old_ref, at)
+        for g in range(REACH):
+            x = part_ref[g, at, :] + low[g]
+            down_ref[g, at, :] = x
             f_ref[g, at, :] = x
+            e = SUB - REACH + g
+            x = part_ref[e, at, :] + high[g]
+            up_ref[g, at, :] = x
+            f_ref[e, at, :] = x
         return 0
 
-    lax.fori_loop(0, part_ref.shape[1] // SUB, group, 0)
-
-
-def edge(pairs, before, after, part):
+    lax.fori_loop(0, part_ref.shape[1] // SUB, group, 0, unroll=2)
+
+
+def edge(pairs, before, after, old, part):
     rows = part.shape[1]
     return pl.pallas_call(
         edge_kernel,
-        in_specs=[spec(pltpu.VMEM)] * 4,
+        in_specs=[spec(pltpu.VMEM)] * 5,
         out_specs=[spec(pltpu.VMEM)] * 3,
         out_shape=[array(SUB, rows, LANES), array(REACH, rows, LANES), array(REACH, rows, LANES)],
+        input_output_aliases={4: 0},
         compiler_params=params(),
         name="edge",
-    )(pairs, before, after, part)
-
-
-def last_edge_kernel(geo_in, pairs_ref, before_ref, after_ref, part_ref, out_hbm, sums_out, native_ref, sems):
+    )(pairs, before, after, old, part)
+
+
+def last_edge_kernel(
+    geo_in, pairs_ref, before_ref, after_ref, f_ref, part_ref, out_hbm, sums_out, native_ref, sems
+):
     rows = part_ref.shape[0] // SUB
     planes = rows // CHUNKS
     tiles = rows // SUB
@@ -654,7 +653,7 @@
 
         def group(j, _):
             at = at_rows(j * SUB)
-            low, high = halo_terms(pairs_ref, before_ref, after_ref, at)
+            low, high = halo_terms(pairs_ref, before_ref, after_ref, f_ref, at)
             terms = low + [None] * (SUB - 2 * REACH) + high
             for g in range(SUB):
                 where = (pl.ds(j * SUB * SUB + g, SUB, stride=SUB), slice(None))
@@ -662,7 +661,7 @@
                 native_ref[where] = x if terms[g] is None else x + terms[g]
             return 0
 
-        lax.fori_loop(i * part, (i + 1) * part, group, 0)
+        lax.fori_loop(i * part, (i + 1) * part, group, 0, unroll=2)
         at = pl.ds(i * part * SUB * SUB, part * SUB * SUB)
         copies.append(pltpu.make_async_copy(native_ref.at[at], out_hbm.at[at], sems.at[i]))
         copies[-1].start()
@@ -675,16 +674,16 @@
 LAST_PARTS = 4
 
 
-def last_edge(geo, pairs, before, after, part):
+def last_edge(geo, pairs, before, after, f, part):
     return pl.pallas_call(
         last_edge_kernel,
-        in_specs=[spec(pltpu.VMEM)] * 5,
+        in_specs=[spec(pltpu.VMEM)] * 6,
         out_specs=[spec(pltpu.HBM), spec(pltpu.VMEM)],
         out_shape=[array(*part.shape), array(SUB, LANES)],
         scratch_shapes=[pltpu.VMEM(part.shape, F32), pltpu.SemaphoreType.DMA((LAST_PARTS,))],
         compiler_params=params(),
         name="last_edge",
-    )(geo, pairs, before, after, part)
+    )(geo, pairs, before, after, f, part)
 
 
 def exchange(up, down):
@@ -717,13 +716,13 @@
     f, up, down = split_profile(pltpu.with_memory_space_constraint(native, pltpu.HBM))
     before, after = exchange(up, down)
     tiles = gather_sums(local_sums(True, links, geo, f))
-    outflow, pairs = geometry(links, geo, rows)
-    part, absorbed = inner(False, links, geo, None, tiles, f, outflow)
-    f, up, down = edge(pairs, before, after, part)
+    pairs = geometry(links, geo, rows)
+    part, absorbed = inner(False, links, geo, None, tiles, f)
+    f, up, down = edge(pairs, before, after, f, part)
     before, after = exchange(up, down)
     tiles = gather_sums(local_sums(False, links, geo, f))
-    part, _ = inner(True, links, geo, absorbed, tiles, f, outflow)
-    native, sums = last_edge(geo, pairs, before, after, part)
+    part, _ = inner(True, links, geo, absorbed, tiles, f)
+    native, sums = last_edge(geo, pairs, before, after, f, part)
     macro_quantities = macro(gather_sums(sums))
     evolved = native.reshape(rows, cells, LANES).transpose(1, 0, 2).reshape(cells, points)
     return evolved, macro_quantities

time: 69 us -> 63.2 us (0.916)
  the two profiles are of different devices: /device:TPU:4 before, /device:TPU:1 now
where the time goes in v2:
time: 63.2 us; the launch traced here: 62.6 us
  Pallas kernels  28 us (44%)
  starting transfers between devices  22.5 us (36%)
  waiting for transfers between devices  9.61 us (15%)
  local copies, waits for them, and re-layouts  1.67 us (3%)
  between operations  0.8 us (1%)
    pallas_call x2, Pallas kernels, inner(): pl.pallas_call(kernel, in_specs=[spec(pltpu.SMEM)] + [vmem] * (len(given)...  12.1 us
    ppermute x9, starting transfers between devices, gather_sums(): lax.ppermute(tile, 'vel', [(i, i ^ s) for i in range(size)])  10.9 us
    ppermute x2, starting transfers between devices, exchange(): lax.ppermute(up, 'space', forward)  7.76 us
    ppermute x9, waiting for transfers between devices, gather_sums(): lax.ppermute(tile, 'vel', [(i, i ^ s) for i in range(size)])  5.11 us
    pallas_call x2, Pallas kernels, local_sums(): pl.pallas_call(functools.partial(sums_kernel, with_absorbed), in_specs=[s...  4.99 us
    ppermute x2, waiting for transfers between devices, exchange(): lax.ppermute(down, 'space', backward)  4.49 us
    ppermute x2, starting transfers between devices, exchange(): lax.ppermute(down, 'space', backward)  3.84 us
    pallas_call x1, Pallas kernels, split_profile(): pl.pallas_call(split_kernel, in_specs=[spec(pltpu.HBM)], out_specs=[spec(...  2.84 us
  transfers between devices with their start and end apart: 13, of which 7 were waited for; matrix products, arithmetic and copies ran while one was open for 1% of the time, Pallas kernels for 31%

profile of v2, /device:TPU:1, one launch (start us, length us, event | category | flops | bytes accessed | tf_op | source)
XLA Modules:
  0.0 62.6 jit_solution(13140850868109750426)
XLA Ops:
  0.6 0.0 copy-start.5
  0.6 0.0 copy-start.6
  0.7 0.0 copy-start.7
  0.7 0.0 copy-start.1
  0.7 2.8 %split_profile.1 = (f32[8,512,128]{2,1,0:T(8,128)S(1)}, f32[3,512,128]{2,1,0:T(8,128)}, f32[3,512,128]{2,1,0:T(8,128)}) custom-call(f32[4096,128]{1,0:T(8,128)} %bitcast.13), custom_call_target="tpu_custom_call" | custom-call | tf_op jit(solution)/shard_map/split_profile/pallas_call | solution.py:326
  3.5 4.5 %collective-permute-start = (f32[3,512,128]{2,1,0:T(8,128)}, f32[3,512,128]{2,1,0:T(8,128)S(1)}, u32[]{:S(2)}, u32[]{:S(2)}) collective-permute-start(f32[3,512,128]{2,1,0:T(8,128)} %get-tuple-element.13), channel_id=1, source_target_pairs={{0,4},{4,8},{8,12},{12,16},{16,20},{20,24},{24,28},{1,5},{5,9},{9,... | collective-permute-start | bytes 2359304 | tf_op jit(solution)/shard_map/ppermute | solution.py:693
  8.0 1.9 %collective-permute-start.1 = (f32[3,512,128]{2,1,0:T(8,128)}, f32[3,512,128]{2,1,0:T(8,128)}, u32[]{:S(2)}, u32[]{:S(2)}) collective-permute-start(f32[3,512,128]{2,1,0:T(8,128)} %get-tuple-element.14), channel_id=1, source_target_pairs={{4,0},{8,4},{12,8},{16,12},{20,16},{24,20},{28,24},{5,1},{9,5},{13... | collective-permute-start | bytes 2359304 | tf_op jit(solution)/shard_map/ppermute | solution.py:693
  10.0 0.1 copy.19
  10.1 0.0 copy-done.6
  10.1 0.1 copy.21
  10.2 0.1 copy.22
  10.2 0.1 copy.23.links_ref
  10.3 0.1 copy.28
  10.4 0.1 concatenate.3
  10.5 2.6 %local_sums.2.refs_0_ = f32[8,128]{1,0:T(8,128)S(1)} custom-call(s32[6,8]{1,0:T(8,128)S(1)} %copy.23.links_ref, f32[8,128]{1,0:T(8,128)S(1)} %pad.4.geo_in, f32[8,512,128]{2,1,0:T(8,128)S(1)} %get-tuple-element.15.f_ref.refs_4_.old_ref), custom_call_target="tpu_custom_call" | custom-call | tf_op jit(solution)/shard_map/local_sums/pallas_call | solution.py:276
  13.1 3.4 %collective-permute-start.4 = (f32[8,128]{1,0:T(8,128)S(1)}, f32[8,128]{1,0:T(8,128)S(1)}, u32[]{:S(2)}, u32[]{:S(2)}) collective-permute-start(f32[8,128]{1,0:T(8,128)S(1)} %local_sums.2.refs_0_), channel_id=1, source_target_pairs={{0,3},{1,2},{2,1},{3,0},{4,7},{5,6},{6,5},{7,4},{8,11},{9,10},{10,... | collective-permute-start | bytes 12296 | tf_op jit(solution)/shard_map/ppermute | solution.py:398
  16.5 0.0 collective-permute-start.3
  16.5 0.4 collective-permute-start.2
  16.9 2.4 %geometry.1.pairs_ref = f32[12,512,128]{2,1,0:T(8,128)S(1)} custom-call(s32[6,8]{1,0:T(8,128)S(1)} %copy.23.links_ref, f32[8,128]{1,0:T(8,128)S(1)} %pad.4.geo_in), custom_call_target="tpu_custom_call" | custom-call | tf_op jit(solution)/shard_map/geometry/pallas_call | solution.py:383
  19.3 0.0 collective-permute-done.4.refs_3_
  19.3 0.5 collective-permute-done.3.refs_2_
  19.9 0.0 collective-permute-done.2.refs_1_
  19.9 5.6 %inner.2 = (f32[8,512,128]{2,1,0:T(8,128)S(1)}, f32[8,128]{1,0:T(8,128)S(1)}) custom-call(s32[6,8]{1,0:T(8,128)S(1)} %copy.23.links_ref, f32[8,128]{1,0:T(8,128)S(1)} %pad.4.geo_in, f32[8,128]{1,0:T(8,128)S(1)} %local_sums.2.refs_0_, f32[8,128]{1,0:T(8,128)S(1)} %collective-permute-done.2.refs_1_, f32[8,128]{1,0:T(8,128)S(1)} %collective-permute-done.3.refs_2_, ...), custom_call_target="tpu_custom_call" | custom-call | tf_op jit(solution)/shard_map/inner/pallas_call | solution.py:578
  25.5 0.0 collective-permute-done.before_ref
  25.5 1.8 %collective-permute-done.1.after_ref = f32[3,512,128]{2,1,0:T(8,128)} collective-permute-done((f32[3,512,128]{2,1,0:T(8,128)}, f32[3,512,128]{2,1,0:T(8,128)}, u32[]{:S(2)}, u32[]{:S(2)}) %collective-permute-start.1) | collective-permute-done | bytes 786464 | tf_op jit(solution)/shard_map/ppermute | solution.py:693
  27.3 2.3 %edge.1 = (f32[8,512,128]{2,1,0:T(8,128)S(1)}, f32[3,512,128]{2,1,0:T(8,128)S(1)}, f32[3,512,128]{2,1,0:T(8,128)S(1)}) custom-call(f32[12,512,128]{2,1,0:T(8,128)S(1)} %geometry.1.pairs_ref, f32[3,512,128]{2,1,0:T(8,128)S(1)} %collective-permute-done.before_ref, f32[3,512,128]{2,1,0:T(8,128)} %collective-permute-done.1.after_ref, ...), custom_call_target="tpu_custom_call", output_to_operand_aliasing={{0}: (4, {})} | custom-call | tf_op jit(solution)/shard_map/edge/pallas_call | solution.py:633
  29.7 3.2 %collective-permute-start.5 = (f32[3,512,128]{2,1,0:T(8,128)S(1)}, f32[3,512,128]{2,1,0:T(8,128)S(1)}, u32[]{:S(2)}, u32[]{:S(2)}) collective-permute-start(f32[3,512,128]{2,1,0:T(8,128)S(1)} %get-tuple-element.17), channel_id=1, source_target_pairs={{0,4},{4,8},{8,12},{12,16},{16,20},{20,24},{24,28},{1,5},{5,9},{9,... | collective-permute-start | bytes 2359304 | tf_op jit(solution)/shard_map/ppermute | solution.py:693
  32.9 1.9 %collective-permute-start.6 = (f32[3,512,128]{2,1,0:T(8,128)S(1)}, f32[3,512,128]{2,1,0:T(8,128)S(1)}, u32[]{:S(2)}, u32[]{:S(2)}) collective-permute-start(f32[3,512,128]{2,1,0:T(8,128)S(1)} %get-tuple-element.18), channel_id=1, source_target_pairs={{4,0},{8,4},{12,8},{16,12},{20,16},{24,20},{28,24},{5,1},{9,5},{13... | collective-permute-start | bytes 2359304 | tf_op jit(solution)/shard_map/ppermute | solution.py:693
  34.8 2.3 %local_sums.3.refs_1_ = f32[8,128]{1,0:T(8,128)S(1)} custom-call(s32[6,8]{1,0:T(8,128)S(1)} %copy.23.links_ref, f32[8,128]{1,0:T(8,128)S(1)} %pad.4.geo_in, f32[8,512,128]{2,1,0:T(8,128)S(1)} %get-tuple-element.19.f_ref.refs_5_), custom_call_target="tpu_custom_call" | custom-call | tf_op jit(solution)/shard_map/local_sums/pallas_call | solution.py:276
  37.2 2.5 %collective-permute-start.9 = (f32[8,128]{1,0:T(8,128)S(1)}, f32[8,128]{1,0:T(8,128)S(1)}, u32[]{:S(2)}, u32[]{:S(2)}) collective-permute-start(f32[8,128]{1,0:T(8,128)S(1)} %local_sums.3.refs_1_), channel_id=1, source_target_pairs={{0,3},{1,2},{2,1},{3,0},{4,7},{5,6},{6,5},{7,4},{8,11},{9,10},{10,... | collective-permute-start | bytes 12296 | tf_op jit(solution)/shard_map/ppermute | solution.py:398
  39.7 0.0 collective-permute-start.8
  39.7 1.0 %collective-permute-start.7 = (f32[8,128]{1,0:T(8,128)S(1)}, f32[8,128]{1,0:T(8,128)S(1)}, u32[]{:S(2)}, u32[]{:S(2)}) collective-permute-start(f32[8,128]{1,0:T(8,128)S(1)} %local_sums.3.refs_1_), channel_id=1, source_target_pairs={{0,1},{1,0},{2,3},{3,2},{4,5},{5,4},{6,7},{7,6},{8,9},{9,8},{10,11... | collective-permute-start | bytes 12296 | tf_op jit(solution)/shard_map/ppermute | solution.py:398
  40.7 0.7 %collective-permute-done.9.refs_4_ = f32[8,128]{1,0:T(8,128)S(1)} collective-permute-done((f32[8,128]{1,0:T(8,128)S(1)}, f32[8,128]{1,0:T(8,128)S(1)}, u32[]{:S(2)}, u32[]{:S(2)}) %collective-permute-start.9) | collective-permute-done | bytes 4128 | tf_op jit(solution)/shard_map/ppermute | solution.py:398
  41.5 1.6 %collective-permute-done.8.refs_3_ = f32[8,128]{1,0:T(8,128)S(1)} collective-permute-done((f32[8,128]{1,0:T(8,128)S(1)}, f32[8,128]{1,0:T(8,128)S(1)}, u32[]{:S(2)}, u32[]{:S(2)}) %collective-permute-start.8) | collective-permute-done | bytes 4128 | tf_op jit(solution)/shard_map/ppermute | solution.py:398
  43.1 0.0 collective-permute-done.7.refs_2_
  43.1 6.5 %inner.3 = (f32[4096,128]{1,0:T(8,128)S(1)}, f32[8,128]{1,0:T(8,128)}) custom-call(s32[6,8]{1,0:T(8,128)S(1)} %copy.23.links_ref, f32[8,128]{1,0:T(8,128)S(1)} %pad.4.geo_in, f32[8,128]{1,0:T(8,128)S(1)} %get-tuple-element.20.refs_0_, f32[8,128]{1,0:T(8,128)S(1)} %local_sums.3.refs_1_, f32[8,128]{1,0:T(8,128)S(1)} %collective-permute-done.7.refs_2_, ...), custom_call_target="tpu_custom_call" | custom-call | tf_op jit(solution)/shard_map/inner/pallas_call | solution.py:578
  49.6 0.0 collective-permute-done.5.before_ref
  49.6 2.7 %collective-permute-done.6.after_ref = f32[3,512,128]{2,1,0:T(8,128)S(1)} collective-permute-done((f32[3,512,128]{2,1,0:T(8,128)S(1)}, f32[3,512,128]{2,1,0:T(8,128)S(1)}, u32[]{:S(2)}, u32[]{:S(2)}) %collective-permute-start.6) | collective-permute-done | bytes 786464 | tf_op jit(solution)/shard_map/ppermute | solution.py:693
  52.2 1.9 %last_edge.1 = (f32[4096,128]{1,0:T(8,128)}, f32[8,128]{1,0:T(8,128)S(1)}) custom-call(f32[8,128]{1,0:T(8,128)S(1)} %pad.4.geo_in, f32[12,512,128]{2,1,0:T(8,128)S(1)} %geometry.1.pairs_ref, f32[3,512,128]{2,1,0:T(8,128)S(1)} %collective-permute-done.5.before_ref, f32[3,512,128]{2,1,0:T(8,128)S(1)} %collective-permute-done.6.after_ref, ...), custom_call_target="tpu_custom_call" | custom-call | tf_op jit(solution)/shard_map/last_edge/pallas_call | solution.py:678
  54.1 2.5 %collective-permute-start.12 = (f32[8,128]{1,0:T(8,128)S(1)}, f32[8,128]{1,0:T(8,128)S(1)}, u32[]{:S(2)}, u32[]{:S(2)}) collective-permute-start(f32[8,128]{1,0:T(8,128)S(1)} %get-tuple-element.23.refs_0_), channel_id=1, source_target_pairs={{0,3},{1,2},{2,1},{3,0},{4,7},{5,6},{6,5},{7,4},{8,11},{9,10},{10,... | collective-permute-start | bytes 12296 | tf_op jit(solution)/shard_map/ppermute | solution.py:398
  56.6 0.0 collective-permute-start.11
  56.6 1.1 %collective-permute-start.10 = (f32[8,128]{1,0:T(8,128)S(1)}, f32[8,128]{1,0:T(8,128)S(1)}, u32[]{:S(2)}, u32[]{:S(2)}) collective-permute-start(f32[8,128]{1,0:T(8,128)S(1)} %get-tuple-element.23.refs_0_), channel_id=1, source_target_pairs={{0,1},{1,0},{2,3},{3,2},{4,5},{5,4},{6,7},{7,6},{8,9},{9,8},{10,11... | collective-permute-start | bytes 12296 | tf_op jit(solution)/shard_map/ppermute | solution.py:398
  57.8 0.7 %collective-permute-done.12.refs_3_ = f32[8,128]{1,0:T(8,128)S(1)} collective-permute-done((f32[8,128]{1,0:T(8,128)S(1)}, f32[8,128]{1,0:T(8,128)S(1)}, u32[]{:S(2)}, u32[]{:S(2)}) %collective-permute-start.12) | collective-permute-done | bytes 4128 | tf_op jit(solution)/shard_map/ppermute | solution.py:398
  58.5 1.5 %collective-permute-done.11.refs_2_ = f32[8,128]{1,0:T(8,128)S(1)} collective-permute-done((f32[8,128]{1,0:T(8,128)S(1)}, f32[8,128]{1,0:T(8,128)S(1)}, u32[]{:S(2)}, u32[]{:S(2)}) %collective-permute-start.11) | collective-permute-done | bytes 4128 | tf_op jit(solution)/shard_map/ppermute | solution.py:398
  60.0 0.0 collective-permute-done.10.refs_1_
  60.0 0.6 copy-done.3
  60.6 0.6 copy-done.4
  61.2 1.4 %macro.1 = f32[8,8]{1,0:T(8,128)} custom-call(f32[8,128]{1,0:T(8,128)} %copy-done, f32[8,128]{1,0:T(8,128)} %copy-done.4, f32[8,128]{1,0:T(8,128)} %copy-done.3, f32[8,128]{1,0:T(8,128)} %copy-done.2), custom_call_target="tpu_custom_call" | custom-call | tf_op jit(solution)/shard_map/macro/pallas_call | solution.py:436
  (13 shorter events, 0.0 us)
Async XLA Ops:
  0.6 9.3 %copy-start.5 = (s32[6,8]{1,0:T(8,128)S(1)}, s32[6,8]{1,0:T(8,128)}, u32[]{:S(2)}) copy-start(s32[6,8]{1,0:T(8,128)} %param.6) | copy-start | bytes 580
  0.6 9.4 %copy-start.6 = (f32[8]{0:T(128)S(1)}, f32[8]{0:T(128)}, u32[]{:S(2)}) copy-start(f32[8]{0:T(128)} %param.8) | copy-start | bytes 100
  0.7 9.5 %copy-start.7 = (f32[8]{0:T(128)S(1)}, f32[8]{0:T(128)}, u32[]{:S(2)}) copy-start(f32[8]{0:T(128)} %param.9) | copy-start | bytes 100
  0.7 9.7 %copy-start.1 = (f32[3,6,8]{2,1,0:T(8,128)S(1)}, f32[3,6,8]{2,1,0:T(8,128)}, u32[]{:S(2)}) copy-start(f32[3,6,8]{2,1,0:T(8,128)} %param.7) | copy-start | bytes 1732
  3.5 22.0 %collective-permute-start = (f32[3,512,128]{2,1,0:T(8,128)}, f32[3,512,128]{2,1,0:T(8,128)S(1)}, u32[]{:S(2)}, u32[]{:S(2)}) collective-permute-start(f32[3,512,128]{2,1,0:T(8,128)} %get-tuple-element.13), channel_id=1, source_target_pairs={{0,4},{4,8},{8,12},{12,16},{16,20},{20,24},{24,28},{1,5},{5,9},{9,... | collective-permute-start | bytes 2359304 | tf_op jit(solution)/shard_map/ppermute | solution.py:693
  8.0 19.3 %collective-permute-start.1 = (f32[3,512,128]{2,1,0:T(8,128)}, f32[3,512,128]{2,1,0:T(8,128)}, u32[]{:S(2)}, u32[]{:S(2)}) collective-permute-start(f32[3,512,128]{2,1,0:T(8,128)} %get-tuple-element.14), channel_id=1, source_target_pairs={{4,0},{8,4},{12,8},{16,12},{20,16},{24,20},{28,24},{5,1},{9,5},{13... | collective-permute-start | bytes 2359304 | tf_op jit(solution)/shard_map/ppermute | solution.py:693
  13.1 6.2 %collective-permute-start.4 = (f32[8,128]{1,0:T(8,128)S(1)}, f32[8,128]{1,0:T(8,128)S(1)}, u32[]{:S(2)}, u32[]{:S(2)}) collective-permute-start(f32[8,128]{1,0:T(8,128)S(1)} %local_sums.2.refs_0_), channel_id=1, source_target_pairs={{0,3},{1,2},{2,1},{3,0},{4,7},{5,6},{6,5},{7,4},{8,11},{9,10},{10,... | collective-permute-start | bytes 12296 | tf_op jit(solution)/shard_map/ppermute | solution.py:398
  16.5 3.4 %collective-permute-start.3 = (f32[8,128]{1,0:T(8,128)S(1)}, f32[8,128]{1,0:T(8,128)S(1)}, u32[]{:S(2)}, u32[]{:S(2)}) collective-permute-start(f32[8,128]{1,0:T(8,128)S(1)} %local_sums.2.refs_0_), channel_id=1, source_target_pairs={{0,2},{1,3},{2,0},{3,1},{4,6},{5,7},{6,4},{7,5},{8,10},{9,11},{10,... | collective-permute-start | bytes 12296 | tf_op jit(solution)/shard_map/ppermute | solution.py:398
  16.5 3.4 %collective-permute-start.2 = (f32[8,128]{1,0:T(8,128)S(1)}, f32[8,128]{1,0:T(8,128)S(1)}, u32[]{:S(2)}, u32[]{:S(2)}) collective-permute-start(f32[8,128]{1,0:T(8,128)S(1)} %local_sums.2.refs_0_), channel_id=1, source_target_pairs={{0,1},{1,0},{2,3},{3,2},{4,5},{5,4},{6,7},{7,6},{8,9},{9,8},{10,11... | collective-permute-start | bytes 12296 | tf_op jit(solution)/shard_map/ppermute | solution.py:398
  29.7 19.9 %collective-permute-start.5 = (f32[3,512,128]{2,1,0:T(8,128)S(1)}, f32[3,512,128]{2,1,0:T(8,128)S(1)}, u32[]{:S(2)}, u32[]{:S(2)}) collective-permute-start(f32[3,512,128]{2,1,0:T(8,128)S(1)} %get-tuple-element.17), channel_id=1, source_target_pairs={{0,4},{4,8},{8,12},{12,16},{16,20},{20,24},{24,28},{1,5},{5,9},{9,... | collective-permute-start | bytes 2359304 | tf_op jit(solution)/shard_map/ppermute | solution.py:693
  32.9 19.3 %collective-permute-start.6 = (f32[3,512,128]{2,1,0:T(8,128)S(1)}, f32[3,512,128]{2,1,0:T(8,128)S(1)}, u32[]{:S(2)}, u32[]{:S(2)}) collective-permute-start(f32[3,512,128]{2,1,0:T(8,128)S(1)} %get-tuple-element.18), channel_id=1, source_target_pairs={{4,0},{8,4},{12,8},{16,12},{20,16},{24,20},{28,24},{5,1},{9,5},{13... | collective-permute-start | bytes 2359304 | tf_op jit(solution)/shard_map/ppermute | solution.py:693
  37.2 4.3 %collective-permute-start.9 = (f32[8,128]{1,0:T(8,128)S(1)}, f32[8,128]{1,0:T(8,128)S(1)}, u32[]{:S(2)}, u32[]{:S(2)}) collective-permute-start(f32[8,128]{1,0:T(8,128)S(1)} %local_sums.3.refs_1_), channel_id=1, source_target_pairs={{0,3},{1,2},{2,1},{3,0},{4,7},{5,6},{6,5},{7,4},{8,11},{9,10},{10,... | collective-permute-start | bytes 12296 | tf_op jit(solution)/shard_map/ppermute | solution.py:398
  39.7 3.4 %collective-permute-start.8 = (f32[8,128]{1,0:T(8,128)S(1)}, f32[8,128]{1,0:T(8,128)S(1)}, u32[]{:S(2)}, u32[]{:S(2)}) collective-permute-start(f32[8,128]{1,0:T(8,128)S(1)} %local_sums.3.refs_1_), channel_id=1, source_target_pairs={{0,2},{1,3},{2,0},{3,1},{4,6},{5,7},{6,4},{7,5},{8,10},{9,11},{10,... | collective-permute-start | bytes 12296 | tf_op jit(solution)/shard_map/ppermute | solution.py:398
  39.7 3.4 %collective-permute-start.7 = (f32[8,128]{1,0:T(8,128)S(1)}, f32[8,128]{1,0:T(8,128)S(1)}, u32[]{:S(2)}, u32[]{:S(2)}) collective-permute-start(f32[8,128]{1,0:T(8,128)S(1)} %local_sums.3.refs_1_), channel_id=1, source_target_pairs={{0,1},{1,0},{2,3},{3,2},{4,5},{5,4},{6,7},{7,6},{8,9},{9,8},{10,11... | collective-permute-start | bytes 12296 | tf_op jit(solution)/shard_map/ppermute | solution.py:398
  54.1 5.9 %copy-start = (f32[8,128]{1,0:T(8,128)}, f32[8,128]{1,0:T(8,128)S(1)}, u32[]{:S(2)}) copy-start(f32[8,128]{1,0:T(8,128)S(1)} %get-tuple-element.23.refs_0_) | copy-start | bytes 12292
  54.1 4.3 %collective-permute-start.12 = (f32[8,128]{1,0:T(8,128)S(1)}, f32[8,128]{1,0:T(8,128)S(1)}, u32[]{:S(2)}, u32[]{:S(2)}) collective-permute-start(f32[8,128]{1,0:T(8,128)S(1)} %get-tuple-element.23.refs_0_), channel_id=1, source_target_pairs={{0,3},{1,2},{2,1},{3,0},{4,7},{5,6},{6,5},{7,4},{8,11},{9,10},{10,... | collective-permute-start | bytes 12296 | tf_op jit(solution)/shard_map/ppermute | solution.py:398
  56.6 3.4 %collective-permute-start.11 = (f32[8,128]{1,0:T(8,128)S(1)}, f32[8,128]{1,0:T(8,128)S(1)}, u32[]{:S(2)}, u32[]{:S(2)}) collective-permute-start(f32[8,128]{1,0:T(8,128)S(1)} %get-tuple-element.23.refs_0_), channel_id=1, source_target_pairs={{0,2},{1,3},{2,0},{3,1},{4,6},{5,7},{6,4},{7,5},{8,10},{9,11},{10,... | collective-permute-start | bytes 12296 | tf_op jit(solution)/shard_map/ppermute | solution.py:398
  56.6 3.4 %collective-permute-start.10 = (f32[8,128]{1,0:T(8,128)S(1)}, f32[8,128]{1,0:T(8,128)S(1)}, u32[]{:S(2)}, u32[]{:S(2)}) collective-permute-start(f32[8,128]{1,0:T(8,128)S(1)} %get-tuple-element.23.refs_0_), channel_id=1, source_target_pairs={{0,1},{1,0},{2,3},{3,2},{4,5},{5,4},{6,7},{7,6},{8,9},{9,8},{10,11... | collective-permute-start | bytes 12296 | tf_op jit(solution)/shard_map/ppermute | solution.py:398
  58.5 1.5 %copy-start.2 = (f32[8,128]{1,0:T(8,128)}, f32[8,128]{1,0:T(8,128)S(1)}, u32[]{:S(2)}) copy-start(f32[8,128]{1,0:T(8,128)S(1)} %collective-permute-done.12.refs_3_) | copy-start | bytes 12292
  60.0 0.6 copy-start.3
  60.6 0.6 copy-start.4

commit v3 on v2

--- a/solution.py
+++ b/solution.py
@@ -224,7 +224,7 @@
                     shape = wall_tiles(wt)
 
                 def plane(a, acc):
-                    out, back = acc
+                    out, back = list(acc[0]), list(acc[1])
                     xa = first + a.astype(F32) * H
                     sa = v0 * xa
                     if with_absorbed:
@@ -232,13 +232,15 @@
                     for t in range(TILES):
                         s = sa + base[t]
                         f = f_ref[g, at_rows((a * TILES + t) * SUB), :]
-                        out = out + jnp.maximum(s, 0.0) * f
+                        out[t] = out[t] + jnp.maximum(s, 0.0) * f
                         if with_absorbed:
-                            back = back + jnp.maximum(-s, 0.0) * (wa * shape[t])
-                    return out, back
-
-                zero = jnp.zeros((SUB, LANES), F32)
-                out, back = lax.fori_loop(0, planes, plane, (zero, zero), unroll=2)
+                            back[t] = back[t] + jnp.maximum(-s, 0.0) * (wa * shape[t])
+                    return tuple(out), tuple(back)
+
+                zeros = (jnp.zeros((SUB, LANES), F32),) * TILES
+                out, back = lax.fori_loop(0, planes, plane, (zeros, zeros), unroll=4)
+                out = (out[0] + out[1]) + (out[2] + out[3])
+                back = (back[0] + back[1]) + (back[2] + back[3])
                 at = at_rows(g * SUB)
                 sums_ref[k, at, :] = out
                 if with_absorbed:
@@ -249,15 +251,30 @@
     lax.fori_loop(0, SUB, cell, 0)
 
 
-def sums_kernel(with_absorbed, links_ref, geo_in, f_ref, sums_out, geo_ref, parts_ref, face_ref):
+def sums_kernel(links_ref, geo_in, f_ref, sums_out, geo_ref, parts_ref, face_ref):
     planes = f_ref.shape[1] // CHUNKS
     unpack_geo(geo_in, geo_ref)
-    first = geo_ref[FIRST]
     y = polynomial_sums(f_ref, planes, parts_ref)
-    packed = pack_sums(finish_polynomials(y, first, planes), 0)
-    wall_sums(f_ref, planes, links_ref, geo_ref, face_ref, with_absorbed)
-    faces = 2 * FACES if with_absorbed else FACES
-    sums_out[...] = packed + pack_sums([over_sublanes(face_ref, k) for k in range(faces)], EMIT)
+    packed = pack_sums(finish_polynomials(y, geo_ref[FIRST], planes), 0)
+    wall_sums(f_ref, planes, links_ref, geo_ref, face_ref, False)
+    sums_out[...] = packed + pack_sums([over_sublanes(face_ref, k) for k in range(FACES)], EMIT)
+
+
+def first_sums_kernel(links_ref, geo_in, native_ref, f_ref, sums_out, geo_ref, face_ref):
+    rows = f_ref.shape[1]
+    planes = rows // CHUNKS
+    unpack_geo(geo_in, geo_ref)
+
+    def group(j, _):
+        for g in range(SUB):
+            f_ref[g, at_rows(j * SUB), :] = native_ref[pl.ds(j * SUB * SUB + g, SUB, stride=SUB), :]
+        return 0
+
+    lax.fori_loop(0, rows // SUB, group, 0, unroll=2)
+    y = native_polynomial_sums(native_ref, planes)
+    packed = pack_sums(finish_polynomials(y, geo_ref[FIRST], planes), 0)
+    wall_sums(f_ref, planes, links_ref, geo_ref, face_ref, True)
+    sums_out[...] = packed + pack_sums([over_sublanes(face_ref, k) for k in range(2 * FACES)], EMIT)
 
 
 def spec(space):
@@ -272,26 +289,46 @@
     return pltpu.CompilerParams(vmem_limit_bytes=VMEM_LIMIT)
 
 
-def local_sums(with_absorbed, links, geo, f):
+def local_sums(links, geo, f):
     return pl.pallas_call(
-        functools.partial(sums_kernel, with_absorbed),
+        sums_kernel,
         in_specs=[spec(pltpu.SMEM), spec(pltpu.VMEM), spec(pltpu.VMEM)],
         out_specs=spec(pltpu.VMEM),
         out_shape=array(SUB, LANES),
         scratch_shapes=[
             pltpu.VMEM((GEO, SUB, LANES), F32),
             pltpu.VMEM((10, SUB * SUB, LANES), F32),
-            pltpu.VMEM(((2 if with_absorbed else 1) * FACES, SUB * SUB, LANES), F32),
+            pltpu.VMEM((FACES, SUB * SUB, LANES), F32),
         ],
         compiler_params=params(),
         name="local_sums",
     )(links, geo, f)
 
 
+def first_sums(links, geo, native):
+    rows = native.shape[0] // SUB
+    return pl.pallas_call(
+        first_sums_kernel,
+        in_specs=[spec(pltpu.SMEM), spec(pltpu.VMEM), spec(pltpu.VMEM)],
+        out_specs=[spec(pltpu.VMEM)] * 2,
+        out_shape=[array(SUB, rows, LANES), array(SUB, LANES)],
+        scratch_shapes=[
+            pltpu.VMEM((GEO, SUB, LANES), F32),
+            pltpu.VMEM((2 * FACES, SUB * SUB, LANES), F32),
+        ],
+        compiler_params=params(),
+        name="first_sums",
+    )(links, geo, native)
+
+
 SPLIT_PARTS = 4
 
 
-def split_kernel(native_hbm, f_ref, up_ref, down_ref, native_ref, sems):
+def is_odd():
+    return lax.rem(lax.axis_index("space"), 2) == 1
+
+
+def first_rows_kernel(native_hbm, native_ref, far_ref, near_ref, sems):
     rows = native_ref.shape[0]
     part = rows // SPLIT_PARTS
     copies = [
@@ -302,36 +339,35 @@
     ]
     for c in copies:
         c.start()
+    odd = is_odd()
+    far = jnp.where(odd, SUB - REACH, 0)
+    near = jnp.where(odd, 0, SUB - REACH)
     groups = part // (SUB * SUB)
 
     for i, c in enumerate(copies):
         c.wait()
 
         def group(j, _):
-            for g in range(SUB):
-                x = native_ref[pl.ds(j * SUB * SUB + g, SUB, stride=SUB), :]
+            for r in range(REACH):
                 at = at_rows(j * SUB)
-                f_ref[g, at, :] = x
-                if g < REACH:
-                    down_ref[g, at, :] = x
-                if g >= SUB - REACH:
-                    up_ref[g - (SUB - REACH), at, :] = x
+                far_ref[r, at, :] = native_ref[pl.ds(j * SUB * SUB + far + r, SUB, stride=SUB), :]
+                near_ref[r, at, :] = native_ref[pl.ds(j * SUB * SUB + near + r, SUB, stride=SUB), :]
             return 0
 
-        lax.fori_loop(i * groups, (i + 1) * groups, group, 0, unroll=2)
-
-
-def split_profile(native):
+        lax.fori_loop(i * groups, (i + 1) * groups, group, 0, unroll=4)
+
+
+def first_rows(native):
     rows = native.shape[0] // SUB
     return pl.pallas_call(
-        split_kernel,
+        first_rows_kernel,
         in_specs=[spec(pltpu.HBM)],
         out_specs=[spec(pltpu.VMEM)] * 3,
-        out_shape=[array(SUB, rows, LANES), array(REACH, rows, LANES), array(REACH, rows, LANES)],
-        scratch_shapes=[pltpu.VMEM((SUB * rows, LANES), F32), pltpu.SemaphoreType.DMA((SPLIT_PARTS,))],
+        out_shape=[array(*native.shape), array(REACH, rows, LANES), array(REACH, rows, LANES)],
+        scratch_shapes=[pltpu.SemaphoreType.DMA((SPLIT_PARTS,))],
         compiler_params=params(),
-        name="split_profile",
-    )(native)
+        name="first_rows",
+    )(pltpu.with_memory_space_constraint(native, pltpu.HBM))
 
 
 def geometry_kernel(links_ref, geo_in, pairs_ref, geo_ref):
@@ -442,80 +478,45 @@
     )(*tiles)
 
 
-def inner_kernel(last, count, links_ref, geo_in, absorbed_in, *refs):
-    sums_refs, (f_ref, out_ref, sum_out, geo_ref, ta, coef) = refs[:count], refs[count:]
+def placer(native):
+    def place(g, tile):
+        if native:
+            return (pl.ds(tile * SUB * SUB + g, SUB, stride=SUB), slice(None))
+        return (g, at_rows(tile * SUB), slice(None))
+
+    return place
+
+
+def flux_kernel(native, links_ref, geo_in, f_ref, out_ref, geo_ref, coef):
     planes = f_ref.shape[1] // CHUNKS
+    place = placer(native)
     unpack_geo(geo_in, geo_ref)
-    sums = add_tiles(sums_refs)
-    sum_out[...] = sums
-    absorbed = sums if absorbed_in is None else absorbed_in[...]
-    n, u, temperature, q = quantities(sums)
-    rt = 1.0 / temperature
-    rate = TIME_STEP * n * temperature / (SHEAR * jnp.exp(POWER * jnp.log(temperature)))
-    height = rate * n * rt * jnp.sqrt(rt)
-    slope = (1.0 / 3.0) / (5.0 * n * temperature * temperature)
     scale = -TIME_STEP / geo_ref[VOL]
-    coef[0] = 1.0 - rate
-    coef[1] = rt
-    coef[2], coef[3] = u[1], u[2]
-    coef[4], coef[5] = slope * q[1], slope * q[2]
     for i in range(3):
         whole = None
         for k in range(FACES):
             x = scale * geo_ref[FV + FACES * i + k]
-            coef[6 + FACES * i + k] = x
+            coef[FACES * i + k] = x * geo_ref[LOCAL + k]
             whole = x if whole is None else whole + x
-        coef[24 + i] = whole
-    for k in range(FACES):
-        wall = geo_ref[WALL + k] > 0.5
-        coef[27 + k] = column(sums, EMIT + k) / jnp.where(wall, column(absorbed, ABSORB + k), 1.0)
-
-    first = geo_ref[FIRST]
-
-    def plane_table(a, _):
-        ca = first + a.astype(F32) * H - u[0]
-        za = ca * ca * rt
-        ta[0, a] = height * jnp.exp(-0.5 * za)
-        ta[1, a] = slope * q[0] * ca
-        ta[2, a] = za - 5.0
-        return 0
-
-    lax.fori_loop(0, planes, plane_table, 0, unroll=4)
-
-    def place(g, tile):
-        if last:
-            return (pl.ds(tile * SUB * SUB + g, SUB, stride=SUB), slice(None))
-        return (g, at_rows(tile * SUB), slice(None))
+        coef[3 * FACES + i] = whole
 
     def cell(g, _):
-        source, weight = [], []
+        source = []
         for k in range(FACES):
             j = links_ref[k, g]
-            own = jnp.logical_and(j >= 0, j < SUB)
-            source.append(jnp.where(own, j, g))
-            weight.append([splat(coef, 6 + FACES * i + k, g) * splat(geo_ref, LOCAL + k, g) for i in range(3)])
-        keep, rtg = splat(coef, 0, g), splat(coef, 1, g)
-        ub, uc = splat(coef, 2, g), splat(coef, 3, g)
-        qb, qc = splat(coef, 4, g), splat(coef, 5, g)
-        whole = [splat(coef, 24 + i, g) for i in range(3)]
+            source.append(jnp.where(jnp.logical_and(j >= 0, j < SUB), j, g))
+        weight = [[splat(coef, FACES * i + k, g) for i in range(3)] for k in range(FACES)]
+        whole = [splat(coef, 3 * FACES + i, g) for i in range(3)]
         x0 = splat(geo_ref, FIRST, g)
         for pair in range(TILES // 2):
-            base, bell, heat, zz, stay = [], [], [], [], []
+            base, stay = [], []
             for t in (2 * pair, 2 * pair + 1):
                 xb, xc = tile_nodes(t)
-                cb, cc = xb - ub, xc - uc
-                z = (cb * cb + cc * cc) * rtg
-                bell.append(jnp.exp(-0.5 * z))
-                heat.append(cb * qb + cc * qc)
-                zz.append(z)
                 base.append([weight[k][1] * xb + weight[k][2] * xc for k in range(FACES)])
-                stay.append(keep + whole[1] * xb + whole[2] * xc)
+                stay.append(1.0 + whole[1] * xb + whole[2] * xc)
 
             def plane(a, _):
                 xa = x0 + a.astype(F32) * H
-                height_a, heat_a, z_a = [
-                    jnp.broadcast_to(ta[i, a, pl.ds(g, 1), :], (SUB, LANES)) for i in range(3)
-                ]
                 sa = [weight[k][0] * xa for k in range(FACES)]
                 stay_a = whole[0] * xa
                 for i in range(2):
@@ -526,21 +527,101 @@
                         jnp.maximum(sa[k] + base[i][k], 0.0) * (f_ref[source[k], at, :] - f)
                         for k in range(FACES)
                     ]
-                    target = (height_a * bell[i]) * (1.0 + (heat_a + heat[i]) * (z_a + zz[i]))
                     inflow = (terms[0] + terms[1]) + (terms[2] + terms[3]) + (terms[4] + terms[5])
-                    out_ref[place(g, tile)] = (f * (stay_a + stay[i]) + target) + inflow
+                    out_ref[place(g, tile)] = f * (stay_a + stay[i]) + inflow
                 return 0
 
             lax.fori_loop(0, planes, plane, 0, unroll=4)
+        return 0
+
+    lax.fori_loop(0, SUB, cell, 0)
+
+
+def flux(native, links, geo, f):
+    rows = f.shape[1]
+    return pl.pallas_call(
+        functools.partial(flux_kernel, native),
+        in_specs=[spec(pltpu.SMEM), spec(pltpu.VMEM), spec(pltpu.VMEM)],
+        out_specs=spec(pltpu.VMEM),
+        out_shape=array(SUB * rows, LANES) if native else array(SUB, rows, LANES),
+        scratch_shapes=[
+            pltpu.VMEM((GEO, SUB, LANES), F32),
+            pltpu.VMEM((3 * FACES + 3, SUB, LANES), F32),
+        ],
+        compiler_params=params(),
+        name="flux",
+    )(links, geo, f)
+
+
+def target_kernel(native, count, links_ref, geo_in, absorbed_in, *refs):
+    sums_refs, (f_ref, part_ref, out_ref, sum_out, geo_ref, ta, coef) = refs[:count], refs[count:]
+    planes = f_ref.shape[1] // CHUNKS
+    place = placer(native)
+    unpack_geo(geo_in, geo_ref)
+    sums = add_tiles(sums_refs)
+    sum_out[...] = sums
+    absorbed = sums if absorbed_in is None else absorbed_in[...]
+    n, u, temperature, q = quantities(sums)
+    rt = 1.0 / temperature
+    rate = TIME_STEP * n * temperature / (SHEAR * jnp.exp(POWER * jnp.log(temperature)))
+    height = rate * n * rt * jnp.sqrt(rt)
+    slope = (1.0 / 3.0) / (5.0 * n * temperature * temperature)
+    coef[0] = rate
+    coef[1] = rt
+    coef[2], coef[3] = u[1], u[2]
+    coef[4], coef[5] = slope * q[1], slope * q[2]
+    for k in range(FACES):
+        wall = geo_ref[WALL + k] > 0.5
+        coef[6 + k] = column(sums, EMIT + k) / jnp.where(wall, column(absorbed, ABSORB + k), 1.0)
+    first = geo_ref[FIRST]
+
+    def plane_table(a, _):
+        ca = first + a.astype(F32) * H - u[0]
+        za = ca * ca * rt
+        ta[0, a] = height * jnp.exp(-0.5 * za)
+        ta[1, a] = slope * q[0] * ca
+        ta[2, a] = za - 5.0
+        return 0
+
+    lax.fori_loop(0, planes, plane_table, 0, unroll=4)
+
+    def cell(g, _):
+        rate_g, rtg = splat(coef, 0, g), splat(coef, 1, g)
+        ub, uc = splat(coef, 2, g), splat(coef, 3, g)
+        qb, qc = splat(coef, 4, g), splat(coef, 5, g)
+        x0 = splat(geo_ref, FIRST, g)
+        bell, heat, zz = [], [], []
+        for t in range(TILES):
+            xb, xc = tile_nodes(t)
+            cb, cc = xb - ub, xc - uc
+            z = (cb * cb + cc * cc) * rtg
+            bell.append(jnp.exp(-0.5 * z))
+            heat.append(cb * qb + cc * qc)
+            zz.append(z)
+
+        def plane(a, _):
+            height_a, heat_a, z_a = [
+                jnp.broadcast_to(ta[i, a, pl.ds(g, 1), :], (SUB, LANES)) for i in range(3)
+            ]
+            for t in range(TILES):
+                tile = a * TILES + t
+                where = place(g, tile)
+                f = f_ref[g, at_rows(tile * SUB), :]
+                target = (height_a * bell[t]) * (1.0 + (heat_a + heat[t]) * (z_a + zz[t]))
+                out_ref[where] = (part_ref[where] - rate_g * f) + target
+            return 0
+
+        lax.fori_loop(0, planes, plane, 0, unroll=4)
 
         for k in range(FACES):
 
             @pl.when(links_ref[k, g] == WALL_LINK)
             def _():
                 wt = splat(geo_ref, WT, g)
-                ratio = splat(coef, 27 + k, g)
+                ratio = splat(coef, 6 + k, g)
                 shape = [ratio * x for x in wall_tiles(wt)]
-                v0, v1, v2 = [splat(coef, 6 + FACES * i + k, g) for i in range(3)]
+                scale = -TIME_STEP / splat(geo_ref, VOL, g)
+                v0, v1, v2 = [scale * x for x in face_coefficients(geo_ref, k, g)]
                 base = []
                 for t in range(TILES):
                     xb, xc = tile_nodes(t)
@@ -564,32 +645,30 @@
     lax.fori_loop(0, SUB, cell, 0)
 
 
-def inner(last, links, geo, absorbed, tiles, f):
+def add_target(native, links, geo, absorbed, tiles, f, part):
     rows = f.shape[1]
     vmem = spec(pltpu.VMEM)
-    given = [links, geo] + ([] if absorbed is None else [absorbed]) + list(tiles) + [f]
+    given = [links, geo] + ([] if absorbed is None else [absorbed]) + list(tiles) + [f, part]
 
     def kernel(links_ref, geo_in, *refs):
         if absorbed is None:
-            inner_kernel(last, len(tiles), links_ref, geo_in, None, *refs)
+            target_kernel(native, len(tiles), links_ref, geo_in, None, *refs)
         else:
-            inner_kernel(last, len(tiles), links_ref, geo_in, *refs)
+            target_kernel(native, len(tiles), links_ref, geo_in, *refs)
 
     return pl.pallas_call(
         kernel,
         in_specs=[spec(pltpu.SMEM)] + [vmem] * (len(given) - 1),
         out_specs=[vmem] * 2,
-        out_shape=[
-            array(SUB * rows, LANES) if last else array(SUB, rows, LANES),
-            array(SUB, LANES),
-        ],
+        out_shape=[array(*part.shape), array(SUB, LANES)],
+        input_output_aliases={len(given) - 1: 0},
         scratch_shapes=[
             pltpu.VMEM((GEO, SUB, LANES), F32),
             pltpu.VMEM((3, rows // CHUNKS, SUB, LANES), F32),
-            pltpu.VMEM((27 + FACES, SUB, LANES), F32),
+            pltpu.VMEM((6 + FACES, SUB, LANES), F32),
         ],
         compiler_params=params(),
-        name="inner",
+        name="add_target",
     )(*given)
 
 
@@ -611,24 +690,41 @@
     return low, high
 
 
-def edge_kernel(pairs_ref, before_ref, after_ref, old_ref, part_ref, f_ref, up_ref, down_ref):
-    def group(j, _):
-        at = at_rows(j * SUB)
-        low, high = halo_terms(pairs_ref, before_ref, after_ref, old_ref, at)
-        for g in range(REACH):
-            x = part_ref[g, at, :] + low[g]
-            down_ref[g, at, :] = x
-            f_ref[g, at, :] = x
-            e = SUB - REACH + g
-            x = part_ref[e, at, :] + high[g]
-            up_ref[g, at, :] = x
-            f_ref[e, at, :] = x
-        return 0
-
-    lax.fori_loop(0, part_ref.shape[1] // SUB, group, 0, unroll=2)
-
-
-def edge(pairs, before, after, old, part):
+def by_side(far_ref, near_ref, run):
+    odd = is_odd()
+
+    @pl.when(odd)
+    def _():
+        run(near_ref, far_ref)
+
+    @pl.when(jnp.logical_not(odd))
+    def _():
+        run(far_ref, near_ref)
+
+
+def edge_kernel(pairs_ref, far_in, near_in, old_ref, part_ref, f_ref, far_out, near_out):
+    def run(before_ref, after_ref):
+        down_out, up_out = (near_out, far_out) if after_ref is far_in else (far_out, near_out)
+
+        def group(j, _):
+            at = at_rows(j * SUB)
+            low, high = halo_terms(pairs_ref, before_ref, after_ref, old_ref, at)
+            for g in range(REACH):
+                x = part_ref[g, at, :] + low[g]
+                down_out[g, at, :] = x
+                f_ref[g, at, :] = x
+                e = SUB - REACH + g
+                x = part_ref[e, at, :] + high[g]
+                up_out[g, at, :] = x
+                f_ref[e, at, :] = x
+            return 0
+
+        lax.fori_loop(0, part_ref.shape[1] // SUB, group, 0, unroll=2)
+
+    by_side(far_in, near_in, run)
+
+
+def edge(pairs, far, near, old, part):
     rows = part.shape[1]
     return pl.pallas_call(
         edge_kernel,
@@ -638,43 +734,47 @@
         input_output_aliases={4: 0},
         compiler_params=params(),
         name="edge",
-    )(pairs, before, after, old, part)
+    )(pairs, far, near, old, part)
 
 
 def last_edge_kernel(
-    geo_in, pairs_ref, before_ref, after_ref, f_ref, part_ref, out_hbm, sums_out, native_ref, sems
+    geo_in, pairs_ref, far_ref, near_ref, f_ref, part_ref, out_hbm, sums_out, native_ref, sems
 ):
     rows = part_ref.shape[0] // SUB
     planes = rows // CHUNKS
-    tiles = rows // SUB
-    part = tiles // LAST_PARTS
-    copies = []
-    for i in range(LAST_PARTS):
-
-        def group(j, _):
-            at = at_rows(j * SUB)
-            low, high = halo_terms(pairs_ref, before_ref, after_ref, f_ref, at)
-            terms = low + [None] * (SUB - 2 * REACH) + high
-            for g in range(SUB):
-                where = (pl.ds(j * SUB * SUB + g, SUB, stride=SUB), slice(None))
-                x = part_ref[where]
-                native_ref[where] = x if terms[g] is None else x + terms[g]
-            return 0
-
-        lax.fori_loop(i * part, (i + 1) * part, group, 0, unroll=2)
+    part = rows // SUB // LAST_PARTS
+
+    def copy(i):
         at = pl.ds(i * part * SUB * SUB, part * SUB * SUB)
-        copies.append(pltpu.make_async_copy(native_ref.at[at], out_hbm.at[at], sems.at[i]))
-        copies[-1].start()
+        return pltpu.make_async_copy(native_ref.at[at], out_hbm.at[at], sems.at[i])
+
+    def run(before_ref, after_ref):
+        for i in range(LAST_PARTS):
+
+            def group(j, _):
+                at = at_rows(j * SUB)
+                low, high = halo_terms(pairs_ref, before_ref, after_ref, f_ref, at)
+                terms = low + [None] * (SUB - 2 * REACH) + high
+                for g in range(SUB):
+                    where = (pl.ds(j * SUB * SUB + g, SUB, stride=SUB), slice(None))
+                    x = part_ref[where]
+                    native_ref[where] = x if terms[g] is None else x + terms[g]
+                return 0
+
+            lax.fori_loop(i * part, (i + 1) * part, group, 0, unroll=2)
+            copy(i).start()
+
+    by_side(far_ref, near_ref, run)
     y = native_polynomial_sums(native_ref, planes)
     sums_out[...] = pack_sums(finish_polynomials(y, column(geo_in[...], FIRST), planes), 0)
-    for c in copies:
-        c.wait()
+    for i in range(LAST_PARTS):
+        copy(i).wait()
 
 
 LAST_PARTS = 4
 
 
-def last_edge(geo, pairs, before, after, f, part):
+def last_edge(geo, pairs, far, near, f, part):
     return pl.pallas_call(
         last_edge_kernel,
         in_specs=[spec(pltpu.VMEM)] * 6,
@@ -683,14 +783,16 @@
         scratch_shapes=[pltpu.VMEM(part.shape, F32), pltpu.SemaphoreType.DMA((LAST_PARTS,))],
         compiler_params=params(),
         name="last_edge",
-    )(geo, pairs, before, after, f, part)
-
-
-def exchange(up, down):
+    )(geo, pairs, far, near, f, part)
+
+
+def exchange(far, near):
     size = lax.axis_size("space")
-    forward = [(i, i + 1) for i in range(size - 1)]
-    backward = [(i + 1, i) for i in range(size - 1)]
-    return lax.ppermute(up, "space", forward), lax.ppermute(down, "space", backward)
+    out = []
+    for x, start in ((far, 1), (near, 0)):
+        pairs = [(i, i + 1) for i in range(start, size - 1, 2)]
+        out.append(lax.ppermute(x, "space", pairs + [(j, i) for i, j in pairs]))
+    return out
 
 
 def per_device(particle_profile, neighbors, face_vectors, volumes, wall_temp):
@@ -713,16 +815,19 @@
         ]
     )
     geo = jnp.pad(geo.T, ((0, 0), (0, LANES - GEO)))
-    f, up, down = split_profile(pltpu.with_memory_space_constraint(native, pltpu.HBM))
-    before, after = exchange(up, down)
-    tiles = gather_sums(local_sums(True, links, geo, f))
+    native, far, near = first_rows(native)
+    far, near = exchange(far, near)
+    f, sums = first_sums(links, geo, native)
+    tiles = gather_sums(sums)
     pairs = geometry(links, geo, rows)
-    part, absorbed = inner(False, links, geo, None, tiles, f)
-    f, up, down = edge(pairs, before, after, f, part)
-    before, after = exchange(up, down)
-    tiles = gather_sums(local_sums(False, links, geo, f))
-    part, _ = inner(True, links, geo, absorbed, tiles, f)
-    native, sums = last_edge(geo, pairs, before, after, f, part)
+    part = flux(False, links, geo, f)
+    part, absorbed = add_target(False, links, geo, None, tiles, f, part)
+    f, far, near = edge(pairs, far, near, f, part)
+    far, near = exchange(far, near)
+    tiles = gather_sums(local_sums(links, geo, f))
+    part = flux(True, links, geo, f)
+    part, _ = add_target(True, links, geo, absorbed, tiles, f, part)
+    native, sums = last_edge(geo, pairs, far, near, f, part)
     macro_quantities = macro(gather_sums(sums))
     evolved = native.reshape(rows, cells, LANES).transpose(1, 0, 2).reshape(cells, points)
     return evolved, macro_quantities

time: 63.2 us -> 63.4 us (level)
  the two profiles are of different devices: /device:TPU:1 before, /device:TPU:4 now
where the time goes in v3:
time: 63.4 us; the launch traced here: 62.2 us
  Pallas kernels  32.1 us (51%)
  starting transfers between devices  20.6 us (32%)
  waiting for transfers between devices  6.96 us (11%)
  local copies, waits for them, and re-layouts  1.68 us (3%)
  between operations  0.82 us (1%)
    ppermute x9, starting transfers between devices, gather_sums(): lax.ppermute(tile, 'vel', [(i, i ^ s) for i in range(size)])  13.3 us
    pallas_call x2, Pallas kernels, add_target(): pl.pallas_call(kernel, in_specs=[spec(pltpu.SMEM)] + [vmem] * (len(given)...  8.81 us
    pallas_call x2, Pallas kernels, flux(): pl.pallas_call(functools.partial(flux_kernel, native), in_specs=[spec(plt...  8.06 us
    ppermute x4, starting transfers between devices, exchange(): out.append(lax.ppermute(x, 'space', pairs + [(j, i) for i, j in pairs]))  7.3 us
    ppermute x9, waiting for transfers between devices, gather_sums(): lax.ppermute(tile, 'vel', [(i, i ^ s) for i in range(size)])  3.73 us
    ppermute x4, waiting for transfers between devices, exchange(): out.append(lax.ppermute(x, 'space', pairs + [(j, i) for i, j in pairs]))  3.23 us
    pallas_call x1, Pallas kernels, first_rows(): pl.pallas_call(first_rows_kernel, in_specs=[spec(pltpu.HBM)], out_specs=[...  2.8 us
    pallas_call x1, Pallas kernels, first_sums(): pl.pallas_call(first_sums_kernel, in_specs=[spec(pltpu.SMEM), spec(pltpu....  2.58 us
  transfers between devices with their start and end apart: 13, of which 4 were waited for; matrix products, arithmetic and copies ran while one was open for 1% of the time, Pallas kernels for 38%

profile of v3, /device:TPU:4, one launch (start us, length us, event | category | flops | bytes accessed | tf_op | source)
XLA Modules:
  0.0 62.2 jit_solution(16269012460657749634)
XLA Ops:
  0.6 0.0 copy-start.5
  0.6 0.0 copy-start.6
  0.7 2.8 %first_rows.1 = (f32[4096,128]{1,0:T(8,128)S(1)}, f32[3,512,128]{2,1,0:T(8,128)}, f32[3,512,128]{2,1,0:T(8,128)}) custom-call(f32[4096,128]{1,0:T(8,128)} %bitcast.13), custom_call_target="tpu_custom_call" | custom-call | tf_op jit(solution)/shard_map/first_rows/pallas_call | solution.py:362
  3.5 2.8 %collective-permute-start = (f32[3,512,128]{2,1,0:T(8,128)}, f32[3,512,128]{2,1,0:T(8,128)S(1)}, u32[]{:S(2)}, u32[]{:S(2)}) collective-permute-start(f32[3,512,128]{2,1,0:T(8,128)} %get-tuple-element.15), channel_id=1, source_target_pairs={{4,8},{12,16},{20,24},{8,4},{16,12},{24,20},{5,9},{13,17},{21,25},... | collective-permute-start | bytes 2359304 | tf_op jit(solution)/shard_map/ppermute | solution.py:794
  6.3 0.8 %collective-permute-start.1 = (f32[3,512,128]{2,1,0:T(8,128)}, f32[3,512,128]{2,1,0:T(8,128)}, u32[]{:S(2)}, u32[]{:S(2)}) collective-permute-start(f32[3,512,128]{2,1,0:T(8,128)} %get-tuple-element.16), channel_id=1, source_target_pairs={{0,4},{8,12},{16,20},{24,28},{4,0},{12,8},{20,16},{28,24},{1,5},{9... | collective-permute-start | bytes 2359304 | tf_op jit(solution)/shard_map/ppermute | solution.py:794
  7.1 0.1 copy.23
  7.1 0.1 copy.25
  7.2 0.1 copy.26
  7.3 0.1 copy.27.links_ref
  7.4 0.1 copy.34
  7.5 0.1 concatenate.3
  7.6 2.6 %first_sums.1 = (f32[8,512,128]{2,1,0:T(8,128)S(1)}, f32[8,128]{1,0:T(8,128)S(1)}) custom-call(s32[6,8]{1,0:T(8,128)S(1)} %copy.27.links_ref, f32[8,128]{1,0:T(8,128)S(1)} %pad.4.geo_in, f32[4096,128]{1,0:T(8,128)S(1)} %get-tuple-element.17.native_ref), custom_call_target="tpu_custom_call" | custom-call | tf_op jit(solution)/shard_map/first_sums/pallas_call | solution.py:310
  10.2 3.7 %collective-permute-start.4 = (f32[8,128]{1,0:T(8,128)S(1)}, f32[8,128]{1,0:T(8,128)S(1)}, u32[]{:S(2)}, u32[]{:S(2)}) collective-permute-start(f32[8,128]{1,0:T(8,128)S(1)} %get-tuple-element.19.refs_0_), channel_id=1, source_target_pairs={{0,3},{1,2},{2,1},{3,0},{4,7},{5,6},{6,5},{7,4},{8,11},{9,10},{10,... | collective-permute-start | bytes 12296 | tf_op jit(solution)/shard_map/ppermute | solution.py:434
  13.8 0.0 collective-permute-start.3
  13.8 0.8 %collective-permute-start.2 = (f32[8,128]{1,0:T(8,128)S(1)}, f32[8,128]{1,0:T(8,128)S(1)}, u32[]{:S(2)}, u32[]{:S(2)}) collective-permute-start(f32[8,128]{1,0:T(8,128)S(1)} %get-tuple-element.19.refs_0_), channel_id=1, source_target_pairs={{0,1},{1,0},{2,3},{3,2},{4,5},{5,4},{6,7},{7,6},{8,9},{9,8},{10,11... | collective-permute-start | bytes 12296 | tf_op jit(solution)/shard_map/ppermute | solution.py:434
  14.6 2.2 %geometry.1.pairs_ref = f32[12,512,128]{2,1,0:T(8,128)S(1)} custom-call(s32[6,8]{1,0:T(8,128)S(1)} %copy.27.links_ref, f32[8,128]{1,0:T(8,128)S(1)} %pad.4.geo_in), custom_call_target="tpu_custom_call" | custom-call | tf_op jit(solution)/shard_map/geometry/pallas_call | solution.py:419
  16.8 4.0 %flux.2.refs_5_ = f32[8,512,128]{2,1,0:T(8,128)S(1)} custom-call(s32[6,8]{1,0:T(8,128)S(1)} %copy.27.links_ref, f32[8,128]{1,0:T(8,128)S(1)} %pad.4.geo_in, f32[8,512,128]{2,1,0:T(8,128)S(1)} %get-tuple-element.18.f_ref.refs_4_.old_ref), custom_call_target="tpu_custom_call" | custom-call | tf_op jit(solution)/shard_map/flux/pallas_call | solution.py:542
  20.8 0.0 collective-permute-done.4.refs_3_
  20.8 0.0 collective-permute-done.3.refs_2_
  20.9 0.0 collective-permute-done.2.refs_1_
  20.9 3.6 %add_target.2 = (f32[8,512,128]{2,1,0:T(8,128)S(1)}, f32[8,128]{1,0:T(8,128)S(1)}) custom-call(s32[6,8]{1,0:T(8,128)S(1)} %copy.27.links_ref, f32[8,128]{1,0:T(8,128)S(1)} %pad.4.geo_in, f32[8,128]{1,0:T(8,128)S(1)} %get-tuple-element.19.refs_0_, f32[8,128]{1,0:T(8,128)S(1)} %collective-permute-done.2.refs_1_, ...), custom_call_target="tpu_custom_call", output_to_operand_aliasing={{0}: (7, {})} | custom-call | tf_op jit(solution)/shard_map/add_target/pallas_call | solution.py:659
  24.5 1.0 %collective-permute-done.far_in = f32[3,512,128]{2,1,0:T(8,128)S(1)} collective-permute-done((f32[3,512,128]{2,1,0:T(8,128)}, f32[3,512,128]{2,1,0:T(8,128)S(1)}, u32[]{:S(2)}, u32[]{:S(2)}) %collective-permute-start) | collective-permute-done | bytes 786464 | tf_op jit(solution)/shard_map/ppermute | solution.py:794
  25.4 0.0 collective-permute-done.1.near_in
  25.4 2.3 %edge.1 = (f32[8,512,128]{2,1,0:T(8,128)S(1)}, f32[3,512,128]{2,1,0:T(8,128)S(1)}, f32[3,512,128]{2,1,0:T(8,128)S(1)}) custom-call(f32[12,512,128]{2,1,0:T(8,128)S(1)} %geometry.1.pairs_ref, f32[3,512,128]{2,1,0:T(8,128)S(1)} %collective-permute-done.far_in, f32[3,512,128]{2,1,0:T(8,128)} %collective-permute-done.1.near_in, ...), custom_call_target="tpu_custom_call", output_to_operand_aliasing={{0}: (4, {})} | custom-call | tf_op jit(solution)/shard_map/edge/pallas_call | solution.py:729
  27.7 3.6 %collective-permute-start.5 = (f32[3,512,128]{2,1,0:T(8,128)S(1)}, f32[3,512,128]{2,1,0:T(8,128)S(1)}, u32[]{:S(2)}, u32[]{:S(2)}) collective-permute-start(f32[3,512,128]{2,1,0:T(8,128)S(1)} %get-tuple-element.21), channel_id=1, source_target_pairs={{4,8},{12,16},{20,24},{8,4},{16,12},{24,20},{5,9},{13,17},{21,25},... | collective-permute-start | bytes 2359304 | tf_op jit(solution)/shard_map/ppermute | solution.py:794
  31.4 0.1 collective-permute-start.6
  31.5 2.0 %local_sums.1.refs_1_ = f32[8,128]{1,0:T(8,128)S(1)} custom-call(s32[6,8]{1,0:T(8,128)S(1)} %copy.27.links_ref, f32[8,128]{1,0:T(8,128)S(1)} %pad.4.geo_in, f32[8,512,128]{2,1,0:T(8,128)S(1)} %get-tuple-element.23.f_ref.refs_5_), custom_call_target="tpu_custom_call" | custom-call | tf_op jit(solution)/shard_map/local_sums/pallas_call | solution.py:293
  33.5 3.6 %collective-permute-start.9 = (f32[8,128]{1,0:T(8,128)S(1)}, f32[8,128]{1,0:T(8,128)S(1)}, u32[]{:S(2)}, u32[]{:S(2)}) collective-permute-start(f32[8,128]{1,0:T(8,128)S(1)} %local_sums.1.refs_1_), channel_id=1, source_target_pairs={{0,3},{1,2},{2,1},{3,0},{4,7},{5,6},{6,5},{7,4},{8,11},{9,10},{10,... | collective-permute-start | bytes 12296 | tf_op jit(solution)/shard_map/ppermute | solution.py:434
  37.1 0.0 collective-permute-start.8
  37.1 0.8 %collective-permute-start.7 = (f32[8,128]{1,0:T(8,128)S(1)}, f32[8,128]{1,0:T(8,128)S(1)}, u32[]{:S(2)}, u32[]{:S(2)}) collective-permute-start(f32[8,128]{1,0:T(8,128)S(1)} %local_sums.1.refs_1_), channel_id=1, source_target_pairs={{0,1},{1,0},{2,3},{3,2},{4,5},{5,4},{6,7},{7,6},{8,9},{9,8},{10,11... | collective-permute-start | bytes 12296 | tf_op jit(solution)/shard_map/ppermute | solution.py:434
  37.9 4.1 %flux.3.refs_6_ = f32[4096,128]{1,0:T(8,128)S(1)} custom-call(s32[6,8]{1,0:T(8,128)S(1)} %copy.27.links_ref, f32[8,128]{1,0:T(8,128)S(1)} %pad.4.geo_in, f32[8,512,128]{2,1,0:T(8,128)S(1)} %get-tuple-element.23.f_ref.refs_5_), custom_call_target="tpu_custom_call" | custom-call | tf_op jit(solution)/shard_map/flux/pallas_call | solution.py:542
  41.9 0.0 collective-permute-done.9.refs_4_
  42.0 0.0 collective-permute-done.8.refs_3_
  42.0 0.0 collective-permute-done.7.refs_2_
  42.0 5.2 %add_target.3 = (f32[4096,128]{1,0:T(8,128)S(1)}, f32[8,128]{1,0:T(8,128)}) custom-call(s32[6,8]{1,0:T(8,128)S(1)} %copy.27.links_ref, f32[8,128]{1,0:T(8,128)S(1)} %pad.4.geo_in, f32[8,128]{1,0:T(8,128)S(1)} %get-tuple-element.24.refs_0_, f32[8,128]{1,0:T(8,128)S(1)} %local_sums.1.refs_1_, ...), custom_call_target="tpu_custom_call", output_to_operand_aliasing={{0}: (8, {})} | custom-call | tf_op jit(solution)/shard_map/add_target/pallas_call | solution.py:659
  47.2 2.3 %collective-permute-done.5.far_ref = f32[3,512,128]{2,1,0:T(8,128)S(1)} collective-permute-done((f32[3,512,128]{2,1,0:T(8,128)S(1)}, f32[3,512,128]{2,1,0:T(8,128)S(1)}, u32[]{:S(2)}, u32[]{:S(2)}) %collective-permute-start.5) | collective-permute-done | bytes 786464 | tf_op jit(solution)/shard_map/ppermute | solution.py:794
  49.5 0.0 collective-permute-done.6.near_ref
  49.5 1.9 %last_edge.1 = (f32[4096,128]{1,0:T(8,128)}, f32[8,128]{1,0:T(8,128)S(1)}) custom-call(f32[8,128]{1,0:T(8,128)S(1)} %pad.4.geo_in, f32[12,512,128]{2,1,0:T(8,128)S(1)} %geometry.1.pairs_ref, f32[3,512,128]{2,1,0:T(8,128)S(1)} %collective-permute-done.5.far_ref, f32[3,512,128]{2,1,0:T(8,128)S(1)} %collective-permute-done.6.near_ref, ...), custom_call_target="tpu_custom_call" | custom-call | tf_op jit(solution)/shard_map/last_edge/pallas_call | solution.py:778
  51.4 3.7 %collective-permute-start.12 = (f32[8,128]{1,0:T(8,128)S(1)}, f32[8,128]{1,0:T(8,128)S(1)}, u32[]{:S(2)}, u32[]{:S(2)}) collective-permute-start(f32[8,128]{1,0:T(8,128)S(1)} %get-tuple-element.27.refs_0_), channel_id=1, source_target_pairs={{0,3},{1,2},{2,1},{3,0},{4,7},{5,6},{6,5},{7,4},{8,11},{9,10},{10,... | collective-permute-start | bytes 12296 | tf_op jit(solution)/shard_map/ppermute | solution.py:434
  55.1 0.0 collective-permute-start.11
  55.1 0.8 %collective-permute-start.10 = (f32[8,128]{1,0:T(8,128)S(1)}, f32[8,128]{1,0:T(8,128)S(1)}, u32[]{:S(2)}, u32[]{:S(2)}) collective-permute-start(f32[8,128]{1,0:T(8,128)S(1)} %get-tuple-element.27.refs_0_), channel_id=1, source_target_pairs={{0,1},{1,0},{2,3},{3,2},{4,5},{5,4},{6,7},{7,6},{8,9},{9,8},{10,11... | collective-permute-start | bytes 12296 | tf_op jit(solution)/shard_map/ppermute | solution.py:434
  55.9 1.0 %collective-permute-done.12.refs_3_ = f32[8,128]{1,0:T(8,128)S(1)} collective-permute-done((f32[8,128]{1,0:T(8,128)S(1)}, f32[8,128]{1,0:T(8,128)S(1)}, u32[]{:S(2)}, u32[]{:S(2)}) %collective-permute-start.12) | collective-permute-done | bytes 4128 | tf_op jit(solution)/shard_map/ppermute | solution.py:434
  56.9 2.7 %collective-permute-done.11.refs_2_ = f32[8,128]{1,0:T(8,128)S(1)} collective-permute-done((f32[8,128]{1,0:T(8,128)S(1)}, f32[8,128]{1,0:T(8,128)S(1)}, u32[]{:S(2)}, u32[]{:S(2)}) %collective-permute-start.11) | collective-permute-done | bytes 4128 | tf_op jit(solution)/shard_map/ppermute | solution.py:434
  59.6 0.0 collective-permute-done.10.refs_1_
  59.6 0.0 copy-done
  59.6 0.6 copy-done.3
  60.2 0.6 copy-done.4
  60.8 1.4 %macro.1 = f32[8,8]{1,0:T(8,128)} custom-call(f32[8,128]{1,0:T(8,128)} %copy-done, f32[8,128]{1,0:T(8,128)} %copy-done.4, f32[8,128]{1,0:T(8,128)} %copy-done.3, f32[8,128]{1,0:T(8,128)} %copy-done.2), custom_call_target="tpu_custom_call" | custom-call | tf_op jit(solution)/shard_map/macro/pallas_call | solution.py:472
  (15 shorter events, 0.0 us)
Async XLA Ops:
  0.6 6.4 %copy-start.5 = (s32[6,8]{1,0:T(8,128)S(1)}, s32[6,8]{1,0:T(8,128)}, u32[]{:S(2)}) copy-start(s32[6,8]{1,0:T(8,128)} %param.6) | copy-start | bytes 580
  0.6 6.5 %copy-start.6 = (f32[8]{0:T(128)S(1)}, f32[8]{0:T(128)}, u32[]{:S(2)}) copy-start(f32[8]{0:T(128)} %param.8) | copy-start | bytes 100
  0.7 6.6 %copy-start.7 = (f32[8]{0:T(128)S(1)}, f32[8]{0:T(128)}, u32[]{:S(2)}) copy-start(f32[8]{0:T(128)} %param.9) | copy-start | bytes 100
  0.7 6.7 %copy-start.1 = (f32[3,6,8]{2,1,0:T(8,128)S(1)}, f32[3,6,8]{2,1,0:T(8,128)}, u32[]{:S(2)}) copy-start(f32[3,6,8]{2,1,0:T(8,128)} %param.7) | copy-start | bytes 1732
  3.5 21.9 %collective-permute-start = (f32[3,512,128]{2,1,0:T(8,128)}, f32[3,512,128]{2,1,0:T(8,128)S(1)}, u32[]{:S(2)}, u32[]{:S(2)}) collective-permute-start(f32[3,512,128]{2,1,0:T(8,128)} %get-tuple-element.15), channel_id=1, source_target_pairs={{4,8},{12,16},{20,24},{8,4},{16,12},{24,20},{5,9},{13,17},{21,25},... | collective-permute-start | bytes 2359304 | tf_op jit(solution)/shard_map/ppermute | solution.py:794
  6.3 19.2 %collective-permute-start.1 = (f32[3,512,128]{2,1,0:T(8,128)}, f32[3,512,128]{2,1,0:T(8,128)}, u32[]{:S(2)}, u32[]{:S(2)}) collective-permute-start(f32[3,512,128]{2,1,0:T(8,128)} %get-tuple-element.16), channel_id=1, source_target_pairs={{0,4},{8,12},{16,20},{24,28},{4,0},{12,8},{20,16},{28,24},{1,5},{9... | collective-permute-start | bytes 2359304 | tf_op jit(solution)/shard_map/ppermute | solution.py:794
  10.2 10.7 %collective-permute-start.4 = (f32[8,128]{1,0:T(8,128)S(1)}, f32[8,128]{1,0:T(8,128)S(1)}, u32[]{:S(2)}, u32[]{:S(2)}) collective-permute-start(f32[8,128]{1,0:T(8,128)S(1)} %get-tuple-element.19.refs_0_), channel_id=1, source_target_pairs={{0,3},{1,2},{2,1},{3,0},{4,7},{5,6},{6,5},{7,4},{8,11},{9,10},{10,... | collective-permute-start | bytes 12296 | tf_op jit(solution)/shard_map/ppermute | solution.py:434
  13.8 7.0 %collective-permute-start.3 = (f32[8,128]{1,0:T(8,128)S(1)}, f32[8,128]{1,0:T(8,128)S(1)}, u32[]{:S(2)}, u32[]{:S(2)}) collective-permute-start(f32[8,128]{1,0:T(8,128)S(1)} %get-tuple-element.19.refs_0_), channel_id=1, source_target_pairs={{0,2},{1,3},{2,0},{3,1},{4,6},{5,7},{6,4},{7,5},{8,10},{9,11},{10,... | collective-permute-start | bytes 12296 | tf_op jit(solution)/shard_map/ppermute | solution.py:434
  13.8 7.0 %collective-permute-start.2 = (f32[8,128]{1,0:T(8,128)S(1)}, f32[8,128]{1,0:T(8,128)S(1)}, u32[]{:S(2)}, u32[]{:S(2)}) collective-permute-start(f32[8,128]{1,0:T(8,128)S(1)} %get-tuple-element.19.refs_0_), channel_id=1, source_target_pairs={{0,1},{1,0},{2,3},{3,2},{4,5},{5,4},{6,7},{7,6},{8,9},{9,8},{10,11... | collective-permute-start | bytes 12296 | tf_op jit(solution)/shard_map/ppermute | solution.py:434
  27.7 21.7 %collective-permute-start.5 = (f32[3,512,128]{2,1,0:T(8,128)S(1)}, f32[3,512,128]{2,1,0:T(8,128)S(1)}, u32[]{:S(2)}, u32[]{:S(2)}) collective-permute-start(f32[3,512,128]{2,1,0:T(8,128)S(1)} %get-tuple-element.21), channel_id=1, source_target_pairs={{4,8},{12,16},{20,24},{8,4},{16,12},{24,20},{5,9},{13,17},{21,25},... | collective-permute-start | bytes 2359304 | tf_op jit(solution)/shard_map/ppermute | solution.py:794
  31.4 18.1 %collective-permute-start.6 = (f32[3,512,128]{2,1,0:T(8,128)S(1)}, f32[3,512,128]{2,1,0:T(8,128)S(1)}, u32[]{:S(2)}, u32[]{:S(2)}) collective-permute-start(f32[3,512,128]{2,1,0:T(8,128)S(1)} %get-tuple-element.22), channel_id=1, source_target_pairs={{0,4},{8,12},{16,20},{24,28},{4,0},{12,8},{20,16},{28,24},{1,5},{9... | collective-permute-start | bytes 2359304 | tf_op jit(solution)/shard_map/ppermute | solution.py:794
  33.5 8.5 %collective-permute-start.9 = (f32[8,128]{1,0:T(8,128)S(1)}, f32[8,128]{1,0:T(8,128)S(1)}, u32[]{:S(2)}, u32[]{:S(2)}) collective-permute-start(f32[8,128]{1,0:T(8,128)S(1)} %local_sums.1.refs_1_), channel_id=1, source_target_pairs={{0,3},{1,2},{2,1},{3,0},{4,7},{5,6},{6,5},{7,4},{8,11},{9,10},{10,... | collective-permute-start | bytes 12296 | tf_op jit(solution)/shard_map/ppermute | solution.py:434
  37.1 4.9 %collective-permute-start.8 = (f32[8,128]{1,0:T(8,128)S(1)}, f32[8,128]{1,0:T(8,128)S(1)}, u32[]{:S(2)}, u32[]{:S(2)}) collective-permute-start(f32[8,128]{1,0:T(8,128)S(1)} %local_sums.1.refs_1_), channel_id=1, source_target_pairs={{0,2},{1,3},{2,0},{3,1},{4,6},{5,7},{6,4},{7,5},{8,10},{9,11},{10,... | collective-permute-start | bytes 12296 | tf_op jit(solution)/shard_map/ppermute | solution.py:434
  37.1 4.9 %collective-permute-start.7 = (f32[8,128]{1,0:T(8,128)S(1)}, f32[8,128]{1,0:T(8,128)S(1)}, u32[]{:S(2)}, u32[]{:S(2)}) collective-permute-start(f32[8,128]{1,0:T(8,128)S(1)} %local_sums.1.refs_1_), channel_id=1, source_target_pairs={{0,1},{1,0},{2,3},{3,2},{4,5},{5,4},{6,7},{7,6},{8,9},{9,8},{10,11... | collective-permute-start | bytes 12296 | tf_op jit(solution)/shard_map/ppermute | solution.py:434
  51.4 8.2 %copy-start = (f32[8,128]{1,0:T(8,128)}, f32[8,128]{1,0:T(8,128)S(1)}, u32[]{:S(2)}) copy-start(f32[8,128]{1,0:T(8,128)S(1)} %get-tuple-element.27.refs_0_) | copy-start | bytes 12292
  51.4 5.5 %collective-permute-start.12 = (f32[8,128]{1,0:T(8,128)S(1)}, f32[8,128]{1,0:T(8,128)S(1)}, u32[]{:S(2)}, u32[]{:S(2)}) collective-permute-start(f32[8,128]{1,0:T(8,128)S(1)} %get-tuple-element.27.refs_0_), channel_id=1, source_target_pairs={{0,3},{1,2},{2,1},{3,0},{4,7},{5,6},{6,5},{7,4},{8,11},{9,10},{10,... | collective-permute-start | bytes 12296 | tf_op jit(solution)/shard_map/ppermute | solution.py:434
  55.1 4.5 %collective-permute-start.11 = (f32[8,128]{1,0:T(8,128)S(1)}, f32[8,128]{1,0:T(8,128)S(1)}, u32[]{:S(2)}, u32[]{:S(2)}) collective-permute-start(f32[8,128]{1,0:T(8,128)S(1)} %get-tuple-element.27.refs_0_), channel_id=1, source_target_pairs={{0,2},{1,3},{2,0},{3,1},{4,6},{5,7},{6,4},{7,5},{8,10},{9,11},{10,... | collective-permute-start | bytes 12296 | tf_op jit(solution)/shard_map/ppermute | solution.py:434
  55.1 4.5 %collective-permute-start.10 = (f32[8,128]{1,0:T(8,128)S(1)}, f32[8,128]{1,0:T(8,128)S(1)}, u32[]{:S(2)}, u32[]{:S(2)}) collective-permute-start(f32[8,128]{1,0:T(8,128)S(1)} %get-tuple-element.27.refs_0_), channel_id=1, source_target_pairs={{0,1},{1,0},{2,3},{3,2},{4,5},{5,4},{6,7},{7,6},{8,9},{9,8},{10,11... | collective-permute-start | bytes 12296 | tf_op jit(solution)/shard_map/ppermute | solution.py:434
  56.9 2.7 %copy-start.2 = (f32[8,128]{1,0:T(8,128)}, f32[8,128]{1,0:T(8,128)S(1)}, u32[]{:S(2)}) copy-start(f32[8,128]{1,0:T(8,128)S(1)} %collective-permute-done.12.refs_3_) | copy-start | bytes 12292
  59.6 0.6 copy-start.3
  60.2 0.6 copy-start.4

commit v4 on v3

--- a/solution.py
+++ b/solution.py
@@ -328,7 +328,7 @@
     return lax.rem(lax.axis_index("space"), 2) == 1
 
 
-def first_rows_kernel(native_hbm, native_ref, far_ref, near_ref, sems):
+def first_rows_kernel(native_hbm, native_ref, far1_ref, far2_ref, near_ref, sems):
     rows = native_ref.shape[0]
     part = rows // SPLIT_PARTS
     copies = [
@@ -347,14 +347,22 @@
     for i, c in enumerate(copies):
         c.wait()
 
+        far_ref = (far1_ref, far2_ref)[2 * i // SPLIT_PARTS]
+        begin = far_ref.shape[1] // SUB * (2 * i // SPLIT_PARTS)
+
         def group(j, _):
             for r in range(REACH):
-                at = at_rows(j * SUB)
-                far_ref[r, at, :] = native_ref[pl.ds(j * SUB * SUB + far + r, SUB, stride=SUB), :]
-                near_ref[r, at, :] = native_ref[pl.ds(j * SUB * SUB + near + r, SUB, stride=SUB), :]
+                x = native_ref[pl.ds(j * SUB * SUB + far + r, SUB, stride=SUB), :]
+                far_ref[r, at_rows((j - begin) * SUB), :] = x
+                x = native_ref[pl.ds(j * SUB * SUB + near + r, SUB, stride=SUB), :]
+                near_ref[r, at_rows(j * SUB), :] = x
             return 0
 
         lax.fori_loop(i * groups, (i + 1) * groups, group, 0, unroll=4)
+
+
+def halo_arrays(rows):
+    return [array(REACH, rows // 2, LANES), array(REACH, rows // 2, LANES), array(REACH, rows, LANES)]
 
 
 def first_rows(native):
@@ -362,8 +370,8 @@
     return pl.pallas_call(
         first_rows_kernel,
         in_specs=[spec(pltpu.HBM)],
-        out_specs=[spec(pltpu.VMEM)] * 3,
-        out_shape=[array(*native.shape), array(REACH, rows, LANES), array(REACH, rows, LANES)],
+        out_specs=[spec(pltpu.VMEM)] * 4,
+        out_shape=[array(*native.shape)] + halo_arrays(rows),
         scratch_shapes=[pltpu.SemaphoreType.DMA((SPLIT_PARTS,))],
         compiler_params=params(),
         name="first_rows",
@@ -672,88 +680,111 @@
     )(*given)
 
 
-def halo_terms(pairs_ref, before_ref, after_ref, f_ref, at):
+def halo_terms(pairs_ref, before, after, f_ref, at):
     low, high = [None] * REACH, [None] * REACH
-    rows = [before_ref[r, at, :] for r in range(REACH)]
     own = [f_ref[g, at, :] for g in range(REACH)]
     for p, (g, r) in enumerate(BEFORE_PAIRS):
-        term = pairs_ref[p, at, :] * (rows[r] - own[g])
+        term = pairs_ref[p, at, :] * (before[r] - own[g])
         low[g] = term if low[g] is None else low[g] + term
-    rows = [after_ref[r, at, :] for r in range(REACH)]
     own = [f_ref[SUB - REACH + e, at, :] for e in range(REACH)]
     p = len(BEFORE_PAIRS)
     for e in range(REACH):
         for r in range(e + 1):
-            term = pairs_ref[p, at, :] * (rows[r] - own[e])
+            term = pairs_ref[p, at, :] * (after[r] - own[e])
             high[e] = term if high[e] is None else high[e] + term
             p += 1
     return low, high
 
 
-def by_side(far_ref, near_ref, run):
-    odd = is_odd()
-
-    @pl.when(odd)
-    def _():
-        run(near_ref, far_ref)
-
-    @pl.when(jnp.logical_not(odd))
-    def _():
-        run(far_ref, near_ref)
-
-
-def edge_kernel(pairs_ref, far_in, near_in, old_ref, part_ref, f_ref, far_out, near_out):
-    def run(before_ref, after_ref):
-        down_out, up_out = (near_out, far_out) if after_ref is far_in else (far_out, near_out)
+def over_halves(halo, groups, run):
+    far1_ref, far2_ref, near_ref = halo[:3]
+
+    def variant(half, odd, far_ref):
+        begin = half * (groups // 2)
+
+        def load(j):
+            far_at, near_at = at_rows((j - begin) * SUB), at_rows(j * SUB)
+            far = [far_ref[r, far_at, :] for r in range(REACH)]
+            near = [near_ref[r, near_at, :] for r in range(REACH)]
+            return (near, far) if odd else (far, near)
+
+        run(half, odd, load)
+
+    def choose(half, far_ref, wanted):
+        odd = is_odd()
+        for side in (True, False):
+
+            @pl.when(jnp.logical_and(odd == side, wanted))
+            def _():
+                variant(half, side, far_ref)
+
+    choose(0, far1_ref, True)
+    if len(halo) == 3:
+        choose(1, far2_ref, True)
+    else:
+        me = lax.axis_index("space")
+        relayed = me < 0
+        for _first, _between, last in RELAYS:
+            relayed = jnp.logical_or(relayed, me == last)
+        choose(1, halo[3], relayed)
+        choose(1, far2_ref, jnp.logical_not(relayed))
+
+
+def edge_kernel(count, pairs_ref, *refs):
+    halo, (old_ref, part_ref, f_ref, far1_out, far2_out, near_out) = refs[:count], refs[count:]
+    groups = part_ref.shape[1] // SUB
+
+    def run(half, odd, load):
+        far_out = (far1_out, far2_out)[half]
+        begin = half * (groups // 2)
 
         def group(j, _):
-            at = at_rows(j * SUB)
-            low, high = halo_terms(pairs_ref, before_ref, after_ref, old_ref, at)
+            at, far_at = at_rows(j * SUB), at_rows((j - begin) * SUB)
+            low, high = halo_terms(pairs_ref, *load(j), old_ref, at)
             for g in range(REACH):
                 x = part_ref[g, at, :] + low[g]
-                down_out[g, at, :] = x
                 f_ref[g, at, :] = x
                 e = SUB - REACH + g
-                x = part_ref[e, at, :] + high[g]
-                up_out[g, at, :] = x
-                f_ref[e, at, :] = x
+                y = part_ref[e, at, :] + high[g]
+                f_ref[e, at, :] = y
+                far_out[g, far_at, :] = y if odd else x
+                near_out[g, at, :] = x if odd else y
             return 0
 
-        lax.fori_loop(0, part_ref.shape[1] // SUB, group, 0, unroll=2)
-
-    by_side(far_in, near_in, run)
-
-
-def edge(pairs, far, near, old, part):
+        lax.fori_loop(begin, begin + groups // 2, group, 0, unroll=2)
+
+    over_halves(halo, groups, run)
+
+
+def edge(pairs, halo, old, part):
     rows = part.shape[1]
     return pl.pallas_call(
-        edge_kernel,
-        in_specs=[spec(pltpu.VMEM)] * 5,
-        out_specs=[spec(pltpu.VMEM)] * 3,
-        out_shape=[array(SUB, rows, LANES), array(REACH, rows, LANES), array(REACH, rows, LANES)],
-        input_output_aliases={4: 0},
+        functools.partial(edge_kernel, len(halo)),
+        in_specs=[spec(pltpu.VMEM)] * (3 + len(halo)),
+        out_specs=[spec(pltpu.VMEM)] * 4,
+        out_shape=[array(SUB, rows, LANES)] + halo_arrays(rows),
+        input_output_aliases={2 + len(halo): 0},
         compiler_params=params(),
         name="edge",
-    )(pairs, far, near, old, part)
-
-
-def last_edge_kernel(
-    geo_in, pairs_ref, far_ref, near_ref, f_ref, part_ref, out_hbm, sums_out, native_ref, sems
-):
+    )(pairs, *halo, old, part)
+
+
+def last_edge_kernel(count, geo_in, pairs_ref, *refs):
+    halo, (f_ref, part_ref, out_hbm, sums_out, native_ref, sems) = refs[:count], refs[count:]
     rows = part_ref.shape[0] // SUB
     planes = rows // CHUNKS
-    part = rows // SUB // LAST_PARTS
+    groups = rows // SUB
+    part = groups // LAST_PARTS
 
     def copy(i):
         at = pl.ds(i * part * SUB * SUB, part * SUB * SUB)
         return pltpu.make_async_copy(native_ref.at[at], out_hbm.at[at], sems.at[i])
 
-    def run(before_ref, after_ref):
-        for i in range(LAST_PARTS):
+    def run(half, odd, load):
+        for i in range(half * LAST_PARTS // 2, (half + 1) * LAST_PARTS // 2):
 
             def group(j, _):
-                at = at_rows(j * SUB)
-                low, high = halo_terms(pairs_ref, before_ref, after_ref, f_ref, at)
+                low, high = halo_terms(pairs_ref, *load(j), f_ref, at_rows(j * SUB))
                 terms = low + [None] * (SUB - 2 * REACH) + high
                 for g in range(SUB):
                     where = (pl.ds(j * SUB * SUB + g, SUB, stride=SUB), slice(None))
@@ -764,7 +795,7 @@
             lax.fori_loop(i * part, (i + 1) * part, group, 0, unroll=2)
             copy(i).start()
 
-    by_side(far_ref, near_ref, run)
+    over_halves(halo, groups, run)
     y = native_polynomial_sums(native_ref, planes)
     sums_out[...] = pack_sums(finish_polynomials(y, column(geo_in[...], FIRST), planes), 0)
     for i in range(LAST_PARTS):
@@ -774,24 +805,36 @@
 LAST_PARTS = 4
 
 
-def last_edge(geo, pairs, far, near, f, part):
+def last_edge(geo, pairs, halo, f, part):
     return pl.pallas_call(
-        last_edge_kernel,
-        in_specs=[spec(pltpu.VMEM)] * 6,
+        functools.partial(last_edge_kernel, len(halo)),
+        in_specs=[spec(pltpu.VMEM)] * (4 + len(halo)),
         out_specs=[spec(pltpu.HBM), spec(pltpu.VMEM)],
         out_shape=[array(*part.shape), array(SUB, LANES)],
         scratch_shapes=[pltpu.VMEM(part.shape, F32), pltpu.SemaphoreType.DMA((LAST_PARTS,))],
         compiler_params=params(),
         name="last_edge",
-    )(geo, pairs, far, near, f, part)
-
-
-def exchange(far, near):
+    )(geo, pairs, *halo, f, part)
+
+
+RELAY_SLABS = 8
+RELAYS = ((3, 7, 4), (4, 0, 3))
+
+
+def both_ways(pairs):
+    return pairs + [(j, i) for i, j in pairs]
+
+
+def exchange(far1, far2, near):
     size = lax.axis_size("space")
-    out = []
-    for x, start in ((far, 1), (near, 0)):
-        pairs = [(i, i + 1) for i in range(start, size - 1, 2)]
-        out.append(lax.ppermute(x, "space", pairs + [(j, i) for i, j in pairs]))
+    far_pairs = both_ways([(i, i + 1) for i in range(1, size - 1, 2)])
+    near_pairs = both_ways([(i, i + 1) for i in range(0, size - 1, 2)])
+    relays = RELAYS if size == RELAY_SLABS else ()
+    direct = [p for p in far_pairs if p not in [(first, last) for first, _, last in relays]]
+    far2 = lax.ppermute(far2, "space", direct + [(first, between) for first, between, _ in relays])
+    out = [lax.ppermute(far1, "space", far_pairs), far2, lax.ppermute(near, "space", near_pairs)]
+    if relays:
+        out.append(lax.ppermute(far2, "space", [(between, last) for _, between, last in relays]))
     return out
 
 
@@ -815,19 +858,19 @@
         ]
     )
     geo = jnp.pad(geo.T, ((0, 0), (0, LANES - GEO)))
-    native, far, near = first_rows(native)
-    far, near = exchange(far, near)
+    native, *halo = first_rows(native)
+    halo = exchange(*halo)
     f, sums = first_sums(links, geo, native)
     tiles = gather_sums(sums)
     pairs = geometry(links, geo, rows)
     part = flux(False, links, geo, f)
     part, absorbed = add_target(False, links, geo, None, tiles, f, part)
-    f, far, near = edge(pairs, far, near, f, part)
-    far, near = exchange(far, near)
+    f, *halo = edge(pairs, halo, f, part)
+    halo = exchange(*halo)
     tiles = gather_sums(local_sums(links, geo, f))
     part = flux(True, links, geo, f)
     part, _ = add_target(True, links, geo, absorbed, tiles, f, part)
-    native, sums = last_edge(geo, pairs, far, near, f, part)
+    native, sums = last_edge(geo, pairs, halo, f, part)
     macro_quantities = macro(gather_sums(sums))
     evolved = native.reshape(rows, cells, LANES).transpose(1, 0, 2).reshape(cells, points)
     return evolved, macro_quantities

time: 63.4 us -> 80.4 us (1.27)
  the two profiles are of different devices: /device:TPU:4 before, /device:TPU:0 now
where the time goes in v4:
time: 80.4 us; the launch traced here: 80 us
  Pallas kernels  34.1 us (42%)
  starting transfers between devices  27 us (34%)
  waiting for transfers between devices  16.4 us (20%)
  local copies, waits for them, and re-layouts  1.68 us (2%)
  between operations  0.84 us (1%)
    ppermute x9, starting transfers between devices, gather_sums(): lax.ppermute(tile, 'vel', [(i, i ^ s) for i in range(size)])  14 us
    ppermute x2, waiting for transfers between devices, exchange(): lax.ppermute(far2, 'space', direct + [(first, between) for first, between...  10.8 us
    pallas_call x2, Pallas kernels, add_target(): pl.pallas_call(kernel, in_specs=[spec(pltpu.SMEM)] + [vmem] * (len(given)...  10.1 us
    pallas_call x2, Pallas kernels, flux(): pl.pallas_call(functools.partial(flux_kernel, native), in_specs=[spec(plt...  8.06 us
    ppermute x9, waiting for transfers between devices, gather_sums(): lax.ppermute(tile, 'vel', [(i, i ^ s) for i in range(size)])  5.58 us
    ppermute x2, starting transfers between devices, exchange(): lax.ppermute(far2, 'space', [(between, last) for _, between, last in rela...  4.2 us
    ppermute x2, starting transfers between devices, exchange(): lax.ppermute(near, 'space', near_pairs)  4.14 us
    pallas_call x1, Pallas kernels, first_sums(): pl.pallas_call(first_sums_kernel, in_specs=[spec(pltpu.SMEM), spec(pltpu....  3.26 us
  transfers between devices with their start and end apart: 17, of which 6 were waited for; matrix products, arithmetic and copies ran while one was open for 1% of the time, Pallas kernels for 32%

profile of v4, /device:TPU:0, one launch (start us, length us, event | category | flops | bytes accessed | tf_op | source)
XLA Modules:
  0.0 80.0 jit_solution(1339427914560307622)
XLA Ops:
  0.7 2.7 %first_rows.1 = (f32[4096,128]{1,0:T(8,128)S(1)}, f32[3,256,128]{2,1,0:T(8,128)}, f32[3,256,128]{2,1,0:T(8,128)S(1)}, f32[3,512,128]{2,1,0:T(8,128)}) custom-call(f32[4096,128]{1,0:T(8,128)} %bitcast.13), custom_call_target="tpu_custom_call" | custom-call | tf_op jit(solution)/shard_map/first_rows/pallas_call | solution.py:370
  3.3 1.3 %collective-permute-start.1 = (f32[3,256,128]{2,1,0:T(8,128)S(1)}, f32[3,256,128]{2,1,0:T(8,128)S(1)}, u32[]{:S(2)}, u32[]{:S(2)}) collective-permute-start(f32[3,256,128]{2,1,0:T(8,128)S(1)} %get-tuple-element.18), channel_id=1, source_target_pairs={{4,8},{20,24},{8,4},{24,20},{12,28},{16,0},{5,9},{21,25},{9,5},{25... | collective-permute-start | bytes 1179656 | tf_op jit(solution)/shard_map/ppermute | solution.py:834
  4.6 3.7 %collective-permute-start.2 = (f32[3,512,128]{2,1,0:T(8,128)}, f32[3,512,128]{2,1,0:T(8,128)S(1)}, u32[]{:S(2)}, u32[]{:S(2)}) collective-permute-start(f32[3,512,128]{2,1,0:T(8,128)} %get-tuple-element.19), channel_id=1, source_target_pairs={{0,4},{8,12},{16,20},{24,28},{4,0},{12,8},{20,16},{28,24},{1,5},{9... | collective-permute-start | bytes 2359304 | tf_op jit(solution)/shard_map/ppermute | solution.py:835
  8.4 1.4 %collective-permute-start = (f32[3,256,128]{2,1,0:T(8,128)}, f32[3,256,128]{2,1,0:T(8,128)}, u32[]{:S(2)}, u32[]{:S(2)}) collective-permute-start(f32[3,256,128]{2,1,0:T(8,128)} %get-tuple-element.17), channel_id=1, source_target_pairs={{4,8},{12,16},{20,24},{8,4},{16,12},{24,20},{5,9},{13,17},{21,25},... | collective-permute-start | bytes 1179656 | tf_op jit(solution)/shard_map/ppermute | solution.py:835
  9.8 3.5 %collective-permute-done.1.refs_1_ = f32[3,256,128]{2,1,0:T(8,128)S(1)} collective-permute-done((f32[3,256,128]{2,1,0:T(8,128)S(1)}, f32[3,256,128]{2,1,0:T(8,128)S(1)}, u32[]{:S(2)}, u32[]{:S(2)}) %collective-permute-start.1) | collective-permute-done | bytes 393248 | tf_op jit(solution)/shard_map/ppermute | solution.py:834
  13.3 2.9 %collective-permute-start.3 = (f32[3,256,128]{2,1,0:T(8,128)S(1)}, f32[3,256,128]{2,1,0:T(8,128)}, u32[]{:S(2)}, u32[]{:S(2)}) collective-permute-start(f32[3,256,128]{2,1,0:T(8,128)S(1)} %collective-permute-done.1.refs_1_), channel_id=1, source_target_pairs={{28,16},{0,12},{29,17},{1,13},{30,18},{2,14},{31,19},{3,15}} | collective-permute-start | bytes 1179656 | tf_op jit(solution)/shard_map/ppermute | solution.py:837
  16.2 0.1 copy.23
  16.3 0.1 copy.25
  16.4 0.1 copy.26
  16.5 0.1 copy.27.links_ref
  16.6 0.1 copy.34
  16.7 0.1 concatenate.3
  16.7 3.3 %first_sums.1 = (f32[8,512,128]{2,1,0:T(8,128)S(1)}, f32[8,128]{1,0:T(8,128)S(1)}) custom-call(s32[6,8]{1,0:T(8,128)S(1)} %copy.27.links_ref, f32[8,128]{1,0:T(8,128)S(1)} %pad.4.geo_in, f32[4096,128]{1,0:T(8,128)S(1)} %get-tuple-element.20.native_ref), custom_call_target="tpu_custom_call" | custom-call | tf_op jit(solution)/shard_map/first_sums/pallas_call | solution.py:310
  20.0 3.9 %collective-permute-start.6 = (f32[8,128]{1,0:T(8,128)S(1)}, f32[8,128]{1,0:T(8,128)S(1)}, u32[]{:S(2)}, u32[]{:S(2)}) collective-permute-start(f32[8,128]{1,0:T(8,128)S(1)} %get-tuple-element.22.refs_0_), channel_id=1, source_target_pairs={{0,3},{1,2},{2,1},{3,0},{4,7},{5,6},{6,5},{7,4},{8,11},{9,10},{10,... | collective-permute-start | bytes 12296 | tf_op jit(solution)/shard_map/ppermute | solution.py:442
  23.9 1.6 %collective-permute-done.6.refs_3_ = f32[8,128]{1,0:T(8,128)S(1)} collective-permute-done((f32[8,128]{1,0:T(8,128)S(1)}, f32[8,128]{1,0:T(8,128)S(1)}, u32[]{:S(2)}, u32[]{:S(2)}) %collective-permute-start.6) | collective-permute-done | bytes 4128 | tf_op jit(solution)/shard_map/ppermute | solution.py:442
  25.5 0.0 collective-permute-start.4
  25.5 1.9 %geometry.1.pairs_ref = f32[12,512,128]{2,1,0:T(8,128)S(1)} custom-call(s32[6,8]{1,0:T(8,128)S(1)} %copy.27.links_ref, f32[8,128]{1,0:T(8,128)S(1)} %pad.4.geo_in), custom_call_target="tpu_custom_call" | custom-call | tf_op jit(solution)/shard_map/geometry/pallas_call | solution.py:427
  27.5 4.0 %flux.2.refs_5_ = f32[8,512,128]{2,1,0:T(8,128)S(1)} custom-call(s32[6,8]{1,0:T(8,128)S(1)} %copy.27.links_ref, f32[8,128]{1,0:T(8,128)S(1)} %pad.4.geo_in, f32[8,512,128]{2,1,0:T(8,128)S(1)} %get-tuple-element.21.f_ref.refs_4_), custom_call_target="tpu_custom_call" | custom-call | tf_op jit(solution)/shard_map/flux/pallas_call | solution.py:550
  31.5 0.0 collective-permute-done.5.refs_2_
  31.5 4.1 %add_target.2 = (f32[8,512,128]{2,1,0:T(8,128)S(1)}, f32[8,128]{1,0:T(8,128)S(1)}) custom-call(s32[6,8]{1,0:T(8,128)S(1)} %copy.27.links_ref, f32[8,128]{1,0:T(8,128)S(1)} %pad.4.geo_in, f32[8,128]{1,0:T(8,128)S(1)} %get-tuple-element.22.refs_0_, f32[8,128]{1,0:T(8,128)S(1)} %collective-permute-done.4.refs_1_, ...), custom_call_target="tpu_custom_call", output_to_operand_aliasing={{0}: (7, {})} | custom-call | tf_op jit(solution)/shard_map/add_target/pallas_call | solution.py:667
  35.6 0.0 collective-permute-done.refs_0_
  35.6 0.0 collective-permute-done.3.refs_3_
  35.6 2.3 %edge.1 = (f32[8,512,128]{2,1,0:T(8,128)S(1)}, f32[3,256,128]{2,1,0:T(8,128)S(1)}, f32[3,256,128]{2,1,0:T(8,128)S(1)}, f32[3,512,128]{2,1,0:T(8,128)S(1)}) custom-call(f32[12,512,128]{2,1,0:T(8,128)S(1)} %geometry.1.pairs_ref, f32[3,256,128]{2,1,0:T(8,128)} %collective-permute-done.refs_0_, ...), custom_call_target="tpu_custom_call", output_to_operand_aliasing={{0}: (6, {})} | custom-call | tf_op jit(solution)/shard_map/edge/pallas_call | solution.py:761
  38.0 1.3 %collective-permute-start.8 = (f32[3,256,128]{2,1,0:T(8,128)S(1)}, f32[3,256,128]{2,1,0:T(8,128)S(1)}, u32[]{:S(2)}, u32[]{:S(2)}) collective-permute-start(f32[3,256,128]{2,1,0:T(8,128)S(1)} %get-tuple-element.25), channel_id=1, source_target_pairs={{4,8},{20,24},{8,4},{24,20},{12,28},{16,0},{5,9},{21,25},{9,5},{25... | collective-permute-start | bytes 1179656 | tf_op jit(solution)/shard_map/ppermute | solution.py:834
  39.3 0.4 collective-permute-start.9
  39.7 0.7 collective-permute-start.7
  40.4 7.3 %collective-permute-done.8.refs_1_ = f32[3,256,128]{2,1,0:T(8,128)S(1)} collective-permute-done((f32[3,256,128]{2,1,0:T(8,128)S(1)}, f32[3,256,128]{2,1,0:T(8,128)S(1)}, u32[]{:S(2)}, u32[]{:S(2)}) %collective-permute-start.8) | collective-permute-done | bytes 393248 | tf_op jit(solution)/shard_map/ppermute | solution.py:834
  47.7 1.3 %collective-permute-start.10 = (f32[3,256,128]{2,1,0:T(8,128)S(1)}, f32[3,256,128]{2,1,0:T(8,128)S(1)}, u32[]{:S(2)}, u32[]{:S(2)}) collective-permute-start(f32[3,256,128]{2,1,0:T(8,128)S(1)} %collective-permute-done.8.refs_1_), channel_id=1, source_target_pairs={{28,16},{0,12},{29,17},{1,13},{30,18},{2,14},{31,19},{3,15}} | collective-permute-start | bytes 1179656 | tf_op jit(solution)/shard_map/ppermute | solution.py:837
  49.0 2.4 %local_sums.1.refs_1_ = f32[8,128]{1,0:T(8,128)S(1)} custom-call(s32[6,8]{1,0:T(8,128)S(1)} %copy.27.links_ref, f32[8,128]{1,0:T(8,128)S(1)} %pad.4.geo_in, f32[8,512,128]{2,1,0:T(8,128)S(1)} %get-tuple-element.27.f_ref.refs_5_.refs_4_), custom_call_target="tpu_custom_call" | custom-call | tf_op jit(solution)/shard_map/local_sums/pallas_call | solution.py:293
  51.3 3.8 %collective-permute-start.13 = (f32[8,128]{1,0:T(8,128)S(1)}, f32[8,128]{1,0:T(8,128)S(1)}, u32[]{:S(2)}, u32[]{:S(2)}) collective-permute-start(f32[8,128]{1,0:T(8,128)S(1)} %local_sums.1.refs_1_), channel_id=1, source_target_pairs={{0,3},{1,2},{2,1},{3,0},{4,7},{5,6},{6,5},{7,4},{8,11},{9,10},{10,... | collective-permute-start | bytes 12296 | tf_op jit(solution)/shard_map/ppermute | solution.py:442
  55.2 0.6 collective-permute-start.12
  55.8 0.9 %collective-permute-done.13.refs_4_ = f32[8,128]{1,0:T(8,128)S(1)} collective-permute-done((f32[8,128]{1,0:T(8,128)S(1)}, f32[8,128]{1,0:T(8,128)S(1)}, u32[]{:S(2)}, u32[]{:S(2)}) %collective-permute-start.13) | collective-permute-done | bytes 4128 | tf_op jit(solution)/shard_map/ppermute | solution.py:442
  56.8 1.1 %collective-permute-start.11 = (f32[8,128]{1,0:T(8,128)S(1)}, f32[8,128]{1,0:T(8,128)S(1)}, u32[]{:S(2)}, u32[]{:S(2)}) collective-permute-start(f32[8,128]{1,0:T(8,128)S(1)} %local_sums.1.refs_1_), channel_id=1, source_target_pairs={{0,1},{1,0},{2,3},{3,2},{4,5},{5,4},{6,7},{7,6},{8,9},{9,8},{10,11... | collective-permute-start | bytes 12296 | tf_op jit(solution)/shard_map/ppermute | solution.py:442
  57.9 4.1 %flux.3.refs_6_ = f32[4096,128]{1,0:T(8,128)S(1)} custom-call(s32[6,8]{1,0:T(8,128)S(1)} %copy.27.links_ref, f32[8,128]{1,0:T(8,128)S(1)} %pad.4.geo_in, f32[8,512,128]{2,1,0:T(8,128)S(1)} %get-tuple-element.27.f_ref.refs_5_.refs_4_), custom_call_target="tpu_custom_call" | custom-call | tf_op jit(solution)/shard_map/flux/pallas_call | solution.py:550
  62.0 0.0 collective-permute-done.11.refs_2_
  62.0 6.0 %add_target.3 = (f32[4096,128]{1,0:T(8,128)S(1)}, f32[8,128]{1,0:T(8,128)}) custom-call(s32[6,8]{1,0:T(8,128)S(1)} %copy.27.links_ref, f32[8,128]{1,0:T(8,128)S(1)} %pad.4.geo_in, f32[8,128]{1,0:T(8,128)S(1)} %get-tuple-element.28.refs_0_, f32[8,128]{1,0:T(8,128)S(1)} %local_sums.1.refs_1_, ...), custom_call_target="tpu_custom_call", output_to_operand_aliasing={{0}: (8, {})} | custom-call | tf_op jit(solution)/shard_map/add_target/pallas_call | solution.py:667
  68.0 0.0 collective-permute-done.7.refs_0_
  68.0 0.0 collective-permute-done.10.refs_3_
  68.0 2.0 %last_edge.1 = (f32[4096,128]{1,0:T(8,128)}, f32[8,128]{1,0:T(8,128)S(1)}) custom-call(f32[8,128]{1,0:T(8,128)S(1)} %pad.4.geo_in, f32[12,512,128]{2,1,0:T(8,128)S(1)} %geometry.1.pairs_ref, f32[3,256,128]{2,1,0:T(8,128)S(1)} %collective-permute-done.7.refs_0_, f32[3,256,128]{2,1,0:T(8,128)S(1)} %collective-permute-done.8.refs_1_, ...), custom_call_target="tpu_custom_call" | custom-call | tf_op jit(solution)/shard_map/last_edge/pallas_call | solution.py:809
  70.0 3.0 %collective-permute-start.16 = (f32[8,128]{1,0:T(8,128)S(1)}, f32[8,128]{1,0:T(8,128)S(1)}, u32[]{:S(2)}, u32[]{:S(2)}) collective-permute-start(f32[8,128]{1,0:T(8,128)S(1)} %get-tuple-element.31.refs_0_), channel_id=1, source_target_pairs={{0,3},{1,2},{2,1},{3,0},{4,7},{5,6},{6,5},{7,4},{8,11},{9,10},{10,... | collective-permute-start | bytes 12296 | tf_op jit(solution)/shard_map/ppermute | solution.py:442
  72.9 0.4 collective-permute-start.15
  73.4 1.1 %collective-permute-start.14 = (f32[8,128]{1,0:T(8,128)S(1)}, f32[8,128]{1,0:T(8,128)S(1)}, u32[]{:S(2)}, u32[]{:S(2)}) collective-permute-start(f32[8,128]{1,0:T(8,128)S(1)} %get-tuple-element.31.refs_0_), channel_id=1, source_target_pairs={{0,1},{1,0},{2,3},{3,2},{4,5},{5,4},{6,7},{7,6},{8,9},{9,8},{10,11... | collective-permute-start | bytes 12296 | tf_op jit(solution)/shard_map/ppermute | solution.py:442
  74.4 1.0 %collective-permute-done.16.refs_3_ = f32[8,128]{1,0:T(8,128)S(1)} collective-permute-done((f32[8,128]{1,0:T(8,128)S(1)}, f32[8,128]{1,0:T(8,128)S(1)}, u32[]{:S(2)}, u32[]{:S(2)}) %collective-permute-start.16) | collective-permute-done | bytes 4128 | tf_op jit(solution)/shard_map/ppermute | solution.py:442
  75.4 2.0 %collective-permute-done.15.refs_2_ = f32[8,128]{1,0:T(8,128)S(1)} collective-permute-done((f32[8,128]{1,0:T(8,128)S(1)}, f32[8,128]{1,0:T(8,128)S(1)}, u32[]{:S(2)}, u32[]{:S(2)}) %collective-permute-start.15) | collective-permute-done | bytes 4128 | tf_op jit(solution)/shard_map/ppermute | solution.py:442
  77.5 0.0 collective-permute-done.14.refs_1_
  77.5 0.6 copy-done.3
  78.1 0.6 copy-done.4
  78.6 1.4 %macro.1 = f32[8,8]{1,0:T(8,128)} custom-call(f32[8,128]{1,0:T(8,128)} %copy-done, f32[8,128]{1,0:T(8,128)} %copy-done.4, f32[8,128]{1,0:T(8,128)} %copy-done.3, f32[8,128]{1,0:T(8,128)} %copy-done.2), custom_call_target="tpu_custom_call" | custom-call | tf_op jit(solution)/shard_map/macro/pallas_call | solution.py:480
  (23 shorter events, 0.1 us)
Async XLA Ops:
  0.6 15.6 %copy-start.5 = (s32[6,8]{1,0:T(8,128)S(1)}, s32[6,8]{1,0:T(8,128)}, u32[]{:S(2)}) copy-start(s32[6,8]{1,0:T(8,128)} %param.6) | copy-start | bytes 580
  0.6 15.7 %copy-start.6 = (f32[8]{0:T(128)S(1)}, f32[8]{0:T(128)}, u32[]{:S(2)}) copy-start(f32[8]{0:T(128)} %param.8) | copy-start | bytes 100
  0.7 15.7 %copy-start.7 = (f32[8]{0:T(128)S(1)}, f32[8]{0:T(128)}, u32[]{:S(2)}) copy-start(f32[8]{0:T(128)} %param.9) | copy-start | bytes 100
  0.7 15.9 %copy-start.1 = (f32[3,6,8]{2,1,0:T(8,128)S(1)}, f32[3,6,8]{2,1,0:T(8,128)}, u32[]{:S(2)}) copy-start(f32[3,6,8]{2,1,0:T(8,128)} %param.7) | copy-start | bytes 1732
  3.3 10.0 %collective-permute-start.1 = (f32[3,256,128]{2,1,0:T(8,128)S(1)}, f32[3,256,128]{2,1,0:T(8,128)S(1)}, u32[]{:S(2)}, u32[]{:S(2)}) collective-permute-start(f32[3,256,128]{2,1,0:T(8,128)S(1)} %get-tuple-element.18), channel_id=1, source_target_pairs={{4,8},{20,24},{8,4},{24,20},{12,28},{16,0},{5,9},{21,25},{9,5},{25... | collective-permute-start | bytes 1179656 | tf_op jit(solution)/shard_map/ppermute | solution.py:834
  4.6 31.0 %collective-permute-start.2 = (f32[3,512,128]{2,1,0:T(8,128)}, f32[3,512,128]{2,1,0:T(8,128)S(1)}, u32[]{:S(2)}, u32[]{:S(2)}) collective-permute-start(f32[3,512,128]{2,1,0:T(8,128)} %get-tuple-element.19), channel_id=1, source_target_pairs={{0,4},{8,12},{16,20},{24,28},{4,0},{12,8},{20,16},{28,24},{1,5},{9... | collective-permute-start | bytes 2359304 | tf_op jit(solution)/shard_map/ppermute | solution.py:835
  8.4 27.2 %collective-permute-start = (f32[3,256,128]{2,1,0:T(8,128)}, f32[3,256,128]{2,1,0:T(8,128)}, u32[]{:S(2)}, u32[]{:S(2)}) collective-permute-start(f32[3,256,128]{2,1,0:T(8,128)} %get-tuple-element.17), channel_id=1, source_target_pairs={{4,8},{12,16},{20,24},{8,4},{16,12},{24,20},{5,9},{13,17},{21,25},... | collective-permute-start | bytes 1179656 | tf_op jit(solution)/shard_map/ppermute | solution.py:835
  13.3 22.3 %collective-permute-start.3 = (f32[3,256,128]{2,1,0:T(8,128)S(1)}, f32[3,256,128]{2,1,0:T(8,128)}, u32[]{:S(2)}, u32[]{:S(2)}) collective-permute-start(f32[3,256,128]{2,1,0:T(8,128)S(1)} %collective-permute-done.1.refs_1_), channel_id=1, source_target_pairs={{28,16},{0,12},{29,17},{1,13},{30,18},{2,14},{31,19},{3,15}} | collective-permute-start | bytes 1179656 | tf_op jit(solution)/shard_map/ppermute | solution.py:837
  20.0 5.5 %collective-permute-start.6 = (f32[8,128]{1,0:T(8,128)S(1)}, f32[8,128]{1,0:T(8,128)S(1)}, u32[]{:S(2)}, u32[]{:S(2)}) collective-permute-start(f32[8,128]{1,0:T(8,128)S(1)} %get-tuple-element.22.refs_0_), channel_id=1, source_target_pairs={{0,3},{1,2},{2,1},{3,0},{4,7},{5,6},{6,5},{7,4},{8,11},{9,10},{10,... | collective-permute-start | bytes 12296 | tf_op jit(solution)/shard_map/ppermute | solution.py:442
  23.9 7.6 %collective-permute-start.5 = (f32[8,128]{1,0:T(8,128)S(1)}, f32[8,128]{1,0:T(8,128)S(1)}, u32[]{:S(2)}, u32[]{:S(2)}) collective-permute-start(f32[8,128]{1,0:T(8,128)S(1)} %get-tuple-element.22.refs_0_), channel_id=1, source_target_pairs={{0,2},{1,3},{2,0},{3,1},{4,6},{5,7},{6,4},{7,5},{8,10},{9,11},{10,... | collective-permute-start | bytes 12296 | tf_op jit(solution)/shard_map/ppermute | solution.py:442
  25.5 6.0 %collective-permute-start.4 = (f32[8,128]{1,0:T(8,128)S(1)}, f32[8,128]{1,0:T(8,128)S(1)}, u32[]{:S(2)}, u32[]{:S(2)}) collective-permute-start(f32[8,128]{1,0:T(8,128)S(1)} %get-tuple-element.22.refs_0_), channel_id=1, source_target_pairs={{0,1},{1,0},{2,3},{3,2},{4,5},{5,4},{6,7},{7,6},{8,9},{9,8},{10,11... | collective-permute-start | bytes 12296 | tf_op jit(solution)/shard_map/ppermute | solution.py:442
  38.0 9.7 %collective-permute-start.8 = (f32[3,256,128]{2,1,0:T(8,128)S(1)}, f32[3,256,128]{2,1,0:T(8,128)S(1)}, u32[]{:S(2)}, u32[]{:S(2)}) collective-permute-start(f32[3,256,128]{2,1,0:T(8,128)S(1)} %get-tuple-element.25), channel_id=1, source_target_pairs={{4,8},{20,24},{8,4},{24,20},{12,28},{16,0},{5,9},{21,25},{9,5},{25... | collective-permute-start | bytes 1179656 | tf_op jit(solution)/shard_map/ppermute | solution.py:834
  39.3 28.7 %collective-permute-start.9 = (f32[3,512,128]{2,1,0:T(8,128)S(1)}, f32[3,512,128]{2,1,0:T(8,128)S(1)}, u32[]{:S(2)}, u32[]{:S(2)}) collective-permute-start(f32[3,512,128]{2,1,0:T(8,128)S(1)} %get-tuple-element.26), channel_id=1, source_target_pairs={{0,4},{8,12},{16,20},{24,28},{4,0},{12,8},{20,16},{28,24},{1,5},{9... | collective-permute-start | bytes 2359304 | tf_op jit(solution)/shard_map/ppermute | solution.py:835
  39.7 28.3 %collective-permute-start.7 = (f32[3,256,128]{2,1,0:T(8,128)S(1)}, f32[3,256,128]{2,1,0:T(8,128)S(1)}, u32[]{:S(2)}, u32[]{:S(2)}) collective-permute-start(f32[3,256,128]{2,1,0:T(8,128)S(1)} %get-tuple-element.24), channel_id=1, source_target_pairs={{4,8},{12,16},{20,24},{8,4},{16,12},{24,20},{5,9},{13,17},{21,25},... | collective-permute-start | bytes 1179656 | tf_op jit(solution)/shard_map/ppermute | solution.py:835
  47.7 20.3 %collective-permute-start.10 = (f32[3,256,128]{2,1,0:T(8,128)S(1)}, f32[3,256,128]{2,1,0:T(8,128)S(1)}, u32[]{:S(2)}, u32[]{:S(2)}) collective-permute-start(f32[3,256,128]{2,1,0:T(8,128)S(1)} %collective-permute-done.8.refs_1_), channel_id=1, source_target_pairs={{28,16},{0,12},{29,17},{1,13},{30,18},{2,14},{31,19},{3,15}} | collective-permute-start | bytes 1179656 | tf_op jit(solution)/shard_map/ppermute | solution.py:837
  51.3 5.4 %collective-permute-start.13 = (f32[8,128]{1,0:T(8,128)S(1)}, f32[8,128]{1,0:T(8,128)S(1)}, u32[]{:S(2)}, u32[]{:S(2)}) collective-permute-start(f32[8,128]{1,0:T(8,128)S(1)} %local_sums.1.refs_1_), channel_id=1, source_target_pairs={{0,3},{1,2},{2,1},{3,0},{4,7},{5,6},{6,5},{7,4},{8,11},{9,10},{10,... | collective-permute-start | bytes 12296 | tf_op jit(solution)/shard_map/ppermute | solution.py:442
  55.2 6.8 %collective-permute-start.12 = (f32[8,128]{1,0:T(8,128)S(1)}, f32[8,128]{1,0:T(8,128)S(1)}, u32[]{:S(2)}, u32[]{:S(2)}) collective-permute-start(f32[8,128]{1,0:T(8,128)S(1)} %local_sums.1.refs_1_), channel_id=1, source_target_pairs={{0,2},{1,3},{2,0},{3,1},{4,6},{5,7},{6,4},{7,5},{8,10},{9,11},{10,... | collective-permute-start | bytes 12296 | tf_op jit(solution)/shard_map/ppermute | solution.py:442
  56.8 5.2 %collective-permute-start.11 = (f32[8,128]{1,0:T(8,128)S(1)}, f32[8,128]{1,0:T(8,128)S(1)}, u32[]{:S(2)}, u32[]{:S(2)}) collective-permute-start(f32[8,128]{1,0:T(8,128)S(1)} %local_sums.1.refs_1_), channel_id=1, source_target_pairs={{0,1},{1,0},{2,3},{3,2},{4,5},{5,4},{6,7},{7,6},{8,9},{9,8},{10,11... | collective-permute-start | bytes 12296 | tf_op jit(solution)/shard_map/ppermute | solution.py:442
  70.0 7.5 %copy-start = (f32[8,128]{1,0:T(8,128)}, f32[8,128]{1,0:T(8,128)S(1)}, u32[]{:S(2)}) copy-start(f32[8,128]{1,0:T(8,128)S(1)} %get-tuple-element.31.refs_0_) | copy-start | bytes 12292
  70.0 5.5 %collective-permute-start.16 = (f32[8,128]{1,0:T(8,128)S(1)}, f32[8,128]{1,0:T(8,128)S(1)}, u32[]{:S(2)}, u32[]{:S(2)}) collective-permute-start(f32[8,128]{1,0:T(8,128)S(1)} %get-tuple-element.31.refs_0_), channel_id=1, source_target_pairs={{0,3},{1,2},{2,1},{3,0},{4,7},{5,6},{6,5},{7,4},{8,11},{9,10},{10,... | collective-permute-start | bytes 12296 | tf_op jit(solution)/shard_map/ppermute | solution.py:442
  72.9 4.5 %collective-permute-start.15 = (f32[8,128]{1,0:T(8,128)S(1)}, f32[8,128]{1,0:T(8,128)S(1)}, u32[]{:S(2)}, u32[]{:S(2)}) collective-permute-start(f32[8,128]{1,0:T(8,128)S(1)} %get-tuple-element.31.refs_0_), channel_id=1, source_target_pairs={{0,2},{1,3},{2,0},{3,1},{4,6},{5,7},{6,4},{7,5},{8,10},{9,11},{10,... | collective-permute-start | bytes 12296 | tf_op jit(solution)/shard_map/ppermute | solution.py:442
  73.4 4.1 %collective-permute-start.14 = (f32[8,128]{1,0:T(8,128)S(1)}, f32[8,128]{1,0:T(8,128)S(1)}, u32[]{:S(2)}, u32[]{:S(2)}) collective-permute-start(f32[8,128]{1,0:T(8,128)S(1)} %get-tuple-element.31.refs_0_), channel_id=1, source_target_pairs={{0,1},{1,0},{2,3},{3,2},{4,5},{5,4},{6,7},{7,6},{8,9},{9,8},{10,11... | collective-permute-start | bytes 12296 | tf_op jit(solution)/shard_map/ppermute | solution.py:442
  75.4 2.0 %copy-start.2 = (f32[8,128]{1,0:T(8,128)}, f32[8,128]{1,0:T(8,128)S(1)}, u32[]{:S(2)}) copy-start(f32[8,128]{1,0:T(8,128)S(1)} %collective-permute-done.16.refs_3_) | copy-start | bytes 12292
  77.5 0.6 copy-start.3
  78.0 0.6 copy-start.4

commit v5 on v4

--- a/solution.py
+++ b/solution.py
@@ -289,6 +289,11 @@
     return pltpu.CompilerParams(vmem_limit_bytes=VMEM_LIMIT)
 
 
+def traffic(rows, profiles):
+    size = SUB * rows * LANES
+    return pl.CostEstimate(flops=8 * profiles * size, bytes_accessed=4 * profiles * size, transcendentals=0)
+
+
 def local_sums(links, geo, f):
     return pl.pallas_call(
         sums_kernel,
@@ -301,6 +306,7 @@
             pltpu.VMEM((FACES, SUB * SUB, LANES), F32),
         ],
         compiler_params=params(),
+        cost_estimate=traffic(f.shape[1], 4),
         name="local_sums",
     )(links, geo, f)
 
@@ -317,6 +323,7 @@
             pltpu.VMEM((2 * FACES, SUB * SUB, LANES), F32),
         ],
         compiler_params=params(),
+        cost_estimate=traffic(rows, 5),
         name="first_sums",
     )(links, geo, native)
 
@@ -374,6 +381,7 @@
         out_shape=[array(*native.shape)] + halo_arrays(rows),
         scratch_shapes=[pltpu.SemaphoreType.DMA((SPLIT_PARTS,))],
         compiler_params=params(),
+        cost_estimate=traffic(rows, 4),
         name="first_rows",
     )(pltpu.with_memory_space_constraint(native, pltpu.HBM))
 
@@ -431,6 +439,7 @@
         out_shape=array(2 * len(BEFORE_PAIRS), rows, LANES),
         scratch_shapes=[pltpu.VMEM((GEO, SUB, LANES), F32)],
         compiler_params=params(),
+        cost_estimate=traffic(rows, 4),
         name="geometry",
     )(links, geo)
 
@@ -557,6 +566,7 @@
             pltpu.VMEM((3 * FACES + 3, SUB, LANES), F32),
         ],
         compiler_params=params(),
+        cost_estimate=traffic(rows, 7),
         name="flux",
     )(links, geo, f)
 
@@ -676,6 +686,7 @@
             pltpu.VMEM((6 + FACES, SUB, LANES), F32),
         ],
         compiler_params=params(),
+        cost_estimate=traffic(rows, 7),
         name="add_target",
     )(*given)
 
@@ -765,6 +776,7 @@
         out_shape=[array(SUB, rows, LANES)] + halo_arrays(rows),
         input_output_aliases={2 + len(halo): 0},
         compiler_params=params(),
+        cost_estimate=traffic(rows, 4),
         name="edge",
     )(pairs, *halo, old, part)
 
@@ -813,6 +825,7 @@
         out_shape=[array(*part.shape), array(SUB, LANES)],
         scratch_shapes=[pltpu.VMEM(part.shape, F32), pltpu.SemaphoreType.DMA((LAST_PARTS,))],
         compiler_params=params(),
+        cost_estimate=traffic(part.shape[0] // SUB, 4),
         name="last_edge",
     )(geo, pairs, *halo, f, part)
 
@@ -832,10 +845,15 @@
     relays = RELAYS if size == RELAY_SLABS else ()
     direct = [p for p in far_pairs if p not in [(first, last) for first, _, last in relays]]
     far2 = lax.ppermute(far2, "space", direct + [(first, between) for first, between, _ in relays])
-    out = [lax.ppermute(far1, "space", far_pairs), far2, lax.ppermute(near, "space", near_pairs)]
-    if relays:
-        out.append(lax.ppermute(far2, "space", [(between, last) for _, between, last in relays]))
-    return out
+    return [lax.ppermute(far1, "space", far_pairs), far2, lax.ppermute(near, "space", near_pairs)]
+
+
+def pass_on(halo, after):
+    size = lax.axis_size("space")
+    if size != RELAY_SLABS:
+        return halo
+    rows, _ = lax.optimization_barrier((halo[1], after))
+    return [*halo, lax.ppermute(rows, "space", [(between, last) for _, between, last in RELAYS])]
 
 
 def per_device(particle_profile, neighbors, face_vectors, volumes, wall_temp):
@@ -861,13 +879,16 @@
     native, *halo = first_rows(native)
     halo = exchange(*halo)
     f, sums = first_sums(links, geo, native)
+    halo = pass_on(halo, sums)
     tiles = gather_sums(sums)
     pairs = geometry(links, geo, rows)
     part = flux(False, links, geo, f)
     part, absorbed = add_target(False, links, geo, None, tiles, f, part)
     f, *halo = edge(pairs, halo, f, part)
     halo = exchange(*halo)
-    tiles = gather_sums(local_sums(links, geo, f))
+    sums = local_sums(links, geo, f)
+    halo = pass_on(halo, sums)
+    tiles = gather_sums(sums)
     part = flux(True, links, geo, f)
     part, _ = add_target(True, links, geo, absorbed, tiles, f, part)
     native, sums = last_edge(geo, pairs, halo, f, part)

time: 80.4 us -> 76.6 us (0.953)
  waiting for transfers between devices: 16.4 us -> 11.1 us
  Pallas kernels: 34.1 us -> 35.2 us
    ppermute x2, waiting for transfers between devices: 10.8 us -> 5.11 us  [exchange(): lax.ppermute(far2, 'space', direct + [(first, between) for first, between...]
    ppermute x2, starting transfers between devices: 4.2 us -> 5.59 us  [pass_on(): lax.ppermute(rows, 'space', [(between, last) for _, between, last in RELA...]
  transfers between devices with their start and end apart: 17 -> 17, of which waited for: 6 -> 5; matrix products, arithmetic and copies ran while one was open for 1% -> 1% of each run, Pallas kernels for 32% -> 35%
where the time goes in v5:
time: 76.6 us; the launch traced here: 76.3 us
  Pallas kernels  35.2 us (46%)
  starting transfers between devices  27.4 us (36%)
  waiting for transfers between devices  11.1 us (14%)
  local copies, waits for them, and re-layouts  1.68 us (2%)
  between operations  0.86 us (1%)
    ppermute x9, starting transfers between devices, gather_sums(): lax.ppermute(tile, 'vel', [(i, i ^ s) for i in range(size)])  13.3 us
    pallas_call x2, Pallas kernels, add_target(): pl.pallas_call(kernel, in_specs=[spec(pltpu.SMEM)] + [vmem] * (len(given)...  10.6 us
    pallas_call x2, Pallas kernels, flux(): pl.pallas_call(functools.partial(flux_kernel, native), in_specs=[spec(plt...  8.06 us
    ppermute x9, waiting for transfers between devices, gather_sums(): lax.ppermute(tile, 'vel', [(i, i ^ s) for i in range(size)])  6.01 us
    ppermute x2, starting transfers between devices, pass_on(): lax.ppermute(rows, 'space', [(between, last) for _, between, last in RELA...  5.59 us
    ppermute x2, waiting for transfers between devices, exchange(): lax.ppermute(far2, 'space', direct + [(first, between) for first, between...  5.11 us
    ppermute x2, starting transfers between devices, exchange(): lax.ppermute(near, 'space', near_pairs)  3.81 us
    pallas_call x1, Pallas kernels, first_sums(): pl.pallas_call(first_sums_kernel, in_specs=[spec(pltpu.SMEM), spec(pltpu....  3.53 us
  transfers between devices with their start and end apart: 17, of which 5 were waited for; matrix products, arithmetic and copies ran while one was open for 1% of the time, Pallas kernels for 35%

profile of v5, /device:TPU:0, one launch (start us, length us, event | category | flops | bytes accessed | tf_op | source)
XLA Modules:
  0.0 76.3 jit_solution(13288491837204066668)
XLA Ops:
  0.7 2.8 %first_rows.1 = (f32[4096,128]{1,0:T(8,128)S(1)}, f32[3,256,128]{2,1,0:T(8,128)}, f32[3,256,128]{2,1,0:T(8,128)}, f32[3,512,128]{2,1,0:T(8,128)}) custom-call(f32[4096,128]{1,0:T(8,128)} %bitcast.13), custom_call_target="tpu_custom_call" | custom-call | flops 16777216 | bytes 8388608 | tf_op jit(solution)/shard_map/first_rows/pallas_call | solution.py:377
  3.5 1.3 %collective-permute-start.1 = (f32[3,256,128]{2,1,0:T(8,128)}, f32[3,256,128]{2,1,0:T(8,128)S(1)}, u32[]{:S(2)}, u32[]{:S(2)}) collective-permute-start(f32[3,256,128]{2,1,0:T(8,128)} %get-tuple-element.20), channel_id=1, source_target_pairs={{4,8},{20,24},{8,4},{24,20},{12,28},{16,0},{5,9},{21,25},{9,5},{25... | collective-permute-start | bytes 1179656 | tf_op jit(solution)/shard_map/ppermute | solution.py:847
  4.8 3.7 %collective-permute-start.2 = (f32[3,512,128]{2,1,0:T(8,128)}, f32[3,512,128]{2,1,0:T(8,128)S(1)}, u32[]{:S(2)}, u32[]{:S(2)}) collective-permute-start(f32[3,512,128]{2,1,0:T(8,128)} %get-tuple-element.21), channel_id=1, source_target_pairs={{0,4},{8,12},{16,20},{24,28},{4,0},{12,8},{20,16},{28,24},{1,5},{9... | collective-permute-start | bytes 2359304 | tf_op jit(solution)/shard_map/ppermute | solution.py:848
  8.5 1.4 %collective-permute-start = (f32[3,256,128]{2,1,0:T(8,128)}, f32[3,256,128]{2,1,0:T(8,128)}, u32[]{:S(2)}, u32[]{:S(2)}) collective-permute-start(f32[3,256,128]{2,1,0:T(8,128)} %get-tuple-element.19), channel_id=1, source_target_pairs={{4,8},{12,16},{20,24},{8,4},{16,12},{24,20},{5,9},{13,17},{21,25},... | collective-permute-start | bytes 1179656 | tf_op jit(solution)/shard_map/ppermute | solution.py:848
  9.9 0.1 copy.23
  10.0 0.1 copy.25
  10.1 0.1 copy.26
  10.2 0.1 copy.27.links_ref
  10.3 0.1 copy.34
  10.3 0.1 concatenate.3
  10.4 3.5 %first_sums.1 = (f32[8,512,128]{2,1,0:T(8,128)S(1)}, f32[8,128]{1,0:T(8,128)S(1)}) custom-call(s32[6,8]{1,0:T(8,128)S(1)} %copy.27.links_ref, f32[8,128]{1,0:T(8,128)S(1)} %pad.4.geo_in, f32[4096,128]{1,0:T(8,128)S(1)} %get-tuple-element.22.native_ref), custom_call_target="tpu_custom_call" | custom-call | flops 20971520 | bytes 10485760 | tf_op jit(solution)/shard_map/first_sums/pallas_call | solution.py:316
  14.0 0.0 collective-permute-done.1.refs_1_
  14.0 4.2 %collective-permute-start.3 = (f32[3,256,128]{2,1,0:T(8,128)S(1)}, f32[3,256,128]{2,1,0:T(8,128)S(1)}, u32[]{:S(2)}, u32[]{:S(2)}) collective-permute-start(f32[3,256,128]{2,1,0:T(8,128)S(1)} %collective-permute-done.1.refs_1_), channel_id=1, source_target_pairs={{28,16},{0,12},{29,17},{1,13},{30,18},{2,14},{31,19},{3,15}} | collective-permute-start | bytes 1179656 | tf_op jit(solution)/shard_map/ppermute | solution.py:856
  18.2 3.7 %collective-permute-start.6 = (f32[8,128]{1,0:T(8,128)S(1)}, f32[8,128]{1,0:T(8,128)S(1)}, u32[]{:S(2)}, u32[]{:S(2)}) collective-permute-start(f32[8,128]{1,0:T(8,128)S(1)} %get-tuple-element.23.refs_0_), channel_id=1, source_target_pairs={{0,3},{1,2},{2,1},{3,0},{4,7},{5,6},{6,5},{7,4},{8,11},{9,10},{10,... | collective-permute-start | bytes 12296 | tf_op jit(solution)/shard_map/ppermute | solution.py:451
  21.8 0.0 collective-permute-start.5
  21.8 1.8 %collective-permute-done.6.refs_3_ = f32[8,128]{1,0:T(8,128)S(1)} collective-permute-done((f32[8,128]{1,0:T(8,128)S(1)}, f32[8,128]{1,0:T(8,128)S(1)}, u32[]{:S(2)}, u32[]{:S(2)}) %collective-permute-start.6) | collective-permute-done | bytes 4128 | tf_op jit(solution)/shard_map/ppermute | solution.py:451
  23.6 0.0 collective-permute-start.4
  23.6 2.1 %geometry.1.pairs_ref = f32[12,512,128]{2,1,0:T(8,128)S(1)} custom-call(s32[6,8]{1,0:T(8,128)S(1)} %copy.27.links_ref, f32[8,128]{1,0:T(8,128)S(1)} %pad.4.geo_in), custom_call_target="tpu_custom_call" | custom-call | flops 16777216 | bytes 8388608 | tf_op jit(solution)/shard_map/geometry/pallas_call | solution.py:435
  25.7 4.0 %flux.2.refs_5_ = f32[8,512,128]{2,1,0:T(8,128)S(1)} custom-call(s32[6,8]{1,0:T(8,128)S(1)} %copy.27.links_ref, f32[8,128]{1,0:T(8,128)S(1)} %pad.4.geo_in, f32[8,512,128]{2,1,0:T(8,128)S(1)} %get-tuple-element.25.f_ref.refs_4_), custom_call_target="tpu_custom_call" | custom-call | flops 29360128 | bytes 14680064 | tf_op jit(solution)/shard_map/flux/pallas_call | solution.py:559
  29.7 0.0 collective-permute-done.5.refs_2_
  29.7 0.0 collective-permute-done.4.refs_1_
  29.8 4.3 %add_target.2 = (f32[8,512,128]{2,1,0:T(8,128)S(1)}, f32[8,128]{1,0:T(8,128)S(1)}) custom-call(s32[6,8]{1,0:T(8,128)S(1)} %copy.27.links_ref, f32[8,128]{1,0:T(8,128)S(1)} %pad.4.geo_in, f32[8,128]{1,0:T(8,128)S(1)} %get-tuple-element.23.refs_0_, f32[8,128]{1,0:T(8,128)S(1)} %collective-permute-done.4.refs_1_, ...), custom_call_target="tpu_custom_call", output_to_operand_aliasing={{0}: (7, {})} | custom-call | flops 29360128 | bytes 14680064 | tf_op jit(solution)/shard_map/add_target/pallas_call | solution.py:677
  34.1 0.0 collective-permute-done.refs_0_
  34.1 2.2 %edge.1 = (f32[8,512,128]{2,1,0:T(8,128)S(1)}, f32[3,256,128]{2,1,0:T(8,128)S(1)}, f32[3,256,128]{2,1,0:T(8,128)S(1)}, f32[3,512,128]{2,1,0:T(8,128)S(1)}) custom-call(f32[12,512,128]{2,1,0:T(8,128)S(1)} %geometry.1.pairs_ref, f32[3,256,128]{2,1,0:T(8,128)} %collective-permute-done.refs_0_, ...), custom_call_target="tpu_custom_call", output_to_operand_aliasing={{0}: (6, {})} | custom-call | flops 16777216 | bytes 8388608 | tf_op jit(solution)/shard_map/edge/pallas_call | solution.py:772
  36.3 1.3 %collective-permute-start.8 = (f32[3,256,128]{2,1,0:T(8,128)S(1)}, f32[3,256,128]{2,1,0:T(8,128)S(1)}, u32[]{:S(2)}, u32[]{:S(2)}) collective-permute-start(f32[3,256,128]{2,1,0:T(8,128)S(1)} %get-tuple-element.28), channel_id=1, source_target_pairs={{4,8},{20,24},{8,4},{24,20},{12,28},{16,0},{5,9},{21,25},{9,5},{25... | collective-permute-start | bytes 1179656 | tf_op jit(solution)/shard_map/ppermute | solution.py:847
  37.6 0.1 collective-permute-start.9
  37.7 0.7 collective-permute-start.7
  38.4 2.5 %local_sums.1.refs_1_ = f32[8,128]{1,0:T(8,128)S(1)} custom-call(s32[6,8]{1,0:T(8,128)S(1)} %copy.27.links_ref, f32[8,128]{1,0:T(8,128)S(1)} %pad.4.geo_in, f32[8,512,128]{2,1,0:T(8,128)S(1)} %get-tuple-element.30.f_ref.refs_5_.refs_4_), custom_call_target="tpu_custom_call" | custom-call | flops 16777216 | bytes 8388608 | tf_op jit(solution)/shard_map/local_sums/pallas_call | solution.py:298
  40.9 5.1 %collective-permute-done.8.refs_1_ = f32[3,256,128]{2,1,0:T(8,128)S(1)} collective-permute-done((f32[3,256,128]{2,1,0:T(8,128)S(1)}, f32[3,256,128]{2,1,0:T(8,128)S(1)}, u32[]{:S(2)}, u32[]{:S(2)}) %collective-permute-start.8) | collective-permute-done | bytes 393248 | tf_op jit(solution)/shard_map/ppermute | solution.py:847
  46.0 1.4 %collective-permute-start.10 = (f32[3,256,128]{2,1,0:T(8,128)S(1)}, f32[3,256,128]{2,1,0:T(8,128)S(1)}, u32[]{:S(2)}, u32[]{:S(2)}) collective-permute-start(f32[3,256,128]{2,1,0:T(8,128)S(1)} %collective-permute-done.8.refs_1_), channel_id=1, source_target_pairs={{28,16},{0,12},{29,17},{1,13},{30,18},{2,14},{31,19},{3,15}} | collective-permute-start | bytes 1179656 | tf_op jit(solution)/shard_map/ppermute | solution.py:856
  47.4 3.7 %collective-permute-start.13 = (f32[8,128]{1,0:T(8,128)S(1)}, f32[8,128]{1,0:T(8,128)S(1)}, u32[]{:S(2)}, u32[]{:S(2)}) collective-permute-start(f32[8,128]{1,0:T(8,128)S(1)} %local_sums.1.refs_1_), channel_id=1, source_target_pairs={{0,3},{1,2},{2,1},{3,0},{4,7},{5,6},{6,5},{7,4},{8,11},{9,10},{10,... | collective-permute-start | bytes 12296 | tf_op jit(solution)/shard_map/ppermute | solution.py:451
  51.1 0.6 collective-permute-start.12
  51.7 1.2 %collective-permute-done.13.refs_4_ = f32[8,128]{1,0:T(8,128)S(1)} collective-permute-done((f32[8,128]{1,0:T(8,128)S(1)}, f32[8,128]{1,0:T(8,128)S(1)}, u32[]{:S(2)}, u32[]{:S(2)}) %collective-permute-start.13) | collective-permute-done | bytes 4128 | tf_op jit(solution)/shard_map/ppermute | solution.py:451
  52.9 0.9 %collective-permute-start.11 = (f32[8,128]{1,0:T(8,128)S(1)}, f32[8,128]{1,0:T(8,128)S(1)}, u32[]{:S(2)}, u32[]{:S(2)}) collective-permute-start(f32[8,128]{1,0:T(8,128)S(1)} %local_sums.1.refs_1_), channel_id=1, source_target_pairs={{0,1},{1,0},{2,3},{3,2},{4,5},{5,4},{6,7},{7,6},{8,9},{9,8},{10,11... | collective-permute-start | bytes 12296 | tf_op jit(solution)/shard_map/ppermute | solution.py:451
  53.8 4.1 %flux.3.refs_6_ = f32[4096,128]{1,0:T(8,128)S(1)} custom-call(s32[6,8]{1,0:T(8,128)S(1)} %copy.27.links_ref, f32[8,128]{1,0:T(8,128)S(1)} %pad.4.geo_in, f32[8,512,128]{2,1,0:T(8,128)S(1)} %get-tuple-element.30.f_ref.refs_5_.refs_4_), custom_call_target="tpu_custom_call" | custom-call | flops 29360128 | bytes 14680064 | tf_op jit(solution)/shard_map/flux/pallas_call | solution.py:559
  57.9 0.0 collective-permute-done.12.refs_3_
  57.9 0.0 collective-permute-done.11.refs_2_
  57.9 6.3 %add_target.3 = (f32[4096,128]{1,0:T(8,128)S(1)}, f32[8,128]{1,0:T(8,128)}) custom-call(s32[6,8]{1,0:T(8,128)S(1)} %copy.27.links_ref, f32[8,128]{1,0:T(8,128)S(1)} %pad.4.geo_in, f32[8,128]{1,0:T(8,128)S(1)} %get-tuple-element.32.refs_0_, f32[8,128]{1,0:T(8,128)S(1)} %local_sums.1.refs_1_, ...), custom_call_target="tpu_custom_call", output_to_operand_aliasing={{0}: (8, {})} | custom-call | flops 29360128 | bytes 14680064 | tf_op jit(solution)/shard_map/add_target/pallas_call | solution.py:677
  64.2 0.0 collective-permute-done.7.refs_0_
  64.2 2.0 %last_edge.1 = (f32[4096,128]{1,0:T(8,128)}, f32[8,128]{1,0:T(8,128)S(1)}) custom-call(f32[8,128]{1,0:T(8,128)S(1)} %pad.4.geo_in, f32[12,512,128]{2,1,0:T(8,128)S(1)} %geometry.1.pairs_ref, f32[3,256,128]{2,1,0:T(8,128)S(1)} %collective-permute-done.7.refs_0_, f32[3,256,128]{2,1,0:T(8,128)S(1)} %collective-permute-done.8.refs_1_, ...), custom_call_target="tpu_custom_call" | custom-call | flops 16777216 | bytes 8388608 | tf_op jit(solution)/shard_map/last_edge/pallas_call | solution.py:821
  66.2 3.0 %collective-permute-start.16 = (f32[8,128]{1,0:T(8,128)S(1)}, f32[8,128]{1,0:T(8,128)S(1)}, u32[]{:S(2)}, u32[]{:S(2)}) collective-permute-start(f32[8,128]{1,0:T(8,128)S(1)} %get-tuple-element.35.refs_0_), channel_id=1, source_target_pairs={{0,3},{1,2},{2,1},{3,0},{4,7},{5,6},{6,5},{7,4},{8,11},{9,10},{10,... | collective-permute-start | bytes 12296 | tf_op jit(solution)/shard_map/ppermute | solution.py:451
  69.2 0.4 collective-permute-start.15
  69.6 1.1 %collective-permute-start.14 = (f32[8,128]{1,0:T(8,128)S(1)}, f32[8,128]{1,0:T(8,128)S(1)}, u32[]{:S(2)}, u32[]{:S(2)}) collective-permute-start(f32[8,128]{1,0:T(8,128)S(1)} %get-tuple-element.35.refs_0_), channel_id=1, source_target_pairs={{0,1},{1,0},{2,3},{3,2},{4,5},{5,4},{6,7},{7,6},{8,9},{9,8},{10,11... | collective-permute-start | bytes 12296 | tf_op jit(solution)/shard_map/ppermute | solution.py:451
  70.7 1.0 %collective-permute-done.16.refs_3_ = f32[8,128]{1,0:T(8,128)S(1)} collective-permute-done((f32[8,128]{1,0:T(8,128)S(1)}, f32[8,128]{1,0:T(8,128)S(1)}, u32[]{:S(2)}, u32[]{:S(2)}) %collective-permute-start.16) | collective-permute-done | bytes 4128 | tf_op jit(solution)/shard_map/ppermute | solution.py:451
  71.7 2.0 %collective-permute-done.15.refs_2_ = f32[8,128]{1,0:T(8,128)S(1)} collective-permute-done((f32[8,128]{1,0:T(8,128)S(1)}, f32[8,128]{1,0:T(8,128)S(1)}, u32[]{:S(2)}, u32[]{:S(2)}) %collective-permute-start.15) | collective-permute-done | bytes 4128 | tf_op jit(solution)/shard_map/ppermute | solution.py:451
  73.7 0.6 copy-done.3
  74.3 0.6 copy-done.4
  74.9 1.4 %macro.1 = f32[8,8]{1,0:T(8,128)} custom-call(f32[8,128]{1,0:T(8,128)} %copy-done, f32[8,128]{1,0:T(8,128)} %copy-done.4, f32[8,128]{1,0:T(8,128)} %copy-done.3, f32[8,128]{1,0:T(8,128)} %copy-done.2), custom_call_target="tpu_custom_call" | custom-call | tf_op jit(solution)/shard_map/macro/pallas_call | solution.py:489
  (23 shorter events, 0.1 us)
Async XLA Ops:
  0.6 9.3 %copy-start.5 = (s32[6,8]{1,0:T(8,128)S(1)}, s32[6,8]{1,0:T(8,128)}, u32[]{:S(2)}) copy-start(s32[6,8]{1,0:T(8,128)} %param.6) | copy-start | bytes 580
  0.6 9.4 %copy-start.6 = (f32[8]{0:T(128)S(1)}, f32[8]{0:T(128)}, u32[]{:S(2)}) copy-start(f32[8]{0:T(128)} %param.8) | copy-start | bytes 100
  0.7 9.4 %copy-start.7 = (f32[8]{0:T(128)S(1)}, f32[8]{0:T(128)}, u32[]{:S(2)}) copy-start(f32[8]{0:T(128)} %param.9) | copy-start | bytes 100
  0.7 9.6 %copy-start.1 = (f32[3,6,8]{2,1,0:T(8,128)S(1)}, f32[3,6,8]{2,1,0:T(8,128)}, u32[]{:S(2)}) copy-start(f32[3,6,8]{2,1,0:T(8,128)} %param.7) | copy-start | bytes 1732
  3.5 10.5 %collective-permute-start.1 = (f32[3,256,128]{2,1,0:T(8,128)}, f32[3,256,128]{2,1,0:T(8,128)S(1)}, u32[]{:S(2)}, u32[]{:S(2)}) collective-permute-start(f32[3,256,128]{2,1,0:T(8,128)} %get-tuple-element.20), channel_id=1, source_target_pairs={{4,8},{20,24},{8,4},{24,20},{12,28},{16,0},{5,9},{21,25},{9,5},{25... | collective-permute-start | bytes 1179656 | tf_op jit(solution)/shard_map/ppermute | solution.py:847
  4.8 29.3 %collective-permute-start.2 = (f32[3,512,128]{2,1,0:T(8,128)}, f32[3,512,128]{2,1,0:T(8,128)S(1)}, u32[]{:S(2)}, u32[]{:S(2)}) collective-permute-start(f32[3,512,128]{2,1,0:T(8,128)} %get-tuple-element.21), channel_id=1, source_target_pairs={{0,4},{8,12},{16,20},{24,28},{4,0},{12,8},{20,16},{28,24},{1,5},{9... | collective-permute-start | bytes 2359304 | tf_op jit(solution)/shard_map/ppermute | solution.py:848
  8.5 25.6 %collective-permute-start = (f32[3,256,128]{2,1,0:T(8,128)}, f32[3,256,128]{2,1,0:T(8,128)}, u32[]{:S(2)}, u32[]{:S(2)}) collective-permute-start(f32[3,256,128]{2,1,0:T(8,128)} %get-tuple-element.19), channel_id=1, source_target_pairs={{4,8},{12,16},{20,24},{8,4},{16,12},{24,20},{5,9},{13,17},{21,25},... | collective-permute-start | bytes 1179656 | tf_op jit(solution)/shard_map/ppermute | solution.py:848
  14.0 20.1 %collective-permute-start.3 = (f32[3,256,128]{2,1,0:T(8,128)S(1)}, f32[3,256,128]{2,1,0:T(8,128)S(1)}, u32[]{:S(2)}, u32[]{:S(2)}) collective-permute-start(f32[3,256,128]{2,1,0:T(8,128)S(1)} %collective-permute-done.1.refs_1_), channel_id=1, source_target_pairs={{28,16},{0,12},{29,17},{1,13},{30,18},{2,14},{31,19},{3,15}} | collective-permute-start | bytes 1179656 | tf_op jit(solution)/shard_map/ppermute | solution.py:856
  18.2 5.5 %collective-permute-start.6 = (f32[8,128]{1,0:T(8,128)S(1)}, f32[8,128]{1,0:T(8,128)S(1)}, u32[]{:S(2)}, u32[]{:S(2)}) collective-permute-start(f32[8,128]{1,0:T(8,128)S(1)} %get-tuple-element.23.refs_0_), channel_id=1, source_target_pairs={{0,3},{1,2},{2,1},{3,0},{4,7},{5,6},{6,5},{7,4},{8,11},{9,10},{10,... | collective-permute-start | bytes 12296 | tf_op jit(solution)/shard_map/ppermute | solution.py:451
  21.8 7.9 %collective-permute-start.5 = (f32[8,128]{1,0:T(8,128)S(1)}, f32[8,128]{1,0:T(8,128)S(1)}, u32[]{:S(2)}, u32[]{:S(2)}) collective-permute-start(f32[8,128]{1,0:T(8,128)S(1)} %get-tuple-element.23.refs_0_), channel_id=1, source_target_pairs={{0,2},{1,3},{2,0},{3,1},{4,6},{5,7},{6,4},{7,5},{8,10},{9,11},{10,... | collective-permute-start | bytes 12296 | tf_op jit(solution)/shard_map/ppermute | solution.py:451
  23.6 6.1 %collective-permute-start.4 = (f32[8,128]{1,0:T(8,128)S(1)}, f32[8,128]{1,0:T(8,128)S(1)}, u32[]{:S(2)}, u32[]{:S(2)}) collective-permute-start(f32[8,128]{1,0:T(8,128)S(1)} %get-tuple-element.23.refs_0_), channel_id=1, source_target_pairs={{0,1},{1,0},{2,3},{3,2},{4,5},{5,4},{6,7},{7,6},{8,9},{9,8},{10,11... | collective-permute-start | bytes 12296 | tf_op jit(solution)/shard_map/ppermute | solution.py:451
  36.3 9.7 %collective-permute-start.8 = (f32[3,256,128]{2,1,0:T(8,128)S(1)}, f32[3,256,128]{2,1,0:T(8,128)S(1)}, u32[]{:S(2)}, u32[]{:S(2)}) collective-permute-start(f32[3,256,128]{2,1,0:T(8,128)S(1)} %get-tuple-element.28), channel_id=1, source_target_pairs={{4,8},{20,24},{8,4},{24,20},{12,28},{16,0},{5,9},{21,25},{9,5},{25... | collective-permute-start | bytes 1179656 | tf_op jit(solution)/shard_map/ppermute | solution.py:847
  37.6 26.6 %collective-permute-start.9 = (f32[3,512,128]{2,1,0:T(8,128)S(1)}, f32[3,512,128]{2,1,0:T(8,128)S(1)}, u32[]{:S(2)}, u32[]{:S(2)}) collective-permute-start(f32[3,512,128]{2,1,0:T(8,128)S(1)} %get-tuple-element.29), channel_id=1, source_target_pairs={{0,4},{8,12},{16,20},{24,28},{4,0},{12,8},{20,16},{28,24},{1,5},{9... | collective-permute-start | bytes 2359304 | tf_op jit(solution)/shard_map/ppermute | solution.py:848
  37.7 26.5 %collective-permute-start.7 = (f32[3,256,128]{2,1,0:T(8,128)S(1)}, f32[3,256,128]{2,1,0:T(8,128)S(1)}, u32[]{:S(2)}, u32[]{:S(2)}) collective-permute-start(f32[3,256,128]{2,1,0:T(8,128)S(1)} %get-tuple-element.27), channel_id=1, source_target_pairs={{4,8},{12,16},{20,24},{8,4},{16,12},{24,20},{5,9},{13,17},{21,25},... | collective-permute-start | bytes 1179656 | tf_op jit(solution)/shard_map/ppermute | solution.py:848
  46.0 18.2 %collective-permute-start.10 = (f32[3,256,128]{2,1,0:T(8,128)S(1)}, f32[3,256,128]{2,1,0:T(8,128)S(1)}, u32[]{:S(2)}, u32[]{:S(2)}) collective-permute-start(f32[3,256,128]{2,1,0:T(8,128)S(1)} %collective-permute-done.8.refs_1_), channel_id=1, source_target_pairs={{28,16},{0,12},{29,17},{1,13},{30,18},{2,14},{31,19},{3,15}} | collective-permute-start | bytes 1179656 | tf_op jit(solution)/shard_map/ppermute | solution.py:856
  47.4 5.5 %collective-permute-start.13 = (f32[8,128]{1,0:T(8,128)S(1)}, f32[8,128]{1,0:T(8,128)S(1)}, u32[]{:S(2)}, u32[]{:S(2)}) collective-permute-start(f32[8,128]{1,0:T(8,128)S(1)} %local_sums.1.refs_1_), channel_id=1, source_target_pairs={{0,3},{1,2},{2,1},{3,0},{4,7},{5,6},{6,5},{7,4},{8,11},{9,10},{10,... | collective-permute-start | bytes 12296 | tf_op jit(solution)/shard_map/ppermute | solution.py:451
  51.1 6.8 %collective-permute-start.12 = (f32[8,128]{1,0:T(8,128)S(1)}, f32[8,128]{1,0:T(8,128)S(1)}, u32[]{:S(2)}, u32[]{:S(2)}) collective-permute-start(f32[8,128]{1,0:T(8,128)S(1)} %local_sums.1.refs_1_), channel_id=1, source_target_pairs={{0,2},{1,3},{2,0},{3,1},{4,6},{5,7},{6,4},{7,5},{8,10},{9,11},{10,... | collective-permute-start | bytes 12296 | tf_op jit(solution)/shard_map/ppermute | solution.py:451
  52.9 5.0 %collective-permute-start.11 = (f32[8,128]{1,0:T(8,128)S(1)}, f32[8,128]{1,0:T(8,128)S(1)}, u32[]{:S(2)}, u32[]{:S(2)}) collective-permute-start(f32[8,128]{1,0:T(8,128)S(1)} %local_sums.1.refs_1_), channel_id=1, source_target_pairs={{0,1},{1,0},{2,3},{3,2},{4,5},{5,4},{6,7},{7,6},{8,9},{9,8},{10,11... | collective-permute-start | bytes 12296 | tf_op jit(solution)/shard_map/ppermute | solution.py:451
  66.2 7.5 %copy-start = (f32[8,128]{1,0:T(8,128)}, f32[8,128]{1,0:T(8,128)S(1)}, u32[]{:S(2)}) copy-start(f32[8,128]{1,0:T(8,128)S(1)} %get-tuple-element.35.refs_0_) | copy-start | bytes 12292
  66.2 5.5 %collective-permute-start.16 = (f32[8,128]{1,0:T(8,128)S(1)}, f32[8,128]{1,0:T(8,128)S(1)}, u32[]{:S(2)}, u32[]{:S(2)}) collective-permute-start(f32[8,128]{1,0:T(8,128)S(1)} %get-tuple-element.35.refs_0_), channel_id=1, source_target_pairs={{0,3},{1,2},{2,1},{3,0},{4,7},{5,6},{6,5},{7,4},{8,11},{9,10},{10,... | collective-permute-start | bytes 12296 | tf_op jit(solution)/shard_map/ppermute | solution.py:451
  69.2 4.5 %collective-permute-start.15 = (f32[8,128]{1,0:T(8,128)S(1)}, f32[8,128]{1,0:T(8,128)S(1)}, u32[]{:S(2)}, u32[]{:S(2)}) collective-permute-start(f32[8,128]{1,0:T(8,128)S(1)} %get-tuple-element.35.refs_0_), channel_id=1, source_target_pairs={{0,2},{1,3},{2,0},{3,1},{4,6},{5,7},{6,4},{7,5},{8,10},{9,11},{10,... | collective-permute-start | bytes 12296 | tf_op jit(solution)/shard_map/ppermute | solution.py:451
  69.6 4.1 %collective-permute-start.14 = (f32[8,128]{1,0:T(8,128)S(1)}, f32[8,128]{1,0:T(8,128)S(1)}, u32[]{:S(2)}, u32[]{:S(2)}) collective-permute-start(f32[8,128]{1,0:T(8,128)S(1)} %get-tuple-element.35.refs_0_), channel_id=1, source_target_pairs={{0,1},{1,0},{2,3},{3,2},{4,5},{5,4},{6,7},{7,6},{8,9},{9,8},{10,11... | collective-permute-start | bytes 12296 | tf_op jit(solution)/shard_map/ppermute | solution.py:451
  71.7 2.0 %copy-start.2 = (f32[8,128]{1,0:T(8,128)}, f32[8,128]{1,0:T(8,128)S(1)}, u32[]{:S(2)}) copy-start(f32[8,128]{1,0:T(8,128)S(1)} %collective-permute-done.16.refs_3_) | copy-start | bytes 12292
  73.7 0.6 copy-start.3
  74.3 0.6 copy-start.4

commit v6 on v3

--- a/solution.py
+++ b/solution.py
@@ -428,18 +428,14 @@
 
 
 def gather_sums(tile):
-    size = lax.axis_size("vel")
-    if size not in (2, 4):
-        return [lax.psum(tile, "vel")]
-    others = [lax.ppermute(tile, "vel", [(i, i ^ s) for i in range(size)]) for s in range(1, size)]
-    return [tile, *others]
-
-
-def add_tiles(refs):
-    tiles = [r[...] for r in refs]
-    while len(tiles) > 1:
-        tiles = [tiles[i] + tiles[i + 1] for i in range(0, len(tiles), 2)]
-    return tiles[0]
+    return lax.all_gather(tile, "vel")
+
+
+def add_tiles(ref):
+    out = ref[0]
+    for i in range(1, ref.shape[0]):
+        out = out + ref[i]
+    return out
 
 
 def quantities(tile):
@@ -459,9 +455,8 @@
     return n, u, temperature, q
 
 
-def macro_kernel(*refs):
-    out_ref = refs[-1]
-    n, u, temperature, q = quantities(add_tiles(refs[:-1]))
+def macro_kernel(sums_ref, out_ref):
+    n, u, temperature, q = quantities(add_tiles(sums_ref))
     lane, sub = lane_iota(), sub_iota()
     for i, x in enumerate((n, *u, temperature, *q)):
         row = jnp.sum(jnp.where(lane == sub, x, 0.0), axis=0, keepdims=True)
@@ -471,11 +466,11 @@
 def macro(tiles):
     return pl.pallas_call(
         macro_kernel,
-        in_specs=[spec(pltpu.VMEM)] * len(tiles),
+        in_specs=[spec(pltpu.VMEM)],
         out_specs=spec(pltpu.VMEM),
         out_shape=array(8, SUB),
         name="macro",
-    )(*tiles)
+    )(tiles)
 
 
 def placer(native):
@@ -553,12 +548,12 @@
     )(links, geo, f)
 
 
-def target_kernel(native, count, links_ref, geo_in, absorbed_in, *refs):
-    sums_refs, (f_ref, part_ref, out_ref, sum_out, geo_ref, ta, coef) = refs[:count], refs[count:]
+def target_kernel(native, links_ref, geo_in, absorbed_in, *refs):
+    tiles_ref, f_ref, part_ref, out_ref, sum_out, geo_ref, ta, coef = refs
     planes = f_ref.shape[1] // CHUNKS
     place = placer(native)
     unpack_geo(geo_in, geo_ref)
-    sums = add_tiles(sums_refs)
+    sums = add_tiles(tiles_ref)
     sum_out[...] = sums
     absorbed = sums if absorbed_in is None else absorbed_in[...]
     n, u, temperature, q = quantities(sums)
@@ -648,13 +643,13 @@
 def add_target(native, links, geo, absorbed, tiles, f, part):
     rows = f.shape[1]
     vmem = spec(pltpu.VMEM)
-    given = [links, geo] + ([] if absorbed is None else [absorbed]) + list(tiles) + [f, part]
+    given = [links, geo] + ([] if absorbed is None else [absorbed]) + [tiles, f, part]
 
     def kernel(links_ref, geo_in, *refs):
         if absorbed is None:
-            target_kernel(native, len(tiles), links_ref, geo_in, None, *refs)
+            target_kernel(native, links_ref, geo_in, None, *refs)
         else:
-            target_kernel(native, len(tiles), links_ref, geo_in, *refs)
+            target_kernel(native, links_ref, geo_in, *refs)
 
     return pl.pallas_call(
         kernel,

time: 63.4 us -> 85 us (1.34)
  the two profiles are of different devices: /device:TPU:4 before, /device:TPU:0 now
where the time goes in v6:
time: 85 us; the launch traced here: 84.2 us
  blocking collectives  40.3 us (47%)
  Pallas kernels  34.1 us (40%)
  starting transfers between devices  8.5 us (10%)
    all_gather x3, blocking collectives, gather_sums(): return lax.all_gather(tile, 'vel')  40.3 us
    pallas_call x2, Pallas kernels, add_target(): pl.pallas_call(kernel, in_specs=[spec(pltpu.SMEM)] + [vmem] * (len(given)...  10.1 us
    ppermute x4, starting transfers between devices, exchange(): out.append(lax.ppermute(x, 'space', pairs + [(j, i) for i, j in pairs]))  8.5 us
    pallas_call x2, Pallas kernels, flux(): pl.pallas_call(functools.partial(flux_kernel, native), in_specs=[spec(plt...  8.07 us
    pallas_call x1, Pallas kernels, first_sums(): pl.pallas_call(first_sums_kernel, in_specs=[spec(pltpu.SMEM), spec(pltpu....  3.26 us
    pallas_call x1, Pallas kernels, first_rows(): pl.pallas_call(first_rows_kernel, in_specs=[spec(pltpu.HBM)], out_specs=[...  2.82 us
    pallas_call x1, Pallas kernels, local_sums(): pl.pallas_call(sums_kernel, in_specs=[spec(pltpu.SMEM), spec(pltpu.VMEM),...  2.35 us
    pallas_call x1, Pallas kernels, edge(): pl.pallas_call(edge_kernel, in_specs=[spec(pltpu.VMEM)] * 5, out_specs=[s...  2.32 us
  transfers between devices with their start and end apart: 4, of which 0 were waited for; matrix products, arithmetic and copies ran while one was open for 1% of the time, Pallas kernels for 30%

profile of v6, /device:TPU:0, one launch (start us, length us, event | category | flops | bytes accessed | tf_op | source)
XLA Modules:
  0.0 84.2 jit_solution(7878747551392504615)
XLA Ops:
  0.6 0.0 copy-start.1
  0.6 0.0 copy-start.2
  0.7 0.0 copy-start.3
  0.7 0.0 copy-start
  0.7 2.8 %first_rows.1 = (f32[4096,128]{1,0:T(8,128)S(1)}, f32[3,512,128]{2,1,0:T(8,128)}, f32[3,512,128]{2,1,0:T(8,128)}) custom-call(f32[4096,128]{1,0:T(8,128)} %bitcast.18), custom_call_target="tpu_custom_call" | custom-call | tf_op jit(solution)/shard_map/first_rows/pallas_call | solution.py:362
  3.5 0.7 collective-permute-start
  4.2 4.3 %collective-permute-start.1 = (f32[3,512,128]{2,1,0:T(8,128)}, f32[3,512,128]{2,1,0:T(8,128)}, u32[]{:S(2)}, u32[]{:S(2)}) collective-permute-start(f32[3,512,128]{2,1,0:T(8,128)} %get-tuple-element.16), channel_id=1, source_target_pairs={{0,4},{8,12},{16,20},{24,28},{4,0},{12,8},{20,16},{28,24},{1,5},{9... | collective-permute-start | bytes 2359304 | tf_op jit(solution)/shard_map/ppermute | solution.py:789
  8.5 0.0 copy-done.1
  8.5 0.1 copy.23
  8.6 0.0 copy-done.2
  8.6 0.1 copy.25
  8.7 0.0 copy-done.3
  8.7 0.1 copy.26
  8.8 0.1 copy.27.links_ref
  8.9 0.0 copy-done
  8.9 0.1 copy.34
  9.0 0.1 concatenate.3
  9.1 1.9 %geometry.1.pairs_ref = f32[12,512,128]{2,1,0:T(8,128)S(1)} custom-call(s32[6,8]{1,0:T(8,128)S(1)} %copy.27.links_ref, f32[8,128]{1,0:T(8,128)S(1)} %pad.4.geo_in), custom_call_target="tpu_custom_call" | custom-call | tf_op jit(solution)/shard_map/geometry/pallas_call | solution.py:419
  10.9 3.3 %first_sums.1 = (f32[8,512,128]{2,1,0:T(8,128)S(1)}, f32[8,128]{1,0:T(8,128)S(1)}) custom-call(s32[6,8]{1,0:T(8,128)S(1)} %copy.27.links_ref, f32[8,128]{1,0:T(8,128)S(1)} %pad.4.geo_in, f32[4096,128]{1,0:T(8,128)S(1)} %get-tuple-element.17.native_ref), custom_call_target="tpu_custom_call" | custom-call | tf_op jit(solution)/shard_map/first_sums/pallas_call | solution.py:310
  14.2 4.0 %flux.2.refs_2_ = f32[8,512,128]{2,1,0:T(8,128)S(1)} custom-call(s32[6,8]{1,0:T(8,128)S(1)} %copy.27.links_ref, f32[8,128]{1,0:T(8,128)S(1)} %pad.4.geo_in, f32[8,512,128]{2,1,0:T(8,128)S(1)} %get-tuple-element.18.f_ref.refs_1_.old_ref), custom_call_target="tpu_custom_call" | custom-call | tf_op jit(solution)/shard_map/flux/pallas_call | solution.py:537
  18.2 13.4 %all-gather = f32[32,128]{1,0:T(8,128)S(1)} all-gather(f32[8,128]{1,0:T(8,128)S(1)} %get-tuple-element.19), channel_id=2, replica_groups=mesh['space'=8,'vel'=4] {'vel'}, dimensions={0}, use_global_device_ids=true | all-gather | bytes 20480 | tf_op jit(solution)/shard_map/all_gather | solution.py:431
  31.6 4.1 %add_target.2 = (f32[8,512,128]{2,1,0:T(8,128)S(1)}, f32[8,128]{1,0:T(8,128)S(1)}) custom-call(s32[6,8]{1,0:T(8,128)S(1)} %copy.27.links_ref, f32[8,128]{1,0:T(8,128)S(1)} %pad.4.geo_in, f32[4,8,128]{2,1,0:T(8,128)S(1)} %bitcast.17, f32[8,512,128]{2,1,0:T(8,128)S(1)} %get-tuple-element.18.f_ref.refs_1_.old_ref, ...), custom_call_target="tpu_custom_call", output_to_operand_aliasing={{0}: (4, {})} | custom-call | tf_op jit(solution)/shard_map/add_target/pallas_call | solution.py:654
  35.7 0.0 collective-permute-done.far_in
  35.7 0.0 collective-permute-done.1.near_in
  35.7 2.3 %edge.1 = (f32[8,512,128]{2,1,0:T(8,128)S(1)}, f32[3,512,128]{2,1,0:T(8,128)S(1)}, f32[3,512,128]{2,1,0:T(8,128)S(1)}) custom-call(f32[12,512,128]{2,1,0:T(8,128)S(1)} %geometry.1.pairs_ref, f32[3,512,128]{2,1,0:T(8,128)S(1)} %collective-permute-done.far_in, f32[3,512,128]{2,1,0:T(8,128)} %collective-permute-done.1.near_in, ...), custom_call_target="tpu_custom_call", output_to_operand_aliasing={{0}: (4, {})} | custom-call | tf_op jit(solution)/shard_map/edge/pallas_call | solution.py:724
  38.0 0.7 collective-permute-start.2
  38.7 2.8 %collective-permute-start.3 = (f32[3,512,128]{2,1,0:T(8,128)S(1)}, f32[3,512,128]{2,1,0:T(8,128)S(1)}, u32[]{:S(2)}, u32[]{:S(2)}) collective-permute-start(f32[3,512,128]{2,1,0:T(8,128)S(1)} %get-tuple-element.22), channel_id=1, source_target_pairs={{0,4},{8,12},{16,20},{24,28},{4,0},{12,8},{20,16},{28,24},{1,5},{9... | collective-permute-start | bytes 2359304 | tf_op jit(solution)/shard_map/ppermute | solution.py:789
  41.5 2.3 %local_sums.1 = f32[8,128]{1,0:T(8,128)S(1)} custom-call(s32[6,8]{1,0:T(8,128)S(1)} %copy.27.links_ref, f32[8,128]{1,0:T(8,128)S(1)} %pad.4.geo_in, f32[8,512,128]{2,1,0:T(8,128)S(1)} %get-tuple-element.23.f_ref.refs_2_), custom_call_target="tpu_custom_call" | custom-call | tf_op jit(solution)/shard_map/local_sums/pallas_call | solution.py:293
  43.8 4.1 %flux.3.refs_3_ = f32[4096,128]{1,0:T(8,128)S(1)} custom-call(s32[6,8]{1,0:T(8,128)S(1)} %copy.27.links_ref, f32[8,128]{1,0:T(8,128)S(1)} %pad.4.geo_in, f32[8,512,128]{2,1,0:T(8,128)S(1)} %get-tuple-element.23.f_ref.refs_2_), custom_call_target="tpu_custom_call" | custom-call | tf_op jit(solution)/shard_map/flux/pallas_call | solution.py:537
  47.9 13.1 %all-gather.1 = f32[32,128]{1,0:T(8,128)S(1)} all-gather(f32[8,128]{1,0:T(8,128)S(1)} %local_sums.1), channel_id=3, replica_groups=mesh['space'=8,'vel'=4] {'vel'}, dimensions={0}, use_global_device_ids=true | all-gather | bytes 20480 | tf_op jit(solution)/shard_map/all_gather | solution.py:431
  61.1 6.0 %add_target.3 = (f32[4096,128]{1,0:T(8,128)S(1)}, f32[8,128]{1,0:T(8,128)}) custom-call(s32[6,8]{1,0:T(8,128)S(1)} %copy.27.links_ref, f32[8,128]{1,0:T(8,128)S(1)} %pad.4.geo_in, f32[8,128]{1,0:T(8,128)S(1)} %get-tuple-element.24.refs_0_, f32[4,8,128]{2,1,0:T(8,128)S(1)} %bitcast.16, ...), custom_call_target="tpu_custom_call", output_to_operand_aliasing={{0}: (5, {})} | custom-call | tf_op jit(solution)/shard_map/add_target/pallas_call | solution.py:654
  67.0 0.0 collective-permute-done.2.far_ref
  67.0 0.0 collective-permute-done.3.near_ref
  67.0 1.9 %last_edge.1 = (f32[4096,128]{1,0:T(8,128)}, f32[8,128]{1,0:T(8,128)S(1)}) custom-call(f32[8,128]{1,0:T(8,128)S(1)} %pad.4.geo_in, f32[12,512,128]{2,1,0:T(8,128)S(1)} %geometry.1.pairs_ref, f32[3,512,128]{2,1,0:T(8,128)S(1)} %collective-permute-done.2.far_ref, f32[3,512,128]{2,1,0:T(8,128)S(1)} %collective-permute-done.3.near_ref, ...), custom_call_target="tpu_custom_call" | custom-call | tf_op jit(solution)/shard_map/last_edge/pallas_call | solution.py:773
  69.0 13.8 %all-gather.2 = f32[32,128]{1,0:T(8,128)} all-gather(f32[8,128]{1,0:T(8,128)S(1)} %get-tuple-element.27), channel_id=4, replica_groups=mesh['space'=8,'vel'=4] {'vel'}, dimensions={0}, use_global_device_ids=true | all-gather | bytes 20480 | tf_op jit(solution)/shard_map/all_gather | solution.py:431
  82.8 1.4 %macro.1 = f32[8,8]{1,0:T(8,128)} custom-call(f32[4,8,128]{2,1,0:T(8,128)} %bitcast.19), custom_call_target="tpu_custom_call" | custom-call | tf_op jit(solution)/shard_map/macro/pallas_call | solution.py:467
  (4 shorter events, 0.0 us)
Async XLA Ops:
  0.6 7.9 %copy-start.1 = (s32[6,8]{1,0:T(8,128)S(1)}, s32[6,8]{1,0:T(8,128)}, u32[]{:S(2)}) copy-start(s32[6,8]{1,0:T(8,128)} %param.6) | copy-start | bytes 580
  0.6 8.0 %copy-start.2 = (f32[8]{0:T(128)S(1)}, f32[8]{0:T(128)}, u32[]{:S(2)}) copy-start(f32[8]{0:T(128)} %param.8) | copy-start | bytes 100
  0.7 8.1 %copy-start.3 = (f32[8]{0:T(128)S(1)}, f32[8]{0:T(128)}, u32[]{:S(2)}) copy-start(f32[8]{0:T(128)} %param.9) | copy-start | bytes 100
  0.7 8.2 %copy-start = (f32[3,6,8]{2,1,0:T(8,128)S(1)}, f32[3,6,8]{2,1,0:T(8,128)}, u32[]{:S(2)}) copy-start(f32[3,6,8]{2,1,0:T(8,128)} %param.7) | copy-start | bytes 1732
  3.5 32.2 %collective-permute-start = (f32[3,512,128]{2,1,0:T(8,128)}, f32[3,512,128]{2,1,0:T(8,128)S(1)}, u32[]{:S(2)}, u32[]{:S(2)}) collective-permute-start(f32[3,512,128]{2,1,0:T(8,128)} %get-tuple-element.15), channel_id=1, source_target_pairs={{4,8},{12,16},{20,24},{8,4},{16,12},{24,20},{5,9},{13,17},{21,25},... | collective-permute-start | bytes 2359304 | tf_op jit(solution)/shard_map/ppermute | solution.py:789
  4.2 31.5 %collective-permute-start.1 = (f32[3,512,128]{2,1,0:T(8,128)}, f32[3,512,128]{2,1,0:T(8,128)}, u32[]{:S(2)}, u32[]{:S(2)}) collective-permute-start(f32[3,512,128]{2,1,0:T(8,128)} %get-tuple-element.16), channel_id=1, source_target_pairs={{0,4},{8,12},{16,20},{24,28},{4,0},{12,8},{20,16},{28,24},{1,5},{9... | collective-permute-start | bytes 2359304 | tf_op jit(solution)/shard_map/ppermute | solution.py:789
  38.0 29.0 %collective-permute-start.2 = (f32[3,512,128]{2,1,0:T(8,128)S(1)}, f32[3,512,128]{2,1,0:T(8,128)S(1)}, u32[]{:S(2)}, u32[]{:S(2)}) collective-permute-start(f32[3,512,128]{2,1,0:T(8,128)S(1)} %get-tuple-element.21), channel_id=1, source_target_pairs={{4,8},{12,16},{20,24},{8,4},{16,12},{24,20},{5,9},{13,17},{21,25},... | collective-permute-start | bytes 2359304 | tf_op jit(solution)/shard_map/ppermute | solution.py:789
  38.7 28.3 %collective-permute-start.3 = (f32[3,512,128]{2,1,0:T(8,128)S(1)}, f32[3,512,128]{2,1,0:T(8,128)S(1)}, u32[]{:S(2)}, u32[]{:S(2)}) collective-permute-start(f32[3,512,128]{2,1,0:T(8,128)S(1)} %get-tuple-element.22), channel_id=1, source_target_pairs={{0,4},{8,12},{16,20},{24,28},{4,0},{12,8},{20,16},{28,24},{1,5},{9... | collective-permute-start | bytes 2359304 | tf_op jit(solution)/shard_map/ppermute | solution.py:789

commit v7 on v3

--- a/solution.py
+++ b/solution.py
@@ -87,12 +87,6 @@
         xb, xc = tile_nodes(t)
         out.append(scale * jnp.exp(-0.5 * (xb * xb + xc * xc) * rt))
     return out
-
-
-def unpack_geo(geo_in, geo_ref):
-    tile = geo_in[...]
-    for p in range(GEO):
-        geo_ref[p] = column(tile, p)
 
 
 def pack_sums(arrays, start):
@@ -251,19 +245,17 @@
     lax.fori_loop(0, SUB, cell, 0)
 
 
-def sums_kernel(links_ref, geo_in, f_ref, sums_out, geo_ref, parts_ref, face_ref):
+def sums_kernel(links_ref, geo_ref, f_ref, sums_out, parts_ref, face_ref):
     planes = f_ref.shape[1] // CHUNKS
-    unpack_geo(geo_in, geo_ref)
     y = polynomial_sums(f_ref, planes, parts_ref)
     packed = pack_sums(finish_polynomials(y, geo_ref[FIRST], planes), 0)
     wall_sums(f_ref, planes, links_ref, geo_ref, face_ref, False)
     sums_out[...] = packed + pack_sums([over_sublanes(face_ref, k) for k in range(FACES)], EMIT)
 
 
-def first_sums_kernel(links_ref, geo_in, native_ref, f_ref, sums_out, geo_ref, face_ref):
+def first_sums_kernel(links_ref, geo_ref, native_ref, f_ref, sums_out, face_ref):
     rows = f_ref.shape[1]
     planes = rows // CHUNKS
-    unpack_geo(geo_in, geo_ref)
 
     def group(j, _):
         for g in range(SUB):
@@ -287,6 +279,11 @@
 
 def params():
     return pltpu.CompilerParams(vmem_limit_bytes=VMEM_LIMIT)
+
+
+def traffic(rows, profiles):
+    size = SUB * rows * LANES
+    return pl.CostEstimate(flops=8 * profiles * size, bytes_accessed=4 * profiles * size, transcendentals=0)
 
 
 def local_sums(links, geo, f):
@@ -296,11 +293,11 @@
         out_specs=spec(pltpu.VMEM),
         out_shape=array(SUB, LANES),
         scratch_shapes=[
-            pltpu.VMEM((GEO, SUB, LANES), F32),
-            pltpu.VMEM((10, SUB * SUB, LANES), F32),
+                pltpu.VMEM((10, SUB * SUB, LANES), F32),
             pltpu.VMEM((FACES, SUB * SUB, LANES), F32),
         ],
         compiler_params=params(),
+        cost_estimate=traffic(f.shape[1], 4),
         name="local_sums",
     )(links, geo, f)
 
@@ -313,10 +310,10 @@
         out_specs=[spec(pltpu.VMEM)] * 2,
         out_shape=[array(SUB, rows, LANES), array(SUB, LANES)],
         scratch_shapes=[
-            pltpu.VMEM((GEO, SUB, LANES), F32),
-            pltpu.VMEM((2 * FACES, SUB * SUB, LANES), F32),
+                pltpu.VMEM((2 * FACES, SUB * SUB, LANES), F32),
         ],
         compiler_params=params(),
+        cost_estimate=traffic(rows, 5),
         name="first_sums",
     )(links, geo, native)
 
@@ -366,14 +363,14 @@
         out_shape=[array(*native.shape), array(REACH, rows, LANES), array(REACH, rows, LANES)],
         scratch_shapes=[pltpu.SemaphoreType.DMA((SPLIT_PARTS,))],
         compiler_params=params(),
+        cost_estimate=traffic(rows, 4),
         name="first_rows",
     )(pltpu.with_memory_space_constraint(native, pltpu.HBM))
 
 
-def geometry_kernel(links_ref, geo_in, pairs_ref, geo_ref):
+def geometry_kernel(links_ref, geo_ref, pairs_ref):
     rows = pairs_ref.shape[1]
     planes = rows // CHUNKS
-    unpack_geo(geo_in, geo_ref)
     first = splat(geo_ref, FIRST, 0)
 
     def clear(j, _):
@@ -421,8 +418,8 @@
         in_specs=[spec(pltpu.SMEM), spec(pltpu.VMEM)],
         out_specs=spec(pltpu.VMEM),
         out_shape=array(2 * len(BEFORE_PAIRS), rows, LANES),
-        scratch_shapes=[pltpu.VMEM((GEO, SUB, LANES), F32)],
         compiler_params=params(),
+        cost_estimate=traffic(rows, 4),
         name="geometry",
     )(links, geo)
 
@@ -478,86 +475,82 @@
     )(*tiles)
 
 
-def placer(native):
-    def place(g, tile):
-        if native:
-            return (pl.ds(tile * SUB * SUB + g, SUB, stride=SUB), slice(None))
-        return (g, at_rows(tile * SUB), slice(None))
-
-    return place
-
-
-def flux_kernel(native, links_ref, geo_in, f_ref, out_ref, geo_ref, coef):
+def flux_kernel(links_ref, geo_ref, f_ref, out_ref, coef, source, face):
     planes = f_ref.shape[1] // CHUNKS
-    place = placer(native)
-    unpack_geo(geo_in, geo_ref)
     scale = -TIME_STEP / geo_ref[VOL]
     for i in range(3):
         whole = None
         for k in range(FACES):
             x = scale * geo_ref[FV + FACES * i + k]
-            coef[FACES * i + k] = x * geo_ref[LOCAL + k]
+            coef[FACES * i + k] = x
             whole = x if whole is None else whole + x
         coef[3 * FACES + i] = whole
 
     def cell(g, _):
-        source = []
+        count = 0
         for k in range(FACES):
             j = links_ref[k, g]
-            source.append(jnp.where(jnp.logical_and(j >= 0, j < SUB), j, g))
-        weight = [[splat(coef, FACES * i + k, g) for i in range(3)] for k in range(FACES)]
+            source[count] = j
+            face[count] = k
+            count = count + jnp.logical_and(j >= 0, j < SUB).astype(jnp.int32)
+        for n in range(FACES + 1):
+
+            @pl.when(count == n)
+            def _():
+                own_faces(g, n)
+
+        return 0
+
+    def own_faces(g, n):
+        at_source = [source[i] for i in range(n)]
+        weight = [[splat(coef, FACES * i + face[k], g) for i in range(3)] for k in range(n)]
         whole = [splat(coef, 3 * FACES + i, g) for i in range(3)]
         x0 = splat(geo_ref, FIRST, g)
         for pair in range(TILES // 2):
             base, stay = [], []
             for t in (2 * pair, 2 * pair + 1):
                 xb, xc = tile_nodes(t)
-                base.append([weight[k][1] * xb + weight[k][2] * xc for k in range(FACES)])
+                base.append([w[1] * xb + w[2] * xc for w in weight])
                 stay.append(1.0 + whole[1] * xb + whole[2] * xc)
 
             def plane(a, _):
                 xa = x0 + a.astype(F32) * H
-                sa = [weight[k][0] * xa for k in range(FACES)]
+                sa = [w[0] * xa for w in weight]
                 stay_a = whole[0] * xa
                 for i in range(2):
-                    tile = a * TILES + 2 * pair + i
-                    at = at_rows(tile * SUB)
+                    at = at_rows((a * TILES + 2 * pair + i) * SUB)
                     f = f_ref[g, at, :]
-                    terms = [
-                        jnp.maximum(sa[k] + base[i][k], 0.0) * (f_ref[source[k], at, :] - f)
-                        for k in range(FACES)
-                    ]
-                    inflow = (terms[0] + terms[1]) + (terms[2] + terms[3]) + (terms[4] + terms[5])
-                    out_ref[place(g, tile)] = f * (stay_a + stay[i]) + inflow
+                    acc = f * (stay_a + stay[i])
+                    for k in range(n):
+                        acc = acc + jnp.maximum(sa[k] + base[i][k], 0.0) * (f_ref[at_source[k], at, :] - f)
+                    out_ref[g, at, :] = acc
                 return 0
 
-            lax.fori_loop(0, planes, plane, 0, unroll=4)
-        return 0
+            lax.fori_loop(0, planes, plane, 0, unroll=math.gcd(planes, 8))
 
     lax.fori_loop(0, SUB, cell, 0)
 
 
-def flux(native, links, geo, f):
-    rows = f.shape[1]
+def flux(links, geo, f):
     return pl.pallas_call(
-        functools.partial(flux_kernel, native),
+        flux_kernel,
         in_specs=[spec(pltpu.SMEM), spec(pltpu.VMEM), spec(pltpu.VMEM)],
         out_specs=spec(pltpu.VMEM),
-        out_shape=array(SUB * rows, LANES) if native else array(SUB, rows, LANES),
+        out_shape=array(*f.shape),
         scratch_shapes=[
-            pltpu.VMEM((GEO, SUB, LANES), F32),
             pltpu.VMEM((3 * FACES + 3, SUB, LANES), F32),
+            pltpu.SMEM((FACES + 1,), jnp.int32),
+            pltpu.SMEM((FACES + 1,), jnp.int32),
         ],
         compiler_params=params(),
+        cost_estimate=traffic(f.shape[1], 7),
         name="flux",
     )(links, geo, f)
 
 
-def target_kernel(native, count, links_ref, geo_in, absorbed_in, *refs):
-    sums_refs, (f_ref, part_ref, out_ref, sum_out, geo_ref, ta, coef) = refs[:count], refs[count:]
+def target_kernel(count, links_ref, geo_ref, absorbed_in, *refs):
+    sums_refs, (f_ref, part_ref, out_ref, sum_out, ta, coef) = refs[:count], refs[count:]
     planes = f_ref.shape[1] // CHUNKS
-    place = placer(native)
-    unpack_geo(geo_in, geo_ref)
     sums = add_tiles(sums_refs)
     sum_out[...] = sums
     absorbed = sums if absorbed_in is None else absorbed_in[...]
@@ -604,14 +597,13 @@
                 jnp.broadcast_to(ta[i, a, pl.ds(g, 1), :], (SUB, LANES)) for i in range(3)
             ]
             for t in range(TILES):
-                tile = a * TILES + t
-                where = place(g, tile)
-                f = f_ref[g, at_rows(tile * SUB), :]
+                where = (g, at_rows((a * TILES + t) * SUB), slice(None))
+                f = f_ref[where]
                 target = (height_a * bell[t]) * (1.0 + (heat_a + heat[t]) * (z_a + zz[t]))
                 out_ref[where] = (part_ref[where] - rate_g * f) + target
             return 0
 
-        lax.fori_loop(0, planes, plane, 0, unroll=4)
+        lax.fori_loop(0, planes, plane, 0, unroll=math.gcd(planes, 8))
 
         for k in range(FACES):
 
@@ -632,9 +624,8 @@
                     wa = jnp.exp(-0.5 * xa * xa / wt)
                     sa = v0 * xa
                     for t in range(TILES):
-                        tile = a * TILES + t
-                        where = place(g, tile)
-                        f = f_ref[g, at_rows(tile * SUB), :]
+                        where = (g, at_rows((a * TILES + t) * SUB), slice(None))
+                        f = f_ref[where]
                         out_ref[where] = out_ref[where] + jnp.maximum(sa + base[t], 0.0) * (wa * shape[t] - f)
                     return 0
 
@@ -645,16 +636,16 @@
     lax.fori_loop(0, SUB, cell, 0)
 
 
-def add_target(native, links, geo, absorbed, tiles, f, part):
+def add_target(links, geo, absorbed, tiles, f, part):
     rows = f.shape[1]
     vmem = spec(pltpu.VMEM)
     given = [links, geo] + ([] if absorbed is None else [absorbed]) + list(tiles) + [f, part]
 
     def kernel(links_ref, geo_in, *refs):
         if absorbed is None:
-            target_kernel(native, len(tiles), links_ref, geo_in, None, *refs)
+            target_kernel(len(tiles), links_ref, geo_in, None, *refs)
         else:
-            target_kernel(native, len(tiles), links_ref, geo_in, *refs)
+            target_kernel(len(tiles), links_ref, geo_in, *refs)
 
     return pl.pallas_call(
         kernel,
@@ -663,11 +654,11 @@
         out_shape=[array(*part.shape), array(SUB, LANES)],
         input_output_aliases={len(given) - 1: 0},
         scratch_shapes=[
-            pltpu.VMEM((GEO, SUB, LANES), F32),
-            pltpu.VMEM((3, rows // CHUNKS, SUB, LANES), F32),
+                pltpu.VMEM((3, rows // CHUNKS, SUB, LANES), F32),
             pltpu.VMEM((6 + FACES, SUB, LANES), F32),
         ],
         compiler_params=params(),
+        cost_estimate=traffic(rows, 7),
         name="add_target",
     )(*given)
 
@@ -733,14 +724,15 @@
         out_shape=[array(SUB, rows, LANES), array(REACH, rows, LANES), array(REACH, rows, LANES)],
         input_output_aliases={4: 0},
         compiler_params=params(),
+        cost_estimate=traffic(rows, 4),
         name="edge",
     )(pairs, far, near, old, part)
 
 
 def last_edge_kernel(
-    geo_in, pairs_ref, far_ref, near_ref, f_ref, part_ref, out_hbm, sums_out, native_ref, sems
+    geo_ref, pairs_ref, far_ref, near_ref, f_ref, part_ref, out_hbm, sums_out, native_ref, sems
 ):
-    rows = part_ref.shape[0] // SUB
+    rows = part_ref.shape[1]
     planes = rows // CHUNKS
     part = rows // SUB // LAST_PARTS
 
@@ -756,8 +748,8 @@
                 low, high = halo_terms(pairs_ref, before_ref, after_ref, f_ref, at)
                 terms = low + [None] * (SUB - 2 * REACH) + high
                 for g in range(SUB):
+                    x = part_ref[g, at, :]
                     where = (pl.ds(j * SUB * SUB + g, SUB, stride=SUB), slice(None))
-                    x = part_ref[where]
                     native_ref[where] = x if terms[g] is None else x + terms[g]
                 return 0
 
@@ -766,7 +758,7 @@
 
     by_side(far_ref, near_ref, run)
     y = native_polynomial_sums(native_ref, planes)
-    sums_out[...] = pack_sums(finish_polynomials(y, column(geo_in[...], FIRST), planes), 0)
+    sums_out[...] = pack_sums(finish_polynomials(y, geo_ref[FIRST], planes), 0)
     for i in range(LAST_PARTS):
         copy(i).wait()
 
@@ -775,13 +767,15 @@
 
 
 def last_edge(geo, pairs, far, near, f, part):
+    native = (SUB * part.shape[1], LANES)
     return pl.pallas_call(
         last_edge_kernel,
         in_specs=[spec(pltpu.VMEM)] * 6,
         out_specs=[spec(pltpu.HBM), spec(pltpu.VMEM)],
-        out_shape=[array(*part.shape), array(SUB, LANES)],
-        scratch_shapes=[pltpu.VMEM(part.shape, F32), pltpu.SemaphoreType.DMA((LAST_PARTS,))],
+        out_shape=[array(*native), array(SUB, LANES)],
+        scratch_shapes=[pltpu.VMEM(native, F32), pltpu.SemaphoreType.DMA((LAST_PARTS,))],
         compiler_params=params(),
+        cost_estimate=traffic(part.shape[1], 4),
         name="last_edge",
     )(geo, pairs, far, near, f, part)
 
@@ -814,19 +808,19 @@
             jnp.full((1, cells), first, F32),
         ]
     )
-    geo = jnp.pad(geo.T, ((0, 0), (0, LANES - GEO)))
+    geo = jnp.broadcast_to(geo[:, :, None], (GEO, cells, LANES))
     native, far, near = first_rows(native)
     far, near = exchange(far, near)
     f, sums = first_sums(links, geo, native)
     tiles = gather_sums(sums)
     pairs = geometry(links, geo, rows)
-    part = flux(False, links, geo, f)
-    part, absorbed = add_target(False, links, geo, None, tiles, f, part)
+    part = flux(links, geo, f)
+    part, absorbed = add_target(links, geo, None, tiles, f, part)
     f, far, near = edge(pairs, far, near, f, part)
     far, near = exchange(far, near)
     tiles = gather_sums(local_sums(links, geo, f))
-    part = flux(True, links, geo, f)
-    part, _ = add_target(True, links, geo, absorbed, tiles, f, part)
+    part = flux(links, geo, f)
+    part, _ = add_target(links, geo, absorbed, tiles, f, part)
     native, sums = last_edge(geo, pairs, far, near, f, part)
     macro_quantities = macro(gather_sums(sums))
     evolved = native.reshape(rows, cells, LANES).transpose(1, 0, 2).reshape(cells, points)

time: 63.4 us -> 61.6 us (0.972); the launches traced: 62.2 us -> 61.1 us
  Pallas kernels: 32.1 us -> 30.2 us
  waiting for transfers between devices: 6.96 us -> 7.64 us
    pallas_call x2, Pallas kernels: 8.06 us -> 6.15 us  [flux(): pl.pallas_call(flux_kernel, in_specs=[spec(pltpu.SMEM), spec(pltpu.VMEM),...]
    unnamed x17 -> x16, local copies, waits for them, and re-layouts: 1.27 us -> 1.19 us
  transfers between devices with their start and end apart: 13 -> 13, of which waited for: 4 -> 5; matrix products, arithmetic and copies ran while one was open for 1% -> 1% of each run, Pallas kernels for 38% -> 36%
where the time goes in v7:
time: 61.6 us; the launch traced here: 61.1 us
  Pallas kernels  30.2 us (49%)
  starting transfers between devices  20.6 us (33%)
  waiting for transfers between devices  7.64 us (12%)
  local copies, waits for them, and re-layouts  1.86 us (3%)
  between operations  0.82 us (1%)
    ppermute x9, starting transfers between devices, gather_sums(): lax.ppermute(tile, 'vel', [(i, i ^ s) for i in range(size)])  13.3 us
    pallas_call x2, Pallas kernels, add_target(): pl.pallas_call(kernel, in_specs=[spec(pltpu.SMEM)] + [vmem] * (len(given)...  8.33 us
    ppermute x4, starting transfers between devices, exchange(): out.append(lax.ppermute(x, 'space', pairs + [(j, i) for i, j in pairs]))  7.3 us
    pallas_call x2, Pallas kernels, flux(): pl.pallas_call(flux_kernel, in_specs=[spec(pltpu.SMEM), spec(pltpu.VMEM),...  6.15 us
    ppermute x9, waiting for transfers between devices, gather_sums(): lax.ppermute(tile, 'vel', [(i, i ^ s) for i in range(size)])  4.36 us
    ppermute x4, waiting for transfers between devices, exchange(): out.append(lax.ppermute(x, 'space', pairs + [(j, i) for i, j in pairs]))  3.28 us
    pallas_call x1, Pallas kernels, first_sums(): pl.pallas_call(first_sums_kernel, in_specs=[spec(pltpu.SMEM), spec(pltpu....  3.01 us
    pallas_call x1, Pallas kernels, first_rows(): pl.pallas_call(first_rows_kernel, in_specs=[spec(pltpu.HBM)], out_specs=[...  2.8 us
  transfers between devices with their start and end apart: 13, of which 5 were waited for; matrix products, arithmetic and copies ran while one was open for 1% of the time, Pallas kernels for 36%

profile of v7, /device:TPU:4, one launch (start us, length us, event | category | flops | bytes accessed | tf_op | source)
XLA Modules:
  0.0 61.1 jit_solution(17143518170838552184)
XLA Ops:
  0.6 0.0 copy-start.6
  0.7 2.8 %first_rows.1 = (f32[4096,128]{1,0:T(8,128)S(1)}, f32[3,512,128]{2,1,0:T(8,128)}, f32[3,512,128]{2,1,0:T(8,128)}) custom-call(f32[4096,128]{1,0:T(8,128)} %bitcast.12), custom_call_target="tpu_custom_call" | custom-call | flops 16777216 | bytes 8388608 | tf_op jit(solution)/shard_map/first_rows/pallas_call | solution.py:359
  3.5 2.8 %collective-permute-start = (f32[3,512,128]{2,1,0:T(8,128)}, f32[3,512,128]{2,1,0:T(8,128)S(1)}, u32[]{:S(2)}, u32[]{:S(2)}) collective-permute-start(f32[3,512,128]{2,1,0:T(8,128)} %get-tuple-element.15), channel_id=1, source_target_pairs={{4,8},{12,16},{20,24},{8,4},{16,12},{24,20},{5,9},{13,17},{21,25},... | collective-permute-start | bytes 2359304 | tf_op jit(solution)/shard_map/ppermute | solution.py:788
  6.3 0.8 %collective-permute-start.1 = (f32[3,512,128]{2,1,0:T(8,128)}, f32[3,512,128]{2,1,0:T(8,128)}, u32[]{:S(2)}, u32[]{:S(2)}) collective-permute-start(f32[3,512,128]{2,1,0:T(8,128)} %get-tuple-element.16), channel_id=1, source_target_pairs={{0,4},{8,12},{16,20},{24,28},{4,0},{12,8},{20,16},{28,24},{1,5},{9... | collective-permute-start | bytes 2359304 | tf_op jit(solution)/shard_map/ppermute | solution.py:788
  7.1 0.1 copy.11
  7.1 0.1 copy.12
  7.2 0.1 copy.14
  7.3 0.1 copy.13
  7.4 0.1 copy.16
  7.5 0.1 concatenate.3
  7.6 0.1 copy.15
  7.7 0.1 broadcast_in_dim.23.geo_ref.geo_in
  7.8 3.0 %first_sums.1 = (f32[8,512,128]{2,1,0:T(8,128)S(1)}, f32[8,128]{1,0:T(8,128)S(1)}) custom-call(s32[6,8]{1,0:T(8,128)S(1)} %get-tuple-element.29.links_ref, f32[33,8,128]{2,1,0:T(8,128)S(1)} %broadcast_in_dim.23.geo_ref.geo_in, f32[4096,128]{1,0:T(8,128)S(1)} %get-tuple-element.17.native_ref), custom_call_target="tpu_custom_call" | custom-call | flops 20971520 | bytes 10485760 | tf_op jit(solution)/shard_map/first_sums/pallas_call | solution.py:307
  10.8 3.7 %collective-permute-start.4 = (f32[8,128]{1,0:T(8,128)S(1)}, f32[8,128]{1,0:T(8,128)S(1)}, u32[]{:S(2)}, u32[]{:S(2)}) collective-permute-start(f32[8,128]{1,0:T(8,128)S(1)} %get-tuple-element.19.refs_0_), channel_id=1, source_target_pairs={{0,3},{1,2},{2,1},{3,0},{4,7},{5,6},{6,5},{7,4},{8,11},{9,10},{10,... | collective-permute-start | bytes 12296 | tf_op jit(solution)/shard_map/ppermute | solution.py:431
  14.4 0.0 collective-permute-start.3
  14.4 0.8 %collective-permute-start.2 = (f32[8,128]{1,0:T(8,128)S(1)}, f32[8,128]{1,0:T(8,128)S(1)}, u32[]{:S(2)}, u32[]{:S(2)}) collective-permute-start(f32[8,128]{1,0:T(8,128)S(1)} %get-tuple-element.19.refs_0_), channel_id=1, source_target_pairs={{0,1},{1,0},{2,3},{3,2},{4,5},{5,4},{6,7},{7,6},{8,9},{9,8},{10,11... | collective-permute-start | bytes 12296 | tf_op jit(solution)/shard_map/ppermute | solution.py:431
  15.2 2.4 %geometry.1.pairs_ref = f32[12,512,128]{2,1,0:T(8,128)S(1)} custom-call(s32[6,8]{1,0:T(8,128)S(1)} %get-tuple-element.29.links_ref, f32[33,8,128]{2,1,0:T(8,128)S(1)} %broadcast_in_dim.23.geo_ref.geo_in), custom_call_target="tpu_custom_call" | custom-call | flops 16777216 | bytes 8388608 | tf_op jit(solution)/shard_map/geometry/pallas_call | solution.py:416
  17.6 3.1 %flux.2.refs_5_ = f32[8,512,128]{2,1,0:T(8,128)S(1)} custom-call(s32[6,8]{1,0:T(8,128)S(1)} %get-tuple-element.29.links_ref, f32[33,8,128]{2,1,0:T(8,128)S(1)} %broadcast_in_dim.23.geo_ref.geo_in, f32[8,512,128]{2,1,0:T(8,128)S(1)} %get-tuple-element.18.f_ref.refs_4_.old_ref), custom_call_target="tpu_custom_call" | custom-call | flops 29360128 | bytes 14680064 | tf_op jit(solution)/shard_map/flux/pallas_call | solution.py:535
  20.7 0.0 collective-permute-done.4.refs_3_
  20.7 0.0 collective-permute-done.3.refs_2_
  20.7 0.0 collective-permute-done.2.refs_1_
  20.7 3.9 %add_target.2 = (f32[8,512,128]{2,1,0:T(8,128)S(1)}, f32[8,128]{1,0:T(8,128)S(1)}) custom-call(s32[6,8]{1,0:T(8,128)S(1)} %get-tuple-element.29.links_ref, f32[33,8,128]{2,1,0:T(8,128)S(1)} %broadcast_in_dim.23.geo_ref.geo_in, f32[8,128]{1,0:T(8,128)S(1)} %get-tuple-element.19.refs_0_, ...), custom_call_target="tpu_custom_call", output_to_operand_aliasing={{0}: (7, {})} | custom-call | flops 29360128 | bytes 14680064 | tf_op jit(solution)/shard_map/add_target/pallas_call | solution.py:650
  24.6 0.8 %collective-permute-done.far_in = f32[3,512,128]{2,1,0:T(8,128)S(1)} collective-permute-done((f32[3,512,128]{2,1,0:T(8,128)}, f32[3,512,128]{2,1,0:T(8,128)S(1)}, u32[]{:S(2)}, u32[]{:S(2)}) %collective-permute-start) | collective-permute-done | bytes 786464 | tf_op jit(solution)/shard_map/ppermute | solution.py:788
  25.4 0.0 collective-permute-done.1.near_in
  25.4 2.3 %edge.1 = (f32[8,512,128]{2,1,0:T(8,128)S(1)}, f32[3,512,128]{2,1,0:T(8,128)S(1)}, f32[3,512,128]{2,1,0:T(8,128)S(1)}) custom-call(f32[12,512,128]{2,1,0:T(8,128)S(1)} %geometry.1.pairs_ref, f32[3,512,128]{2,1,0:T(8,128)S(1)} %collective-permute-done.far_in, f32[3,512,128]{2,1,0:T(8,128)} %collective-permute-done.1.near_in, ...), custom_call_target="tpu_custom_call", output_to_operand_aliasing={{0}: (4, {})} | custom-call | flops 16777216 | bytes 8388608 | tf_op jit(solution)/shard_map/edge/pallas_call | solution.py:720
  27.7 3.6 %collective-permute-start.5 = (f32[3,512,128]{2,1,0:T(8,128)S(1)}, f32[3,512,128]{2,1,0:T(8,128)S(1)}, u32[]{:S(2)}, u32[]{:S(2)}) collective-permute-start(f32[3,512,128]{2,1,0:T(8,128)S(1)} %get-tuple-element.21), channel_id=1, source_target_pairs={{4,8},{12,16},{20,24},{8,4},{16,12},{24,20},{5,9},{13,17},{21,25},... | collective-permute-start | bytes 2359304 | tf_op jit(solution)/shard_map/ppermute | solution.py:788
  31.4 0.1 collective-permute-start.6
  31.5 2.2 %local_sums.1.refs_1_ = f32[8,128]{1,0:T(8,128)S(1)} custom-call(s32[6,8]{1,0:T(8,128)S(1)} %get-tuple-element.29.links_ref, f32[33,8,128]{2,1,0:T(8,128)S(1)} %broadcast_in_dim.23.geo_ref.geo_in, f32[8,512,128]{2,1,0:T(8,128)S(1)} %get-tuple-element.23.f_ref.refs_5_), custom_call_target="tpu_custom_call" | custom-call | flops 16777216 | bytes 8388608 | tf_op jit(solution)/shard_map/local_sums/pallas_call | solution.py:290
  33.6 3.6 %collective-permute-start.9 = (f32[8,128]{1,0:T(8,128)S(1)}, f32[8,128]{1,0:T(8,128)S(1)}, u32[]{:S(2)}, u32[]{:S(2)}) collective-permute-start(f32[8,128]{1,0:T(8,128)S(1)} %local_sums.1.refs_1_), channel_id=1, source_target_pairs={{0,3},{1,2},{2,1},{3,0},{4,7},{5,6},{6,5},{7,4},{8,11},{9,10},{10,... | collective-permute-start | bytes 12296 | tf_op jit(solution)/shard_map/ppermute | solution.py:431
  37.3 0.0 collective-permute-start.8
  37.3 0.8 %collective-permute-start.7 = (f32[8,128]{1,0:T(8,128)S(1)}, f32[8,128]{1,0:T(8,128)S(1)}, u32[]{:S(2)}, u32[]{:S(2)}) collective-permute-start(f32[8,128]{1,0:T(8,128)S(1)} %local_sums.1.refs_1_), channel_id=1, source_target_pairs={{0,1},{1,0},{2,3},{3,2},{4,5},{5,4},{6,7},{7,6},{8,9},{9,8},{10,11... | collective-permute-start | bytes 12296 | tf_op jit(solution)/shard_map/ppermute | solution.py:431
  38.0 3.1 %flux.3.refs_6_ = f32[8,512,128]{2,1,0:T(8,128)S(1)} custom-call(s32[6,8]{1,0:T(8,128)S(1)} %get-tuple-element.29.links_ref, f32[33,8,128]{2,1,0:T(8,128)S(1)} %broadcast_in_dim.23.geo_ref.geo_in, f32[8,512,128]{2,1,0:T(8,128)S(1)} %get-tuple-element.23.f_ref.refs_5_), custom_call_target="tpu_custom_call" | custom-call | flops 29360128 | bytes 14680064 | tf_op jit(solution)/shard_map/flux/pallas_call | solution.py:535
  41.1 0.0 collective-permute-done.9.refs_4_
  41.1 0.6 %collective-permute-done.8.refs_3_ = f32[8,128]{1,0:T(8,128)S(1)} collective-permute-done((f32[8,128]{1,0:T(8,128)S(1)}, f32[8,128]{1,0:T(8,128)S(1)}, u32[]{:S(2)}, u32[]{:S(2)}) %collective-permute-start.8) | collective-permute-done | bytes 4128 | tf_op jit(solution)/shard_map/ppermute | solution.py:431
  41.8 0.0 collective-permute-done.7.refs_2_
  41.8 4.5 %add_target.3 = (f32[8,512,128]{2,1,0:T(8,128)S(1)}, f32[8,128]{1,0:T(8,128)}) custom-call(s32[6,8]{1,0:T(8,128)S(1)} %get-tuple-element.29.links_ref, f32[33,8,128]{2,1,0:T(8,128)S(1)} %broadcast_in_dim.23.geo_ref.geo_in, f32[8,128]{1,0:T(8,128)S(1)} %get-tuple-element.24.refs_0_, f32[8,128]{1,0:T(8,128)S(1)} %local_sums.1.refs_1_, ...), custom_call_target="tpu_custom_call", output_to_operand_aliasing={{0}: (8, {})} | custom-call | flops 29360128 | bytes 14680064 | tf_op jit(solution)/shard_map/add_target/pallas_call | solution.py:650
  46.2 2.4 %collective-permute-done.5.far_ref = f32[3,512,128]{2,1,0:T(8,128)S(1)} collective-permute-done((f32[3,512,128]{2,1,0:T(8,128)S(1)}, f32[3,512,128]{2,1,0:T(8,128)S(1)}, u32[]{:S(2)}, u32[]{:S(2)}) %collective-permute-start.5) | collective-permute-done | bytes 786464 | tf_op jit(solution)/shard_map/ppermute | solution.py:788
  48.7 0.0 collective-permute-done.6.near_ref
  48.7 1.6 %last_edge.1 = (f32[4096,128]{1,0:T(8,128)}, f32[8,128]{1,0:T(8,128)S(1)}) custom-call(f32[33,8,128]{2,1,0:T(8,128)S(1)} %broadcast_in_dim.23.geo_ref.geo_in, f32[12,512,128]{2,1,0:T(8,128)S(1)} %geometry.1.pairs_ref, f32[3,512,128]{2,1,0:T(8,128)S(1)} %collective-permute-done.5.far_ref, f32[3,512,128]{2,1,0:T(8,128)S(1)} %collective-permute-done.6.near_ref, ...), custom_call_target="tpu_custom_call" | custom-call | flops 16777216 | bytes 8388608 | tf_op jit(solution)/shard_map/last_edge/pallas_call | solution.py:771
  50.3 3.7 %collective-permute-start.12 = (f32[8,128]{1,0:T(8,128)S(1)}, f32[8,128]{1,0:T(8,128)S(1)}, u32[]{:S(2)}, u32[]{:S(2)}) collective-permute-start(f32[8,128]{1,0:T(8,128)S(1)} %get-tuple-element.27.refs_0_), channel_id=1, source_target_pairs={{0,3},{1,2},{2,1},{3,0},{4,7},{5,6},{6,5},{7,4},{8,11},{9,10},{10,... | collective-permute-start | bytes 12296 | tf_op jit(solution)/shard_map/ppermute | solution.py:431
  54.0 0.0 collective-permute-start.11
  54.0 0.8 %collective-permute-start.10 = (f32[8,128]{1,0:T(8,128)S(1)}, f32[8,128]{1,0:T(8,128)S(1)}, u32[]{:S(2)}, u32[]{:S(2)}) collective-permute-start(f32[8,128]{1,0:T(8,128)S(1)} %get-tuple-element.27.refs_0_), channel_id=1, source_target_pairs={{0,1},{1,0},{2,3},{3,2},{4,5},{5,4},{6,7},{7,6},{8,9},{9,8},{10,11... | collective-permute-start | bytes 12296 | tf_op jit(solution)/shard_map/ppermute | solution.py:431
  54.8 1.0 %collective-permute-done.12.refs_3_ = f32[8,128]{1,0:T(8,128)S(1)} collective-permute-done((f32[8,128]{1,0:T(8,128)S(1)}, f32[8,128]{1,0:T(8,128)S(1)}, u32[]{:S(2)}, u32[]{:S(2)}) %collective-permute-start.12) | collective-permute-done | bytes 4128 | tf_op jit(solution)/shard_map/ppermute | solution.py:431
  55.8 2.7 %collective-permute-done.11.refs_2_ = f32[8,128]{1,0:T(8,128)S(1)} collective-permute-done((f32[8,128]{1,0:T(8,128)S(1)}, f32[8,128]{1,0:T(8,128)S(1)}, u32[]{:S(2)}, u32[]{:S(2)}) %collective-permute-start.11) | collective-permute-done | bytes 4128 | tf_op jit(solution)/shard_map/ppermute | solution.py:431
  58.5 0.0 collective-permute-done.10.refs_1_
  58.5 0.6 copy-done.3
  59.1 0.6 copy-done.4
  59.7 1.4 %macro.1 = f32[8,8]{1,0:T(8,128)} custom-call(f32[8,128]{1,0:T(8,128)} %copy-done, f32[8,128]{1,0:T(8,128)} %copy-done.4, f32[8,128]{1,0:T(8,128)} %copy-done.3, f32[8,128]{1,0:T(8,128)} %copy-done.2), custom_call_target="tpu_custom_call" | custom-call | tf_op jit(solution)/shard_map/macro/pallas_call | solution.py:469
  (16 shorter events, 0.0 us)
Async XLA Ops:
  0.6 6.4 %copy-start.6 = (f32[8]{0:T(128)S(1)}, f32[8]{0:T(128)}, u32[]{:S(2)}) copy-start(f32[8]{0:T(128)} %param.8) | copy-start | bytes 100
  0.6 6.5 %copy-start.7 = (f32[8]{0:T(128)S(1)}, f32[8]{0:T(128)}, u32[]{:S(2)}) copy-start(f32[8]{0:T(128)} %param.9) | copy-start | bytes 100
  0.7 6.6 %copy-start.5 = (s32[6,8]{1,0:T(8,128)S(1)}, s32[6,8]{1,0:T(8,128)}, u32[]{:S(2)}) copy-start(s32[6,8]{1,0:T(8,128)} %param.6) | copy-start | bytes 580
  0.7 6.7 %copy-start.1 = (f32[3,6,8]{2,1,0:T(8,128)S(1)}, f32[3,6,8]{2,1,0:T(8,128)}, u32[]{:S(2)}) copy-start(f32[3,6,8]{2,1,0:T(8,128)} %param.7) | copy-start | bytes 1732
  3.5 21.9 %collective-permute-start = (f32[3,512,128]{2,1,0:T(8,128)}, f32[3,512,128]{2,1,0:T(8,128)S(1)}, u32[]{:S(2)}, u32[]{:S(2)}) collective-permute-start(f32[3,512,128]{2,1,0:T(8,128)} %get-tuple-element.15), channel_id=1, source_target_pairs={{4,8},{12,16},{20,24},{8,4},{16,12},{24,20},{5,9},{13,17},{21,25},... | collective-permute-start | bytes 2359304 | tf_op jit(solution)/shard_map/ppermute | solution.py:788
  6.3 19.2 %collective-permute-start.1 = (f32[3,512,128]{2,1,0:T(8,128)}, f32[3,512,128]{2,1,0:T(8,128)}, u32[]{:S(2)}, u32[]{:S(2)}) collective-permute-start(f32[3,512,128]{2,1,0:T(8,128)} %get-tuple-element.16), channel_id=1, source_target_pairs={{0,4},{8,12},{16,20},{24,28},{4,0},{12,8},{20,16},{28,24},{1,5},{9... | collective-permute-start | bytes 2359304 | tf_op jit(solution)/shard_map/ppermute | solution.py:788
  10.8 9.9 %collective-permute-start.4 = (f32[8,128]{1,0:T(8,128)S(1)}, f32[8,128]{1,0:T(8,128)S(1)}, u32[]{:S(2)}, u32[]{:S(2)}) collective-permute-start(f32[8,128]{1,0:T(8,128)S(1)} %get-tuple-element.19.refs_0_), channel_id=1, source_target_pairs={{0,3},{1,2},{2,1},{3,0},{4,7},{5,6},{6,5},{7,4},{8,11},{9,10},{10,... | collective-permute-start | bytes 12296 | tf_op jit(solution)/shard_map/ppermute | solution.py:431
  14.4 6.3 %collective-permute-start.3 = (f32[8,128]{1,0:T(8,128)S(1)}, f32[8,128]{1,0:T(8,128)S(1)}, u32[]{:S(2)}, u32[]{:S(2)}) collective-permute-start(f32[8,128]{1,0:T(8,128)S(1)} %get-tuple-element.19.refs_0_), channel_id=1, source_target_pairs={{0,2},{1,3},{2,0},{3,1},{4,6},{5,7},{6,4},{7,5},{8,10},{9,11},{10,... | collective-permute-start | bytes 12296 | tf_op jit(solution)/shard_map/ppermute | solution.py:431
  14.4 6.3 %collective-permute-start.2 = (f32[8,128]{1,0:T(8,128)S(1)}, f32[8,128]{1,0:T(8,128)S(1)}, u32[]{:S(2)}, u32[]{:S(2)}) collective-permute-start(f32[8,128]{1,0:T(8,128)S(1)} %get-tuple-element.19.refs_0_), channel_id=1, source_target_pairs={{0,1},{1,0},{2,3},{3,2},{4,5},{5,4},{6,7},{7,6},{8,9},{9,8},{10,11... | collective-permute-start | bytes 12296 | tf_op jit(solution)/shard_map/ppermute | solution.py:431
  27.7 20.9 %collective-permute-start.5 = (f32[3,512,128]{2,1,0:T(8,128)S(1)}, f32[3,512,128]{2,1,0:T(8,128)S(1)}, u32[]{:S(2)}, u32[]{:S(2)}) collective-permute-start(f32[3,512,128]{2,1,0:T(8,128)S(1)} %get-tuple-element.21), channel_id=1, source_target_pairs={{4,8},{12,16},{20,24},{8,4},{16,12},{24,20},{5,9},{13,17},{21,25},... | collective-permute-start | bytes 2359304 | tf_op jit(solution)/shard_map/ppermute | solution.py:788
  31.4 17.3 %collective-permute-start.6 = (f32[3,512,128]{2,1,0:T(8,128)S(1)}, f32[3,512,128]{2,1,0:T(8,128)S(1)}, u32[]{:S(2)}, u32[]{:S(2)}) collective-permute-start(f32[3,512,128]{2,1,0:T(8,128)S(1)} %get-tuple-element.22), channel_id=1, source_target_pairs={{0,4},{8,12},{16,20},{24,28},{4,0},{12,8},{20,16},{28,24},{1,5},{9... | collective-permute-start | bytes 2359304 | tf_op jit(solution)/shard_map/ppermute | solution.py:788
  33.6 7.5 %collective-permute-start.9 = (f32[8,128]{1,0:T(8,128)S(1)}, f32[8,128]{1,0:T(8,128)S(1)}, u32[]{:S(2)}, u32[]{:S(2)}) collective-permute-start(f32[8,128]{1,0:T(8,128)S(1)} %local_sums.1.refs_1_), channel_id=1, source_target_pairs={{0,3},{1,2},{2,1},{3,0},{4,7},{5,6},{6,5},{7,4},{8,11},{9,10},{10,... | collective-permute-start | bytes 12296 | tf_op jit(solution)/shard_map/ppermute | solution.py:431
  37.3 4.5 %collective-permute-start.8 = (f32[8,128]{1,0:T(8,128)S(1)}, f32[8,128]{1,0:T(8,128)S(1)}, u32[]{:S(2)}, u32[]{:S(2)}) collective-permute-start(f32[8,128]{1,0:T(8,128)S(1)} %local_sums.1.refs_1_), channel_id=1, source_target_pairs={{0,2},{1,3},{2,0},{3,1},{4,6},{5,7},{6,4},{7,5},{8,10},{9,11},{10,... | collective-permute-start | bytes 12296 | tf_op jit(solution)/shard_map/ppermute | solution.py:431
  37.3 4.5 %collective-permute-start.7 = (f32[8,128]{1,0:T(8,128)S(1)}, f32[8,128]{1,0:T(8,128)S(1)}, u32[]{:S(2)}, u32[]{:S(2)}) collective-permute-start(f32[8,128]{1,0:T(8,128)S(1)} %local_sums.1.refs_1_), channel_id=1, source_target_pairs={{0,1},{1,0},{2,3},{3,2},{4,5},{5,4},{6,7},{7,6},{8,9},{9,8},{10,11... | collective-permute-start | bytes 12296 | tf_op jit(solution)/shard_map/ppermute | solution.py:431
  50.3 8.2 %copy-start = (f32[8,128]{1,0:T(8,128)}, f32[8,128]{1,0:T(8,128)S(1)}, u32[]{:S(2)}) copy-start(f32[8,128]{1,0:T(8,128)S(1)} %get-tuple-element.27.refs_0_) | copy-start | bytes 12292
  50.3 5.5 %collective-permute-start.12 = (f32[8,128]{1,0:T(8,128)S(1)}, f32[8,128]{1,0:T(8,128)S(1)}, u32[]{:S(2)}, u32[]{:S(2)}) collective-permute-start(f32[8,128]{1,0:T(8,128)S(1)} %get-tuple-element.27.refs_0_), channel_id=1, source_target_pairs={{0,3},{1,2},{2,1},{3,0},{4,7},{5,6},{6,5},{7,4},{8,11},{9,10},{10,... | collective-permute-start | bytes 12296 | tf_op jit(solution)/shard_map/ppermute | solution.py:431
  54.0 4.5 %collective-permute-start.11 = (f32[8,128]{1,0:T(8,128)S(1)}, f32[8,128]{1,0:T(8,128)S(1)}, u32[]{:S(2)}, u32[]{:S(2)}) collective-permute-start(f32[8,128]{1,0:T(8,128)S(1)} %get-tuple-element.27.refs_0_), channel_id=1, source_target_pairs={{0,2},{1,3},{2,0},{3,1},{4,6},{5,7},{6,4},{7,5},{8,10},{9,11},{10,... | collective-permute-start | bytes 12296 | tf_op jit(solution)/shard_map/ppermute | solution.py:431
  54.0 4.5 %collective-permute-start.10 = (f32[8,128]{1,0:T(8,128)S(1)}, f32[8,128]{1,0:T(8,128)S(1)}, u32[]{:S(2)}, u32[]{:S(2)}) collective-permute-start(f32[8,128]{1,0:T(8,128)S(1)} %get-tuple-element.27.refs_0_), channel_id=1, source_target_pairs={{0,1},{1,0},{2,3},{3,2},{4,5},{5,4},{6,7},{7,6},{8,9},{9,8},{10,11... | collective-permute-start | bytes 12296 | tf_op jit(solution)/shard_map/ppermute | solution.py:431
  55.8 2.7 %copy-start.2 = (f32[8,128]{1,0:T(8,128)}, f32[8,128]{1,0:T(8,128)S(1)}, u32[]{:S(2)}) copy-start(f32[8,128]{1,0:T(8,128)S(1)} %collective-permute-done.12.refs_3_) | copy-start | bytes 12292
  58.5 0.6 copy-start.3
  59.1 0.6 copy-start.4

commit v8 on v7

--- a/solution.py
+++ b/solution.py
@@ -33,7 +33,6 @@
 SUMS = 25
 
 F32 = jnp.float32
-VMEM_LIMIT = 16 * 1024 * 1024
 
 
 def lane_iota():
@@ -277,8 +276,8 @@
     return jax.ShapeDtypeStruct(shape, F32)
 
 
-def params():
-    return pltpu.CompilerParams(vmem_limit_bytes=VMEM_LIMIT)
+def params(mib=16):
+    return pltpu.CompilerParams(vmem_limit_bytes=mib * 1024 * 1024)
 
 
 def traffic(rows, profiles):
@@ -360,7 +359,7 @@
         first_rows_kernel,
         in_specs=[spec(pltpu.HBM)],
         out_specs=[spec(pltpu.VMEM)] * 3,
-        out_shape=[array(*native.shape), array(REACH, rows, LANES), array(REACH, rows, LANES)],
+        out_shape=[pltpu.VMEM(native.shape, F32)] + [pltpu.VMEM((REACH, rows, LANES), F32)] * 2,
         scratch_shapes=[pltpu.SemaphoreType.DMA((SPLIT_PARTS,))],
         compiler_params=params(),
         cost_estimate=traffic(rows, 4),
@@ -430,6 +429,14 @@
         return [lax.psum(tile, "vel")]
     others = [lax.ppermute(tile, "vel", [(i, i ^ s) for i in range(size)]) for s in range(1, size)]
     return [tile, *others]
+
+
+def doubling_sums(tile):
+    size = lax.axis_size("vel")
+    if size != 4:
+        return gather_sums(tile)
+    pair = tile + lax.ppermute(tile, "vel", [(i, i ^ 1) for i in range(size)])
+    return [pair, lax.ppermute(pair, "vel", [(i, i ^ 2) for i in range(size)])]
 
 
 def add_tiles(refs):
@@ -471,6 +478,7 @@
         in_specs=[spec(pltpu.VMEM)] * len(tiles),
         out_specs=spec(pltpu.VMEM),
         out_shape=array(8, SUB),
+        compiler_params=params(1),
         name="macro",
     )(*tiles)
 
@@ -822,7 +830,7 @@
     part = flux(links, geo, f)
     part, _ = add_target(links, geo, absorbed, tiles, f, part)
     native, sums = last_edge(geo, pairs, far, near, f, part)
-    macro_quantities = macro(gather_sums(sums))
+    macro_quantities = macro(doubling_sums(sums))
     evolved = native.reshape(rows, cells, LANES).transpose(1, 0, 2).reshape(cells, points)
     return evolved, macro_quantities
 

time: 61.6 us -> 59.4 us (0.964)
  local copies, waits for them, and re-layouts: 1.86 us -> 0.69 us
  Pallas kernels: 30.2 us -> 29.5 us
    ppermute x9 -> x6, starting transfers between devices: 13.3 us -> 8.84 us  [gather_sums(): lax.ppermute(tile, 'vel', [(i, i ^ s) for i in range(size)])]
    ppermute x0 -> x2, starting transfers between devices: none -> 4.23 us  [the longest x1 2.59 us: doubling_sums(): return [pair, lax.ppermute(pair, 'vel', [(i, i ^ 2) for i in range(size)])]]
    ppermute x0 -> x2, waiting for transfers between devices: none -> 3.95 us  [the longest x1 2.03 us: doubling_sums(): pair = tile + lax.ppermute(tile, 'vel', [(i, i ^ 1) for i in range(size)])]
    ppermute x9 -> x6, waiting for transfers between devices: 4.36 us -> 0.65 us  [gather_sums(): lax.ppermute(tile, 'vel', [(i, i ^ s) for i in range(size)])]
    unnamed x16 -> x8, local copies, waits for them, and re-layouts: 1.19 us -> 0.02 us
    pallas_call x1, Pallas kernels: 1.39 us -> 0.69 us  [macro(): pl.pallas_call(macro_kernel, in_specs=[spec(pltpu.VMEM)] * len(tiles), ou...]
  transfers between devices with their start and end apart: 13 -> 12, of which waited for: 5 -> 5; matrix products, arithmetic and copies ran while one was open for 1% -> 1% of each run, Pallas kernels for 36% -> 37%
where the time goes in v8:
time: 59.4 us; the launch traced here: 59.1 us
  Pallas kernels  29.5 us (50%)
  starting transfers between devices  20.4 us (34%)
  waiting for transfers between devices  7.79 us (13%)
  between operations  0.79 us (1%)
  local copies, waits for them, and re-layouts  0.69 us (1%)
    ppermute x6, starting transfers between devices, gather_sums(): lax.ppermute(tile, 'vel', [(i, i ^ s) for i in range(size)])  8.84 us
    pallas_call x2, Pallas kernels, add_target(): pl.pallas_call(kernel, in_specs=[spec(pltpu.SMEM)] + [vmem] * (len(given)...  8.33 us
    ppermute x4, starting transfers between devices, exchange(): out.append(lax.ppermute(x, 'space', pairs + [(j, i) for i, j in pairs]))  7.3 us
    pallas_call x2, Pallas kernels, flux(): pl.pallas_call(flux_kernel, in_specs=[spec(pltpu.SMEM), spec(pltpu.VMEM),...  6.13 us
    ppermute x4, waiting for transfers between devices, exchange(): out.append(lax.ppermute(x, 'space', pairs + [(j, i) for i, j in pairs]))  3.2 us
    pallas_call x1, Pallas kernels, first_sums(): pl.pallas_call(first_sums_kernel, in_specs=[spec(pltpu.SMEM), spec(pltpu....  3.01 us
    pallas_call x1, Pallas kernels, first_rows(): pl.pallas_call(first_rows_kernel, in_specs=[spec(pltpu.HBM)], out_specs=[...  2.8 us
    ppermute x1, starting transfers between devices, doubling_sums(): return [pair, lax.ppermute(pair, 'vel', [(i, i ^ 2) for i in range(size)])]  2.59 us
  transfers between devices with their start and end apart: 12, of which 5 were waited for; matrix products, arithmetic and copies ran while one was open for 1% of the time, Pallas kernels for 37%

profile of v8, /device:TPU:4, one launch (start us, length us, event | category | flops | bytes accessed | tf_op | source)
XLA Modules:
  0.0 59.1 jit_solution(2138274756075590717)
XLA Ops:
  0.6 0.0 copy-start.2
  0.6 0.0 copy-start.3
  0.7 0.0 copy-start.1
  0.7 0.0 copy-start
  0.7 2.8 %first_rows.1 = (f32[4096,128]{1,0:T(8,128)S(1)}, f32[3,512,128]{2,1,0:T(8,128)}, f32[3,512,128]{2,1,0:T(8,128)}) custom-call(f32[4096,128]{1,0:T(8,128)} %bitcast.12), custom_call_target="tpu_custom_call" | custom-call | flops 16777216 | bytes 8388608 | tf_op jit(solution)/shard_map/first_rows/pallas_call | solution.py:358
  3.5 2.8 %collective-permute-start = (f32[3,512,128]{2,1,0:T(8,128)}, f32[3,512,128]{2,1,0:T(8,128)S(1)}, u32[]{:S(2)}, u32[]{:S(2)}) collective-permute-start(f32[3,512,128]{2,1,0:T(8,128)} %get-tuple-element.15), channel_id=1, source_target_pairs={{4,8},{12,16},{20,24},{8,4},{16,12},{24,20},{5,9},{13,17},{21,25},... | collective-permute-start | bytes 2359304 | tf_op jit(solution)/shard_map/ppermute | solution.py:796
  6.3 0.8 %collective-permute-start.1 = (f32[3,512,128]{2,1,0:T(8,128)}, f32[3,512,128]{2,1,0:T(8,128)}, u32[]{:S(2)}, u32[]{:S(2)}) collective-permute-start(f32[3,512,128]{2,1,0:T(8,128)} %get-tuple-element.16), channel_id=1, source_target_pairs={{0,4},{8,12},{16,20},{24,28},{4,0},{12,8},{20,16},{28,24},{1,5},{9... | collective-permute-start | bytes 2359304 | tf_op jit(solution)/shard_map/ppermute | solution.py:796
  7.1 0.1 copy.11
  7.2 0.0 copy-done.3
  7.2 0.1 copy.12
  7.2 0.1 copy.14
  7.3 0.1 copy.13
  7.4 0.1 copy.16
  7.5 0.1 concatenate.3
  7.6 0.1 copy.15
  7.7 0.1 broadcast_in_dim.23.geo_ref.geo_in
  7.8 3.0 %first_sums.1 = (f32[8,512,128]{2,1,0:T(8,128)S(1)}, f32[8,128]{1,0:T(8,128)S(1)}) custom-call(s32[6,8]{1,0:T(8,128)S(1)} %get-tuple-element.29.links_ref, f32[33,8,128]{2,1,0:T(8,128)S(1)} %broadcast_in_dim.23.geo_ref.geo_in, f32[4096,128]{1,0:T(8,128)S(1)} %get-tuple-element.17.native_ref), custom_call_target="tpu_custom_call" | custom-call | flops 20971520 | bytes 10485760 | tf_op jit(solution)/shard_map/first_sums/pallas_call | solution.py:306
  10.8 3.7 %collective-permute-start.4 = (f32[8,128]{1,0:T(8,128)S(1)}, f32[8,128]{1,0:T(8,128)S(1)}, u32[]{:S(2)}, u32[]{:S(2)}) collective-permute-start(f32[8,128]{1,0:T(8,128)S(1)} %get-tuple-element.19.refs_0_), channel_id=1, source_target_pairs={{0,3},{1,2},{2,1},{3,0},{4,7},{5,6},{6,5},{7,4},{8,11},{9,10},{10,... | collective-permute-start | bytes 12296 | tf_op jit(solution)/shard_map/ppermute | solution.py:430
  14.4 0.0 collective-permute-start.3
  14.4 0.8 %collective-permute-start.2 = (f32[8,128]{1,0:T(8,128)S(1)}, f32[8,128]{1,0:T(8,128)S(1)}, u32[]{:S(2)}, u32[]{:S(2)}) collective-permute-start(f32[8,128]{1,0:T(8,128)S(1)} %get-tuple-element.19.refs_0_), channel_id=1, source_target_pairs={{0,1},{1,0},{2,3},{3,2},{4,5},{5,4},{6,7},{7,6},{8,9},{9,8},{10,11... | collective-permute-start | bytes 12296 | tf_op jit(solution)/shard_map/ppermute | solution.py:430
  15.2 2.4 %geometry.1.pairs_ref = f32[12,512,128]{2,1,0:T(8,128)S(1)} custom-call(s32[6,8]{1,0:T(8,128)S(1)} %get-tuple-element.29.links_ref, f32[33,8,128]{2,1,0:T(8,128)S(1)} %broadcast_in_dim.23.geo_ref.geo_in), custom_call_target="tpu_custom_call" | custom-call | flops 16777216 | bytes 8388608 | tf_op jit(solution)/shard_map/geometry/pallas_call | solution.py:415
  17.6 3.1 %flux.2.refs_5_ = f32[8,512,128]{2,1,0:T(8,128)S(1)} custom-call(s32[6,8]{1,0:T(8,128)S(1)} %get-tuple-element.29.links_ref, f32[33,8,128]{2,1,0:T(8,128)S(1)} %broadcast_in_dim.23.geo_ref.geo_in, f32[8,512,128]{2,1,0:T(8,128)S(1)} %get-tuple-element.18.f_ref.refs_4_.old_ref), custom_call_target="tpu_custom_call" | custom-call | flops 29360128 | bytes 14680064 | tf_op jit(solution)/shard_map/flux/pallas_call | solution.py:543
  20.7 0.0 collective-permute-done.4.refs_3_
  20.7 0.0 collective-permute-done.3.refs_2_
  20.7 0.0 collective-permute-done.2.refs_1_
  20.7 3.9 %add_target.2 = (f32[8,512,128]{2,1,0:T(8,128)S(1)}, f32[8,128]{1,0:T(8,128)S(1)}) custom-call(s32[6,8]{1,0:T(8,128)S(1)} %get-tuple-element.29.links_ref, f32[33,8,128]{2,1,0:T(8,128)S(1)} %broadcast_in_dim.23.geo_ref.geo_in, f32[8,128]{1,0:T(8,128)S(1)} %get-tuple-element.19.refs_0_, ...), custom_call_target="tpu_custom_call", output_to_operand_aliasing={{0}: (7, {})} | custom-call | flops 29360128 | bytes 14680064 | tf_op jit(solution)/shard_map/add_target/pallas_call | solution.py:658
  24.6 0.8 %collective-permute-done.far_in = f32[3,512,128]{2,1,0:T(8,128)S(1)} collective-permute-done((f32[3,512,128]{2,1,0:T(8,128)}, f32[3,512,128]{2,1,0:T(8,128)S(1)}, u32[]{:S(2)}, u32[]{:S(2)}) %collective-permute-start) | collective-permute-done | bytes 786464 | tf_op jit(solution)/shard_map/ppermute | solution.py:796
  25.4 0.0 collective-permute-done.1.near_in
  25.4 2.3 %edge.1 = (f32[8,512,128]{2,1,0:T(8,128)S(1)}, f32[3,512,128]{2,1,0:T(8,128)S(1)}, f32[3,512,128]{2,1,0:T(8,128)S(1)}) custom-call(f32[12,512,128]{2,1,0:T(8,128)S(1)} %geometry.1.pairs_ref, f32[3,512,128]{2,1,0:T(8,128)S(1)} %collective-permute-done.far_in, f32[3,512,128]{2,1,0:T(8,128)} %collective-permute-done.1.near_in, ...), custom_call_target="tpu_custom_call", output_to_operand_aliasing={{0}: (4, {})} | custom-call | flops 16777216 | bytes 8388608 | tf_op jit(solution)/shard_map/edge/pallas_call | solution.py:728
  27.7 3.6 %collective-permute-start.5 = (f32[3,512,128]{2,1,0:T(8,128)S(1)}, f32[3,512,128]{2,1,0:T(8,128)S(1)}, u32[]{:S(2)}, u32[]{:S(2)}) collective-permute-start(f32[3,512,128]{2,1,0:T(8,128)S(1)} %get-tuple-element.21), channel_id=1, source_target_pairs={{4,8},{12,16},{20,24},{8,4},{16,12},{24,20},{5,9},{13,17},{21,25},... | collective-permute-start | bytes 2359304 | tf_op jit(solution)/shard_map/ppermute | solution.py:796
  31.4 0.1 collective-permute-start.6
  31.5 2.2 %local_sums.1.refs_1_ = f32[8,128]{1,0:T(8,128)S(1)} custom-call(s32[6,8]{1,0:T(8,128)S(1)} %get-tuple-element.29.links_ref, f32[33,8,128]{2,1,0:T(8,128)S(1)} %broadcast_in_dim.23.geo_ref.geo_in, f32[8,512,128]{2,1,0:T(8,128)S(1)} %get-tuple-element.23.f_ref.refs_5_), custom_call_target="tpu_custom_call" | custom-call | flops 16777216 | bytes 8388608 | tf_op jit(solution)/shard_map/local_sums/pallas_call | solution.py:289
  33.6 3.6 %collective-permute-start.9 = (f32[8,128]{1,0:T(8,128)S(1)}, f32[8,128]{1,0:T(8,128)S(1)}, u32[]{:S(2)}, u32[]{:S(2)}) collective-permute-start(f32[8,128]{1,0:T(8,128)S(1)} %local_sums.1.refs_1_), channel_id=1, source_target_pairs={{0,3},{1,2},{2,1},{3,0},{4,7},{5,6},{6,5},{7,4},{8,11},{9,10},{10,... | collective-permute-start | bytes 12296 | tf_op jit(solution)/shard_map/ppermute | solution.py:430
  37.3 0.0 collective-permute-start.8
  37.3 0.8 %collective-permute-start.7 = (f32[8,128]{1,0:T(8,128)S(1)}, f32[8,128]{1,0:T(8,128)S(1)}, u32[]{:S(2)}, u32[]{:S(2)}) collective-permute-start(f32[8,128]{1,0:T(8,128)S(1)} %local_sums.1.refs_1_), channel_id=1, source_target_pairs={{0,1},{1,0},{2,3},{3,2},{4,5},{5,4},{6,7},{7,6},{8,9},{9,8},{10,11... | collective-permute-start | bytes 12296 | tf_op jit(solution)/shard_map/ppermute | solution.py:430
  38.0 3.1 %flux.3.refs_6_ = f32[8,512,128]{2,1,0:T(8,128)S(1)} custom-call(s32[6,8]{1,0:T(8,128)S(1)} %get-tuple-element.29.links_ref, f32[33,8,128]{2,1,0:T(8,128)S(1)} %broadcast_in_dim.23.geo_ref.geo_in, f32[8,512,128]{2,1,0:T(8,128)S(1)} %get-tuple-element.23.f_ref.refs_5_), custom_call_target="tpu_custom_call" | custom-call | flops 29360128 | bytes 14680064 | tf_op jit(solution)/shard_map/flux/pallas_call | solution.py:543
  41.1 0.0 collective-permute-done.9.refs_4_
  41.1 0.6 %collective-permute-done.8.refs_3_ = f32[8,128]{1,0:T(8,128)S(1)} collective-permute-done((f32[8,128]{1,0:T(8,128)S(1)}, f32[8,128]{1,0:T(8,128)S(1)}, u32[]{:S(2)}, u32[]{:S(2)}) %collective-permute-start.8) | collective-permute-done | bytes 4128 | tf_op jit(solution)/shard_map/ppermute | solution.py:430
  41.8 0.0 collective-permute-done.7.refs_2_
  41.8 4.5 %add_target.3 = (f32[8,512,128]{2,1,0:T(8,128)S(1)}, f32[8,128]{1,0:T(8,128)}) custom-call(s32[6,8]{1,0:T(8,128)S(1)} %get-tuple-element.29.links_ref, f32[33,8,128]{2,1,0:T(8,128)S(1)} %broadcast_in_dim.23.geo_ref.geo_in, f32[8,128]{1,0:T(8,128)S(1)} %get-tuple-element.24.refs_0_, f32[8,128]{1,0:T(8,128)S(1)} %local_sums.1.refs_1_, ...), custom_call_target="tpu_custom_call", output_to_operand_aliasing={{0}: (8, {})} | custom-call | flops 29360128 | bytes 14680064 | tf_op jit(solution)/shard_map/add_target/pallas_call | solution.py:658
  46.2 2.4 %collective-permute-done.5.far_ref = f32[3,512,128]{2,1,0:T(8,128)S(1)} collective-permute-done((f32[3,512,128]{2,1,0:T(8,128)S(1)}, f32[3,512,128]{2,1,0:T(8,128)S(1)}, u32[]{:S(2)}, u32[]{:S(2)}) %collective-permute-start.5) | collective-permute-done | bytes 786464 | tf_op jit(solution)/shard_map/ppermute | solution.py:796
  48.6 0.0 collective-permute-done.6.near_ref
  48.6 1.6 %last_edge.1 = (f32[4096,128]{1,0:T(8,128)}, f32[8,128]{1,0:T(8,128)S(1)}) custom-call(f32[33,8,128]{2,1,0:T(8,128)S(1)} %broadcast_in_dim.23.geo_ref.geo_in, f32[12,512,128]{2,1,0:T(8,128)S(1)} %geometry.1.pairs_ref, f32[3,512,128]{2,1,0:T(8,128)S(1)} %collective-permute-done.5.far_ref, f32[3,512,128]{2,1,0:T(8,128)S(1)} %collective-permute-done.6.near_ref, ...), custom_call_target="tpu_custom_call" | custom-call | flops 16777216 | bytes 8388608 | tf_op jit(solution)/shard_map/last_edge/pallas_call | solution.py:779
  50.2 1.6 %collective-permute-start.10 = (f32[8,128]{1,0:T(8,128)S(1)}, f32[8,128]{1,0:T(8,128)S(1)}, u32[]{:S(2)}, u32[]{:S(2)}) collective-permute-start(f32[8,128]{1,0:T(8,128)S(1)} %get-tuple-element.27), channel_id=1, source_target_pairs={{0,1},{1,0},{2,3},{3,2},{4,5},{5,4},{6,7},{7,6},{8,9},{9,8},{10,11... | collective-permute-start | bytes 12296 | tf_op jit(solution)/shard_map/ppermute | solution.py:438
  51.9 2.0 %collective-permute-done.10 = f32[8,128]{1,0:T(8,128)S(1)} collective-permute-done((f32[8,128]{1,0:T(8,128)S(1)}, f32[8,128]{1,0:T(8,128)S(1)}, u32[]{:S(2)}, u32[]{:S(2)}) %collective-permute-start.10) | collective-permute-done | bytes 4128 | tf_op jit(solution)/shard_map/ppermute | solution.py:438
  53.9 2.6 %collective-permute-start.11 = (f32[8,128]{1,0:T(8,128)S(1)}, f32[8,128]{1,0:T(8,128)S(1)}, u32[]{:S(2)}, u32[]{:S(2)}) collective-permute-start(f32[8,128]{1,0:T(8,128)S(1)} %add.7.refs_0_), channel_id=1, source_target_pairs={{0,2},{1,3},{2,0},{3,1},{4,6},{5,7},{6,4},{7,5},{8,10},{9,11},{10,... | collective-permute-start | bytes 12296 | tf_op jit(solution)/shard_map/ppermute | solution.py:439
  56.5 1.9 %collective-permute-done.11.refs_1_ = f32[8,128]{1,0:T(8,128)S(1)} collective-permute-done((f32[8,128]{1,0:T(8,128)S(1)}, f32[8,128]{1,0:T(8,128)S(1)}, u32[]{:S(2)}, u32[]{:S(2)}) %collective-permute-start.11) | collective-permute-done | bytes 4128 | tf_op jit(solution)/shard_map/ppermute | solution.py:439
  58.4 0.7 %macro.1 = f32[8,8]{1,0:T(8,128)} custom-call(f32[8,128]{1,0:T(8,128)S(1)} %add.7.refs_0_, f32[8,128]{1,0:T(8,128)S(1)} %collective-permute-done.11.refs_1_), custom_call_target="tpu_custom_call" | custom-call | tf_op jit(solution)/shard_map/macro/pallas_call | solution.py:476
  (7 shorter events, 0.0 us)
Async XLA Ops:
  0.6 6.4 %copy-start.2 = (f32[8]{0:T(128)S(1)}, f32[8]{0:T(128)}, u32[]{:S(2)}) copy-start(f32[8]{0:T(128)} %param.8) | copy-start | bytes 100
  0.6 6.5 %copy-start.3 = (f32[8]{0:T(128)S(1)}, f32[8]{0:T(128)}, u32[]{:S(2)}) copy-start(f32[8]{0:T(128)} %param.9) | copy-start | bytes 100
  0.7 6.6 %copy-start.1 = (s32[6,8]{1,0:T(8,128)S(1)}, s32[6,8]{1,0:T(8,128)}, u32[]{:S(2)}) copy-start(s32[6,8]{1,0:T(8,128)} %param.6) | copy-start | bytes 580
  0.7 6.8 %copy-start = (f32[3,6,8]{2,1,0:T(8,128)S(1)}, f32[3,6,8]{2,1,0:T(8,128)}, u32[]{:S(2)}) copy-start(f32[3,6,8]{2,1,0:T(8,128)} %param.7) | copy-start | bytes 1732
  3.5 21.9 %collective-permute-start = (f32[3,512,128]{2,1,0:T(8,128)}, f32[3,512,128]{2,1,0:T(8,128)S(1)}, u32[]{:S(2)}, u32[]{:S(2)}) collective-permute-start(f32[3,512,128]{2,1,0:T(8,128)} %get-tuple-element.15), channel_id=1, source_target_pairs={{4,8},{12,16},{20,24},{8,4},{16,12},{24,20},{5,9},{13,17},{21,25},... | collective-permute-start | bytes 2359304 | tf_op jit(solution)/shard_map/ppermute | solution.py:796
  6.3 19.2 %collective-permute-start.1 = (f32[3,512,128]{2,1,0:T(8,128)}, f32[3,512,128]{2,1,0:T(8,128)}, u32[]{:S(2)}, u32[]{:S(2)}) collective-permute-start(f32[3,512,128]{2,1,0:T(8,128)} %get-tuple-element.16), channel_id=1, source_target_pairs={{0,4},{8,12},{16,20},{24,28},{4,0},{12,8},{20,16},{28,24},{1,5},{9... | collective-permute-start | bytes 2359304 | tf_op jit(solution)/shard_map/ppermute | solution.py:796
  10.8 9.9 %collective-permute-start.4 = (f32[8,128]{1,0:T(8,128)S(1)}, f32[8,128]{1,0:T(8,128)S(1)}, u32[]{:S(2)}, u32[]{:S(2)}) collective-permute-start(f32[8,128]{1,0:T(8,128)S(1)} %get-tuple-element.19.refs_0_), channel_id=1, source_target_pairs={{0,3},{1,2},{2,1},{3,0},{4,7},{5,6},{6,5},{7,4},{8,11},{9,10},{10,... | collective-permute-start | bytes 12296 | tf_op jit(solution)/shard_map/ppermute | solution.py:430
  14.4 6.3 %collective-permute-start.3 = (f32[8,128]{1,0:T(8,128)S(1)}, f32[8,128]{1,0:T(8,128)S(1)}, u32[]{:S(2)}, u32[]{:S(2)}) collective-permute-start(f32[8,128]{1,0:T(8,128)S(1)} %get-tuple-element.19.refs_0_), channel_id=1, source_target_pairs={{0,2},{1,3},{2,0},{3,1},{4,6},{5,7},{6,4},{7,5},{8,10},{9,11},{10,... | collective-permute-start | bytes 12296 | tf_op jit(solution)/shard_map/ppermute | solution.py:430
  14.4 6.3 %collective-permute-start.2 = (f32[8,128]{1,0:T(8,128)S(1)}, f32[8,128]{1,0:T(8,128)S(1)}, u32[]{:S(2)}, u32[]{:S(2)}) collective-permute-start(f32[8,128]{1,0:T(8,128)S(1)} %get-tuple-element.19.refs_0_), channel_id=1, source_target_pairs={{0,1},{1,0},{2,3},{3,2},{4,5},{5,4},{6,7},{7,6},{8,9},{9,8},{10,11... | collective-permute-start | bytes 12296 | tf_op jit(solution)/shard_map/ppermute | solution.py:430
  27.7 20.9 %collective-permute-start.5 = (f32[3,512,128]{2,1,0:T(8,128)S(1)}, f32[3,512,128]{2,1,0:T(8,128)S(1)}, u32[]{:S(2)}, u32[]{:S(2)}) collective-permute-start(f32[3,512,128]{2,1,0:T(8,128)S(1)} %get-tuple-element.21), channel_id=1, source_target_pairs={{4,8},{12,16},{20,24},{8,4},{16,12},{24,20},{5,9},{13,17},{21,25},... | collective-permute-start | bytes 2359304 | tf_op jit(solution)/shard_map/ppermute | solution.py:796
  31.4 17.2 %collective-permute-start.6 = (f32[3,512,128]{2,1,0:T(8,128)S(1)}, f32[3,512,128]{2,1,0:T(8,128)S(1)}, u32[]{:S(2)}, u32[]{:S(2)}) collective-permute-start(f32[3,512,128]{2,1,0:T(8,128)S(1)} %get-tuple-element.22), channel_id=1, source_target_pairs={{0,4},{8,12},{16,20},{24,28},{4,0},{12,8},{20,16},{28,24},{1,5},{9... | collective-permute-start | bytes 2359304 | tf_op jit(solution)/shard_map/ppermute | solution.py:796
  33.6 7.5 %collective-permute-start.9 = (f32[8,128]{1,0:T(8,128)S(1)}, f32[8,128]{1,0:T(8,128)S(1)}, u32[]{:S(2)}, u32[]{:S(2)}) collective-permute-start(f32[8,128]{1,0:T(8,128)S(1)} %local_sums.1.refs_1_), channel_id=1, source_target_pairs={{0,3},{1,2},{2,1},{3,0},{4,7},{5,6},{6,5},{7,4},{8,11},{9,10},{10,... | collective-permute-start | bytes 12296 | tf_op jit(solution)/shard_map/ppermute | solution.py:430
  37.3 4.5 %collective-permute-start.8 = (f32[8,128]{1,0:T(8,128)S(1)}, f32[8,128]{1,0:T(8,128)S(1)}, u32[]{:S(2)}, u32[]{:S(2)}) collective-permute-start(f32[8,128]{1,0:T(8,128)S(1)} %local_sums.1.refs_1_), channel_id=1, source_target_pairs={{0,2},{1,3},{2,0},{3,1},{4,6},{5,7},{6,4},{7,5},{8,10},{9,11},{10,... | collective-permute-start | bytes 12296 | tf_op jit(solution)/shard_map/ppermute | solution.py:430
  37.3 4.5 %collective-permute-start.7 = (f32[8,128]{1,0:T(8,128)S(1)}, f32[8,128]{1,0:T(8,128)S(1)}, u32[]{:S(2)}, u32[]{:S(2)}) collective-permute-start(f32[8,128]{1,0:T(8,128)S(1)} %local_sums.1.refs_1_), channel_id=1, source_target_pairs={{0,1},{1,0},{2,3},{3,2},{4,5},{5,4},{6,7},{7,6},{8,9},{9,8},{10,11... | collective-permute-start | bytes 12296 | tf_op jit(solution)/shard_map/ppermute | solution.py:430
  50.2 3.7 %collective-permute-start.10 = (f32[8,128]{1,0:T(8,128)S(1)}, f32[8,128]{1,0:T(8,128)S(1)}, u32[]{:S(2)}, u32[]{:S(2)}) collective-permute-start(f32[8,128]{1,0:T(8,128)S(1)} %get-tuple-element.27), channel_id=1, source_target_pairs={{0,1},{1,0},{2,3},{3,2},{4,5},{5,4},{6,7},{7,6},{8,9},{9,8},{10,11... | collective-permute-start | bytes 12296 | tf_op jit(solution)/shard_map/ppermute | solution.py:438
  53.9 4.5 %collective-permute-start.11 = (f32[8,128]{1,0:T(8,128)S(1)}, f32[8,128]{1,0:T(8,128)S(1)}, u32[]{:S(2)}, u32[]{:S(2)}) collective-permute-start(f32[8,128]{1,0:T(8,128)S(1)} %add.7.refs_0_), channel_id=1, source_target_pairs={{0,2},{1,3},{2,0},{3,1},{4,6},{5,7},{6,4},{7,5},{8,10},{9,11},{10,... | collective-permute-start | bytes 12296 | tf_op jit(solution)/shard_map/ppermute | solution.py:439

commit v9 on v8

--- a/solution.py
+++ b/solution.py
@@ -101,6 +101,33 @@
     for s in range(1, SUB):
         out = out + ref[k, pl.ds(s, SUB, stride=SUB), :]
     return out
+
+
+def list_faces(links_ref, wanted, cell_ref, face_ref):
+    def cell(g, count):
+        for k in range(FACES):
+            cell_ref[count] = g
+            face_ref[count] = k
+            count = count + wanted(links_ref[k, g]).astype(jnp.int32)
+        return count
+
+    return lax.fori_loop(0, SUB, cell, 0)
+
+
+def is_wall(j):
+    return j == WALL_LINK
+
+
+def is_remote(j):
+    return jnp.logical_or(j >= SUB, jnp.logical_and(j < 0, j != WALL_LINK))
+
+
+def face_lists():
+    return [pltpu.SMEM((FACES * SUB + 1,), jnp.int32)] * 2
+
+
+def unroll(planes, most):
+    return math.gcd(planes, most)
 
 
 def finish_polynomials(y, first, planes):
@@ -198,61 +225,55 @@
     ]
 
 
-def wall_sums(f_ref, planes, links_ref, geo_ref, sums_ref, with_absorbed):
+def wall_sums(f_ref, planes, links_ref, geo_ref, sums_ref, cells, faces, with_absorbed):
     sums_ref[...] = jnp.zeros_like(sums_ref)
 
-    def cell(g, _):
-        for k in range(FACES):
-
-            @pl.when(links_ref[k, g] == WALL_LINK)
-            def _():
-                v0, v1, v2 = face_coefficients(geo_ref, k, g)
-                first = splat(geo_ref, FIRST, g)
-                base = []
-                for t in range(TILES):
-                    xb, xc = tile_nodes(t)
-                    base.append(v1 * xb + v2 * xc)
+    def wall(i, _):
+        g, k = cells[i], faces[i]
+        v0, v1, v2 = face_coefficients(geo_ref, k, g)
+        first = splat(geo_ref, FIRST, g)
+        base = []
+        for t in range(TILES):
+            xb, xc = tile_nodes(t)
+            base.append(v1 * xb + v2 * xc)
+        if with_absorbed:
+            wt = splat(geo_ref, WT, g)
+            shape = wall_tiles(wt)
+
+        def plane(a, acc):
+            out, back = list(acc[0]), list(acc[1])
+            xa = first + a.astype(F32) * H
+            sa = v0 * xa
+            if with_absorbed:
+                wa = jnp.exp(-0.5 * xa * xa / wt)
+            for t in range(TILES):
+                s = sa + base[t]
+                f = f_ref[g, at_rows((a * TILES + t) * SUB), :]
+                out[t] = out[t] + jnp.maximum(s, 0.0) * f
                 if with_absorbed:
-                    wt = splat(geo_ref, WT, g)
-                    shape = wall_tiles(wt)
-
-                def plane(a, acc):
-                    out, back = list(acc[0]), list(acc[1])
-                    xa = first + a.astype(F32) * H
-                    sa = v0 * xa
-                    if with_absorbed:
-                        wa = jnp.exp(-0.5 * xa * xa / wt)
-                    for t in range(TILES):
-                        s = sa + base[t]
-                        f = f_ref[g, at_rows((a * TILES + t) * SUB), :]
-                        out[t] = out[t] + jnp.maximum(s, 0.0) * f
-                        if with_absorbed:
-                            back[t] = back[t] + jnp.maximum(-s, 0.0) * (wa * shape[t])
-                    return tuple(out), tuple(back)
-
-                zeros = (jnp.zeros((SUB, LANES), F32),) * TILES
-                out, back = lax.fori_loop(0, planes, plane, (zeros, zeros), unroll=4)
-                out = (out[0] + out[1]) + (out[2] + out[3])
-                back = (back[0] + back[1]) + (back[2] + back[3])
-                at = at_rows(g * SUB)
-                sums_ref[k, at, :] = out
-                if with_absorbed:
-                    sums_ref[FACES + k, at, :] = back
-
+                    back[t] = back[t] + jnp.maximum(-s, 0.0) * (wa * shape[t])
+            return tuple(out), tuple(back)
+
+        zeros = (jnp.zeros((SUB, LANES), F32),) * TILES
+        out, back = lax.fori_loop(0, planes, plane, (zeros, zeros), unroll=unroll(planes, 16))
+        at = at_rows(g * SUB)
+        sums_ref[k, at, :] = (out[0] + out[1]) + (out[2] + out[3])
+        if with_absorbed:
+            sums_ref[FACES + k, at, :] = (back[0] + back[1]) + (back[2] + back[3])
         return 0
 
-    lax.fori_loop(0, SUB, cell, 0)
-
-
-def sums_kernel(links_ref, geo_ref, f_ref, sums_out, parts_ref, face_ref):
+    lax.fori_loop(0, list_faces(links_ref, is_wall, cells, faces), wall, 0)
+
+
+def sums_kernel(links_ref, geo_ref, f_ref, sums_out, parts_ref, face_ref, cells, faces):
     planes = f_ref.shape[1] // CHUNKS
     y = polynomial_sums(f_ref, planes, parts_ref)
     packed = pack_sums(finish_polynomials(y, geo_ref[FIRST], planes), 0)
-    wall_sums(f_ref, planes, links_ref, geo_ref, face_ref, False)
+    wall_sums(f_ref, planes, links_ref, geo_ref, face_ref, cells, faces, False)
     sums_out[...] = packed + pack_sums([over_sublanes(face_ref, k) for k in range(FACES)], EMIT)
 
 
-def first_sums_kernel(links_ref, geo_ref, native_ref, f_ref, sums_out, face_ref):
+def first_sums_kernel(links_ref, geo_ref, native_ref, f_ref, sums_out, face_ref, cells, faces):
     rows = f_ref.shape[1]
     planes = rows // CHUNKS
 
@@ -264,7 +285,7 @@
     lax.fori_loop(0, rows // SUB, group, 0, unroll=2)
     y = native_polynomial_sums(native_ref, planes)
     packed = pack_sums(finish_polynomials(y, geo_ref[FIRST], planes), 0)
-    wall_sums(f_ref, planes, links_ref, geo_ref, face_ref, True)
+    wall_sums(f_ref, planes, links_ref, geo_ref, face_ref, cells, faces, True)
     sums_out[...] = packed + pack_sums([over_sublanes(face_ref, k) for k in range(2 * FACES)], EMIT)
 
 
@@ -276,7 +297,7 @@
     return jax.ShapeDtypeStruct(shape, F32)
 
 
-def params(mib=16):
+def params(mib=8):
     return pltpu.CompilerParams(vmem_limit_bytes=mib * 1024 * 1024)
 
 
@@ -294,6 +315,7 @@
         scratch_shapes=[
                 pltpu.VMEM((10, SUB * SUB, LANES), F32),
             pltpu.VMEM((FACES, SUB * SUB, LANES), F32),
+            *face_lists(),
         ],
         compiler_params=params(),
         cost_estimate=traffic(f.shape[1], 4),
@@ -310,6 +332,7 @@
         out_shape=[array(SUB, rows, LANES), array(SUB, LANES)],
         scratch_shapes=[
                 pltpu.VMEM((2 * FACES, SUB * SUB, LANES), F32),
+            *face_lists(),
         ],
         compiler_params=params(),
         cost_estimate=traffic(rows, 5),
@@ -324,7 +347,7 @@
     return lax.rem(lax.axis_index("space"), 2) == 1
 
 
-def first_rows_kernel(native_hbm, native_ref, far_ref, near_ref, sems):
+def first_rows_kernel(native_hbm, native_ref, far_any, near_any, far_ref, near_ref, sems, far_sems, near_sems):
     rows = native_ref.shape[0]
     part = rows // SPLIT_PARTS
     copies = [
@@ -339,6 +362,7 @@
     far = jnp.where(odd, SUB - REACH, 0)
     near = jnp.where(odd, 0, SUB - REACH)
     groups = part // (SUB * SUB)
+    out = []
 
     for i, c in enumerate(copies):
         c.wait()
@@ -350,24 +374,32 @@
                 near_ref[r, at, :] = native_ref[pl.ds(j * SUB * SUB + near + r, SUB, stride=SUB), :]
             return 0
 
-        lax.fori_loop(i * groups, (i + 1) * groups, group, 0, unroll=4)
+        lax.fori_loop(i * groups, (i + 1) * groups, group, 0, unroll=unroll(groups, 8))
+        at = pl.ds(i * groups * SUB, groups * SUB)
+        out.append(pltpu.make_async_copy(far_ref.at[:, at], far_any.at[:, at], far_sems.at[i]))
+        out.append(pltpu.make_async_copy(near_ref.at[:, at], near_any.at[:, at], near_sems.at[i]))
+        out[-2].start()
+        out[-1].start()
+    for c in out:
+        c.wait()
 
 
 def first_rows(native):
     rows = native.shape[0] // SUB
+    halo = (REACH, rows, LANES)
     return pl.pallas_call(
         first_rows_kernel,
         in_specs=[spec(pltpu.HBM)],
-        out_specs=[spec(pltpu.VMEM)] * 3,
-        out_shape=[pltpu.VMEM(native.shape, F32)] + [pltpu.VMEM((REACH, rows, LANES), F32)] * 2,
-        scratch_shapes=[pltpu.SemaphoreType.DMA((SPLIT_PARTS,))],
+        out_specs=[spec(pltpu.VMEM), spec(pl.ANY), spec(pl.ANY)],
+        out_shape=[array(*native.shape), array(*halo), array(*halo)],
+        scratch_shapes=[pltpu.VMEM(halo, F32)] * 2 + [pltpu.SemaphoreType.DMA((SPLIT_PARTS,))] * 3,
         compiler_params=params(),
         cost_estimate=traffic(rows, 4),
         name="first_rows",
     )(pltpu.with_memory_space_constraint(native, pltpu.HBM))
 
 
-def geometry_kernel(links_ref, geo_ref, pairs_ref):
+def geometry_kernel(links_ref, geo_ref, pairs_ref, cells, faces):
     rows = pairs_ref.shape[1]
     planes = rows // CHUNKS
     first = splat(geo_ref, FIRST, 0)
@@ -377,38 +409,33 @@
             pairs_ref[p, at_rows(j * SUB), :] = jnp.zeros((SUB, LANES), F32)
         return 0
 
-    lax.fori_loop(0, rows // SUB, clear, 0, unroll=2)
-
-    def cell(g, _):
+    lax.fori_loop(0, rows // SUB, clear, 0, unroll=4)
+
+    def remote(i, _):
+        g, k = cells[i], faces[i]
+        j = links_ref[k, g]
         edge = g - (SUB - REACH)
-        for k in range(FACES):
-            j = links_ref[k, g]
-            is_before = jnp.logical_and(j < 0, j != WALL_LINK)
-
-            @pl.when(jnp.logical_or(is_before, j >= SUB))
-            def _():
-                before = g * REACH - g * (g - 1) // 2 + (j + REACH) - g
-                after = len(BEFORE_PAIRS) + edge * (edge + 1) // 2 + j - SUB
-                at_pair = jnp.where(is_before, before, after)
-                scale = -TIME_STEP / splat(geo_ref, VOL, g)
-                v0, v1, v2 = [scale * x for x in face_coefficients(geo_ref, k, g)]
-                base = []
-                for t in range(TILES):
-                    xb, xc = tile_nodes(t)
-                    base.append(v1 * xb + v2 * xc)
-
-                def plane(a, _):
-                    sa = v0 * (first + a.astype(F32) * H)
-                    for t in range(TILES):
-                        at = at_rows((a * TILES + t) * SUB)
-                        pairs_ref[at_pair, at, :] = pairs_ref[at_pair, at, :] + jnp.maximum(sa + base[t], 0.0)
-                    return 0
-
-                lax.fori_loop(0, planes, plane, 0, unroll=4)
-
+        before = g * REACH - g * (g - 1) // 2 + (j + REACH) - g
+        after = len(BEFORE_PAIRS) + edge * (edge + 1) // 2 + j - SUB
+        at_pair = jnp.where(j < 0, before, after)
+        scale = -TIME_STEP / splat(geo_ref, VOL, g)
+        v0, v1, v2 = [scale * x for x in face_coefficients(geo_ref, k, g)]
+        base = []
+        for t in range(TILES):
+            xb, xc = tile_nodes(t)
+            base.append(v1 * xb + v2 * xc)
+
+        def plane(a, _):
+            sa = v0 * (first + a.astype(F32) * H)
+            for t in range(TILES):
+                at = at_rows((a * TILES + t) * SUB)
+                pairs_ref[at_pair, at, :] = pairs_ref[at_pair, at, :] + jnp.maximum(sa + base[t], 0.0)
+            return 0
+
+        lax.fori_loop(0, planes, plane, 0, unroll=unroll(planes, 8))
         return 0
 
-    lax.fori_loop(0, SUB, cell, 0)
+    lax.fori_loop(0, list_faces(links_ref, is_remote, cells, faces), remote, 0)
 
 
 def geometry(links, geo, rows):
@@ -417,6 +444,7 @@
         in_specs=[spec(pltpu.SMEM), spec(pltpu.VMEM)],
         out_specs=spec(pltpu.VMEM),
         out_shape=array(2 * len(BEFORE_PAIRS), rows, LANES),
+        scratch_shapes=face_lists(),
         compiler_params=params(),
         cost_estimate=traffic(rows, 4),
         name="geometry",
@@ -514,27 +542,26 @@
         weight = [[splat(coef, FACES * i + face[k], g) for i in range(3)] for k in range(n)]
         whole = [splat(coef, 3 * FACES + i, g) for i in range(3)]
         x0 = splat(geo_ref, FIRST, g)
-        for pair in range(TILES // 2):
-            base, stay = [], []
-            for t in (2 * pair, 2 * pair + 1):
-                xb, xc = tile_nodes(t)
-                base.append([w[1] * xb + w[2] * xc for w in weight])
-                stay.append(1.0 + whole[1] * xb + whole[2] * xc)
-
-            def plane(a, _):
-                xa = x0 + a.astype(F32) * H
-                sa = [w[0] * xa for w in weight]
-                stay_a = whole[0] * xa
-                for i in range(2):
-                    at = at_rows((a * TILES + 2 * pair + i) * SUB)
-                    f = f_ref[g, at, :]
-                    acc = f * (stay_a + stay[i])
-                    for k in range(n):
-                        acc = acc + jnp.maximum(sa[k] + base[i][k], 0.0) * (f_ref[at_source[k], at, :] - f)
-                    out_ref[g, at, :] = acc
-                return 0
-
-            lax.fori_loop(0, planes, plane, 0, unroll=math.gcd(planes, 8))
+        base, stay = [], []
+        for t in range(TILES):
+            xb, xc = tile_nodes(t)
+            base.append([w[1] * xb + w[2] * xc for w in weight])
+            stay.append(1.0 + whole[1] * xb + whole[2] * xc)
+
+        def plane(a, _):
+            xa = x0 + a.astype(F32) * H
+            sa = [w[0] * xa for w in weight]
+            stay_a = whole[0] * xa
+            for t in range(TILES):
+                at = at_rows((a * TILES + t) * SUB)
+                f = f_ref[g, at, :]
+                acc = f * (stay_a + stay[t])
+                for k in range(n):
+                    acc = acc + jnp.maximum(sa[k] + base[t][k], 0.0) * (f_ref[at_source[k], at, :] - f)
+                out_ref[g, at, :] = acc
+            return 0
+
+        lax.fori_loop(0, planes, plane, 0, unroll=unroll(planes, 8))
 
     lax.fori_loop(0, SUB, cell, 0)
 
@@ -557,7 +584,7 @@
 
 
 def target_kernel(count, links_ref, geo_ref, absorbed_in, *refs):
-    sums_refs, (f_ref, part_ref, out_ref, sum_out, ta, coef) = refs[:count], refs[count:]
+    sums_refs, (f_ref, part_ref, out_ref, sum_out, ta, coef, cells, faces) = refs[:count], refs[count:]
     planes = f_ref.shape[1] // CHUNKS
     sums = add_tiles(sums_refs)
     sum_out[...] = sums
@@ -590,7 +617,6 @@
         rate_g, rtg = splat(coef, 0, g), splat(coef, 1, g)
         ub, uc = splat(coef, 2, g), splat(coef, 3, g)
         qb, qc = splat(coef, 4, g), splat(coef, 5, g)
-        x0 = splat(geo_ref, FIRST, g)
         bell, heat, zz = [], [], []
         for t in range(TILES):
             xb, xc = tile_nodes(t)
@@ -611,37 +637,38 @@
                 out_ref[where] = (part_ref[where] - rate_g * f) + target
             return 0
 
-        lax.fori_loop(0, planes, plane, 0, unroll=math.gcd(planes, 8))
-
-        for k in range(FACES):
-
-            @pl.when(links_ref[k, g] == WALL_LINK)
-            def _():
-                wt = splat(geo_ref, WT, g)
-                ratio = splat(coef, 6 + k, g)
-                shape = [ratio * x for x in wall_tiles(wt)]
-                scale = -TIME_STEP / splat(geo_ref, VOL, g)
-                v0, v1, v2 = [scale * x for x in face_coefficients(geo_ref, k, g)]
-                base = []
-                for t in range(TILES):
-                    xb, xc = tile_nodes(t)
-                    base.append(v1 * xb + v2 * xc)
-
-                def plane(a, _):
-                    xa = x0 + a.astype(F32) * H
-                    wa = jnp.exp(-0.5 * xa * xa / wt)
-                    sa = v0 * xa
-                    for t in range(TILES):
-                        where = (g, at_rows((a * TILES + t) * SUB), slice(None))
-                        f = f_ref[where]
-                        out_ref[where] = out_ref[where] + jnp.maximum(sa + base[t], 0.0) * (wa * shape[t] - f)
-                    return 0
-
-                lax.fori_loop(0, planes, plane, 0, unroll=4)
-
+        lax.fori_loop(0, planes, plane, 0, unroll=unroll(planes, 16))
         return 0
 
     lax.fori_loop(0, SUB, cell, 0)
+
+    def wall(i, _):
+        g, k = cells[i], faces[i]
+        x0 = splat(geo_ref, FIRST, g)
+        wt = splat(geo_ref, WT, g)
+        ratio = splat(coef, 6 + k, g)
+        shape = [ratio * x for x in wall_tiles(wt)]
+        scale = -TIME_STEP / splat(geo_ref, VOL, g)
+        v0, v1, v2 = [scale * x for x in face_coefficients(geo_ref, k, g)]
+        base = []
+        for t in range(TILES):
+            xb, xc = tile_nodes(t)
+            base.append(v1 * xb + v2 * xc)
+
+        def plane(a, _):
+            xa = x0 + a.astype(F32) * H
+            wa = jnp.exp(-0.5 * xa * xa / wt)
+            sa = v0 * xa
+            for t in range(TILES):
+                where = (g, at_rows((a * TILES + t) * SUB), slice(None))
+                f = f_ref[where]
+                out_ref[where] = out_ref[where] + jnp.maximum(sa + base[t], 0.0) * (wa * shape[t] - f)
+            return 0
+
+        lax.fori_loop(0, planes, plane, 0, unroll=unroll(planes, 8))
+        return 0
+
+    lax.fori_loop(0, list_faces(links_ref, is_wall, cells, faces), wall, 0)
 
 
 def add_target(links, geo, absorbed, tiles, f, part):
@@ -664,6 +691,7 @@
         scratch_shapes=[
                 pltpu.VMEM((3, rows // CHUNKS, SUB, LANES), F32),
             pltpu.VMEM((6 + FACES, SUB, LANES), F32),
+            *face_lists(),
         ],
         compiler_params=params(),
         cost_estimate=traffic(rows, 7),
@@ -718,7 +746,7 @@
                 f_ref[e, at, :] = x
             return 0
 
-        lax.fori_loop(0, part_ref.shape[1] // SUB, group, 0, unroll=2)
+        lax.fori_loop(0, part_ref.shape[1] // SUB, group, 0, unroll=4)
 
     by_side(far_in, near_in, run)
 

time: 59.4 us -> 59 us (level)
  Pallas kernels: 29.5 us -> 27.5 us
  waiting for transfers between devices: 7.79 us -> 9.36 us
    ppermute x4, waiting for transfers between devices: 3.2 us -> 4.58 us  [exchange(): out.append(lax.ppermute(x, 'space', pairs + [(j, i) for i, j in pairs]))]
  transfers between devices with their start and end apart: 12 -> 12, of which waited for: 5 -> 5; matrix products, arithmetic and copies ran while one was open for 1% -> 1% of each run, Pallas kernels for 37% -> 35%
where the time goes in v9:
time: 59 us; the launch traced here: 58.7 us
  Pallas kernels  27.5 us (47%)
  starting transfers between devices  20.4 us (35%)
  waiting for transfers between devices  9.36 us (16%)
  between operations  0.79 us (1%)
  local copies, waits for them, and re-layouts  0.69 us (1%)
    ppermute x6, starting transfers between devices, gather_sums(): lax.ppermute(tile, 'vel', [(i, i ^ s) for i in range(size)])  8.84 us
    pallas_call x2, Pallas kernels, add_target(): pl.pallas_call(kernel, in_specs=[spec(pltpu.SMEM)] + [vmem] * (len(given)...  8.42 us
    ppermute x4, starting transfers between devices, exchange(): out.append(lax.ppermute(x, 'space', pairs + [(j, i) for i, j in pairs]))  7.3 us
    pallas_call x2, Pallas kernels, flux(): pl.pallas_call(flux_kernel, in_specs=[spec(pltpu.SMEM), spec(pltpu.VMEM),...  5.76 us
    ppermute x4, waiting for transfers between devices, exchange(): out.append(lax.ppermute(x, 'space', pairs + [(j, i) for i, j in pairs]))  4.58 us
    ppermute x1, starting transfers between devices, doubling_sums(): return [pair, lax.ppermute(pair, 'vel', [(i, i ^ 2) for i in range(size)])]  2.59 us
    pallas_call x1, Pallas kernels, first_sums(): pl.pallas_call(first_sums_kernel, in_specs=[spec(pltpu.SMEM), spec(pltpu....  2.55 us
    pallas_call x1, Pallas kernels, first_rows(): pl.pallas_call(first_rows_kernel, in_specs=[spec(pltpu.HBM)], out_specs=[...  2.5 us
  transfers between devices with their start and end apart: 12, of which 5 were waited for; matrix products, arithmetic and copies ran while one was open for 1% of the time, Pallas kernels for 35%

profile of v9, /device:TPU:4, one launch (start us, length us, event | category | flops | bytes accessed | tf_op | source)
XLA Modules:
  0.0 58.7 jit_solution(6791818001603568525)
XLA Ops:
  0.6 0.0 copy-start.2
  0.6 0.0 copy-start.3
  0.7 0.0 copy-start.1
  0.7 0.0 copy-start
  0.7 2.5 %first_rows.1 = (f32[4096,128]{1,0:T(8,128)S(1)}, f32[3,512,128]{2,1,0:T(8,128)}, f32[3,512,128]{2,1,0:T(8,128)}) custom-call(f32[4096,128]{1,0:T(8,128)} %bitcast.12), custom_call_target="tpu_custom_call" | custom-call | flops 16777216 | bytes 8388608 | tf_op jit(solution)/shard_map/first_rows/pallas_call | solution.py:390
  3.2 2.8 %collective-permute-start = (f32[3,512,128]{2,1,0:T(8,128)}, f32[3,512,128]{2,1,0:T(8,128)S(1)}, u32[]{:S(2)}, u32[]{:S(2)}) collective-permute-start(f32[3,512,128]{2,1,0:T(8,128)} %get-tuple-element.15), channel_id=1, source_target_pairs={{4,8},{12,16},{20,24},{8,4},{16,12},{24,20},{5,9},{13,17},{21,25},... | collective-permute-start | bytes 2359304 | tf_op jit(solution)/shard_map/ppermute | solution.py:824
  6.0 0.8 %collective-permute-start.1 = (f32[3,512,128]{2,1,0:T(8,128)}, f32[3,512,128]{2,1,0:T(8,128)}, u32[]{:S(2)}, u32[]{:S(2)}) collective-permute-start(f32[3,512,128]{2,1,0:T(8,128)} %get-tuple-element.16), channel_id=1, source_target_pairs={{0,4},{8,12},{16,20},{24,28},{4,0},{12,8},{20,16},{28,24},{1,5},{9... | collective-permute-start | bytes 2359304 | tf_op jit(solution)/shard_map/ppermute | solution.py:824
  6.8 0.1 copy.11
  6.8 0.1 copy.12
  6.9 0.0 copy-done.1
  6.9 0.1 copy.14
  7.0 0.1 copy.13
  7.1 0.1 copy.16
  7.2 0.1 concatenate.3
  7.3 0.1 copy.15
  7.4 0.1 broadcast_in_dim.23.geo_ref.geo_in
  7.5 2.6 %first_sums.1 = (f32[8,512,128]{2,1,0:T(8,128)S(1)}, f32[8,128]{1,0:T(8,128)S(1)}) custom-call(s32[6,8]{1,0:T(8,128)S(1)} %get-tuple-element.29.links_ref, f32[33,8,128]{2,1,0:T(8,128)S(1)} %broadcast_in_dim.23.geo_ref.geo_in, f32[4096,128]{1,0:T(8,128)S(1)} %get-tuple-element.17.native_ref), custom_call_target="tpu_custom_call" | custom-call | flops 20971520 | bytes 10485760 | tf_op jit(solution)/shard_map/first_sums/pallas_call | solution.py:328
  10.0 3.7 %collective-permute-start.4 = (f32[8,128]{1,0:T(8,128)S(1)}, f32[8,128]{1,0:T(8,128)S(1)}, u32[]{:S(2)}, u32[]{:S(2)}) collective-permute-start(f32[8,128]{1,0:T(8,128)S(1)} %get-tuple-element.19.refs_0_), channel_id=1, source_target_pairs={{0,3},{1,2},{2,1},{3,0},{4,7},{5,6},{6,5},{7,4},{8,11},{9,10},{10,... | collective-permute-start | bytes 12296 | tf_op jit(solution)/shard_map/ppermute | solution.py:458
  13.7 0.0 collective-permute-start.3
  13.7 0.8 %collective-permute-start.2 = (f32[8,128]{1,0:T(8,128)S(1)}, f32[8,128]{1,0:T(8,128)S(1)}, u32[]{:S(2)}, u32[]{:S(2)}) collective-permute-start(f32[8,128]{1,0:T(8,128)S(1)} %get-tuple-element.19.refs_0_), channel_id=1, source_target_pairs={{0,1},{1,0},{2,3},{3,2},{4,5},{5,4},{6,7},{7,6},{8,9},{9,8},{10,11... | collective-permute-start | bytes 12296 | tf_op jit(solution)/shard_map/ppermute | solution.py:458
  14.5 2.0 %geometry.1.pairs_ref = f32[12,512,128]{2,1,0:T(8,128)S(1)} custom-call(s32[6,8]{1,0:T(8,128)S(1)} %get-tuple-element.29.links_ref, f32[33,8,128]{2,1,0:T(8,128)S(1)} %broadcast_in_dim.23.geo_ref.geo_in), custom_call_target="tpu_custom_call" | custom-call | flops 16777216 | bytes 8388608 | tf_op jit(solution)/shard_map/geometry/pallas_call | solution.py:442
  16.5 2.9 %flux.2.refs_5_ = f32[8,512,128]{2,1,0:T(8,128)S(1)} custom-call(s32[6,8]{1,0:T(8,128)S(1)} %get-tuple-element.29.links_ref, f32[33,8,128]{2,1,0:T(8,128)S(1)} %broadcast_in_dim.23.geo_ref.geo_in, f32[8,512,128]{2,1,0:T(8,128)S(1)} %get-tuple-element.18.f_ref.refs_4_.old_ref), custom_call_target="tpu_custom_call" | custom-call | flops 29360128 | bytes 14680064 | tf_op jit(solution)/shard_map/flux/pallas_call | solution.py:570
  19.3 0.0 collective-permute-done.4.refs_3_
  19.3 0.0 collective-permute-done.3.refs_2_
  19.4 0.0 collective-permute-done.2.refs_1_
  19.4 3.9 %add_target.2 = (f32[8,512,128]{2,1,0:T(8,128)S(1)}, f32[8,128]{1,0:T(8,128)S(1)}) custom-call(s32[6,8]{1,0:T(8,128)S(1)} %get-tuple-element.29.links_ref, f32[33,8,128]{2,1,0:T(8,128)S(1)} %broadcast_in_dim.23.geo_ref.geo_in, f32[8,128]{1,0:T(8,128)S(1)} %get-tuple-element.19.refs_0_, ...), custom_call_target="tpu_custom_call", output_to_operand_aliasing={{0}: (7, {})} | custom-call | flops 29360128 | bytes 14680064 | tf_op jit(solution)/shard_map/add_target/pallas_call | solution.py:685
  23.3 1.8 %collective-permute-done.far_in = f32[3,512,128]{2,1,0:T(8,128)S(1)} collective-permute-done((f32[3,512,128]{2,1,0:T(8,128)}, f32[3,512,128]{2,1,0:T(8,128)S(1)}, u32[]{:S(2)}, u32[]{:S(2)}) %collective-permute-start) | collective-permute-done | bytes 786464 | tf_op jit(solution)/shard_map/ppermute | solution.py:824
  25.1 0.0 collective-permute-done.1.near_in
  25.1 2.3 %edge.1 = (f32[8,512,128]{2,1,0:T(8,128)S(1)}, f32[3,512,128]{2,1,0:T(8,128)S(1)}, f32[3,512,128]{2,1,0:T(8,128)S(1)}) custom-call(f32[12,512,128]{2,1,0:T(8,128)S(1)} %geometry.1.pairs_ref, f32[3,512,128]{2,1,0:T(8,128)S(1)} %collective-permute-done.far_in, f32[3,512,128]{2,1,0:T(8,128)} %collective-permute-done.1.near_in, ...), custom_call_target="tpu_custom_call", output_to_operand_aliasing={{0}: (4, {})} | custom-call | flops 16777216 | bytes 8388608 | tf_op jit(solution)/shard_map/edge/pallas_call | solution.py:756
  27.4 3.6 %collective-permute-start.5 = (f32[3,512,128]{2,1,0:T(8,128)S(1)}, f32[3,512,128]{2,1,0:T(8,128)S(1)}, u32[]{:S(2)}, u32[]{:S(2)}) collective-permute-start(f32[3,512,128]{2,1,0:T(8,128)S(1)} %get-tuple-element.21), channel_id=1, source_target_pairs={{4,8},{12,16},{20,24},{8,4},{16,12},{24,20},{5,9},{13,17},{21,25},... | collective-permute-start | bytes 2359304 | tf_op jit(solution)/shard_map/ppermute | solution.py:824
  31.0 0.1 collective-permute-start.6
  31.1 1.7 %local_sums.1.refs_1_ = f32[8,128]{1,0:T(8,128)S(1)} custom-call(s32[6,8]{1,0:T(8,128)S(1)} %get-tuple-element.29.links_ref, f32[33,8,128]{2,1,0:T(8,128)S(1)} %broadcast_in_dim.23.geo_ref.geo_in, f32[8,512,128]{2,1,0:T(8,128)S(1)} %get-tuple-element.23.f_ref.refs_5_), custom_call_target="tpu_custom_call" | custom-call | flops 16777216 | bytes 8388608 | tf_op jit(solution)/shard_map/local_sums/pallas_call | solution.py:310
  32.8 3.6 %collective-permute-start.9 = (f32[8,128]{1,0:T(8,128)S(1)}, f32[8,128]{1,0:T(8,128)S(1)}, u32[]{:S(2)}, u32[]{:S(2)}) collective-permute-start(f32[8,128]{1,0:T(8,128)S(1)} %local_sums.1.refs_1_), channel_id=1, source_target_pairs={{0,3},{1,2},{2,1},{3,0},{4,7},{5,6},{6,5},{7,4},{8,11},{9,10},{10,... | collective-permute-start | bytes 12296 | tf_op jit(solution)/shard_map/ppermute | solution.py:458
  36.5 0.0 collective-permute-start.8
  36.5 0.8 %collective-permute-start.7 = (f32[8,128]{1,0:T(8,128)S(1)}, f32[8,128]{1,0:T(8,128)S(1)}, u32[]{:S(2)}, u32[]{:S(2)}) collective-permute-start(f32[8,128]{1,0:T(8,128)S(1)} %local_sums.1.refs_1_), channel_id=1, source_target_pairs={{0,1},{1,0},{2,3},{3,2},{4,5},{5,4},{6,7},{7,6},{8,9},{9,8},{10,11... | collective-permute-start | bytes 12296 | tf_op jit(solution)/shard_map/ppermute | solution.py:458
  37.3 2.9 %flux.3.refs_6_ = f32[8,512,128]{2,1,0:T(8,128)S(1)} custom-call(s32[6,8]{1,0:T(8,128)S(1)} %get-tuple-element.29.links_ref, f32[33,8,128]{2,1,0:T(8,128)S(1)} %broadcast_in_dim.23.geo_ref.geo_in, f32[8,512,128]{2,1,0:T(8,128)S(1)} %get-tuple-element.23.f_ref.refs_5_), custom_call_target="tpu_custom_call" | custom-call | flops 29360128 | bytes 14680064 | tf_op jit(solution)/shard_map/flux/pallas_call | solution.py:570
  40.1 0.0 collective-permute-done.9.refs_4_
  40.1 0.8 %collective-permute-done.8.refs_3_ = f32[8,128]{1,0:T(8,128)S(1)} collective-permute-done((f32[8,128]{1,0:T(8,128)S(1)}, f32[8,128]{1,0:T(8,128)S(1)}, u32[]{:S(2)}, u32[]{:S(2)}) %collective-permute-start.8) | collective-permute-done | bytes 4128 | tf_op jit(solution)/shard_map/ppermute | solution.py:458
  41.0 0.0 collective-permute-done.7.refs_2_
  41.0 4.5 %add_target.3 = (f32[8,512,128]{2,1,0:T(8,128)S(1)}, f32[8,128]{1,0:T(8,128)}) custom-call(s32[6,8]{1,0:T(8,128)S(1)} %get-tuple-element.29.links_ref, f32[33,8,128]{2,1,0:T(8,128)S(1)} %broadcast_in_dim.23.geo_ref.geo_in, f32[8,128]{1,0:T(8,128)S(1)} %get-tuple-element.24.refs_0_, f32[8,128]{1,0:T(8,128)S(1)} %local_sums.1.refs_1_, ...), custom_call_target="tpu_custom_call", output_to_operand_aliasing={{0}: (8, {})} | custom-call | flops 29360128 | bytes 14680064 | tf_op jit(solution)/shard_map/add_target/pallas_call | solution.py:685
  45.5 2.7 %collective-permute-done.5.far_ref = f32[3,512,128]{2,1,0:T(8,128)S(1)} collective-permute-done((f32[3,512,128]{2,1,0:T(8,128)S(1)}, f32[3,512,128]{2,1,0:T(8,128)S(1)}, u32[]{:S(2)}, u32[]{:S(2)}) %collective-permute-start.5) | collective-permute-done | bytes 786464 | tf_op jit(solution)/shard_map/ppermute | solution.py:824
  48.2 0.0 collective-permute-done.6.near_ref
  48.2 1.6 %last_edge.1 = (f32[4096,128]{1,0:T(8,128)}, f32[8,128]{1,0:T(8,128)S(1)}) custom-call(f32[33,8,128]{2,1,0:T(8,128)S(1)} %broadcast_in_dim.23.geo_ref.geo_in, f32[12,512,128]{2,1,0:T(8,128)S(1)} %geometry.1.pairs_ref, f32[3,512,128]{2,1,0:T(8,128)S(1)} %collective-permute-done.5.far_ref, f32[3,512,128]{2,1,0:T(8,128)S(1)} %collective-permute-done.6.near_ref, ...), custom_call_target="tpu_custom_call" | custom-call | flops 16777216 | bytes 8388608 | tf_op jit(solution)/shard_map/last_edge/pallas_call | solution.py:807
  49.9 1.6 %collective-permute-start.10 = (f32[8,128]{1,0:T(8,128)S(1)}, f32[8,128]{1,0:T(8,128)S(1)}, u32[]{:S(2)}, u32[]{:S(2)}) collective-permute-start(f32[8,128]{1,0:T(8,128)S(1)} %get-tuple-element.27), channel_id=1, source_target_pairs={{0,1},{1,0},{2,3},{3,2},{4,5},{5,4},{6,7},{7,6},{8,9},{9,8},{10,11... | collective-permute-start | bytes 12296 | tf_op jit(solution)/shard_map/ppermute | solution.py:466
  51.5 2.0 %collective-permute-done.10 = f32[8,128]{1,0:T(8,128)S(1)} collective-permute-done((f32[8,128]{1,0:T(8,128)S(1)}, f32[8,128]{1,0:T(8,128)S(1)}, u32[]{:S(2)}, u32[]{:S(2)}) %collective-permute-start.10) | collective-permute-done | bytes 4128 | tf_op jit(solution)/shard_map/ppermute | solution.py:466
  53.5 2.6 %collective-permute-start.11 = (f32[8,128]{1,0:T(8,128)S(1)}, f32[8,128]{1,0:T(8,128)S(1)}, u32[]{:S(2)}, u32[]{:S(2)}) collective-permute-start(f32[8,128]{1,0:T(8,128)S(1)} %add.7.refs_0_), channel_id=1, source_target_pairs={{0,2},{1,3},{2,0},{3,1},{4,6},{5,7},{6,4},{7,5},{8,10},{9,11},{10,... | collective-permute-start | bytes 12296 | tf_op jit(solution)/shard_map/ppermute | solution.py:467
  56.1 1.9 %collective-permute-done.11.refs_1_ = f32[8,128]{1,0:T(8,128)S(1)} collective-permute-done((f32[8,128]{1,0:T(8,128)S(1)}, f32[8,128]{1,0:T(8,128)S(1)}, u32[]{:S(2)}, u32[]{:S(2)}) %collective-permute-start.11) | collective-permute-done | bytes 4128 | tf_op jit(solution)/shard_map/ppermute | solution.py:467
  58.1 0.7 %macro.1 = f32[8,8]{1,0:T(8,128)} custom-call(f32[8,128]{1,0:T(8,128)S(1)} %add.7.refs_0_, f32[8,128]{1,0:T(8,128)S(1)} %collective-permute-done.11.refs_1_), custom_call_target="tpu_custom_call" | custom-call | tf_op jit(solution)/shard_map/macro/pallas_call | solution.py:504
  (7 shorter events, 0.0 us)
Async XLA Ops:
  0.6 6.1 %copy-start.2 = (f32[8]{0:T(128)S(1)}, f32[8]{0:T(128)}, u32[]{:S(2)}) copy-start(f32[8]{0:T(128)} %param.8) | copy-start | bytes 100
  0.6 6.2 %copy-start.3 = (f32[8]{0:T(128)S(1)}, f32[8]{0:T(128)}, u32[]{:S(2)}) copy-start(f32[8]{0:T(128)} %param.9) | copy-start | bytes 100
  0.7 6.3 %copy-start.1 = (s32[6,8]{1,0:T(8,128)S(1)}, s32[6,8]{1,0:T(8,128)}, u32[]{:S(2)}) copy-start(s32[6,8]{1,0:T(8,128)} %param.6) | copy-start | bytes 580
  0.7 6.4 %copy-start = (f32[3,6,8]{2,1,0:T(8,128)S(1)}, f32[3,6,8]{2,1,0:T(8,128)}, u32[]{:S(2)}) copy-start(f32[3,6,8]{2,1,0:T(8,128)} %param.7) | copy-start | bytes 1732
  3.2 21.9 %collective-permute-start = (f32[3,512,128]{2,1,0:T(8,128)}, f32[3,512,128]{2,1,0:T(8,128)S(1)}, u32[]{:S(2)}, u32[]{:S(2)}) collective-permute-start(f32[3,512,128]{2,1,0:T(8,128)} %get-tuple-element.15), channel_id=1, source_target_pairs={{4,8},{12,16},{20,24},{8,4},{16,12},{24,20},{5,9},{13,17},{21,25},... | collective-permute-start | bytes 2359304 | tf_op jit(solution)/shard_map/ppermute | solution.py:824
  6.0 19.2 %collective-permute-start.1 = (f32[3,512,128]{2,1,0:T(8,128)}, f32[3,512,128]{2,1,0:T(8,128)}, u32[]{:S(2)}, u32[]{:S(2)}) collective-permute-start(f32[3,512,128]{2,1,0:T(8,128)} %get-tuple-element.16), channel_id=1, source_target_pairs={{0,4},{8,12},{16,20},{24,28},{4,0},{12,8},{20,16},{28,24},{1,5},{9... | collective-permute-start | bytes 2359304 | tf_op jit(solution)/shard_map/ppermute | solution.py:824
  10.0 9.3 %collective-permute-start.4 = (f32[8,128]{1,0:T(8,128)S(1)}, f32[8,128]{1,0:T(8,128)S(1)}, u32[]{:S(2)}, u32[]{:S(2)}) collective-permute-start(f32[8,128]{1,0:T(8,128)S(1)} %get-tuple-element.19.refs_0_), channel_id=1, source_target_pairs={{0,3},{1,2},{2,1},{3,0},{4,7},{5,6},{6,5},{7,4},{8,11},{9,10},{10,... | collective-permute-start | bytes 12296 | tf_op jit(solution)/shard_map/ppermute | solution.py:458
  13.7 5.7 %collective-permute-start.3 = (f32[8,128]{1,0:T(8,128)S(1)}, f32[8,128]{1,0:T(8,128)S(1)}, u32[]{:S(2)}, u32[]{:S(2)}) collective-permute-start(f32[8,128]{1,0:T(8,128)S(1)} %get-tuple-element.19.refs_0_), channel_id=1, source_target_pairs={{0,2},{1,3},{2,0},{3,1},{4,6},{5,7},{6,4},{7,5},{8,10},{9,11},{10,... | collective-permute-start | bytes 12296 | tf_op jit(solution)/shard_map/ppermute | solution.py:458
  13.7 5.7 %collective-permute-start.2 = (f32[8,128]{1,0:T(8,128)S(1)}, f32[8,128]{1,0:T(8,128)S(1)}, u32[]{:S(2)}, u32[]{:S(2)}) collective-permute-start(f32[8,128]{1,0:T(8,128)S(1)} %get-tuple-element.19.refs_0_), channel_id=1, source_target_pairs={{0,1},{1,0},{2,3},{3,2},{4,5},{5,4},{6,7},{7,6},{8,9},{9,8},{10,11... | collective-permute-start | bytes 12296 | tf_op jit(solution)/shard_map/ppermute | solution.py:458
  27.4 20.9 %collective-permute-start.5 = (f32[3,512,128]{2,1,0:T(8,128)S(1)}, f32[3,512,128]{2,1,0:T(8,128)S(1)}, u32[]{:S(2)}, u32[]{:S(2)}) collective-permute-start(f32[3,512,128]{2,1,0:T(8,128)S(1)} %get-tuple-element.21), channel_id=1, source_target_pairs={{4,8},{12,16},{20,24},{8,4},{16,12},{24,20},{5,9},{13,17},{21,25},... | collective-permute-start | bytes 2359304 | tf_op jit(solution)/shard_map/ppermute | solution.py:824
  31.0 17.2 %collective-permute-start.6 = (f32[3,512,128]{2,1,0:T(8,128)S(1)}, f32[3,512,128]{2,1,0:T(8,128)S(1)}, u32[]{:S(2)}, u32[]{:S(2)}) collective-permute-start(f32[3,512,128]{2,1,0:T(8,128)S(1)} %get-tuple-element.22), channel_id=1, source_target_pairs={{0,4},{8,12},{16,20},{24,28},{4,0},{12,8},{20,16},{28,24},{1,5},{9... | collective-permute-start | bytes 2359304 | tf_op jit(solution)/shard_map/ppermute | solution.py:824
  32.8 7.3 %collective-permute-start.9 = (f32[8,128]{1,0:T(8,128)S(1)}, f32[8,128]{1,0:T(8,128)S(1)}, u32[]{:S(2)}, u32[]{:S(2)}) collective-permute-start(f32[8,128]{1,0:T(8,128)S(1)} %local_sums.1.refs_1_), channel_id=1, source_target_pairs={{0,3},{1,2},{2,1},{3,0},{4,7},{5,6},{6,5},{7,4},{8,11},{9,10},{10,... | collective-permute-start | bytes 12296 | tf_op jit(solution)/shard_map/ppermute | solution.py:458
  36.5 4.5 %collective-permute-start.8 = (f32[8,128]{1,0:T(8,128)S(1)}, f32[8,128]{1,0:T(8,128)S(1)}, u32[]{:S(2)}, u32[]{:S(2)}) collective-permute-start(f32[8,128]{1,0:T(8,128)S(1)} %local_sums.1.refs_1_), channel_id=1, source_target_pairs={{0,2},{1,3},{2,0},{3,1},{4,6},{5,7},{6,4},{7,5},{8,10},{9,11},{10,... | collective-permute-start | bytes 12296 | tf_op jit(solution)/shard_map/ppermute | solution.py:458
  36.5 4.5 %collective-permute-start.7 = (f32[8,128]{1,0:T(8,128)S(1)}, f32[8,128]{1,0:T(8,128)S(1)}, u32[]{:S(2)}, u32[]{:S(2)}) collective-permute-start(f32[8,128]{1,0:T(8,128)S(1)} %local_sums.1.refs_1_), channel_id=1, source_target_pairs={{0,1},{1,0},{2,3},{3,2},{4,5},{5,4},{6,7},{7,6},{8,9},{9,8},{10,11... | collective-permute-start | bytes 12296 | tf_op jit(solution)/shard_map/ppermute | solution.py:458
  49.9 3.7 %collective-permute-start.10 = (f32[8,128]{1,0:T(8,128)S(1)}, f32[8,128]{1,0:T(8,128)S(1)}, u32[]{:S(2)}, u32[]{:S(2)}) collective-permute-start(f32[8,128]{1,0:T(8,128)S(1)} %get-tuple-element.27), channel_id=1, source_target_pairs={{0,1},{1,0},{2,3},{3,2},{4,5},{5,4},{6,7},{7,6},{8,9},{9,8},{10,11... | collective-permute-start | bytes 12296 | tf_op jit(solution)/shard_map/ppermute | solution.py:466
  53.5 4.5 %collective-permute-start.11 = (f32[8,128]{1,0:T(8,128)S(1)}, f32[8,128]{1,0:T(8,128)S(1)}, u32[]{:S(2)}, u32[]{:S(2)}) collective-permute-start(f32[8,128]{1,0:T(8,128)S(1)} %add.7.refs_0_), channel_id=1, source_target_pairs={{0,2},{1,3},{2,0},{3,1},{4,6},{5,7},{6,4},{7,5},{8,10},{9,11},{10,... | collective-permute-start | bytes 12296 | tf_op jit(solution)/shard_map/ppermute | solution.py:467

commit v10 on v9

--- a/solution.py
+++ b/solution.py
@@ -459,16 +459,14 @@
     return [tile, *others]
 
 
-def doubling_sums(tile):
+def exchanged_sums(tile):
     size = lax.axis_size("vel")
-    if size != 4:
-        return gather_sums(tile)
-    pair = tile + lax.ppermute(tile, "vel", [(i, i ^ 1) for i in range(size)])
-    return [pair, lax.ppermute(pair, "vel", [(i, i ^ 2) for i in range(size)])]
+    parts = lax.all_to_all(jnp.broadcast_to(tile, (size, SUB, LANES)), "vel", 0, 0)
+    return [parts]
 
 
 def add_tiles(refs):
-    tiles = [r[...] for r in refs]
+    tiles = [r[...] for r in refs] if len(refs[0].shape) == 2 else [refs[0][i] for i in range(refs[0].shape[0])]
     while len(tiles) > 1:
         tiles = [tiles[i] + tiles[i + 1] for i in range(0, len(tiles), 2)]
     return tiles[0]
@@ -858,7 +856,7 @@
     part = flux(links, geo, f)
     part, _ = add_target(links, geo, absorbed, tiles, f, part)
     native, sums = last_edge(geo, pairs, far, near, f, part)
-    macro_quantities = macro(doubling_sums(sums))
+    macro_quantities = macro(exchanged_sums(sums))
     evolved = native.reshape(rows, cells, LANES).transpose(1, 0, 2).reshape(cells, points)
     return evolved, macro_quantities
 

time: 59 us -> 61.4 us (1.041)
  blocking collectives: 0 us -> 10.3 us
  starting transfers between devices: 20.4 us -> 16.1 us
  waiting for transfers between devices: 9.36 us -> 5.62 us
    all_to_all x0 -> x1, blocking collectives: none -> 10.3 us  [exchanged_sums(): lax.all_to_all(jnp.broadcast_to(tile, (size, SUB, LANES)), 'vel', 0, 0)]
    ppermute x2 -> x0, starting transfers between devices: 4.23 us -> none  [the longest x1 2.59 us: doubling_sums(): return [pair, lax.ppermute(pair, 'vel', [(i, i ^ 2) for i in range(size)])]]
    ppermute x2 -> x0, waiting for transfers between devices: 3.95 us -> none  [the longest x1 2.03 us: doubling_sums(): pair = tile + lax.ppermute(tile, 'vel', [(i, i ^ 1) for i in range(size)])]
  transfers between devices with their start and end apart: 12 -> 10, of which waited for: 5 -> 3; matrix products, arithmetic and copies ran while one was open for 1% -> 1% of each run, Pallas kernels for 35% -> 33%
where the time goes in v10:
time: 61.4 us; the launch traced here: 60.8 us
  Pallas kernels  27.3 us (44%)
  starting transfers between devices  16.1 us (26%)
  blocking collectives  10.3 us (17%)
  waiting for transfers between devices  5.62 us (9%)
  between operations  0.8 us (1%)
  local copies, waits for them, and re-layouts  0.69 us (1%)
    all_to_all x1, blocking collectives, exchanged_sums(): lax.all_to_all(jnp.broadcast_to(tile, (size, SUB, LANES)), 'vel', 0, 0)  10.3 us
    ppermute x6, starting transfers between devices, gather_sums(): lax.ppermute(tile, 'vel', [(i, i ^ s) for i in range(size)])  8.84 us
    pallas_call x2, Pallas kernels, add_target(): pl.pallas_call(kernel, in_specs=[spec(pltpu.SMEM)] + [vmem] * (len(given)...  8.2 us
    ppermute x4, starting transfers between devices, exchange(): out.append(lax.ppermute(x, 'space', pairs + [(j, i) for i, j in pairs]))  7.3 us
    pallas_call x2, Pallas kernels, flux(): pl.pallas_call(flux_kernel, in_specs=[spec(pltpu.SMEM), spec(pltpu.VMEM),...  6.21 us
    ppermute x4, waiting for transfers between devices, exchange(): out.append(lax.ppermute(x, 'space', pairs + [(j, i) for i, j in pairs]))  5.01 us
    pallas_call x1, Pallas kernels, first_rows(): pl.pallas_call(first_rows_kernel, in_specs=[spec(pltpu.HBM)], out_specs=[...  2.48 us
    pallas_call x1, Pallas kernels, first_sums(): pl.pallas_call(first_sums_kernel, in_specs=[spec(pltpu.SMEM), spec(pltpu....  2.45 us
  transfers between devices with their start and end apart: 10, of which 3 were waited for; matrix products, arithmetic and copies ran while one was open for 1% of the time, Pallas kernels for 33%

profile of v10, /device:TPU:4, one launch (start us, length us, event | category | flops | bytes accessed | tf_op | source)
XLA Modules:
  0.0 60.8 jit_solution(16926737335530551539)
XLA Ops:
  0.6 0.0 copy-start.2
  0.6 0.0 copy-start.3
  0.7 0.0 copy-start.1
  0.7 0.0 copy-start
  0.7 2.5 %first_rows.1 = (f32[4096,128]{1,0:T(8,128)S(1)}, f32[3,512,128]{2,1,0:T(8,128)}, f32[3,512,128]{2,1,0:T(8,128)}) custom-call(f32[4096,128]{1,0:T(8,128)} %bitcast.12), custom_call_target="tpu_custom_call" | custom-call | flops 16777216 | bytes 8388608 | tf_op jit(solution)/shard_map/first_rows/pallas_call | solution.py:390
  3.2 2.8 %collective-permute-start = (f32[3,512,128]{2,1,0:T(8,128)}, f32[3,512,128]{2,1,0:T(8,128)S(1)}, u32[]{:S(2)}, u32[]{:S(2)}) collective-permute-start(f32[3,512,128]{2,1,0:T(8,128)} %get-tuple-element.15), channel_id=1, source_target_pairs={{4,8},{12,16},{20,24},{8,4},{16,12},{24,20},{5,9},{13,17},{21,25},... | collective-permute-start | bytes 2359304 | tf_op jit(solution)/shard_map/ppermute | solution.py:822
  5.9 0.8 %collective-permute-start.1 = (f32[3,512,128]{2,1,0:T(8,128)}, f32[3,512,128]{2,1,0:T(8,128)}, u32[]{:S(2)}, u32[]{:S(2)}) collective-permute-start(f32[3,512,128]{2,1,0:T(8,128)} %get-tuple-element.16), channel_id=1, source_target_pairs={{0,4},{8,12},{16,20},{24,28},{4,0},{12,8},{20,16},{28,24},{1,5},{9... | collective-permute-start | bytes 2359304 | tf_op jit(solution)/shard_map/ppermute | solution.py:822
  6.7 0.0 copy-done.2
  6.7 0.1 copy.11
  6.8 0.0 copy-done.3
  6.8 0.1 copy.12
  6.9 0.0 copy-done.1
  6.9 0.1 copy.14
  7.0 0.1 copy.13
  7.1 0.0 copy-done
  7.1 0.1 copy.16
  7.2 0.1 concatenate.3
  7.3 0.1 copy.15
  7.3 0.1 broadcast_in_dim.26.geo_ref.geo_in
  7.4 2.4 %first_sums.1 = (f32[8,512,128]{2,1,0:T(8,128)S(1)}, f32[8,128]{1,0:T(8,128)S(1)}) custom-call(s32[6,8]{1,0:T(8,128)S(1)} %get-tuple-element.29.links_ref, f32[33,8,128]{2,1,0:T(8,128)S(1)} %broadcast_in_dim.26.geo_ref.geo_in, f32[4096,128]{1,0:T(8,128)S(1)} %get-tuple-element.17.native_ref), custom_call_target="tpu_custom_call" | custom-call | flops 20971520 | bytes 10485760 | tf_op jit(solution)/shard_map/first_sums/pallas_call | solution.py:328
  9.9 3.7 %collective-permute-start.4 = (f32[8,128]{1,0:T(8,128)S(1)}, f32[8,128]{1,0:T(8,128)S(1)}, u32[]{:S(2)}, u32[]{:S(2)}) collective-permute-start(f32[8,128]{1,0:T(8,128)S(1)} %get-tuple-element.19.refs_0_), channel_id=1, source_target_pairs={{0,3},{1,2},{2,1},{3,0},{4,7},{5,6},{6,5},{7,4},{8,11},{9,10},{10,... | collective-permute-start | bytes 12296 | tf_op jit(solution)/shard_map/ppermute | solution.py:458
  13.5 0.0 collective-permute-start.3
  13.5 0.8 %collective-permute-start.2 = (f32[8,128]{1,0:T(8,128)S(1)}, f32[8,128]{1,0:T(8,128)S(1)}, u32[]{:S(2)}, u32[]{:S(2)}) collective-permute-start(f32[8,128]{1,0:T(8,128)S(1)} %get-tuple-element.19.refs_0_), channel_id=1, source_target_pairs={{0,1},{1,0},{2,3},{3,2},{4,5},{5,4},{6,7},{7,6},{8,9},{9,8},{10,11... | collective-permute-start | bytes 12296 | tf_op jit(solution)/shard_map/ppermute | solution.py:458
  14.3 1.7 %geometry.1.pairs_ref = f32[12,512,128]{2,1,0:T(8,128)S(1)} custom-call(s32[6,8]{1,0:T(8,128)S(1)} %get-tuple-element.29.links_ref, f32[33,8,128]{2,1,0:T(8,128)S(1)} %broadcast_in_dim.26.geo_ref.geo_in), custom_call_target="tpu_custom_call" | custom-call | flops 16777216 | bytes 8388608 | tf_op jit(solution)/shard_map/geometry/pallas_call | solution.py:442
  16.0 3.1 %flux.2.refs_5_ = f32[8,512,128]{2,1,0:T(8,128)S(1)} custom-call(s32[6,8]{1,0:T(8,128)S(1)} %get-tuple-element.29.links_ref, f32[33,8,128]{2,1,0:T(8,128)S(1)} %broadcast_in_dim.26.geo_ref.geo_in, f32[8,512,128]{2,1,0:T(8,128)S(1)} %get-tuple-element.18.f_ref.refs_4_.old_ref), custom_call_target="tpu_custom_call" | custom-call | flops 29360128 | bytes 14680064 | tf_op jit(solution)/shard_map/flux/pallas_call | solution.py:568
  19.2 0.0 collective-permute-done.4.refs_3_
  19.2 0.0 collective-permute-done.3.refs_2_
  19.2 0.0 collective-permute-done.2.refs_1_
  19.2 3.8 %add_target.2 = (f32[8,512,128]{2,1,0:T(8,128)S(1)}, f32[8,128]{1,0:T(8,128)S(1)}) custom-call(s32[6,8]{1,0:T(8,128)S(1)} %get-tuple-element.29.links_ref, f32[33,8,128]{2,1,0:T(8,128)S(1)} %broadcast_in_dim.26.geo_ref.geo_in, f32[8,128]{1,0:T(8,128)S(1)} %get-tuple-element.19.refs_0_, ...), custom_call_target="tpu_custom_call", output_to_operand_aliasing={{0}: (7, {})} | custom-call | flops 29360128 | bytes 14680064 | tf_op jit(solution)/shard_map/add_target/pallas_call | solution.py:683
  23.0 2.1 %collective-permute-done.far_in = f32[3,512,128]{2,1,0:T(8,128)S(1)} collective-permute-done((f32[3,512,128]{2,1,0:T(8,128)}, f32[3,512,128]{2,1,0:T(8,128)S(1)}, u32[]{:S(2)}, u32[]{:S(2)}) %collective-permute-start) | collective-permute-done | bytes 786464 | tf_op jit(solution)/shard_map/ppermute | solution.py:822
  25.1 0.0 collective-permute-done.1.near_in
  25.1 2.3 %edge.1 = (f32[8,512,128]{2,1,0:T(8,128)S(1)}, f32[3,512,128]{2,1,0:T(8,128)S(1)}, f32[3,512,128]{2,1,0:T(8,128)S(1)}) custom-call(f32[12,512,128]{2,1,0:T(8,128)S(1)} %geometry.1.pairs_ref, f32[3,512,128]{2,1,0:T(8,128)S(1)} %collective-permute-done.far_in, f32[3,512,128]{2,1,0:T(8,128)} %collective-permute-done.1.near_in, ...), custom_call_target="tpu_custom_call", output_to_operand_aliasing={{0}: (4, {})} | custom-call | flops 16777216 | bytes 8388608 | tf_op jit(solution)/shard_map/edge/pallas_call | solution.py:754
  27.4 3.6 %collective-permute-start.5 = (f32[3,512,128]{2,1,0:T(8,128)S(1)}, f32[3,512,128]{2,1,0:T(8,128)S(1)}, u32[]{:S(2)}, u32[]{:S(2)}) collective-permute-start(f32[3,512,128]{2,1,0:T(8,128)S(1)} %get-tuple-element.21), channel_id=1, source_target_pairs={{4,8},{12,16},{20,24},{8,4},{16,12},{24,20},{5,9},{13,17},{21,25},... | collective-permute-start | bytes 2359304 | tf_op jit(solution)/shard_map/ppermute | solution.py:822
  31.0 0.1 collective-permute-start.6
  31.1 1.7 %local_sums.1.refs_1_ = f32[8,128]{1,0:T(8,128)S(1)} custom-call(s32[6,8]{1,0:T(8,128)S(1)} %get-tuple-element.29.links_ref, f32[33,8,128]{2,1,0:T(8,128)S(1)} %broadcast_in_dim.26.geo_ref.geo_in, f32[8,512,128]{2,1,0:T(8,128)S(1)} %get-tuple-element.23.f_ref.refs_5_), custom_call_target="tpu_custom_call" | custom-call | flops 16777216 | bytes 8388608 | tf_op jit(solution)/shard_map/local_sums/pallas_call | solution.py:310
  32.8 3.6 %collective-permute-start.9 = (f32[8,128]{1,0:T(8,128)S(1)}, f32[8,128]{1,0:T(8,128)S(1)}, u32[]{:S(2)}, u32[]{:S(2)}) collective-permute-start(f32[8,128]{1,0:T(8,128)S(1)} %local_sums.1.refs_1_), channel_id=1, source_target_pairs={{0,3},{1,2},{2,1},{3,0},{4,7},{5,6},{6,5},{7,4},{8,11},{9,10},{10,... | collective-permute-start | bytes 12296 | tf_op jit(solution)/shard_map/ppermute | solution.py:458
  36.4 0.0 collective-permute-start.8
  36.4 0.8 %collective-permute-start.7 = (f32[8,128]{1,0:T(8,128)S(1)}, f32[8,128]{1,0:T(8,128)S(1)}, u32[]{:S(2)}, u32[]{:S(2)}) collective-permute-start(f32[8,128]{1,0:T(8,128)S(1)} %local_sums.1.refs_1_), channel_id=1, source_target_pairs={{0,1},{1,0},{2,3},{3,2},{4,5},{5,4},{6,7},{7,6},{8,9},{9,8},{10,11... | collective-permute-start | bytes 12296 | tf_op jit(solution)/shard_map/ppermute | solution.py:458
  37.2 3.1 %flux.3.refs_6_ = f32[8,512,128]{2,1,0:T(8,128)S(1)} custom-call(s32[6,8]{1,0:T(8,128)S(1)} %get-tuple-element.29.links_ref, f32[33,8,128]{2,1,0:T(8,128)S(1)} %broadcast_in_dim.26.geo_ref.geo_in, f32[8,512,128]{2,1,0:T(8,128)S(1)} %get-tuple-element.23.f_ref.refs_5_), custom_call_target="tpu_custom_call" | custom-call | flops 29360128 | bytes 14680064 | tf_op jit(solution)/shard_map/flux/pallas_call | solution.py:568
  40.3 0.0 collective-permute-done.9.refs_4_
  40.3 0.6 collective-permute-done.8.refs_3_
  40.9 0.0 collective-permute-done.7.refs_2_
  40.9 4.4 %add_target.3 = (f32[8,512,128]{2,1,0:T(8,128)S(1)}, f32[8,128]{1,0:T(8,128)}) custom-call(s32[6,8]{1,0:T(8,128)S(1)} %get-tuple-element.29.links_ref, f32[33,8,128]{2,1,0:T(8,128)S(1)} %broadcast_in_dim.26.geo_ref.geo_in, f32[8,128]{1,0:T(8,128)S(1)} %get-tuple-element.24.refs_0_, f32[8,128]{1,0:T(8,128)S(1)} %local_sums.1.refs_1_, ...), custom_call_target="tpu_custom_call", output_to_operand_aliasing={{0}: (8, {})} | custom-call | flops 29360128 | bytes 14680064 | tf_op jit(solution)/shard_map/add_target/pallas_call | solution.py:683
  45.3 2.9 %collective-permute-done.5.far_ref = f32[3,512,128]{2,1,0:T(8,128)S(1)} collective-permute-done((f32[3,512,128]{2,1,0:T(8,128)S(1)}, f32[3,512,128]{2,1,0:T(8,128)S(1)}, u32[]{:S(2)}, u32[]{:S(2)}) %collective-permute-start.5) | collective-permute-done | bytes 786464 | tf_op jit(solution)/shard_map/ppermute | solution.py:822
  48.2 0.0 collective-permute-done.6.near_ref
  48.2 1.6 %last_edge.1 = (f32[4096,128]{1,0:T(8,128)}, f32[8,128]{1,0:T(8,128)S(1)}) custom-call(f32[33,8,128]{2,1,0:T(8,128)S(1)} %broadcast_in_dim.26.geo_ref.geo_in, f32[12,512,128]{2,1,0:T(8,128)S(1)} %geometry.1.pairs_ref, f32[3,512,128]{2,1,0:T(8,128)S(1)} %collective-permute-done.5.far_ref, f32[3,512,128]{2,1,0:T(8,128)S(1)} %collective-permute-done.6.near_ref, ...), custom_call_target="tpu_custom_call" | custom-call | flops 16777216 | bytes 8388608 | tf_op jit(solution)/shard_map/last_edge/pallas_call | solution.py:805
  49.9 10.3 %all_to_all.5.refs_0_ = f32[4,8,128]{2,1,0:T(8,128)S(1)} all-to-all(f32[4,8,128]{2,1,0:T(8,128)S(1)} %broadcast_in_dim.27), channel_id=1, replica_groups=mesh['space'=8,'vel'=4] {'vel'}, dimensions={0} | all-to-all | bytes 32768 | tf_op jit(solution)/shard_map/all_to_all | solution.py:464
  60.1 0.7 %macro.1 = f32[8,8]{1,0:T(8,128)} custom-call(f32[4,8,128]{2,1,0:T(8,128)S(1)} %all_to_all.5.refs_0_), custom_call_target="tpu_custom_call" | custom-call | tf_op jit(solution)/shard_map/macro/pallas_call | solution.py:502
  (4 shorter events, 0.0 us)
Async XLA Ops:
  0.6 6.1 %copy-start.2 = (f32[8]{0:T(128)S(1)}, f32[8]{0:T(128)}, u32[]{:S(2)}) copy-start(f32[8]{0:T(128)} %param.8) | copy-start | bytes 100
  0.6 6.2 %copy-start.3 = (f32[8]{0:T(128)S(1)}, f32[8]{0:T(128)}, u32[]{:S(2)}) copy-start(f32[8]{0:T(128)} %param.9) | copy-start | bytes 100
  0.7 6.3 %copy-start.1 = (s32[6,8]{1,0:T(8,128)S(1)}, s32[6,8]{1,0:T(8,128)}, u32[]{:S(2)}) copy-start(s32[6,8]{1,0:T(8,128)} %param.6) | copy-start | bytes 580
  0.7 6.4 %copy-start = (f32[3,6,8]{2,1,0:T(8,128)S(1)}, f32[3,6,8]{2,1,0:T(8,128)}, u32[]{:S(2)}) copy-start(f32[3,6,8]{2,1,0:T(8,128)} %param.7) | copy-start | bytes 1732
  3.2 21.9 %collective-permute-start = (f32[3,512,128]{2,1,0:T(8,128)}, f32[3,512,128]{2,1,0:T(8,128)S(1)}, u32[]{:S(2)}, u32[]{:S(2)}) collective-permute-start(f32[3,512,128]{2,1,0:T(8,128)} %get-tuple-element.15), channel_id=1, source_target_pairs={{4,8},{12,16},{20,24},{8,4},{16,12},{24,20},{5,9},{13,17},{21,25},... | collective-permute-start | bytes 2359304 | tf_op jit(solution)/shard_map/ppermute | solution.py:822
  5.9 19.2 %collective-permute-start.1 = (f32[3,512,128]{2,1,0:T(8,128)}, f32[3,512,128]{2,1,0:T(8,128)}, u32[]{:S(2)}, u32[]{:S(2)}) collective-permute-start(f32[3,512,128]{2,1,0:T(8,128)} %get-tuple-element.16), channel_id=1, source_target_pairs={{0,4},{8,12},{16,20},{24,28},{4,0},{12,8},{20,16},{28,24},{1,5},{9... | collective-permute-start | bytes 2359304 | tf_op jit(solution)/shard_map/ppermute | solution.py:822
  9.9 9.3 %collective-permute-start.4 = (f32[8,128]{1,0:T(8,128)S(1)}, f32[8,128]{1,0:T(8,128)S(1)}, u32[]{:S(2)}, u32[]{:S(2)}) collective-permute-start(f32[8,128]{1,0:T(8,128)S(1)} %get-tuple-element.19.refs_0_), channel_id=1, source_target_pairs={{0,3},{1,2},{2,1},{3,0},{4,7},{5,6},{6,5},{7,4},{8,11},{9,10},{10,... | collective-permute-start | bytes 12296 | tf_op jit(solution)/shard_map/ppermute | solution.py:458
  13.5 5.6 %collective-permute-start.3 = (f32[8,128]{1,0:T(8,128)S(1)}, f32[8,128]{1,0:T(8,128)S(1)}, u32[]{:S(2)}, u32[]{:S(2)}) collective-permute-start(f32[8,128]{1,0:T(8,128)S(1)} %get-tuple-element.19.refs_0_), channel_id=1, source_target_pairs={{0,2},{1,3},{2,0},{3,1},{4,6},{5,7},{6,4},{7,5},{8,10},{9,11},{10,... | collective-permute-start | bytes 12296 | tf_op jit(solution)/shard_map/ppermute | solution.py:458
  13.5 5.6 %collective-permute-start.2 = (f32[8,128]{1,0:T(8,128)S(1)}, f32[8,128]{1,0:T(8,128)S(1)}, u32[]{:S(2)}, u32[]{:S(2)}) collective-permute-start(f32[8,128]{1,0:T(8,128)S(1)} %get-tuple-element.19.refs_0_), channel_id=1, source_target_pairs={{0,1},{1,0},{2,3},{3,2},{4,5},{5,4},{6,7},{7,6},{8,9},{9,8},{10,11... | collective-permute-start | bytes 12296 | tf_op jit(solution)/shard_map/ppermute | solution.py:458
  27.4 20.9 %collective-permute-start.5 = (f32[3,512,128]{2,1,0:T(8,128)S(1)}, f32[3,512,128]{2,1,0:T(8,128)S(1)}, u32[]{:S(2)}, u32[]{:S(2)}) collective-permute-start(f32[3,512,128]{2,1,0:T(8,128)S(1)} %get-tuple-element.21), channel_id=1, source_target_pairs={{4,8},{12,16},{20,24},{8,4},{16,12},{24,20},{5,9},{13,17},{21,25},... | collective-permute-start | bytes 2359304 | tf_op jit(solution)/shard_map/ppermute | solution.py:822
  31.0 17.2 %collective-permute-start.6 = (f32[3,512,128]{2,1,0:T(8,128)S(1)}, f32[3,512,128]{2,1,0:T(8,128)S(1)}, u32[]{:S(2)}, u32[]{:S(2)}) collective-permute-start(f32[3,512,128]{2,1,0:T(8,128)S(1)} %get-tuple-element.22), channel_id=1, source_target_pairs={{0,4},{8,12},{16,20},{24,28},{4,0},{12,8},{20,16},{28,24},{1,5},{9... | collective-permute-start | bytes 2359304 | tf_op jit(solution)/shard_map/ppermute | solution.py:822
  32.8 7.5 %collective-permute-start.9 = (f32[8,128]{1,0:T(8,128)S(1)}, f32[8,128]{1,0:T(8,128)S(1)}, u32[]{:S(2)}, u32[]{:S(2)}) collective-permute-start(f32[8,128]{1,0:T(8,128)S(1)} %local_sums.1.refs_1_), channel_id=1, source_target_pairs={{0,3},{1,2},{2,1},{3,0},{4,7},{5,6},{6,5},{7,4},{8,11},{9,10},{10,... | collective-permute-start | bytes 12296 | tf_op jit(solution)/shard_map/ppermute | solution.py:458
  36.4 4.5 %collective-permute-start.8 = (f32[8,128]{1,0:T(8,128)S(1)}, f32[8,128]{1,0:T(8,128)S(1)}, u32[]{:S(2)}, u32[]{:S(2)}) collective-permute-start(f32[8,128]{1,0:T(8,128)S(1)} %local_sums.1.refs_1_), channel_id=1, source_target_pairs={{0,2},{1,3},{2,0},{3,1},{4,6},{5,7},{6,4},{7,5},{8,10},{9,11},{10,... | collective-permute-start | bytes 12296 | tf_op jit(solution)/shard_map/ppermute | solution.py:458
  36.4 4.5 %collective-permute-start.7 = (f32[8,128]{1,0:T(8,128)S(1)}, f32[8,128]{1,0:T(8,128)S(1)}, u32[]{:S(2)}, u32[]{:S(2)}) collective-permute-start(f32[8,128]{1,0:T(8,128)S(1)} %local_sums.1.refs_1_), channel_id=1, source_target_pairs={{0,1},{1,0},{2,3},{3,2},{4,5},{5,4},{6,7},{7,6},{8,9},{9,8},{10,11... | collective-permute-start | bytes 12296 | tf_op jit(solution)/shard_map/ppermute | solution.py:458

commit v11 on v9

--- a/solution.py
+++ b/solution.py
@@ -699,75 +699,64 @@
     )(*given)
 
 
-def halo_terms(pairs_ref, before_ref, after_ref, f_ref, at):
-    low, high = [None] * REACH, [None] * REACH
-    rows = [before_ref[r, at, :] for r in range(REACH)]
-    own = [f_ref[g, at, :] for g in range(REACH)]
-    for p, (g, r) in enumerate(BEFORE_PAIRS):
-        term = pairs_ref[p, at, :] * (rows[r] - own[g])
-        low[g] = term if low[g] is None else low[g] + term
-    rows = [after_ref[r, at, :] for r in range(REACH)]
-    own = [f_ref[SUB - REACH + e, at, :] for e in range(REACH)]
-    p = len(BEFORE_PAIRS)
-    for e in range(REACH):
-        for r in range(e + 1):
-            term = pairs_ref[p, at, :] * (rows[r] - own[e])
-            high[e] = term if high[e] is None else high[e] + term
-            p += 1
-    return low, high
-
-
-def by_side(far_ref, near_ref, run):
+def side_terms(high, pairs_ref, halo_ref, f_ref, at):
+    terms = [None] * REACH
+    rows = [halo_ref[r, at, :] for r in range(REACH)]
+    first = SUB - REACH if high else 0
+    own = [f_ref[first + e, at, :] for e in range(REACH)]
+    count = len(BEFORE_PAIRS)
+    pairs = [(e, r) for e in range(REACH) for r in range(e + 1)] if high else BEFORE_PAIRS
+    for p, (e, r) in enumerate(pairs):
+        term = pairs_ref[p + count if high else p, at, :] * (rows[r] - own[e])
+        terms[e] = term if terms[e] is None else terms[e] + term
+    return first, terms
+
+
+def for_side(far, run):
     odd = is_odd()
 
     @pl.when(odd)
     def _():
-        run(near_ref, far_ref)
+        run(far)
 
     @pl.when(jnp.logical_not(odd))
     def _():
-        run(far_ref, near_ref)
-
-
-def edge_kernel(pairs_ref, far_in, near_in, old_ref, part_ref, f_ref, far_out, near_out):
-    def run(before_ref, after_ref):
-        down_out, up_out = (near_out, far_out) if after_ref is far_in else (far_out, near_out)
-
+        run(not far)
+
+
+def edge_kernel(far, pairs_ref, halo_ref, old_ref, part_ref, f_ref, *rows_refs):
+    def run(high):
         def group(j, _):
             at = at_rows(j * SUB)
-            low, high = halo_terms(pairs_ref, before_ref, after_ref, old_ref, at)
-            for g in range(REACH):
-                x = part_ref[g, at, :] + low[g]
-                down_out[g, at, :] = x
-                f_ref[g, at, :] = x
-                e = SUB - REACH + g
-                x = part_ref[e, at, :] + high[g]
-                up_out[g, at, :] = x
-                f_ref[e, at, :] = x
+            first, terms = side_terms(high, pairs_ref, halo_ref, old_ref, at)
+            for e in range(REACH):
+                x = part_ref[first + e, at, :] + terms[e]
+                f_ref[first + e, at, :] = x
+                for rows_ref in rows_refs:
+                    rows_ref[e, at, :] = x
             return 0
 
-        lax.fori_loop(0, part_ref.shape[1] // SUB, group, 0, unroll=4)
-
-    by_side(far_in, near_in, run)
-
-
-def edge(pairs, far, near, old, part):
+        groups = part_ref.shape[1] // SUB
+        lax.fori_loop(0, groups, group, 0, unroll=unroll(groups, 8))
+
+    for_side(far, run)
+
+
+def edge(far, pairs, halo, old, part, keep_rows):
     rows = part.shape[1]
     return pl.pallas_call(
-        edge_kernel,
-        in_specs=[spec(pltpu.VMEM)] * 5,
-        out_specs=[spec(pltpu.VMEM)] * 3,
-        out_shape=[array(SUB, rows, LANES), array(REACH, rows, LANES), array(REACH, rows, LANES)],
-        input_output_aliases={4: 0},
+        functools.partial(edge_kernel, far),
+        in_specs=[spec(pltpu.VMEM)] * 4,
+        out_specs=[spec(pltpu.VMEM)] * (2 if keep_rows else 1),
+        out_shape=[array(SUB, rows, LANES), array(REACH, rows, LANES)][: 2 if keep_rows else 1],
+        input_output_aliases={3: 0},
         compiler_params=params(),
-        cost_estimate=traffic(rows, 4),
-        name="edge",
-    )(pairs, far, near, old, part)
-
-
-def last_edge_kernel(
-    geo_ref, pairs_ref, far_ref, near_ref, f_ref, part_ref, out_hbm, sums_out, native_ref, sems
-):
+        cost_estimate=traffic(rows, 2),
+        name="far_edge" if far else "near_edge",
+    )(pairs, halo, old, part)
+
+
+def last_edge_kernel(geo_ref, pairs_ref, far_ref, f_ref, part_ref, out_hbm, sums_out, native_ref, sems):
     rows = part_ref.shape[1]
     planes = rows // CHUNKS
     part = rows // SUB // LAST_PARTS
@@ -776,23 +765,23 @@
         at = pl.ds(i * part * SUB * SUB, part * SUB * SUB)
         return pltpu.make_async_copy(native_ref.at[at], out_hbm.at[at], sems.at[i])
 
-    def run(before_ref, after_ref):
+    def run(high):
         for i in range(LAST_PARTS):
 
             def group(j, _):
                 at = at_rows(j * SUB)
-                low, high = halo_terms(pairs_ref, before_ref, after_ref, f_ref, at)
-                terms = low + [None] * (SUB - 2 * REACH) + high
+                first, terms = side_terms(high, pairs_ref, far_ref, f_ref, at)
                 for g in range(SUB):
                     x = part_ref[g, at, :]
-                    where = (pl.ds(j * SUB * SUB + g, SUB, stride=SUB), slice(None))
-                    native_ref[where] = x if terms[g] is None else x + terms[g]
+                    if 0 <= g - first < REACH:
+                        x = x + terms[g - first]
+                    native_ref[pl.ds(j * SUB * SUB + g, SUB, stride=SUB), :] = x
                 return 0
 
-            lax.fori_loop(i * part, (i + 1) * part, group, 0, unroll=2)
+            lax.fori_loop(i * part, (i + 1) * part, group, 0, unroll=unroll(part, 4))
             copy(i).start()
 
-    by_side(far_ref, near_ref, run)
+    for_side(True, run)
     y = native_polynomial_sums(native_ref, planes)
     sums_out[...] = pack_sums(finish_polynomials(y, geo_ref[FIRST], planes), 0)
     for i in range(LAST_PARTS):
@@ -802,27 +791,23 @@
 LAST_PARTS = 4
 
 
-def last_edge(geo, pairs, far, near, f, part):
+def last_edge(geo, pairs, far, f, part):
     native = (SUB * part.shape[1], LANES)
     return pl.pallas_call(
         last_edge_kernel,
-        in_specs=[spec(pltpu.VMEM)] * 6,
+        in_specs=[spec(pltpu.VMEM)] * 5,
         out_specs=[spec(pltpu.HBM), spec(pltpu.VMEM)],
         out_shape=[array(*native), array(SUB, LANES)],
         scratch_shapes=[pltpu.VMEM(native, F32), pltpu.SemaphoreType.DMA((LAST_PARTS,))],
         compiler_params=params(),
         cost_estimate=traffic(part.shape[1], 4),
         name="last_edge",
-    )(geo, pairs, far, near, f, part)
-
-
-def exchange(far, near):
-    size = lax.axis_size("space")
-    out = []
-    for x, start in ((far, 1), (near, 0)):
-        pairs = [(i, i + 1) for i in range(start, size - 1, 2)]
-        out.append(lax.ppermute(x, "space", pairs + [(j, i) for i, j in pairs]))
-    return out
+    )(geo, pairs, far, f, part)
+
+
+def swap(rows, start):
+    pairs = [(i, i + 1) for i in range(start, lax.axis_size("space") - 1, 2)]
+    return lax.ppermute(rows, "space", pairs + [(j, i) for i, j in pairs])
 
 
 def per_device(particle_profile, neighbors, face_vectors, volumes, wall_temp):
@@ -846,18 +831,21 @@
     )
     geo = jnp.broadcast_to(geo[:, :, None], (GEO, cells, LANES))
     native, far, near = first_rows(native)
-    far, near = exchange(far, near)
+    far, near = swap(far, 1), swap(near, 0)
     f, sums = first_sums(links, geo, native)
     tiles = gather_sums(sums)
     pairs = geometry(links, geo, rows)
     part = flux(links, geo, f)
     part, absorbed = add_target(links, geo, None, tiles, f, part)
-    f, far, near = edge(pairs, far, near, f, part)
-    far, near = exchange(far, near)
+    part, near = edge(False, pairs, near, f, part, True)
+    near = swap(near, 0)
+    f, far = edge(True, pairs, far, f, part, True)
+    far = swap(far, 1)
     tiles = gather_sums(local_sums(links, geo, f))
     part = flux(links, geo, f)
     part, _ = add_target(links, geo, absorbed, tiles, f, part)
-    native, sums = last_edge(geo, pairs, far, near, f, part)
+    (part,) = edge(False, pairs, near, f, part, False)
+    native, sums = last_edge(geo, pairs, far, f, part)
     macro_quantities = macro(doubling_sums(sums))
     evolved = native.reshape(rows, cells, LANES).transpose(1, 0, 2).reshape(cells, points)
     return evolved, macro_quantities

time: 59 us -> 58.4 us (0.990)
  waiting for transfers between devices: 9.36 us -> 6.69 us
  starting transfers between devices: 20.4 us -> 21.3 us
  Pallas kernels: 27.5 us -> 28.3 us
    ppermute x4, waiting for transfers between devices: 4.58 us -> 2.77 us  [swap(): return lax.ppermute(rows, 'space', pairs + [(j, i) for i, j in pairs])]
    pallas_call x2 -> x4, Pallas kernels: 3.89 us -> 4.39 us  [the longest x3 2.91 us: edge(): pl.pallas_call(functools.partial(edge_kernel, far), in_specs=[spec(pltpu....]
  transfers between devices with their start and end apart: 12 -> 12, of which waited for: 5 -> 5; matrix products, arithmetic and copies ran while one was open for 1% -> 1% of each run, Pallas kernels for 35% -> 41%
where the time goes in v11:
time: 58.4 us; the launch traced here: 57.8 us
  Pallas kernels  28.3 us (48%)
  starting transfers between devices  21.3 us (36%)
  waiting for transfers between devices  6.69 us (11%)
  between operations  0.83 us (1%)
  local copies, waits for them, and re-layouts  0.69 us (1%)
    ppermute x6, starting transfers between devices, gather_sums(): lax.ppermute(tile, 'vel', [(i, i ^ s) for i in range(size)])  8.84 us
    pallas_call x2, Pallas kernels, add_target(): pl.pallas_call(kernel, in_specs=[spec(pltpu.SMEM)] + [vmem] * (len(given)...  8.64 us
    ppermute x4, starting transfers between devices, swap(): return lax.ppermute(rows, 'space', pairs + [(j, i) for i, j in pairs])  7.29 us
    pallas_call x2, Pallas kernels, flux(): pl.pallas_call(flux_kernel, in_specs=[spec(pltpu.SMEM), spec(pltpu.VMEM),...  5.93 us
    ppermute x1, starting transfers between devices, doubling_sums(): return [pair, lax.ppermute(pair, 'vel', [(i, i ^ 2) for i in range(size)])]  3.03 us
    pallas_call x3, Pallas kernels, edge(): pl.pallas_call(functools.partial(edge_kernel, far), in_specs=[spec(pltpu....  2.91 us
    ppermute x4, waiting for transfers between devices, swap(): return lax.ppermute(rows, 'space', pairs + [(j, i) for i, j in pairs])  2.77 us
    pallas_call x1, Pallas kernels, first_sums(): pl.pallas_call(first_sums_kernel, in_specs=[spec(pltpu.SMEM), spec(pltpu....  2.66 us
  transfers between devices with their start and end apart: 12, of which 5 were waited for; matrix products, arithmetic and copies ran while one was open for 1% of the time, Pallas kernels for 41%

profile of v11, /device:TPU:4, one launch (start us, length us, event | category | flops | bytes accessed | tf_op | source)
XLA Modules:
  0.0 57.8 jit_solution(5337947149797072073)
XLA Ops:
  0.6 0.0 copy-start.2
  0.7 2.5 %first_rows.1 = (f32[4096,128]{1,0:T(8,128)S(1)}, f32[3,512,128]{2,1,0:T(8,128)}, f32[3,512,128]{2,1,0:T(8,128)}) custom-call(f32[4096,128]{1,0:T(8,128)} %bitcast.12), custom_call_target="tpu_custom_call" | custom-call | flops 16777216 | bytes 8388608 | tf_op jit(solution)/shard_map/first_rows/pallas_call | solution.py:390
  3.1 0.1 collective-permute-start.1
  3.2 3.4 %collective-permute-start = (f32[3,512,128]{2,1,0:T(8,128)}, f32[3,512,128]{2,1,0:T(8,128)S(1)}, u32[]{:S(2)}, u32[]{:S(2)}) collective-permute-start(f32[3,512,128]{2,1,0:T(8,128)} %get-tuple-element.16), channel_id=1, source_target_pairs={{4,8},{12,16},{20,24},{8,4},{16,12},{24,20},{5,9},{13,17},{21,25},... | collective-permute-start | bytes 2359304 | tf_op jit(solution)/shard_map/ppermute | solution.py:810
  6.7 0.0 copy-done.2
  6.7 0.1 copy.13
  6.8 0.1 copy.14
  6.8 0.1 copy.16
  6.9 0.1 copy.15
  7.0 0.0 copy-done
  7.0 0.1 copy.18
  7.1 0.1 concatenate.3
  7.2 0.1 copy.17
  7.3 0.1 broadcast_in_dim.23.geo_ref.geo_in
  7.4 2.7 %first_sums.1 = (f32[8,512,128]{2,1,0:T(8,128)S(1)}, f32[8,128]{1,0:T(8,128)S(1)}) custom-call(s32[6,8]{1,0:T(8,128)S(1)} %get-tuple-element.31.links_ref, f32[33,8,128]{2,1,0:T(8,128)S(1)} %broadcast_in_dim.23.geo_ref.geo_in, f32[4096,128]{1,0:T(8,128)S(1)} %get-tuple-element.17.native_ref), custom_call_target="tpu_custom_call" | custom-call | flops 20971520 | bytes 10485760 | tf_op jit(solution)/shard_map/first_sums/pallas_call | solution.py:328
  10.0 3.7 %collective-permute-start.4 = (f32[8,128]{1,0:T(8,128)S(1)}, f32[8,128]{1,0:T(8,128)S(1)}, u32[]{:S(2)}, u32[]{:S(2)}) collective-permute-start(f32[8,128]{1,0:T(8,128)S(1)} %get-tuple-element.20.refs_0_), channel_id=1, source_target_pairs={{0,3},{1,2},{2,1},{3,0},{4,7},{5,6},{6,5},{7,4},{8,11},{9,10},{10,... | collective-permute-start | bytes 12296 | tf_op jit(solution)/shard_map/ppermute | solution.py:458
  13.7 0.0 collective-permute-start.3
  13.7 0.8 %collective-permute-start.2 = (f32[8,128]{1,0:T(8,128)S(1)}, f32[8,128]{1,0:T(8,128)S(1)}, u32[]{:S(2)}, u32[]{:S(2)}) collective-permute-start(f32[8,128]{1,0:T(8,128)S(1)} %get-tuple-element.20.refs_0_), channel_id=1, source_target_pairs={{0,1},{1,0},{2,3},{3,2},{4,5},{5,4},{6,7},{7,6},{8,9},{9,8},{10,11... | collective-permute-start | bytes 12296 | tf_op jit(solution)/shard_map/ppermute | solution.py:458
  14.5 1.8 %geometry.1.pairs_ref = f32[12,512,128]{2,1,0:T(8,128)S(1)} custom-call(s32[6,8]{1,0:T(8,128)S(1)} %get-tuple-element.31.links_ref, f32[33,8,128]{2,1,0:T(8,128)S(1)} %broadcast_in_dim.23.geo_ref.geo_in), custom_call_target="tpu_custom_call" | custom-call | flops 16777216 | bytes 8388608 | tf_op jit(solution)/shard_map/geometry/pallas_call | solution.py:442
  16.3 3.0 %flux.2.refs_5_ = f32[8,512,128]{2,1,0:T(8,128)S(1)} custom-call(s32[6,8]{1,0:T(8,128)S(1)} %get-tuple-element.31.links_ref, f32[33,8,128]{2,1,0:T(8,128)S(1)} %broadcast_in_dim.23.geo_ref.geo_in, f32[8,512,128]{2,1,0:T(8,128)S(1)} %get-tuple-element.18.f_ref.refs_4_.old_ref), custom_call_target="tpu_custom_call" | custom-call | flops 29360128 | bytes 14680064 | tf_op jit(solution)/shard_map/flux/pallas_call | solution.py:570
  19.2 0.0 collective-permute-done.4.refs_3_
  19.2 0.0 collective-permute-done.3.refs_2_
  19.2 0.0 collective-permute-done.2.refs_1_
  19.3 4.0 %add_target.2 = (f32[8,512,128]{2,1,0:T(8,128)S(1)}, f32[8,128]{1,0:T(8,128)S(1)}) custom-call(s32[6,8]{1,0:T(8,128)S(1)} %get-tuple-element.31.links_ref, f32[33,8,128]{2,1,0:T(8,128)S(1)} %broadcast_in_dim.23.geo_ref.geo_in, f32[8,128]{1,0:T(8,128)S(1)} %get-tuple-element.20.refs_0_, ...), custom_call_target="tpu_custom_call", output_to_operand_aliasing={{0}: (7, {})} | custom-call | flops 29360128 | bytes 14680064 | tf_op jit(solution)/shard_map/add_target/pallas_call | solution.py:685
  23.3 0.0 collective-permute-done.1.halo_ref
  23.3 1.7 %near_edge.2 = (f32[8,512,128]{2,1,0:T(8,128)S(1)}, f32[3,512,128]{2,1,0:T(8,128)S(1)}) custom-call(f32[12,512,128]{2,1,0:T(8,128)S(1)} %geometry.1.pairs_ref, f32[3,512,128]{2,1,0:T(8,128)} %collective-permute-done.1.halo_ref, f32[8,512,128]{2,1,0:T(8,128)S(1)} %get-tuple-element.18.f_ref.refs_4_.old_ref, ...), custom_call_target="tpu_custom_call", output_to_operand_aliasing={{0}: (3, {})} | custom-call | flops 8388608 | bytes 4194304 | tf_op jit(solution)/shard_map/near_edge/pallas_call | solution.py:747
  25.0 0.1 collective-permute-start.6
  25.1 0.1 collective-permute-done.halo_ref
  25.2 0.6 %far_edge.1 = (f32[8,512,128]{2,1,0:T(8,128)S(1)}, f32[3,512,128]{2,1,0:T(8,128)S(1)}) custom-call(f32[12,512,128]{2,1,0:T(8,128)S(1)} %geometry.1.pairs_ref, f32[3,512,128]{2,1,0:T(8,128)S(1)} %collective-permute-done.halo_ref, f32[8,512,128]{2,1,0:T(8,128)S(1)} %get-tuple-element.18.f_ref.refs_4_.old_ref, ...), custom_call_target="tpu_custom_call", output_to_operand_aliasing={{0}: (3, {})} | custom-call | flops 8388608 | bytes 4194304 | tf_op jit(solution)/shard_map/far_edge/pallas_call | solution.py:747
  25.8 3.7 %collective-permute-start.5 = (f32[3,512,128]{2,1,0:T(8,128)S(1)}, f32[3,512,128]{2,1,0:T(8,128)S(1)}, u32[]{:S(2)}, u32[]{:S(2)}) collective-permute-start(f32[3,512,128]{2,1,0:T(8,128)S(1)} %get-tuple-element.23), channel_id=1, source_target_pairs={{4,8},{12,16},{20,24},{8,4},{16,12},{24,20},{5,9},{13,17},{21,25},... | collective-permute-start | bytes 2359304 | tf_op jit(solution)/shard_map/ppermute | solution.py:810
  29.5 1.8 %local_sums.1.refs_1_ = f32[8,128]{1,0:T(8,128)S(1)} custom-call(s32[6,8]{1,0:T(8,128)S(1)} %get-tuple-element.31.links_ref, f32[33,8,128]{2,1,0:T(8,128)S(1)} %broadcast_in_dim.23.geo_ref.geo_in, f32[8,512,128]{2,1,0:T(8,128)S(1)} %get-tuple-element.24.f_ref.refs_5_.old_ref), custom_call_target="tpu_custom_call" | custom-call | flops 16777216 | bytes 8388608 | tf_op jit(solution)/shard_map/local_sums/pallas_call | solution.py:310
  31.3 3.6 %collective-permute-start.9 = (f32[8,128]{1,0:T(8,128)S(1)}, f32[8,128]{1,0:T(8,128)S(1)}, u32[]{:S(2)}, u32[]{:S(2)}) collective-permute-start(f32[8,128]{1,0:T(8,128)S(1)} %local_sums.1.refs_1_), channel_id=1, source_target_pairs={{0,3},{1,2},{2,1},{3,0},{4,7},{5,6},{6,5},{7,4},{8,11},{9,10},{10,... | collective-permute-start | bytes 12296 | tf_op jit(solution)/shard_map/ppermute | solution.py:458
  34.9 0.0 collective-permute-start.8
  34.9 0.8 %collective-permute-start.7 = (f32[8,128]{1,0:T(8,128)S(1)}, f32[8,128]{1,0:T(8,128)S(1)}, u32[]{:S(2)}, u32[]{:S(2)}) collective-permute-start(f32[8,128]{1,0:T(8,128)S(1)} %local_sums.1.refs_1_), channel_id=1, source_target_pairs={{0,1},{1,0},{2,3},{3,2},{4,5},{5,4},{6,7},{7,6},{8,9},{9,8},{10,11... | collective-permute-start | bytes 12296 | tf_op jit(solution)/shard_map/ppermute | solution.py:458
  35.7 3.0 %flux.3.refs_6_ = f32[8,512,128]{2,1,0:T(8,128)S(1)} custom-call(s32[6,8]{1,0:T(8,128)S(1)} %get-tuple-element.31.links_ref, f32[33,8,128]{2,1,0:T(8,128)S(1)} %broadcast_in_dim.23.geo_ref.geo_in, f32[8,512,128]{2,1,0:T(8,128)S(1)} %get-tuple-element.24.f_ref.refs_5_.old_ref), custom_call_target="tpu_custom_call" | custom-call | flops 29360128 | bytes 14680064 | tf_op jit(solution)/shard_map/flux/pallas_call | solution.py:570
  38.6 0.0 collective-permute-done.9.refs_4_
  38.7 0.7 %collective-permute-done.8.refs_3_ = f32[8,128]{1,0:T(8,128)S(1)} collective-permute-done((f32[8,128]{1,0:T(8,128)S(1)}, f32[8,128]{1,0:T(8,128)S(1)}, u32[]{:S(2)}, u32[]{:S(2)}) %collective-permute-start.8) | collective-permute-done | bytes 4128 | tf_op jit(solution)/shard_map/ppermute | solution.py:458
  39.4 0.0 collective-permute-done.7.refs_2_
  39.4 4.6 %add_target.3 = (f32[8,512,128]{2,1,0:T(8,128)S(1)}, f32[8,128]{1,0:T(8,128)}) custom-call(s32[6,8]{1,0:T(8,128)S(1)} %get-tuple-element.31.links_ref, f32[33,8,128]{2,1,0:T(8,128)S(1)} %broadcast_in_dim.23.geo_ref.geo_in, f32[8,128]{1,0:T(8,128)S(1)} %get-tuple-element.26.refs_0_, f32[8,128]{1,0:T(8,128)S(1)} %local_sums.1.refs_1_, ...), custom_call_target="tpu_custom_call", output_to_operand_aliasing={{0}: (8, {})} | custom-call | flops 29360128 | bytes 14680064 | tf_op jit(solution)/shard_map/add_target/pallas_call | solution.py:685
  44.0 0.0 collective-permute-done.6.halo_ref
  44.0 0.6 %near_edge.3.part_ref = f32[8,512,128]{2,1,0:T(8,128)S(1)} custom-call(f32[12,512,128]{2,1,0:T(8,128)S(1)} %geometry.1.pairs_ref, f32[3,512,128]{2,1,0:T(8,128)S(1)} %collective-permute-done.6.halo_ref, f32[8,512,128]{2,1,0:T(8,128)S(1)} %get-tuple-element.24.f_ref.refs_5_.old_ref, ...), custom_call_target="tpu_custom_call", output_to_operand_aliasing={{}: (3, {})} | custom-call | flops 8388608 | bytes 4194304 | tf_op jit(solution)/shard_map/near_edge/pallas_call | solution.py:747
  44.6 2.7 %collective-permute-done.5.far_ref = f32[3,512,128]{2,1,0:T(8,128)S(1)} collective-permute-done((f32[3,512,128]{2,1,0:T(8,128)S(1)}, f32[3,512,128]{2,1,0:T(8,128)S(1)}, u32[]{:S(2)}, u32[]{:S(2)}) %collective-permute-start.5) | collective-permute-done | bytes 786464 | tf_op jit(solution)/shard_map/ppermute | solution.py:810
  47.3 1.5 %last_edge.1 = (f32[4096,128]{1,0:T(8,128)}, f32[8,128]{1,0:T(8,128)S(1)}) custom-call(f32[33,8,128]{2,1,0:T(8,128)S(1)} %broadcast_in_dim.23.geo_ref.geo_in, f32[12,512,128]{2,1,0:T(8,128)S(1)} %geometry.1.pairs_ref, f32[3,512,128]{2,1,0:T(8,128)S(1)} %collective-permute-done.5.far_ref, f32[8,512,128]{2,1,0:T(8,128)S(1)} %get-tuple-element.24.f_ref.refs_5_.old_ref, ...), custom_call_target="tpu_custom_call" | custom-call | flops 16777216 | bytes 8388608 | tf_op jit(solution)/shard_map/last_edge/pallas_call | solution.py:796
  48.8 2.1 %collective-permute-start.10 = (f32[8,128]{1,0:T(8,128)S(1)}, f32[8,128]{1,0:T(8,128)S(1)}, u32[]{:S(2)}, u32[]{:S(2)}) collective-permute-start(f32[8,128]{1,0:T(8,128)S(1)} %get-tuple-element.29), channel_id=1, source_target_pairs={{0,1},{1,0},{2,3},{3,2},{4,5},{5,4},{6,7},{7,6},{8,9},{9,8},{10,11... | collective-permute-start | bytes 12296 | tf_op jit(solution)/shard_map/ppermute | solution.py:466
  50.9 1.6 %collective-permute-done.10 = f32[8,128]{1,0:T(8,128)S(1)} collective-permute-done((f32[8,128]{1,0:T(8,128)S(1)}, f32[8,128]{1,0:T(8,128)S(1)}, u32[]{:S(2)}, u32[]{:S(2)}) %collective-permute-start.10) | collective-permute-done | bytes 4128 | tf_op jit(solution)/shard_map/ppermute | solution.py:466
  52.5 3.0 %collective-permute-start.11 = (f32[8,128]{1,0:T(8,128)S(1)}, f32[8,128]{1,0:T(8,128)S(1)}, u32[]{:S(2)}, u32[]{:S(2)}) collective-permute-start(f32[8,128]{1,0:T(8,128)S(1)} %add.7.refs_0_), channel_id=1, source_target_pairs={{0,2},{1,3},{2,0},{3,1},{4,6},{5,7},{6,4},{7,5},{8,10},{9,11},{10,... | collective-permute-start | bytes 12296 | tf_op jit(solution)/shard_map/ppermute | solution.py:467
  55.5 1.6 %collective-permute-done.11.refs_1_ = f32[8,128]{1,0:T(8,128)S(1)} collective-permute-done((f32[8,128]{1,0:T(8,128)S(1)}, f32[8,128]{1,0:T(8,128)S(1)}, u32[]{:S(2)}, u32[]{:S(2)}) %collective-permute-start.11) | collective-permute-done | bytes 4128 | tf_op jit(solution)/shard_map/ppermute | solution.py:467
  57.1 0.7 %macro.1 = f32[8,8]{1,0:T(8,128)} custom-call(f32[8,128]{1,0:T(8,128)S(1)} %add.7.refs_0_, f32[8,128]{1,0:T(8,128)S(1)} %collective-permute-done.11.refs_1_), custom_call_target="tpu_custom_call" | custom-call | tf_op jit(solution)/shard_map/macro/pallas_call | solution.py:504
  (9 shorter events, 0.0 us)
Async XLA Ops:
  0.6 6.0 %copy-start.2 = (f32[8]{0:T(128)S(1)}, f32[8]{0:T(128)}, u32[]{:S(2)}) copy-start(f32[8]{0:T(128)} %param.8) | copy-start | bytes 100
  0.6 6.1 %copy-start.3 = (f32[8]{0:T(128)S(1)}, f32[8]{0:T(128)}, u32[]{:S(2)}) copy-start(f32[8]{0:T(128)} %param.9) | copy-start | bytes 100
  0.7 6.2 %copy-start.1 = (s32[6,8]{1,0:T(8,128)S(1)}, s32[6,8]{1,0:T(8,128)}, u32[]{:S(2)}) copy-start(s32[6,8]{1,0:T(8,128)} %param.6) | copy-start | bytes 580
  0.7 6.4 %copy-start = (f32[3,6,8]{2,1,0:T(8,128)S(1)}, f32[3,6,8]{2,1,0:T(8,128)}, u32[]{:S(2)}) copy-start(f32[3,6,8]{2,1,0:T(8,128)} %param.7) | copy-start | bytes 1732
  3.1 20.2 %collective-permute-start.1 = (f32[3,512,128]{2,1,0:T(8,128)}, f32[3,512,128]{2,1,0:T(8,128)}, u32[]{:S(2)}, u32[]{:S(2)}) collective-permute-start(f32[3,512,128]{2,1,0:T(8,128)} %get-tuple-element.19), channel_id=1, source_target_pairs={{0,4},{8,12},{16,20},{24,28},{4,0},{12,8},{20,16},{28,24},{1,5},{9... | collective-permute-start | bytes 2359304 | tf_op jit(solution)/shard_map/ppermute | solution.py:810
  3.2 21.9 %collective-permute-start = (f32[3,512,128]{2,1,0:T(8,128)}, f32[3,512,128]{2,1,0:T(8,128)S(1)}, u32[]{:S(2)}, u32[]{:S(2)}) collective-permute-start(f32[3,512,128]{2,1,0:T(8,128)} %get-tuple-element.16), channel_id=1, source_target_pairs={{4,8},{12,16},{20,24},{8,4},{16,12},{24,20},{5,9},{13,17},{21,25},... | collective-permute-start | bytes 2359304 | tf_op jit(solution)/shard_map/ppermute | solution.py:810
  10.0 9.2 %collective-permute-start.4 = (f32[8,128]{1,0:T(8,128)S(1)}, f32[8,128]{1,0:T(8,128)S(1)}, u32[]{:S(2)}, u32[]{:S(2)}) collective-permute-start(f32[8,128]{1,0:T(8,128)S(1)} %get-tuple-element.20.refs_0_), channel_id=1, source_target_pairs={{0,3},{1,2},{2,1},{3,0},{4,7},{5,6},{6,5},{7,4},{8,11},{9,10},{10,... | collective-permute-start | bytes 12296 | tf_op jit(solution)/shard_map/ppermute | solution.py:458
  13.7 5.6 %collective-permute-start.3 = (f32[8,128]{1,0:T(8,128)S(1)}, f32[8,128]{1,0:T(8,128)S(1)}, u32[]{:S(2)}, u32[]{:S(2)}) collective-permute-start(f32[8,128]{1,0:T(8,128)S(1)} %get-tuple-element.20.refs_0_), channel_id=1, source_target_pairs={{0,2},{1,3},{2,0},{3,1},{4,6},{5,7},{6,4},{7,5},{8,10},{9,11},{10,... | collective-permute-start | bytes 12296 | tf_op jit(solution)/shard_map/ppermute | solution.py:458
  13.7 5.6 %collective-permute-start.2 = (f32[8,128]{1,0:T(8,128)S(1)}, f32[8,128]{1,0:T(8,128)S(1)}, u32[]{:S(2)}, u32[]{:S(2)}) collective-permute-start(f32[8,128]{1,0:T(8,128)S(1)} %get-tuple-element.20.refs_0_), channel_id=1, source_target_pairs={{0,1},{1,0},{2,3},{3,2},{4,5},{5,4},{6,7},{7,6},{8,9},{9,8},{10,11... | collective-permute-start | bytes 12296 | tf_op jit(solution)/shard_map/ppermute | solution.py:458
  25.0 19.0 %collective-permute-start.6 = (f32[3,512,128]{2,1,0:T(8,128)S(1)}, f32[3,512,128]{2,1,0:T(8,128)S(1)}, u32[]{:S(2)}, u32[]{:S(2)}) collective-permute-start(f32[3,512,128]{2,1,0:T(8,128)S(1)} %get-tuple-element.25), channel_id=1, source_target_pairs={{0,4},{8,12},{16,20},{24,28},{4,0},{12,8},{20,16},{28,24},{1,5},{9... | collective-permute-start | bytes 2359304 | tf_op jit(solution)/shard_map/ppermute | solution.py:810
  25.8 21.5 %collective-permute-start.5 = (f32[3,512,128]{2,1,0:T(8,128)S(1)}, f32[3,512,128]{2,1,0:T(8,128)S(1)}, u32[]{:S(2)}, u32[]{:S(2)}) collective-permute-start(f32[3,512,128]{2,1,0:T(8,128)S(1)} %get-tuple-element.23), channel_id=1, source_target_pairs={{4,8},{12,16},{20,24},{8,4},{16,12},{24,20},{5,9},{13,17},{21,25},... | collective-permute-start | bytes 2359304 | tf_op jit(solution)/shard_map/ppermute | solution.py:810
  31.3 7.4 %collective-permute-start.9 = (f32[8,128]{1,0:T(8,128)S(1)}, f32[8,128]{1,0:T(8,128)S(1)}, u32[]{:S(2)}, u32[]{:S(2)}) collective-permute-start(f32[8,128]{1,0:T(8,128)S(1)} %local_sums.1.refs_1_), channel_id=1, source_target_pairs={{0,3},{1,2},{2,1},{3,0},{4,7},{5,6},{6,5},{7,4},{8,11},{9,10},{10,... | collective-permute-start | bytes 12296 | tf_op jit(solution)/shard_map/ppermute | solution.py:458
  34.9 4.5 %collective-permute-start.8 = (f32[8,128]{1,0:T(8,128)S(1)}, f32[8,128]{1,0:T(8,128)S(1)}, u32[]{:S(2)}, u32[]{:S(2)}) collective-permute-start(f32[8,128]{1,0:T(8,128)S(1)} %local_sums.1.refs_1_), channel_id=1, source_target_pairs={{0,2},{1,3},{2,0},{3,1},{4,6},{5,7},{6,4},{7,5},{8,10},{9,11},{10,... | collective-permute-start | bytes 12296 | tf_op jit(solution)/shard_map/ppermute | solution.py:458
  34.9 4.5 %collective-permute-start.7 = (f32[8,128]{1,0:T(8,128)S(1)}, f32[8,128]{1,0:T(8,128)S(1)}, u32[]{:S(2)}, u32[]{:S(2)}) collective-permute-start(f32[8,128]{1,0:T(8,128)S(1)} %local_sums.1.refs_1_), channel_id=1, source_target_pairs={{0,1},{1,0},{2,3},{3,2},{4,5},{5,4},{6,7},{7,6},{8,9},{9,8},{10,11... | collective-permute-start | bytes 12296 | tf_op jit(solution)/shard_map/ppermute | solution.py:458
  48.8 3.7 %collective-permute-start.10 = (f32[8,128]{1,0:T(8,128)S(1)}, f32[8,128]{1,0:T(8,128)S(1)}, u32[]{:S(2)}, u32[]{:S(2)}) collective-permute-start(f32[8,128]{1,0:T(8,128)S(1)} %get-tuple-element.29), channel_id=1, source_target_pairs={{0,1},{1,0},{2,3},{3,2},{4,5},{5,4},{6,7},{7,6},{8,9},{9,8},{10,11... | collective-permute-start | bytes 12296 | tf_op jit(solution)/shard_map/ppermute | solution.py:466
  52.5 4.6 %collective-permute-start.11 = (f32[8,128]{1,0:T(8,128)S(1)}, f32[8,128]{1,0:T(8,128)S(1)}, u32[]{:S(2)}, u32[]{:S(2)}) collective-permute-start(f32[8,128]{1,0:T(8,128)S(1)} %add.7.refs_0_), channel_id=1, source_target_pairs={{0,2},{1,3},{2,0},{3,1},{4,6},{5,7},{6,4},{7,5},{8,10},{9,11},{10,... | collective-permute-start | bytes 12296 | tf_op jit(solution)/shard_map/ppermute | solution.py:467

commit v12 on v11

--- a/solution.py
+++ b/solution.py
@@ -104,14 +104,13 @@
 
 
 def list_faces(links_ref, wanted, cell_ref, face_ref):
-    def cell(g, count):
+    count = 0
+    for g in range(SUB):
         for k in range(FACES):
             cell_ref[count] = g
             face_ref[count] = k
             count = count + wanted(links_ref[k, g]).astype(jnp.int32)
-        return count
-
-    return lax.fori_loop(0, SUB, cell, 0)
+    return count
 
 
 def is_wall(j):
@@ -297,7 +296,7 @@
     return jax.ShapeDtypeStruct(shape, F32)
 
 
-def params(mib=8):
+def params(mib=4):
     return pltpu.CompilerParams(vmem_limit_bytes=mib * 1024 * 1024)
 
 
@@ -399,7 +398,7 @@
     )(pltpu.with_memory_space_constraint(native, pltpu.HBM))
 
 
-def geometry_kernel(links_ref, geo_ref, pairs_ref, cells, faces):
+def pair_weights(links_ref, geo_ref, pairs_ref, cells, faces):
     rows = pairs_ref.shape[1]
     planes = rows // CHUNKS
     first = splat(geo_ref, FIRST, 0)
@@ -436,19 +435,6 @@
         return 0
 
     lax.fori_loop(0, list_faces(links_ref, is_remote, cells, faces), remote, 0)
-
-
-def geometry(links, geo, rows):
-    return pl.pallas_call(
-        geometry_kernel,
-        in_specs=[spec(pltpu.SMEM), spec(pltpu.VMEM)],
-        out_specs=spec(pltpu.VMEM),
-        out_shape=array(2 * len(BEFORE_PAIRS), rows, LANES),
-        scratch_shapes=face_lists(),
-        compiler_params=params(),
-        cost_estimate=traffic(rows, 4),
-        name="geometry",
-    )(links, geo)
 
 
 def gather_sums(tile):
@@ -511,7 +497,12 @@
     )(*tiles)
 
 
-def flux_kernel(links_ref, geo_ref, f_ref, out_ref, coef, source, face):
+def flux_kernel(with_pairs, links_ref, geo_ref, f_ref, out_ref, *refs):
+    if with_pairs:
+        pairs_ref, cells, faces = refs[0], refs[-2], refs[-1]
+        pair_weights(links_ref, geo_ref, pairs_ref, cells, faces)
+        refs = refs[1:-2]
+    coef, bases, stays, source, face = refs
     planes = f_ref.shape[1] // CHUNKS
     scale = -TIME_STEP / geo_ref[VOL]
     for i in range(3):
@@ -522,6 +513,18 @@
             whole = x if whole is None else whole + x
         coef[3 * FACES + i] = whole
 
+    def table(g, _):
+        w = [[splat(coef, FACES * i + k, g) for i in (1, 2)] for k in range(FACES)]
+        whole = [splat(coef, 3 * FACES + i, g) for i in (1, 2)]
+        for t in range(TILES):
+            xb, xc = tile_nodes(t)
+            for k in range(FACES):
+                bases[k, g * TILES + t] = w[k][0] * xb + w[k][1] * xc
+            stays[g * TILES + t] = 1.0 + whole[0] * xb + whole[1] * xc
+        return 0
+
+    lax.fori_loop(0, SUB, table, 0, unroll=2)
+
     def cell(g, _):
         count = 0
         for k in range(FACES):
@@ -539,19 +542,16 @@
 
     def own_faces(g, n):
         at_source = [source[i] for i in range(n)]
-        weight = [[splat(coef, FACES * i + face[k], g) for i in range(3)] for k in range(n)]
-        whole = [splat(coef, 3 * FACES + i, g) for i in range(3)]
+        first_weight = [splat(coef, face[k], g) for k in range(n)]
+        whole = splat(coef, 3 * FACES, g)
         x0 = splat(geo_ref, FIRST, g)
-        base, stay = [], []
-        for t in range(TILES):
-            xb, xc = tile_nodes(t)
-            base.append([w[1] * xb + w[2] * xc for w in weight])
-            stay.append(1.0 + whole[1] * xb + whole[2] * xc)
+        base = [[bases[face[k], g * TILES + t] for k in range(n)] for t in range(TILES)]
+        stay = [stays[g * TILES + t] for t in range(TILES)]
 
         def plane(a, _):
             xa = x0 + a.astype(F32) * H
-            sa = [w[0] * xa for w in weight]
-            stay_a = whole[0] * xa
+            sa = [w * xa for w in first_weight]
+            stay_a = whole * xa
             for t in range(TILES):
                 at = at_rows((a * TILES + t) * SUB)
                 f = f_ref[g, at, :]
@@ -566,25 +566,30 @@
     lax.fori_loop(0, SUB, cell, 0)
 
 
-def flux(links, geo, f):
+def flux(with_pairs, links, geo, f):
+    rows = f.shape[1]
+    pairs = 2 * len(BEFORE_PAIRS)
     return pl.pallas_call(
-        flux_kernel,
+        functools.partial(flux_kernel, with_pairs),
         in_specs=[spec(pltpu.SMEM), spec(pltpu.VMEM), spec(pltpu.VMEM)],
-        out_specs=spec(pltpu.VMEM),
-        out_shape=array(*f.shape),
+        out_specs=[spec(pltpu.VMEM)] * (2 if with_pairs else 1),
+        out_shape=[array(*f.shape)] + ([array(pairs, rows, LANES)] if with_pairs else []),
         scratch_shapes=[
             pltpu.VMEM((3 * FACES + 3, SUB, LANES), F32),
+            pltpu.VMEM((FACES, SUB * TILES, SUB, LANES), F32),
+            pltpu.VMEM((SUB * TILES, SUB, LANES), F32),
             pltpu.SMEM((FACES + 1,), jnp.int32),
             pltpu.SMEM((FACES + 1,), jnp.int32),
-        ],
+        ]
+        + (face_lists() if with_pairs else []),
         compiler_params=params(),
-        cost_estimate=traffic(f.shape[1], 7),
+        cost_estimate=traffic(rows, 9 if with_pairs else 7),
         name="flux",
     )(links, geo, f)
 
 
 def target_kernel(count, links_ref, geo_ref, absorbed_in, *refs):
-    sums_refs, (f_ref, part_ref, out_ref, sum_out, ta, coef, cells, faces) = refs[:count], refs[count:]
+    sums_refs, (f_ref, part_ref, out_ref, sum_out, ta, tiles_ref, coef, cells, faces) = refs[:count], refs[count:]
     planes = f_ref.shape[1] // CHUNKS
     sums = add_tiles(sums_refs)
     sum_out[...] = sums
@@ -603,33 +608,47 @@
         coef[6 + k] = column(sums, EMIT + k) / jnp.where(wall, column(absorbed, ABSORB + k), 1.0)
     first = geo_ref[FIRST]
 
+    wt = geo_ref[WT]
+
     def plane_table(a, _):
-        ca = first + a.astype(F32) * H - u[0]
+        xa = first + a.astype(F32) * H
+        ca = xa - u[0]
         za = ca * ca * rt
         ta[0, a] = height * jnp.exp(-0.5 * za)
         ta[1, a] = slope * q[0] * ca
         ta[2, a] = za - 5.0
-        return 0
-
-    lax.fori_loop(0, planes, plane_table, 0, unroll=4)
-
-    def cell(g, _):
-        rate_g, rtg = splat(coef, 0, g), splat(coef, 1, g)
+        ta[3, a] = jnp.exp(-0.5 * xa * xa / wt)
+        return 0
+
+    lax.fori_loop(0, planes, plane_table, 0, unroll=unroll(planes, 8))
+
+    def tile_table(g, _):
+        rtg = splat(coef, 1, g)
         ub, uc = splat(coef, 2, g), splat(coef, 3, g)
         qb, qc = splat(coef, 4, g), splat(coef, 5, g)
-        bell, heat, zz = [], [], []
+        shape = wall_tiles(splat(geo_ref, WT, g))
         for t in range(TILES):
             xb, xc = tile_nodes(t)
             cb, cc = xb - ub, xc - uc
             z = (cb * cb + cc * cc) * rtg
-            bell.append(jnp.exp(-0.5 * z))
-            heat.append(cb * qb + cc * qc)
-            zz.append(z)
+            at = g * TILES + t
+            tiles_ref[0, at] = jnp.exp(-0.5 * z)
+            tiles_ref[1, at] = cb * qb + cc * qc
+            tiles_ref[2, at] = z
+            tiles_ref[3, at] = shape[t]
+        return 0
+
+    lax.fori_loop(0, SUB, tile_table, 0, unroll=4)
+
+    def at_plane(i, a, g):
+        return jnp.broadcast_to(ta[i, a, pl.ds(g, 1), :], (SUB, LANES))
+
+    def cell(g, _):
+        rate_g = splat(coef, 0, g)
+        bell, heat, zz = [[tiles_ref[i, g * TILES + t] for t in range(TILES)] for i in range(3)]
 
         def plane(a, _):
-            height_a, heat_a, z_a = [
-                jnp.broadcast_to(ta[i, a, pl.ds(g, 1), :], (SUB, LANES)) for i in range(3)
-            ]
+            height_a, heat_a, z_a = [at_plane(i, a, g) for i in range(3)]
             for t in range(TILES):
                 where = (g, at_rows((a * TILES + t) * SUB), slice(None))
                 f = f_ref[where]
@@ -645,27 +664,25 @@
     def wall(i, _):
         g, k = cells[i], faces[i]
         x0 = splat(geo_ref, FIRST, g)
-        wt = splat(geo_ref, WT, g)
         ratio = splat(coef, 6 + k, g)
-        shape = [ratio * x for x in wall_tiles(wt)]
         scale = -TIME_STEP / splat(geo_ref, VOL, g)
         v0, v1, v2 = [scale * x for x in face_coefficients(geo_ref, k, g)]
-        base = []
+        base, shape = [], []
         for t in range(TILES):
             xb, xc = tile_nodes(t)
             base.append(v1 * xb + v2 * xc)
+            shape.append(ratio * tiles_ref[3, g * TILES + t])
 
         def plane(a, _):
-            xa = x0 + a.astype(F32) * H
-            wa = jnp.exp(-0.5 * xa * xa / wt)
-            sa = v0 * xa
+            wa = at_plane(3, a, g)
+            sa = v0 * (x0 + a.astype(F32) * H)
             for t in range(TILES):
                 where = (g, at_rows((a * TILES + t) * SUB), slice(None))
                 f = f_ref[where]
                 out_ref[where] = out_ref[where] + jnp.maximum(sa + base[t], 0.0) * (wa * shape[t] - f)
             return 0
 
-        lax.fori_loop(0, planes, plane, 0, unroll=unroll(planes, 8))
+        lax.fori_loop(0, planes, plane, 0, unroll=unroll(planes, 16))
         return 0
 
     lax.fori_loop(0, list_faces(links_ref, is_wall, cells, faces), wall, 0)
@@ -689,7 +706,8 @@
         out_shape=[array(*part.shape), array(SUB, LANES)],
         input_output_aliases={len(given) - 1: 0},
         scratch_shapes=[
-                pltpu.VMEM((3, rows // CHUNKS, SUB, LANES), F32),
+                pltpu.VMEM((4, rows // CHUNKS, SUB, LANES), F32),
+            pltpu.VMEM((4, SUB * TILES, SUB, LANES), F32),
             pltpu.VMEM((6 + FACES, SUB, LANES), F32),
             *face_lists(),
         ],
@@ -834,15 +852,14 @@
     far, near = swap(far, 1), swap(near, 0)
     f, sums = first_sums(links, geo, native)
     tiles = gather_sums(sums)
-    pairs = geometry(links, geo, rows)
-    part = flux(links, geo, f)
+    part, pairs = flux(True, links, geo, f)
     part, absorbed = add_target(links, geo, None, tiles, f, part)
     part, near = edge(False, pairs, near, f, part, True)
     near = swap(near, 0)
     f, far = edge(True, pairs, far, f, part, True)
     far = swap(far, 1)
     tiles = gather_sums(local_sums(links, geo, f))
-    part = flux(links, geo, f)
+    (part,) = flux(False, links, geo, f)
     part, _ = add_target(links, geo, absorbed, tiles, f, part)
     (part,) = edge(False, pairs, near, f, part, False)
     native, sums = last_edge(geo, pairs, far, f, part)

time: 58.4 us -> 58.4 us (level)
  Pallas kernels: 28.3 us -> 26.2 us
  waiting for transfers between devices: 6.69 us -> 8.09 us
  starting transfers between devices: 21.3 us -> 22 us
    ppermute x4, waiting for transfers between devices: 2.77 us -> 4.41 us  [swap(): return lax.ppermute(rows, 'space', pairs + [(j, i) for i, j in pairs])]
    pallas_call x2, Pallas kernels: 8.64 us -> 7.46 us  [add_target(): pl.pallas_call(kernel, in_specs=[spec(pltpu.SMEM)] + [vmem] * (len(given)...]
    ppermute x1, starting transfers between devices: 2.13 us -> 2.84 us  [doubling_sums(): pair = tile + lax.ppermute(tile, 'vel', [(i, i ^ 1) for i in range(size)])]
    pallas_call x3 -> x2, Pallas kernels: 7.7 us -> 7.51 us  [flux(): pl.pallas_call(functools.partial(flux_kernel, with_pairs), in_specs=[spec...]
  transfers between devices with their start and end apart: 12 -> 12, of which waited for: 5 -> 5; matrix products, arithmetic and copies ran while one was open for 1% -> 1% of each run, Pallas kernels for 41% -> 37%
where the time goes in v12:
time: 58.4 us; the launch traced here: 57.9 us
  Pallas kernels  26.2 us (45%)
  starting transfers between devices  22 us (38%)
  waiting for transfers between devices  8.09 us (14%)
  between operations  0.82 us (1%)
  local copies, waits for them, and re-layouts  0.69 us (1%)
    ppermute x6, starting transfers between devices, gather_sums(): lax.ppermute(tile, 'vel', [(i, i ^ s) for i in range(size)])  8.84 us
    pallas_call x2, Pallas kernels, flux(): pl.pallas_call(functools.partial(flux_kernel, with_pairs), in_specs=[spec...  7.51 us
    pallas_call x2, Pallas kernels, add_target(): pl.pallas_call(kernel, in_specs=[spec(pltpu.SMEM)] + [vmem] * (len(given)...  7.46 us
    ppermute x4, starting transfers between devices, swap(): return lax.ppermute(rows, 'space', pairs + [(j, i) for i, j in pairs])  7.3 us
    ppermute x4, waiting for transfers between devices, swap(): return lax.ppermute(rows, 'space', pairs + [(j, i) for i, j in pairs])  4.41 us
    ppermute x1, starting transfers between devices, doubling_sums(): return [pair, lax.ppermute(pair, 'vel', [(i, i ^ 2) for i in range(size)])]  3.03 us
    pallas_call x3, Pallas kernels, edge(): pl.pallas_call(functools.partial(edge_kernel, far), in_specs=[spec(pltpu....  2.95 us
    ppermute x1, starting transfers between devices, doubling_sums(): pair = tile + lax.ppermute(tile, 'vel', [(i, i ^ 1) for i in range(size)])  2.84 us
  transfers between devices with their start and end apart: 12, of which 5 were waited for; matrix products, arithmetic and copies ran while one was open for 1% of the time, Pallas kernels for 37%

profile of v12, /device:TPU:4, one launch (start us, length us, event | category | flops | bytes accessed | tf_op | source)
XLA Modules:
  0.0 57.9 jit_solution(17663788660217459704)
XLA Ops:
  0.6 0.0 copy-start.2
  0.6 0.0 copy-start.3
  0.7 0.0 copy-start.1
  0.7 0.0 copy-start
  0.7 2.5 %first_rows.1 = (f32[4096,128]{1,0:T(8,128)S(1)}, f32[3,512,128]{2,1,0:T(8,128)}, f32[3,512,128]{2,1,0:T(8,128)}) custom-call(f32[4096,128]{1,0:T(8,128)} %bitcast.12), custom_call_target="tpu_custom_call" | custom-call | flops 16777216 | bytes 8388608 | tf_op jit(solution)/shard_map/first_rows/pallas_call | solution.py:389
  3.1 0.1 collective-permute-start.1
  3.2 3.4 %collective-permute-start = (f32[3,512,128]{2,1,0:T(8,128)}, f32[3,512,128]{2,1,0:T(8,128)S(1)}, u32[]{:S(2)}, u32[]{:S(2)}) collective-permute-start(f32[3,512,128]{2,1,0:T(8,128)} %get-tuple-element.21), channel_id=1, source_target_pairs={{4,8},{12,16},{20,24},{8,4},{16,12},{24,20},{5,9},{13,17},{21,25},... | collective-permute-start | bytes 2359304 | tf_op jit(solution)/shard_map/ppermute | solution.py:828
  6.7 0.1 copy.13
  6.8 0.1 copy.14
  6.9 0.1 copy.16
  6.9 0.1 copy.15
  7.0 0.1 copy.18
  7.1 0.1 concatenate.3
  7.2 0.1 copy.17
  7.3 0.1 broadcast_in_dim.23.geo_ref.geo_in
  7.4 2.2 %first_sums.1 = (f32[8,512,128]{2,1,0:T(8,128)S(1)}, f32[8,128]{1,0:T(8,128)S(1)}) custom-call(s32[6,8]{1,0:T(8,128)S(1)} %get-tuple-element.35.links_ref, f32[33,8,128]{2,1,0:T(8,128)S(1)} %broadcast_in_dim.23.geo_ref.geo_in, f32[4096,128]{1,0:T(8,128)S(1)} %get-tuple-element.18.native_ref), custom_call_target="tpu_custom_call" | custom-call | flops 20971520 | bytes 10485760 | tf_op jit(solution)/shard_map/first_sums/pallas_call | solution.py:327
  9.6 3.7 %collective-permute-start.4 = (f32[8,128]{1,0:T(8,128)S(1)}, f32[8,128]{1,0:T(8,128)S(1)}, u32[]{:S(2)}, u32[]{:S(2)}) collective-permute-start(f32[8,128]{1,0:T(8,128)S(1)} %get-tuple-element.23.refs_0_), channel_id=1, source_target_pairs={{0,3},{1,2},{2,1},{3,0},{4,7},{5,6},{6,5},{7,4},{8,11},{9,10},{10,... | collective-permute-start | bytes 12296 | tf_op jit(solution)/shard_map/ppermute | solution.py:444
  13.2 0.0 collective-permute-start.3
  13.2 0.8 %collective-permute-start.2 = (f32[8,128]{1,0:T(8,128)S(1)}, f32[8,128]{1,0:T(8,128)S(1)}, u32[]{:S(2)}, u32[]{:S(2)}) collective-permute-start(f32[8,128]{1,0:T(8,128)S(1)} %get-tuple-element.23.refs_0_), channel_id=1, source_target_pairs={{0,1},{1,0},{2,3},{3,2},{4,5},{5,4},{6,7},{7,6},{8,9},{9,8},{10,11... | collective-permute-start | bytes 12296 | tf_op jit(solution)/shard_map/ppermute | solution.py:444
  14.0 4.3 %flux.2 = (f32[8,512,128]{2,1,0:T(8,128)S(1)}, f32[12,512,128]{2,1,0:T(8,128)S(1)}) custom-call(s32[6,8]{1,0:T(8,128)S(1)} %get-tuple-element.35.links_ref, f32[33,8,128]{2,1,0:T(8,128)S(1)} %broadcast_in_dim.23.geo_ref.geo_in, f32[8,512,128]{2,1,0:T(8,128)S(1)} %get-tuple-element.19.f_ref.refs_4_.old_ref), custom_call_target="tpu_custom_call" | custom-call | flops 37748736 | bytes 18874368 | tf_op jit(solution)/shard_map/flux/pallas_call | solution.py:572
  18.3 0.0 collective-permute-done.4.refs_3_
  18.3 0.0 collective-permute-done.3.refs_2_
  18.3 0.0 collective-permute-done.2.refs_1_
  18.3 3.4 %add_target.2 = (f32[8,512,128]{2,1,0:T(8,128)S(1)}, f32[8,128]{1,0:T(8,128)S(1)}) custom-call(s32[6,8]{1,0:T(8,128)S(1)} %get-tuple-element.35.links_ref, f32[33,8,128]{2,1,0:T(8,128)S(1)} %broadcast_in_dim.23.geo_ref.geo_in, f32[8,128]{1,0:T(8,128)S(1)} %get-tuple-element.23.refs_0_, ...), custom_call_target="tpu_custom_call", output_to_operand_aliasing={{0}: (7, {})} | custom-call | flops 29360128 | bytes 14680064 | tf_op jit(solution)/shard_map/add_target/pallas_call | solution.py:702
  21.8 0.0 collective-permute-done.1.halo_ref
  21.8 1.7 %near_edge.2 = (f32[8,512,128]{2,1,0:T(8,128)S(1)}, f32[3,512,128]{2,1,0:T(8,128)S(1)}) custom-call(f32[12,512,128]{2,1,0:T(8,128)S(1)} %get-tuple-element.20.pairs_ref, f32[3,512,128]{2,1,0:T(8,128)} %collective-permute-done.1.halo_ref, f32[8,512,128]{2,1,0:T(8,128)S(1)} %get-tuple-element.19.f_ref.refs_4_.old_ref, ...), custom_call_target="tpu_custom_call", output_to_operand_aliasing={{0}: (3, {})} | custom-call | flops 8388608 | bytes 4194304 | tf_op jit(solution)/shard_map/near_edge/pallas_call | solution.py:765
  23.6 0.1 collective-permute-start.6
  23.6 1.5 %collective-permute-done.halo_ref = f32[3,512,128]{2,1,0:T(8,128)S(1)} collective-permute-done((f32[3,512,128]{2,1,0:T(8,128)}, f32[3,512,128]{2,1,0:T(8,128)S(1)}, u32[]{:S(2)}, u32[]{:S(2)}) %collective-permute-start) | collective-permute-done | bytes 786464 | tf_op jit(solution)/shard_map/ppermute | solution.py:828
  25.2 0.6 %far_edge.1 = (f32[8,512,128]{2,1,0:T(8,128)S(1)}, f32[3,512,128]{2,1,0:T(8,128)S(1)}) custom-call(f32[12,512,128]{2,1,0:T(8,128)S(1)} %get-tuple-element.20.pairs_ref, f32[3,512,128]{2,1,0:T(8,128)S(1)} %collective-permute-done.halo_ref, f32[8,512,128]{2,1,0:T(8,128)S(1)} %get-tuple-element.19.f_ref.refs_4_.old_ref, ...), custom_call_target="tpu_custom_call", output_to_operand_aliasing={{0}: (3, {})} | custom-call | flops 8388608 | bytes 4194304 | tf_op jit(solution)/shard_map/far_edge/pallas_call | solution.py:765
  25.8 3.7 %collective-permute-start.5 = (f32[3,512,128]{2,1,0:T(8,128)S(1)}, f32[3,512,128]{2,1,0:T(8,128)S(1)}, u32[]{:S(2)}, u32[]{:S(2)}) collective-permute-start(f32[3,512,128]{2,1,0:T(8,128)S(1)} %get-tuple-element.27), channel_id=1, source_target_pairs={{4,8},{12,16},{20,24},{8,4},{16,12},{24,20},{5,9},{13,17},{21,25},... | collective-permute-start | bytes 2359304 | tf_op jit(solution)/shard_map/ppermute | solution.py:828
  29.5 1.5 %local_sums.1.refs_1_ = f32[8,128]{1,0:T(8,128)S(1)} custom-call(s32[6,8]{1,0:T(8,128)S(1)} %get-tuple-element.35.links_ref, f32[33,8,128]{2,1,0:T(8,128)S(1)} %broadcast_in_dim.23.geo_ref.geo_in, f32[8,512,128]{2,1,0:T(8,128)S(1)} %get-tuple-element.28.f_ref.refs_5_.old_ref), custom_call_target="tpu_custom_call" | custom-call | flops 16777216 | bytes 8388608 | tf_op jit(solution)/shard_map/local_sums/pallas_call | solution.py:309
  31.0 3.6 %collective-permute-start.9 = (f32[8,128]{1,0:T(8,128)S(1)}, f32[8,128]{1,0:T(8,128)S(1)}, u32[]{:S(2)}, u32[]{:S(2)}) collective-permute-start(f32[8,128]{1,0:T(8,128)S(1)} %local_sums.1.refs_1_), channel_id=1, source_target_pairs={{0,3},{1,2},{2,1},{3,0},{4,7},{5,6},{6,5},{7,4},{8,11},{9,10},{10,... | collective-permute-start | bytes 12296 | tf_op jit(solution)/shard_map/ppermute | solution.py:444
  34.6 0.0 collective-permute-start.8
  34.6 0.8 %collective-permute-start.7 = (f32[8,128]{1,0:T(8,128)S(1)}, f32[8,128]{1,0:T(8,128)S(1)}, u32[]{:S(2)}, u32[]{:S(2)}) collective-permute-start(f32[8,128]{1,0:T(8,128)S(1)} %local_sums.1.refs_1_), channel_id=1, source_target_pairs={{0,1},{1,0},{2,3},{3,2},{4,5},{5,4},{6,7},{7,6},{8,9},{9,8},{10,11... | collective-permute-start | bytes 12296 | tf_op jit(solution)/shard_map/ppermute | solution.py:444
  35.4 3.2 %flux.3.refs_6_ = f32[8,512,128]{2,1,0:T(8,128)S(1)} custom-call(s32[6,8]{1,0:T(8,128)S(1)} %get-tuple-element.35.links_ref, f32[33,8,128]{2,1,0:T(8,128)S(1)} %broadcast_in_dim.23.geo_ref.geo_in, f32[8,512,128]{2,1,0:T(8,128)S(1)} %get-tuple-element.28.f_ref.refs_5_.old_ref), custom_call_target="tpu_custom_call" | custom-call | flops 29360128 | bytes 14680064 | tf_op jit(solution)/shard_map/flux/pallas_call | solution.py:572
  38.6 0.0 collective-permute-done.9.refs_4_
  38.6 0.5 collective-permute-done.8.refs_3_
  39.1 0.0 collective-permute-done.7.refs_2_
  39.1 4.0 %add_target.3 = (f32[8,512,128]{2,1,0:T(8,128)S(1)}, f32[8,128]{1,0:T(8,128)}) custom-call(s32[6,8]{1,0:T(8,128)S(1)} %get-tuple-element.35.links_ref, f32[33,8,128]{2,1,0:T(8,128)S(1)} %broadcast_in_dim.23.geo_ref.geo_in, f32[8,128]{1,0:T(8,128)S(1)} %get-tuple-element.30.refs_0_, f32[8,128]{1,0:T(8,128)S(1)} %local_sums.1.refs_1_, ...), custom_call_target="tpu_custom_call", output_to_operand_aliasing={{0}: (8, {})} | custom-call | flops 29360128 | bytes 14680064 | tf_op jit(solution)/shard_map/add_target/pallas_call | solution.py:702
  43.2 0.0 collective-permute-done.6.halo_ref
  43.2 0.6 %near_edge.3.part_ref = f32[8,512,128]{2,1,0:T(8,128)S(1)} custom-call(f32[12,512,128]{2,1,0:T(8,128)S(1)} %get-tuple-element.20.pairs_ref, f32[3,512,128]{2,1,0:T(8,128)S(1)} %collective-permute-done.6.halo_ref, f32[8,512,128]{2,1,0:T(8,128)S(1)} %get-tuple-element.28.f_ref.refs_5_.old_ref, ...), custom_call_target="tpu_custom_call", output_to_operand_aliasing={{}: (3, {})} | custom-call | flops 8388608 | bytes 4194304 | tf_op jit(solution)/shard_map/near_edge/pallas_call | solution.py:765
  43.8 2.9 %collective-permute-done.5.far_ref = f32[3,512,128]{2,1,0:T(8,128)S(1)} collective-permute-done((f32[3,512,128]{2,1,0:T(8,128)S(1)}, f32[3,512,128]{2,1,0:T(8,128)S(1)}, u32[]{:S(2)}, u32[]{:S(2)}) %collective-permute-start.5) | collective-permute-done | bytes 786464 | tf_op jit(solution)/shard_map/ppermute | solution.py:828
  46.6 1.5 %last_edge.1 = (f32[4096,128]{1,0:T(8,128)}, f32[8,128]{1,0:T(8,128)S(1)}) custom-call(f32[33,8,128]{2,1,0:T(8,128)S(1)} %broadcast_in_dim.23.geo_ref.geo_in, f32[12,512,128]{2,1,0:T(8,128)S(1)} %get-tuple-element.20.pairs_ref, f32[3,512,128]{2,1,0:T(8,128)S(1)} %collective-permute-done.5.far_ref, ...), custom_call_target="tpu_custom_call" | custom-call | flops 16777216 | bytes 8388608 | tf_op jit(solution)/shard_map/last_edge/pallas_call | solution.py:814
  48.1 2.8 %collective-permute-start.10 = (f32[8,128]{1,0:T(8,128)S(1)}, f32[8,128]{1,0:T(8,128)S(1)}, u32[]{:S(2)}, u32[]{:S(2)}) collective-permute-start(f32[8,128]{1,0:T(8,128)S(1)} %get-tuple-element.33), channel_id=1, source_target_pairs={{0,1},{1,0},{2,3},{3,2},{4,5},{5,4},{6,7},{7,6},{8,9},{9,8},{10,11... | collective-permute-start | bytes 12296 | tf_op jit(solution)/shard_map/ppermute | solution.py:452
  51.0 1.6 %collective-permute-done.10 = f32[8,128]{1,0:T(8,128)S(1)} collective-permute-done((f32[8,128]{1,0:T(8,128)S(1)}, f32[8,128]{1,0:T(8,128)S(1)}, u32[]{:S(2)}, u32[]{:S(2)}) %collective-permute-start.10) | collective-permute-done | bytes 4128 | tf_op jit(solution)/shard_map/ppermute | solution.py:452
  52.6 3.0 %collective-permute-start.11 = (f32[8,128]{1,0:T(8,128)S(1)}, f32[8,128]{1,0:T(8,128)S(1)}, u32[]{:S(2)}, u32[]{:S(2)}) collective-permute-start(f32[8,128]{1,0:T(8,128)S(1)} %add.7.refs_0_), channel_id=1, source_target_pairs={{0,2},{1,3},{2,0},{3,1},{4,6},{5,7},{6,4},{7,5},{8,10},{9,11},{10,... | collective-permute-start | bytes 12296 | tf_op jit(solution)/shard_map/ppermute | solution.py:453
  55.6 1.6 %collective-permute-done.11.refs_1_ = f32[8,128]{1,0:T(8,128)S(1)} collective-permute-done((f32[8,128]{1,0:T(8,128)S(1)}, f32[8,128]{1,0:T(8,128)S(1)}, u32[]{:S(2)}, u32[]{:S(2)}) %collective-permute-start.11) | collective-permute-done | bytes 4128 | tf_op jit(solution)/shard_map/ppermute | solution.py:453
  57.2 0.7 %macro.1 = f32[8,8]{1,0:T(8,128)} custom-call(f32[8,128]{1,0:T(8,128)S(1)} %add.7.refs_0_, f32[8,128]{1,0:T(8,128)S(1)} %collective-permute-done.11.refs_1_), custom_call_target="tpu_custom_call" | custom-call | tf_op jit(solution)/shard_map/macro/pallas_call | solution.py:490
  (8 shorter events, 0.0 us)
Async XLA Ops:
  0.6 6.0 %copy-start.2 = (f32[8]{0:T(128)S(1)}, f32[8]{0:T(128)}, u32[]{:S(2)}) copy-start(f32[8]{0:T(128)} %param.8) | copy-start | bytes 100
  0.6 6.1 %copy-start.3 = (f32[8]{0:T(128)S(1)}, f32[8]{0:T(128)}, u32[]{:S(2)}) copy-start(f32[8]{0:T(128)} %param.9) | copy-start | bytes 100
  0.7 6.2 %copy-start.1 = (s32[6,8]{1,0:T(8,128)S(1)}, s32[6,8]{1,0:T(8,128)}, u32[]{:S(2)}) copy-start(s32[6,8]{1,0:T(8,128)} %param.6) | copy-start | bytes 580
  0.7 6.4 %copy-start = (f32[3,6,8]{2,1,0:T(8,128)S(1)}, f32[3,6,8]{2,1,0:T(8,128)}, u32[]{:S(2)}) copy-start(f32[3,6,8]{2,1,0:T(8,128)} %param.7) | copy-start | bytes 1732
  3.1 18.7 %collective-permute-start.1 = (f32[3,512,128]{2,1,0:T(8,128)}, f32[3,512,128]{2,1,0:T(8,128)}, u32[]{:S(2)}, u32[]{:S(2)}) collective-permute-start(f32[3,512,128]{2,1,0:T(8,128)} %get-tuple-element.22), channel_id=1, source_target_pairs={{0,4},{8,12},{16,20},{24,28},{4,0},{12,8},{20,16},{28,24},{1,5},{9... | collective-permute-start | bytes 2359304 | tf_op jit(solution)/shard_map/ppermute | solution.py:828
  3.2 21.9 %collective-permute-start = (f32[3,512,128]{2,1,0:T(8,128)}, f32[3,512,128]{2,1,0:T(8,128)S(1)}, u32[]{:S(2)}, u32[]{:S(2)}) collective-permute-start(f32[3,512,128]{2,1,0:T(8,128)} %get-tuple-element.21), channel_id=1, source_target_pairs={{4,8},{12,16},{20,24},{8,4},{16,12},{24,20},{5,9},{13,17},{21,25},... | collective-permute-start | bytes 2359304 | tf_op jit(solution)/shard_map/ppermute | solution.py:828
  9.6 8.8 %collective-permute-start.4 = (f32[8,128]{1,0:T(8,128)S(1)}, f32[8,128]{1,0:T(8,128)S(1)}, u32[]{:S(2)}, u32[]{:S(2)}) collective-permute-start(f32[8,128]{1,0:T(8,128)S(1)} %get-tuple-element.23.refs_0_), channel_id=1, source_target_pairs={{0,3},{1,2},{2,1},{3,0},{4,7},{5,6},{6,5},{7,4},{8,11},{9,10},{10,... | collective-permute-start | bytes 12296 | tf_op jit(solution)/shard_map/ppermute | solution.py:444
  13.2 5.1 %collective-permute-start.3 = (f32[8,128]{1,0:T(8,128)S(1)}, f32[8,128]{1,0:T(8,128)S(1)}, u32[]{:S(2)}, u32[]{:S(2)}) collective-permute-start(f32[8,128]{1,0:T(8,128)S(1)} %get-tuple-element.23.refs_0_), channel_id=1, source_target_pairs={{0,2},{1,3},{2,0},{3,1},{4,6},{5,7},{6,4},{7,5},{8,10},{9,11},{10,... | collective-permute-start | bytes 12296 | tf_op jit(solution)/shard_map/ppermute | solution.py:444
  13.2 5.1 %collective-permute-start.2 = (f32[8,128]{1,0:T(8,128)S(1)}, f32[8,128]{1,0:T(8,128)S(1)}, u32[]{:S(2)}, u32[]{:S(2)}) collective-permute-start(f32[8,128]{1,0:T(8,128)S(1)} %get-tuple-element.23.refs_0_), channel_id=1, source_target_pairs={{0,1},{1,0},{2,3},{3,2},{4,5},{5,4},{6,7},{7,6},{8,9},{9,8},{10,11... | collective-permute-start | bytes 12296 | tf_op jit(solution)/shard_map/ppermute | solution.py:444
  23.6 19.6 %collective-permute-start.6 = (f32[3,512,128]{2,1,0:T(8,128)S(1)}, f32[3,512,128]{2,1,0:T(8,128)S(1)}, u32[]{:S(2)}, u32[]{:S(2)}) collective-permute-start(f32[3,512,128]{2,1,0:T(8,128)S(1)} %get-tuple-element.29), channel_id=1, source_target_pairs={{0,4},{8,12},{16,20},{24,28},{4,0},{12,8},{20,16},{28,24},{1,5},{9... | collective-permute-start | bytes 2359304 | tf_op jit(solution)/shard_map/ppermute | solution.py:828
  25.8 20.8 %collective-permute-start.5 = (f32[3,512,128]{2,1,0:T(8,128)S(1)}, f32[3,512,128]{2,1,0:T(8,128)S(1)}, u32[]{:S(2)}, u32[]{:S(2)}) collective-permute-start(f32[3,512,128]{2,1,0:T(8,128)S(1)} %get-tuple-element.27), channel_id=1, source_target_pairs={{4,8},{12,16},{20,24},{8,4},{16,12},{24,20},{5,9},{13,17},{21,25},... | collective-permute-start | bytes 2359304 | tf_op jit(solution)/shard_map/ppermute | solution.py:828
  31.0 7.6 %collective-permute-start.9 = (f32[8,128]{1,0:T(8,128)S(1)}, f32[8,128]{1,0:T(8,128)S(1)}, u32[]{:S(2)}, u32[]{:S(2)}) collective-permute-start(f32[8,128]{1,0:T(8,128)S(1)} %local_sums.1.refs_1_), channel_id=1, source_target_pairs={{0,3},{1,2},{2,1},{3,0},{4,7},{5,6},{6,5},{7,4},{8,11},{9,10},{10,... | collective-permute-start | bytes 12296 | tf_op jit(solution)/shard_map/ppermute | solution.py:444
  34.6 4.5 %collective-permute-start.8 = (f32[8,128]{1,0:T(8,128)S(1)}, f32[8,128]{1,0:T(8,128)S(1)}, u32[]{:S(2)}, u32[]{:S(2)}) collective-permute-start(f32[8,128]{1,0:T(8,128)S(1)} %local_sums.1.refs_1_), channel_id=1, source_target_pairs={{0,2},{1,3},{2,0},{3,1},{4,6},{5,7},{6,4},{7,5},{8,10},{9,11},{10,... | collective-permute-start | bytes 12296 | tf_op jit(solution)/shard_map/ppermute | solution.py:444
  34.6 4.5 %collective-permute-start.7 = (f32[8,128]{1,0:T(8,128)S(1)}, f32[8,128]{1,0:T(8,128)S(1)}, u32[]{:S(2)}, u32[]{:S(2)}) collective-permute-start(f32[8,128]{1,0:T(8,128)S(1)} %local_sums.1.refs_1_), channel_id=1, source_target_pairs={{0,1},{1,0},{2,3},{3,2},{4,5},{5,4},{6,7},{7,6},{8,9},{9,8},{10,11... | collective-permute-start | bytes 12296 | tf_op jit(solution)/shard_map/ppermute | solution.py:444
  48.1 4.4 %collective-permute-start.10 = (f32[8,128]{1,0:T(8,128)S(1)}, f32[8,128]{1,0:T(8,128)S(1)}, u32[]{:S(2)}, u32[]{:S(2)}) collective-permute-start(f32[8,128]{1,0:T(8,128)S(1)} %get-tuple-element.33), channel_id=1, source_target_pairs={{0,1},{1,0},{2,3},{3,2},{4,5},{5,4},{6,7},{7,6},{8,9},{9,8},{10,11... | collective-permute-start | bytes 12296 | tf_op jit(solution)/shard_map/ppermute | solution.py:452
  52.6 4.6 %collective-permute-start.11 = (f32[8,128]{1,0:T(8,128)S(1)}, f32[8,128]{1,0:T(8,128)S(1)}, u32[]{:S(2)}, u32[]{:S(2)}) collective-permute-start(f32[8,128]{1,0:T(8,128)S(1)} %add.7.refs_0_), channel_id=1, source_target_pairs={{0,2},{1,3},{2,0},{3,1},{4,6},{5,7},{6,4},{7,5},{8,10},{9,11},{10,... | collective-permute-start | bytes 12296 | tf_op jit(solution)/shard_map/ppermute | solution.py:453

commit v13 on v12

--- a/solution.py
+++ b/solution.py
@@ -157,7 +157,7 @@
     )
 
 
-def polynomial_sums(f_ref, planes, parts_ref):
+def polynomial_sums(f_ref, planes, parts_ref, first=0):
     half = planes // 2
 
     def cell(g, _):
@@ -178,10 +178,10 @@
             terms = (y0, y1, y2, y3, b * y0, b * y1, b * y2, bb * y0, bb * y1, bb * (b * y0))
             out = [x if o is None else o + x for o, x in zip(out, terms)]
         for p in range(10):
-            parts_ref[p, at_rows(g * SUB), :] = out[p]
-        return 0
-
-    lax.fori_loop(0, SUB, cell, 0)
+            parts_ref[p, at_rows((first + g) * SUB), :] = out[p]
+        return 0
+
+    lax.fori_loop(0, f_ref.shape[0], cell, 0)
     return [over_sublanes(parts_ref, p) for p in range(10)]
 
 
@@ -339,7 +339,7 @@
     )(links, geo, native)
 
 
-SPLIT_PARTS = 4
+SPLIT_PARTS = 8
 
 
 def is_odd():
@@ -589,10 +589,11 @@
 
 
 def target_kernel(count, links_ref, geo_ref, absorbed_in, *refs):
-    sums_refs, (f_ref, part_ref, out_ref, sum_out, ta, tiles_ref, coef, cells, faces) = refs[:count], refs[count:]
+    sums_refs, (f_ref, part_ref, out_ref, *sum_out, ta, tiles_ref, coef, cells, faces) = refs[:count], refs[count:]
     planes = f_ref.shape[1] // CHUNKS
     sums = add_tiles(sums_refs)
-    sum_out[...] = sums
+    for ref in sum_out:
+        ref[...] = sums
     absorbed = sums if absorbed_in is None else absorbed_in[...]
     n, u, temperature, q = quantities(sums)
     rt = 1.0 / temperature
@@ -702,8 +703,8 @@
     return pl.pallas_call(
         kernel,
         in_specs=[spec(pltpu.SMEM)] + [vmem] * (len(given) - 1),
-        out_specs=[vmem] * 2,
-        out_shape=[array(*part.shape), array(SUB, LANES)],
+        out_specs=[vmem] * (2 if absorbed is None else 1),
+        out_shape=[array(*part.shape)] + ([array(SUB, LANES)] if absorbed is None else []),
         input_output_aliases={len(given) - 1: 0},
         scratch_shapes=[
                 pltpu.VMEM((4, rows // CHUNKS, SUB, LANES), F32),
@@ -742,7 +743,7 @@
         run(not far)
 
 
-def edge_kernel(far, pairs_ref, halo_ref, old_ref, part_ref, f_ref, *rows_refs):
+def add_side(far, pairs_ref, halo_ref, old_ref, part_ref, f_ref, rows_ref):
     def run(high):
         def group(j, _):
             at = at_rows(j * SUB)
@@ -750,7 +751,7 @@
             for e in range(REACH):
                 x = part_ref[first + e, at, :] + terms[e]
                 f_ref[first + e, at, :] = x
-                for rows_ref in rows_refs:
+                if rows_ref is not None:
                     rows_ref[e, at, :] = x
             return 0
 
@@ -760,13 +761,13 @@
     for_side(far, run)
 
 
-def edge(far, pairs, halo, old, part, keep_rows):
+def edge(far, pairs, halo, old, part):
     rows = part.shape[1]
     return pl.pallas_call(
-        functools.partial(edge_kernel, far),
+        functools.partial(add_side, far),
         in_specs=[spec(pltpu.VMEM)] * 4,
-        out_specs=[spec(pltpu.VMEM)] * (2 if keep_rows else 1),
-        out_shape=[array(SUB, rows, LANES), array(REACH, rows, LANES)][: 2 if keep_rows else 1],
+        out_specs=[spec(pltpu.VMEM)] * 2,
+        out_shape=[array(SUB, rows, LANES), array(REACH, rows, LANES)],
         input_output_aliases={3: 0},
         compiler_params=params(),
         cost_estimate=traffic(rows, 2),
@@ -774,25 +775,82 @@
     )(pairs, halo, old, part)
 
 
-def last_edge_kernel(geo_ref, pairs_ref, far_ref, f_ref, part_ref, out_hbm, sums_out, native_ref, sems):
-    rows = part_ref.shape[1]
+def last_near_kernel(geo_ref, pairs_ref, halo_ref, old_ref, part_ref, f_ref, sums_out, parts_ref):
+    add_side(False, pairs_ref, halo_ref, old_ref, part_ref, f_ref, None)
+    planes = f_ref.shape[1] // CHUNKS
+    y = polynomial_sums(f_ref, planes, parts_ref)
+    sums_out[...] = pack_sums(finish_polynomials(y, geo_ref[FIRST], planes), 0)
+
+
+def last_near(geo, pairs, near, old, part):
+    rows = part.shape[1]
+    return pl.pallas_call(
+        last_near_kernel,
+        in_specs=[spec(pltpu.VMEM)] * 5,
+        out_specs=[spec(pltpu.VMEM)] * 2,
+        out_shape=[array(SUB, rows, LANES), array(SUB, LANES)],
+        input_output_aliases={4: 0},
+        scratch_shapes=[pltpu.VMEM((10, SUB * SUB, LANES), F32)],
+        compiler_params=params(),
+        cost_estimate=traffic(rows, 3),
+        name="last_near",
+    )(geo, pairs, near, old, part)
+
+
+def last_far_kernel(geo_ref, pairs_ref, halo_ref, old_ref, sums_in, terms_ref, sums_out, parts_ref):
+    rows = old_ref.shape[1]
     planes = rows // CHUNKS
-    part = rows // SUB // LAST_PARTS
+    parts_ref[...] = jnp.zeros_like(parts_ref)
+
+    def run(high):
+        def group(j, _):
+            at = at_rows(j * SUB)
+            _first, terms = side_terms(high, pairs_ref, halo_ref, old_ref, at)
+            for e in range(REACH):
+                terms_ref[e, at, :] = terms[e]
+            return 0
+
+        lax.fori_loop(0, rows // SUB, group, 0, unroll=unroll(rows // SUB, 8))
+        y = polynomial_sums(terms_ref, planes, parts_ref, SUB - REACH if high else 0)
+        sums_out[...] = sums_in[...] + pack_sums(finish_polynomials(y, geo_ref[FIRST], planes), 0)
+
+    for_side(True, run)
+
+
+def last_far(geo, pairs, far, old, sums):
+    rows = old.shape[1]
+    return pl.pallas_call(
+        last_far_kernel,
+        in_specs=[spec(pltpu.VMEM)] * 5,
+        out_specs=[spec(pltpu.VMEM)] * 2,
+        out_shape=[array(REACH, rows, LANES), array(SUB, LANES)],
+        scratch_shapes=[pltpu.VMEM((10, SUB * SUB, LANES), F32)],
+        compiler_params=params(),
+        cost_estimate=traffic(rows, 2),
+        name="last_far",
+    )(geo, pairs, far, old, sums)
+
+
+LAST_PARTS = 4
+
+
+def result_kernel(part_ref, terms_ref, out_hbm, native_ref, sems):
+    part = part_ref.shape[1] // SUB // LAST_PARTS
 
     def copy(i):
         at = pl.ds(i * part * SUB * SUB, part * SUB * SUB)
         return pltpu.make_async_copy(native_ref.at[at], out_hbm.at[at], sems.at[i])
 
     def run(high):
+        first = SUB - REACH if high else 0
         for i in range(LAST_PARTS):
 
             def group(j, _):
                 at = at_rows(j * SUB)
-                first, terms = side_terms(high, pairs_ref, far_ref, f_ref, at)
                 for g in range(SUB):
                     x = part_ref[g, at, :]
                     if 0 <= g - first < REACH:
-                        x = x + terms[g - first]
+                        x = x + terms_ref[g - first, at, :]
                     native_ref[pl.ds(j * SUB * SUB + g, SUB, stride=SUB), :] = x
                 return 0
 
@@ -800,27 +858,23 @@
             copy(i).start()
 
     for_side(True, run)
-    y = native_polynomial_sums(native_ref, planes)
-    sums_out[...] = pack_sums(finish_polynomials(y, geo_ref[FIRST], planes), 0)
     for i in range(LAST_PARTS):
         copy(i).wait()
 
 
-LAST_PARTS = 4
-
-
-def last_edge(geo, pairs, far, f, part):
-    native = (SUB * part.shape[1], LANES)
+def result(part, terms):
+    rows = part.shape[1]
+    native = (SUB * rows, LANES)
     return pl.pallas_call(
-        last_edge_kernel,
-        in_specs=[spec(pltpu.VMEM)] * 5,
-        out_specs=[spec(pltpu.HBM), spec(pltpu.VMEM)],
-        out_shape=[array(*native), array(SUB, LANES)],
+        result_kernel,
+        in_specs=[spec(pltpu.VMEM)] * 2,
+        out_specs=spec(pltpu.HBM),
+        out_shape=array(*native),
         scratch_shapes=[pltpu.VMEM(native, F32), pltpu.SemaphoreType.DMA((LAST_PARTS,))],
         compiler_params=params(),
-        cost_estimate=traffic(part.shape[1], 4),
-        name="last_edge",
-    )(geo, pairs, far, f, part)
+        cost_estimate=traffic(rows, 3),
+        name="result",
+    )(part, terms)
 
 
 def swap(rows, start):
@@ -854,16 +908,18 @@
     tiles = gather_sums(sums)
     part, pairs = flux(True, links, geo, f)
     part, absorbed = add_target(links, geo, None, tiles, f, part)
-    part, near = edge(False, pairs, near, f, part, True)
+    part, near = edge(False, pairs, near, f, part)
     near = swap(near, 0)
-    f, far = edge(True, pairs, far, f, part, True)
+    f, far = edge(True, pairs, far, f, part)
     far = swap(far, 1)
     tiles = gather_sums(local_sums(links, geo, f))
     (part,) = flux(False, links, geo, f)
-    part, _ = add_target(links, geo, absorbed, tiles, f, part)
-    (part,) = edge(False, pairs, near, f, part, False)
-    native, sums = last_edge(geo, pairs, far, f, part)
-    macro_quantities = macro(doubling_sums(sums))
+    (part,) = add_target(links, geo, absorbed, tiles, f, part)
+    part, sums = last_near(geo, pairs, near, f, part)
+    terms, sums = last_far(geo, pairs, far, f, sums)
+    tiles = doubling_sums(sums)
+    native = result(part, terms)
+    macro_quantities = macro(tiles)
     evolved = native.reshape(rows, cells, LANES).transpose(1, 0, 2).reshape(cells, points)
     return evolved, macro_quantities
 

time: 58.4 us -> 57.4 us (0.983)
  waiting for transfers between devices: 8.09 us -> 6.33 us
  Pallas kernels: 26.2 us -> 27 us
    ppermute x1, waiting for transfers between devices: 1.58 us -> 0.13 us  [doubling_sums(): return [pair, lax.ppermute(pair, 'vel', [(i, i ^ 2) for i in range(size)])]]
    pallas_call x4 -> x5, Pallas kernels: 4.43 us -> 5.48 us  [the longest x2 2.36 us: edge(): pl.pallas_call(functools.partial(add_side, far), in_specs=[spec(pltpu.VME...]
  transfers between devices with their start and end apart: 12 -> 12, of which waited for: 5 -> 5; matrix products, arithmetic and copies ran while one was open for 1% -> 1% of each run, Pallas kernels for 37% -> 41%
where the time goes in v13:
time: 57.4 us; the launch traced here: 56.9 us
  Pallas kernels  27 us (47%)
  starting transfers between devices  22 us (38%)
  waiting for transfers between devices  6.33 us (11%)
  between operations  0.83 us (1%)
  local copies, waits for them, and re-layouts  0.69 us (1%)
    ppermute x6, starting transfers between devices, gather_sums(): lax.ppermute(tile, 'vel', [(i, i ^ s) for i in range(size)])  8.84 us
    ppermute x4, starting transfers between devices, swap(): return lax.ppermute(rows, 'space', pairs + [(j, i) for i, j in pairs])  7.3 us
    pallas_call x2, Pallas kernels, flux(): pl.pallas_call(functools.partial(flux_kernel, with_pairs), in_specs=[spec...  7.24 us
    pallas_call x2, Pallas kernels, add_target(): pl.pallas_call(kernel, in_specs=[spec(pltpu.SMEM)] + [vmem] * (len(given)...  7.14 us
    ppermute x4, waiting for transfers between devices, swap(): return lax.ppermute(rows, 'space', pairs + [(j, i) for i, j in pairs])  3.86 us
    ppermute x1, starting transfers between devices, doubling_sums(): return [pair, lax.ppermute(pair, 'vel', [(i, i ^ 2) for i in range(size)])]  3.03 us
    ppermute x1, starting transfers between devices, doubling_sums(): pair = tile + lax.ppermute(tile, 'vel', [(i, i ^ 1) for i in range(size)])  2.84 us
    pallas_call x1, Pallas kernels, first_rows(): pl.pallas_call(first_rows_kernel, in_specs=[spec(pltpu.HBM)], out_specs=[...  2.45 us
  transfers between devices with their start and end apart: 12, of which 5 were waited for; matrix products, arithmetic and copies ran while one was open for 1% of the time, Pallas kernels for 41%

profile of v13, /device:TPU:4, one launch (start us, length us, event | category | flops | bytes accessed | tf_op | source)
XLA Modules:
  0.0 56.9 jit_solution(15102657972984416386)
XLA Ops:
  0.6 0.0 copy-start.2
  0.6 0.0 copy-start.3
  0.7 2.5 %first_rows.1 = (f32[4096,128]{1,0:T(8,128)S(1)}, f32[3,512,128]{2,1,0:T(8,128)}, f32[3,512,128]{2,1,0:T(8,128)}) custom-call(f32[4096,128]{1,0:T(8,128)} %bitcast.12), custom_call_target="tpu_custom_call" | custom-call | flops 16777216 | bytes 8388608 | tf_op jit(solution)/shard_map/first_rows/pallas_call | solution.py:389
  3.1 0.1 collective-permute-start
  3.2 3.4 %collective-permute-start.5 = (f32[3,512,128]{2,1,0:T(8,128)}, f32[3,512,128]{2,1,0:T(8,128)S(1)}, u32[]{:S(2)}, u32[]{:S(2)}) collective-permute-start(f32[3,512,128]{2,1,0:T(8,128)} %get-tuple-element.27), channel_id=1, source_target_pairs={{4,8},{12,16},{20,24},{8,4},{16,12},{24,20},{5,9},{13,17},{21,25},... | collective-permute-start | bytes 2359304 | tf_op jit(solution)/shard_map/ppermute | solution.py:882
  6.7 0.1 copy.13
  6.7 0.0 copy-done.3
  6.8 0.1 copy.14
  6.8 0.1 copy.16
  6.9 0.1 copy.15
  7.0 0.1 copy.18
  7.1 0.1 concatenate.3
  7.2 0.1 copy.17
  7.3 0.1 broadcast_in_dim.23.geo_ref.geo_in
  7.4 2.4 %first_sums.1 = (f32[8,512,128]{2,1,0:T(8,128)S(1)}, f32[8,128]{1,0:T(8,128)S(1)}) custom-call(s32[6,8]{1,0:T(8,128)S(1)} %get-tuple-element.37.links_ref, f32[33,8,128]{2,1,0:T(8,128)S(1)} %broadcast_in_dim.23.geo_ref.geo_in, f32[4096,128]{1,0:T(8,128)S(1)} %get-tuple-element.19.native_ref), custom_call_target="tpu_custom_call" | custom-call | flops 20971520 | bytes 10485760 | tf_op jit(solution)/shard_map/first_sums/pallas_call | solution.py:327
  9.8 3.7 %collective-permute-start.3 = (f32[8,128]{1,0:T(8,128)S(1)}, f32[8,128]{1,0:T(8,128)S(1)}, u32[]{:S(2)}, u32[]{:S(2)}) collective-permute-start(f32[8,128]{1,0:T(8,128)S(1)} %get-tuple-element.23.refs_0_), channel_id=1, source_target_pairs={{0,3},{1,2},{2,1},{3,0},{4,7},{5,6},{6,5},{7,4},{8,11},{9,10},{10,... | collective-permute-start | bytes 12296 | tf_op jit(solution)/shard_map/ppermute | solution.py:444
  13.4 0.0 collective-permute-start.2
  13.4 0.8 %collective-permute-start.1 = (f32[8,128]{1,0:T(8,128)S(1)}, f32[8,128]{1,0:T(8,128)S(1)}, u32[]{:S(2)}, u32[]{:S(2)}) collective-permute-start(f32[8,128]{1,0:T(8,128)S(1)} %get-tuple-element.23.refs_0_), channel_id=1, source_target_pairs={{0,1},{1,0},{2,3},{3,2},{4,5},{5,4},{6,7},{7,6},{8,9},{9,8},{10,11... | collective-permute-start | bytes 12296 | tf_op jit(solution)/shard_map/ppermute | solution.py:444
  14.2 4.3 %flux.2 = (f32[8,512,128]{2,1,0:T(8,128)S(1)}, f32[12,512,128]{2,1,0:T(8,128)S(1)}) custom-call(s32[6,8]{1,0:T(8,128)S(1)} %get-tuple-element.37.links_ref, f32[33,8,128]{2,1,0:T(8,128)S(1)} %broadcast_in_dim.23.geo_ref.geo_in, f32[8,512,128]{2,1,0:T(8,128)S(1)} %get-tuple-element.20.f_ref.refs_4_.old_ref), custom_call_target="tpu_custom_call" | custom-call | flops 37748736 | bytes 18874368 | tf_op jit(solution)/shard_map/flux/pallas_call | solution.py:572
  18.5 0.0 collective-permute-done.3.refs_3_
  18.5 0.0 collective-permute-done.2.refs_2_
  18.5 0.0 collective-permute-done.1.refs_1_
  18.5 3.6 %add_target.2 = (f32[8,512,128]{2,1,0:T(8,128)S(1)}, f32[8,128]{1,0:T(8,128)S(1)}) custom-call(s32[6,8]{1,0:T(8,128)S(1)} %get-tuple-element.37.links_ref, f32[33,8,128]{2,1,0:T(8,128)S(1)} %broadcast_in_dim.23.geo_ref.geo_in, f32[8,128]{1,0:T(8,128)S(1)} %get-tuple-element.23.refs_0_, ...), custom_call_target="tpu_custom_call", output_to_operand_aliasing={{0}: (7, {})} | custom-call | flops 29360128 | bytes 14680064 | tf_op jit(solution)/shard_map/add_target/pallas_call | solution.py:703
  22.1 0.0 collective-permute-done.halo_ref
  22.1 1.7 %near_edge.1 = (f32[8,512,128]{2,1,0:T(8,128)S(1)}, f32[3,512,128]{2,1,0:T(8,128)S(1)}) custom-call(f32[12,512,128]{2,1,0:T(8,128)S(1)} %get-tuple-element.21.pairs_ref, f32[3,512,128]{2,1,0:T(8,128)} %collective-permute-done.halo_ref, f32[8,512,128]{2,1,0:T(8,128)S(1)} %get-tuple-element.20.f_ref.refs_4_.old_ref, ...), custom_call_target="tpu_custom_call", output_to_operand_aliasing={{0}: (3, {})} | custom-call | flops 8388608 | bytes 4194304 | tf_op jit(solution)/shard_map/near_edge/pallas_call | solution.py:766
  23.9 0.1 collective-permute-start.4
  23.9 1.2 %collective-permute-done.5.halo_ref = f32[3,512,128]{2,1,0:T(8,128)S(1)} collective-permute-done((f32[3,512,128]{2,1,0:T(8,128)}, f32[3,512,128]{2,1,0:T(8,128)S(1)}, u32[]{:S(2)}, u32[]{:S(2)}) %collective-permute-start.5) | collective-permute-done | bytes 786464 | tf_op jit(solution)/shard_map/ppermute | solution.py:882
  25.2 0.6 %far_edge.1 = (f32[8,512,128]{2,1,0:T(8,128)S(1)}, f32[3,512,128]{2,1,0:T(8,128)S(1)}) custom-call(f32[12,512,128]{2,1,0:T(8,128)S(1)} %get-tuple-element.21.pairs_ref, f32[3,512,128]{2,1,0:T(8,128)S(1)} %collective-permute-done.5.halo_ref, f32[8,512,128]{2,1,0:T(8,128)S(1)} %get-tuple-element.20.f_ref.refs_4_.old_ref, ...), custom_call_target="tpu_custom_call", output_to_operand_aliasing={{0}: (3, {})} | custom-call | flops 8388608 | bytes 4194304 | tf_op jit(solution)/shard_map/far_edge/pallas_call | solution.py:766
  25.8 3.7 %collective-permute-start.9 = (f32[3,512,128]{2,1,0:T(8,128)S(1)}, f32[3,512,128]{2,1,0:T(8,128)S(1)}, u32[]{:S(2)}, u32[]{:S(2)}) collective-permute-start(f32[3,512,128]{2,1,0:T(8,128)S(1)} %get-tuple-element.32), channel_id=1, source_target_pairs={{4,8},{12,16},{20,24},{8,4},{16,12},{24,20},{5,9},{13,17},{21,25},... | collective-permute-start | bytes 2359304 | tf_op jit(solution)/shard_map/ppermute | solution.py:882
  29.5 1.6 %local_sums.1.refs_1_ = f32[8,128]{1,0:T(8,128)S(1)} custom-call(s32[6,8]{1,0:T(8,128)S(1)} %get-tuple-element.37.links_ref, f32[33,8,128]{2,1,0:T(8,128)S(1)} %broadcast_in_dim.23.geo_ref.geo_in, f32[8,512,128]{2,1,0:T(8,128)S(1)} %get-tuple-element.29.f_ref.refs_5_.old_ref), custom_call_target="tpu_custom_call" | custom-call | flops 16777216 | bytes 8388608 | tf_op jit(solution)/shard_map/local_sums/pallas_call | solution.py:309
  31.1 3.6 %collective-permute-start.8 = (f32[8,128]{1,0:T(8,128)S(1)}, f32[8,128]{1,0:T(8,128)S(1)}, u32[]{:S(2)}, u32[]{:S(2)}) collective-permute-start(f32[8,128]{1,0:T(8,128)S(1)} %local_sums.1.refs_1_), channel_id=1, source_target_pairs={{0,3},{1,2},{2,1},{3,0},{4,7},{5,6},{6,5},{7,4},{8,11},{9,10},{10,... | collective-permute-start | bytes 12296 | tf_op jit(solution)/shard_map/ppermute | solution.py:444
  34.7 0.0 collective-permute-start.7
  34.7 0.8 %collective-permute-start.6 = (f32[8,128]{1,0:T(8,128)S(1)}, f32[8,128]{1,0:T(8,128)S(1)}, u32[]{:S(2)}, u32[]{:S(2)}) collective-permute-start(f32[8,128]{1,0:T(8,128)S(1)} %local_sums.1.refs_1_), channel_id=1, source_target_pairs={{0,1},{1,0},{2,3},{3,2},{4,5},{5,4},{6,7},{7,6},{8,9},{9,8},{10,11... | collective-permute-start | bytes 12296 | tf_op jit(solution)/shard_map/ppermute | solution.py:444
  35.5 3.0 %flux.3.refs_6_ = f32[8,512,128]{2,1,0:T(8,128)S(1)} custom-call(s32[6,8]{1,0:T(8,128)S(1)} %get-tuple-element.37.links_ref, f32[33,8,128]{2,1,0:T(8,128)S(1)} %broadcast_in_dim.23.geo_ref.geo_in, f32[8,512,128]{2,1,0:T(8,128)S(1)} %get-tuple-element.29.f_ref.refs_5_.old_ref), custom_call_target="tpu_custom_call" | custom-call | flops 29360128 | bytes 14680064 | tf_op jit(solution)/shard_map/flux/pallas_call | solution.py:572
  38.5 0.0 collective-permute-done.8.refs_4_
  38.5 0.7 %collective-permute-done.7.refs_3_ = f32[8,128]{1,0:T(8,128)S(1)} collective-permute-done((f32[8,128]{1,0:T(8,128)S(1)}, f32[8,128]{1,0:T(8,128)S(1)}, u32[]{:S(2)}, u32[]{:S(2)}) %collective-permute-start.7) | collective-permute-done | bytes 4128 | tf_op jit(solution)/shard_map/ppermute | solution.py:444
  39.2 0.0 collective-permute-done.6.refs_2_
  39.2 3.5 %add_target.3.part_ref = f32[8,512,128]{2,1,0:T(8,128)S(1)} custom-call(s32[6,8]{1,0:T(8,128)S(1)} %get-tuple-element.37.links_ref, f32[33,8,128]{2,1,0:T(8,128)S(1)} %broadcast_in_dim.23.geo_ref.geo_in, f32[8,128]{1,0:T(8,128)S(1)} %get-tuple-element.30.refs_0_, f32[8,128]{1,0:T(8,128)S(1)} %local_sums.1.refs_1_, ...), custom_call_target="tpu_custom_call", output_to_operand_aliasing={{}: (8, {})} | custom-call | flops 29360128 | bytes 14680064 | tf_op jit(solution)/shard_map/add_target/pallas_call | solution.py:703
  42.8 0.0 collective-permute-done.4.halo_ref
  42.8 1.2 %last_near.1 = (f32[8,512,128]{2,1,0:T(8,128)S(1)}, f32[8,128]{1,0:T(8,128)S(1)}) custom-call(f32[33,8,128]{2,1,0:T(8,128)S(1)} %broadcast_in_dim.23.geo_ref.geo_in, f32[12,512,128]{2,1,0:T(8,128)S(1)} %get-tuple-element.21.pairs_ref, f32[3,512,128]{2,1,0:T(8,128)S(1)} %collective-permute-done.4.halo_ref, ...), custom_call_target="tpu_custom_call", output_to_operand_aliasing={{0}: (4, {})} | custom-call | flops 12582912 | bytes 6291456 | tf_op jit(solution)/shard_map/last_near/pallas_call | solution.py:787
  44.0 2.6 %collective-permute-done.9.halo_ref = f32[3,512,128]{2,1,0:T(8,128)S(1)} collective-permute-done((f32[3,512,128]{2,1,0:T(8,128)S(1)}, f32[3,512,128]{2,1,0:T(8,128)S(1)}, u32[]{:S(2)}, u32[]{:S(2)}) %collective-permute-start.9) | collective-permute-done | bytes 786464 | tf_op jit(solution)/shard_map/ppermute | solution.py:882
  46.6 0.5 last_far.1
  47.1 2.8 %collective-permute-start.10 = (f32[8,128]{1,0:T(8,128)S(1)}, f32[8,128]{1,0:T(8,128)S(1)}, u32[]{:S(2)}, u32[]{:S(2)}) collective-permute-start(f32[8,128]{1,0:T(8,128)S(1)} %get-tuple-element.35), channel_id=1, source_target_pairs={{0,1},{1,0},{2,3},{3,2},{4,5},{5,4},{6,7},{7,6},{8,9},{9,8},{10,11... | collective-permute-start | bytes 12296 | tf_op jit(solution)/shard_map/ppermute | solution.py:452
  50.0 1.6 %collective-permute-done.10 = f32[8,128]{1,0:T(8,128)S(1)} collective-permute-done((f32[8,128]{1,0:T(8,128)S(1)}, f32[8,128]{1,0:T(8,128)S(1)}, u32[]{:S(2)}, u32[]{:S(2)}) %collective-permute-start.10) | collective-permute-done | bytes 4128 | tf_op jit(solution)/shard_map/ppermute | solution.py:452
  51.5 3.0 %collective-permute-start.11 = (f32[8,128]{1,0:T(8,128)S(1)}, f32[8,128]{1,0:T(8,128)S(1)}, u32[]{:S(2)}, u32[]{:S(2)}) collective-permute-start(f32[8,128]{1,0:T(8,128)S(1)} %add.7.refs_0_), channel_id=1, source_target_pairs={{0,2},{1,3},{2,0},{3,1},{4,6},{5,7},{6,4},{7,5},{8,10},{9,11},{10,... | collective-permute-start | bytes 12296 | tf_op jit(solution)/shard_map/ppermute | solution.py:453
  54.6 1.4 %result.1 = f32[4096,128]{1,0:T(8,128)} custom-call(f32[8,512,128]{2,1,0:T(8,128)S(1)} %get-tuple-element.31.part_ref, f32[3,512,128]{2,1,0:T(8,128)S(1)} %get-tuple-element.34.terms_ref), custom_call_target="tpu_custom_call" | custom-call | flops 12582912 | bytes 6291456 | tf_op jit(solution)/shard_map/result/pallas_call | solution.py:868
  56.0 0.1 collective-permute-done.11.refs_1_
  56.2 0.7 %macro.1 = f32[8,8]{1,0:T(8,128)} custom-call(f32[8,128]{1,0:T(8,128)S(1)} %add.7.refs_0_, f32[8,128]{1,0:T(8,128)S(1)} %collective-permute-done.11.refs_1_), custom_call_target="tpu_custom_call" | custom-call | tf_op jit(solution)/shard_map/macro/pallas_call | solution.py:490
  (9 shorter events, 0.0 us)
Async XLA Ops:
  0.6 6.0 %copy-start.2 = (f32[8]{0:T(128)S(1)}, f32[8]{0:T(128)}, u32[]{:S(2)}) copy-start(f32[8]{0:T(128)} %param.8) | copy-start | bytes 100
  0.6 6.1 %copy-start.3 = (f32[8]{0:T(128)S(1)}, f32[8]{0:T(128)}, u32[]{:S(2)}) copy-start(f32[8]{0:T(128)} %param.9) | copy-start | bytes 100
  0.7 6.2 %copy-start.1 = (s32[6,8]{1,0:T(8,128)S(1)}, s32[6,8]{1,0:T(8,128)}, u32[]{:S(2)}) copy-start(s32[6,8]{1,0:T(8,128)} %param.6) | copy-start | bytes 580
  0.7 6.3 %copy-start = (f32[3,6,8]{2,1,0:T(8,128)S(1)}, f32[3,6,8]{2,1,0:T(8,128)}, u32[]{:S(2)}) copy-start(f32[3,6,8]{2,1,0:T(8,128)} %param.7) | copy-start | bytes 1732
  3.1 19.0 %collective-permute-start = (f32[3,512,128]{2,1,0:T(8,128)}, f32[3,512,128]{2,1,0:T(8,128)}, u32[]{:S(2)}, u32[]{:S(2)}) collective-permute-start(f32[3,512,128]{2,1,0:T(8,128)} %get-tuple-element.22), channel_id=1, source_target_pairs={{0,4},{8,12},{16,20},{24,28},{4,0},{12,8},{20,16},{28,24},{1,5},{9... | collective-permute-start | bytes 2359304 | tf_op jit(solution)/shard_map/ppermute | solution.py:882
  3.2 21.9 %collective-permute-start.5 = (f32[3,512,128]{2,1,0:T(8,128)}, f32[3,512,128]{2,1,0:T(8,128)S(1)}, u32[]{:S(2)}, u32[]{:S(2)}) collective-permute-start(f32[3,512,128]{2,1,0:T(8,128)} %get-tuple-element.27), channel_id=1, source_target_pairs={{4,8},{12,16},{20,24},{8,4},{16,12},{24,20},{5,9},{13,17},{21,25},... | collective-permute-start | bytes 2359304 | tf_op jit(solution)/shard_map/ppermute | solution.py:882
  9.8 8.7 %collective-permute-start.3 = (f32[8,128]{1,0:T(8,128)S(1)}, f32[8,128]{1,0:T(8,128)S(1)}, u32[]{:S(2)}, u32[]{:S(2)}) collective-permute-start(f32[8,128]{1,0:T(8,128)S(1)} %get-tuple-element.23.refs_0_), channel_id=1, source_target_pairs={{0,3},{1,2},{2,1},{3,0},{4,7},{5,6},{6,5},{7,4},{8,11},{9,10},{10,... | collective-permute-start | bytes 12296 | tf_op jit(solution)/shard_map/ppermute | solution.py:444
  13.4 5.1 %collective-permute-start.2 = (f32[8,128]{1,0:T(8,128)S(1)}, f32[8,128]{1,0:T(8,128)S(1)}, u32[]{:S(2)}, u32[]{:S(2)}) collective-permute-start(f32[8,128]{1,0:T(8,128)S(1)} %get-tuple-element.23.refs_0_), channel_id=1, source_target_pairs={{0,2},{1,3},{2,0},{3,1},{4,6},{5,7},{6,4},{7,5},{8,10},{9,11},{10,... | collective-permute-start | bytes 12296 | tf_op jit(solution)/shard_map/ppermute | solution.py:444
  13.4 5.1 %collective-permute-start.1 = (f32[8,128]{1,0:T(8,128)S(1)}, f32[8,128]{1,0:T(8,128)S(1)}, u32[]{:S(2)}, u32[]{:S(2)}) collective-permute-start(f32[8,128]{1,0:T(8,128)S(1)} %get-tuple-element.23.refs_0_), channel_id=1, source_target_pairs={{0,1},{1,0},{2,3},{3,2},{4,5},{5,4},{6,7},{7,6},{8,9},{9,8},{10,11... | collective-permute-start | bytes 12296 | tf_op jit(solution)/shard_map/ppermute | solution.py:444
  23.9 18.9 %collective-permute-start.4 = (f32[3,512,128]{2,1,0:T(8,128)S(1)}, f32[3,512,128]{2,1,0:T(8,128)S(1)}, u32[]{:S(2)}, u32[]{:S(2)}) collective-permute-start(f32[3,512,128]{2,1,0:T(8,128)S(1)} %get-tuple-element.26), channel_id=1, source_target_pairs={{0,4},{8,12},{16,20},{24,28},{4,0},{12,8},{20,16},{28,24},{1,5},{9... | collective-permute-start | bytes 2359304 | tf_op jit(solution)/shard_map/ppermute | solution.py:882
  25.8 20.8 %collective-permute-start.9 = (f32[3,512,128]{2,1,0:T(8,128)S(1)}, f32[3,512,128]{2,1,0:T(8,128)S(1)}, u32[]{:S(2)}, u32[]{:S(2)}) collective-permute-start(f32[3,512,128]{2,1,0:T(8,128)S(1)} %get-tuple-element.32), channel_id=1, source_target_pairs={{4,8},{12,16},{20,24},{8,4},{16,12},{24,20},{5,9},{13,17},{21,25},... | collective-permute-start | bytes 2359304 | tf_op jit(solution)/shard_map/ppermute | solution.py:882
  31.1 7.4 %collective-permute-start.8 = (f32[8,128]{1,0:T(8,128)S(1)}, f32[8,128]{1,0:T(8,128)S(1)}, u32[]{:S(2)}, u32[]{:S(2)}) collective-permute-start(f32[8,128]{1,0:T(8,128)S(1)} %local_sums.1.refs_1_), channel_id=1, source_target_pairs={{0,3},{1,2},{2,1},{3,0},{4,7},{5,6},{6,5},{7,4},{8,11},{9,10},{10,... | collective-permute-start | bytes 12296 | tf_op jit(solution)/shard_map/ppermute | solution.py:444
  34.7 4.5 %collective-permute-start.7 = (f32[8,128]{1,0:T(8,128)S(1)}, f32[8,128]{1,0:T(8,128)S(1)}, u32[]{:S(2)}, u32[]{:S(2)}) collective-permute-start(f32[8,128]{1,0:T(8,128)S(1)} %local_sums.1.refs_1_), channel_id=1, source_target_pairs={{0,2},{1,3},{2,0},{3,1},{4,6},{5,7},{6,4},{7,5},{8,10},{9,11},{10,... | collective-permute-start | bytes 12296 | tf_op jit(solution)/shard_map/ppermute | solution.py:444
  34.7 4.5 %collective-permute-start.6 = (f32[8,128]{1,0:T(8,128)S(1)}, f32[8,128]{1,0:T(8,128)S(1)}, u32[]{:S(2)}, u32[]{:S(2)}) collective-permute-start(f32[8,128]{1,0:T(8,128)S(1)} %local_sums.1.refs_1_), channel_id=1, source_target_pairs={{0,1},{1,0},{2,3},{3,2},{4,5},{5,4},{6,7},{7,6},{8,9},{9,8},{10,11... | collective-permute-start | bytes 12296 | tf_op jit(solution)/shard_map/ppermute | solution.py:444
  47.1 4.4 %collective-permute-start.10 = (f32[8,128]{1,0:T(8,128)S(1)}, f32[8,128]{1,0:T(8,128)S(1)}, u32[]{:S(2)}, u32[]{:S(2)}) collective-permute-start(f32[8,128]{1,0:T(8,128)S(1)} %get-tuple-element.35), channel_id=1, source_target_pairs={{0,1},{1,0},{2,3},{3,2},{4,5},{5,4},{6,7},{7,6},{8,9},{9,8},{10,11... | collective-permute-start | bytes 12296 | tf_op jit(solution)/shard_map/ppermute | solution.py:452
  51.5 4.6 %collective-permute-start.11 = (f32[8,128]{1,0:T(8,128)S(1)}, f32[8,128]{1,0:T(8,128)S(1)}, u32[]{:S(2)}, u32[]{:S(2)}) collective-permute-start(f32[8,128]{1,0:T(8,128)S(1)} %add.7.refs_0_), channel_id=1, source_target_pairs={{0,2},{1,3},{2,0},{3,1},{4,6},{5,7},{6,4},{7,5},{8,10},{9,11},{10,... | collective-permute-start | bytes 12296 | tf_op jit(solution)/shard_map/ppermute | solution.py:453

commit v14 on v13

--- a/solution.py
+++ b/solution.py
@@ -339,59 +339,47 @@
     )(links, geo, native)
 
 
-SPLIT_PARTS = 8
-
-
 def is_odd():
     return lax.rem(lax.axis_index("space"), 2) == 1
 
 
-def first_rows_kernel(native_hbm, native_ref, far_any, near_any, far_ref, near_ref, sems, far_sems, near_sems):
-    rows = native_ref.shape[0]
-    part = rows // SPLIT_PARTS
-    copies = [
-        pltpu.make_async_copy(
-            native_hbm.at[pl.ds(i * part, part)], native_ref.at[pl.ds(i * part, part)], sems.at[i]
-        )
-        for i in range(SPLIT_PARTS)
-    ]
-    for c in copies:
-        c.start()
+def first_rows_kernel(native_hbm, native_ref, far_any, near_any, sem, far_sems, near_sems):
+    whole = pltpu.make_async_copy(native_hbm, native_ref, sem)
+
+    def copies(far, near):
+        out = []
+        for r in range(REACH):
+            out.append(pltpu.make_async_copy(native_hbm.at[:, far + r, :], far_any.at[r], far_sems.at[r]))
+            out.append(pltpu.make_async_copy(native_hbm.at[:, near + r, :], near_any.at[r], near_sems.at[r]))
+        return out
+
     odd = is_odd()
-    far = jnp.where(odd, SUB - REACH, 0)
-    near = jnp.where(odd, 0, SUB - REACH)
-    groups = part // (SUB * SUB)
-    out = []
-
-    for i, c in enumerate(copies):
+
+    @pl.when(odd)
+    def _():
+        for c in copies(SUB - REACH, 0):
+            c.start()
+
+    @pl.when(jnp.logical_not(odd))
+    def _():
+        for c in copies(0, SUB - REACH):
+            c.start()
+
+    whole.start()
+    for c in copies(0, SUB - REACH):
         c.wait()
-
-        def group(j, _):
-            for r in range(REACH):
-                at = at_rows(j * SUB)
-                far_ref[r, at, :] = native_ref[pl.ds(j * SUB * SUB + far + r, SUB, stride=SUB), :]
-                near_ref[r, at, :] = native_ref[pl.ds(j * SUB * SUB + near + r, SUB, stride=SUB), :]
-            return 0
-
-        lax.fori_loop(i * groups, (i + 1) * groups, group, 0, unroll=unroll(groups, 8))
-        at = pl.ds(i * groups * SUB, groups * SUB)
-        out.append(pltpu.make_async_copy(far_ref.at[:, at], far_any.at[:, at], far_sems.at[i]))
-        out.append(pltpu.make_async_copy(near_ref.at[:, at], near_any.at[:, at], near_sems.at[i]))
-        out[-2].start()
-        out[-1].start()
-    for c in out:
-        c.wait()
+    whole.wait()
 
 
 def first_rows(native):
-    rows = native.shape[0] // SUB
+    rows = native.shape[0]
     halo = (REACH, rows, LANES)
     return pl.pallas_call(
         first_rows_kernel,
         in_specs=[spec(pltpu.HBM)],
         out_specs=[spec(pltpu.VMEM), spec(pl.ANY), spec(pl.ANY)],
         out_shape=[array(*native.shape), array(*halo), array(*halo)],
-        scratch_shapes=[pltpu.VMEM(halo, F32)] * 2 + [pltpu.SemaphoreType.DMA((SPLIT_PARTS,))] * 3,
+        scratch_shapes=[pltpu.SemaphoreType.DMA] + [pltpu.SemaphoreType.DMA((REACH,))] * 2,
         compiler_params=params(),
         cost_estimate=traffic(rows, 4),
         name="first_rows",
@@ -886,7 +874,7 @@
     cells, points = particle_profile.shape
     rows = points // LANES
     plane_count = NV // lax.axis_size("vel")
-    native = particle_profile.reshape(cells, rows, LANES).transpose(1, 0, 2).reshape(cells * rows, LANES)
+    native = particle_profile.reshape(cells, rows, LANES).transpose(1, 0, 2)
     wall = neighbors < 0
     links = jnp.where(wall, WALL_LINK, neighbors - lax.axis_index("space") * cells)
     own = (links >= 0) & (links < cells)
@@ -904,7 +892,7 @@
     geo = jnp.broadcast_to(geo[:, :, None], (GEO, cells, LANES))
     native, far, near = first_rows(native)
     far, near = swap(far, 1), swap(near, 0)
-    f, sums = first_sums(links, geo, native)
+    f, sums = first_sums(links, geo, native.reshape(rows * cells, LANES))
     tiles = gather_sums(sums)
     part, pairs = flux(True, links, geo, f)
     part, absorbed = add_target(links, geo, None, tiles, f, part)

time: 57.4 us -> 104 us (1.81)
  Pallas kernels: 27 us -> 73.6 us
    pallas_call x1, Pallas kernels: 2.45 us -> 48.8 us  [first_rows(): pl.pallas_call(first_rows_kernel, in_specs=[spec(pltpu.HBM)], out_specs=[...]
  transfers between devices with their start and end apart: 12 -> 12, of which waited for: 5 -> 5; matrix products, arithmetic and copies ran while one was open for 1% -> 1% of each run, Pallas kernels for 41% -> 23%
where the time goes in v14:
time: 104 us; the launch traced here: 103 us
  Pallas kernels  73.6 us (71%)
  starting transfers between devices  22 us (21%)
  waiting for transfers between devices  6.09 us (6%)
    pallas_call x1, Pallas kernels, first_rows(): pl.pallas_call(first_rows_kernel, in_specs=[spec(pltpu.HBM)], out_specs=[...  48.8 us
    ppermute x6, starting transfers between devices, gather_sums(): lax.ppermute(tile, 'vel', [(i, i ^ s) for i in range(size)])  8.84 us
    ppermute x4, starting transfers between devices, swap(): return lax.ppermute(rows, 'space', pairs + [(j, i) for i, j in pairs])  7.3 us
    pallas_call x2, Pallas kernels, add_target(): pl.pallas_call(kernel, in_specs=[spec(pltpu.SMEM)] + [vmem] * (len(given)...  7.27 us
    pallas_call x2, Pallas kernels, flux(): pl.pallas_call(functools.partial(flux_kernel, with_pairs), in_specs=[spec...  7.18 us
    ppermute x4, waiting for transfers between devices, swap(): return lax.ppermute(rows, 'space', pairs + [(j, i) for i, j in pairs])  3.62 us
    ppermute x1, starting transfers between devices, doubling_sums(): return [pair, lax.ppermute(pair, 'vel', [(i, i ^ 2) for i in range(size)])]  3.03 us
    ppermute x1, starting transfers between devices, doubling_sums(): pair = tile + lax.ppermute(tile, 'vel', [(i, i ^ 1) for i in range(size)])  2.84 us
  transfers between devices with their start and end apart: 12, of which 5 were waited for; matrix products, arithmetic and copies ran while one was open for 1% of the time, Pallas kernels for 23%

profile of v14, /device:TPU:4, one launch (start us, length us, event | category | flops | bytes accessed | tf_op | source)
XLA Modules:
  0.0 103.2 jit_solution(2423192028308456859)
XLA Ops:
  0.6 0.0 copy-start.2
  0.6 0.0 copy-start.3
  0.7 48.8 %first_rows.1 = (f32[512,8,128]{2,1,0:T(8,128)S(1)}, f32[3,512,128]{2,1,0:T(8,128)}, f32[3,512,128]{2,1,0:T(8,128)}) custom-call(f32[512,8,128]{2,1,0:T(8,128)} %bitcast.12), custom_call_target="tpu_custom_call" | custom-call | flops 16777216 | bytes 8388608 | tf_op jit(solution)/shard_map/first_rows/pallas_call | solution.py:377
  49.5 0.1 collective-permute-start
  49.6 3.4 %collective-permute-start.5 = (f32[3,512,128]{2,1,0:T(8,128)}, f32[3,512,128]{2,1,0:T(8,128)S(1)}, u32[]{:S(2)}, u32[]{:S(2)}) collective-permute-start(f32[3,512,128]{2,1,0:T(8,128)} %get-tuple-element.27), channel_id=1, source_target_pairs={{4,8},{12,16},{20,24},{8,4},{16,12},{24,20},{5,9},{13,17},{21,25},... | collective-permute-start | bytes 2359304 | tf_op jit(solution)/shard_map/ppermute | solution.py:870
  53.1 0.1 copy.13
  53.1 0.1 copy.14
  53.2 0.0 copy-done.1
  53.2 0.1 copy.16
  53.3 0.1 copy.15
  53.4 0.1 copy.18
  53.5 0.1 concatenate.3
  53.6 0.1 copy.17
  53.7 0.1 broadcast_in_dim.23.geo_ref.geo_in
  53.8 2.5 %first_sums.1 = (f32[8,512,128]{2,1,0:T(8,128)S(1)}, f32[8,128]{1,0:T(8,128)S(1)}) custom-call(s32[6,8]{1,0:T(8,128)S(1)} %get-tuple-element.37.links_ref, f32[33,8,128]{2,1,0:T(8,128)S(1)} %broadcast_in_dim.23.geo_ref.geo_in, f32[4096,128]{1,0:T(8,128)S(1)} %bitcast.11), custom_call_target="tpu_custom_call" | custom-call | flops 20971520 | bytes 10485760 | tf_op jit(solution)/shard_map/first_sums/pallas_call | solution.py:327
  56.3 3.7 %collective-permute-start.3 = (f32[8,128]{1,0:T(8,128)S(1)}, f32[8,128]{1,0:T(8,128)S(1)}, u32[]{:S(2)}, u32[]{:S(2)}) collective-permute-start(f32[8,128]{1,0:T(8,128)S(1)} %get-tuple-element.23.refs_0_), channel_id=1, source_target_pairs={{0,3},{1,2},{2,1},{3,0},{4,7},{5,6},{6,5},{7,4},{8,11},{9,10},{10,... | collective-permute-start | bytes 12296 | tf_op jit(solution)/shard_map/ppermute | solution.py:432
  59.9 0.0 collective-permute-start.2
  59.9 0.8 collective-permute-start.1
  60.7 4.2 %flux.2 = (f32[8,512,128]{2,1,0:T(8,128)S(1)}, f32[12,512,128]{2,1,0:T(8,128)S(1)}) custom-call(s32[6,8]{1,0:T(8,128)S(1)} %get-tuple-element.37.links_ref, f32[33,8,128]{2,1,0:T(8,128)S(1)} %broadcast_in_dim.23.geo_ref.geo_in, f32[8,512,128]{2,1,0:T(8,128)S(1)} %get-tuple-element.20.f_ref.refs_4_.old_ref), custom_call_target="tpu_custom_call" | custom-call | flops 37748736 | bytes 18874368 | tf_op jit(solution)/shard_map/flux/pallas_call | solution.py:560
  64.9 0.0 collective-permute-done.3.refs_3_
  64.9 0.0 collective-permute-done.2.refs_2_
  64.9 0.0 collective-permute-done.1.refs_1_
  64.9 3.7 %add_target.2 = (f32[8,512,128]{2,1,0:T(8,128)S(1)}, f32[8,128]{1,0:T(8,128)S(1)}) custom-call(s32[6,8]{1,0:T(8,128)S(1)} %get-tuple-element.37.links_ref, f32[33,8,128]{2,1,0:T(8,128)S(1)} %broadcast_in_dim.23.geo_ref.geo_in, f32[8,128]{1,0:T(8,128)S(1)} %get-tuple-element.23.refs_0_, ...), custom_call_target="tpu_custom_call", output_to_operand_aliasing={{0}: (7, {})} | custom-call | flops 29360128 | bytes 14680064 | tf_op jit(solution)/shard_map/add_target/pallas_call | solution.py:691
  68.6 0.0 collective-permute-done.halo_ref
  68.6 1.7 %near_edge.1 = (f32[8,512,128]{2,1,0:T(8,128)S(1)}, f32[3,512,128]{2,1,0:T(8,128)S(1)}) custom-call(f32[12,512,128]{2,1,0:T(8,128)S(1)} %get-tuple-element.21.pairs_ref, f32[3,512,128]{2,1,0:T(8,128)} %collective-permute-done.halo_ref, f32[8,512,128]{2,1,0:T(8,128)S(1)} %get-tuple-element.20.f_ref.refs_4_.old_ref, ...), custom_call_target="tpu_custom_call", output_to_operand_aliasing={{0}: (3, {})} | custom-call | flops 8388608 | bytes 4194304 | tf_op jit(solution)/shard_map/near_edge/pallas_call | solution.py:754
  70.4 0.1 collective-permute-start.4
  70.5 1.1 %collective-permute-done.5.halo_ref = f32[3,512,128]{2,1,0:T(8,128)S(1)} collective-permute-done((f32[3,512,128]{2,1,0:T(8,128)}, f32[3,512,128]{2,1,0:T(8,128)S(1)}, u32[]{:S(2)}, u32[]{:S(2)}) %collective-permute-start.5) | collective-permute-done | bytes 786464 | tf_op jit(solution)/shard_map/ppermute | solution.py:870
  71.5 0.6 far_edge.1
  72.2 3.7 %collective-permute-start.9 = (f32[3,512,128]{2,1,0:T(8,128)S(1)}, f32[3,512,128]{2,1,0:T(8,128)S(1)}, u32[]{:S(2)}, u32[]{:S(2)}) collective-permute-start(f32[3,512,128]{2,1,0:T(8,128)S(1)} %get-tuple-element.32), channel_id=1, source_target_pairs={{4,8},{12,16},{20,24},{8,4},{16,12},{24,20},{5,9},{13,17},{21,25},... | collective-permute-start | bytes 2359304 | tf_op jit(solution)/shard_map/ppermute | solution.py:870
  75.9 1.6 %local_sums.1.refs_1_ = f32[8,128]{1,0:T(8,128)S(1)} custom-call(s32[6,8]{1,0:T(8,128)S(1)} %get-tuple-element.37.links_ref, f32[33,8,128]{2,1,0:T(8,128)S(1)} %broadcast_in_dim.23.geo_ref.geo_in, f32[8,512,128]{2,1,0:T(8,128)S(1)} %get-tuple-element.29.f_ref.refs_5_.old_ref), custom_call_target="tpu_custom_call" | custom-call | flops 16777216 | bytes 8388608 | tf_op jit(solution)/shard_map/local_sums/pallas_call | solution.py:309
  77.5 3.6 %collective-permute-start.8 = (f32[8,128]{1,0:T(8,128)S(1)}, f32[8,128]{1,0:T(8,128)S(1)}, u32[]{:S(2)}, u32[]{:S(2)}) collective-permute-start(f32[8,128]{1,0:T(8,128)S(1)} %local_sums.1.refs_1_), channel_id=1, source_target_pairs={{0,3},{1,2},{2,1},{3,0},{4,7},{5,6},{6,5},{7,4},{8,11},{9,10},{10,... | collective-permute-start | bytes 12296 | tf_op jit(solution)/shard_map/ppermute | solution.py:432
  81.2 0.0 collective-permute-start.7
  81.2 0.8 collective-permute-start.6
  81.9 3.0 %flux.3.refs_6_ = f32[8,512,128]{2,1,0:T(8,128)S(1)} custom-call(s32[6,8]{1,0:T(8,128)S(1)} %get-tuple-element.37.links_ref, f32[33,8,128]{2,1,0:T(8,128)S(1)} %broadcast_in_dim.23.geo_ref.geo_in, f32[8,512,128]{2,1,0:T(8,128)S(1)} %get-tuple-element.29.f_ref.refs_5_.old_ref), custom_call_target="tpu_custom_call" | custom-call | flops 29360128 | bytes 14680064 | tf_op jit(solution)/shard_map/flux/pallas_call | solution.py:560
  84.9 0.0 collective-permute-done.8.refs_4_
  84.9 0.7 collective-permute-done.7.refs_3_
  85.7 0.0 collective-permute-done.6.refs_2_
  85.7 3.6 %add_target.3.part_ref = f32[8,512,128]{2,1,0:T(8,128)S(1)} custom-call(s32[6,8]{1,0:T(8,128)S(1)} %get-tuple-element.37.links_ref, f32[33,8,128]{2,1,0:T(8,128)S(1)} %broadcast_in_dim.23.geo_ref.geo_in, f32[8,128]{1,0:T(8,128)S(1)} %get-tuple-element.30.refs_0_, f32[8,128]{1,0:T(8,128)S(1)} %local_sums.1.refs_1_, ...), custom_call_target="tpu_custom_call", output_to_operand_aliasing={{}: (8, {})} | custom-call | flops 29360128 | bytes 14680064 | tf_op jit(solution)/shard_map/add_target/pallas_call | solution.py:691
  89.3 0.0 collective-permute-done.4.halo_ref
  89.3 1.2 %last_near.1 = (f32[8,512,128]{2,1,0:T(8,128)S(1)}, f32[8,128]{1,0:T(8,128)S(1)}) custom-call(f32[33,8,128]{2,1,0:T(8,128)S(1)} %broadcast_in_dim.23.geo_ref.geo_in, f32[12,512,128]{2,1,0:T(8,128)S(1)} %get-tuple-element.21.pairs_ref, f32[3,512,128]{2,1,0:T(8,128)S(1)} %collective-permute-done.4.halo_ref, ...), custom_call_target="tpu_custom_call", output_to_operand_aliasing={{0}: (4, {})} | custom-call | flops 12582912 | bytes 6291456 | tf_op jit(solution)/shard_map/last_near/pallas_call | solution.py:775
  90.5 2.5 %collective-permute-done.9.halo_ref = f32[3,512,128]{2,1,0:T(8,128)S(1)} collective-permute-done((f32[3,512,128]{2,1,0:T(8,128)S(1)}, f32[3,512,128]{2,1,0:T(8,128)S(1)}, u32[]{:S(2)}, u32[]{:S(2)}) %collective-permute-start.9) | collective-permute-done | bytes 786464 | tf_op jit(solution)/shard_map/ppermute | solution.py:870
  93.0 0.5 last_far.1
  93.5 2.8 %collective-permute-start.10 = (f32[8,128]{1,0:T(8,128)S(1)}, f32[8,128]{1,0:T(8,128)S(1)}, u32[]{:S(2)}, u32[]{:S(2)}) collective-permute-start(f32[8,128]{1,0:T(8,128)S(1)} %get-tuple-element.35), channel_id=1, source_target_pairs={{0,1},{1,0},{2,3},{3,2},{4,5},{5,4},{6,7},{7,6},{8,9},{9,8},{10,11... | collective-permute-start | bytes 12296 | tf_op jit(solution)/shard_map/ppermute | solution.py:440
  96.3 1.6 %collective-permute-done.10 = f32[8,128]{1,0:T(8,128)S(1)} collective-permute-done((f32[8,128]{1,0:T(8,128)S(1)}, f32[8,128]{1,0:T(8,128)S(1)}, u32[]{:S(2)}, u32[]{:S(2)}) %collective-permute-start.10) | collective-permute-done | bytes 4128 | tf_op jit(solution)/shard_map/ppermute | solution.py:440
  97.9 3.0 %collective-permute-start.11 = (f32[8,128]{1,0:T(8,128)S(1)}, f32[8,128]{1,0:T(8,128)S(1)}, u32[]{:S(2)}, u32[]{:S(2)}) collective-permute-start(f32[8,128]{1,0:T(8,128)S(1)} %add.7.refs_0_), channel_id=1, source_target_pairs={{0,2},{1,3},{2,0},{3,1},{4,6},{5,7},{6,4},{7,5},{8,10},{9,11},{10,... | collective-permute-start | bytes 12296 | tf_op jit(solution)/shard_map/ppermute | solution.py:441
  101.0 1.4 %result.1 = f32[4096,128]{1,0:T(8,128)} custom-call(f32[8,512,128]{2,1,0:T(8,128)S(1)} %get-tuple-element.31.part_ref, f32[3,512,128]{2,1,0:T(8,128)S(1)} %get-tuple-element.34.terms_ref), custom_call_target="tpu_custom_call" | custom-call | flops 12582912 | bytes 6291456 | tf_op jit(solution)/shard_map/result/pallas_call | solution.py:856
  102.4 0.1 collective-permute-done.11.refs_1_
  102.6 0.7 macro.1
  (9 shorter events, 0.0 us)
Async XLA Ops:
  0.6 52.4 %copy-start.2 = (f32[8]{0:T(128)S(1)}, f32[8]{0:T(128)}, u32[]{:S(2)}) copy-start(f32[8]{0:T(128)} %param.8) | copy-start | bytes 100
  0.6 52.5 %copy-start.3 = (f32[8]{0:T(128)S(1)}, f32[8]{0:T(128)}, u32[]{:S(2)}) copy-start(f32[8]{0:T(128)} %param.9) | copy-start | bytes 100
  0.7 52.6 %copy-start.1 = (s32[6,8]{1,0:T(8,128)S(1)}, s32[6,8]{1,0:T(8,128)}, u32[]{:S(2)}) copy-start(s32[6,8]{1,0:T(8,128)} %param.6) | copy-start | bytes 580
  0.7 52.7 %copy-start = (f32[3,6,8]{2,1,0:T(8,128)S(1)}, f32[3,6,8]{2,1,0:T(8,128)}, u32[]{:S(2)}) copy-start(f32[3,6,8]{2,1,0:T(8,128)} %param.7) | copy-start | bytes 1732
  49.5 19.1 %collective-permute-start = (f32[3,512,128]{2,1,0:T(8,128)}, f32[3,512,128]{2,1,0:T(8,128)}, u32[]{:S(2)}, u32[]{:S(2)}) collective-permute-start(f32[3,512,128]{2,1,0:T(8,128)} %get-tuple-element.22), channel_id=1, source_target_pairs={{0,4},{8,12},{16,20},{24,28},{4,0},{12,8},{20,16},{28,24},{1,5},{9... | collective-permute-start | bytes 2359304 | tf_op jit(solution)/shard_map/ppermute | solution.py:870
  49.6 21.9 %collective-permute-start.5 = (f32[3,512,128]{2,1,0:T(8,128)}, f32[3,512,128]{2,1,0:T(8,128)S(1)}, u32[]{:S(2)}, u32[]{:S(2)}) collective-permute-start(f32[3,512,128]{2,1,0:T(8,128)} %get-tuple-element.27), channel_id=1, source_target_pairs={{4,8},{12,16},{20,24},{8,4},{16,12},{24,20},{5,9},{13,17},{21,25},... | collective-permute-start | bytes 2359304 | tf_op jit(solution)/shard_map/ppermute | solution.py:870
  56.3 8.7 %collective-permute-start.3 = (f32[8,128]{1,0:T(8,128)S(1)}, f32[8,128]{1,0:T(8,128)S(1)}, u32[]{:S(2)}, u32[]{:S(2)}) collective-permute-start(f32[8,128]{1,0:T(8,128)S(1)} %get-tuple-element.23.refs_0_), channel_id=1, source_target_pairs={{0,3},{1,2},{2,1},{3,0},{4,7},{5,6},{6,5},{7,4},{8,11},{9,10},{10,... | collective-permute-start | bytes 12296 | tf_op jit(solution)/shard_map/ppermute | solution.py:432
  59.9 5.0 %collective-permute-start.2 = (f32[8,128]{1,0:T(8,128)S(1)}, f32[8,128]{1,0:T(8,128)S(1)}, u32[]{:S(2)}, u32[]{:S(2)}) collective-permute-start(f32[8,128]{1,0:T(8,128)S(1)} %get-tuple-element.23.refs_0_), channel_id=1, source_target_pairs={{0,2},{1,3},{2,0},{3,1},{4,6},{5,7},{6,4},{7,5},{8,10},{9,11},{10,... | collective-permute-start | bytes 12296 | tf_op jit(solution)/shard_map/ppermute | solution.py:432
  59.9 5.0 %collective-permute-start.1 = (f32[8,128]{1,0:T(8,128)S(1)}, f32[8,128]{1,0:T(8,128)S(1)}, u32[]{:S(2)}, u32[]{:S(2)}) collective-permute-start(f32[8,128]{1,0:T(8,128)S(1)} %get-tuple-element.23.refs_0_), channel_id=1, source_target_pairs={{0,1},{1,0},{2,3},{3,2},{4,5},{5,4},{6,7},{7,6},{8,9},{9,8},{10,11... | collective-permute-start | bytes 12296 | tf_op jit(solution)/shard_map/ppermute | solution.py:432
  70.4 18.9 %collective-permute-start.4 = (f32[3,512,128]{2,1,0:T(8,128)S(1)}, f32[3,512,128]{2,1,0:T(8,128)S(1)}, u32[]{:S(2)}, u32[]{:S(2)}) collective-permute-start(f32[3,512,128]{2,1,0:T(8,128)S(1)} %get-tuple-element.26), channel_id=1, source_target_pairs={{0,4},{8,12},{16,20},{24,28},{4,0},{12,8},{20,16},{28,24},{1,5},{9... | collective-permute-start | bytes 2359304 | tf_op jit(solution)/shard_map/ppermute | solution.py:870
  72.2 20.8 %collective-permute-start.9 = (f32[3,512,128]{2,1,0:T(8,128)S(1)}, f32[3,512,128]{2,1,0:T(8,128)S(1)}, u32[]{:S(2)}, u32[]{:S(2)}) collective-permute-start(f32[3,512,128]{2,1,0:T(8,128)S(1)} %get-tuple-element.32), channel_id=1, source_target_pairs={{4,8},{12,16},{20,24},{8,4},{16,12},{24,20},{5,9},{13,17},{21,25},... | collective-permute-start | bytes 2359304 | tf_op jit(solution)/shard_map/ppermute | solution.py:870
  77.5 7.4 %collective-permute-start.8 = (f32[8,128]{1,0:T(8,128)S(1)}, f32[8,128]{1,0:T(8,128)S(1)}, u32[]{:S(2)}, u32[]{:S(2)}) collective-permute-start(f32[8,128]{1,0:T(8,128)S(1)} %local_sums.1.refs_1_), channel_id=1, source_target_pairs={{0,3},{1,2},{2,1},{3,0},{4,7},{5,6},{6,5},{7,4},{8,11},{9,10},{10,... | collective-permute-start | bytes 12296 | tf_op jit(solution)/shard_map/ppermute | solution.py:432
  81.2 4.5 %collective-permute-start.7 = (f32[8,128]{1,0:T(8,128)S(1)}, f32[8,128]{1,0:T(8,128)S(1)}, u32[]{:S(2)}, u32[]{:S(2)}) collective-permute-start(f32[8,128]{1,0:T(8,128)S(1)} %local_sums.1.refs_1_), channel_id=1, source_target_pairs={{0,2},{1,3},{2,0},{3,1},{4,6},{5,7},{6,4},{7,5},{8,10},{9,11},{10,... | collective-permute-start | bytes 12296 | tf_op jit(solution)/shard_map/ppermute | solution.py:432
  81.2 4.5 %collective-permute-start.6 = (f32[8,128]{1,0:T(8,128)S(1)}, f32[8,128]{1,0:T(8,128)S(1)}, u32[]{:S(2)}, u32[]{:S(2)}) collective-permute-start(f32[8,128]{1,0:T(8,128)S(1)} %local_sums.1.refs_1_), channel_id=1, source_target_pairs={{0,1},{1,0},{2,3},{3,2},{4,5},{5,4},{6,7},{7,6},{8,9},{9,8},{10,11... | collective-permute-start | bytes 12296 | tf_op jit(solution)/shard_map/ppermute | solution.py:432
  93.5 4.4 %collective-permute-start.10 = (f32[8,128]{1,0:T(8,128)S(1)}, f32[8,128]{1,0:T(8,128)S(1)}, u32[]{:S(2)}, u32[]{:S(2)}) collective-permute-start(f32[8,128]{1,0:T(8,128)S(1)} %get-tuple-element.35), channel_id=1, source_target_pairs={{0,1},{1,0},{2,3},{3,2},{4,5},{5,4},{6,7},{7,6},{8,9},{9,8},{10,11... | collective-permute-start | bytes 12296 | tf_op jit(solution)/shard_map/ppermute | solution.py:440
  97.9 4.6 %collective-permute-start.11 = (f32[8,128]{1,0:T(8,128)S(1)}, f32[8,128]{1,0:T(8,128)S(1)}, u32[]{:S(2)}, u32[]{:S(2)}) collective-permute-start(f32[8,128]{1,0:T(8,128)S(1)} %add.7.refs_0_), channel_id=1, source_target_pairs={{0,2},{1,3},{2,0},{3,1},{4,6},{5,7},{6,4},{7,5},{8,10},{9,11},{10,... | collective-permute-start | bytes 12296 | tf_op jit(solution)/shard_map/ppermute | solution.py:441

commit v15 on v13

--- a/solution.py
+++ b/solution.py
@@ -797,12 +797,16 @@
     )(geo, pairs, near, old, part)
 
 
-def last_far_kernel(geo_ref, pairs_ref, halo_ref, old_ref, sums_in, terms_ref, sums_out, parts_ref):
+def last_far_kernel(
+    geo_ref, pairs_ref, to_odd_ref, to_even_ref, old_ref, sums_in, terms_ref, sums_out, parts_ref
+):
     rows = old_ref.shape[1]
     planes = rows // CHUNKS
     parts_ref[...] = jnp.zeros_like(parts_ref)
 
     def run(high):
+        halo_ref = to_odd_ref if high else to_even_ref
+
         def group(j, _):
             at = at_rows(j * SUB)
             _first, terms = side_terms(high, pairs_ref, halo_ref, old_ref, at)
@@ -821,14 +825,14 @@
     rows = old.shape[1]
     return pl.pallas_call(
         last_far_kernel,
-        in_specs=[spec(pltpu.VMEM)] * 5,
+        in_specs=[spec(pltpu.VMEM)] * 6,
         out_specs=[spec(pltpu.VMEM)] * 2,
         out_shape=[array(REACH, rows, LANES), array(SUB, LANES)],
         scratch_shapes=[pltpu.VMEM((10, SUB * SUB, LANES), F32)],
         compiler_params=params(),
         cost_estimate=traffic(rows, 2),
         name="last_far",
-    )(geo, pairs, far, old, sums)
+    )(geo, pairs, far[1], far[0], old, sums)
 
 
 LAST_PARTS = 4
@@ -880,6 +884,12 @@
 def swap(rows, start):
     pairs = [(i, i + 1) for i in range(start, lax.axis_size("space") - 1, 2)]
     return lax.ppermute(rows, "space", pairs + [(j, i) for i, j in pairs])
+
+
+def swap_far_one_way(rows):
+    pairs = [(i, i + 1) for i in range(1, lax.axis_size("space") - 1, 2)]
+    to_odd = lax.ppermute(rows, "space", [(j, i) for i, j in pairs])
+    return lax.ppermute(rows, "space", pairs), to_odd
 
 
 def per_device(particle_profile, neighbors, face_vectors, volumes, wall_temp):
@@ -911,7 +921,7 @@
     part, near = edge(False, pairs, near, f, part)
     near = swap(near, 0)
     f, far = edge(True, pairs, far, f, part)
-    far = swap(far, 1)
+    far = swap_far_one_way(far)
     tiles = gather_sums(local_sums(links, geo, f))
     (part,) = flux(False, links, geo, f)
     (part,) = add_target(links, geo, absorbed, tiles, f, part)

time: 57.4 us -> 59.1 us (1.030)
  starting transfers between devices: 22 us -> 23.9 us
    ppermute x0 -> x2, starting transfers between devices: none -> 6.55 us  [the longest x1 5.26 us: swap_far_one_way(): to_odd = lax.ppermute(rows, 'space', [(j, i) for i, j in pairs])]
    ppermute x4 -> x3, starting transfers between devices: 7.3 us -> 3.57 us  [swap(): return lax.ppermute(rows, 'space', pairs + [(j, i) for i, j in pairs])]
    ppermute x6, starting transfers between devices: 8.84 us -> 12.3 us  [gather_sums(): lax.ppermute(tile, 'vel', [(i, i ^ s) for i in range(size)])]
    ppermute x4 -> x3, waiting for transfers between devices: 3.86 us -> 0.52 us  [swap(): return lax.ppermute(rows, 'space', pairs + [(j, i) for i, j in pairs])]
    ppermute x1, starting transfers between devices: 2.84 us -> 0.27 us  [doubling_sums(): pair = tile + lax.ppermute(tile, 'vel', [(i, i ^ 1) for i in range(size)])]
    ppermute x1, starting transfers between devices: 3.03 us -> 1.22 us  [doubling_sums(): return [pair, lax.ppermute(pair, 'vel', [(i, i ^ 2) for i in range(size)])]]
    ppermute x1, waiting for transfers between devices: 1.59 us -> 3.4 us  [doubling_sums(): pair = tile + lax.ppermute(tile, 'vel', [(i, i ^ 1) for i in range(size)])]
    ppermute x1, waiting for transfers between devices: 0.13 us -> 1.83 us  [doubling_sums(): return [pair, lax.ppermute(pair, 'vel', [(i, i ^ 2) for i in range(size)])]]
  transfers between devices with their start and end apart: 12 -> 13, of which waited for: 5 -> 4; matrix products, arithmetic and copies ran while one was open for 1% -> 1% of each run, Pallas kernels for 41% -> 39%
where the time goes in v15:
time: 59.1 us
  Pallas kernels  26.9 us (46%)
  starting transfers between devices  23.9 us (40%)
  waiting for transfers between devices  6.71 us (11%)
  between operations  0.85 us (1%)
  local copies, waits for them, and re-layouts  0.69 us (1%)
    ppermute x6, starting transfers between devices, gather_sums(): lax.ppermute(tile, 'vel', [(i, i ^ s) for i in range(size)])  12.3 us
    pallas_call x2, Pallas kernels, flux(): pl.pallas_call(functools.partial(flux_kernel, with_pairs), in_specs=[spec...  7.46 us
    pallas_call x2, Pallas kernels, add_target(): pl.pallas_call(kernel, in_specs=[spec(pltpu.SMEM)] + [vmem] * (len(given)...  6.99 us
    ppermute x1, starting transfers between devices, swap_far_one_way(): to_odd = lax.ppermute(rows, 'space', [(j, i) for i, j in pairs])  5.26 us
    ppermute x3, starting transfers between devices, swap(): return lax.ppermute(rows, 'space', pairs + [(j, i) for i, j in pairs])  3.57 us
    ppermute x1, waiting for transfers between devices, doubling_sums(): pair = tile + lax.ppermute(tile, 'vel', [(i, i ^ 1) for i in range(size)])  3.4 us
    pallas_call x1, Pallas kernels, first_rows(): pl.pallas_call(first_rows_kernel, in_specs=[spec(pltpu.HBM)], out_specs=[...  2.44 us
    pallas_call x2, Pallas kernels, edge(): pl.pallas_call(functools.partial(add_side, far), in_specs=[spec(pltpu.VME...  2.36 us
  transfers between devices with their start and end apart: 13, of which 4 were waited for; matrix products, arithmetic and copies ran while one was open for 1% of the time, Pallas kernels for 39%

profile of v15, /device:TPU:4, one launch (start us, length us, event | category | flops | bytes accessed | tf_op | source)
XLA Modules:
  0.0 59.1 jit_solution(12968573076790153698)
XLA Ops:
  0.6 0.0 copy-start.1
  0.7 2.4 %first_rows.1 = (f32[4096,128]{1,0:T(8,128)S(1)}, f32[3,512,128]{2,1,0:T(8,128)}, f32[3,512,128]{2,1,0:T(8,128)}) custom-call(f32[4096,128]{1,0:T(8,128)} %bitcast.12), custom_call_target="tpu_custom_call" | custom-call | flops 16777216 | bytes 8388608 | tf_op jit(solution)/shard_map/first_rows/pallas_call | solution.py:389
  3.1 0.1 collective-permute-start
  3.2 3.4 %collective-permute-start.5 = (f32[3,512,128]{2,1,0:T(8,128)}, f32[3,512,128]{2,1,0:T(8,128)S(1)}, u32[]{:S(2)}, u32[]{:S(2)}) collective-permute-start(f32[3,512,128]{2,1,0:T(8,128)} %get-tuple-element.27), channel_id=1, source_target_pairs={{4,8},{12,16},{20,24},{8,4},{16,12},{24,20},{5,9},{13,17},{21,25},... | collective-permute-start | bytes 2359304 | tf_op jit(solution)/shard_map/ppermute | solution.py:886
  6.7 0.1 copy.15
  6.7 0.1 copy.16
  6.8 0.1 copy.18
  6.9 0.1 copy.13
  7.0 0.1 copy.14
  7.1 0.1 concatenate.3
  7.2 0.1 copy.17
  7.3 0.1 broadcast_in_dim.23.geo_ref.geo_in
  7.4 2.3 %first_sums.1 = (f32[8,512,128]{2,1,0:T(8,128)S(1)}, f32[8,128]{1,0:T(8,128)S(1)}) custom-call(s32[6,8]{1,0:T(8,128)S(1)} %get-tuple-element.37.links_ref, f32[33,8,128]{2,1,0:T(8,128)S(1)} %broadcast_in_dim.23.geo_ref.geo_in, f32[4096,128]{1,0:T(8,128)S(1)} %get-tuple-element.19.native_ref), custom_call_target="tpu_custom_call" | custom-call | flops 20971520 | bytes 10485760 | tf_op jit(solution)/shard_map/first_sums/pallas_call | solution.py:327
  9.6 1.6 %collective-permute-start.1 = (f32[8,128]{1,0:T(8,128)S(1)}, f32[8,128]{1,0:T(8,128)S(1)}, u32[]{:S(2)}, u32[]{:S(2)}) collective-permute-start(f32[8,128]{1,0:T(8,128)S(1)} %get-tuple-element.23.refs_0_), channel_id=1, source_target_pairs={{0,1},{1,0},{2,3},{3,2},{4,5},{5,4},{6,7},{7,6},{8,9},{9,8},{10,11... | collective-permute-start | bytes 12296 | tf_op jit(solution)/shard_map/ppermute | solution.py:444
  11.3 2.6 %collective-permute-start.2 = (f32[8,128]{1,0:T(8,128)S(1)}, f32[8,128]{1,0:T(8,128)S(1)}, u32[]{:S(2)}, u32[]{:S(2)}) collective-permute-start(f32[8,128]{1,0:T(8,128)S(1)} %get-tuple-element.23.refs_0_), channel_id=1, source_target_pairs={{0,2},{1,3},{2,0},{3,1},{4,6},{5,7},{6,4},{7,5},{8,10},{9,11},{10,... | collective-permute-start | bytes 12296 | tf_op jit(solution)/shard_map/ppermute | solution.py:444
  13.9 0.2 collective-permute-start.3
  14.1 4.2 %flux.2 = (f32[8,512,128]{2,1,0:T(8,128)S(1)}, f32[12,512,128]{2,1,0:T(8,128)S(1)}) custom-call(s32[6,8]{1,0:T(8,128)S(1)} %get-tuple-element.37.links_ref, f32[33,8,128]{2,1,0:T(8,128)S(1)} %broadcast_in_dim.23.geo_ref.geo_in, f32[8,512,128]{2,1,0:T(8,128)S(1)} %get-tuple-element.20.f_ref.refs_4_.old_ref), custom_call_target="tpu_custom_call" | custom-call | flops 37748736 | bytes 18874368 | tf_op jit(solution)/shard_map/flux/pallas_call | solution.py:572
  18.3 0.0 collective-permute-done.1.refs_1_
  18.3 0.0 collective-permute-done.2.refs_2_
  18.3 0.9 %collective-permute-done.3.refs_3_ = f32[8,128]{1,0:T(8,128)S(1)} collective-permute-done((f32[8,128]{1,0:T(8,128)S(1)}, f32[8,128]{1,0:T(8,128)S(1)}, u32[]{:S(2)}, u32[]{:S(2)}) %collective-permute-start.3) | collective-permute-done | bytes 4128 | tf_op jit(solution)/shard_map/ppermute | solution.py:444
  19.3 3.5 %add_target.2 = (f32[8,512,128]{2,1,0:T(8,128)S(1)}, f32[8,128]{1,0:T(8,128)S(1)}) custom-call(s32[6,8]{1,0:T(8,128)S(1)} %get-tuple-element.37.links_ref, f32[33,8,128]{2,1,0:T(8,128)S(1)} %broadcast_in_dim.23.geo_ref.geo_in, f32[8,128]{1,0:T(8,128)S(1)} %get-tuple-element.23.refs_0_, ...), custom_call_target="tpu_custom_call", output_to_operand_aliasing={{0}: (7, {})} | custom-call | flops 29360128 | bytes 14680064 | tf_op jit(solution)/shard_map/add_target/pallas_call | solution.py:703
  22.8 0.0 collective-permute-done.halo_ref
  22.8 1.7 %near_edge.1 = (f32[8,512,128]{2,1,0:T(8,128)S(1)}, f32[3,512,128]{2,1,0:T(8,128)S(1)}) custom-call(f32[12,512,128]{2,1,0:T(8,128)S(1)} %get-tuple-element.21.pairs_ref, f32[3,512,128]{2,1,0:T(8,128)} %collective-permute-done.halo_ref, f32[8,512,128]{2,1,0:T(8,128)S(1)} %get-tuple-element.20.f_ref.refs_4_.old_ref, ...), custom_call_target="tpu_custom_call", output_to_operand_aliasing={{0}: (3, {})} | custom-call | flops 8388608 | bytes 4194304 | tf_op jit(solution)/shard_map/near_edge/pallas_call | solution.py:766
  24.5 0.1 collective-permute-start.4
  24.6 0.5 collective-permute-done.5.halo_ref
  25.1 0.6 %far_edge.1 = (f32[8,512,128]{2,1,0:T(8,128)S(1)}, f32[3,512,128]{2,1,0:T(8,128)S(1)}) custom-call(f32[12,512,128]{2,1,0:T(8,128)S(1)} %get-tuple-element.21.pairs_ref, f32[3,512,128]{2,1,0:T(8,128)S(1)} %collective-permute-done.5.halo_ref, f32[8,512,128]{2,1,0:T(8,128)S(1)} %get-tuple-element.20.f_ref.refs_4_.old_ref, ...), custom_call_target="tpu_custom_call", output_to_operand_aliasing={{0}: (3, {})} | custom-call | flops 8388608 | bytes 4194304 | tf_op jit(solution)/shard_map/far_edge/pallas_call | solution.py:766
  25.8 1.3 %collective-permute-start.10 = (f32[3,512,128]{2,1,0:T(8,128)S(1)}, f32[3,512,128]{2,1,0:T(8,128)S(1)}, u32[]{:S(2)}, u32[]{:S(2)}) collective-permute-start(f32[3,512,128]{2,1,0:T(8,128)S(1)} %get-tuple-element.32), channel_id=1, source_target_pairs={{4,8},{12,16},{20,24},{5,9},{13,17},{21,25},{6,10},{14,18},{22,26}... | collective-permute-start | bytes 2359304 | tf_op jit(solution)/shard_map/ppermute | solution.py:892
  27.1 5.3 %collective-permute-start.9 = (f32[3,512,128]{2,1,0:T(8,128)S(1)}, f32[3,512,128]{2,1,0:T(8,128)S(1)}, u32[]{:S(2)}, u32[]{:S(2)}) collective-permute-start(f32[3,512,128]{2,1,0:T(8,128)S(1)} %get-tuple-element.32), channel_id=1, source_target_pairs={{8,4},{16,12},{24,20},{9,5},{17,13},{25,21},{10,6},{18,14},{26,22}... | collective-permute-start | bytes 2359304 | tf_op jit(solution)/shard_map/ppermute | solution.py:891
  32.3 1.5 %local_sums.1.refs_1_ = f32[8,128]{1,0:T(8,128)S(1)} custom-call(s32[6,8]{1,0:T(8,128)S(1)} %get-tuple-element.37.links_ref, f32[33,8,128]{2,1,0:T(8,128)S(1)} %broadcast_in_dim.23.geo_ref.geo_in, f32[8,512,128]{2,1,0:T(8,128)S(1)} %get-tuple-element.29.f_ref.refs_5_.old_ref), custom_call_target="tpu_custom_call" | custom-call | flops 16777216 | bytes 8388608 | tf_op jit(solution)/shard_map/local_sums/pallas_call | solution.py:309
  33.9 2.2 %collective-permute-start.6 = (f32[8,128]{1,0:T(8,128)S(1)}, f32[8,128]{1,0:T(8,128)S(1)}, u32[]{:S(2)}, u32[]{:S(2)}) collective-permute-start(f32[8,128]{1,0:T(8,128)S(1)} %local_sums.1.refs_1_), channel_id=1, source_target_pairs={{0,1},{1,0},{2,3},{3,2},{4,5},{5,4},{6,7},{7,6},{8,9},{9,8},{10,11... | collective-permute-start | bytes 12296 | tf_op jit(solution)/shard_map/ppermute | solution.py:444
  36.1 2.6 %collective-permute-start.7 = (f32[8,128]{1,0:T(8,128)S(1)}, f32[8,128]{1,0:T(8,128)S(1)}, u32[]{:S(2)}, u32[]{:S(2)}) collective-permute-start(f32[8,128]{1,0:T(8,128)S(1)} %local_sums.1.refs_1_), channel_id=1, source_target_pairs={{0,2},{1,3},{2,0},{3,1},{4,6},{5,7},{6,4},{7,5},{8,10},{9,11},{10,... | collective-permute-start | bytes 12296 | tf_op jit(solution)/shard_map/ppermute | solution.py:444
  38.7 0.0 collective-permute-done.6.refs_2_
  38.7 3.0 %collective-permute-start.8 = (f32[8,128]{1,0:T(8,128)S(1)}, f32[8,128]{1,0:T(8,128)S(1)}, u32[]{:S(2)}, u32[]{:S(2)}) collective-permute-start(f32[8,128]{1,0:T(8,128)S(1)} %local_sums.1.refs_1_), channel_id=1, source_target_pairs={{0,3},{1,2},{2,1},{3,0},{4,7},{5,6},{6,5},{7,4},{8,11},{9,10},{10,... | collective-permute-start | bytes 12296 | tf_op jit(solution)/shard_map/ppermute | solution.py:444
  41.7 3.3 %flux.3.refs_6_ = f32[8,512,128]{2,1,0:T(8,128)S(1)} custom-call(s32[6,8]{1,0:T(8,128)S(1)} %get-tuple-element.37.links_ref, f32[33,8,128]{2,1,0:T(8,128)S(1)} %broadcast_in_dim.23.geo_ref.geo_in, f32[8,512,128]{2,1,0:T(8,128)S(1)} %get-tuple-element.29.f_ref.refs_5_.old_ref), custom_call_target="tpu_custom_call" | custom-call | flops 29360128 | bytes 14680064 | tf_op jit(solution)/shard_map/flux/pallas_call | solution.py:572
  45.0 0.0 collective-permute-done.7.refs_3_
  45.0 0.0 collective-permute-done.8.refs_4_
  45.0 3.5 %add_target.3.part_ref = f32[8,512,128]{2,1,0:T(8,128)S(1)} custom-call(s32[6,8]{1,0:T(8,128)S(1)} %get-tuple-element.37.links_ref, f32[33,8,128]{2,1,0:T(8,128)S(1)} %broadcast_in_dim.23.geo_ref.geo_in, f32[8,128]{1,0:T(8,128)S(1)} %get-tuple-element.30.refs_0_, f32[8,128]{1,0:T(8,128)S(1)} %local_sums.1.refs_1_, ...), custom_call_target="tpu_custom_call", output_to_operand_aliasing={{}: (8, {})} | custom-call | flops 29360128 | bytes 14680064 | tf_op jit(solution)/shard_map/add_target/pallas_call | solution.py:703
  48.5 0.0 collective-permute-done.4.halo_ref
  48.5 1.2 %last_near.1 = (f32[8,512,128]{2,1,0:T(8,128)S(1)}, f32[8,128]{1,0:T(8,128)S(1)}) custom-call(f32[33,8,128]{2,1,0:T(8,128)S(1)} %broadcast_in_dim.23.geo_ref.geo_in, f32[12,512,128]{2,1,0:T(8,128)S(1)} %get-tuple-element.21.pairs_ref, f32[3,512,128]{2,1,0:T(8,128)S(1)} %collective-permute-done.4.halo_ref, ...), custom_call_target="tpu_custom_call", output_to_operand_aliasing={{0}: (4, {})} | custom-call | flops 12582912 | bytes 6291456 | tf_op jit(solution)/shard_map/last_near/pallas_call | solution.py:787
  49.7 0.0 collective-permute-done.10.to_even_ref
  49.7 0.0 collective-permute-done.9.to_odd_ref
  49.7 0.5 last_far.1
  50.2 0.3 collective-permute-start.11
  50.5 3.4 %collective-permute-done.11 = f32[8,128]{1,0:T(8,128)S(1)} collective-permute-done((f32[8,128]{1,0:T(8,128)S(1)}, f32[8,128]{1,0:T(8,128)S(1)}, u32[]{:S(2)}, u32[]{:S(2)}) %collective-permute-start.11) | collective-permute-done | bytes 4128 | tf_op jit(solution)/shard_map/ppermute | solution.py:452
  53.9 1.2 %collective-permute-start.12 = (f32[8,128]{1,0:T(8,128)S(1)}, f32[8,128]{1,0:T(8,128)S(1)}, u32[]{:S(2)}, u32[]{:S(2)}) collective-permute-start(f32[8,128]{1,0:T(8,128)S(1)} %add.7.refs_0_), channel_id=1, source_target_pairs={{0,2},{1,3},{2,0},{3,1},{4,6},{5,7},{6,4},{7,5},{8,10},{9,11},{10,... | collective-permute-start | bytes 12296 | tf_op jit(solution)/shard_map/ppermute | solution.py:453
  55.1 1.4 %result.1 = f32[4096,128]{1,0:T(8,128)} custom-call(f32[8,512,128]{2,1,0:T(8,128)S(1)} %get-tuple-element.31.part_ref, f32[3,512,128]{2,1,0:T(8,128)S(1)} %get-tuple-element.34.terms_ref), custom_call_target="tpu_custom_call" | custom-call | flops 12582912 | bytes 6291456 | tf_op jit(solution)/shard_map/result/pallas_call | solution.py:872
  56.5 1.8 %collective-permute-done.12.refs_1_ = f32[8,128]{1,0:T(8,128)S(1)} collective-permute-done((f32[8,128]{1,0:T(8,128)S(1)}, f32[8,128]{1,0:T(8,128)S(1)}, u32[]{:S(2)}, u32[]{:S(2)}) %collective-permute-start.12) | collective-permute-done | bytes 4128 | tf_op jit(solution)/shard_map/ppermute | solution.py:453
  58.4 0.7 %macro.1 = f32[8,8]{1,0:T(8,128)} custom-call(f32[8,128]{1,0:T(8,128)S(1)} %add.7.refs_0_, f32[8,128]{1,0:T(8,128)S(1)} %collective-permute-done.12.refs_1_), custom_call_target="tpu_custom_call" | custom-call | tf_op jit(solution)/shard_map/macro/pallas_call | solution.py:490
  (11 shorter events, 0.0 us)
Async XLA Ops:
  0.6 6.0 %copy-start.1 = (s32[6,8]{1,0:T(8,128)S(1)}, s32[6,8]{1,0:T(8,128)}, u32[]{:S(2)}) copy-start(s32[6,8]{1,0:T(8,128)} %param.6) | copy-start | bytes 580
  0.6 6.2 %copy-start = (f32[3,6,8]{2,1,0:T(8,128)S(1)}, f32[3,6,8]{2,1,0:T(8,128)}, u32[]{:S(2)}) copy-start(f32[3,6,8]{2,1,0:T(8,128)} %param.7) | copy-start | bytes 1732
  0.7 6.3 %copy-start.2 = (f32[8]{0:T(128)S(1)}, f32[8]{0:T(128)}, u32[]{:S(2)}) copy-start(f32[8]{0:T(128)} %param.8) | copy-start | bytes 100
  0.7 6.3 %copy-start.3 = (f32[8]{0:T(128)S(1)}, f32[8]{0:T(128)}, u32[]{:S(2)}) copy-start(f32[8]{0:T(128)} %param.9) | copy-start | bytes 100
  3.1 19.7 %collective-permute-start = (f32[3,512,128]{2,1,0:T(8,128)}, f32[3,512,128]{2,1,0:T(8,128)}, u32[]{:S(2)}, u32[]{:S(2)}) collective-permute-start(f32[3,512,128]{2,1,0:T(8,128)} %get-tuple-element.22), channel_id=1, source_target_pairs={{0,4},{8,12},{16,20},{24,28},{4,0},{12,8},{20,16},{28,24},{1,5},{9... | collective-permute-start | bytes 2359304 | tf_op jit(solution)/shard_map/ppermute | solution.py:886
  3.2 21.9 %collective-permute-start.5 = (f32[3,512,128]{2,1,0:T(8,128)}, f32[3,512,128]{2,1,0:T(8,128)S(1)}, u32[]{:S(2)}, u32[]{:S(2)}) collective-permute-start(f32[3,512,128]{2,1,0:T(8,128)} %get-tuple-element.27), channel_id=1, source_target_pairs={{4,8},{12,16},{20,24},{8,4},{16,12},{24,20},{5,9},{13,17},{21,25},... | collective-permute-start | bytes 2359304 | tf_op jit(solution)/shard_map/ppermute | solution.py:886
  9.6 8.7 %collective-permute-start.1 = (f32[8,128]{1,0:T(8,128)S(1)}, f32[8,128]{1,0:T(8,128)S(1)}, u32[]{:S(2)}, u32[]{:S(2)}) collective-permute-start(f32[8,128]{1,0:T(8,128)S(1)} %get-tuple-element.23.refs_0_), channel_id=1, source_target_pairs={{0,1},{1,0},{2,3},{3,2},{4,5},{5,4},{6,7},{7,6},{8,9},{9,8},{10,11... | collective-permute-start | bytes 12296 | tf_op jit(solution)/shard_map/ppermute | solution.py:444
  11.3 7.0 %collective-permute-start.2 = (f32[8,128]{1,0:T(8,128)S(1)}, f32[8,128]{1,0:T(8,128)S(1)}, u32[]{:S(2)}, u32[]{:S(2)}) collective-permute-start(f32[8,128]{1,0:T(8,128)S(1)} %get-tuple-element.23.refs_0_), channel_id=1, source_target_pairs={{0,2},{1,3},{2,0},{3,1},{4,6},{5,7},{6,4},{7,5},{8,10},{9,11},{10,... | collective-permute-start | bytes 12296 | tf_op jit(solution)/shard_map/ppermute | solution.py:444
  13.9 5.4 %collective-permute-start.3 = (f32[8,128]{1,0:T(8,128)S(1)}, f32[8,128]{1,0:T(8,128)S(1)}, u32[]{:S(2)}, u32[]{:S(2)}) collective-permute-start(f32[8,128]{1,0:T(8,128)S(1)} %get-tuple-element.23.refs_0_), channel_id=1, source_target_pairs={{0,3},{1,2},{2,1},{3,0},{4,7},{5,6},{6,5},{7,4},{8,11},{9,10},{10,... | collective-permute-start | bytes 12296 | tf_op jit(solution)/shard_map/ppermute | solution.py:444
  24.5 23.9 %collective-permute-start.4 = (f32[3,512,128]{2,1,0:T(8,128)S(1)}, f32[3,512,128]{2,1,0:T(8,128)S(1)}, u32[]{:S(2)}, u32[]{:S(2)}) collective-permute-start(f32[3,512,128]{2,1,0:T(8,128)S(1)} %get-tuple-element.26), channel_id=1, source_target_pairs={{0,4},{8,12},{16,20},{24,28},{4,0},{12,8},{20,16},{28,24},{1,5},{9... | collective-permute-start | bytes 2359304 | tf_op jit(solution)/shard_map/ppermute | solution.py:886
  25.8 23.9 %collective-permute-start.10 = (f32[3,512,128]{2,1,0:T(8,128)S(1)}, f32[3,512,128]{2,1,0:T(8,128)S(1)}, u32[]{:S(2)}, u32[]{:S(2)}) collective-permute-start(f32[3,512,128]{2,1,0:T(8,128)S(1)} %get-tuple-element.32), channel_id=1, source_target_pairs={{4,8},{12,16},{20,24},{5,9},{13,17},{21,25},{6,10},{14,18},{22,26}... | collective-permute-start | bytes 2359304 | tf_op jit(solution)/shard_map/ppermute | solution.py:892
  27.1 22.6 %collective-permute-start.9 = (f32[3,512,128]{2,1,0:T(8,128)S(1)}, f32[3,512,128]{2,1,0:T(8,128)S(1)}, u32[]{:S(2)}, u32[]{:S(2)}) collective-permute-start(f32[3,512,128]{2,1,0:T(8,128)S(1)} %get-tuple-element.32), channel_id=1, source_target_pairs={{8,4},{16,12},{24,20},{9,5},{17,13},{25,21},{10,6},{18,14},{26,22}... | collective-permute-start | bytes 2359304 | tf_op jit(solution)/shard_map/ppermute | solution.py:891
  33.9 4.8 %collective-permute-start.6 = (f32[8,128]{1,0:T(8,128)S(1)}, f32[8,128]{1,0:T(8,128)S(1)}, u32[]{:S(2)}, u32[]{:S(2)}) collective-permute-start(f32[8,128]{1,0:T(8,128)S(1)} %local_sums.1.refs_1_), channel_id=1, source_target_pairs={{0,1},{1,0},{2,3},{3,2},{4,5},{5,4},{6,7},{7,6},{8,9},{9,8},{10,11... | collective-permute-start | bytes 12296 | tf_op jit(solution)/shard_map/ppermute | solution.py:444
  36.1 8.9 %collective-permute-start.7 = (f32[8,128]{1,0:T(8,128)S(1)}, f32[8,128]{1,0:T(8,128)S(1)}, u32[]{:S(2)}, u32[]{:S(2)}) collective-permute-start(f32[8,128]{1,0:T(8,128)S(1)} %local_sums.1.refs_1_), channel_id=1, source_target_pairs={{0,2},{1,3},{2,0},{3,1},{4,6},{5,7},{6,4},{7,5},{8,10},{9,11},{10,... | collective-permute-start | bytes 12296 | tf_op jit(solution)/shard_map/ppermute | solution.py:444
  38.7 6.3 %collective-permute-start.8 = (f32[8,128]{1,0:T(8,128)S(1)}, f32[8,128]{1,0:T(8,128)S(1)}, u32[]{:S(2)}, u32[]{:S(2)}) collective-permute-start(f32[8,128]{1,0:T(8,128)S(1)} %local_sums.1.refs_1_), channel_id=1, source_target_pairs={{0,3},{1,2},{2,1},{3,0},{4,7},{5,6},{6,5},{7,4},{8,11},{9,10},{10,... | collective-permute-start | bytes 12296 | tf_op jit(solution)/shard_map/ppermute | solution.py:444
  50.2 3.7 %collective-permute-start.11 = (f32[8,128]{1,0:T(8,128)S(1)}, f32[8,128]{1,0:T(8,128)S(1)}, u32[]{:S(2)}, u32[]{:S(2)}) collective-permute-start(f32[8,128]{1,0:T(8,128)S(1)} %get-tuple-element.35), channel_id=1, source_target_pairs={{0,1},{1,0},{2,3},{3,2},{4,5},{5,4},{6,7},{7,6},{8,9},{9,8},{10,11... | collective-permute-start | bytes 12296 | tf_op jit(solution)/shard_map/ppermute | solution.py:452
  53.9 4.5 %collective-permute-start.12 = (f32[8,128]{1,0:T(8,128)S(1)}, f32[8,128]{1,0:T(8,128)S(1)}, u32[]{:S(2)}, u32[]{:S(2)}) collective-permute-start(f32[8,128]{1,0:T(8,128)S(1)} %add.7.refs_0_), channel_id=1, source_target_pairs={{0,2},{1,3},{2,0},{3,1},{4,6},{5,7},{6,4},{7,5},{8,10},{9,11},{10,... | collective-permute-start | bytes 12296 | tf_op jit(solution)/shard_map/ppermute | solution.py:453

commit v16 on v13

--- a/solution.py
+++ b/solution.py
@@ -442,7 +442,7 @@
     if size not in (2, 4):
         return [lax.psum(tile, "vel")]
     others = [lax.ppermute(tile, "vel", [(i, i ^ s) for i in range(size)]) for s in range(1, size)]
-    return [tile, *others]
+    return [tile, *reversed(others)]
 
 
 def doubling_sums(tile):
@@ -455,6 +455,7 @@
 
 def add_tiles(refs):
     tiles = [r[...] for r in refs]
+    tiles = tiles[:1] + tiles[:0:-1]
     while len(tiles) > 1:
         tiles = [tiles[i] + tiles[i + 1] for i in range(0, len(tiles), 2)]
     return tiles[0]
@@ -797,38 +798,54 @@
     )(geo, pairs, near, old, part)
 
 
-def last_far_kernel(geo_ref, pairs_ref, halo_ref, old_ref, sums_in, terms_ref, sums_out, parts_ref):
+def last_far_kernel(count, geo_ref, pairs_ref, *refs):
+    halos, (old_ref, sums_in, terms_ref, sums_out, parts_ref) = refs[:count], refs[count:]
     rows = old_ref.shape[1]
     planes = rows // CHUNKS
     parts_ref[...] = jnp.zeros_like(parts_ref)
 
     def run(high):
-        def group(j, _):
-            at = at_rows(j * SUB)
-            _first, terms = side_terms(high, pairs_ref, halo_ref, old_ref, at)
-            for e in range(REACH):
-                terms_ref[e, at, :] = terms[e]
-            return 0
-
-        lax.fori_loop(0, rows // SUB, group, 0, unroll=unroll(rows // SUB, 8))
+        def add(halo_ref):
+            def group(j, _):
+                at = at_rows(j * SUB)
+                _first, terms = side_terms(high, pairs_ref, halo_ref, old_ref, at)
+                for e in range(REACH):
+                    terms_ref[e, at, :] = terms[e]
+                return 0
+
+            lax.fori_loop(0, rows // SUB, group, 0, unroll=unroll(rows // SUB, 8))
+
+        if count == 1 or not high:
+            add(halos[0])
+        else:
+            late = lax.axis_index("space") == LATE_FLOW[1]
+
+            @pl.when(late)
+            def _():
+                add(halos[1])
+
+            @pl.when(jnp.logical_not(late))
+            def _():
+                add(halos[0])
+
         y = polynomial_sums(terms_ref, planes, parts_ref, SUB - REACH if high else 0)
         sums_out[...] = sums_in[...] + pack_sums(finish_polynomials(y, geo_ref[FIRST], planes), 0)
 
     for_side(True, run)
 
 
-def last_far(geo, pairs, far, old, sums):
+def last_far(geo, pairs, halos, old, sums):
     rows = old.shape[1]
     return pl.pallas_call(
-        last_far_kernel,
-        in_specs=[spec(pltpu.VMEM)] * 5,
+        functools.partial(last_far_kernel, len(halos)),
+        in_specs=[spec(pltpu.VMEM)] * (4 + len(halos)),
         out_specs=[spec(pltpu.VMEM)] * 2,
         out_shape=[array(REACH, rows, LANES), array(SUB, LANES)],
         scratch_shapes=[pltpu.VMEM((10, SUB * SUB, LANES), F32)],
         compiler_params=params(),
         cost_estimate=traffic(rows, 2),
         name="last_far",
-    )(geo, pairs, far, old, sums)
+    )(geo, pairs, *halos, old, sums)
 
 
 LAST_PARTS = 4
@@ -877,9 +894,19 @@
     )(part, terms)
 
 
-def swap(rows, start):
+LATE_SLABS = 8
+LATE_FLOW = (2, 1)
+
+
+def swap(rows, start, without=()):
     pairs = [(i, i + 1) for i in range(start, lax.axis_size("space") - 1, 2)]
-    return lax.ppermute(rows, "space", pairs + [(j, i) for i, j in pairs])
+    pairs = pairs + [(j, i) for i, j in pairs]
+    return lax.ppermute(rows, "space", [p for p in pairs if p not in without])
+
+
+def late_flow(rows, after):
+    rows, _ = lax.optimization_barrier((rows, after))
+    return lax.ppermute(rows, "space", [LATE_FLOW])
 
 
 def per_device(particle_profile, neighbors, face_vectors, volumes, wall_temp):
@@ -911,12 +938,17 @@
     part, near = edge(False, pairs, near, f, part)
     near = swap(near, 0)
     f, far = edge(True, pairs, far, f, part)
-    far = swap(far, 1)
-    tiles = gather_sums(local_sums(links, geo, f))
+    sums = local_sums(links, geo, f)
+    if lax.axis_size("space") == LATE_SLABS:
+        halos = [swap(far, 1, (LATE_FLOW,)), late_flow(far, sums)]
+        sums, near = lax.optimization_barrier((sums, near))
+    else:
+        halos = [swap(far, 1)]
+    tiles = gather_sums(sums)
     (part,) = flux(False, links, geo, f)
     (part,) = add_target(links, geo, absorbed, tiles, f, part)
     part, sums = last_near(geo, pairs, near, f, part)
-    terms, sums = last_far(geo, pairs, far, f, sums)
+    terms, sums = last_far(geo, pairs, halos, f, sums)
     tiles = doubling_sums(sums)
     native = result(part, terms)
     macro_quantities = macro(tiles)

time: 57.4 us -> 57.6 us (level)
  the two profiles are of different devices: /device:TPU:4 before, /device:TPU:1 now
where the time goes in v16:
time: 57.6 us; the launch traced here: 57.4 us
  Pallas kernels  26.6 us (46%)
  starting transfers between devices  20.7 us (36%)
  waiting for transfers between devices  8.53 us (15%)
  between operations  0.86 us (1%)
  local copies, waits for them, and re-layouts  0.69 us (1%)
    ppermute x6, starting transfers between devices, gather_sums(): lax.ppermute(tile, 'vel', [(i, i ^ s) for i in range(size)])  7.94 us
    pallas_call x2, Pallas kernels, flux(): pl.pallas_call(functools.partial(flux_kernel, with_pairs), in_specs=[spec...  7.4 us
    ppermute x4, starting transfers between devices, swap(): return lax.ppermute(rows, 'space', [p for p in pairs if p not in without])  7.3 us
    pallas_call x2, Pallas kernels, add_target(): pl.pallas_call(kernel, in_specs=[spec(pltpu.SMEM)] + [vmem] * (len(given)...  6.86 us
    ppermute x1, waiting for transfers between devices, late_flow(): return lax.ppermute(rows, 'space', [LATE_FLOW])  6.49 us
    ppermute x1, starting transfers between devices, doubling_sums(): return [pair, lax.ppermute(pair, 'vel', [(i, i ^ 2) for i in range(size)])]  2.47 us
    pallas_call x1, Pallas kernels, first_rows(): pl.pallas_call(first_rows_kernel, in_specs=[spec(pltpu.HBM)], out_specs=[...  2.44 us
    pallas_call x2, Pallas kernels, edge(): pl.pallas_call(functools.partial(add_side, far), in_specs=[spec(pltpu.VME...  2.36 us
  transfers between devices with their start and end apart: 13, of which 3 were waited for; matrix products, arithmetic and copies ran while one was open for 1% of the time, Pallas kernels for 40%

profile of v16, /device:TPU:1, one launch (start us, length us, event | category | flops | bytes accessed | tf_op | source)
XLA Modules:
  0.0 57.4 jit_solution(18073214942513087104)
XLA Ops:
  0.7 2.4 %first_rows.1 = (f32[4096,128]{1,0:T(8,128)S(1)}, f32[3,512,128]{2,1,0:T(8,128)}, f32[3,512,128]{2,1,0:T(8,128)}) custom-call(f32[4096,128]{1,0:T(8,128)} %bitcast.12), custom_call_target="tpu_custom_call" | custom-call | flops 16777216 | bytes 8388608 | tf_op jit(solution)/shard_map/first_rows/pallas_call | solution.py:389
  3.1 0.1 collective-permute-start.1
  3.2 4.5 %collective-permute-start = (f32[3,512,128]{2,1,0:T(8,128)}, f32[3,512,128]{2,1,0:T(8,128)S(1)}, u32[]{:S(2)}, u32[]{:S(2)}) collective-permute-start(f32[3,512,128]{2,1,0:T(8,128)} %get-tuple-element.25), channel_id=1, source_target_pairs={{4,8},{12,16},{20,24},{8,4},{16,12},{24,20},{5,9},{13,17},{21,25},... | collective-permute-start | bytes 2359304 | tf_op jit(solution)/shard_map/ppermute | solution.py:904
  7.7 0.1 copy.18
  7.8 0.1 copy.13
  7.9 0.0 copy-done.3
  7.9 0.1 copy.14
  8.0 0.1 copy.15
  8.1 0.1 copy.16
  8.2 0.1 concatenate.3
  8.2 0.1 copy.17
  8.3 0.1 broadcast_in_dim.23.geo_ref.geo_in
  8.4 2.2 %first_sums.1 = (f32[8,512,128]{2,1,0:T(8,128)S(1)}, f32[8,128]{1,0:T(8,128)S(1)}) custom-call(s32[6,8]{1,0:T(8,128)S(1)} %get-tuple-element.43.links_ref, f32[33,8,128]{2,1,0:T(8,128)S(1)} %broadcast_in_dim.23.geo_ref.geo_in, f32[4096,128]{1,0:T(8,128)S(1)} %get-tuple-element.22.native_ref), custom_call_target="tpu_custom_call" | custom-call | flops 20971520 | bytes 10485760 | tf_op jit(solution)/shard_map/first_sums/pallas_call | solution.py:327
  10.6 3.4 %collective-permute-start.2 = (f32[8,128]{1,0:T(8,128)S(1)}, f32[8,128]{1,0:T(8,128)S(1)}, u32[]{:S(2)}, u32[]{:S(2)}) collective-permute-start(f32[8,128]{1,0:T(8,128)S(1)} %get-tuple-element.27.refs_0_), channel_id=1, source_target_pairs={{0,3},{1,2},{2,1},{3,0},{4,7},{5,6},{6,5},{7,4},{8,11},{9,10},{10,... | collective-permute-start | bytes 12296 | tf_op jit(solution)/shard_map/ppermute | solution.py:444
  14.0 0.0 collective-permute-start.3
  14.0 0.4 collective-permute-start.4
  14.3 4.4 %flux.2 = (f32[8,512,128]{2,1,0:T(8,128)S(1)}, f32[12,512,128]{2,1,0:T(8,128)S(1)}) custom-call(s32[6,8]{1,0:T(8,128)S(1)} %get-tuple-element.43.links_ref, f32[33,8,128]{2,1,0:T(8,128)S(1)} %broadcast_in_dim.23.geo_ref.geo_in, f32[8,512,128]{2,1,0:T(8,128)S(1)} %get-tuple-element.23.f_ref.refs_4_.old_ref), custom_call_target="tpu_custom_call" | custom-call | flops 37748736 | bytes 18874368 | tf_op jit(solution)/shard_map/flux/pallas_call | solution.py:573
  18.8 0.0 collective-permute-done.2.refs_1_
  18.8 0.0 collective-permute-done.3.refs_2_
  18.8 0.0 collective-permute-done.4.refs_3_
  18.8 3.4 %add_target.2 = (f32[8,512,128]{2,1,0:T(8,128)S(1)}, f32[8,128]{1,0:T(8,128)S(1)}) custom-call(s32[6,8]{1,0:T(8,128)S(1)} %get-tuple-element.43.links_ref, f32[33,8,128]{2,1,0:T(8,128)S(1)} %broadcast_in_dim.23.geo_ref.geo_in, f32[8,128]{1,0:T(8,128)S(1)} %get-tuple-element.27.refs_0_, ...), custom_call_target="tpu_custom_call", output_to_operand_aliasing={{0}: (7, {})} | custom-call | flops 29360128 | bytes 14680064 | tf_op jit(solution)/shard_map/add_target/pallas_call | solution.py:704
  22.3 0.0 collective-permute-done.1.halo_ref
  22.3 1.8 %near_edge.1 = (f32[8,512,128]{2,1,0:T(8,128)S(1)}, f32[3,512,128]{2,1,0:T(8,128)S(1)}) custom-call(f32[12,512,128]{2,1,0:T(8,128)S(1)} %get-tuple-element.24.pairs_ref, f32[3,512,128]{2,1,0:T(8,128)} %collective-permute-done.1.halo_ref, f32[8,512,128]{2,1,0:T(8,128)S(1)} %get-tuple-element.23.f_ref.refs_4_.old_ref, ...), custom_call_target="tpu_custom_call", output_to_operand_aliasing={{0}: (3, {})} | custom-call | flops 8388608 | bytes 4194304 | tf_op jit(solution)/shard_map/near_edge/pallas_call | solution.py:767
  24.0 0.1 collective-permute-start.5
  24.1 1.0 %collective-permute-done.halo_ref = f32[3,512,128]{2,1,0:T(8,128)S(1)} collective-permute-done((f32[3,512,128]{2,1,0:T(8,128)}, f32[3,512,128]{2,1,0:T(8,128)S(1)}, u32[]{:S(2)}, u32[]{:S(2)}) %collective-permute-start) | collective-permute-done | bytes 786464 | tf_op jit(solution)/shard_map/ppermute | solution.py:904
  25.1 0.6 %far_edge.1 = (f32[8,512,128]{2,1,0:T(8,128)S(1)}, f32[3,512,128]{2,1,0:T(8,128)S(1)}) custom-call(f32[12,512,128]{2,1,0:T(8,128)S(1)} %get-tuple-element.24.pairs_ref, f32[3,512,128]{2,1,0:T(8,128)S(1)} %collective-permute-done.halo_ref, f32[8,512,128]{2,1,0:T(8,128)S(1)} %get-tuple-element.23.f_ref.refs_4_.old_ref, ...), custom_call_target="tpu_custom_call", output_to_operand_aliasing={{0}: (3, {})} | custom-call | flops 8388608 | bytes 4194304 | tf_op jit(solution)/shard_map/far_edge/pallas_call | solution.py:767
  25.7 2.6 %collective-permute-start.9 = (f32[3,512,128]{2,1,0:T(8,128)S(1)}, f32[3,512,128]{2,1,0:T(8,128)S(1)}, u32[]{:S(2)}, u32[]{:S(2)}) collective-permute-start(f32[3,512,128]{2,1,0:T(8,128)S(1)} %get-tuple-element.38), channel_id=1, source_target_pairs={{4,8},{12,16},{20,24},{16,12},{24,20},{5,9},{13,17},{21,25},{17,13... | collective-permute-start | bytes 2359304 | tf_op jit(solution)/shard_map/ppermute | solution.py:904
  28.4 1.5 %local_sums.1.refs_1_ = f32[8,128]{1,0:T(8,128)S(1)} custom-call(s32[6,8]{1,0:T(8,128)S(1)} %get-tuple-element.43.links_ref, f32[33,8,128]{2,1,0:T(8,128)S(1)} %broadcast_in_dim.23.geo_ref.geo_in, f32[8,512,128]{2,1,0:T(8,128)S(1)} %get-tuple-element.31.f_ref.refs_5_.old_ref.refs_2_), custom_call_target="tpu_custom_call" | custom-call | flops 16777216 | bytes 8388608 | tf_op jit(solution)/shard_map/local_sums/pallas_call | solution.py:309
  29.9 1.3 %collective-permute-start.10 = (f32[3,512,128]{2,1,0:T(8,128)S(1)}, f32[3,512,128]{2,1,0:T(8,128)S(1)}, u32[]{:S(2)}, u32[]{:S(2)}) collective-permute-start(f32[3,512,128]{2,1,0:T(8,128)S(1)} %get-tuple-element.38), channel_id=1, source_target_pairs={{8,4},{9,5},{10,6},{11,7}} | collective-permute-start | bytes 2359304 | tf_op jit(solution)/shard_map/ppermute | solution.py:909
  31.2 0.0 collective-permute-done.5.halo_ref
  31.2 3.8 %collective-permute-start.6 = (f32[8,128]{1,0:T(8,128)S(1)}, f32[8,128]{1,0:T(8,128)S(1)}, u32[]{:S(2)}, u32[]{:S(2)}) collective-permute-start(f32[8,128]{1,0:T(8,128)S(1)} %local_sums.1.refs_1_), channel_id=1, source_target_pairs={{0,3},{1,2},{2,1},{3,0},{4,7},{5,6},{6,5},{7,4},{8,11},{9,10},{10,... | collective-permute-start | bytes 12296 | tf_op jit(solution)/shard_map/ppermute | solution.py:444
  35.0 0.0 collective-permute-start.7
  35.0 0.4 collective-permute-start.8
  35.4 3.0 %flux.3.refs_6_ = f32[8,512,128]{2,1,0:T(8,128)S(1)} custom-call(s32[6,8]{1,0:T(8,128)S(1)} %get-tuple-element.43.links_ref, f32[33,8,128]{2,1,0:T(8,128)S(1)} %broadcast_in_dim.23.geo_ref.geo_in, f32[8,512,128]{2,1,0:T(8,128)S(1)} %get-tuple-element.31.f_ref.refs_5_.old_ref.refs_2_), custom_call_target="tpu_custom_call" | custom-call | flops 29360128 | bytes 14680064 | tf_op jit(solution)/shard_map/flux/pallas_call | solution.py:573
  38.4 0.0 collective-permute-done.6.refs_2_
  38.4 0.0 collective-permute-done.7.refs_3_
  38.4 0.0 collective-permute-done.8.refs_4_
  38.4 3.4 %add_target.3.part_ref = f32[8,512,128]{2,1,0:T(8,128)S(1)} custom-call(s32[6,8]{1,0:T(8,128)S(1)} %get-tuple-element.43.links_ref, f32[33,8,128]{2,1,0:T(8,128)S(1)} %broadcast_in_dim.23.geo_ref.geo_in, f32[8,128]{1,0:T(8,128)S(1)} %get-tuple-element.34.refs_0_, f32[8,128]{1,0:T(8,128)S(1)} %local_sums.1.refs_1_, ...), custom_call_target="tpu_custom_call", output_to_operand_aliasing={{}: (8, {})} | custom-call | flops 29360128 | bytes 14680064 | tf_op jit(solution)/shard_map/add_target/pallas_call | solution.py:704
  41.8 1.2 %last_near.1 = (f32[8,512,128]{2,1,0:T(8,128)S(1)}, f32[8,128]{1,0:T(8,128)S(1)}) custom-call(f32[33,8,128]{2,1,0:T(8,128)S(1)} %broadcast_in_dim.23.geo_ref.geo_in, f32[12,512,128]{2,1,0:T(8,128)S(1)} %get-tuple-element.24.pairs_ref, f32[3,512,128]{2,1,0:T(8,128)S(1)} %collective-permute-done.5.halo_ref, ...), custom_call_target="tpu_custom_call", output_to_operand_aliasing={{0}: (4, {})} | custom-call | flops 12582912 | bytes 6291456 | tf_op jit(solution)/shard_map/last_near/pallas_call | solution.py:788
  43.1 0.0 collective-permute-done.9.refs_0_
  43.1 6.5 %collective-permute-done.10.refs_1_ = f32[3,512,128]{2,1,0:T(8,128)S(1)} collective-permute-done((f32[3,512,128]{2,1,0:T(8,128)S(1)}, f32[3,512,128]{2,1,0:T(8,128)S(1)}, u32[]{:S(2)}, u32[]{:S(2)}) %collective-permute-start.10) | collective-permute-done | bytes 786464 | tf_op jit(solution)/shard_map/ppermute | solution.py:909
  49.6 0.5 last_far.1
  50.1 1.7 %collective-permute-start.11 = (f32[8,128]{1,0:T(8,128)S(1)}, f32[8,128]{1,0:T(8,128)S(1)}, u32[]{:S(2)}, u32[]{:S(2)}) collective-permute-start(f32[8,128]{1,0:T(8,128)S(1)} %get-tuple-element.41), channel_id=1, source_target_pairs={{0,1},{1,0},{2,3},{3,2},{4,5},{5,4},{6,7},{7,6},{8,9},{9,8},{10,11... | collective-permute-start | bytes 12296 | tf_op jit(solution)/shard_map/ppermute | solution.py:452
  51.8 1.0 %collective-permute-done.11 = f32[8,128]{1,0:T(8,128)S(1)} collective-permute-done((f32[8,128]{1,0:T(8,128)S(1)}, f32[8,128]{1,0:T(8,128)S(1)}, u32[]{:S(2)}, u32[]{:S(2)}) %collective-permute-start.11) | collective-permute-done | bytes 4128 | tf_op jit(solution)/shard_map/ppermute | solution.py:452
  52.8 2.5 %collective-permute-start.12 = (f32[8,128]{1,0:T(8,128)S(1)}, f32[8,128]{1,0:T(8,128)S(1)}, u32[]{:S(2)}, u32[]{:S(2)}) collective-permute-start(f32[8,128]{1,0:T(8,128)S(1)} %add.7.refs_0_), channel_id=1, source_target_pairs={{0,2},{1,3},{2,0},{3,1},{4,6},{5,7},{6,4},{7,5},{8,10},{9,11},{10,... | collective-permute-start | bytes 12296 | tf_op jit(solution)/shard_map/ppermute | solution.py:453
  55.2 1.4 %result.1 = f32[4096,128]{1,0:T(8,128)} custom-call(f32[8,512,128]{2,1,0:T(8,128)S(1)} %get-tuple-element.36.part_ref, f32[3,512,128]{2,1,0:T(8,128)S(1)} %get-tuple-element.40.terms_ref), custom_call_target="tpu_custom_call" | custom-call | flops 12582912 | bytes 6291456 | tf_op jit(solution)/shard_map/result/pallas_call | solution.py:885
  56.7 0.0 collective-permute-done.12.refs_1_
  56.7 0.7 %macro.1 = f32[8,8]{1,0:T(8,128)} custom-call(f32[8,128]{1,0:T(8,128)S(1)} %add.7.refs_0_, f32[8,128]{1,0:T(8,128)S(1)} %collective-permute-done.12.refs_1_), custom_call_target="tpu_custom_call" | custom-call | tf_op jit(solution)/shard_map/macro/pallas_call | solution.py:491
  (11 shorter events, 0.0 us)
Async XLA Ops:
  0.6 7.1 %copy-start = (f32[3,6,8]{2,1,0:T(8,128)S(1)}, f32[3,6,8]{2,1,0:T(8,128)}, u32[]{:S(2)}) copy-start(f32[3,6,8]{2,1,0:T(8,128)} %param.7) | copy-start | bytes 1732
  0.6 7.2 %copy-start.2 = (f32[8]{0:T(128)S(1)}, f32[8]{0:T(128)}, u32[]{:S(2)}) copy-start(f32[8]{0:T(128)} %param.8) | copy-start | bytes 100
  0.7 7.2 %copy-start.3 = (f32[8]{0:T(128)S(1)}, f32[8]{0:T(128)}, u32[]{:S(2)}) copy-start(f32[8]{0:T(128)} %param.9) | copy-start | bytes 100
  0.7 7.3 %copy-start.1 = (s32[6,8]{1,0:T(8,128)S(1)}, s32[6,8]{1,0:T(8,128)}, u32[]{:S(2)}) copy-start(s32[6,8]{1,0:T(8,128)} %param.6) | copy-start | bytes 580
  3.1 19.1 %collective-permute-start.1 = (f32[3,512,128]{2,1,0:T(8,128)}, f32[3,512,128]{2,1,0:T(8,128)}, u32[]{:S(2)}, u32[]{:S(2)}) collective-permute-start(f32[3,512,128]{2,1,0:T(8,128)} %get-tuple-element.26), channel_id=1, source_target_pairs={{0,4},{8,12},{16,20},{24,28},{4,0},{12,8},{20,16},{28,24},{1,5},{9... | collective-permute-start | bytes 2359304 | tf_op jit(solution)/shard_map/ppermute | solution.py:904
  3.2 21.9 %collective-permute-start = (f32[3,512,128]{2,1,0:T(8,128)}, f32[3,512,128]{2,1,0:T(8,128)S(1)}, u32[]{:S(2)}, u32[]{:S(2)}) collective-permute-start(f32[3,512,128]{2,1,0:T(8,128)} %get-tuple-element.25), channel_id=1, source_target_pairs={{4,8},{12,16},{20,24},{8,4},{16,12},{24,20},{5,9},{13,17},{21,25},... | collective-permute-start | bytes 2359304 | tf_op jit(solution)/shard_map/ppermute | solution.py:904
  10.6 8.2 %collective-permute-start.2 = (f32[8,128]{1,0:T(8,128)S(1)}, f32[8,128]{1,0:T(8,128)S(1)}, u32[]{:S(2)}, u32[]{:S(2)}) collective-permute-start(f32[8,128]{1,0:T(8,128)S(1)} %get-tuple-element.27.refs_0_), channel_id=1, source_target_pairs={{0,3},{1,2},{2,1},{3,0},{4,7},{5,6},{6,5},{7,4},{8,11},{9,10},{10,... | collective-permute-start | bytes 12296 | tf_op jit(solution)/shard_map/ppermute | solution.py:444
  14.0 4.8 %collective-permute-start.3 = (f32[8,128]{1,0:T(8,128)S(1)}, f32[8,128]{1,0:T(8,128)S(1)}, u32[]{:S(2)}, u32[]{:S(2)}) collective-permute-start(f32[8,128]{1,0:T(8,128)S(1)} %get-tuple-element.27.refs_0_), channel_id=1, source_target_pairs={{0,2},{1,3},{2,0},{3,1},{4,6},{5,7},{6,4},{7,5},{8,10},{9,11},{10,... | collective-permute-start | bytes 12296 | tf_op jit(solution)/shard_map/ppermute | solution.py:444
  14.0 4.8 %collective-permute-start.4 = (f32[8,128]{1,0:T(8,128)S(1)}, f32[8,128]{1,0:T(8,128)S(1)}, u32[]{:S(2)}, u32[]{:S(2)}) collective-permute-start(f32[8,128]{1,0:T(8,128)S(1)} %get-tuple-element.27.refs_0_), channel_id=1, source_target_pairs={{0,1},{1,0},{2,3},{3,2},{4,5},{5,4},{6,7},{7,6},{8,9},{9,8},{10,11... | collective-permute-start | bytes 12296 | tf_op jit(solution)/shard_map/ppermute | solution.py:444
  24.0 7.2 %collective-permute-start.5 = (f32[3,512,128]{2,1,0:T(8,128)S(1)}, f32[3,512,128]{2,1,0:T(8,128)S(1)}, u32[]{:S(2)}, u32[]{:S(2)}) collective-permute-start(f32[3,512,128]{2,1,0:T(8,128)S(1)} %get-tuple-element.32), channel_id=1, source_target_pairs={{0,4},{8,12},{16,20},{24,28},{4,0},{12,8},{20,16},{28,24},{1,5},{9... | collective-permute-start | bytes 2359304 | tf_op jit(solution)/shard_map/ppermute | solution.py:904
  25.7 17.3 %collective-permute-start.9 = (f32[3,512,128]{2,1,0:T(8,128)S(1)}, f32[3,512,128]{2,1,0:T(8,128)S(1)}, u32[]{:S(2)}, u32[]{:S(2)}) collective-permute-start(f32[3,512,128]{2,1,0:T(8,128)S(1)} %get-tuple-element.38), channel_id=1, source_target_pairs={{4,8},{12,16},{20,24},{16,12},{24,20},{5,9},{13,17},{21,25},{17,13... | collective-permute-start | bytes 2359304 | tf_op jit(solution)/shard_map/ppermute | solution.py:904
  29.9 19.7 %collective-permute-start.10 = (f32[3,512,128]{2,1,0:T(8,128)S(1)}, f32[3,512,128]{2,1,0:T(8,128)S(1)}, u32[]{:S(2)}, u32[]{:S(2)}) collective-permute-start(f32[3,512,128]{2,1,0:T(8,128)S(1)} %get-tuple-element.38), channel_id=1, source_target_pairs={{8,4},{9,5},{10,6},{11,7}} | collective-permute-start | bytes 2359304 | tf_op jit(solution)/shard_map/ppermute | solution.py:909
  31.2 7.2 %collective-permute-start.6 = (f32[8,128]{1,0:T(8,128)S(1)}, f32[8,128]{1,0:T(8,128)S(1)}, u32[]{:S(2)}, u32[]{:S(2)}) collective-permute-start(f32[8,128]{1,0:T(8,128)S(1)} %local_sums.1.refs_1_), channel_id=1, source_target_pairs={{0,3},{1,2},{2,1},{3,0},{4,7},{5,6},{6,5},{7,4},{8,11},{9,10},{10,... | collective-permute-start | bytes 12296 | tf_op jit(solution)/shard_map/ppermute | solution.py:444
  35.0 3.4 %collective-permute-start.7 = (f32[8,128]{1,0:T(8,128)S(1)}, f32[8,128]{1,0:T(8,128)S(1)}, u32[]{:S(2)}, u32[]{:S(2)}) collective-permute-start(f32[8,128]{1,0:T(8,128)S(1)} %local_sums.1.refs_1_), channel_id=1, source_target_pairs={{0,2},{1,3},{2,0},{3,1},{4,6},{5,7},{6,4},{7,5},{8,10},{9,11},{10,... | collective-permute-start | bytes 12296 | tf_op jit(solution)/shard_map/ppermute | solution.py:444
  35.0 3.4 %collective-permute-start.8 = (f32[8,128]{1,0:T(8,128)S(1)}, f32[8,128]{1,0:T(8,128)S(1)}, u32[]{:S(2)}, u32[]{:S(2)}) collective-permute-start(f32[8,128]{1,0:T(8,128)S(1)} %local_sums.1.refs_1_), channel_id=1, source_target_pairs={{0,1},{1,0},{2,3},{3,2},{4,5},{5,4},{6,7},{7,6},{8,9},{9,8},{10,11... | collective-permute-start | bytes 12296 | tf_op jit(solution)/shard_map/ppermute | solution.py:444
  50.1 2.7 %collective-permute-start.11 = (f32[8,128]{1,0:T(8,128)S(1)}, f32[8,128]{1,0:T(8,128)S(1)}, u32[]{:S(2)}, u32[]{:S(2)}) collective-permute-start(f32[8,128]{1,0:T(8,128)S(1)} %get-tuple-element.41), channel_id=1, source_target_pairs={{0,1},{1,0},{2,3},{3,2},{4,5},{5,4},{6,7},{7,6},{8,9},{9,8},{10,11... | collective-permute-start | bytes 12296 | tf_op jit(solution)/shard_map/ppermute | solution.py:452
  52.8 3.9 %collective-permute-start.12 = (f32[8,128]{1,0:T(8,128)S(1)}, f32[8,128]{1,0:T(8,128)S(1)}, u32[]{:S(2)}, u32[]{:S(2)}) collective-permute-start(f32[8,128]{1,0:T(8,128)S(1)} %add.7.refs_0_), channel_id=1, source_target_pairs={{0,2},{1,3},{2,0},{3,1},{4,6},{5,7},{6,4},{7,5},{8,10},{9,11},{10,... | collective-permute-start | bytes 12296 | tf_op jit(solution)/shard_map/ppermute | solution.py:453

commit v17 on v16

--- a/solution.py
+++ b/solution.py
@@ -816,17 +816,17 @@
             lax.fori_loop(0, rows // SUB, group, 0, unroll=unroll(rows // SUB, 8))
 
         if count == 1 or not high:
-            add(halos[0])
+            add(halos[-1])
         else:
             late = lax.axis_index("space") == LATE_FLOW[1]
 
             @pl.when(late)
             def _():
-                add(halos[1])
+                add(halos[0])
 
             @pl.when(jnp.logical_not(late))
             def _():
-                add(halos[0])
+                add(halos[-1])
 
         y = polynomial_sums(terms_ref, planes, parts_ref, SUB - REACH if high else 0)
         sums_out[...] = sums_in[...] + pack_sums(finish_polynomials(y, geo_ref[FIRST], planes), 0)
@@ -904,8 +904,7 @@
     return lax.ppermute(rows, "space", [p for p in pairs if p not in without])
 
 
-def late_flow(rows, after):
-    rows, _ = lax.optimization_barrier((rows, after))
+def late_flow(rows):
     return lax.ppermute(rows, "space", [LATE_FLOW])
 
 
@@ -940,7 +939,7 @@
     f, far = edge(True, pairs, far, f, part)
     sums = local_sums(links, geo, f)
     if lax.axis_size("space") == LATE_SLABS:
-        halos = [swap(far, 1, (LATE_FLOW,)), late_flow(far, sums)]
+        halos = [late_flow(far), swap(far, 1, (LATE_FLOW,))]
         sums, near = lax.optimization_barrier((sums, near))
     else:
         halos = [swap(far, 1)]

time: 57.6 us -> 57.9 us (level)
  the two profiles are of different devices: /device:TPU:1 before, /device:TPU:4 now
where the time goes in v17:
time: 57.9 us; the launch traced here: 57.4 us
  Pallas kernels  26.7 us (46%)
  starting transfers between devices  22.3 us (39%)
  waiting for transfers between devices  6.93 us (12%)
  between operations  0.83 us (1%)
  local copies, waits for them, and re-layouts  0.69 us (1%)
    ppermute x6, starting transfers between devices, gather_sums(): lax.ppermute(tile, 'vel', [(i, i ^ s) for i in range(size)])  8.88 us
    pallas_call x2, Pallas kernels, flux(): pl.pallas_call(functools.partial(flux_kernel, with_pairs), in_specs=[spec...  7.49 us
    ppermute x4, starting transfers between devices, swap(): return lax.ppermute(rows, 'space', [p for p in pairs if p not in without])  7.3 us
    pallas_call x2, Pallas kernels, add_target(): pl.pallas_call(kernel, in_specs=[spec(pltpu.SMEM)] + [vmem] * (len(given)...  6.85 us
    ppermute x4, waiting for transfers between devices, swap(): return lax.ppermute(rows, 'space', [p for p in pairs if p not in without])  4.65 us
    ppermute x1, starting transfers between devices, doubling_sums(): return [pair, lax.ppermute(pair, 'vel', [(i, i ^ 2) for i in range(size)])]  3.03 us
    pallas_call x1, Pallas kernels, first_rows(): pl.pallas_call(first_rows_kernel, in_specs=[spec(pltpu.HBM)], out_specs=[...  2.44 us
    pallas_call x2, Pallas kernels, edge(): pl.pallas_call(functools.partial(add_side, far), in_specs=[spec(pltpu.VME...  2.36 us
  transfers between devices with their start and end apart: 13, of which 5 were waited for; matrix products, arithmetic and copies ran while one was open for 1% of the time, Pallas kernels for 40%

profile of v17, /device:TPU:4, one launch (start us, length us, event | category | flops | bytes accessed | tf_op | source)
XLA Modules:
  0.0 57.4 jit_solution(12620802588396170525)
XLA Ops:
  0.6 0.0 copy-start.1
  0.7 2.4 %first_rows.1 = (f32[4096,128]{1,0:T(8,128)S(1)}, f32[3,512,128]{2,1,0:T(8,128)}, f32[3,512,128]{2,1,0:T(8,128)}) custom-call(f32[4096,128]{1,0:T(8,128)} %bitcast.12), custom_call_target="tpu_custom_call" | custom-call | flops 16777216 | bytes 8388608 | tf_op jit(solution)/shard_map/first_rows/pallas_call | solution.py:389
  3.1 0.1 collective-permute-start.1
  3.2 3.4 %collective-permute-start = (f32[3,512,128]{2,1,0:T(8,128)}, f32[3,512,128]{2,1,0:T(8,128)S(1)}, u32[]{:S(2)}, u32[]{:S(2)}) collective-permute-start(f32[3,512,128]{2,1,0:T(8,128)} %get-tuple-element.24), channel_id=1, source_target_pairs={{4,8},{12,16},{20,24},{8,4},{16,12},{24,20},{5,9},{13,17},{21,25},... | collective-permute-start | bytes 2359304 | tf_op jit(solution)/shard_map/ppermute | solution.py:904
  6.7 0.1 copy.15
  6.7 0.1 copy.16
  6.8 0.1 copy.18
  6.9 0.1 copy.13
  7.0 0.1 copy.14
  7.1 0.1 concatenate.3
  7.2 0.1 copy.17
  7.3 0.1 broadcast_in_dim.23.geo_ref.geo_in
  7.4 2.2 %first_sums.1 = (f32[8,512,128]{2,1,0:T(8,128)S(1)}, f32[8,128]{1,0:T(8,128)S(1)}) custom-call(s32[6,8]{1,0:T(8,128)S(1)} %get-tuple-element.41.links_ref, f32[33,8,128]{2,1,0:T(8,128)S(1)} %broadcast_in_dim.23.geo_ref.geo_in, f32[4096,128]{1,0:T(8,128)S(1)} %get-tuple-element.21.native_ref), custom_call_target="tpu_custom_call" | custom-call | flops 20971520 | bytes 10485760 | tf_op jit(solution)/shard_map/first_sums/pallas_call | solution.py:327
  9.5 3.7 %collective-permute-start.2 = (f32[8,128]{1,0:T(8,128)S(1)}, f32[8,128]{1,0:T(8,128)S(1)}, u32[]{:S(2)}, u32[]{:S(2)}) collective-permute-start(f32[8,128]{1,0:T(8,128)S(1)} %get-tuple-element.26.refs_0_), channel_id=1, source_target_pairs={{0,3},{1,2},{2,1},{3,0},{4,7},{5,6},{6,5},{7,4},{8,11},{9,10},{10,... | collective-permute-start | bytes 12296 | tf_op jit(solution)/shard_map/ppermute | solution.py:444
  13.2 0.0 collective-permute-start.3
  13.2 0.8 %collective-permute-start.4 = (f32[8,128]{1,0:T(8,128)S(1)}, f32[8,128]{1,0:T(8,128)S(1)}, u32[]{:S(2)}, u32[]{:S(2)}) collective-permute-start(f32[8,128]{1,0:T(8,128)S(1)} %get-tuple-element.26.refs_0_), channel_id=1, source_target_pairs={{0,1},{1,0},{2,3},{3,2},{4,5},{5,4},{6,7},{7,6},{8,9},{9,8},{10,11... | collective-permute-start | bytes 12296 | tf_op jit(solution)/shard_map/ppermute | solution.py:444
  14.0 4.3 %flux.2 = (f32[8,512,128]{2,1,0:T(8,128)S(1)}, f32[12,512,128]{2,1,0:T(8,128)S(1)}) custom-call(s32[6,8]{1,0:T(8,128)S(1)} %get-tuple-element.41.links_ref, f32[33,8,128]{2,1,0:T(8,128)S(1)} %broadcast_in_dim.23.geo_ref.geo_in, f32[8,512,128]{2,1,0:T(8,128)S(1)} %get-tuple-element.22.f_ref.refs_4_.old_ref), custom_call_target="tpu_custom_call" | custom-call | flops 37748736 | bytes 18874368 | tf_op jit(solution)/shard_map/flux/pallas_call | solution.py:573
  18.3 0.0 collective-permute-done.2.refs_1_
  18.3 0.0 collective-permute-done.3.refs_2_
  18.3 0.0 collective-permute-done.4.refs_3_
  18.3 3.4 %add_target.2 = (f32[8,512,128]{2,1,0:T(8,128)S(1)}, f32[8,128]{1,0:T(8,128)S(1)}) custom-call(s32[6,8]{1,0:T(8,128)S(1)} %get-tuple-element.41.links_ref, f32[33,8,128]{2,1,0:T(8,128)S(1)} %broadcast_in_dim.23.geo_ref.geo_in, f32[8,128]{1,0:T(8,128)S(1)} %get-tuple-element.26.refs_0_, ...), custom_call_target="tpu_custom_call", output_to_operand_aliasing={{0}: (7, {})} | custom-call | flops 29360128 | bytes 14680064 | tf_op jit(solution)/shard_map/add_target/pallas_call | solution.py:704
  21.8 0.0 collective-permute-done.1.halo_ref
  21.8 1.7 %near_edge.1 = (f32[8,512,128]{2,1,0:T(8,128)S(1)}, f32[3,512,128]{2,1,0:T(8,128)S(1)}) custom-call(f32[12,512,128]{2,1,0:T(8,128)S(1)} %get-tuple-element.23.pairs_ref, f32[3,512,128]{2,1,0:T(8,128)} %collective-permute-done.1.halo_ref, f32[8,512,128]{2,1,0:T(8,128)S(1)} %get-tuple-element.22.f_ref.refs_4_.old_ref, ...), custom_call_target="tpu_custom_call", output_to_operand_aliasing={{0}: (3, {})} | custom-call | flops 8388608 | bytes 4194304 | tf_op jit(solution)/shard_map/near_edge/pallas_call | solution.py:767
  23.5 0.1 collective-permute-start.5
  23.6 1.5 %collective-permute-done.halo_ref = f32[3,512,128]{2,1,0:T(8,128)S(1)} collective-permute-done((f32[3,512,128]{2,1,0:T(8,128)}, f32[3,512,128]{2,1,0:T(8,128)S(1)}, u32[]{:S(2)}, u32[]{:S(2)}) %collective-permute-start) | collective-permute-done | bytes 786464 | tf_op jit(solution)/shard_map/ppermute | solution.py:904
  25.1 0.6 %far_edge.1 = (f32[8,512,128]{2,1,0:T(8,128)S(1)}, f32[3,512,128]{2,1,0:T(8,128)S(1)}) custom-call(f32[12,512,128]{2,1,0:T(8,128)S(1)} %get-tuple-element.23.pairs_ref, f32[3,512,128]{2,1,0:T(8,128)S(1)} %collective-permute-done.halo_ref, f32[8,512,128]{2,1,0:T(8,128)S(1)} %get-tuple-element.22.f_ref.refs_4_.old_ref, ...), custom_call_target="tpu_custom_call", output_to_operand_aliasing={{0}: (3, {})} | custom-call | flops 8388608 | bytes 4194304 | tf_op jit(solution)/shard_map/far_edge/pallas_call | solution.py:767
  25.8 3.7 %collective-permute-start.10 = (f32[3,512,128]{2,1,0:T(8,128)S(1)}, f32[3,512,128]{2,1,0:T(8,128)S(1)}, u32[]{:S(2)}, u32[]{:S(2)}) collective-permute-start(f32[3,512,128]{2,1,0:T(8,128)S(1)} %get-tuple-element.36), channel_id=1, source_target_pairs={{4,8},{12,16},{20,24},{16,12},{24,20},{5,9},{13,17},{21,25},{17,13... | collective-permute-start | bytes 2359304 | tf_op jit(solution)/shard_map/ppermute | solution.py:904
  29.5 0.7 %collective-permute-start.9 = (f32[3,512,128]{2,1,0:T(8,128)S(1)}, f32[3,512,128]{2,1,0:T(8,128)S(1)}, u32[]{:S(2)}, u32[]{:S(2)}) collective-permute-start(f32[3,512,128]{2,1,0:T(8,128)S(1)} %get-tuple-element.36), channel_id=1, source_target_pairs={{8,4},{9,5},{10,6},{11,7}} | collective-permute-start | bytes 2359304 | tf_op jit(solution)/shard_map/ppermute | solution.py:908
  30.2 1.5 %local_sums.1.refs_1_ = f32[8,128]{1,0:T(8,128)S(1)} custom-call(s32[6,8]{1,0:T(8,128)S(1)} %get-tuple-element.41.links_ref, f32[33,8,128]{2,1,0:T(8,128)S(1)} %broadcast_in_dim.23.geo_ref.geo_in, f32[8,512,128]{2,1,0:T(8,128)S(1)} %get-tuple-element.30.f_ref.refs_5_.old_ref.refs_2_), custom_call_target="tpu_custom_call" | custom-call | flops 16777216 | bytes 8388608 | tf_op jit(solution)/shard_map/local_sums/pallas_call | solution.py:309
  31.7 0.0 collective-permute-done.5.halo_ref
  31.7 3.7 %collective-permute-start.6 = (f32[8,128]{1,0:T(8,128)S(1)}, f32[8,128]{1,0:T(8,128)S(1)}, u32[]{:S(2)}, u32[]{:S(2)}) collective-permute-start(f32[8,128]{1,0:T(8,128)S(1)} %local_sums.1.refs_1_), channel_id=1, source_target_pairs={{0,3},{1,2},{2,1},{3,0},{4,7},{5,6},{6,5},{7,4},{8,11},{9,10},{10,... | collective-permute-start | bytes 12296 | tf_op jit(solution)/shard_map/ppermute | solution.py:444
  35.4 0.0 collective-permute-start.7
  35.4 0.8 %collective-permute-start.8 = (f32[8,128]{1,0:T(8,128)S(1)}, f32[8,128]{1,0:T(8,128)S(1)}, u32[]{:S(2)}, u32[]{:S(2)}) collective-permute-start(f32[8,128]{1,0:T(8,128)S(1)} %local_sums.1.refs_1_), channel_id=1, source_target_pairs={{0,1},{1,0},{2,3},{3,2},{4,5},{5,4},{6,7},{7,6},{8,9},{9,8},{10,11... | collective-permute-start | bytes 12296 | tf_op jit(solution)/shard_map/ppermute | solution.py:444
  36.2 3.2 %flux.3.refs_6_ = f32[8,512,128]{2,1,0:T(8,128)S(1)} custom-call(s32[6,8]{1,0:T(8,128)S(1)} %get-tuple-element.41.links_ref, f32[33,8,128]{2,1,0:T(8,128)S(1)} %broadcast_in_dim.23.geo_ref.geo_in, f32[8,512,128]{2,1,0:T(8,128)S(1)} %get-tuple-element.30.f_ref.refs_5_.old_ref.refs_2_), custom_call_target="tpu_custom_call" | custom-call | flops 29360128 | bytes 14680064 | tf_op jit(solution)/shard_map/flux/pallas_call | solution.py:573
  39.3 0.0 collective-permute-done.6.refs_2_
  39.3 0.5 collective-permute-done.7.refs_3_
  39.9 0.0 collective-permute-done.8.refs_4_
  39.9 3.4 %add_target.3.part_ref = f32[8,512,128]{2,1,0:T(8,128)S(1)} custom-call(s32[6,8]{1,0:T(8,128)S(1)} %get-tuple-element.41.links_ref, f32[33,8,128]{2,1,0:T(8,128)S(1)} %broadcast_in_dim.23.geo_ref.geo_in, f32[8,128]{1,0:T(8,128)S(1)} %get-tuple-element.33.refs_0_, f32[8,128]{1,0:T(8,128)S(1)} %local_sums.1.refs_1_, ...), custom_call_target="tpu_custom_call", output_to_operand_aliasing={{}: (8, {})} | custom-call | flops 29360128 | bytes 14680064 | tf_op jit(solution)/shard_map/add_target/pallas_call | solution.py:704
  43.3 1.2 %last_near.1 = (f32[8,512,128]{2,1,0:T(8,128)S(1)}, f32[8,128]{1,0:T(8,128)S(1)}) custom-call(f32[33,8,128]{2,1,0:T(8,128)S(1)} %broadcast_in_dim.23.geo_ref.geo_in, f32[12,512,128]{2,1,0:T(8,128)S(1)} %get-tuple-element.23.pairs_ref, f32[3,512,128]{2,1,0:T(8,128)S(1)} %collective-permute-done.5.halo_ref, ...), custom_call_target="tpu_custom_call", output_to_operand_aliasing={{0}: (4, {})} | custom-call | flops 12582912 | bytes 6291456 | tf_op jit(solution)/shard_map/last_near/pallas_call | solution.py:788
  44.5 3.1 %collective-permute-done.10.refs_1_ = f32[3,512,128]{2,1,0:T(8,128)S(1)} collective-permute-done((f32[3,512,128]{2,1,0:T(8,128)S(1)}, f32[3,512,128]{2,1,0:T(8,128)S(1)}, u32[]{:S(2)}, u32[]{:S(2)}) %collective-permute-start.10) | collective-permute-done | bytes 786464 | tf_op jit(solution)/shard_map/ppermute | solution.py:904
  47.6 0.0 collective-permute-done.9.refs_0_
  47.6 0.5 last_far.1
  48.1 2.3 %collective-permute-start.11 = (f32[8,128]{1,0:T(8,128)S(1)}, f32[8,128]{1,0:T(8,128)S(1)}, u32[]{:S(2)}, u32[]{:S(2)}) collective-permute-start(f32[8,128]{1,0:T(8,128)S(1)} %get-tuple-element.39), channel_id=1, source_target_pairs={{0,1},{1,0},{2,3},{3,2},{4,5},{5,4},{6,7},{7,6},{8,9},{9,8},{10,11... | collective-permute-start | bytes 12296 | tf_op jit(solution)/shard_map/ppermute | solution.py:452
  50.5 1.6 %collective-permute-done.11 = f32[8,128]{1,0:T(8,128)S(1)} collective-permute-done((f32[8,128]{1,0:T(8,128)S(1)}, f32[8,128]{1,0:T(8,128)S(1)}, u32[]{:S(2)}, u32[]{:S(2)}) %collective-permute-start.11) | collective-permute-done | bytes 4128 | tf_op jit(solution)/shard_map/ppermute | solution.py:452
  52.1 3.0 %collective-permute-start.12 = (f32[8,128]{1,0:T(8,128)S(1)}, f32[8,128]{1,0:T(8,128)S(1)}, u32[]{:S(2)}, u32[]{:S(2)}) collective-permute-start(f32[8,128]{1,0:T(8,128)S(1)} %add.7.refs_0_), channel_id=1, source_target_pairs={{0,2},{1,3},{2,0},{3,1},{4,6},{5,7},{6,4},{7,5},{8,10},{9,11},{10,... | collective-permute-start | bytes 12296 | tf_op jit(solution)/shard_map/ppermute | solution.py:453
  55.1 1.4 %result.1 = f32[4096,128]{1,0:T(8,128)} custom-call(f32[8,512,128]{2,1,0:T(8,128)S(1)} %get-tuple-element.35.part_ref, f32[3,512,128]{2,1,0:T(8,128)S(1)} %get-tuple-element.38.terms_ref), custom_call_target="tpu_custom_call" | custom-call | flops 12582912 | bytes 6291456 | tf_op jit(solution)/shard_map/result/pallas_call | solution.py:885
  56.5 0.1 collective-permute-done.12.refs_1_
  56.7 0.7 %macro.1 = f32[8,8]{1,0:T(8,128)} custom-call(f32[8,128]{1,0:T(8,128)S(1)} %add.7.refs_0_, f32[8,128]{1,0:T(8,128)S(1)} %collective-permute-done.12.refs_1_), custom_call_target="tpu_custom_call" | custom-call | tf_op jit(solution)/shard_map/macro/pallas_call | solution.py:491
  (11 shorter events, 0.0 us)
Async XLA Ops:
  0.6 6.0 %copy-start.1 = (s32[6,8]{1,0:T(8,128)S(1)}, s32[6,8]{1,0:T(8,128)}, u32[]{:S(2)}) copy-start(s32[6,8]{1,0:T(8,128)} %param.6) | copy-start | bytes 580
  0.6 6.2 %copy-start = (f32[3,6,8]{2,1,0:T(8,128)S(1)}, f32[3,6,8]{2,1,0:T(8,128)}, u32[]{:S(2)}) copy-start(f32[3,6,8]{2,1,0:T(8,128)} %param.7) | copy-start | bytes 1732
  0.7 6.3 %copy-start.2 = (f32[8]{0:T(128)S(1)}, f32[8]{0:T(128)}, u32[]{:S(2)}) copy-start(f32[8]{0:T(128)} %param.8) | copy-start | bytes 100
  0.7 6.3 %copy-start.3 = (f32[8]{0:T(128)S(1)}, f32[8]{0:T(128)}, u32[]{:S(2)}) copy-start(f32[8]{0:T(128)} %param.9) | copy-start | bytes 100
  3.1 18.7 %collective-permute-start.1 = (f32[3,512,128]{2,1,0:T(8,128)}, f32[3,512,128]{2,1,0:T(8,128)}, u32[]{:S(2)}, u32[]{:S(2)}) collective-permute-start(f32[3,512,128]{2,1,0:T(8,128)} %get-tuple-element.25), channel_id=1, source_target_pairs={{0,4},{8,12},{16,20},{24,28},{4,0},{12,8},{20,16},{28,24},{1,5},{9... | collective-permute-start | bytes 2359304 | tf_op jit(solution)/shard_map/ppermute | solution.py:904
  3.2 21.9 %collective-permute-start = (f32[3,512,128]{2,1,0:T(8,128)}, f32[3,512,128]{2,1,0:T(8,128)S(1)}, u32[]{:S(2)}, u32[]{:S(2)}) collective-permute-start(f32[3,512,128]{2,1,0:T(8,128)} %get-tuple-element.24), channel_id=1, source_target_pairs={{4,8},{12,16},{20,24},{8,4},{16,12},{24,20},{5,9},{13,17},{21,25},... | collective-permute-start | bytes 2359304 | tf_op jit(solution)/shard_map/ppermute | solution.py:904
  9.5 8.8 %collective-permute-start.2 = (f32[8,128]{1,0:T(8,128)S(1)}, f32[8,128]{1,0:T(8,128)S(1)}, u32[]{:S(2)}, u32[]{:S(2)}) collective-permute-start(f32[8,128]{1,0:T(8,128)S(1)} %get-tuple-element.26.refs_0_), channel_id=1, source_target_pairs={{0,3},{1,2},{2,1},{3,0},{4,7},{5,6},{6,5},{7,4},{8,11},{9,10},{10,... | collective-permute-start | bytes 12296 | tf_op jit(solution)/shard_map/ppermute | solution.py:444
  13.2 5.1 %collective-permute-start.3 = (f32[8,128]{1,0:T(8,128)S(1)}, f32[8,128]{1,0:T(8,128)S(1)}, u32[]{:S(2)}, u32[]{:S(2)}) collective-permute-start(f32[8,128]{1,0:T(8,128)S(1)} %get-tuple-element.26.refs_0_), channel_id=1, source_target_pairs={{0,2},{1,3},{2,0},{3,1},{4,6},{5,7},{6,4},{7,5},{8,10},{9,11},{10,... | collective-permute-start | bytes 12296 | tf_op jit(solution)/shard_map/ppermute | solution.py:444
  13.2 5.1 %collective-permute-start.4 = (f32[8,128]{1,0:T(8,128)S(1)}, f32[8,128]{1,0:T(8,128)S(1)}, u32[]{:S(2)}, u32[]{:S(2)}) collective-permute-start(f32[8,128]{1,0:T(8,128)S(1)} %get-tuple-element.26.refs_0_), channel_id=1, source_target_pairs={{0,1},{1,0},{2,3},{3,2},{4,5},{5,4},{6,7},{7,6},{8,9},{9,8},{10,11... | collective-permute-start | bytes 12296 | tf_op jit(solution)/shard_map/ppermute | solution.py:444
  23.5 8.2 %collective-permute-start.5 = (f32[3,512,128]{2,1,0:T(8,128)S(1)}, f32[3,512,128]{2,1,0:T(8,128)S(1)}, u32[]{:S(2)}, u32[]{:S(2)}) collective-permute-start(f32[3,512,128]{2,1,0:T(8,128)S(1)} %get-tuple-element.31), channel_id=1, source_target_pairs={{0,4},{8,12},{16,20},{24,28},{4,0},{12,8},{20,16},{28,24},{1,5},{9... | collective-permute-start | bytes 2359304 | tf_op jit(solution)/shard_map/ppermute | solution.py:904
  25.8 21.9 %collective-permute-start.10 = (f32[3,512,128]{2,1,0:T(8,128)S(1)}, f32[3,512,128]{2,1,0:T(8,128)S(1)}, u32[]{:S(2)}, u32[]{:S(2)}) collective-permute-start(f32[3,512,128]{2,1,0:T(8,128)S(1)} %get-tuple-element.36), channel_id=1, source_target_pairs={{4,8},{12,16},{20,24},{16,12},{24,20},{5,9},{13,17},{21,25},{17,13... | collective-permute-start | bytes 2359304 | tf_op jit(solution)/shard_map/ppermute | solution.py:904
  29.5 18.1 %collective-permute-start.9 = (f32[3,512,128]{2,1,0:T(8,128)S(1)}, f32[3,512,128]{2,1,0:T(8,128)S(1)}, u32[]{:S(2)}, u32[]{:S(2)}) collective-permute-start(f32[3,512,128]{2,1,0:T(8,128)S(1)} %get-tuple-element.36), channel_id=1, source_target_pairs={{8,4},{9,5},{10,6},{11,7}} | collective-permute-start | bytes 2359304 | tf_op jit(solution)/shard_map/ppermute | solution.py:908
  31.7 7.6 %collective-permute-start.6 = (f32[8,128]{1,0:T(8,128)S(1)}, f32[8,128]{1,0:T(8,128)S(1)}, u32[]{:S(2)}, u32[]{:S(2)}) collective-permute-start(f32[8,128]{1,0:T(8,128)S(1)} %local_sums.1.refs_1_), channel_id=1, source_target_pairs={{0,3},{1,2},{2,1},{3,0},{4,7},{5,6},{6,5},{7,4},{8,11},{9,10},{10,... | collective-permute-start | bytes 12296 | tf_op jit(solution)/shard_map/ppermute | solution.py:444
  35.4 4.5 %collective-permute-start.7 = (f32[8,128]{1,0:T(8,128)S(1)}, f32[8,128]{1,0:T(8,128)S(1)}, u32[]{:S(2)}, u32[]{:S(2)}) collective-permute-start(f32[8,128]{1,0:T(8,128)S(1)} %local_sums.1.refs_1_), channel_id=1, source_target_pairs={{0,2},{1,3},{2,0},{3,1},{4,6},{5,7},{6,4},{7,5},{8,10},{9,11},{10,... | collective-permute-start | bytes 12296 | tf_op jit(solution)/shard_map/ppermute | solution.py:444
  35.4 4.5 %collective-permute-start.8 = (f32[8,128]{1,0:T(8,128)S(1)}, f32[8,128]{1,0:T(8,128)S(1)}, u32[]{:S(2)}, u32[]{:S(2)}) collective-permute-start(f32[8,128]{1,0:T(8,128)S(1)} %local_sums.1.refs_1_), channel_id=1, source_target_pairs={{0,1},{1,0},{2,3},{3,2},{4,5},{5,4},{6,7},{7,6},{8,9},{9,8},{10,11... | collective-permute-start | bytes 12296 | tf_op jit(solution)/shard_map/ppermute | solution.py:444
  48.1 3.9 %collective-permute-start.11 = (f32[8,128]{1,0:T(8,128)S(1)}, f32[8,128]{1,0:T(8,128)S(1)}, u32[]{:S(2)}, u32[]{:S(2)}) collective-permute-start(f32[8,128]{1,0:T(8,128)S(1)} %get-tuple-element.39), channel_id=1, source_target_pairs={{0,1},{1,0},{2,3},{3,2},{4,5},{5,4},{6,7},{7,6},{8,9},{9,8},{10,11... | collective-permute-start | bytes 12296 | tf_op jit(solution)/shard_map/ppermute | solution.py:452
  52.1 4.6 %collective-permute-start.12 = (f32[8,128]{1,0:T(8,128)S(1)}, f32[8,128]{1,0:T(8,128)S(1)}, u32[]{:S(2)}, u32[]{:S(2)}) collective-permute-start(f32[8,128]{1,0:T(8,128)S(1)} %add.7.refs_0_), channel_id=1, source_target_pairs={{0,2},{1,3},{2,0},{3,1},{4,6},{5,7},{6,4},{7,5},{8,10},{9,11},{10,... | collective-permute-start | bytes 12296 | tf_op jit(solution)/shard_map/ppermute | solution.py:453

commit v18 on v13

--- a/solution.py
+++ b/solution.py
@@ -589,7 +589,7 @@
 
 
 def target_kernel(count, links_ref, geo_ref, absorbed_in, *refs):
-    sums_refs, (f_ref, part_ref, out_ref, *sum_out, ta, tiles_ref, coef, cells, faces) = refs[:count], refs[count:]
+    sums_refs, (f_ref, part_ref, out_ref, *sum_out, tiles_ref, coef, cells, faces) = refs[:count], refs[count:]
     planes = f_ref.shape[1] // CHUNKS
     sums = add_tiles(sums_refs)
     for ref in sum_out:
@@ -604,24 +604,10 @@
     coef[1] = rt
     coef[2], coef[3] = u[1], u[2]
     coef[4], coef[5] = slope * q[1], slope * q[2]
+    coef[6], coef[7], coef[8] = u[0], slope * q[0], height
     for k in range(FACES):
         wall = geo_ref[WALL + k] > 0.5
-        coef[6 + k] = column(sums, EMIT + k) / jnp.where(wall, column(absorbed, ABSORB + k), 1.0)
-    first = geo_ref[FIRST]
-
-    wt = geo_ref[WT]
-
-    def plane_table(a, _):
-        xa = first + a.astype(F32) * H
-        ca = xa - u[0]
-        za = ca * ca * rt
-        ta[0, a] = height * jnp.exp(-0.5 * za)
-        ta[1, a] = slope * q[0] * ca
-        ta[2, a] = za - 5.0
-        ta[3, a] = jnp.exp(-0.5 * xa * xa / wt)
-        return 0
-
-    lax.fori_loop(0, planes, plane_table, 0, unroll=unroll(planes, 8))
+        coef[9 + k] = column(sums, EMIT + k) / jnp.where(wall, column(absorbed, ABSORB + k), 1.0)
 
     def tile_table(g, _):
         rtg = splat(coef, 1, g)
@@ -641,15 +627,17 @@
 
     lax.fori_loop(0, SUB, tile_table, 0, unroll=4)
 
-    def at_plane(i, a, g):
-        return jnp.broadcast_to(ta[i, a, pl.ds(g, 1), :], (SUB, LANES))
-
     def cell(g, _):
-        rate_g = splat(coef, 0, g)
+        rate_g, rtg, u0, q0, height_g = [splat(coef, i, g) for i in (0, 1, 6, 7, 8)]
+        x0 = splat(geo_ref, FIRST, g) - u0
         bell, heat, zz = [[tiles_ref[i, g * TILES + t] for t in range(TILES)] for i in range(3)]
 
         def plane(a, _):
-            height_a, heat_a, z_a = [at_plane(i, a, g) for i in range(3)]
+            ca = x0 + a.astype(F32) * H
+            za = ca * ca * rtg
+            height_a = height_g * jnp.exp(-0.5 * za)
+            heat_a = q0 * ca
+            z_a = za - 5.0
             for t in range(TILES):
                 where = (g, at_rows((a * TILES + t) * SUB), slice(None))
                 f = f_ref[where]
@@ -665,7 +653,7 @@
     def wall(i, _):
         g, k = cells[i], faces[i]
         x0 = splat(geo_ref, FIRST, g)
-        ratio = splat(coef, 6 + k, g)
+        ratio = splat(coef, 9 + k, g)
         scale = -TIME_STEP / splat(geo_ref, VOL, g)
         v0, v1, v2 = [scale * x for x in face_coefficients(geo_ref, k, g)]
         base, shape = [], []
@@ -674,9 +662,12 @@
             base.append(v1 * xb + v2 * xc)
             shape.append(ratio * tiles_ref[3, g * TILES + t])
 
+        rt_wall = -0.5 / splat(geo_ref, WT, g)
+
         def plane(a, _):
-            wa = at_plane(3, a, g)
-            sa = v0 * (x0 + a.astype(F32) * H)
+            xa = x0 + a.astype(F32) * H
+            wa = jnp.exp(xa * xa * rt_wall)
+            sa = v0 * xa
             for t in range(TILES):
                 where = (g, at_rows((a * TILES + t) * SUB), slice(None))
                 f = f_ref[where]
@@ -707,9 +698,8 @@
         out_shape=[array(*part.shape)] + ([array(SUB, LANES)] if absorbed is None else []),
         input_output_aliases={len(given) - 1: 0},
         scratch_shapes=[
-                pltpu.VMEM((4, rows // CHUNKS, SUB, LANES), F32),
-            pltpu.VMEM((4, SUB * TILES, SUB, LANES), F32),
-            pltpu.VMEM((6 + FACES, SUB, LANES), F32),
+                pltpu.VMEM((4, SUB * TILES, SUB, LANES), F32),
+            pltpu.VMEM((9 + FACES, SUB, LANES), F32),
             *face_lists(),
         ],
         compiler_params=params(),
@@ -743,7 +733,7 @@
         run(not far)
 
 
-def add_side(far, pairs_ref, halo_ref, old_ref, part_ref, f_ref, rows_ref):
+def add_side(far, pairs_ref, halo_ref, old_ref, part_ref, f_ref, rows_ref, ready=None):
     def run(high):
         def group(j, _):
             at = at_rows(j * SUB)
@@ -756,19 +746,40 @@
             return 0
 
         groups = part_ref.shape[1] // SUB
-        lax.fori_loop(0, groups, group, 0, unroll=unroll(groups, 8))
+        parts = 1 if ready is None else EDGE_PARTS
+        for i in range(parts):
+            if ready is not None:
+                ready(i)
+            count = groups // parts
+            lax.fori_loop(i * count, (i + 1) * count, group, 0, unroll=unroll(count, 8))
 
     for_side(far, run)
+
+
+EDGE_PARTS = 4
+
+
+def near_edge_kernel(pairs_ref, halo_any, old_ref, part_ref, f_ref, rows_ref, halo_ref, sems):
+    size = halo_ref.shape[1] // EDGE_PARTS
+
+    def copy(i):
+        at = pl.ds(i * size, size)
+        return pltpu.make_async_copy(halo_any.at[:, at], halo_ref.at[:, at], sems.at[i])
+
+    for i in range(EDGE_PARTS):
+        copy(i).start()
+    add_side(False, pairs_ref, halo_ref, old_ref, part_ref, f_ref, rows_ref, lambda i: copy(i).wait())
 
 
 def edge(far, pairs, halo, old, part):
     rows = part.shape[1]
     return pl.pallas_call(
-        functools.partial(add_side, far),
-        in_specs=[spec(pltpu.VMEM)] * 4,
+        functools.partial(add_side, True) if far else near_edge_kernel,
+        in_specs=[spec(pltpu.VMEM), spec(pltpu.VMEM if far else pl.ANY), spec(pltpu.VMEM), spec(pltpu.VMEM)],
         out_specs=[spec(pltpu.VMEM)] * 2,
         out_shape=[array(SUB, rows, LANES), array(REACH, rows, LANES)],
         input_output_aliases={3: 0},
+        scratch_shapes=[] if far else [pltpu.VMEM(halo.shape, F32), pltpu.SemaphoreType.DMA((EDGE_PARTS,))],
         compiler_params=params(),
         cost_estimate=traffic(rows, 2),
         name="far_edge" if far else "near_edge",

time: 57.4 us -> 57.4 us (level)
  Pallas kernels: 27 us -> 26.2 us
    ppermute x4, waiting for transfers between devices: 3.86 us -> 4.56 us  [swap(): return lax.ppermute(rows, 'space', pairs + [(j, i) for i, j in pairs])]
  transfers between devices with their start and end apart: 12 -> 12, of which waited for: 5 -> 5; matrix products, arithmetic and copies ran while one was open for 1% -> 1% of each run, Pallas kernels for 41% -> 40%
where the time goes in v18:
time: 57.4 us; the launch traced here: 56.9 us
  Pallas kernels  26.2 us (46%)
  starting transfers between devices  22.4 us (39%)
  waiting for transfers between devices  6.74 us (12%)
  between operations  0.83 us (1%)
  local copies, waits for them, and re-layouts  0.69 us (1%)
    ppermute x6, starting transfers between devices, gather_sums(): lax.ppermute(tile, 'vel', [(i, i ^ s) for i in range(size)])  8.84 us
    ppermute x4, starting transfers between devices, swap(): return lax.ppermute(rows, 'space', pairs + [(j, i) for i, j in pairs])  7.72 us
    pallas_call x2, Pallas kernels, flux(): pl.pallas_call(functools.partial(flux_kernel, with_pairs), in_specs=[spec...  7.69 us
    pallas_call x2, Pallas kernels, add_target(): pl.pallas_call(kernel, in_specs=[spec(pltpu.SMEM)] + [vmem] * (len(given)...  6.66 us
    ppermute x4, waiting for transfers between devices, swap(): return lax.ppermute(rows, 'space', pairs + [(j, i) for i, j in pairs])  4.56 us
    ppermute x1, starting transfers between devices, doubling_sums(): return [pair, lax.ppermute(pair, 'vel', [(i, i ^ 2) for i in range(size)])]  3.03 us
    ppermute x1, starting transfers between devices, doubling_sums(): pair = tile + lax.ppermute(tile, 'vel', [(i, i ^ 1) for i in range(size)])  2.84 us
    pallas_call x1, Pallas kernels, first_rows(): pl.pallas_call(first_rows_kernel, in_specs=[spec(pltpu.HBM)], out_specs=[...  2.45 us
  transfers between devices with their start and end apart: 12, of which 5 were waited for; matrix products, arithmetic and copies ran while one was open for 1% of the time, Pallas kernels for 40%

profile of v18, /device:TPU:4, one launch (start us, length us, event | category | flops | bytes accessed | tf_op | source)
XLA Modules:
  0.0 56.9 jit_solution(1479502981005404658)
XLA Ops:
  0.6 0.0 copy-start.2
  0.6 0.0 copy-start.3
  0.7 2.5 %first_rows.1 = (f32[4096,128]{1,0:T(8,128)S(1)}, f32[3,512,128]{2,1,0:T(8,128)}, f32[3,512,128]{2,1,0:T(8,128)}) custom-call(f32[4096,128]{1,0:T(8,128)} %bitcast.12), custom_call_target="tpu_custom_call" | custom-call | flops 16777216 | bytes 8388608 | tf_op jit(solution)/shard_map/first_rows/pallas_call | solution.py:389
  3.1 0.1 collective-permute-start
  3.2 3.4 %collective-permute-start.5 = (f32[3,512,128]{2,1,0:T(8,128)}, f32[3,512,128]{2,1,0:T(8,128)S(1)}, u32[]{:S(2)}, u32[]{:S(2)}) collective-permute-start(f32[3,512,128]{2,1,0:T(8,128)} %get-tuple-element.27), channel_id=1, source_target_pairs={{4,8},{12,16},{20,24},{8,4},{16,12},{24,20},{5,9},{13,17},{21,25},... | collective-permute-start | bytes 2359304 | tf_op jit(solution)/shard_map/ppermute | solution.py:893
  6.7 0.1 copy.13
  6.7 0.0 copy-done.3
  6.8 0.1 copy.14
  6.8 0.1 copy.16
  6.9 0.1 copy.15
  7.0 0.1 copy.18
  7.1 0.1 concatenate.3
  7.2 0.1 copy.17
  7.3 0.1 broadcast_in_dim.23.geo_ref.geo_in
  7.4 2.0 %first_sums.1 = (f32[8,512,128]{2,1,0:T(8,128)S(1)}, f32[8,128]{1,0:T(8,128)S(1)}) custom-call(s32[6,8]{1,0:T(8,128)S(1)} %get-tuple-element.37.links_ref, f32[33,8,128]{2,1,0:T(8,128)S(1)} %broadcast_in_dim.23.geo_ref.geo_in, f32[4096,128]{1,0:T(8,128)S(1)} %get-tuple-element.19.native_ref), custom_call_target="tpu_custom_call" | custom-call | flops 20971520 | bytes 10485760 | tf_op jit(solution)/shard_map/first_sums/pallas_call | solution.py:327
  9.3 3.7 %collective-permute-start.3 = (f32[8,128]{1,0:T(8,128)S(1)}, f32[8,128]{1,0:T(8,128)S(1)}, u32[]{:S(2)}, u32[]{:S(2)}) collective-permute-start(f32[8,128]{1,0:T(8,128)S(1)} %get-tuple-element.23.refs_0_), channel_id=1, source_target_pairs={{0,3},{1,2},{2,1},{3,0},{4,7},{5,6},{6,5},{7,4},{8,11},{9,10},{10,... | collective-permute-start | bytes 12296 | tf_op jit(solution)/shard_map/ppermute | solution.py:444
  13.0 0.0 collective-permute-start.2
  13.0 0.8 %collective-permute-start.1 = (f32[8,128]{1,0:T(8,128)S(1)}, f32[8,128]{1,0:T(8,128)S(1)}, u32[]{:S(2)}, u32[]{:S(2)}) collective-permute-start(f32[8,128]{1,0:T(8,128)S(1)} %get-tuple-element.23.refs_0_), channel_id=1, source_target_pairs={{0,1},{1,0},{2,3},{3,2},{4,5},{5,4},{6,7},{7,6},{8,9},{9,8},{10,11... | collective-permute-start | bytes 12296 | tf_op jit(solution)/shard_map/ppermute | solution.py:444
  13.8 4.4 %flux.2 = (f32[8,512,128]{2,1,0:T(8,128)S(1)}, f32[12,512,128]{2,1,0:T(8,128)S(1)}) custom-call(s32[6,8]{1,0:T(8,128)S(1)} %get-tuple-element.37.links_ref, f32[33,8,128]{2,1,0:T(8,128)S(1)} %broadcast_in_dim.23.geo_ref.geo_in, f32[8,512,128]{2,1,0:T(8,128)S(1)} %get-tuple-element.20.f_ref.refs_4_.old_ref), custom_call_target="tpu_custom_call" | custom-call | flops 37748736 | bytes 18874368 | tf_op jit(solution)/shard_map/flux/pallas_call | solution.py:572
  18.2 0.0 collective-permute-done.3.refs_3_
  18.2 0.0 collective-permute-done.2.refs_2_
  18.2 0.0 collective-permute-done.1.refs_1_
  18.2 3.3 %add_target.2 = (f32[8,512,128]{2,1,0:T(8,128)S(1)}, f32[8,128]{1,0:T(8,128)S(1)}) custom-call(s32[6,8]{1,0:T(8,128)S(1)} %get-tuple-element.37.links_ref, f32[33,8,128]{2,1,0:T(8,128)S(1)} %broadcast_in_dim.23.geo_ref.geo_in, f32[8,128]{1,0:T(8,128)S(1)} %get-tuple-element.23.refs_0_, ...), custom_call_target="tpu_custom_call", output_to_operand_aliasing={{0}: (7, {})} | custom-call | flops 29360128 | bytes 14680064 | tf_op jit(solution)/shard_map/add_target/pallas_call | solution.py:694
  21.6 0.0 collective-permute-done.halo_any
  21.6 1.6 %near_edge.1 = (f32[8,512,128]{2,1,0:T(8,128)S(1)}, f32[3,512,128]{2,1,0:T(8,128)S(1)}) custom-call(f32[12,512,128]{2,1,0:T(8,128)S(1)} %get-tuple-element.21.pairs_ref, f32[3,512,128]{2,1,0:T(8,128)} %collective-permute-done.halo_any, f32[8,512,128]{2,1,0:T(8,128)S(1)} %get-tuple-element.20.f_ref.refs_4_.old_ref, ...), custom_call_target="tpu_custom_call", output_to_operand_aliasing={{0}: (3, {})} | custom-call | flops 8388608 | bytes 4194304 | tf_op jit(solution)/shard_map/near_edge/pallas_call | solution.py:776
  23.2 0.5 collective-permute-start.4
  23.7 1.5 %collective-permute-done.5.halo_ref = f32[3,512,128]{2,1,0:T(8,128)S(1)} collective-permute-done((f32[3,512,128]{2,1,0:T(8,128)}, f32[3,512,128]{2,1,0:T(8,128)S(1)}, u32[]{:S(2)}, u32[]{:S(2)}) %collective-permute-start.5) | collective-permute-done | bytes 786464 | tf_op jit(solution)/shard_map/ppermute | solution.py:893
  25.2 0.6 %far_edge.1 = (f32[8,512,128]{2,1,0:T(8,128)S(1)}, f32[3,512,128]{2,1,0:T(8,128)S(1)}) custom-call(f32[12,512,128]{2,1,0:T(8,128)S(1)} %get-tuple-element.21.pairs_ref, f32[3,512,128]{2,1,0:T(8,128)S(1)} %collective-permute-done.5.halo_ref, f32[8,512,128]{2,1,0:T(8,128)S(1)} %get-tuple-element.20.f_ref.refs_4_.old_ref, ...), custom_call_target="tpu_custom_call", output_to_operand_aliasing={{0}: (3, {})} | custom-call | flops 8388608 | bytes 4194304 | tf_op jit(solution)/shard_map/far_edge/pallas_call | solution.py:776
  25.8 3.7 %collective-permute-start.9 = (f32[3,512,128]{2,1,0:T(8,128)S(1)}, f32[3,512,128]{2,1,0:T(8,128)S(1)}, u32[]{:S(2)}, u32[]{:S(2)}) collective-permute-start(f32[3,512,128]{2,1,0:T(8,128)S(1)} %get-tuple-element.32), channel_id=1, source_target_pairs={{4,8},{12,16},{20,24},{8,4},{16,12},{24,20},{5,9},{13,17},{21,25},... | collective-permute-start | bytes 2359304 | tf_op jit(solution)/shard_map/ppermute | solution.py:893
  29.5 1.4 %local_sums.1.refs_1_ = f32[8,128]{1,0:T(8,128)S(1)} custom-call(s32[6,8]{1,0:T(8,128)S(1)} %get-tuple-element.37.links_ref, f32[33,8,128]{2,1,0:T(8,128)S(1)} %broadcast_in_dim.23.geo_ref.geo_in, f32[8,512,128]{2,1,0:T(8,128)S(1)} %get-tuple-element.29.f_ref.refs_5_.old_ref), custom_call_target="tpu_custom_call" | custom-call | flops 16777216 | bytes 8388608 | tf_op jit(solution)/shard_map/local_sums/pallas_call | solution.py:309
  30.9 3.6 %collective-permute-start.8 = (f32[8,128]{1,0:T(8,128)S(1)}, f32[8,128]{1,0:T(8,128)S(1)}, u32[]{:S(2)}, u32[]{:S(2)}) collective-permute-start(f32[8,128]{1,0:T(8,128)S(1)} %local_sums.1.refs_1_), channel_id=1, source_target_pairs={{0,3},{1,2},{2,1},{3,0},{4,7},{5,6},{6,5},{7,4},{8,11},{9,10},{10,... | collective-permute-start | bytes 12296 | tf_op jit(solution)/shard_map/ppermute | solution.py:444
  34.5 0.0 collective-permute-start.7
  34.5 0.8 %collective-permute-start.6 = (f32[8,128]{1,0:T(8,128)S(1)}, f32[8,128]{1,0:T(8,128)S(1)}, u32[]{:S(2)}, u32[]{:S(2)}) collective-permute-start(f32[8,128]{1,0:T(8,128)S(1)} %local_sums.1.refs_1_), channel_id=1, source_target_pairs={{0,1},{1,0},{2,3},{3,2},{4,5},{5,4},{6,7},{7,6},{8,9},{9,8},{10,11... | collective-permute-start | bytes 12296 | tf_op jit(solution)/shard_map/ppermute | solution.py:444
  35.3 3.3 %flux.3.refs_6_ = f32[8,512,128]{2,1,0:T(8,128)S(1)} custom-call(s32[6,8]{1,0:T(8,128)S(1)} %get-tuple-element.37.links_ref, f32[33,8,128]{2,1,0:T(8,128)S(1)} %broadcast_in_dim.23.geo_ref.geo_in, f32[8,512,128]{2,1,0:T(8,128)S(1)} %get-tuple-element.29.f_ref.refs_5_.old_ref), custom_call_target="tpu_custom_call" | custom-call | flops 29360128 | bytes 14680064 | tf_op jit(solution)/shard_map/flux/pallas_call | solution.py:572
  38.6 0.0 collective-permute-done.8.refs_4_
  38.6 0.4 collective-permute-done.7.refs_3_
  39.0 0.0 collective-permute-done.6.refs_2_
  39.0 3.3 %add_target.3.part_ref = f32[8,512,128]{2,1,0:T(8,128)S(1)} custom-call(s32[6,8]{1,0:T(8,128)S(1)} %get-tuple-element.37.links_ref, f32[33,8,128]{2,1,0:T(8,128)S(1)} %broadcast_in_dim.23.geo_ref.geo_in, f32[8,128]{1,0:T(8,128)S(1)} %get-tuple-element.30.refs_0_, f32[8,128]{1,0:T(8,128)S(1)} %local_sums.1.refs_1_, ...), custom_call_target="tpu_custom_call", output_to_operand_aliasing={{}: (8, {})} | custom-call | flops 29360128 | bytes 14680064 | tf_op jit(solution)/shard_map/add_target/pallas_call | solution.py:694
  42.4 0.0 collective-permute-done.4.halo_ref
  42.4 1.2 %last_near.1 = (f32[8,512,128]{2,1,0:T(8,128)S(1)}, f32[8,128]{1,0:T(8,128)S(1)}) custom-call(f32[33,8,128]{2,1,0:T(8,128)S(1)} %broadcast_in_dim.23.geo_ref.geo_in, f32[12,512,128]{2,1,0:T(8,128)S(1)} %get-tuple-element.21.pairs_ref, f32[3,512,128]{2,1,0:T(8,128)S(1)} %collective-permute-done.4.halo_ref, ...), custom_call_target="tpu_custom_call", output_to_operand_aliasing={{0}: (4, {})} | custom-call | flops 12582912 | bytes 6291456 | tf_op jit(solution)/shard_map/last_near/pallas_call | solution.py:798
  43.6 3.1 %collective-permute-done.9.halo_ref = f32[3,512,128]{2,1,0:T(8,128)S(1)} collective-permute-done((f32[3,512,128]{2,1,0:T(8,128)S(1)}, f32[3,512,128]{2,1,0:T(8,128)S(1)}, u32[]{:S(2)}, u32[]{:S(2)}) %collective-permute-start.9) | collective-permute-done | bytes 786464 | tf_op jit(solution)/shard_map/ppermute | solution.py:893
  46.6 0.5 last_far.1
  47.1 2.8 %collective-permute-start.10 = (f32[8,128]{1,0:T(8,128)S(1)}, f32[8,128]{1,0:T(8,128)S(1)}, u32[]{:S(2)}, u32[]{:S(2)}) collective-permute-start(f32[8,128]{1,0:T(8,128)S(1)} %get-tuple-element.35), channel_id=1, source_target_pairs={{0,1},{1,0},{2,3},{3,2},{4,5},{5,4},{6,7},{7,6},{8,9},{9,8},{10,11... | collective-permute-start | bytes 12296 | tf_op jit(solution)/shard_map/ppermute | solution.py:452
  50.0 1.6 %collective-permute-done.10 = f32[8,128]{1,0:T(8,128)S(1)} collective-permute-done((f32[8,128]{1,0:T(8,128)S(1)}, f32[8,128]{1,0:T(8,128)S(1)}, u32[]{:S(2)}, u32[]{:S(2)}) %collective-permute-start.10) | collective-permute-done | bytes 4128 | tf_op jit(solution)/shard_map/ppermute | solution.py:452
  51.5 3.0 %collective-permute-start.11 = (f32[8,128]{1,0:T(8,128)S(1)}, f32[8,128]{1,0:T(8,128)S(1)}, u32[]{:S(2)}, u32[]{:S(2)}) collective-permute-start(f32[8,128]{1,0:T(8,128)S(1)} %add.7.refs_0_), channel_id=1, source_target_pairs={{0,2},{1,3},{2,0},{3,1},{4,6},{5,7},{6,4},{7,5},{8,10},{9,11},{10,... | collective-permute-start | bytes 12296 | tf_op jit(solution)/shard_map/ppermute | solution.py:453
  54.6 1.4 %result.1 = f32[4096,128]{1,0:T(8,128)} custom-call(f32[8,512,128]{2,1,0:T(8,128)S(1)} %get-tuple-element.31.part_ref, f32[3,512,128]{2,1,0:T(8,128)S(1)} %get-tuple-element.34.terms_ref), custom_call_target="tpu_custom_call" | custom-call | flops 12582912 | bytes 6291456 | tf_op jit(solution)/shard_map/result/pallas_call | solution.py:879
  56.0 0.1 collective-permute-done.11.refs_1_
  56.2 0.7 %macro.1 = f32[8,8]{1,0:T(8,128)} custom-call(f32[8,128]{1,0:T(8,128)S(1)} %add.7.refs_0_, f32[8,128]{1,0:T(8,128)S(1)} %collective-permute-done.11.refs_1_), custom_call_target="tpu_custom_call" | custom-call | tf_op jit(solution)/shard_map/macro/pallas_call | solution.py:490
  (9 shorter events, 0.0 us)
Async XLA Ops:
  0.6 6.0 %copy-start.2 = (f32[8]{0:T(128)S(1)}, f32[8]{0:T(128)}, u32[]{:S(2)}) copy-start(f32[8]{0:T(128)} %param.8) | copy-start | bytes 100
  0.6 6.1 %copy-start.3 = (f32[8]{0:T(128)S(1)}, f32[8]{0:T(128)}, u32[]{:S(2)}) copy-start(f32[8]{0:T(128)} %param.9) | copy-start | bytes 100
  0.7 6.2 %copy-start.1 = (s32[6,8]{1,0:T(8,128)S(1)}, s32[6,8]{1,0:T(8,128)}, u32[]{:S(2)}) copy-start(s32[6,8]{1,0:T(8,128)} %param.6) | copy-start | bytes 580
  0.7 6.3 %copy-start = (f32[3,6,8]{2,1,0:T(8,128)S(1)}, f32[3,6,8]{2,1,0:T(8,128)}, u32[]{:S(2)}) copy-start(f32[3,6,8]{2,1,0:T(8,128)} %param.7) | copy-start | bytes 1732
  3.1 18.4 %collective-permute-start = (f32[3,512,128]{2,1,0:T(8,128)}, f32[3,512,128]{2,1,0:T(8,128)}, u32[]{:S(2)}, u32[]{:S(2)}) collective-permute-start(f32[3,512,128]{2,1,0:T(8,128)} %get-tuple-element.22), channel_id=1, source_target_pairs={{0,4},{8,12},{16,20},{24,28},{4,0},{12,8},{20,16},{28,24},{1,5},{9... | collective-permute-start | bytes 2359304 | tf_op jit(solution)/shard_map/ppermute | solution.py:893
  3.2 21.9 %collective-permute-start.5 = (f32[3,512,128]{2,1,0:T(8,128)}, f32[3,512,128]{2,1,0:T(8,128)S(1)}, u32[]{:S(2)}, u32[]{:S(2)}) collective-permute-start(f32[3,512,128]{2,1,0:T(8,128)} %get-tuple-element.27), channel_id=1, source_target_pairs={{4,8},{12,16},{20,24},{8,4},{16,12},{24,20},{5,9},{13,17},{21,25},... | collective-permute-start | bytes 2359304 | tf_op jit(solution)/shard_map/ppermute | solution.py:893
  9.3 8.9 %collective-permute-start.3 = (f32[8,128]{1,0:T(8,128)S(1)}, f32[8,128]{1,0:T(8,128)S(1)}, u32[]{:S(2)}, u32[]{:S(2)}) collective-permute-start(f32[8,128]{1,0:T(8,128)S(1)} %get-tuple-element.23.refs_0_), channel_id=1, source_target_pairs={{0,3},{1,2},{2,1},{3,0},{4,7},{5,6},{6,5},{7,4},{8,11},{9,10},{10,... | collective-permute-start | bytes 12296 | tf_op jit(solution)/shard_map/ppermute | solution.py:444
  13.0 5.2 %collective-permute-start.2 = (f32[8,128]{1,0:T(8,128)S(1)}, f32[8,128]{1,0:T(8,128)S(1)}, u32[]{:S(2)}, u32[]{:S(2)}) collective-permute-start(f32[8,128]{1,0:T(8,128)S(1)} %get-tuple-element.23.refs_0_), channel_id=1, source_target_pairs={{0,2},{1,3},{2,0},{3,1},{4,6},{5,7},{6,4},{7,5},{8,10},{9,11},{10,... | collective-permute-start | bytes 12296 | tf_op jit(solution)/shard_map/ppermute | solution.py:444
  13.0 5.2 %collective-permute-start.1 = (f32[8,128]{1,0:T(8,128)S(1)}, f32[8,128]{1,0:T(8,128)S(1)}, u32[]{:S(2)}, u32[]{:S(2)}) collective-permute-start(f32[8,128]{1,0:T(8,128)S(1)} %get-tuple-element.23.refs_0_), channel_id=1, source_target_pairs={{0,1},{1,0},{2,3},{3,2},{4,5},{5,4},{6,7},{7,6},{8,9},{9,8},{10,11... | collective-permute-start | bytes 12296 | tf_op jit(solution)/shard_map/ppermute | solution.py:444
  23.2 19.2 %collective-permute-start.4 = (f32[3,512,128]{2,1,0:T(8,128)S(1)}, f32[3,512,128]{2,1,0:T(8,128)S(1)}, u32[]{:S(2)}, u32[]{:S(2)}) collective-permute-start(f32[3,512,128]{2,1,0:T(8,128)S(1)} %get-tuple-element.26), channel_id=1, source_target_pairs={{0,4},{8,12},{16,20},{24,28},{4,0},{12,8},{20,16},{28,24},{1,5},{9... | collective-permute-start | bytes 2359304 | tf_op jit(solution)/shard_map/ppermute | solution.py:893
  25.8 20.8 %collective-permute-start.9 = (f32[3,512,128]{2,1,0:T(8,128)S(1)}, f32[3,512,128]{2,1,0:T(8,128)S(1)}, u32[]{:S(2)}, u32[]{:S(2)}) collective-permute-start(f32[3,512,128]{2,1,0:T(8,128)S(1)} %get-tuple-element.32), channel_id=1, source_target_pairs={{4,8},{12,16},{20,24},{8,4},{16,12},{24,20},{5,9},{13,17},{21,25},... | collective-permute-start | bytes 2359304 | tf_op jit(solution)/shard_map/ppermute | solution.py:893
  30.9 7.7 %collective-permute-start.8 = (f32[8,128]{1,0:T(8,128)S(1)}, f32[8,128]{1,0:T(8,128)S(1)}, u32[]{:S(2)}, u32[]{:S(2)}) collective-permute-start(f32[8,128]{1,0:T(8,128)S(1)} %local_sums.1.refs_1_), channel_id=1, source_target_pairs={{0,3},{1,2},{2,1},{3,0},{4,7},{5,6},{6,5},{7,4},{8,11},{9,10},{10,... | collective-permute-start | bytes 12296 | tf_op jit(solution)/shard_map/ppermute | solution.py:444
  34.5 4.5 %collective-permute-start.7 = (f32[8,128]{1,0:T(8,128)S(1)}, f32[8,128]{1,0:T(8,128)S(1)}, u32[]{:S(2)}, u32[]{:S(2)}) collective-permute-start(f32[8,128]{1,0:T(8,128)S(1)} %local_sums.1.refs_1_), channel_id=1, source_target_pairs={{0,2},{1,3},{2,0},{3,1},{4,6},{5,7},{6,4},{7,5},{8,10},{9,11},{10,... | collective-permute-start | bytes 12296 | tf_op jit(solution)/shard_map/ppermute | solution.py:444
  34.5 4.5 %collective-permute-start.6 = (f32[8,128]{1,0:T(8,128)S(1)}, f32[8,128]{1,0:T(8,128)S(1)}, u32[]{:S(2)}, u32[]{:S(2)}) collective-permute-start(f32[8,128]{1,0:T(8,128)S(1)} %local_sums.1.refs_1_), channel_id=1, source_target_pairs={{0,1},{1,0},{2,3},{3,2},{4,5},{5,4},{6,7},{7,6},{8,9},{9,8},{10,11... | collective-permute-start | bytes 12296 | tf_op jit(solution)/shard_map/ppermute | solution.py:444
  47.1 4.4 %collective-permute-start.10 = (f32[8,128]{1,0:T(8,128)S(1)}, f32[8,128]{1,0:T(8,128)S(1)}, u32[]{:S(2)}, u32[]{:S(2)}) collective-permute-start(f32[8,128]{1,0:T(8,128)S(1)} %get-tuple-element.35), channel_id=1, source_target_pairs={{0,1},{1,0},{2,3},{3,2},{4,5},{5,4},{6,7},{7,6},{8,9},{9,8},{10,11... | collective-permute-start | bytes 12296 | tf_op jit(solution)/shard_map/ppermute | solution.py:452
  51.5 4.6 %collective-permute-start.11 = (f32[8,128]{1,0:T(8,128)S(1)}, f32[8,128]{1,0:T(8,128)S(1)}, u32[]{:S(2)}, u32[]{:S(2)}) collective-permute-start(f32[8,128]{1,0:T(8,128)S(1)} %add.7.refs_0_), channel_id=1, source_target_pairs={{0,2},{1,3},{2,0},{3,1},{4,6},{5,7},{6,4},{7,5},{8,10},{9,11},{10,... | collective-permute-start | bytes 12296 | tf_op jit(solution)/shard_map/ppermute | solution.py:453

commit v19 on v18

--- a/solution.py
+++ b/solution.py
@@ -771,19 +771,37 @@
     add_side(False, pairs_ref, halo_ref, old_ref, part_ref, f_ref, rows_ref, lambda i: copy(i).wait())
 
 
-def edge(far, pairs, halo, old, part):
+def far_edge_kernel(count, pairs_ref, *refs):
+    halos, rest = refs[:count], refs[count:]
+    if count == 1:
+        add_side(True, pairs_ref, halos[0], *rest)
+        return
+    me = lax.axis_index("space")
+    late = me < 0
+    for _, last in LATE_FLOWS:
+        late = jnp.logical_or(late, me == last)
+    for halo_ref, wanted in ((halos[0], late), (halos[1], jnp.logical_not(late))):
+
+        @pl.when(wanted)
+        def _():
+            add_side(True, pairs_ref, halo_ref, *rest)
+
+
+def edge(far, pairs, halos, old, part):
     rows = part.shape[1]
     return pl.pallas_call(
-        functools.partial(add_side, True) if far else near_edge_kernel,
-        in_specs=[spec(pltpu.VMEM), spec(pltpu.VMEM if far else pl.ANY), spec(pltpu.VMEM), spec(pltpu.VMEM)],
+        functools.partial(far_edge_kernel, len(halos)) if far else near_edge_kernel,
+        in_specs=[spec(pltpu.VMEM)]
+        + [spec(pltpu.VMEM if far else pl.ANY)] * len(halos)
+        + [spec(pltpu.VMEM), spec(pltpu.VMEM)],
         out_specs=[spec(pltpu.VMEM)] * 2,
         out_shape=[array(SUB, rows, LANES), array(REACH, rows, LANES)],
-        input_output_aliases={3: 0},
-        scratch_shapes=[] if far else [pltpu.VMEM(halo.shape, F32), pltpu.SemaphoreType.DMA((EDGE_PARTS,))],
+        input_output_aliases={len(halos) + 2: 0},
+        scratch_shapes=[] if far else [pltpu.VMEM(halos[0].shape, F32), pltpu.SemaphoreType.DMA((EDGE_PARTS,))],
         compiler_params=params(),
         cost_estimate=traffic(rows, 2),
         name="far_edge" if far else "near_edge",
-    )(pairs, halo, old, part)
+    )(pairs, *halos, old, part)
 
 
 def last_near_kernel(geo_ref, pairs_ref, halo_ref, old_ref, part_ref, f_ref, sums_out, parts_ref):
@@ -888,9 +906,20 @@
     )(part, terms)
 
 
-def swap(rows, start):
+LATE_SLABS = 8
+LATE_FLOWS = ((2, 1), (5, 6))
+
+
+def swap(rows, start, without=()):
     pairs = [(i, i + 1) for i in range(start, lax.axis_size("space") - 1, 2)]
-    return lax.ppermute(rows, "space", pairs + [(j, i) for i, j in pairs])
+    pairs = pairs + [(j, i) for i, j in pairs]
+    return lax.ppermute(rows, "space", [p for p in pairs if p not in without])
+
+
+def swap_far(rows):
+    if lax.axis_size("space") != LATE_SLABS:
+        return [swap(rows, 1)]
+    return [lax.ppermute(rows, "space", LATE_FLOWS), swap(rows, 1, LATE_FLOWS)]
 
 
 def per_device(particle_profile, neighbors, face_vectors, volumes, wall_temp):
@@ -914,12 +943,13 @@
     )
     geo = jnp.broadcast_to(geo[:, :, None], (GEO, cells, LANES))
     native, far, near = first_rows(native)
-    far, near = swap(far, 1), swap(near, 0)
+    far, near = swap_far(far), swap(near, 0)
     f, sums = first_sums(links, geo, native)
+    sums, near = lax.optimization_barrier((sums, near))
     tiles = gather_sums(sums)
     part, pairs = flux(True, links, geo, f)
     part, absorbed = add_target(links, geo, None, tiles, f, part)
-    part, near = edge(False, pairs, near, f, part)
+    part, near = edge(False, pairs, [near], f, part)
     near = swap(near, 0)
     f, far = edge(True, pairs, far, f, part)
     far = swap(far, 1)

time: 57.4 us -> 59.9 us (1.044)
  Pallas kernels: 26.2 us -> 28.8 us
  waiting for transfers between devices: 6.74 us -> 7.47 us
    ppermute x4 -> x5, starting transfers between devices: 7.72 us -> 9.56 us  [the longest x4 8 us: swap(): return lax.ppermute(rows, 'space', [p for p in pairs if p not in without])]
    ppermute x1, starting transfers between devices: 2.84 us -> 1.3 us  [doubling_sums(): pair = tile + lax.ppermute(tile, 'vel', [(i, i ^ 1) for i in range(size)])]
    ppermute x4 -> x5, waiting for transfers between devices: 4.56 us -> 3.35 us  [the longest x4 3.35 us: swap(): return lax.ppermute(rows, 'space', [p for p in pairs if p not in without])]
    pallas_call x2, Pallas kernels: 6.66 us -> 7.8 us  [add_target(): pl.pallas_call(kernel, in_specs=[spec(pltpu.SMEM)] + [vmem] * (len(given)...]
    pallas_call x2, Pallas kernels: 2.2 us -> 3.33 us  [edge(): pl.pallas_call(functools.partial(far_edge_kernel, len(halos)) if far else...]
    ppermute x1, starting transfers between devices: 3.03 us -> 2.14 us  [doubling_sums(): return [pair, lax.ppermute(pair, 'vel', [(i, i ^ 2) for i in range(size)])]]
    ppermute x1, waiting for transfers between devices: 1.59 us -> 2.36 us  [doubling_sums(): pair = tile + lax.ppermute(tile, 'vel', [(i, i ^ 1) for i in range(size)])]
    ppermute x1, waiting for transfers between devices: 0.13 us -> 0.91 us  [doubling_sums(): return [pair, lax.ppermute(pair, 'vel', [(i, i ^ 2) for i in range(size)])]]
  transfers between devices with their start and end apart: 12 -> 13, of which waited for: 5 -> 4; matrix products, arithmetic and copies ran while one was open for 1% -> 1% of each run, Pallas kernels for 40% -> 42%
where the time goes in v19:
time: 59.9 us; the launch traced here: 59.6 us
  Pallas kernels  28.8 us (48%)
  starting transfers between devices  21.9 us (37%)
  waiting for transfers between devices  7.47 us (12%)
  between operations  0.8 us (1%)
  local copies, waits for them, and re-layouts  0.69 us (1%)
    ppermute x6, starting transfers between devices, gather_sums(): lax.ppermute(tile, 'vel', [(i, i ^ s) for i in range(size)])  8.85 us
    ppermute x4, starting transfers between devices, swap(): return lax.ppermute(rows, 'space', [p for p in pairs if p not in without])  8 us
    pallas_call x2, Pallas kernels, add_target(): pl.pallas_call(kernel, in_specs=[spec(pltpu.SMEM)] + [vmem] * (len(given)...  7.8 us
    pallas_call x2, Pallas kernels, flux(): pl.pallas_call(functools.partial(flux_kernel, with_pairs), in_specs=[spec...  6.98 us
    ppermute x4, waiting for transfers between devices, swap(): return lax.ppermute(rows, 'space', [p for p in pairs if p not in without])  3.35 us
    pallas_call x2, Pallas kernels, edge(): pl.pallas_call(functools.partial(far_edge_kernel, len(halos)) if far else...  3.33 us
    pallas_call x1, Pallas kernels, first_sums(): pl.pallas_call(first_sums_kernel, in_specs=[spec(pltpu.SMEM), spec(pltpu....  2.72 us
    pallas_call x1, Pallas kernels, first_rows(): pl.pallas_call(first_rows_kernel, in_specs=[spec(pltpu.HBM)], out_specs=[...  2.44 us
  transfers between devices with their start and end apart: 13, of which 4 were waited for; matrix products, arithmetic and copies ran while one was open for 1% of the time, Pallas kernels for 42%

profile of v19, /device:TPU:4, one launch (start us, length us, event | category | flops | bytes accessed | tf_op | source)
XLA Modules:
  0.0 59.6 jit_solution(15230262001035977455)
XLA Ops:
  0.7 2.4 %first_rows.1 = (f32[4096,128]{1,0:T(8,128)S(1)}, f32[3,512,128]{2,1,0:T(8,128)}, f32[3,512,128]{2,1,0:T(8,128)}) custom-call(f32[4096,128]{1,0:T(8,128)} %bitcast.12), custom_call_target="tpu_custom_call" | custom-call | flops 16777216 | bytes 8388608 | tf_op jit(solution)/shard_map/first_rows/pallas_call | solution.py:389
  3.1 0.1 collective-permute-start
  3.2 3.4 %collective-permute-start.6 = (f32[3,512,128]{2,1,0:T(8,128)}, f32[3,512,128]{2,1,0:T(8,128)S(1)}, u32[]{:S(2)}, u32[]{:S(2)}) collective-permute-start(f32[3,512,128]{2,1,0:T(8,128)} %get-tuple-element.31), channel_id=1, source_target_pairs={{4,8},{12,16},{16,12},{24,20},{5,9},{13,17},{17,13},{25,21},{6,10}... | collective-permute-start | bytes 2359304 | tf_op jit(solution)/shard_map/ppermute | solution.py:916
  6.6 1.6 %collective-permute-start.5 = (f32[3,512,128]{2,1,0:T(8,128)}, f32[3,512,128]{2,1,0:T(8,128)}, u32[]{:S(2)}, u32[]{:S(2)}) collective-permute-start(f32[3,512,128]{2,1,0:T(8,128)} %get-tuple-element.31), channel_id=1, source_target_pairs={{8,4},{20,24},{9,5},{21,25},{10,6},{22,26},{11,7},{23,27}} | collective-permute-start | bytes 2359304 | tf_op jit(solution)/shard_map/ppermute | solution.py:922
  8.2 0.1 copy.13
  8.3 0.0 copy-done.3
  8.3 0.1 copy.14
  8.4 0.1 copy.16
  8.4 0.1 copy.15
  8.5 0.1 copy.18
  8.6 0.1 concatenate.3
  8.7 0.1 copy.17
  8.8 0.1 broadcast_in_dim.23.geo_ref.geo_in
  8.9 2.7 %first_sums.1 = (f32[8,512,128]{2,1,0:T(8,128)S(1)}, f32[8,128]{1,0:T(8,128)S(1)}) custom-call(s32[6,8]{1,0:T(8,128)S(1)} %get-tuple-element.41.links_ref, f32[33,8,128]{2,1,0:T(8,128)S(1)} %broadcast_in_dim.23.geo_ref.geo_in, f32[4096,128]{1,0:T(8,128)S(1)} %get-tuple-element.21.native_ref), custom_call_target="tpu_custom_call" | custom-call | flops 20971520 | bytes 10485760 | tf_op jit(solution)/shard_map/first_sums/pallas_call | solution.py:327
  11.6 0.0 collective-permute-done.halo_any
  11.6 3.7 %collective-permute-start.3 = (f32[8,128]{1,0:T(8,128)S(1)}, f32[8,128]{1,0:T(8,128)S(1)}, u32[]{:S(2)}, u32[]{:S(2)}) collective-permute-start(f32[8,128]{1,0:T(8,128)S(1)} %get-tuple-element.27.refs_0_), channel_id=1, source_target_pairs={{0,3},{1,2},{2,1},{3,0},{4,7},{5,6},{6,5},{7,4},{8,11},{9,10},{10,... | collective-permute-start | bytes 12296 | tf_op jit(solution)/shard_map/ppermute | solution.py:444
  15.3 0.0 collective-permute-start.2
  15.3 0.8 %collective-permute-start.1 = (f32[8,128]{1,0:T(8,128)S(1)}, f32[8,128]{1,0:T(8,128)S(1)}, u32[]{:S(2)}, u32[]{:S(2)}) collective-permute-start(f32[8,128]{1,0:T(8,128)S(1)} %get-tuple-element.27.refs_0_), channel_id=1, source_target_pairs={{0,1},{1,0},{2,3},{3,2},{4,5},{5,4},{6,7},{7,6},{8,9},{9,8},{10,11... | collective-permute-start | bytes 12296 | tf_op jit(solution)/shard_map/ppermute | solution.py:444
  16.1 4.1 %flux.2 = (f32[8,512,128]{2,1,0:T(8,128)S(1)}, f32[12,512,128]{2,1,0:T(8,128)S(1)}) custom-call(s32[6,8]{1,0:T(8,128)S(1)} %get-tuple-element.41.links_ref, f32[33,8,128]{2,1,0:T(8,128)S(1)} %broadcast_in_dim.23.geo_ref.geo_in, f32[8,512,128]{2,1,0:T(8,128)S(1)} %get-tuple-element.22.f_ref.refs_4_.old_ref.refs_2_), custom_call_target="tpu_custom_call" | custom-call | flops 37748736 | bytes 18874368 | tf_op jit(solution)/shard_map/flux/pallas_call | solution.py:572
  20.2 0.0 collective-permute-done.3.refs_3_
  20.2 0.0 collective-permute-done.2.refs_2_
  20.2 0.0 collective-permute-done.1.refs_1_
  20.2 3.9 %add_target.2 = (f32[8,512,128]{2,1,0:T(8,128)S(1)}, f32[8,128]{1,0:T(8,128)S(1)}) custom-call(s32[6,8]{1,0:T(8,128)S(1)} %get-tuple-element.41.links_ref, f32[33,8,128]{2,1,0:T(8,128)S(1)} %broadcast_in_dim.23.geo_ref.geo_in, f32[8,128]{1,0:T(8,128)S(1)} %get-tuple-element.27.refs_0_, ...), custom_call_target="tpu_custom_call", output_to_operand_aliasing={{0}: (7, {})} | custom-call | flops 29360128 | bytes 14680064 | tf_op jit(solution)/shard_map/add_target/pallas_call | solution.py:694
  24.1 1.6 %near_edge.1 = (f32[8,512,128]{2,1,0:T(8,128)S(1)}, f32[3,512,128]{2,1,0:T(8,128)S(1)}) custom-call(f32[12,512,128]{2,1,0:T(8,128)S(1)} %get-tuple-element.23.pairs_ref, f32[3,512,128]{2,1,0:T(8,128)} %collective-permute-done.halo_any, f32[8,512,128]{2,1,0:T(8,128)S(1)} %get-tuple-element.22.f_ref.refs_4_.old_ref.refs_2_, ...), custom_call_target="tpu_custom_call", output_to_operand_aliasing={{0}: (3, {})} | custom-call | flops 8388608 | bytes 4194304 | tf_op jit(solution)/shard_map/near_edge/pallas_call | solution.py:792
  25.7 0.9 %collective-permute-start.4 = (f32[3,512,128]{2,1,0:T(8,128)S(1)}, f32[3,512,128]{2,1,0:T(8,128)S(1)}, u32[]{:S(2)}, u32[]{:S(2)}) collective-permute-start(f32[3,512,128]{2,1,0:T(8,128)S(1)} %get-tuple-element.30), channel_id=1, source_target_pairs={{0,4},{8,12},{16,20},{24,28},{4,0},{12,8},{20,16},{28,24},{1,5},{9... | collective-permute-start | bytes 2359304 | tf_op jit(solution)/shard_map/ppermute | solution.py:916
  26.6 0.0 collective-permute-done.6.refs_1_
  26.6 0.0 collective-permute-done.5.refs_0_
  26.7 1.8 %far_edge.1 = (f32[8,512,128]{2,1,0:T(8,128)S(1)}, f32[3,512,128]{2,1,0:T(8,128)S(1)}) custom-call(f32[12,512,128]{2,1,0:T(8,128)S(1)} %get-tuple-element.23.pairs_ref, f32[3,512,128]{2,1,0:T(8,128)} %collective-permute-done.5.refs_0_, f32[3,512,128]{2,1,0:T(8,128)S(1)} %collective-permute-done.6.refs_1_, ...), custom_call_target="tpu_custom_call", output_to_operand_aliasing={{0}: (4, {})} | custom-call | flops 8388608 | bytes 4194304 | tf_op jit(solution)/shard_map/far_edge/pallas_call | solution.py:792
  28.4 3.6 %collective-permute-start.10 = (f32[3,512,128]{2,1,0:T(8,128)S(1)}, f32[3,512,128]{2,1,0:T(8,128)S(1)}, u32[]{:S(2)}, u32[]{:S(2)}) collective-permute-start(f32[3,512,128]{2,1,0:T(8,128)S(1)} %get-tuple-element.36), channel_id=1, source_target_pairs={{4,8},{12,16},{20,24},{8,4},{16,12},{24,20},{5,9},{13,17},{21,25},... | collective-permute-start | bytes 2359304 | tf_op jit(solution)/shard_map/ppermute | solution.py:916
  32.0 1.7 %local_sums.1.refs_1_ = f32[8,128]{1,0:T(8,128)S(1)} custom-call(s32[6,8]{1,0:T(8,128)S(1)} %get-tuple-element.41.links_ref, f32[33,8,128]{2,1,0:T(8,128)S(1)} %broadcast_in_dim.23.geo_ref.geo_in, f32[8,512,128]{2,1,0:T(8,128)S(1)} %get-tuple-element.33.f_ref.refs_5_.old_ref), custom_call_target="tpu_custom_call" | custom-call | flops 16777216 | bytes 8388608 | tf_op jit(solution)/shard_map/local_sums/pallas_call | solution.py:309
  33.7 3.6 %collective-permute-start.9 = (f32[8,128]{1,0:T(8,128)S(1)}, f32[8,128]{1,0:T(8,128)S(1)}, u32[]{:S(2)}, u32[]{:S(2)}) collective-permute-start(f32[8,128]{1,0:T(8,128)S(1)} %local_sums.1.refs_1_), channel_id=1, source_target_pairs={{0,3},{1,2},{2,1},{3,0},{4,7},{5,6},{6,5},{7,4},{8,11},{9,10},{10,... | collective-permute-start | bytes 12296 | tf_op jit(solution)/shard_map/ppermute | solution.py:444
  37.3 0.0 collective-permute-start.8
  37.3 0.8 %collective-permute-start.7 = (f32[8,128]{1,0:T(8,128)S(1)}, f32[8,128]{1,0:T(8,128)S(1)}, u32[]{:S(2)}, u32[]{:S(2)}) collective-permute-start(f32[8,128]{1,0:T(8,128)S(1)} %local_sums.1.refs_1_), channel_id=1, source_target_pairs={{0,1},{1,0},{2,3},{3,2},{4,5},{5,4},{6,7},{7,6},{8,9},{9,8},{10,11... | collective-permute-start | bytes 12296 | tf_op jit(solution)/shard_map/ppermute | solution.py:444
  38.1 2.9 %flux.3.refs_6_ = f32[8,512,128]{2,1,0:T(8,128)S(1)} custom-call(s32[6,8]{1,0:T(8,128)S(1)} %get-tuple-element.41.links_ref, f32[33,8,128]{2,1,0:T(8,128)S(1)} %broadcast_in_dim.23.geo_ref.geo_in, f32[8,512,128]{2,1,0:T(8,128)S(1)} %get-tuple-element.33.f_ref.refs_5_.old_ref), custom_call_target="tpu_custom_call" | custom-call | flops 29360128 | bytes 14680064 | tf_op jit(solution)/shard_map/flux/pallas_call | solution.py:572
  41.0 0.0 collective-permute-done.9.refs_4_
  41.0 0.8 %collective-permute-done.8.refs_3_ = f32[8,128]{1,0:T(8,128)S(1)} collective-permute-done((f32[8,128]{1,0:T(8,128)S(1)}, f32[8,128]{1,0:T(8,128)S(1)}, u32[]{:S(2)}, u32[]{:S(2)}) %collective-permute-start.8) | collective-permute-done | bytes 4128 | tf_op jit(solution)/shard_map/ppermute | solution.py:444
  41.8 0.0 collective-permute-done.7.refs_2_
  41.8 3.9 %add_target.3.part_ref = f32[8,512,128]{2,1,0:T(8,128)S(1)} custom-call(s32[6,8]{1,0:T(8,128)S(1)} %get-tuple-element.41.links_ref, f32[33,8,128]{2,1,0:T(8,128)S(1)} %broadcast_in_dim.23.geo_ref.geo_in, f32[8,128]{1,0:T(8,128)S(1)} %get-tuple-element.34.refs_0_, f32[8,128]{1,0:T(8,128)S(1)} %local_sums.1.refs_1_, ...), custom_call_target="tpu_custom_call", output_to_operand_aliasing={{}: (8, {})} | custom-call | flops 29360128 | bytes 14680064 | tf_op jit(solution)/shard_map/add_target/pallas_call | solution.py:694
  45.7 0.0 collective-permute-done.4.halo_ref
  45.8 1.2 %last_near.1 = (f32[8,512,128]{2,1,0:T(8,128)S(1)}, f32[8,128]{1,0:T(8,128)S(1)}) custom-call(f32[33,8,128]{2,1,0:T(8,128)S(1)} %broadcast_in_dim.23.geo_ref.geo_in, f32[12,512,128]{2,1,0:T(8,128)S(1)} %get-tuple-element.23.pairs_ref, f32[3,512,128]{2,1,0:T(8,128)S(1)} %collective-permute-done.4.halo_ref, ...), custom_call_target="tpu_custom_call", output_to_operand_aliasing={{0}: (4, {})} | custom-call | flops 12582912 | bytes 6291456 | tf_op jit(solution)/shard_map/last_near/pallas_call | solution.py:816
  46.9 3.3 %collective-permute-done.10.halo_ref = f32[3,512,128]{2,1,0:T(8,128)S(1)} collective-permute-done((f32[3,512,128]{2,1,0:T(8,128)S(1)}, f32[3,512,128]{2,1,0:T(8,128)S(1)}, u32[]{:S(2)}, u32[]{:S(2)}) %collective-permute-start.10) | collective-permute-done | bytes 786464 | tf_op jit(solution)/shard_map/ppermute | solution.py:916
  50.3 0.5 last_far.1
  50.8 1.3 %collective-permute-start.11 = (f32[8,128]{1,0:T(8,128)S(1)}, f32[8,128]{1,0:T(8,128)S(1)}, u32[]{:S(2)}, u32[]{:S(2)}) collective-permute-start(f32[8,128]{1,0:T(8,128)S(1)} %get-tuple-element.39), channel_id=1, source_target_pairs={{0,1},{1,0},{2,3},{3,2},{4,5},{5,4},{6,7},{7,6},{8,9},{9,8},{10,11... | collective-permute-start | bytes 12296 | tf_op jit(solution)/shard_map/ppermute | solution.py:452
  52.1 2.4 %collective-permute-done.11 = f32[8,128]{1,0:T(8,128)S(1)} collective-permute-done((f32[8,128]{1,0:T(8,128)S(1)}, f32[8,128]{1,0:T(8,128)S(1)}, u32[]{:S(2)}, u32[]{:S(2)}) %collective-permute-start.11) | collective-permute-done | bytes 4128 | tf_op jit(solution)/shard_map/ppermute | solution.py:452
  54.4 2.1 %collective-permute-start.12 = (f32[8,128]{1,0:T(8,128)S(1)}, f32[8,128]{1,0:T(8,128)S(1)}, u32[]{:S(2)}, u32[]{:S(2)}) collective-permute-start(f32[8,128]{1,0:T(8,128)S(1)} %add.7.refs_0_), channel_id=1, source_target_pairs={{0,2},{1,3},{2,0},{3,1},{4,6},{5,7},{6,4},{7,5},{8,10},{9,11},{10,... | collective-permute-start | bytes 12296 | tf_op jit(solution)/shard_map/ppermute | solution.py:453
  56.6 1.4 %result.1 = f32[4096,128]{1,0:T(8,128)} custom-call(f32[8,512,128]{2,1,0:T(8,128)S(1)} %get-tuple-element.35.part_ref, f32[3,512,128]{2,1,0:T(8,128)S(1)} %get-tuple-element.38.terms_ref), custom_call_target="tpu_custom_call" | custom-call | flops 12582912 | bytes 6291456 | tf_op jit(solution)/shard_map/result/pallas_call | solution.py:897
  58.0 0.9 %collective-permute-done.12.refs_1_ = f32[8,128]{1,0:T(8,128)S(1)} collective-permute-done((f32[8,128]{1,0:T(8,128)S(1)}, f32[8,128]{1,0:T(8,128)S(1)}, u32[]{:S(2)}, u32[]{:S(2)}) %collective-permute-start.12) | collective-permute-done | bytes 4128 | tf_op jit(solution)/shard_map/ppermute | solution.py:453
  59.0 0.7 %macro.1 = f32[8,8]{1,0:T(8,128)} custom-call(f32[8,128]{1,0:T(8,128)S(1)} %add.7.refs_0_, f32[8,128]{1,0:T(8,128)S(1)} %collective-permute-done.12.refs_1_), custom_call_target="tpu_custom_call" | custom-call | tf_op jit(solution)/shard_map/macro/pallas_call | solution.py:490
  (11 shorter events, 0.0 us)
Async XLA Ops:
  0.6 7.6 %copy-start.2 = (f32[8]{0:T(128)S(1)}, f32[8]{0:T(128)}, u32[]{:S(2)}) copy-start(f32[8]{0:T(128)} %param.8) | copy-start | bytes 100
  0.6 7.6 %copy-start.3 = (f32[8]{0:T(128)S(1)}, f32[8]{0:T(128)}, u32[]{:S(2)}) copy-start(f32[8]{0:T(128)} %param.9) | copy-start | bytes 100
  0.7 7.7 %copy-start.1 = (s32[6,8]{1,0:T(8,128)S(1)}, s32[6,8]{1,0:T(8,128)}, u32[]{:S(2)}) copy-start(s32[6,8]{1,0:T(8,128)} %param.6) | copy-start | bytes 580
  0.7 7.9 %copy-start = (f32[3,6,8]{2,1,0:T(8,128)S(1)}, f32[3,6,8]{2,1,0:T(8,128)}, u32[]{:S(2)}) copy-start(f32[3,6,8]{2,1,0:T(8,128)} %param.7) | copy-start | bytes 1732
  3.1 8.5 %collective-permute-start = (f32[3,512,128]{2,1,0:T(8,128)}, f32[3,512,128]{2,1,0:T(8,128)}, u32[]{:S(2)}, u32[]{:S(2)}) collective-permute-start(f32[3,512,128]{2,1,0:T(8,128)} %get-tuple-element.25), channel_id=1, source_target_pairs={{0,4},{8,12},{16,20},{24,28},{4,0},{12,8},{20,16},{28,24},{1,5},{9... | collective-permute-start | bytes 2359304 | tf_op jit(solution)/shard_map/ppermute | solution.py:916
  3.2 23.5 %collective-permute-start.6 = (f32[3,512,128]{2,1,0:T(8,128)}, f32[3,512,128]{2,1,0:T(8,128)S(1)}, u32[]{:S(2)}, u32[]{:S(2)}) collective-permute-start(f32[3,512,128]{2,1,0:T(8,128)} %get-tuple-element.31), channel_id=1, source_target_pairs={{4,8},{12,16},{16,12},{24,20},{5,9},{13,17},{17,13},{25,21},{6,10}... | collective-permute-start | bytes 2359304 | tf_op jit(solution)/shard_map/ppermute | solution.py:916
  6.6 20.0 %collective-permute-start.5 = (f32[3,512,128]{2,1,0:T(8,128)}, f32[3,512,128]{2,1,0:T(8,128)}, u32[]{:S(2)}, u32[]{:S(2)}) collective-permute-start(f32[3,512,128]{2,1,0:T(8,128)} %get-tuple-element.31), channel_id=1, source_target_pairs={{8,4},{20,24},{9,5},{21,25},{10,6},{22,26},{11,7},{23,27}} | collective-permute-start | bytes 2359304 | tf_op jit(solution)/shard_map/ppermute | solution.py:922
  11.6 8.6 %collective-permute-start.3 = (f32[8,128]{1,0:T(8,128)S(1)}, f32[8,128]{1,0:T(8,128)S(1)}, u32[]{:S(2)}, u32[]{:S(2)}) collective-permute-start(f32[8,128]{1,0:T(8,128)S(1)} %get-tuple-element.27.refs_0_), channel_id=1, source_target_pairs={{0,3},{1,2},{2,1},{3,0},{4,7},{5,6},{6,5},{7,4},{8,11},{9,10},{10,... | collective-permute-start | bytes 12296 | tf_op jit(solution)/shard_map/ppermute | solution.py:444
  15.3 4.9 %collective-permute-start.2 = (f32[8,128]{1,0:T(8,128)S(1)}, f32[8,128]{1,0:T(8,128)S(1)}, u32[]{:S(2)}, u32[]{:S(2)}) collective-permute-start(f32[8,128]{1,0:T(8,128)S(1)} %get-tuple-element.27.refs_0_), channel_id=1, source_target_pairs={{0,2},{1,3},{2,0},{3,1},{4,6},{5,7},{6,4},{7,5},{8,10},{9,11},{10,... | collective-permute-start | bytes 12296 | tf_op jit(solution)/shard_map/ppermute | solution.py:444
  15.3 4.9 %collective-permute-start.1 = (f32[8,128]{1,0:T(8,128)S(1)}, f32[8,128]{1,0:T(8,128)S(1)}, u32[]{:S(2)}, u32[]{:S(2)}) collective-permute-start(f32[8,128]{1,0:T(8,128)S(1)} %get-tuple-element.27.refs_0_), channel_id=1, source_target_pairs={{0,1},{1,0},{2,3},{3,2},{4,5},{5,4},{6,7},{7,6},{8,9},{9,8},{10,11... | collective-permute-start | bytes 12296 | tf_op jit(solution)/shard_map/ppermute | solution.py:444
  25.7 20.0 %collective-permute-start.4 = (f32[3,512,128]{2,1,0:T(8,128)S(1)}, f32[3,512,128]{2,1,0:T(8,128)S(1)}, u32[]{:S(2)}, u32[]{:S(2)}) collective-permute-start(f32[3,512,128]{2,1,0:T(8,128)S(1)} %get-tuple-element.30), channel_id=1, source_target_pairs={{0,4},{8,12},{16,20},{24,28},{4,0},{12,8},{20,16},{28,24},{1,5},{9... | collective-permute-start | bytes 2359304 | tf_op jit(solution)/shard_map/ppermute | solution.py:916
  28.4 21.9 %collective-permute-start.10 = (f32[3,512,128]{2,1,0:T(8,128)S(1)}, f32[3,512,128]{2,1,0:T(8,128)S(1)}, u32[]{:S(2)}, u32[]{:S(2)}) collective-permute-start(f32[3,512,128]{2,1,0:T(8,128)S(1)} %get-tuple-element.36), channel_id=1, source_target_pairs={{4,8},{12,16},{20,24},{8,4},{16,12},{24,20},{5,9},{13,17},{21,25},... | collective-permute-start | bytes 2359304 | tf_op jit(solution)/shard_map/ppermute | solution.py:916
  33.7 7.3 %collective-permute-start.9 = (f32[8,128]{1,0:T(8,128)S(1)}, f32[8,128]{1,0:T(8,128)S(1)}, u32[]{:S(2)}, u32[]{:S(2)}) collective-permute-start(f32[8,128]{1,0:T(8,128)S(1)} %local_sums.1.refs_1_), channel_id=1, source_target_pairs={{0,3},{1,2},{2,1},{3,0},{4,7},{5,6},{6,5},{7,4},{8,11},{9,10},{10,... | collective-permute-start | bytes 12296 | tf_op jit(solution)/shard_map/ppermute | solution.py:444
  37.3 4.5 %collective-permute-start.8 = (f32[8,128]{1,0:T(8,128)S(1)}, f32[8,128]{1,0:T(8,128)S(1)}, u32[]{:S(2)}, u32[]{:S(2)}) collective-permute-start(f32[8,128]{1,0:T(8,128)S(1)} %local_sums.1.refs_1_), channel_id=1, source_target_pairs={{0,2},{1,3},{2,0},{3,1},{4,6},{5,7},{6,4},{7,5},{8,10},{9,11},{10,... | collective-permute-start | bytes 12296 | tf_op jit(solution)/shard_map/ppermute | solution.py:444
  37.3 4.5 %collective-permute-start.7 = (f32[8,128]{1,0:T(8,128)S(1)}, f32[8,128]{1,0:T(8,128)S(1)}, u32[]{:S(2)}, u32[]{:S(2)}) collective-permute-start(f32[8,128]{1,0:T(8,128)S(1)} %local_sums.1.refs_1_), channel_id=1, source_target_pairs={{0,1},{1,0},{2,3},{3,2},{4,5},{5,4},{6,7},{7,6},{8,9},{9,8},{10,11... | collective-permute-start | bytes 12296 | tf_op jit(solution)/shard_map/ppermute | solution.py:444
  50.8 3.7 %collective-permute-start.11 = (f32[8,128]{1,0:T(8,128)S(1)}, f32[8,128]{1,0:T(8,128)S(1)}, u32[]{:S(2)}, u32[]{:S(2)}) collective-permute-start(f32[8,128]{1,0:T(8,128)S(1)} %get-tuple-element.39), channel_id=1, source_target_pairs={{0,1},{1,0},{2,3},{3,2},{4,5},{5,4},{6,7},{7,6},{8,9},{9,8},{10,11... | collective-permute-start | bytes 12296 | tf_op jit(solution)/shard_map/ppermute | solution.py:452
  54.4 4.5 %collective-permute-start.12 = (f32[8,128]{1,0:T(8,128)S(1)}, f32[8,128]{1,0:T(8,128)S(1)}, u32[]{:S(2)}, u32[]{:S(2)}) collective-permute-start(f32[8,128]{1,0:T(8,128)S(1)} %add.7.refs_0_), channel_id=1, source_target_pairs={{0,2},{1,3},{2,0},{3,1},{4,6},{5,7},{6,4},{7,5},{8,10},{9,11},{10,... | collective-permute-start | bytes 12296 | tf_op jit(solution)/shard_map/ppermute | solution.py:453

commit v20 on v18

--- a/solution.py
+++ b/solution.py
@@ -443,14 +443,6 @@
         return [lax.psum(tile, "vel")]
     others = [lax.ppermute(tile, "vel", [(i, i ^ s) for i in range(size)]) for s in range(1, size)]
     return [tile, *others]
-
-
-def doubling_sums(tile):
-    size = lax.axis_size("vel")
-    if size != 4:
-        return gather_sums(tile)
-    pair = tile + lax.ppermute(tile, "vel", [(i, i ^ 1) for i in range(size)])
-    return [pair, lax.ppermute(pair, "vel", [(i, i ^ 2) for i in range(size)])]
 
 
 def add_tiles(refs):
@@ -928,7 +920,7 @@
     (part,) = add_target(links, geo, absorbed, tiles, f, part)
     part, sums = last_near(geo, pairs, near, f, part)
     terms, sums = last_far(geo, pairs, far, f, sums)
-    tiles = doubling_sums(sums)
+    tiles = gather_sums(sums)
     native = result(part, terms)
     macro_quantities = macro(tiles)
     evolved = native.reshape(rows, cells, LANES).transpose(1, 0, 2).reshape(cells, points)

time: 57.4 us -> 57.4 us (level)
  waiting for transfers between devices: 6.74 us -> 8.11 us
  starting transfers between devices: 22.4 us -> 21.6 us
    ppermute x2 -> x0, starting transfers between devices: 5.87 us -> none  [the longest x1 3.03 us: doubling_sums(): return [pair, lax.ppermute(pair, 'vel', [(i, i ^ 2) for i in range(size)])]]
    ppermute x6 -> x9, starting transfers between devices: 8.84 us -> 14.3 us  [gather_sums(): lax.ppermute(tile, 'vel', [(i, i ^ s) for i in range(size)])]
    ppermute x6 -> x9, waiting for transfers between devices: 0.46 us -> 2.92 us  [gather_sums(): lax.ppermute(tile, 'vel', [(i, i ^ s) for i in range(size)])]
    ppermute x2 -> x0, waiting for transfers between devices: 1.72 us -> none  [the longest x1 1.59 us: doubling_sums(): pair = tile + lax.ppermute(tile, 'vel', [(i, i ^ 1) for i in range(size)])]
    ppermute x4, waiting for transfers between devices: 4.56 us -> 5.2 us  [swap(): return lax.ppermute(rows, 'space', pairs + [(j, i) for i, j in pairs])]
  transfers between devices with their start and end apart: 12 -> 13, of which waited for: 5 -> 4; matrix products, arithmetic and copies ran while one was open for 1% -> 1% of each run, Pallas kernels for 40% -> 39%
where the time goes in v20:
time: 57.4 us; the launch traced here: 57.2 us
  Pallas kernels  25.9 us (45%)
  starting transfers between devices  21.6 us (38%)
  waiting for transfers between devices  8.11 us (14%)
  between operations  0.84 us (1%)
  local copies, waits for them, and re-layouts  0.69 us (1%)
    ppermute x9, starting transfers between devices, gather_sums(): lax.ppermute(tile, 'vel', [(i, i ^ s) for i in range(size)])  14.3 us
    pallas_call x2, Pallas kernels, flux(): pl.pallas_call(functools.partial(flux_kernel, with_pairs), in_specs=[spec...  7.72 us
    ppermute x4, starting transfers between devices, swap(): return lax.ppermute(rows, 'space', pairs + [(j, i) for i, j in pairs])  7.3 us
    pallas_call x2, Pallas kernels, add_target(): pl.pallas_call(kernel, in_specs=[spec(pltpu.SMEM)] + [vmem] * (len(given)...  6.49 us
    ppermute x4, waiting for transfers between devices, swap(): return lax.ppermute(rows, 'space', pairs + [(j, i) for i, j in pairs])  5.2 us
    ppermute x9, waiting for transfers between devices, gather_sums(): lax.ppermute(tile, 'vel', [(i, i ^ s) for i in range(size)])  2.92 us
    pallas_call x1, Pallas kernels, first_rows(): pl.pallas_call(first_rows_kernel, in_specs=[spec(pltpu.HBM)], out_specs=[...  2.44 us
    pallas_call x2, Pallas kernels, edge(): pl.pallas_call(functools.partial(add_side, True) if far else near_edge_ke...  2.2 us
  transfers between devices with their start and end apart: 13, of which 4 were waited for; matrix products, arithmetic and copies ran while one was open for 1% of the time, Pallas kernels for 39%

profile of v20, /device:TPU:4, one launch (start us, length us, event | category | flops | bytes accessed | tf_op | source)
XLA Modules:
  0.0 57.2 jit_solution(7375652582471300697)
XLA Ops:
  0.6 0.0 copy-start.2
  0.7 2.4 %first_rows.1 = (f32[4096,128]{1,0:T(8,128)S(1)}, f32[3,512,128]{2,1,0:T(8,128)}, f32[3,512,128]{2,1,0:T(8,128)}) custom-call(f32[4096,128]{1,0:T(8,128)} %bitcast.12), custom_call_target="tpu_custom_call" | custom-call | flops 16777216 | bytes 8388608 | tf_op jit(solution)/shard_map/first_rows/pallas_call | solution.py:389
  3.1 0.1 collective-permute-start
  3.2 3.4 %collective-permute-start.5 = (f32[3,512,128]{2,1,0:T(8,128)}, f32[3,512,128]{2,1,0:T(8,128)S(1)}, u32[]{:S(2)}, u32[]{:S(2)}) collective-permute-start(f32[3,512,128]{2,1,0:T(8,128)} %get-tuple-element.27), channel_id=1, source_target_pairs={{4,8},{12,16},{20,24},{8,4},{16,12},{24,20},{5,9},{13,17},{21,25},... | collective-permute-start | bytes 2359304 | tf_op jit(solution)/shard_map/ppermute | solution.py:885
  6.6 0.1 copy.13
  6.7 0.1 copy.14
  6.8 0.1 copy.16
  6.9 0.1 copy.15
  7.0 0.1 copy.18
  7.1 0.1 concatenate.3
  7.2 0.1 copy.17
  7.2 0.1 broadcast_in_dim.23.geo_ref.geo_in
  7.3 1.8 %first_sums.1 = (f32[8,512,128]{2,1,0:T(8,128)S(1)}, f32[8,128]{1,0:T(8,128)S(1)}) custom-call(s32[6,8]{1,0:T(8,128)S(1)} %get-tuple-element.37.links_ref, f32[33,8,128]{2,1,0:T(8,128)S(1)} %broadcast_in_dim.23.geo_ref.geo_in, f32[4096,128]{1,0:T(8,128)S(1)} %get-tuple-element.19.native_ref), custom_call_target="tpu_custom_call" | custom-call | flops 20971520 | bytes 10485760 | tf_op jit(solution)/shard_map/first_sums/pallas_call | solution.py:327
  9.2 3.7 %collective-permute-start.3 = (f32[8,128]{1,0:T(8,128)S(1)}, f32[8,128]{1,0:T(8,128)S(1)}, u32[]{:S(2)}, u32[]{:S(2)}) collective-permute-start(f32[8,128]{1,0:T(8,128)S(1)} %get-tuple-element.23.refs_0_), channel_id=1, source_target_pairs={{0,3},{1,2},{2,1},{3,0},{4,7},{5,6},{6,5},{7,4},{8,11},{9,10},{10,... | collective-permute-start | bytes 12296 | tf_op jit(solution)/shard_map/ppermute | solution.py:444
  12.8 0.0 collective-permute-start.2
  12.9 0.8 %collective-permute-start.1 = (f32[8,128]{1,0:T(8,128)S(1)}, f32[8,128]{1,0:T(8,128)S(1)}, u32[]{:S(2)}, u32[]{:S(2)}) collective-permute-start(f32[8,128]{1,0:T(8,128)S(1)} %get-tuple-element.23.refs_0_), channel_id=1, source_target_pairs={{0,1},{1,0},{2,3},{3,2},{4,5},{5,4},{6,7},{7,6},{8,9},{9,8},{10,11... | collective-permute-start | bytes 12296 | tf_op jit(solution)/shard_map/ppermute | solution.py:444
  13.6 4.5 %flux.2 = (f32[8,512,128]{2,1,0:T(8,128)S(1)}, f32[12,512,128]{2,1,0:T(8,128)S(1)}) custom-call(s32[6,8]{1,0:T(8,128)S(1)} %get-tuple-element.37.links_ref, f32[33,8,128]{2,1,0:T(8,128)S(1)} %broadcast_in_dim.23.geo_ref.geo_in, f32[8,512,128]{2,1,0:T(8,128)S(1)} %get-tuple-element.20.f_ref.refs_4_.old_ref), custom_call_target="tpu_custom_call" | custom-call | flops 37748736 | bytes 18874368 | tf_op jit(solution)/shard_map/flux/pallas_call | solution.py:564
  18.2 0.0 collective-permute-done.3.refs_3_
  18.2 0.0 collective-permute-done.2.refs_2_
  18.2 0.0 collective-permute-done.1.refs_1_
  18.2 3.3 %add_target.2 = (f32[8,512,128]{2,1,0:T(8,128)S(1)}, f32[8,128]{1,0:T(8,128)S(1)}) custom-call(s32[6,8]{1,0:T(8,128)S(1)} %get-tuple-element.37.links_ref, f32[33,8,128]{2,1,0:T(8,128)S(1)} %broadcast_in_dim.23.geo_ref.geo_in, f32[8,128]{1,0:T(8,128)S(1)} %get-tuple-element.23.refs_0_, ...), custom_call_target="tpu_custom_call", output_to_operand_aliasing={{0}: (7, {})} | custom-call | flops 29360128 | bytes 14680064 | tf_op jit(solution)/shard_map/add_target/pallas_call | solution.py:686
  21.4 0.0 collective-permute-done.halo_any
  21.5 1.6 %near_edge.1 = (f32[8,512,128]{2,1,0:T(8,128)S(1)}, f32[3,512,128]{2,1,0:T(8,128)S(1)}) custom-call(f32[12,512,128]{2,1,0:T(8,128)S(1)} %get-tuple-element.21.pairs_ref, f32[3,512,128]{2,1,0:T(8,128)} %collective-permute-done.halo_any, f32[8,512,128]{2,1,0:T(8,128)S(1)} %get-tuple-element.20.f_ref.refs_4_.old_ref, ...), custom_call_target="tpu_custom_call", output_to_operand_aliasing={{0}: (3, {})} | custom-call | flops 8388608 | bytes 4194304 | tf_op jit(solution)/shard_map/near_edge/pallas_call | solution.py:768
  23.0 0.1 collective-permute-start.4
  23.1 2.0 %collective-permute-done.5.halo_ref = f32[3,512,128]{2,1,0:T(8,128)S(1)} collective-permute-done((f32[3,512,128]{2,1,0:T(8,128)}, f32[3,512,128]{2,1,0:T(8,128)S(1)}, u32[]{:S(2)}, u32[]{:S(2)}) %collective-permute-start.5) | collective-permute-done | bytes 786464 | tf_op jit(solution)/shard_map/ppermute | solution.py:885
  25.1 0.6 %far_edge.1 = (f32[8,512,128]{2,1,0:T(8,128)S(1)}, f32[3,512,128]{2,1,0:T(8,128)S(1)}) custom-call(f32[12,512,128]{2,1,0:T(8,128)S(1)} %get-tuple-element.21.pairs_ref, f32[3,512,128]{2,1,0:T(8,128)S(1)} %collective-permute-done.5.halo_ref, f32[8,512,128]{2,1,0:T(8,128)S(1)} %get-tuple-element.20.f_ref.refs_4_.old_ref, ...), custom_call_target="tpu_custom_call", output_to_operand_aliasing={{0}: (3, {})} | custom-call | flops 8388608 | bytes 4194304 | tf_op jit(solution)/shard_map/far_edge/pallas_call | solution.py:768
  25.8 3.7 %collective-permute-start.9 = (f32[3,512,128]{2,1,0:T(8,128)S(1)}, f32[3,512,128]{2,1,0:T(8,128)S(1)}, u32[]{:S(2)}, u32[]{:S(2)}) collective-permute-start(f32[3,512,128]{2,1,0:T(8,128)S(1)} %get-tuple-element.32), channel_id=1, source_target_pairs={{4,8},{12,16},{20,24},{8,4},{16,12},{24,20},{5,9},{13,17},{21,25},... | collective-permute-start | bytes 2359304 | tf_op jit(solution)/shard_map/ppermute | solution.py:885
  29.5 1.4 %local_sums.1.refs_1_ = f32[8,128]{1,0:T(8,128)S(1)} custom-call(s32[6,8]{1,0:T(8,128)S(1)} %get-tuple-element.37.links_ref, f32[33,8,128]{2,1,0:T(8,128)S(1)} %broadcast_in_dim.23.geo_ref.geo_in, f32[8,512,128]{2,1,0:T(8,128)S(1)} %get-tuple-element.29.f_ref.refs_5_.old_ref), custom_call_target="tpu_custom_call" | custom-call | flops 16777216 | bytes 8388608 | tf_op jit(solution)/shard_map/local_sums/pallas_call | solution.py:309
  30.8 3.6 %collective-permute-start.8 = (f32[8,128]{1,0:T(8,128)S(1)}, f32[8,128]{1,0:T(8,128)S(1)}, u32[]{:S(2)}, u32[]{:S(2)}) collective-permute-start(f32[8,128]{1,0:T(8,128)S(1)} %local_sums.1.refs_1_), channel_id=1, source_target_pairs={{0,3},{1,2},{2,1},{3,0},{4,7},{5,6},{6,5},{7,4},{8,11},{9,10},{10,... | collective-permute-start | bytes 12296 | tf_op jit(solution)/shard_map/ppermute | solution.py:444
  34.5 0.0 collective-permute-start.7
  34.5 0.8 %collective-permute-start.6 = (f32[8,128]{1,0:T(8,128)S(1)}, f32[8,128]{1,0:T(8,128)S(1)}, u32[]{:S(2)}, u32[]{:S(2)}) collective-permute-start(f32[8,128]{1,0:T(8,128)S(1)} %local_sums.1.refs_1_), channel_id=1, source_target_pairs={{0,1},{1,0},{2,3},{3,2},{4,5},{5,4},{6,7},{7,6},{8,9},{9,8},{10,11... | collective-permute-start | bytes 12296 | tf_op jit(solution)/shard_map/ppermute | solution.py:444
  35.3 3.2 %flux.3.refs_6_ = f32[8,512,128]{2,1,0:T(8,128)S(1)} custom-call(s32[6,8]{1,0:T(8,128)S(1)} %get-tuple-element.37.links_ref, f32[33,8,128]{2,1,0:T(8,128)S(1)} %broadcast_in_dim.23.geo_ref.geo_in, f32[8,512,128]{2,1,0:T(8,128)S(1)} %get-tuple-element.29.f_ref.refs_5_.old_ref), custom_call_target="tpu_custom_call" | custom-call | flops 29360128 | bytes 14680064 | tf_op jit(solution)/shard_map/flux/pallas_call | solution.py:564
  38.5 0.0 collective-permute-done.8.refs_4_
  38.5 0.5 collective-permute-done.7.refs_3_
  39.0 0.0 collective-permute-done.6.refs_2_
  39.0 3.2 %add_target.3.part_ref = f32[8,512,128]{2,1,0:T(8,128)S(1)} custom-call(s32[6,8]{1,0:T(8,128)S(1)} %get-tuple-element.37.links_ref, f32[33,8,128]{2,1,0:T(8,128)S(1)} %broadcast_in_dim.23.geo_ref.geo_in, f32[8,128]{1,0:T(8,128)S(1)} %get-tuple-element.30.refs_0_, f32[8,128]{1,0:T(8,128)S(1)} %local_sums.1.refs_1_, ...), custom_call_target="tpu_custom_call", output_to_operand_aliasing={{}: (8, {})} | custom-call | flops 29360128 | bytes 14680064 | tf_op jit(solution)/shard_map/add_target/pallas_call | solution.py:686
  42.2 0.0 collective-permute-done.4.halo_ref
  42.2 1.2 %last_near.1 = (f32[8,512,128]{2,1,0:T(8,128)S(1)}, f32[8,128]{1,0:T(8,128)S(1)}) custom-call(f32[33,8,128]{2,1,0:T(8,128)S(1)} %broadcast_in_dim.23.geo_ref.geo_in, f32[12,512,128]{2,1,0:T(8,128)S(1)} %get-tuple-element.21.pairs_ref, f32[3,512,128]{2,1,0:T(8,128)S(1)} %collective-permute-done.4.halo_ref, ...), custom_call_target="tpu_custom_call", output_to_operand_aliasing={{0}: (4, {})} | custom-call | flops 12582912 | bytes 6291456 | tf_op jit(solution)/shard_map/last_near/pallas_call | solution.py:790
  43.4 3.2 %collective-permute-done.9.halo_ref = f32[3,512,128]{2,1,0:T(8,128)S(1)} collective-permute-done((f32[3,512,128]{2,1,0:T(8,128)S(1)}, f32[3,512,128]{2,1,0:T(8,128)S(1)}, u32[]{:S(2)}, u32[]{:S(2)}) %collective-permute-start.9) | collective-permute-done | bytes 786464 | tf_op jit(solution)/shard_map/ppermute | solution.py:885
  46.6 0.5 last_far.1
  47.1 4.9 %collective-permute-start.12 = (f32[8,128]{1,0:T(8,128)S(1)}, f32[8,128]{1,0:T(8,128)S(1)}, u32[]{:S(2)}, u32[]{:S(2)}) collective-permute-start(f32[8,128]{1,0:T(8,128)S(1)} %get-tuple-element.35.refs_0_), channel_id=1, source_target_pairs={{0,3},{1,2},{2,1},{3,0},{4,7},{5,6},{6,5},{7,4},{8,11},{9,10},{10,... | collective-permute-start | bytes 12296 | tf_op jit(solution)/shard_map/ppermute | solution.py:444
  52.0 0.0 collective-permute-start.11
  52.0 0.6 %collective-permute-start.10 = (f32[8,128]{1,0:T(8,128)S(1)}, f32[8,128]{1,0:T(8,128)S(1)}, u32[]{:S(2)}, u32[]{:S(2)}) collective-permute-start(f32[8,128]{1,0:T(8,128)S(1)} %get-tuple-element.35.refs_0_), channel_id=1, source_target_pairs={{0,1},{1,0},{2,3},{3,2},{4,5},{5,4},{6,7},{7,6},{8,9},{9,8},{10,11... | collective-permute-start | bytes 12296 | tf_op jit(solution)/shard_map/ppermute | solution.py:444
  52.6 1.4 %result.1 = f32[4096,128]{1,0:T(8,128)} custom-call(f32[8,512,128]{2,1,0:T(8,128)S(1)} %get-tuple-element.31.part_ref, f32[3,512,128]{2,1,0:T(8,128)S(1)} %get-tuple-element.34.terms_ref), custom_call_target="tpu_custom_call" | custom-call | flops 12582912 | bytes 6291456 | tf_op jit(solution)/shard_map/result/pallas_call | solution.py:871
  54.1 0.0 collective-permute-done.12.refs_3_
  54.1 2.4 %collective-permute-done.11.refs_2_ = f32[8,128]{1,0:T(8,128)S(1)} collective-permute-done((f32[8,128]{1,0:T(8,128)S(1)}, f32[8,128]{1,0:T(8,128)S(1)}, u32[]{:S(2)}, u32[]{:S(2)}) %collective-permute-start.11) | collective-permute-done | bytes 4128 | tf_op jit(solution)/shard_map/ppermute | solution.py:444
  56.5 0.0 collective-permute-done.10.refs_1_
  56.5 0.7 %macro.1 = f32[8,8]{1,0:T(8,128)} custom-call(f32[8,128]{1,0:T(8,128)S(1)} %get-tuple-element.35.refs_0_, f32[8,128]{1,0:T(8,128)S(1)} %collective-permute-done.10.refs_1_, f32[8,128]{1,0:T(8,128)S(1)} %collective-permute-done.11.refs_2_, f32[8,128]{1,0:T(8,128)S(1)} %collective-permute-done.12.refs_3_), custom_call_target="tpu_custom_call" | custom-call | tf_op jit(solution)/shard_map/macro/pallas_call | solution.py:482
  (10 shorter events, 0.0 us)
Async XLA Ops:
  0.6 6.0 %copy-start.2 = (f32[8]{0:T(128)S(1)}, f32[8]{0:T(128)}, u32[]{:S(2)}) copy-start(f32[8]{0:T(128)} %param.8) | copy-start | bytes 100
  0.6 6.1 %copy-start.3 = (f32[8]{0:T(128)S(1)}, f32[8]{0:T(128)}, u32[]{:S(2)}) copy-start(f32[8]{0:T(128)} %param.9) | copy-start | bytes 100
  0.7 6.2 %copy-start.1 = (s32[6,8]{1,0:T(8,128)S(1)}, s32[6,8]{1,0:T(8,128)}, u32[]{:S(2)}) copy-start(s32[6,8]{1,0:T(8,128)} %param.6) | copy-start | bytes 580
  0.7 6.3 %copy-start = (f32[3,6,8]{2,1,0:T(8,128)S(1)}, f32[3,6,8]{2,1,0:T(8,128)}, u32[]{:S(2)}) copy-start(f32[3,6,8]{2,1,0:T(8,128)} %param.7) | copy-start | bytes 1732
  3.1 18.3 %collective-permute-start = (f32[3,512,128]{2,1,0:T(8,128)}, f32[3,512,128]{2,1,0:T(8,128)}, u32[]{:S(2)}, u32[]{:S(2)}) collective-permute-start(f32[3,512,128]{2,1,0:T(8,128)} %get-tuple-element.22), channel_id=1, source_target_pairs={{0,4},{8,12},{16,20},{24,28},{4,0},{12,8},{20,16},{28,24},{1,5},{9... | collective-permute-start | bytes 2359304 | tf_op jit(solution)/shard_map/ppermute | solution.py:885
  3.2 21.9 %collective-permute-start.5 = (f32[3,512,128]{2,1,0:T(8,128)}, f32[3,512,128]{2,1,0:T(8,128)S(1)}, u32[]{:S(2)}, u32[]{:S(2)}) collective-permute-start(f32[3,512,128]{2,1,0:T(8,128)} %get-tuple-element.27), channel_id=1, source_target_pairs={{4,8},{12,16},{20,24},{8,4},{16,12},{24,20},{5,9},{13,17},{21,25},... | collective-permute-start | bytes 2359304 | tf_op jit(solution)/shard_map/ppermute | solution.py:885
  9.2 9.0 %collective-permute-start.3 = (f32[8,128]{1,0:T(8,128)S(1)}, f32[8,128]{1,0:T(8,128)S(1)}, u32[]{:S(2)}, u32[]{:S(2)}) collective-permute-start(f32[8,128]{1,0:T(8,128)S(1)} %get-tuple-element.23.refs_0_), channel_id=1, source_target_pairs={{0,3},{1,2},{2,1},{3,0},{4,7},{5,6},{6,5},{7,4},{8,11},{9,10},{10,... | collective-permute-start | bytes 12296 | tf_op jit(solution)/shard_map/ppermute | solution.py:444
  12.8 5.3 %collective-permute-start.2 = (f32[8,128]{1,0:T(8,128)S(1)}, f32[8,128]{1,0:T(8,128)S(1)}, u32[]{:S(2)}, u32[]{:S(2)}) collective-permute-start(f32[8,128]{1,0:T(8,128)S(1)} %get-tuple-element.23.refs_0_), channel_id=1, source_target_pairs={{0,2},{1,3},{2,0},{3,1},{4,6},{5,7},{6,4},{7,5},{8,10},{9,11},{10,... | collective-permute-start | bytes 12296 | tf_op jit(solution)/shard_map/ppermute | solution.py:444
  12.9 5.3 %collective-permute-start.1 = (f32[8,128]{1,0:T(8,128)S(1)}, f32[8,128]{1,0:T(8,128)S(1)}, u32[]{:S(2)}, u32[]{:S(2)}) collective-permute-start(f32[8,128]{1,0:T(8,128)S(1)} %get-tuple-element.23.refs_0_), channel_id=1, source_target_pairs={{0,1},{1,0},{2,3},{3,2},{4,5},{5,4},{6,7},{7,6},{8,9},{9,8},{10,11... | collective-permute-start | bytes 12296 | tf_op jit(solution)/shard_map/ppermute | solution.py:444
  23.0 19.2 %collective-permute-start.4 = (f32[3,512,128]{2,1,0:T(8,128)S(1)}, f32[3,512,128]{2,1,0:T(8,128)S(1)}, u32[]{:S(2)}, u32[]{:S(2)}) collective-permute-start(f32[3,512,128]{2,1,0:T(8,128)S(1)} %get-tuple-element.26), channel_id=1, source_target_pairs={{0,4},{8,12},{16,20},{24,28},{4,0},{12,8},{20,16},{28,24},{1,5},{9... | collective-permute-start | bytes 2359304 | tf_op jit(solution)/shard_map/ppermute | solution.py:885
  25.8 20.8 %collective-permute-start.9 = (f32[3,512,128]{2,1,0:T(8,128)S(1)}, f32[3,512,128]{2,1,0:T(8,128)S(1)}, u32[]{:S(2)}, u32[]{:S(2)}) collective-permute-start(f32[3,512,128]{2,1,0:T(8,128)S(1)} %get-tuple-element.32), channel_id=1, source_target_pairs={{4,8},{12,16},{20,24},{8,4},{16,12},{24,20},{5,9},{13,17},{21,25},... | collective-permute-start | bytes 2359304 | tf_op jit(solution)/shard_map/ppermute | solution.py:885
  30.8 7.6 %collective-permute-start.8 = (f32[8,128]{1,0:T(8,128)S(1)}, f32[8,128]{1,0:T(8,128)S(1)}, u32[]{:S(2)}, u32[]{:S(2)}) collective-permute-start(f32[8,128]{1,0:T(8,128)S(1)} %local_sums.1.refs_1_), channel_id=1, source_target_pairs={{0,3},{1,2},{2,1},{3,0},{4,7},{5,6},{6,5},{7,4},{8,11},{9,10},{10,... | collective-permute-start | bytes 12296 | tf_op jit(solution)/shard_map/ppermute | solution.py:444
  34.5 4.5 %collective-permute-start.7 = (f32[8,128]{1,0:T(8,128)S(1)}, f32[8,128]{1,0:T(8,128)S(1)}, u32[]{:S(2)}, u32[]{:S(2)}) collective-permute-start(f32[8,128]{1,0:T(8,128)S(1)} %local_sums.1.refs_1_), channel_id=1, source_target_pairs={{0,2},{1,3},{2,0},{3,1},{4,6},{5,7},{6,4},{7,5},{8,10},{9,11},{10,... | collective-permute-start | bytes 12296 | tf_op jit(solution)/shard_map/ppermute | solution.py:444
  34.5 4.5 %collective-permute-start.6 = (f32[8,128]{1,0:T(8,128)S(1)}, f32[8,128]{1,0:T(8,128)S(1)}, u32[]{:S(2)}, u32[]{:S(2)}) collective-permute-start(f32[8,128]{1,0:T(8,128)S(1)} %local_sums.1.refs_1_), channel_id=1, source_target_pairs={{0,1},{1,0},{2,3},{3,2},{4,5},{5,4},{6,7},{7,6},{8,9},{9,8},{10,11... | collective-permute-start | bytes 12296 | tf_op jit(solution)/shard_map/ppermute | solution.py:444
  47.1 7.0 %collective-permute-start.12 = (f32[8,128]{1,0:T(8,128)S(1)}, f32[8,128]{1,0:T(8,128)S(1)}, u32[]{:S(2)}, u32[]{:S(2)}) collective-permute-start(f32[8,128]{1,0:T(8,128)S(1)} %get-tuple-element.35.refs_0_), channel_id=1, source_target_pairs={{0,3},{1,2},{2,1},{3,0},{4,7},{5,6},{6,5},{7,4},{8,11},{9,10},{10,... | collective-permute-start | bytes 12296 | tf_op jit(solution)/shard_map/ppermute | solution.py:444
  52.0 4.5 %collective-permute-start.11 = (f32[8,128]{1,0:T(8,128)S(1)}, f32[8,128]{1,0:T(8,128)S(1)}, u32[]{:S(2)}, u32[]{:S(2)}) collective-permute-start(f32[8,128]{1,0:T(8,128)S(1)} %get-tuple-element.35.refs_0_), channel_id=1, source_target_pairs={{0,2},{1,3},{2,0},{3,1},{4,6},{5,7},{6,4},{7,5},{8,10},{9,11},{10,... | collective-permute-start | bytes 12296 | tf_op jit(solution)/shard_map/ppermute | solution.py:444
  52.0 4.5 %collective-permute-start.10 = (f32[8,128]{1,0:T(8,128)S(1)}, f32[8,128]{1,0:T(8,128)S(1)}, u32[]{:S(2)}, u32[]{:S(2)}) collective-permute-start(f32[8,128]{1,0:T(8,128)S(1)} %get-tuple-element.35.refs_0_), channel_id=1, source_target_pairs={{0,1},{1,0},{2,3},{3,2},{4,5},{5,4},{6,7},{7,6},{8,9},{9,8},{10,11... | collective-permute-start | bytes 12296 | tf_op jit(solution)/shard_map/ppermute | solution.py:444

commit v21 on v18

--- a/solution.py
+++ b/solution.py
@@ -14,6 +14,7 @@
 STEPS = 2
 LANES = 128
 SUB = 8
+SPARE = SUB
 
 TIME_STEP = 0.015
 SHEAR = 0.1
@@ -312,8 +313,8 @@
         out_specs=spec(pltpu.VMEM),
         out_shape=array(SUB, LANES),
         scratch_shapes=[
-                pltpu.VMEM((10, SUB * SUB, LANES), F32),
-            pltpu.VMEM((FACES, SUB * SUB, LANES), F32),
+                pltpu.VMEM((10, SUB * SUB + SPARE, LANES), F32),
+            pltpu.VMEM((FACES, SUB * SUB + SPARE, LANES), F32),
             *face_lists(),
         ],
         compiler_params=params(),
@@ -323,14 +324,14 @@
 
 
 def first_sums(links, geo, native):
-    rows = native.shape[0] // SUB
+    rows = (native.shape[0] - SPARE) // SUB
     return pl.pallas_call(
         first_sums_kernel,
         in_specs=[spec(pltpu.SMEM), spec(pltpu.VMEM), spec(pltpu.VMEM)],
         out_specs=[spec(pltpu.VMEM)] * 2,
         out_shape=[array(SUB, rows, LANES), array(SUB, LANES)],
         scratch_shapes=[
-                pltpu.VMEM((2 * FACES, SUB * SUB, LANES), F32),
+                pltpu.VMEM((2 * FACES, SUB * SUB + SPARE, LANES), F32),
             *face_lists(),
         ],
         compiler_params=params(),
@@ -347,7 +348,7 @@
 
 
 def first_rows_kernel(native_hbm, native_ref, far_any, near_any, far_ref, near_ref, sems, far_sems, near_sems):
-    rows = native_ref.shape[0]
+    rows = native_hbm.shape[0]
     part = rows // SPLIT_PARTS
     copies = [
         pltpu.make_async_copy(
@@ -390,7 +391,7 @@
         first_rows_kernel,
         in_specs=[spec(pltpu.HBM)],
         out_specs=[spec(pltpu.VMEM), spec(pl.ANY), spec(pl.ANY)],
-        out_shape=[array(*native.shape), array(*halo), array(*halo)],
+        out_shape=[array(native.shape[0] + SPARE, LANES), array(*halo), array(*halo)],
         scratch_shapes=[pltpu.VMEM(halo, F32)] * 2 + [pltpu.SemaphoreType.DMA((SPLIT_PARTS,))] * 3,
         compiler_params=params(),
         cost_estimate=traffic(rows, 4),
@@ -801,7 +802,7 @@
         out_specs=[spec(pltpu.VMEM)] * 2,
         out_shape=[array(SUB, rows, LANES), array(SUB, LANES)],
         input_output_aliases={4: 0},
-        scratch_shapes=[pltpu.VMEM((10, SUB * SUB, LANES), F32)],
+        scratch_shapes=[pltpu.VMEM((10, SUB * SUB + SPARE, LANES), F32)],
         compiler_params=params(),
         cost_estimate=traffic(rows, 3),
         name="last_near",
@@ -835,7 +836,7 @@
         in_specs=[spec(pltpu.VMEM)] * 5,
         out_specs=[spec(pltpu.VMEM)] * 2,
         out_shape=[array(REACH, rows, LANES), array(SUB, LANES)],
-        scratch_shapes=[pltpu.VMEM((10, SUB * SUB, LANES), F32)],
+        scratch_shapes=[pltpu.VMEM((10, SUB * SUB + SPARE, LANES), F32)],
         compiler_params=params(),
         cost_estimate=traffic(rows, 2),
         name="last_far",
@@ -881,7 +882,7 @@
         in_specs=[spec(pltpu.VMEM)] * 2,
         out_specs=spec(pltpu.HBM),
         out_shape=array(*native),
-        scratch_shapes=[pltpu.VMEM(native, F32), pltpu.SemaphoreType.DMA((LAST_PARTS,))],
+        scratch_shapes=[pltpu.VMEM((SUB * rows + SPARE, LANES), F32), pltpu.SemaphoreType.DMA((LAST_PARTS,))],
         compiler_params=params(),
         cost_estimate=traffic(rows, 3),
         name="result",

time: 57.4 us -> 57.4 us (level)
  no operation moved by 1% of the time
where the time goes in v21:
time: 57.4 us; the launch traced here: 56.9 us
  Pallas kernels  26.6 us (46%)
  starting transfers between devices  22.1 us (39%)
  waiting for transfers between devices  6.6 us (11%)
  between operations  0.83 us (1%)
  local copies, waits for them, and re-layouts  0.69 us (1%)
    ppermute x6, starting transfers between devices, gather_sums(): lax.ppermute(tile, 'vel', [(i, i ^ s) for i in range(size)])  8.84 us
    pallas_call x2, Pallas kernels, flux(): pl.pallas_call(functools.partial(flux_kernel, with_pairs), in_specs=[spec...  7.46 us
    ppermute x4, starting transfers between devices, swap(): return lax.ppermute(rows, 'space', pairs + [(j, i) for i, j in pairs])  7.4 us
    pallas_call x2, Pallas kernels, add_target(): pl.pallas_call(kernel, in_specs=[spec(pltpu.SMEM)] + [vmem] * (len(given)...  6.99 us
    ppermute x4, waiting for transfers between devices, swap(): return lax.ppermute(rows, 'space', pairs + [(j, i) for i, j in pairs])  4.27 us
    ppermute x1, starting transfers between devices, doubling_sums(): return [pair, lax.ppermute(pair, 'vel', [(i, i ^ 2) for i in range(size)])]  3.03 us
    ppermute x1, starting transfers between devices, doubling_sums(): pair = tile + lax.ppermute(tile, 'vel', [(i, i ^ 1) for i in range(size)])  2.84 us
    pallas_call x1, Pallas kernels, first_rows(): pl.pallas_call(first_rows_kernel, in_specs=[spec(pltpu.HBM)], out_specs=[...  2.45 us
  transfers between devices with their start and end apart: 12, of which 5 were waited for; matrix products, arithmetic and copies ran while one was open for 1% of the time, Pallas kernels for 40%

profile of v21, /device:TPU:4, one launch (start us, length us, event | category | flops | bytes accessed | tf_op | source)
XLA Modules:
  0.0 56.9 jit_solution(122891014467553729)
XLA Ops:
  0.6 0.0 copy-start.2
  0.6 0.0 copy-start.3
  0.7 2.5 %first_rows.1 = (f32[4104,128]{1,0:T(8,128)S(1)}, f32[3,512,128]{2,1,0:T(8,128)}, f32[3,512,128]{2,1,0:T(8,128)}) custom-call(f32[4096,128]{1,0:T(8,128)} %bitcast.12), custom_call_target="tpu_custom_call" | custom-call | flops 16777216 | bytes 8388608 | tf_op jit(solution)/shard_map/first_rows/pallas_call | solution.py:390
  3.1 0.1 collective-permute-start
  3.2 3.4 %collective-permute-start.5 = (f32[3,512,128]{2,1,0:T(8,128)}, f32[3,512,128]{2,1,0:T(8,128)S(1)}, u32[]{:S(2)}, u32[]{:S(2)}) collective-permute-start(f32[3,512,128]{2,1,0:T(8,128)} %get-tuple-element.27), channel_id=1, source_target_pairs={{4,8},{12,16},{20,24},{8,4},{16,12},{24,20},{5,9},{13,17},{21,25},... | collective-permute-start | bytes 2359304 | tf_op jit(solution)/shard_map/ppermute | solution.py:894
  6.7 0.1 copy.13
  6.7 0.0 copy-done.3
  6.8 0.1 copy.14
  6.8 0.1 copy.16
  6.9 0.1 copy.15
  7.0 0.1 copy.18
  7.1 0.1 concatenate.3
  7.2 0.1 copy.17
  7.3 0.1 broadcast_in_dim.23.geo_ref.geo_in
  7.4 2.2 %first_sums.1 = (f32[8,512,128]{2,1,0:T(8,128)S(1)}, f32[8,128]{1,0:T(8,128)S(1)}) custom-call(s32[6,8]{1,0:T(8,128)S(1)} %get-tuple-element.37.links_ref, f32[33,8,128]{2,1,0:T(8,128)S(1)} %broadcast_in_dim.23.geo_ref.geo_in, f32[4104,128]{1,0:T(8,128)S(1)} %get-tuple-element.19.native_ref), custom_call_target="tpu_custom_call" | custom-call | flops 20971520 | bytes 10485760 | tf_op jit(solution)/shard_map/first_sums/pallas_call | solution.py:328
  9.5 3.7 %collective-permute-start.3 = (f32[8,128]{1,0:T(8,128)S(1)}, f32[8,128]{1,0:T(8,128)S(1)}, u32[]{:S(2)}, u32[]{:S(2)}) collective-permute-start(f32[8,128]{1,0:T(8,128)S(1)} %get-tuple-element.23.refs_0_), channel_id=1, source_target_pairs={{0,3},{1,2},{2,1},{3,0},{4,7},{5,6},{6,5},{7,4},{8,11},{9,10},{10,... | collective-permute-start | bytes 12296 | tf_op jit(solution)/shard_map/ppermute | solution.py:445
  13.2 0.0 collective-permute-start.2
  13.2 0.8 %collective-permute-start.1 = (f32[8,128]{1,0:T(8,128)S(1)}, f32[8,128]{1,0:T(8,128)S(1)}, u32[]{:S(2)}, u32[]{:S(2)}) collective-permute-start(f32[8,128]{1,0:T(8,128)S(1)} %get-tuple-element.23.refs_0_), channel_id=1, source_target_pairs={{0,1},{1,0},{2,3},{3,2},{4,5},{5,4},{6,7},{7,6},{8,9},{9,8},{10,11... | collective-permute-start | bytes 12296 | tf_op jit(solution)/shard_map/ppermute | solution.py:445
  14.0 4.4 %flux.2 = (f32[8,512,128]{2,1,0:T(8,128)S(1)}, f32[12,512,128]{2,1,0:T(8,128)S(1)}) custom-call(s32[6,8]{1,0:T(8,128)S(1)} %get-tuple-element.37.links_ref, f32[33,8,128]{2,1,0:T(8,128)S(1)} %broadcast_in_dim.23.geo_ref.geo_in, f32[8,512,128]{2,1,0:T(8,128)S(1)} %get-tuple-element.20.f_ref.refs_4_.old_ref), custom_call_target="tpu_custom_call" | custom-call | flops 37748736 | bytes 18874368 | tf_op jit(solution)/shard_map/flux/pallas_call | solution.py:573
  18.3 0.0 collective-permute-done.3.refs_3_
  18.4 0.0 collective-permute-done.2.refs_2_
  18.4 0.0 collective-permute-done.1.refs_1_
  18.4 3.5 %add_target.2 = (f32[8,512,128]{2,1,0:T(8,128)S(1)}, f32[8,128]{1,0:T(8,128)S(1)}) custom-call(s32[6,8]{1,0:T(8,128)S(1)} %get-tuple-element.37.links_ref, f32[33,8,128]{2,1,0:T(8,128)S(1)} %broadcast_in_dim.23.geo_ref.geo_in, f32[8,128]{1,0:T(8,128)S(1)} %get-tuple-element.23.refs_0_, ...), custom_call_target="tpu_custom_call", output_to_operand_aliasing={{0}: (7, {})} | custom-call | flops 29360128 | bytes 14680064 | tf_op jit(solution)/shard_map/add_target/pallas_call | solution.py:695
  21.9 0.0 collective-permute-done.halo_any
  21.9 1.6 %near_edge.1 = (f32[8,512,128]{2,1,0:T(8,128)S(1)}, f32[3,512,128]{2,1,0:T(8,128)S(1)}) custom-call(f32[12,512,128]{2,1,0:T(8,128)S(1)} %get-tuple-element.21.pairs_ref, f32[3,512,128]{2,1,0:T(8,128)} %collective-permute-done.halo_any, f32[8,512,128]{2,1,0:T(8,128)S(1)} %get-tuple-element.20.f_ref.refs_4_.old_ref, ...), custom_call_target="tpu_custom_call", output_to_operand_aliasing={{0}: (3, {})} | custom-call | flops 8388608 | bytes 4194304 | tf_op jit(solution)/shard_map/near_edge/pallas_call | solution.py:777
  23.5 0.2 collective-permute-start.4
  23.7 1.5 %collective-permute-done.5.halo_ref = f32[3,512,128]{2,1,0:T(8,128)S(1)} collective-permute-done((f32[3,512,128]{2,1,0:T(8,128)}, f32[3,512,128]{2,1,0:T(8,128)S(1)}, u32[]{:S(2)}, u32[]{:S(2)}) %collective-permute-start.5) | collective-permute-done | bytes 786464 | tf_op jit(solution)/shard_map/ppermute | solution.py:894
  25.2 0.6 %far_edge.1 = (f32[8,512,128]{2,1,0:T(8,128)S(1)}, f32[3,512,128]{2,1,0:T(8,128)S(1)}) custom-call(f32[12,512,128]{2,1,0:T(8,128)S(1)} %get-tuple-element.21.pairs_ref, f32[3,512,128]{2,1,0:T(8,128)S(1)} %collective-permute-done.5.halo_ref, f32[8,512,128]{2,1,0:T(8,128)S(1)} %get-tuple-element.20.f_ref.refs_4_.old_ref, ...), custom_call_target="tpu_custom_call", output_to_operand_aliasing={{0}: (3, {})} | custom-call | flops 8388608 | bytes 4194304 | tf_op jit(solution)/shard_map/far_edge/pallas_call | solution.py:777
  25.8 3.7 %collective-permute-start.9 = (f32[3,512,128]{2,1,0:T(8,128)S(1)}, f32[3,512,128]{2,1,0:T(8,128)S(1)}, u32[]{:S(2)}, u32[]{:S(2)}) collective-permute-start(f32[3,512,128]{2,1,0:T(8,128)S(1)} %get-tuple-element.32), channel_id=1, source_target_pairs={{4,8},{12,16},{20,24},{8,4},{16,12},{24,20},{5,9},{13,17},{21,25},... | collective-permute-start | bytes 2359304 | tf_op jit(solution)/shard_map/ppermute | solution.py:894
  29.5 1.5 %local_sums.1.refs_1_ = f32[8,128]{1,0:T(8,128)S(1)} custom-call(s32[6,8]{1,0:T(8,128)S(1)} %get-tuple-element.37.links_ref, f32[33,8,128]{2,1,0:T(8,128)S(1)} %broadcast_in_dim.23.geo_ref.geo_in, f32[8,512,128]{2,1,0:T(8,128)S(1)} %get-tuple-element.29.f_ref.refs_5_.old_ref), custom_call_target="tpu_custom_call" | custom-call | flops 16777216 | bytes 8388608 | tf_op jit(solution)/shard_map/local_sums/pallas_call | solution.py:310
  31.0 3.6 %collective-permute-start.8 = (f32[8,128]{1,0:T(8,128)S(1)}, f32[8,128]{1,0:T(8,128)S(1)}, u32[]{:S(2)}, u32[]{:S(2)}) collective-permute-start(f32[8,128]{1,0:T(8,128)S(1)} %local_sums.1.refs_1_), channel_id=1, source_target_pairs={{0,3},{1,2},{2,1},{3,0},{4,7},{5,6},{6,5},{7,4},{8,11},{9,10},{10,... | collective-permute-start | bytes 12296 | tf_op jit(solution)/shard_map/ppermute | solution.py:445
  34.6 0.0 collective-permute-start.7
  34.6 0.8 %collective-permute-start.6 = (f32[8,128]{1,0:T(8,128)S(1)}, f32[8,128]{1,0:T(8,128)S(1)}, u32[]{:S(2)}, u32[]{:S(2)}) collective-permute-start(f32[8,128]{1,0:T(8,128)S(1)} %local_sums.1.refs_1_), channel_id=1, source_target_pairs={{0,1},{1,0},{2,3},{3,2},{4,5},{5,4},{6,7},{7,6},{8,9},{9,8},{10,11... | collective-permute-start | bytes 12296 | tf_op jit(solution)/shard_map/ppermute | solution.py:445
  35.4 3.1 %flux.3.refs_6_ = f32[8,512,128]{2,1,0:T(8,128)S(1)} custom-call(s32[6,8]{1,0:T(8,128)S(1)} %get-tuple-element.37.links_ref, f32[33,8,128]{2,1,0:T(8,128)S(1)} %broadcast_in_dim.23.geo_ref.geo_in, f32[8,512,128]{2,1,0:T(8,128)S(1)} %get-tuple-element.29.f_ref.refs_5_.old_ref), custom_call_target="tpu_custom_call" | custom-call | flops 29360128 | bytes 14680064 | tf_op jit(solution)/shard_map/flux/pallas_call | solution.py:573
  38.5 0.0 collective-permute-done.8.refs_4_
  38.5 0.6 %collective-permute-done.7.refs_3_ = f32[8,128]{1,0:T(8,128)S(1)} collective-permute-done((f32[8,128]{1,0:T(8,128)S(1)}, f32[8,128]{1,0:T(8,128)S(1)}, u32[]{:S(2)}, u32[]{:S(2)}) %collective-permute-start.7) | collective-permute-done | bytes 4128 | tf_op jit(solution)/shard_map/ppermute | solution.py:445
  39.1 0.0 collective-permute-done.6.refs_2_
  39.1 3.5 %add_target.3.part_ref = f32[8,512,128]{2,1,0:T(8,128)S(1)} custom-call(s32[6,8]{1,0:T(8,128)S(1)} %get-tuple-element.37.links_ref, f32[33,8,128]{2,1,0:T(8,128)S(1)} %broadcast_in_dim.23.geo_ref.geo_in, f32[8,128]{1,0:T(8,128)S(1)} %get-tuple-element.30.refs_0_, f32[8,128]{1,0:T(8,128)S(1)} %local_sums.1.refs_1_, ...), custom_call_target="tpu_custom_call", output_to_operand_aliasing={{}: (8, {})} | custom-call | flops 29360128 | bytes 14680064 | tf_op jit(solution)/shard_map/add_target/pallas_call | solution.py:695
  42.6 0.0 collective-permute-done.4.halo_ref
  42.6 1.2 %last_near.1 = (f32[8,512,128]{2,1,0:T(8,128)S(1)}, f32[8,128]{1,0:T(8,128)S(1)}) custom-call(f32[33,8,128]{2,1,0:T(8,128)S(1)} %broadcast_in_dim.23.geo_ref.geo_in, f32[12,512,128]{2,1,0:T(8,128)S(1)} %get-tuple-element.21.pairs_ref, f32[3,512,128]{2,1,0:T(8,128)S(1)} %collective-permute-done.4.halo_ref, ...), custom_call_target="tpu_custom_call", output_to_operand_aliasing={{0}: (4, {})} | custom-call | flops 12582912 | bytes 6291456 | tf_op jit(solution)/shard_map/last_near/pallas_call | solution.py:799
  43.8 2.8 %collective-permute-done.9.halo_ref = f32[3,512,128]{2,1,0:T(8,128)S(1)} collective-permute-done((f32[3,512,128]{2,1,0:T(8,128)S(1)}, f32[3,512,128]{2,1,0:T(8,128)S(1)}, u32[]{:S(2)}, u32[]{:S(2)}) %collective-permute-start.9) | collective-permute-done | bytes 786464 | tf_op jit(solution)/shard_map/ppermute | solution.py:894
  46.6 0.5 last_far.1
  47.1 2.8 %collective-permute-start.10 = (f32[8,128]{1,0:T(8,128)S(1)}, f32[8,128]{1,0:T(8,128)S(1)}, u32[]{:S(2)}, u32[]{:S(2)}) collective-permute-start(f32[8,128]{1,0:T(8,128)S(1)} %get-tuple-element.35), channel_id=1, source_target_pairs={{0,1},{1,0},{2,3},{3,2},{4,5},{5,4},{6,7},{7,6},{8,9},{9,8},{10,11... | collective-permute-start | bytes 12296 | tf_op jit(solution)/shard_map/ppermute | solution.py:453
  50.0 1.6 %collective-permute-done.10 = f32[8,128]{1,0:T(8,128)S(1)} collective-permute-done((f32[8,128]{1,0:T(8,128)S(1)}, f32[8,128]{1,0:T(8,128)S(1)}, u32[]{:S(2)}, u32[]{:S(2)}) %collective-permute-start.10) | collective-permute-done | bytes 4128 | tf_op jit(solution)/shard_map/ppermute | solution.py:453
  51.5 3.0 %collective-permute-start.11 = (f32[8,128]{1,0:T(8,128)S(1)}, f32[8,128]{1,0:T(8,128)S(1)}, u32[]{:S(2)}, u32[]{:S(2)}) collective-permute-start(f32[8,128]{1,0:T(8,128)S(1)} %add.7.refs_0_), channel_id=1, source_target_pairs={{0,2},{1,3},{2,0},{3,1},{4,6},{5,7},{6,4},{7,5},{8,10},{9,11},{10,... | collective-permute-start | bytes 12296 | tf_op jit(solution)/shard_map/ppermute | solution.py:454
  54.6 1.4 %result.1 = f32[4096,128]{1,0:T(8,128)} custom-call(f32[8,512,128]{2,1,0:T(8,128)S(1)} %get-tuple-element.31.part_ref, f32[3,512,128]{2,1,0:T(8,128)S(1)} %get-tuple-element.34.terms_ref), custom_call_target="tpu_custom_call" | custom-call | flops 12582912 | bytes 6291456 | tf_op jit(solution)/shard_map/result/pallas_call | solution.py:880
  56.0 0.1 collective-permute-done.11.refs_1_
  56.2 0.7 %macro.1 = f32[8,8]{1,0:T(8,128)} custom-call(f32[8,128]{1,0:T(8,128)S(1)} %add.7.refs_0_, f32[8,128]{1,0:T(8,128)S(1)} %collective-permute-done.11.refs_1_), custom_call_target="tpu_custom_call" | custom-call | tf_op jit(solution)/shard_map/macro/pallas_call | solution.py:491
  (9 shorter events, 0.0 us)
Async XLA Ops:
  0.6 6.0 %copy-start.2 = (f32[8]{0:T(128)S(1)}, f32[8]{0:T(128)}, u32[]{:S(2)}) copy-start(f32[8]{0:T(128)} %param.8) | copy-start | bytes 100
  0.6 6.1 %copy-start.3 = (f32[8]{0:T(128)S(1)}, f32[8]{0:T(128)}, u32[]{:S(2)}) copy-start(f32[8]{0:T(128)} %param.9) | copy-start | bytes 100
  0.7 6.2 %copy-start.1 = (s32[6,8]{1,0:T(8,128)S(1)}, s32[6,8]{1,0:T(8,128)}, u32[]{:S(2)}) copy-start(s32[6,8]{1,0:T(8,128)} %param.6) | copy-start | bytes 580
  0.7 6.3 %copy-start = (f32[3,6,8]{2,1,0:T(8,128)S(1)}, f32[3,6,8]{2,1,0:T(8,128)}, u32[]{:S(2)}) copy-start(f32[3,6,8]{2,1,0:T(8,128)} %param.7) | copy-start | bytes 1732
  3.1 18.7 %collective-permute-start = (f32[3,512,128]{2,1,0:T(8,128)}, f32[3,512,128]{2,1,0:T(8,128)}, u32[]{:S(2)}, u32[]{:S(2)}) collective-permute-start(f32[3,512,128]{2,1,0:T(8,128)} %get-tuple-element.22), channel_id=1, source_target_pairs={{0,4},{8,12},{16,20},{24,28},{4,0},{12,8},{20,16},{28,24},{1,5},{9... | collective-permute-start | bytes 2359304 | tf_op jit(solution)/shard_map/ppermute | solution.py:894
  3.2 21.9 %collective-permute-start.5 = (f32[3,512,128]{2,1,0:T(8,128)}, f32[3,512,128]{2,1,0:T(8,128)S(1)}, u32[]{:S(2)}, u32[]{:S(2)}) collective-permute-start(f32[3,512,128]{2,1,0:T(8,128)} %get-tuple-element.27), channel_id=1, source_target_pairs={{4,8},{12,16},{20,24},{8,4},{16,12},{24,20},{5,9},{13,17},{21,25},... | collective-permute-start | bytes 2359304 | tf_op jit(solution)/shard_map/ppermute | solution.py:894
  9.5 8.8 %collective-permute-start.3 = (f32[8,128]{1,0:T(8,128)S(1)}, f32[8,128]{1,0:T(8,128)S(1)}, u32[]{:S(2)}, u32[]{:S(2)}) collective-permute-start(f32[8,128]{1,0:T(8,128)S(1)} %get-tuple-element.23.refs_0_), channel_id=1, source_target_pairs={{0,3},{1,2},{2,1},{3,0},{4,7},{5,6},{6,5},{7,4},{8,11},{9,10},{10,... | collective-permute-start | bytes 12296 | tf_op jit(solution)/shard_map/ppermute | solution.py:445
  13.2 5.2 %collective-permute-start.2 = (f32[8,128]{1,0:T(8,128)S(1)}, f32[8,128]{1,0:T(8,128)S(1)}, u32[]{:S(2)}, u32[]{:S(2)}) collective-permute-start(f32[8,128]{1,0:T(8,128)S(1)} %get-tuple-element.23.refs_0_), channel_id=1, source_target_pairs={{0,2},{1,3},{2,0},{3,1},{4,6},{5,7},{6,4},{7,5},{8,10},{9,11},{10,... | collective-permute-start | bytes 12296 | tf_op jit(solution)/shard_map/ppermute | solution.py:445
  13.2 5.2 %collective-permute-start.1 = (f32[8,128]{1,0:T(8,128)S(1)}, f32[8,128]{1,0:T(8,128)S(1)}, u32[]{:S(2)}, u32[]{:S(2)}) collective-permute-start(f32[8,128]{1,0:T(8,128)S(1)} %get-tuple-element.23.refs_0_), channel_id=1, source_target_pairs={{0,1},{1,0},{2,3},{3,2},{4,5},{5,4},{6,7},{7,6},{8,9},{9,8},{10,11... | collective-permute-start | bytes 12296 | tf_op jit(solution)/shard_map/ppermute | solution.py:445
  23.5 19.1 %collective-permute-start.4 = (f32[3,512,128]{2,1,0:T(8,128)S(1)}, f32[3,512,128]{2,1,0:T(8,128)S(1)}, u32[]{:S(2)}, u32[]{:S(2)}) collective-permute-start(f32[3,512,128]{2,1,0:T(8,128)S(1)} %get-tuple-element.26), channel_id=1, source_target_pairs={{0,4},{8,12},{16,20},{24,28},{4,0},{12,8},{20,16},{28,24},{1,5},{9... | collective-permute-start | bytes 2359304 | tf_op jit(solution)/shard_map/ppermute | solution.py:894
  25.8 20.8 %collective-permute-start.9 = (f32[3,512,128]{2,1,0:T(8,128)S(1)}, f32[3,512,128]{2,1,0:T(8,128)S(1)}, u32[]{:S(2)}, u32[]{:S(2)}) collective-permute-start(f32[3,512,128]{2,1,0:T(8,128)S(1)} %get-tuple-element.32), channel_id=1, source_target_pairs={{4,8},{12,16},{20,24},{8,4},{16,12},{24,20},{5,9},{13,17},{21,25},... | collective-permute-start | bytes 2359304 | tf_op jit(solution)/shard_map/ppermute | solution.py:894
  31.0 7.5 %collective-permute-start.8 = (f32[8,128]{1,0:T(8,128)S(1)}, f32[8,128]{1,0:T(8,128)S(1)}, u32[]{:S(2)}, u32[]{:S(2)}) collective-permute-start(f32[8,128]{1,0:T(8,128)S(1)} %local_sums.1.refs_1_), channel_id=1, source_target_pairs={{0,3},{1,2},{2,1},{3,0},{4,7},{5,6},{6,5},{7,4},{8,11},{9,10},{10,... | collective-permute-start | bytes 12296 | tf_op jit(solution)/shard_map/ppermute | solution.py:445
  34.6 4.5 %collective-permute-start.7 = (f32[8,128]{1,0:T(8,128)S(1)}, f32[8,128]{1,0:T(8,128)S(1)}, u32[]{:S(2)}, u32[]{:S(2)}) collective-permute-start(f32[8,128]{1,0:T(8,128)S(1)} %local_sums.1.refs_1_), channel_id=1, source_target_pairs={{0,2},{1,3},{2,0},{3,1},{4,6},{5,7},{6,4},{7,5},{8,10},{9,11},{10,... | collective-permute-start | bytes 12296 | tf_op jit(solution)/shard_map/ppermute | solution.py:445
  34.6 4.5 %collective-permute-start.6 = (f32[8,128]{1,0:T(8,128)S(1)}, f32[8,128]{1,0:T(8,128)S(1)}, u32[]{:S(2)}, u32[]{:S(2)}) collective-permute-start(f32[8,128]{1,0:T(8,128)S(1)} %local_sums.1.refs_1_), channel_id=1, source_target_pairs={{0,1},{1,0},{2,3},{3,2},{4,5},{5,4},{6,7},{7,6},{8,9},{9,8},{10,11... | collective-permute-start | bytes 12296 | tf_op jit(solution)/shard_map/ppermute | solution.py:445
  47.1 4.4 %collective-permute-start.10 = (f32[8,128]{1,0:T(8,128)S(1)}, f32[8,128]{1,0:T(8,128)S(1)}, u32[]{:S(2)}, u32[]{:S(2)}) collective-permute-start(f32[8,128]{1,0:T(8,128)S(1)} %get-tuple-element.35), channel_id=1, source_target_pairs={{0,1},{1,0},{2,3},{3,2},{4,5},{5,4},{6,7},{7,6},{8,9},{9,8},{10,11... | collective-permute-start | bytes 12296 | tf_op jit(solution)/shard_map/ppermute | solution.py:453
  51.5 4.6 %collective-permute-start.11 = (f32[8,128]{1,0:T(8,128)S(1)}, f32[8,128]{1,0:T(8,128)S(1)}, u32[]{:S(2)}, u32[]{:S(2)}) collective-permute-start(f32[8,128]{1,0:T(8,128)S(1)} %add.7.refs_0_), channel_id=1, source_target_pairs={{0,2},{1,3},{2,0},{3,1},{4,6},{5,7},{6,4},{7,5},{8,10},{9,11},{10,... | collective-permute-start | bytes 12296 | tf_op jit(solution)/shard_map/ppermute | solution.py:454

commit v22 on v21

--- a/solution.py
+++ b/solution.py
@@ -356,8 +356,8 @@
         )
         for i in range(SPLIT_PARTS)
     ]
-    for c in copies:
-        c.start()
+    for i, c in enumerate(copies):
+        c.start(priority=i % 2)
     odd = is_odd()
     far = jnp.where(odd, SUB - REACH, 0)
     near = jnp.where(odd, 0, SUB - REACH)

time: 57.4 us -> 57.5 us (level)
  Pallas kernels: 26.6 us -> 27.3 us
  transfers between devices with their start and end apart: 12 -> 12, of which waited for: 5 -> 5; matrix products, arithmetic and copies ran while one was open for 1% -> 1% of each run, Pallas kernels for 40% -> 41%
where the time goes in v22:
time: 57.5 us; the launch traced here: 57 us
  Pallas kernels  27.3 us (47%)
  starting transfers between devices  22 us (38%)
  waiting for transfers between devices  6.18 us (11%)
  between operations  0.83 us (1%)
  local copies, waits for them, and re-layouts  0.69 us (1%)
    ppermute x6, starting transfers between devices, gather_sums(): lax.ppermute(tile, 'vel', [(i, i ^ s) for i in range(size)])  8.84 us
    pallas_call x2, Pallas kernels, flux(): pl.pallas_call(functools.partial(flux_kernel, with_pairs), in_specs=[spec...  7.35 us
    pallas_call x2, Pallas kernels, add_target(): pl.pallas_call(kernel, in_specs=[spec(pltpu.SMEM)] + [vmem] * (len(given)...  7.31 us
    ppermute x4, starting transfers between devices, swap(): return lax.ppermute(rows, 'space', pairs + [(j, i) for i, j in pairs])  7.29 us
    ppermute x4, waiting for transfers between devices, swap(): return lax.ppermute(rows, 'space', pairs + [(j, i) for i, j in pairs])  3.9 us
    ppermute x1, starting transfers between devices, doubling_sums(): return [pair, lax.ppermute(pair, 'vel', [(i, i ^ 2) for i in range(size)])]  3.03 us
    ppermute x1, starting transfers between devices, doubling_sums(): pair = tile + lax.ppermute(tile, 'vel', [(i, i ^ 1) for i in range(size)])  2.84 us
    pallas_call x1, Pallas kernels, first_rows(): pl.pallas_call(first_rows_kernel, in_specs=[spec(pltpu.HBM)], out_specs=[...  2.6 us
  transfers between devices with their start and end apart: 12, of which 5 were waited for; matrix products, arithmetic and copies ran while one was open for 1% of the time, Pallas kernels for 41%

profile of v22, /device:TPU:4, one launch (start us, length us, event | category | flops | bytes accessed | tf_op | source)
XLA Modules:
  0.0 57.0 jit_solution(9368964810226594538)
XLA Ops:
  0.6 0.0 copy-start.2
  0.6 0.0 copy-start.3
  0.7 2.6 %first_rows.1 = (f32[4104,128]{1,0:T(8,128)S(1)}, f32[3,512,128]{2,1,0:T(8,128)}, f32[3,512,128]{2,1,0:T(8,128)}) custom-call(f32[4096,128]{1,0:T(8,128)} %bitcast.12), custom_call_target="tpu_custom_call" | custom-call | flops 16777216 | bytes 8388608 | tf_op jit(solution)/shard_map/first_rows/pallas_call | solution.py:390
  3.3 0.1 collective-permute-start
  3.4 3.4 %collective-permute-start.5 = (f32[3,512,128]{2,1,0:T(8,128)}, f32[3,512,128]{2,1,0:T(8,128)S(1)}, u32[]{:S(2)}, u32[]{:S(2)}) collective-permute-start(f32[3,512,128]{2,1,0:T(8,128)} %get-tuple-element.27), channel_id=1, source_target_pairs={{4,8},{12,16},{20,24},{8,4},{16,12},{24,20},{5,9},{13,17},{21,25},... | collective-permute-start | bytes 2359304 | tf_op jit(solution)/shard_map/ppermute | solution.py:894
  6.8 0.1 copy.13
  6.9 0.0 copy-done.3
  6.9 0.1 copy.14
  7.0 0.1 copy.16
  7.1 0.1 copy.15
  7.2 0.1 copy.18
  7.2 0.1 concatenate.3
  7.3 0.1 copy.17
  7.4 0.1 broadcast_in_dim.23.geo_ref.geo_in
  7.5 2.4 %first_sums.1 = (f32[8,512,128]{2,1,0:T(8,128)S(1)}, f32[8,128]{1,0:T(8,128)S(1)}) custom-call(s32[6,8]{1,0:T(8,128)S(1)} %get-tuple-element.37.links_ref, f32[33,8,128]{2,1,0:T(8,128)S(1)} %broadcast_in_dim.23.geo_ref.geo_in, f32[4104,128]{1,0:T(8,128)S(1)} %get-tuple-element.19.native_ref), custom_call_target="tpu_custom_call" | custom-call | flops 20971520 | bytes 10485760 | tf_op jit(solution)/shard_map/first_sums/pallas_call | solution.py:328
  9.9 3.7 %collective-permute-start.3 = (f32[8,128]{1,0:T(8,128)S(1)}, f32[8,128]{1,0:T(8,128)S(1)}, u32[]{:S(2)}, u32[]{:S(2)}) collective-permute-start(f32[8,128]{1,0:T(8,128)S(1)} %get-tuple-element.23.refs_0_), channel_id=1, source_target_pairs={{0,3},{1,2},{2,1},{3,0},{4,7},{5,6},{6,5},{7,4},{8,11},{9,10},{10,... | collective-permute-start | bytes 12296 | tf_op jit(solution)/shard_map/ppermute | solution.py:445
  13.6 0.0 collective-permute-start.2
  13.6 0.8 %collective-permute-start.1 = (f32[8,128]{1,0:T(8,128)S(1)}, f32[8,128]{1,0:T(8,128)S(1)}, u32[]{:S(2)}, u32[]{:S(2)}) collective-permute-start(f32[8,128]{1,0:T(8,128)S(1)} %get-tuple-element.23.refs_0_), channel_id=1, source_target_pairs={{0,1},{1,0},{2,3},{3,2},{4,5},{5,4},{6,7},{7,6},{8,9},{9,8},{10,11... | collective-permute-start | bytes 12296 | tf_op jit(solution)/shard_map/ppermute | solution.py:445
  14.3 4.2 %flux.2 = (f32[8,512,128]{2,1,0:T(8,128)S(1)}, f32[12,512,128]{2,1,0:T(8,128)S(1)}) custom-call(s32[6,8]{1,0:T(8,128)S(1)} %get-tuple-element.37.links_ref, f32[33,8,128]{2,1,0:T(8,128)S(1)} %broadcast_in_dim.23.geo_ref.geo_in, f32[8,512,128]{2,1,0:T(8,128)S(1)} %get-tuple-element.20.f_ref.refs_4_.old_ref), custom_call_target="tpu_custom_call" | custom-call | flops 37748736 | bytes 18874368 | tf_op jit(solution)/shard_map/flux/pallas_call | solution.py:573
  18.5 0.0 collective-permute-done.3.refs_3_
  18.6 0.0 collective-permute-done.2.refs_2_
  18.6 0.0 collective-permute-done.1.refs_1_
  18.6 3.7 %add_target.2 = (f32[8,512,128]{2,1,0:T(8,128)S(1)}, f32[8,128]{1,0:T(8,128)S(1)}) custom-call(s32[6,8]{1,0:T(8,128)S(1)} %get-tuple-element.37.links_ref, f32[33,8,128]{2,1,0:T(8,128)S(1)} %broadcast_in_dim.23.geo_ref.geo_in, f32[8,128]{1,0:T(8,128)S(1)} %get-tuple-element.23.refs_0_, ...), custom_call_target="tpu_custom_call", output_to_operand_aliasing={{0}: (7, {})} | custom-call | flops 29360128 | bytes 14680064 | tf_op jit(solution)/shard_map/add_target/pallas_call | solution.py:695
  22.2 0.0 collective-permute-done.halo_any
  22.3 1.6 %near_edge.1 = (f32[8,512,128]{2,1,0:T(8,128)S(1)}, f32[3,512,128]{2,1,0:T(8,128)S(1)}) custom-call(f32[12,512,128]{2,1,0:T(8,128)S(1)} %get-tuple-element.21.pairs_ref, f32[3,512,128]{2,1,0:T(8,128)} %collective-permute-done.halo_any, f32[8,512,128]{2,1,0:T(8,128)S(1)} %get-tuple-element.20.f_ref.refs_4_.old_ref, ...), custom_call_target="tpu_custom_call", output_to_operand_aliasing={{0}: (3, {})} | custom-call | flops 8388608 | bytes 4194304 | tf_op jit(solution)/shard_map/near_edge/pallas_call | solution.py:777
  23.8 0.1 collective-permute-start.4
  23.9 1.4 %collective-permute-done.5.halo_ref = f32[3,512,128]{2,1,0:T(8,128)S(1)} collective-permute-done((f32[3,512,128]{2,1,0:T(8,128)}, f32[3,512,128]{2,1,0:T(8,128)S(1)}, u32[]{:S(2)}, u32[]{:S(2)}) %collective-permute-start.5) | collective-permute-done | bytes 786464 | tf_op jit(solution)/shard_map/ppermute | solution.py:894
  25.3 0.6 %far_edge.1 = (f32[8,512,128]{2,1,0:T(8,128)S(1)}, f32[3,512,128]{2,1,0:T(8,128)S(1)}) custom-call(f32[12,512,128]{2,1,0:T(8,128)S(1)} %get-tuple-element.21.pairs_ref, f32[3,512,128]{2,1,0:T(8,128)S(1)} %collective-permute-done.5.halo_ref, f32[8,512,128]{2,1,0:T(8,128)S(1)} %get-tuple-element.20.f_ref.refs_4_.old_ref, ...), custom_call_target="tpu_custom_call", output_to_operand_aliasing={{0}: (3, {})} | custom-call | flops 8388608 | bytes 4194304 | tf_op jit(solution)/shard_map/far_edge/pallas_call | solution.py:777
  25.9 3.7 %collective-permute-start.9 = (f32[3,512,128]{2,1,0:T(8,128)S(1)}, f32[3,512,128]{2,1,0:T(8,128)S(1)}, u32[]{:S(2)}, u32[]{:S(2)}) collective-permute-start(f32[3,512,128]{2,1,0:T(8,128)S(1)} %get-tuple-element.32), channel_id=1, source_target_pairs={{4,8},{12,16},{20,24},{8,4},{16,12},{24,20},{5,9},{13,17},{21,25},... | collective-permute-start | bytes 2359304 | tf_op jit(solution)/shard_map/ppermute | solution.py:894
  29.7 1.6 %local_sums.1.refs_1_ = f32[8,128]{1,0:T(8,128)S(1)} custom-call(s32[6,8]{1,0:T(8,128)S(1)} %get-tuple-element.37.links_ref, f32[33,8,128]{2,1,0:T(8,128)S(1)} %broadcast_in_dim.23.geo_ref.geo_in, f32[8,512,128]{2,1,0:T(8,128)S(1)} %get-tuple-element.29.f_ref.refs_5_.old_ref), custom_call_target="tpu_custom_call" | custom-call | flops 16777216 | bytes 8388608 | tf_op jit(solution)/shard_map/local_sums/pallas_call | solution.py:310
  31.2 3.6 %collective-permute-start.8 = (f32[8,128]{1,0:T(8,128)S(1)}, f32[8,128]{1,0:T(8,128)S(1)}, u32[]{:S(2)}, u32[]{:S(2)}) collective-permute-start(f32[8,128]{1,0:T(8,128)S(1)} %local_sums.1.refs_1_), channel_id=1, source_target_pairs={{0,3},{1,2},{2,1},{3,0},{4,7},{5,6},{6,5},{7,4},{8,11},{9,10},{10,... | collective-permute-start | bytes 12296 | tf_op jit(solution)/shard_map/ppermute | solution.py:445
  34.9 0.0 collective-permute-start.7
  34.9 0.8 %collective-permute-start.6 = (f32[8,128]{1,0:T(8,128)S(1)}, f32[8,128]{1,0:T(8,128)S(1)}, u32[]{:S(2)}, u32[]{:S(2)}) collective-permute-start(f32[8,128]{1,0:T(8,128)S(1)} %local_sums.1.refs_1_), channel_id=1, source_target_pairs={{0,1},{1,0},{2,3},{3,2},{4,5},{5,4},{6,7},{7,6},{8,9},{9,8},{10,11... | collective-permute-start | bytes 12296 | tf_op jit(solution)/shard_map/ppermute | solution.py:445
  35.7 3.2 %flux.3.refs_6_ = f32[8,512,128]{2,1,0:T(8,128)S(1)} custom-call(s32[6,8]{1,0:T(8,128)S(1)} %get-tuple-element.37.links_ref, f32[33,8,128]{2,1,0:T(8,128)S(1)} %broadcast_in_dim.23.geo_ref.geo_in, f32[8,512,128]{2,1,0:T(8,128)S(1)} %get-tuple-element.29.f_ref.refs_5_.old_ref), custom_call_target="tpu_custom_call" | custom-call | flops 29360128 | bytes 14680064 | tf_op jit(solution)/shard_map/flux/pallas_call | solution.py:573
  38.8 0.0 collective-permute-done.8.refs_4_
  38.8 0.5 collective-permute-done.7.refs_3_
  39.4 0.0 collective-permute-done.6.refs_2_
  39.4 3.6 %add_target.3.part_ref = f32[8,512,128]{2,1,0:T(8,128)S(1)} custom-call(s32[6,8]{1,0:T(8,128)S(1)} %get-tuple-element.37.links_ref, f32[33,8,128]{2,1,0:T(8,128)S(1)} %broadcast_in_dim.23.geo_ref.geo_in, f32[8,128]{1,0:T(8,128)S(1)} %get-tuple-element.30.refs_0_, f32[8,128]{1,0:T(8,128)S(1)} %local_sums.1.refs_1_, ...), custom_call_target="tpu_custom_call", output_to_operand_aliasing={{}: (8, {})} | custom-call | flops 29360128 | bytes 14680064 | tf_op jit(solution)/shard_map/add_target/pallas_call | solution.py:695
  43.0 0.0 collective-permute-done.4.halo_ref
  43.0 1.2 %last_near.1 = (f32[8,512,128]{2,1,0:T(8,128)S(1)}, f32[8,128]{1,0:T(8,128)S(1)}) custom-call(f32[33,8,128]{2,1,0:T(8,128)S(1)} %broadcast_in_dim.23.geo_ref.geo_in, f32[12,512,128]{2,1,0:T(8,128)S(1)} %get-tuple-element.21.pairs_ref, f32[3,512,128]{2,1,0:T(8,128)S(1)} %collective-permute-done.4.halo_ref, ...), custom_call_target="tpu_custom_call", output_to_operand_aliasing={{0}: (4, {})} | custom-call | flops 12582912 | bytes 6291456 | tf_op jit(solution)/shard_map/last_near/pallas_call | solution.py:799
  44.2 2.5 %collective-permute-done.9.halo_ref = f32[3,512,128]{2,1,0:T(8,128)S(1)} collective-permute-done((f32[3,512,128]{2,1,0:T(8,128)S(1)}, f32[3,512,128]{2,1,0:T(8,128)S(1)}, u32[]{:S(2)}, u32[]{:S(2)}) %collective-permute-start.9) | collective-permute-done | bytes 786464 | tf_op jit(solution)/shard_map/ppermute | solution.py:894
  46.8 0.5 last_far.1
  47.3 2.8 %collective-permute-start.10 = (f32[8,128]{1,0:T(8,128)S(1)}, f32[8,128]{1,0:T(8,128)S(1)}, u32[]{:S(2)}, u32[]{:S(2)}) collective-permute-start(f32[8,128]{1,0:T(8,128)S(1)} %get-tuple-element.35), channel_id=1, source_target_pairs={{0,1},{1,0},{2,3},{3,2},{4,5},{5,4},{6,7},{7,6},{8,9},{9,8},{10,11... | collective-permute-start | bytes 12296 | tf_op jit(solution)/shard_map/ppermute | solution.py:453
  50.1 1.6 %collective-permute-done.10 = f32[8,128]{1,0:T(8,128)S(1)} collective-permute-done((f32[8,128]{1,0:T(8,128)S(1)}, f32[8,128]{1,0:T(8,128)S(1)}, u32[]{:S(2)}, u32[]{:S(2)}) %collective-permute-start.10) | collective-permute-done | bytes 4128 | tf_op jit(solution)/shard_map/ppermute | solution.py:453
  51.7 3.0 %collective-permute-start.11 = (f32[8,128]{1,0:T(8,128)S(1)}, f32[8,128]{1,0:T(8,128)S(1)}, u32[]{:S(2)}, u32[]{:S(2)}) collective-permute-start(f32[8,128]{1,0:T(8,128)S(1)} %add.7.refs_0_), channel_id=1, source_target_pairs={{0,2},{1,3},{2,0},{3,1},{4,6},{5,7},{6,4},{7,5},{8,10},{9,11},{10,... | collective-permute-start | bytes 12296 | tf_op jit(solution)/shard_map/ppermute | solution.py:454
  54.7 1.4 %result.1 = f32[4096,128]{1,0:T(8,128)} custom-call(f32[8,512,128]{2,1,0:T(8,128)S(1)} %get-tuple-element.31.part_ref, f32[3,512,128]{2,1,0:T(8,128)S(1)} %get-tuple-element.34.terms_ref), custom_call_target="tpu_custom_call" | custom-call | flops 12582912 | bytes 6291456 | tf_op jit(solution)/shard_map/result/pallas_call | solution.py:880
  56.2 0.1 collective-permute-done.11.refs_1_
  56.3 0.7 %macro.1 = f32[8,8]{1,0:T(8,128)} custom-call(f32[8,128]{1,0:T(8,128)S(1)} %add.7.refs_0_, f32[8,128]{1,0:T(8,128)S(1)} %collective-permute-done.11.refs_1_), custom_call_target="tpu_custom_call" | custom-call | tf_op jit(solution)/shard_map/macro/pallas_call | solution.py:491
  (9 shorter events, 0.0 us)
Async XLA Ops:
  0.6 6.2 %copy-start.2 = (f32[8]{0:T(128)S(1)}, f32[8]{0:T(128)}, u32[]{:S(2)}) copy-start(f32[8]{0:T(128)} %param.8) | copy-start | bytes 100
  0.6 6.3 %copy-start.3 = (f32[8]{0:T(128)S(1)}, f32[8]{0:T(128)}, u32[]{:S(2)}) copy-start(f32[8]{0:T(128)} %param.9) | copy-start | bytes 100
  0.7 6.3 %copy-start.1 = (s32[6,8]{1,0:T(8,128)S(1)}, s32[6,8]{1,0:T(8,128)}, u32[]{:S(2)}) copy-start(s32[6,8]{1,0:T(8,128)} %param.6) | copy-start | bytes 580
  0.7 6.5 %copy-start = (f32[3,6,8]{2,1,0:T(8,128)S(1)}, f32[3,6,8]{2,1,0:T(8,128)}, u32[]{:S(2)}) copy-start(f32[3,6,8]{2,1,0:T(8,128)} %param.7) | copy-start | bytes 1732
  3.3 19.0 %collective-permute-start = (f32[3,512,128]{2,1,0:T(8,128)}, f32[3,512,128]{2,1,0:T(8,128)}, u32[]{:S(2)}, u32[]{:S(2)}) collective-permute-start(f32[3,512,128]{2,1,0:T(8,128)} %get-tuple-element.22), channel_id=1, source_target_pairs={{0,4},{8,12},{16,20},{24,28},{4,0},{12,8},{20,16},{28,24},{1,5},{9... | collective-permute-start | bytes 2359304 | tf_op jit(solution)/shard_map/ppermute | solution.py:894
  3.4 21.9 %collective-permute-start.5 = (f32[3,512,128]{2,1,0:T(8,128)}, f32[3,512,128]{2,1,0:T(8,128)S(1)}, u32[]{:S(2)}, u32[]{:S(2)}) collective-permute-start(f32[3,512,128]{2,1,0:T(8,128)} %get-tuple-element.27), channel_id=1, source_target_pairs={{4,8},{12,16},{20,24},{8,4},{16,12},{24,20},{5,9},{13,17},{21,25},... | collective-permute-start | bytes 2359304 | tf_op jit(solution)/shard_map/ppermute | solution.py:894
  9.9 8.6 %collective-permute-start.3 = (f32[8,128]{1,0:T(8,128)S(1)}, f32[8,128]{1,0:T(8,128)S(1)}, u32[]{:S(2)}, u32[]{:S(2)}) collective-permute-start(f32[8,128]{1,0:T(8,128)S(1)} %get-tuple-element.23.refs_0_), channel_id=1, source_target_pairs={{0,3},{1,2},{2,1},{3,0},{4,7},{5,6},{6,5},{7,4},{8,11},{9,10},{10,... | collective-permute-start | bytes 12296 | tf_op jit(solution)/shard_map/ppermute | solution.py:445
  13.6 5.0 %collective-permute-start.2 = (f32[8,128]{1,0:T(8,128)S(1)}, f32[8,128]{1,0:T(8,128)S(1)}, u32[]{:S(2)}, u32[]{:S(2)}) collective-permute-start(f32[8,128]{1,0:T(8,128)S(1)} %get-tuple-element.23.refs_0_), channel_id=1, source_target_pairs={{0,2},{1,3},{2,0},{3,1},{4,6},{5,7},{6,4},{7,5},{8,10},{9,11},{10,... | collective-permute-start | bytes 12296 | tf_op jit(solution)/shard_map/ppermute | solution.py:445
  13.6 5.0 %collective-permute-start.1 = (f32[8,128]{1,0:T(8,128)S(1)}, f32[8,128]{1,0:T(8,128)S(1)}, u32[]{:S(2)}, u32[]{:S(2)}) collective-permute-start(f32[8,128]{1,0:T(8,128)S(1)} %get-tuple-element.23.refs_0_), channel_id=1, source_target_pairs={{0,1},{1,0},{2,3},{3,2},{4,5},{5,4},{6,7},{7,6},{8,9},{9,8},{10,11... | collective-permute-start | bytes 12296 | tf_op jit(solution)/shard_map/ppermute | solution.py:445
  23.8 19.2 %collective-permute-start.4 = (f32[3,512,128]{2,1,0:T(8,128)S(1)}, f32[3,512,128]{2,1,0:T(8,128)S(1)}, u32[]{:S(2)}, u32[]{:S(2)}) collective-permute-start(f32[3,512,128]{2,1,0:T(8,128)S(1)} %get-tuple-element.26), channel_id=1, source_target_pairs={{0,4},{8,12},{16,20},{24,28},{4,0},{12,8},{20,16},{28,24},{1,5},{9... | collective-permute-start | bytes 2359304 | tf_op jit(solution)/shard_map/ppermute | solution.py:894
  25.9 20.8 %collective-permute-start.9 = (f32[3,512,128]{2,1,0:T(8,128)S(1)}, f32[3,512,128]{2,1,0:T(8,128)S(1)}, u32[]{:S(2)}, u32[]{:S(2)}) collective-permute-start(f32[3,512,128]{2,1,0:T(8,128)S(1)} %get-tuple-element.32), channel_id=1, source_target_pairs={{4,8},{12,16},{20,24},{8,4},{16,12},{24,20},{5,9},{13,17},{21,25},... | collective-permute-start | bytes 2359304 | tf_op jit(solution)/shard_map/ppermute | solution.py:894
  31.2 7.6 %collective-permute-start.8 = (f32[8,128]{1,0:T(8,128)S(1)}, f32[8,128]{1,0:T(8,128)S(1)}, u32[]{:S(2)}, u32[]{:S(2)}) collective-permute-start(f32[8,128]{1,0:T(8,128)S(1)} %local_sums.1.refs_1_), channel_id=1, source_target_pairs={{0,3},{1,2},{2,1},{3,0},{4,7},{5,6},{6,5},{7,4},{8,11},{9,10},{10,... | collective-permute-start | bytes 12296 | tf_op jit(solution)/shard_map/ppermute | solution.py:445
  34.9 4.5 %collective-permute-start.7 = (f32[8,128]{1,0:T(8,128)S(1)}, f32[8,128]{1,0:T(8,128)S(1)}, u32[]{:S(2)}, u32[]{:S(2)}) collective-permute-start(f32[8,128]{1,0:T(8,128)S(1)} %local_sums.1.refs_1_), channel_id=1, source_target_pairs={{0,2},{1,3},{2,0},{3,1},{4,6},{5,7},{6,4},{7,5},{8,10},{9,11},{10,... | collective-permute-start | bytes 12296 | tf_op jit(solution)/shard_map/ppermute | solution.py:445
  34.9 4.5 %collective-permute-start.6 = (f32[8,128]{1,0:T(8,128)S(1)}, f32[8,128]{1,0:T(8,128)S(1)}, u32[]{:S(2)}, u32[]{:S(2)}) collective-permute-start(f32[8,128]{1,0:T(8,128)S(1)} %local_sums.1.refs_1_), channel_id=1, source_target_pairs={{0,1},{1,0},{2,3},{3,2},{4,5},{5,4},{6,7},{7,6},{8,9},{9,8},{10,11... | collective-permute-start | bytes 12296 | tf_op jit(solution)/shard_map/ppermute | solution.py:445
  47.3 4.4 %collective-permute-start.10 = (f32[8,128]{1,0:T(8,128)S(1)}, f32[8,128]{1,0:T(8,128)S(1)}, u32[]{:S(2)}, u32[]{:S(2)}) collective-permute-start(f32[8,128]{1,0:T(8,128)S(1)} %get-tuple-element.35), channel_id=1, source_target_pairs={{0,1},{1,0},{2,3},{3,2},{4,5},{5,4},{6,7},{7,6},{8,9},{9,8},{10,11... | collective-permute-start | bytes 12296 | tf_op jit(solution)/shard_map/ppermute | solution.py:453
  51.7 4.6 %collective-permute-start.11 = (f32[8,128]{1,0:T(8,128)S(1)}, f32[8,128]{1,0:T(8,128)S(1)}, u32[]{:S(2)}, u32[]{:S(2)}) collective-permute-start(f32[8,128]{1,0:T(8,128)S(1)} %add.7.refs_0_), channel_id=1, source_target_pairs={{0,2},{1,3},{2,0},{3,1},{4,6},{5,7},{6,4},{7,5},{8,10},{9,11},{10,... | collective-permute-start | bytes 12296 | tf_op jit(solution)/shard_map/ppermute | solution.py:454

commit v23 on v21

--- a/solution.py
+++ b/solution.py
@@ -461,8 +461,8 @@
     return tiles[0]
 
 
-def quantities(tile):
-    m = [WEIGHT * column(tile, p) for p in range(13)]
+def quantities(sums):
+    m = [WEIGHT * x for x in sums]
     n = m[0]
     rn = 1.0 / n
     u = [m[1 + i] * rn for i in range(3)]
@@ -480,11 +480,10 @@
 
 def macro_kernel(*refs):
     out_ref = refs[-1]
-    n, u, temperature, q = quantities(add_tiles(refs[:-1]))
-    lane, sub = lane_iota(), sub_iota()
+    by_sum = jnp.transpose(add_tiles(refs[:-1]))
+    n, u, temperature, q = quantities([by_sum[p : p + 1, :] for p in range(13)])
     for i, x in enumerate((n, *u, temperature, *q)):
-        row = jnp.sum(jnp.where(lane == sub, x, 0.0), axis=0, keepdims=True)
-        out_ref[pl.ds(i, 1), :] = row[:, :SUB]
+        out_ref[pl.ds(i, 1), :] = x
 
 
 def macro(tiles):
@@ -596,7 +595,7 @@
     for ref in sum_out:
         ref[...] = sums
     absorbed = sums if absorbed_in is None else absorbed_in[...]
-    n, u, temperature, q = quantities(sums)
+    n, u, temperature, q = quantities([column(sums, p) for p in range(13)])
     rt = 1.0 / temperature
     rate = TIME_STEP * n * temperature / (SHEAR * jnp.exp(POWER * jnp.log(temperature)))
     height = rate * n * rt * jnp.sqrt(rt)

time: 57.4 us -> 57.4 us (level)
  transfers between devices with their start and end apart: 12 -> 12, of which waited for: 5 -> 5; matrix products, arithmetic and copies ran while one was open for 1% -> 1% of each run, Pallas kernels for 40% -> 41%
where the time goes in v23:
time: 57.4 us; the launch traced here: 56.8 us
  Pallas kernels  26.8 us (47%)
  starting transfers between devices  22 us (38%)
  waiting for transfers between devices  6.48 us (11%)
  between operations  0.83 us (1%)
  local copies, waits for them, and re-layouts  0.69 us (1%)
    ppermute x6, starting transfers between devices, gather_sums(): lax.ppermute(tile, 'vel', [(i, i ^ s) for i in range(size)])  8.84 us
    pallas_call x2, Pallas kernels, flux(): pl.pallas_call(functools.partial(flux_kernel, with_pairs), in_specs=[spec...  7.36 us
    ppermute x4, starting transfers between devices, swap(): return lax.ppermute(rows, 'space', pairs + [(j, i) for i, j in pairs])  7.29 us
    pallas_call x2, Pallas kernels, add_target(): pl.pallas_call(kernel, in_specs=[spec(pltpu.SMEM)] + [vmem] * (len(given)...  7.15 us
    ppermute x4, waiting for transfers between devices, swap(): return lax.ppermute(rows, 'space', pairs + [(j, i) for i, j in pairs])  4.11 us
    ppermute x1, starting transfers between devices, doubling_sums(): return [pair, lax.ppermute(pair, 'vel', [(i, i ^ 2) for i in range(size)])]  3.03 us
    ppermute x1, starting transfers between devices, doubling_sums(): pair = tile + lax.ppermute(tile, 'vel', [(i, i ^ 1) for i in range(size)])  2.84 us
    pallas_call x1, Pallas kernels, first_rows(): pl.pallas_call(first_rows_kernel, in_specs=[spec(pltpu.HBM)], out_specs=[...  2.45 us
  transfers between devices with their start and end apart: 12, of which 5 were waited for; matrix products, arithmetic and copies ran while one was open for 1% of the time, Pallas kernels for 41%

profile of v23, /device:TPU:4, one launch (start us, length us, event | category | flops | bytes accessed | tf_op | source)
XLA Modules:
  0.0 56.8 jit_solution(16726132097867953825)
XLA Ops:
  0.6 0.0 copy-start.2
  0.6 0.0 copy-start.3
  0.7 2.5 %first_rows.1 = (f32[4104,128]{1,0:T(8,128)S(1)}, f32[3,512,128]{2,1,0:T(8,128)}, f32[3,512,128]{2,1,0:T(8,128)}) custom-call(f32[4096,128]{1,0:T(8,128)} %bitcast.12), custom_call_target="tpu_custom_call" | custom-call | flops 16777216 | bytes 8388608 | tf_op jit(solution)/shard_map/first_rows/pallas_call | solution.py:390
  3.1 0.1 collective-permute-start
  3.2 3.4 %collective-permute-start.5 = (f32[3,512,128]{2,1,0:T(8,128)}, f32[3,512,128]{2,1,0:T(8,128)S(1)}, u32[]{:S(2)}, u32[]{:S(2)}) collective-permute-start(f32[3,512,128]{2,1,0:T(8,128)} %get-tuple-element.27), channel_id=1, source_target_pairs={{4,8},{12,16},{20,24},{8,4},{16,12},{24,20},{5,9},{13,17},{21,25},... | collective-permute-start | bytes 2359304 | tf_op jit(solution)/shard_map/ppermute | solution.py:893
  6.7 0.1 copy.13
  6.7 0.0 copy-done.3
  6.8 0.1 copy.14
  6.8 0.1 copy.16
  6.9 0.1 copy.15
  7.0 0.1 copy.18
  7.1 0.1 concatenate.3
  7.2 0.1 copy.17
  7.3 0.1 broadcast_in_dim.23.geo_ref.geo_in
  7.4 2.3 %first_sums.1 = (f32[8,512,128]{2,1,0:T(8,128)S(1)}, f32[8,128]{1,0:T(8,128)S(1)}) custom-call(s32[6,8]{1,0:T(8,128)S(1)} %get-tuple-element.37.links_ref, f32[33,8,128]{2,1,0:T(8,128)S(1)} %broadcast_in_dim.23.geo_ref.geo_in, f32[4104,128]{1,0:T(8,128)S(1)} %get-tuple-element.19.native_ref), custom_call_target="tpu_custom_call" | custom-call | flops 20971520 | bytes 10485760 | tf_op jit(solution)/shard_map/first_sums/pallas_call | solution.py:328
  9.7 3.7 %collective-permute-start.3 = (f32[8,128]{1,0:T(8,128)S(1)}, f32[8,128]{1,0:T(8,128)S(1)}, u32[]{:S(2)}, u32[]{:S(2)}) collective-permute-start(f32[8,128]{1,0:T(8,128)S(1)} %get-tuple-element.23.refs_0_), channel_id=1, source_target_pairs={{0,3},{1,2},{2,1},{3,0},{4,7},{5,6},{6,5},{7,4},{8,11},{9,10},{10,... | collective-permute-start | bytes 12296 | tf_op jit(solution)/shard_map/ppermute | solution.py:445
  13.3 0.0 collective-permute-start.2
  13.3 0.8 %collective-permute-start.1 = (f32[8,128]{1,0:T(8,128)S(1)}, f32[8,128]{1,0:T(8,128)S(1)}, u32[]{:S(2)}, u32[]{:S(2)}) collective-permute-start(f32[8,128]{1,0:T(8,128)S(1)} %get-tuple-element.23.refs_0_), channel_id=1, source_target_pairs={{0,1},{1,0},{2,3},{3,2},{4,5},{5,4},{6,7},{7,6},{8,9},{9,8},{10,11... | collective-permute-start | bytes 12296 | tf_op jit(solution)/shard_map/ppermute | solution.py:445
  14.1 4.3 %flux.2 = (f32[8,512,128]{2,1,0:T(8,128)S(1)}, f32[12,512,128]{2,1,0:T(8,128)S(1)}) custom-call(s32[6,8]{1,0:T(8,128)S(1)} %get-tuple-element.37.links_ref, f32[33,8,128]{2,1,0:T(8,128)S(1)} %broadcast_in_dim.23.geo_ref.geo_in, f32[8,512,128]{2,1,0:T(8,128)S(1)} %get-tuple-element.20.f_ref.refs_4_.old_ref), custom_call_target="tpu_custom_call" | custom-call | flops 37748736 | bytes 18874368 | tf_op jit(solution)/shard_map/flux/pallas_call | solution.py:572
  18.4 0.0 collective-permute-done.3.refs_3_
  18.4 0.0 collective-permute-done.2.refs_2_
  18.4 0.0 collective-permute-done.1.refs_1_
  18.4 3.6 %add_target.2 = (f32[8,512,128]{2,1,0:T(8,128)S(1)}, f32[8,128]{1,0:T(8,128)S(1)}) custom-call(s32[6,8]{1,0:T(8,128)S(1)} %get-tuple-element.37.links_ref, f32[33,8,128]{2,1,0:T(8,128)S(1)} %broadcast_in_dim.23.geo_ref.geo_in, f32[8,128]{1,0:T(8,128)S(1)} %get-tuple-element.23.refs_0_, ...), custom_call_target="tpu_custom_call", output_to_operand_aliasing={{0}: (7, {})} | custom-call | flops 29360128 | bytes 14680064 | tf_op jit(solution)/shard_map/add_target/pallas_call | solution.py:694
  22.0 0.0 collective-permute-done.halo_any
  22.0 1.6 %near_edge.1 = (f32[8,512,128]{2,1,0:T(8,128)S(1)}, f32[3,512,128]{2,1,0:T(8,128)S(1)}) custom-call(f32[12,512,128]{2,1,0:T(8,128)S(1)} %get-tuple-element.21.pairs_ref, f32[3,512,128]{2,1,0:T(8,128)} %collective-permute-done.halo_any, f32[8,512,128]{2,1,0:T(8,128)S(1)} %get-tuple-element.20.f_ref.refs_4_.old_ref, ...), custom_call_target="tpu_custom_call", output_to_operand_aliasing={{0}: (3, {})} | custom-call | flops 8388608 | bytes 4194304 | tf_op jit(solution)/shard_map/near_edge/pallas_call | solution.py:776
  23.6 0.1 collective-permute-start.4
  23.7 1.5 %collective-permute-done.5.halo_ref = f32[3,512,128]{2,1,0:T(8,128)S(1)} collective-permute-done((f32[3,512,128]{2,1,0:T(8,128)}, f32[3,512,128]{2,1,0:T(8,128)S(1)}, u32[]{:S(2)}, u32[]{:S(2)}) %collective-permute-start.5) | collective-permute-done | bytes 786464 | tf_op jit(solution)/shard_map/ppermute | solution.py:893
  25.2 0.6 %far_edge.1 = (f32[8,512,128]{2,1,0:T(8,128)S(1)}, f32[3,512,128]{2,1,0:T(8,128)S(1)}) custom-call(f32[12,512,128]{2,1,0:T(8,128)S(1)} %get-tuple-element.21.pairs_ref, f32[3,512,128]{2,1,0:T(8,128)S(1)} %collective-permute-done.5.halo_ref, f32[8,512,128]{2,1,0:T(8,128)S(1)} %get-tuple-element.20.f_ref.refs_4_.old_ref, ...), custom_call_target="tpu_custom_call", output_to_operand_aliasing={{0}: (3, {})} | custom-call | flops 8388608 | bytes 4194304 | tf_op jit(solution)/shard_map/far_edge/pallas_call | solution.py:776
  25.8 3.7 %collective-permute-start.9 = (f32[3,512,128]{2,1,0:T(8,128)S(1)}, f32[3,512,128]{2,1,0:T(8,128)S(1)}, u32[]{:S(2)}, u32[]{:S(2)}) collective-permute-start(f32[3,512,128]{2,1,0:T(8,128)S(1)} %get-tuple-element.32), channel_id=1, source_target_pairs={{4,8},{12,16},{20,24},{8,4},{16,12},{24,20},{5,9},{13,17},{21,25},... | collective-permute-start | bytes 2359304 | tf_op jit(solution)/shard_map/ppermute | solution.py:893
  29.5 1.5 %local_sums.1.refs_1_ = f32[8,128]{1,0:T(8,128)S(1)} custom-call(s32[6,8]{1,0:T(8,128)S(1)} %get-tuple-element.37.links_ref, f32[33,8,128]{2,1,0:T(8,128)S(1)} %broadcast_in_dim.23.geo_ref.geo_in, f32[8,512,128]{2,1,0:T(8,128)S(1)} %get-tuple-element.29.f_ref.refs_5_.old_ref), custom_call_target="tpu_custom_call" | custom-call | flops 16777216 | bytes 8388608 | tf_op jit(solution)/shard_map/local_sums/pallas_call | solution.py:310
  31.1 3.6 %collective-permute-start.8 = (f32[8,128]{1,0:T(8,128)S(1)}, f32[8,128]{1,0:T(8,128)S(1)}, u32[]{:S(2)}, u32[]{:S(2)}) collective-permute-start(f32[8,128]{1,0:T(8,128)S(1)} %local_sums.1.refs_1_), channel_id=1, source_target_pairs={{0,3},{1,2},{2,1},{3,0},{4,7},{5,6},{6,5},{7,4},{8,11},{9,10},{10,... | collective-permute-start | bytes 12296 | tf_op jit(solution)/shard_map/ppermute | solution.py:445
  34.7 0.0 collective-permute-start.7
  34.7 0.8 %collective-permute-start.6 = (f32[8,128]{1,0:T(8,128)S(1)}, f32[8,128]{1,0:T(8,128)S(1)}, u32[]{:S(2)}, u32[]{:S(2)}) collective-permute-start(f32[8,128]{1,0:T(8,128)S(1)} %local_sums.1.refs_1_), channel_id=1, source_target_pairs={{0,1},{1,0},{2,3},{3,2},{4,5},{5,4},{6,7},{7,6},{8,9},{9,8},{10,11... | collective-permute-start | bytes 12296 | tf_op jit(solution)/shard_map/ppermute | solution.py:445
  35.5 3.1 %flux.3.refs_6_ = f32[8,512,128]{2,1,0:T(8,128)S(1)} custom-call(s32[6,8]{1,0:T(8,128)S(1)} %get-tuple-element.37.links_ref, f32[33,8,128]{2,1,0:T(8,128)S(1)} %broadcast_in_dim.23.geo_ref.geo_in, f32[8,512,128]{2,1,0:T(8,128)S(1)} %get-tuple-element.29.f_ref.refs_5_.old_ref), custom_call_target="tpu_custom_call" | custom-call | flops 29360128 | bytes 14680064 | tf_op jit(solution)/shard_map/flux/pallas_call | solution.py:572
  38.5 0.0 collective-permute-done.8.refs_4_
  38.5 0.6 %collective-permute-done.7.refs_3_ = f32[8,128]{1,0:T(8,128)S(1)} collective-permute-done((f32[8,128]{1,0:T(8,128)S(1)}, f32[8,128]{1,0:T(8,128)S(1)}, u32[]{:S(2)}, u32[]{:S(2)}) %collective-permute-start.7) | collective-permute-done | bytes 4128 | tf_op jit(solution)/shard_map/ppermute | solution.py:445
  39.2 0.0 collective-permute-done.6.refs_2_
  39.2 3.6 %add_target.3.part_ref = f32[8,512,128]{2,1,0:T(8,128)S(1)} custom-call(s32[6,8]{1,0:T(8,128)S(1)} %get-tuple-element.37.links_ref, f32[33,8,128]{2,1,0:T(8,128)S(1)} %broadcast_in_dim.23.geo_ref.geo_in, f32[8,128]{1,0:T(8,128)S(1)} %get-tuple-element.30.refs_0_, f32[8,128]{1,0:T(8,128)S(1)} %local_sums.1.refs_1_, ...), custom_call_target="tpu_custom_call", output_to_operand_aliasing={{}: (8, {})} | custom-call | flops 29360128 | bytes 14680064 | tf_op jit(solution)/shard_map/add_target/pallas_call | solution.py:694
  42.7 0.0 collective-permute-done.4.halo_ref
  42.8 1.2 %last_near.1 = (f32[8,512,128]{2,1,0:T(8,128)S(1)}, f32[8,128]{1,0:T(8,128)S(1)}) custom-call(f32[33,8,128]{2,1,0:T(8,128)S(1)} %broadcast_in_dim.23.geo_ref.geo_in, f32[12,512,128]{2,1,0:T(8,128)S(1)} %get-tuple-element.21.pairs_ref, f32[3,512,128]{2,1,0:T(8,128)S(1)} %collective-permute-done.4.halo_ref, ...), custom_call_target="tpu_custom_call", output_to_operand_aliasing={{0}: (4, {})} | custom-call | flops 12582912 | bytes 6291456 | tf_op jit(solution)/shard_map/last_near/pallas_call | solution.py:798
  44.0 2.6 %collective-permute-done.9.halo_ref = f32[3,512,128]{2,1,0:T(8,128)S(1)} collective-permute-done((f32[3,512,128]{2,1,0:T(8,128)S(1)}, f32[3,512,128]{2,1,0:T(8,128)S(1)}, u32[]{:S(2)}, u32[]{:S(2)}) %collective-permute-start.9) | collective-permute-done | bytes 786464 | tf_op jit(solution)/shard_map/ppermute | solution.py:893
  46.6 0.5 last_far.1
  47.1 2.8 %collective-permute-start.10 = (f32[8,128]{1,0:T(8,128)S(1)}, f32[8,128]{1,0:T(8,128)S(1)}, u32[]{:S(2)}, u32[]{:S(2)}) collective-permute-start(f32[8,128]{1,0:T(8,128)S(1)} %get-tuple-element.35), channel_id=1, source_target_pairs={{0,1},{1,0},{2,3},{3,2},{4,5},{5,4},{6,7},{7,6},{8,9},{9,8},{10,11... | collective-permute-start | bytes 12296 | tf_op jit(solution)/shard_map/ppermute | solution.py:453
  50.0 1.6 %collective-permute-done.10 = f32[8,128]{1,0:T(8,128)S(1)} collective-permute-done((f32[8,128]{1,0:T(8,128)S(1)}, f32[8,128]{1,0:T(8,128)S(1)}, u32[]{:S(2)}, u32[]{:S(2)}) %collective-permute-start.10) | collective-permute-done | bytes 4128 | tf_op jit(solution)/shard_map/ppermute | solution.py:453
  51.5 3.0 %collective-permute-start.11 = (f32[8,128]{1,0:T(8,128)S(1)}, f32[8,128]{1,0:T(8,128)S(1)}, u32[]{:S(2)}, u32[]{:S(2)}) collective-permute-start(f32[8,128]{1,0:T(8,128)S(1)} %add.7.refs_0_), channel_id=1, source_target_pairs={{0,2},{1,3},{2,0},{3,1},{4,6},{5,7},{6,4},{7,5},{8,10},{9,11},{10,... | collective-permute-start | bytes 12296 | tf_op jit(solution)/shard_map/ppermute | solution.py:454
  54.6 1.4 %result.1 = f32[4096,128]{1,0:T(8,128)} custom-call(f32[8,512,128]{2,1,0:T(8,128)S(1)} %get-tuple-element.31.part_ref, f32[3,512,128]{2,1,0:T(8,128)S(1)} %get-tuple-element.34.terms_ref), custom_call_target="tpu_custom_call" | custom-call | flops 12582912 | bytes 6291456 | tf_op jit(solution)/shard_map/result/pallas_call | solution.py:879
  56.0 0.1 collective-permute-done.11.refs_1_
  56.2 0.7 %macro.1 = f32[8,8]{1,0:T(8,128)} custom-call(f32[8,128]{1,0:T(8,128)S(1)} %add.7.refs_0_, f32[8,128]{1,0:T(8,128)S(1)} %collective-permute-done.11.refs_1_), custom_call_target="tpu_custom_call" | custom-call | tf_op jit(solution)/shard_map/macro/pallas_call | solution.py:490
  (9 shorter events, 0.0 us)
Async XLA Ops:
  0.6 6.0 %copy-start.2 = (f32[8]{0:T(128)S(1)}, f32[8]{0:T(128)}, u32[]{:S(2)}) copy-start(f32[8]{0:T(128)} %param.8) | copy-start | bytes 100
  0.6 6.1 %copy-start.3 = (f32[8]{0:T(128)S(1)}, f32[8]{0:T(128)}, u32[]{:S(2)}) copy-start(f32[8]{0:T(128)} %param.9) | copy-start | bytes 100
  0.7 6.2 %copy-start.1 = (s32[6,8]{1,0:T(8,128)S(1)}, s32[6,8]{1,0:T(8,128)}, u32[]{:S(2)}) copy-start(s32[6,8]{1,0:T(8,128)} %param.6) | copy-start | bytes 580
  0.7 6.3 %copy-start = (f32[3,6,8]{2,1,0:T(8,128)S(1)}, f32[3,6,8]{2,1,0:T(8,128)}, u32[]{:S(2)}) copy-start(f32[3,6,8]{2,1,0:T(8,128)} %param.7) | copy-start | bytes 1732
  3.1 18.9 %collective-permute-start = (f32[3,512,128]{2,1,0:T(8,128)}, f32[3,512,128]{2,1,0:T(8,128)}, u32[]{:S(2)}, u32[]{:S(2)}) collective-permute-start(f32[3,512,128]{2,1,0:T(8,128)} %get-tuple-element.22), channel_id=1, source_target_pairs={{0,4},{8,12},{16,20},{24,28},{4,0},{12,8},{20,16},{28,24},{1,5},{9... | collective-permute-start | bytes 2359304 | tf_op jit(solution)/shard_map/ppermute | solution.py:893
  3.2 21.9 %collective-permute-start.5 = (f32[3,512,128]{2,1,0:T(8,128)}, f32[3,512,128]{2,1,0:T(8,128)S(1)}, u32[]{:S(2)}, u32[]{:S(2)}) collective-permute-start(f32[3,512,128]{2,1,0:T(8,128)} %get-tuple-element.27), channel_id=1, source_target_pairs={{4,8},{12,16},{20,24},{8,4},{16,12},{24,20},{5,9},{13,17},{21,25},... | collective-permute-start | bytes 2359304 | tf_op jit(solution)/shard_map/ppermute | solution.py:893
  9.7 8.8 %collective-permute-start.3 = (f32[8,128]{1,0:T(8,128)S(1)}, f32[8,128]{1,0:T(8,128)S(1)}, u32[]{:S(2)}, u32[]{:S(2)}) collective-permute-start(f32[8,128]{1,0:T(8,128)S(1)} %get-tuple-element.23.refs_0_), channel_id=1, source_target_pairs={{0,3},{1,2},{2,1},{3,0},{4,7},{5,6},{6,5},{7,4},{8,11},{9,10},{10,... | collective-permute-start | bytes 12296 | tf_op jit(solution)/shard_map/ppermute | solution.py:445
  13.3 5.1 %collective-permute-start.2 = (f32[8,128]{1,0:T(8,128)S(1)}, f32[8,128]{1,0:T(8,128)S(1)}, u32[]{:S(2)}, u32[]{:S(2)}) collective-permute-start(f32[8,128]{1,0:T(8,128)S(1)} %get-tuple-element.23.refs_0_), channel_id=1, source_target_pairs={{0,2},{1,3},{2,0},{3,1},{4,6},{5,7},{6,4},{7,5},{8,10},{9,11},{10,... | collective-permute-start | bytes 12296 | tf_op jit(solution)/shard_map/ppermute | solution.py:445
  13.3 5.1 %collective-permute-start.1 = (f32[8,128]{1,0:T(8,128)S(1)}, f32[8,128]{1,0:T(8,128)S(1)}, u32[]{:S(2)}, u32[]{:S(2)}) collective-permute-start(f32[8,128]{1,0:T(8,128)S(1)} %get-tuple-element.23.refs_0_), channel_id=1, source_target_pairs={{0,1},{1,0},{2,3},{3,2},{4,5},{5,4},{6,7},{7,6},{8,9},{9,8},{10,11... | collective-permute-start | bytes 12296 | tf_op jit(solution)/shard_map/ppermute | solution.py:445
  23.6 19.1 %collective-permute-start.4 = (f32[3,512,128]{2,1,0:T(8,128)S(1)}, f32[3,512,128]{2,1,0:T(8,128)S(1)}, u32[]{:S(2)}, u32[]{:S(2)}) collective-permute-start(f32[3,512,128]{2,1,0:T(8,128)S(1)} %get-tuple-element.26), channel_id=1, source_target_pairs={{0,4},{8,12},{16,20},{24,28},{4,0},{12,8},{20,16},{28,24},{1,5},{9... | collective-permute-start | bytes 2359304 | tf_op jit(solution)/shard_map/ppermute | solution.py:893
  25.8 20.8 %collective-permute-start.9 = (f32[3,512,128]{2,1,0:T(8,128)S(1)}, f32[3,512,128]{2,1,0:T(8,128)S(1)}, u32[]{:S(2)}, u32[]{:S(2)}) collective-permute-start(f32[3,512,128]{2,1,0:T(8,128)S(1)} %get-tuple-element.32), channel_id=1, source_target_pairs={{4,8},{12,16},{20,24},{8,4},{16,12},{24,20},{5,9},{13,17},{21,25},... | collective-permute-start | bytes 2359304 | tf_op jit(solution)/shard_map/ppermute | solution.py:893
  31.1 7.5 %collective-permute-start.8 = (f32[8,128]{1,0:T(8,128)S(1)}, f32[8,128]{1,0:T(8,128)S(1)}, u32[]{:S(2)}, u32[]{:S(2)}) collective-permute-start(f32[8,128]{1,0:T(8,128)S(1)} %local_sums.1.refs_1_), channel_id=1, source_target_pairs={{0,3},{1,2},{2,1},{3,0},{4,7},{5,6},{6,5},{7,4},{8,11},{9,10},{10,... | collective-permute-start | bytes 12296 | tf_op jit(solution)/shard_map/ppermute | solution.py:445
  34.7 4.5 %collective-permute-start.7 = (f32[8,128]{1,0:T(8,128)S(1)}, f32[8,128]{1,0:T(8,128)S(1)}, u32[]{:S(2)}, u32[]{:S(2)}) collective-permute-start(f32[8,128]{1,0:T(8,128)S(1)} %local_sums.1.refs_1_), channel_id=1, source_target_pairs={{0,2},{1,3},{2,0},{3,1},{4,6},{5,7},{6,4},{7,5},{8,10},{9,11},{10,... | collective-permute-start | bytes 12296 | tf_op jit(solution)/shard_map/ppermute | solution.py:445
  34.7 4.5 %collective-permute-start.6 = (f32[8,128]{1,0:T(8,128)S(1)}, f32[8,128]{1,0:T(8,128)S(1)}, u32[]{:S(2)}, u32[]{:S(2)}) collective-permute-start(f32[8,128]{1,0:T(8,128)S(1)} %local_sums.1.refs_1_), channel_id=1, source_target_pairs={{0,1},{1,0},{2,3},{3,2},{4,5},{5,4},{6,7},{7,6},{8,9},{9,8},{10,11... | collective-permute-start | bytes 12296 | tf_op jit(solution)/shard_map/ppermute | solution.py:445
  47.1 4.4 %collective-permute-start.10 = (f32[8,128]{1,0:T(8,128)S(1)}, f32[8,128]{1,0:T(8,128)S(1)}, u32[]{:S(2)}, u32[]{:S(2)}) collective-permute-start(f32[8,128]{1,0:T(8,128)S(1)} %get-tuple-element.35), channel_id=1, source_target_pairs={{0,1},{1,0},{2,3},{3,2},{4,5},{5,4},{6,7},{7,6},{8,9},{9,8},{10,11... | collective-permute-start | bytes 12296 | tf_op jit(solution)/shard_map/ppermute | solution.py:453
  51.5 4.6 %collective-permute-start.11 = (f32[8,128]{1,0:T(8,128)S(1)}, f32[8,128]{1,0:T(8,128)S(1)}, u32[]{:S(2)}, u32[]{:S(2)}) collective-permute-start(f32[8,128]{1,0:T(8,128)S(1)} %add.7.refs_0_), channel_id=1, source_target_pairs={{0,2},{1,3},{2,0},{3,1},{4,6},{5,7},{6,4},{7,5},{8,10},{9,11},{10,... | collective-permute-start | bytes 12296 | tf_op jit(solution)/shard_map/ppermute | solution.py:454

commit v24 on v23

--- a/solution.py
+++ b/solution.py
@@ -478,23 +478,10 @@
     return n, u, temperature, q
 
 
-def macro_kernel(*refs):
-    out_ref = refs[-1]
-    by_sum = jnp.transpose(add_tiles(refs[:-1]))
-    n, u, temperature, q = quantities([by_sum[p : p + 1, :] for p in range(13)])
-    for i, x in enumerate((n, *u, temperature, *q)):
-        out_ref[pl.ds(i, 1), :] = x
-
-
 def macro(tiles):
-    return pl.pallas_call(
-        macro_kernel,
-        in_specs=[spec(pltpu.VMEM)] * len(tiles),
-        out_specs=spec(pltpu.VMEM),
-        out_shape=array(8, SUB),
-        compiler_params=params(1),
-        name="macro",
-    )(*tiles)
+    by_sum = sum(tiles[1:], tiles[0])[:, :13].T
+    n, u, temperature, q = quantities([by_sum[p] for p in range(13)])
+    return jnp.stack([n, *u, temperature, *q])
 
 
 def flux_kernel(with_pairs, links_ref, geo_ref, f_ref, out_ref, *refs):

time: 57.4 us -> 57.6 us (level)
  local copies, waits for them, and re-layouts: 0.69 us -> 1.44 us
    pallas_call x1 -> x0, Pallas kernels: 0.68 us -> none  [macro(): pl.pallas_call(macro_kernel, in_specs=[spec(pltpu.VMEM)] * len(tiles), ou...]
    unnamed x8 -> x9, local copies, waits for them, and re-layouts: 0.02 us -> 0.68 us
  transfers between devices with their start and end apart: 12 -> 12, of which waited for: 5 -> 5; matrix products, arithmetic and copies ran while one was open for 1% -> 1% of each run, Pallas kernels for 41% -> 42%
where the time goes in v24:
time: 57.6 us; the launch traced here: 57.1 us
  Pallas kernels  26.7 us (46%)
  starting transfers between devices  22 us (38%)
  waiting for transfers between devices  5.95 us (10%)
  local copies, waits for them, and re-layouts  1.44 us (2%)
  between operations  0.84 us (1%)
    ppermute x6, starting transfers between devices, gather_sums(): lax.ppermute(tile, 'vel', [(i, i ^ s) for i in range(size)])  8.84 us
    pallas_call x2, Pallas kernels, add_target(): pl.pallas_call(kernel, in_specs=[spec(pltpu.SMEM)] + [vmem] * (len(given)...  7.48 us
    ppermute x4, starting transfers between devices, swap(): return lax.ppermute(rows, 'space', pairs + [(j, i) for i, j in pairs])  7.29 us
    pallas_call x2, Pallas kernels, flux(): pl.pallas_call(functools.partial(flux_kernel, with_pairs), in_specs=[spec...  7.25 us
    ppermute x4, waiting for transfers between devices, swap(): return lax.ppermute(rows, 'space', pairs + [(j, i) for i, j in pairs])  3.63 us
    ppermute x1, starting transfers between devices, doubling_sums(): return [pair, lax.ppermute(pair, 'vel', [(i, i ^ 2) for i in range(size)])]  3.03 us
    ppermute x1, starting transfers between devices, doubling_sums(): pair = tile + lax.ppermute(tile, 'vel', [(i, i ^ 1) for i in range(size)])  2.84 us
    pallas_call x1, Pallas kernels, first_sums(): pl.pallas_call(first_sums_kernel, in_specs=[spec(pltpu.SMEM), spec(pltpu....  2.5 us
  transfers between devices with their start and end apart: 12, of which 5 were waited for; matrix products, arithmetic and copies ran while one was open for 1% of the time, Pallas kernels for 42%

profile of v24, /device:TPU:4, one launch (start us, length us, event | category | flops | bytes accessed | tf_op | source)
XLA Modules:
  0.0 57.1 jit_solution(9475026753098305718)
XLA Ops:
  0.7 2.4 %first_rows.1 = (f32[4104,128]{1,0:T(8,128)S(1)}, f32[3,512,128]{2,1,0:T(8,128)}, f32[3,512,128]{2,1,0:T(8,128)}) custom-call(f32[4096,128]{1,0:T(8,128)} %bitcast.14), custom_call_target="tpu_custom_call" | custom-call | flops 16777216 | bytes 8388608 | tf_op jit(solution)/shard_map/first_rows/pallas_call | solution.py:390
  3.1 0.1 collective-permute-start
  3.2 3.4 %collective-permute-start.5 = (f32[3,512,128]{2,1,0:T(8,128)}, f32[3,512,128]{2,1,0:T(8,128)S(1)}, u32[]{:S(2)}, u32[]{:S(2)}) collective-permute-start(f32[3,512,128]{2,1,0:T(8,128)} %get-tuple-element.27), channel_id=1, source_target_pairs={{4,8},{12,16},{20,24},{8,4},{16,12},{24,20},{5,9},{13,17},{21,25},... | collective-permute-start | bytes 2359304 | tf_op jit(solution)/shard_map/ppermute | solution.py:880
  6.7 0.1 copy.14
  6.7 0.1 copy.15
  6.8 0.1 copy.17
  6.9 0.1 copy.16
  7.0 0.1 copy.20
  7.1 0.1 concatenate.3
  7.2 0.1 copy.18
  7.3 0.1 broadcast_in_dim.23.geo_ref.geo_in
  7.4 2.5 %first_sums.1 = (f32[8,512,128]{2,1,0:T(8,128)S(1)}, f32[8,128]{1,0:T(8,128)S(1)}) custom-call(s32[6,8]{1,0:T(8,128)S(1)} %get-tuple-element.46.links_ref, f32[33,8,128]{2,1,0:T(8,128)S(1)} %broadcast_in_dim.23.geo_ref.geo_in, f32[4104,128]{1,0:T(8,128)S(1)} %get-tuple-element.19.native_ref), custom_call_target="tpu_custom_call" | custom-call | flops 20971520 | bytes 10485760 | tf_op jit(solution)/shard_map/first_sums/pallas_call | solution.py:328
  9.9 3.7 %collective-permute-start.3 = (f32[8,128]{1,0:T(8,128)S(1)}, f32[8,128]{1,0:T(8,128)S(1)}, u32[]{:S(2)}, u32[]{:S(2)}) collective-permute-start(f32[8,128]{1,0:T(8,128)S(1)} %get-tuple-element.23.refs_0_), channel_id=1, source_target_pairs={{0,3},{1,2},{2,1},{3,0},{4,7},{5,6},{6,5},{7,4},{8,11},{9,10},{10,... | collective-permute-start | bytes 12296 | tf_op jit(solution)/shard_map/ppermute | solution.py:445
  13.5 0.0 collective-permute-start.2
  13.5 0.8 %collective-permute-start.1 = (f32[8,128]{1,0:T(8,128)S(1)}, f32[8,128]{1,0:T(8,128)S(1)}, u32[]{:S(2)}, u32[]{:S(2)}) collective-permute-start(f32[8,128]{1,0:T(8,128)S(1)} %get-tuple-element.23.refs_0_), channel_id=1, source_target_pairs={{0,1},{1,0},{2,3},{3,2},{4,5},{5,4},{6,7},{7,6},{8,9},{9,8},{10,11... | collective-permute-start | bytes 12296 | tf_op jit(solution)/shard_map/ppermute | solution.py:445
  14.3 4.1 %flux.2 = (f32[8,512,128]{2,1,0:T(8,128)S(1)}, f32[12,512,128]{2,1,0:T(8,128)S(1)}) custom-call(s32[6,8]{1,0:T(8,128)S(1)} %get-tuple-element.46.links_ref, f32[33,8,128]{2,1,0:T(8,128)S(1)} %broadcast_in_dim.23.geo_ref.geo_in, f32[8,512,128]{2,1,0:T(8,128)S(1)} %get-tuple-element.20.f_ref.refs_4_.old_ref), custom_call_target="tpu_custom_call" | custom-call | flops 37748736 | bytes 18874368 | tf_op jit(solution)/shard_map/flux/pallas_call | solution.py:559
  18.4 0.0 collective-permute-done.3.refs_3_
  18.5 0.0 collective-permute-done.2.refs_2_
  18.5 0.0 collective-permute-done.1.refs_1_
  18.5 3.7 %add_target.2 = (f32[8,512,128]{2,1,0:T(8,128)S(1)}, f32[8,128]{1,0:T(8,128)S(1)}) custom-call(s32[6,8]{1,0:T(8,128)S(1)} %get-tuple-element.46.links_ref, f32[33,8,128]{2,1,0:T(8,128)S(1)} %broadcast_in_dim.23.geo_ref.geo_in, f32[8,128]{1,0:T(8,128)S(1)} %get-tuple-element.23.refs_0_, ...), custom_call_target="tpu_custom_call", output_to_operand_aliasing={{0}: (7, {})} | custom-call | flops 29360128 | bytes 14680064 | tf_op jit(solution)/shard_map/add_target/pallas_call | solution.py:681
  22.2 0.0 collective-permute-done.halo_any
  22.2 1.6 %near_edge.1 = (f32[8,512,128]{2,1,0:T(8,128)S(1)}, f32[3,512,128]{2,1,0:T(8,128)S(1)}) custom-call(f32[12,512,128]{2,1,0:T(8,128)S(1)} %get-tuple-element.21.pairs_ref, f32[3,512,128]{2,1,0:T(8,128)} %collective-permute-done.halo_any, f32[8,512,128]{2,1,0:T(8,128)S(1)} %get-tuple-element.20.f_ref.refs_4_.old_ref, ...), custom_call_target="tpu_custom_call", output_to_operand_aliasing={{0}: (3, {})} | custom-call | flops 8388608 | bytes 4194304 | tf_op jit(solution)/shard_map/near_edge/pallas_call | solution.py:763
  23.8 0.1 collective-permute-start.4
  23.9 1.2 %collective-permute-done.5.halo_ref = f32[3,512,128]{2,1,0:T(8,128)S(1)} collective-permute-done((f32[3,512,128]{2,1,0:T(8,128)}, f32[3,512,128]{2,1,0:T(8,128)S(1)}, u32[]{:S(2)}, u32[]{:S(2)}) %collective-permute-start.5) | collective-permute-done | bytes 786464 | tf_op jit(solution)/shard_map/ppermute | solution.py:880
  25.1 0.6 %far_edge.1 = (f32[8,512,128]{2,1,0:T(8,128)S(1)}, f32[3,512,128]{2,1,0:T(8,128)S(1)}) custom-call(f32[12,512,128]{2,1,0:T(8,128)S(1)} %get-tuple-element.21.pairs_ref, f32[3,512,128]{2,1,0:T(8,128)S(1)} %collective-permute-done.5.halo_ref, f32[8,512,128]{2,1,0:T(8,128)S(1)} %get-tuple-element.20.f_ref.refs_4_.old_ref, ...), custom_call_target="tpu_custom_call", output_to_operand_aliasing={{0}: (3, {})} | custom-call | flops 8388608 | bytes 4194304 | tf_op jit(solution)/shard_map/far_edge/pallas_call | solution.py:763
  25.8 3.7 %collective-permute-start.9 = (f32[3,512,128]{2,1,0:T(8,128)S(1)}, f32[3,512,128]{2,1,0:T(8,128)S(1)}, u32[]{:S(2)}, u32[]{:S(2)}) collective-permute-start(f32[3,512,128]{2,1,0:T(8,128)S(1)} %get-tuple-element.32), channel_id=1, source_target_pairs={{4,8},{12,16},{20,24},{8,4},{16,12},{24,20},{5,9},{13,17},{21,25},... | collective-permute-start | bytes 2359304 | tf_op jit(solution)/shard_map/ppermute | solution.py:880
  29.5 1.6 %local_sums.1.refs_1_ = f32[8,128]{1,0:T(8,128)S(1)} custom-call(s32[6,8]{1,0:T(8,128)S(1)} %get-tuple-element.46.links_ref, f32[33,8,128]{2,1,0:T(8,128)S(1)} %broadcast_in_dim.23.geo_ref.geo_in, f32[8,512,128]{2,1,0:T(8,128)S(1)} %get-tuple-element.29.f_ref.refs_5_.old_ref), custom_call_target="tpu_custom_call" | custom-call | flops 16777216 | bytes 8388608 | tf_op jit(solution)/shard_map/local_sums/pallas_call | solution.py:310
  31.1 3.6 %collective-permute-start.8 = (f32[8,128]{1,0:T(8,128)S(1)}, f32[8,128]{1,0:T(8,128)S(1)}, u32[]{:S(2)}, u32[]{:S(2)}) collective-permute-start(f32[8,128]{1,0:T(8,128)S(1)} %local_sums.1.refs_1_), channel_id=1, source_target_pairs={{0,3},{1,2},{2,1},{3,0},{4,7},{5,6},{6,5},{7,4},{8,11},{9,10},{10,... | collective-permute-start | bytes 12296 | tf_op jit(solution)/shard_map/ppermute | solution.py:445
  34.8 0.0 collective-permute-start.7
  34.8 0.8 %collective-permute-start.6 = (f32[8,128]{1,0:T(8,128)S(1)}, f32[8,128]{1,0:T(8,128)S(1)}, u32[]{:S(2)}, u32[]{:S(2)}) collective-permute-start(f32[8,128]{1,0:T(8,128)S(1)} %local_sums.1.refs_1_), channel_id=1, source_target_pairs={{0,1},{1,0},{2,3},{3,2},{4,5},{5,4},{6,7},{7,6},{8,9},{9,8},{10,11... | collective-permute-start | bytes 12296 | tf_op jit(solution)/shard_map/ppermute | solution.py:445
  35.5 3.1 %flux.3.refs_6_ = f32[8,512,128]{2,1,0:T(8,128)S(1)} custom-call(s32[6,8]{1,0:T(8,128)S(1)} %get-tuple-element.46.links_ref, f32[33,8,128]{2,1,0:T(8,128)S(1)} %broadcast_in_dim.23.geo_ref.geo_in, f32[8,512,128]{2,1,0:T(8,128)S(1)} %get-tuple-element.29.f_ref.refs_5_.old_ref), custom_call_target="tpu_custom_call" | custom-call | flops 29360128 | bytes 14680064 | tf_op jit(solution)/shard_map/flux/pallas_call | solution.py:559
  38.7 0.0 collective-permute-done.8.refs_4_
  38.7 0.6 %collective-permute-done.7.refs_3_ = f32[8,128]{1,0:T(8,128)S(1)} collective-permute-done((f32[8,128]{1,0:T(8,128)S(1)}, f32[8,128]{1,0:T(8,128)S(1)}, u32[]{:S(2)}, u32[]{:S(2)}) %collective-permute-start.7) | collective-permute-done | bytes 4128 | tf_op jit(solution)/shard_map/ppermute | solution.py:445
  39.3 0.0 collective-permute-done.6.refs_2_
  39.3 3.7 %add_target.3.part_ref = f32[8,512,128]{2,1,0:T(8,128)S(1)} custom-call(s32[6,8]{1,0:T(8,128)S(1)} %get-tuple-element.46.links_ref, f32[33,8,128]{2,1,0:T(8,128)S(1)} %broadcast_in_dim.23.geo_ref.geo_in, f32[8,128]{1,0:T(8,128)S(1)} %get-tuple-element.30.refs_0_, f32[8,128]{1,0:T(8,128)S(1)} %local_sums.1.refs_1_, ...), custom_call_target="tpu_custom_call", output_to_operand_aliasing={{}: (8, {})} | custom-call | flops 29360128 | bytes 14680064 | tf_op jit(solution)/shard_map/add_target/pallas_call | solution.py:681
  43.0 0.0 collective-permute-done.4.halo_ref
  43.0 1.2 %last_near.1 = (f32[8,512,128]{2,1,0:T(8,128)S(1)}, f32[8,128]{1,0:T(8,128)S(1)}) custom-call(f32[33,8,128]{2,1,0:T(8,128)S(1)} %broadcast_in_dim.23.geo_ref.geo_in, f32[12,512,128]{2,1,0:T(8,128)S(1)} %get-tuple-element.21.pairs_ref, f32[3,512,128]{2,1,0:T(8,128)S(1)} %collective-permute-done.4.halo_ref, ...), custom_call_target="tpu_custom_call", output_to_operand_aliasing={{0}: (4, {})} | custom-call | flops 12582912 | bytes 6291456 | tf_op jit(solution)/shard_map/last_near/pallas_call | solution.py:785
  44.2 2.4 %collective-permute-done.9.halo_ref = f32[3,512,128]{2,1,0:T(8,128)S(1)} collective-permute-done((f32[3,512,128]{2,1,0:T(8,128)S(1)}, f32[3,512,128]{2,1,0:T(8,128)S(1)}, u32[]{:S(2)}, u32[]{:S(2)}) %collective-permute-start.9) | collective-permute-done | bytes 786464 | tf_op jit(solution)/shard_map/ppermute | solution.py:880
  46.6 0.5 last_far.1
  47.1 2.8 %collective-permute-start.10 = (f32[8,128]{1,0:T(8,128)S(1)}, f32[8,128]{1,0:T(8,128)S(1)}, u32[]{:S(2)}, u32[]{:S(2)}) collective-permute-start(f32[8,128]{1,0:T(8,128)S(1)} %get-tuple-element.35), channel_id=1, source_target_pairs={{0,1},{1,0},{2,3},{3,2},{4,5},{5,4},{6,7},{7,6},{8,9},{9,8},{10,11... | collective-permute-start | bytes 12296 | tf_op jit(solution)/shard_map/ppermute | solution.py:453
  49.9 1.6 %collective-permute-done.10 = f32[8,128]{1,0:T(8,128)S(1)} collective-permute-done((f32[8,128]{1,0:T(8,128)S(1)}, f32[8,128]{1,0:T(8,128)S(1)}, u32[]{:S(2)}, u32[]{:S(2)}) %collective-permute-start.10) | collective-permute-done | bytes 4128 | tf_op jit(solution)/shard_map/ppermute | solution.py:453
  51.5 3.0 %collective-permute-start.11 = (f32[8,128]{1,0:T(8,128)S(1)}, f32[8,128]{1,0:T(8,128)S(1)}, u32[]{:S(2)}, u32[]{:S(2)}) collective-permute-start(f32[8,128]{1,0:T(8,128)S(1)} %add.74), channel_id=1, source_target_pairs={{0,2},{1,3},{2,0},{3,1},{4,6},{5,7},{6,4},{7,5},{8,10},{9,11},{10,... | collective-permute-start | bytes 12296 | tf_op jit(solution)/shard_map/ppermute | solution.py:454
  54.6 1.4 %result.1 = f32[4096,128]{1,0:T(8,128)} custom-call(f32[8,512,128]{2,1,0:T(8,128)S(1)} %get-tuple-element.31.part_ref, f32[3,512,128]{2,1,0:T(8,128)S(1)} %get-tuple-element.34.terms_ref), custom_call_target="tpu_custom_call" | custom-call | flops 12582912 | bytes 6291456 | tf_op jit(solution)/shard_map/result/pallas_call | solution.py:866
  56.0 0.1 collective-permute-done.11
  56.2 0.1 add_multiply_fusion
  56.3 0.1 add_multiply_fusion.1
  56.3 0.1 stack.2
  56.4 0.7 %copy.19 = f32[8,8]{1,0:T(8,128)} copy(f32[8,8]{0,1:T(8,128)S(1)} %stack.2) | data formatting | bytes 512
  (14 shorter events, 0.0 us)
Async XLA Ops:
  0.6 6.0 %copy-start.2 = (f32[8]{0:T(128)S(1)}, f32[8]{0:T(128)}, u32[]{:S(2)}) copy-start(f32[8]{0:T(128)} %param.8) | copy-start | bytes 100
  0.6 6.1 %copy-start.3 = (f32[8]{0:T(128)S(1)}, f32[8]{0:T(128)}, u32[]{:S(2)}) copy-start(f32[8]{0:T(128)} %param.9) | copy-start | bytes 100
  0.7 6.2 %copy-start.1 = (s32[6,8]{1,0:T(8,128)S(1)}, s32[6,8]{1,0:T(8,128)}, u32[]{:S(2)}) copy-start(s32[6,8]{1,0:T(8,128)} %param.6) | copy-start | bytes 580
  0.7 6.3 %copy-start = (f32[3,6,8]{2,1,0:T(8,128)S(1)}, f32[3,6,8]{2,1,0:T(8,128)}, u32[]{:S(2)}) copy-start(f32[3,6,8]{2,1,0:T(8,128)} %param.7) | copy-start | bytes 1732
  3.1 19.1 %collective-permute-start = (f32[3,512,128]{2,1,0:T(8,128)}, f32[3,512,128]{2,1,0:T(8,128)}, u32[]{:S(2)}, u32[]{:S(2)}) collective-permute-start(f32[3,512,128]{2,1,0:T(8,128)} %get-tuple-element.22), channel_id=1, source_target_pairs={{0,4},{8,12},{16,20},{24,28},{4,0},{12,8},{20,16},{28,24},{1,5},{9... | collective-permute-start | bytes 2359304 | tf_op jit(solution)/shard_map/ppermute | solution.py:880
  3.2 21.9 %collective-permute-start.5 = (f32[3,512,128]{2,1,0:T(8,128)}, f32[3,512,128]{2,1,0:T(8,128)S(1)}, u32[]{:S(2)}, u32[]{:S(2)}) collective-permute-start(f32[3,512,128]{2,1,0:T(8,128)} %get-tuple-element.27), channel_id=1, source_target_pairs={{4,8},{12,16},{20,24},{8,4},{16,12},{24,20},{5,9},{13,17},{21,25},... | collective-permute-start | bytes 2359304 | tf_op jit(solution)/shard_map/ppermute | solution.py:880
  9.9 8.6 %collective-permute-start.3 = (f32[8,128]{1,0:T(8,128)S(1)}, f32[8,128]{1,0:T(8,128)S(1)}, u32[]{:S(2)}, u32[]{:S(2)}) collective-permute-start(f32[8,128]{1,0:T(8,128)S(1)} %get-tuple-element.23.refs_0_), channel_id=1, source_target_pairs={{0,3},{1,2},{2,1},{3,0},{4,7},{5,6},{6,5},{7,4},{8,11},{9,10},{10,... | collective-permute-start | bytes 12296 | tf_op jit(solution)/shard_map/ppermute | solution.py:445
  13.5 4.9 %collective-permute-start.2 = (f32[8,128]{1,0:T(8,128)S(1)}, f32[8,128]{1,0:T(8,128)S(1)}, u32[]{:S(2)}, u32[]{:S(2)}) collective-permute-start(f32[8,128]{1,0:T(8,128)S(1)} %get-tuple-element.23.refs_0_), channel_id=1, source_target_pairs={{0,2},{1,3},{2,0},{3,1},{4,6},{5,7},{6,4},{7,5},{8,10},{9,11},{10,... | collective-permute-start | bytes 12296 | tf_op jit(solution)/shard_map/ppermute | solution.py:445
  13.5 5.0 %collective-permute-start.1 = (f32[8,128]{1,0:T(8,128)S(1)}, f32[8,128]{1,0:T(8,128)S(1)}, u32[]{:S(2)}, u32[]{:S(2)}) collective-permute-start(f32[8,128]{1,0:T(8,128)S(1)} %get-tuple-element.23.refs_0_), channel_id=1, source_target_pairs={{0,1},{1,0},{2,3},{3,2},{4,5},{5,4},{6,7},{7,6},{8,9},{9,8},{10,11... | collective-permute-start | bytes 12296 | tf_op jit(solution)/shard_map/ppermute | solution.py:445
  23.8 19.2 %collective-permute-start.4 = (f32[3,512,128]{2,1,0:T(8,128)S(1)}, f32[3,512,128]{2,1,0:T(8,128)S(1)}, u32[]{:S(2)}, u32[]{:S(2)}) collective-permute-start(f32[3,512,128]{2,1,0:T(8,128)S(1)} %get-tuple-element.26), channel_id=1, source_target_pairs={{0,4},{8,12},{16,20},{24,28},{4,0},{12,8},{20,16},{28,24},{1,5},{9... | collective-permute-start | bytes 2359304 | tf_op jit(solution)/shard_map/ppermute | solution.py:880
  25.8 20.8 %collective-permute-start.9 = (f32[3,512,128]{2,1,0:T(8,128)S(1)}, f32[3,512,128]{2,1,0:T(8,128)S(1)}, u32[]{:S(2)}, u32[]{:S(2)}) collective-permute-start(f32[3,512,128]{2,1,0:T(8,128)S(1)} %get-tuple-element.32), channel_id=1, source_target_pairs={{4,8},{12,16},{20,24},{8,4},{16,12},{24,20},{5,9},{13,17},{21,25},... | collective-permute-start | bytes 2359304 | tf_op jit(solution)/shard_map/ppermute | solution.py:880
  31.1 7.5 %collective-permute-start.8 = (f32[8,128]{1,0:T(8,128)S(1)}, f32[8,128]{1,0:T(8,128)S(1)}, u32[]{:S(2)}, u32[]{:S(2)}) collective-permute-start(f32[8,128]{1,0:T(8,128)S(1)} %local_sums.1.refs_1_), channel_id=1, source_target_pairs={{0,3},{1,2},{2,1},{3,0},{4,7},{5,6},{6,5},{7,4},{8,11},{9,10},{10,... | collective-permute-start | bytes 12296 | tf_op jit(solution)/shard_map/ppermute | solution.py:445
  34.8 4.5 %collective-permute-start.7 = (f32[8,128]{1,0:T(8,128)S(1)}, f32[8,128]{1,0:T(8,128)S(1)}, u32[]{:S(2)}, u32[]{:S(2)}) collective-permute-start(f32[8,128]{1,0:T(8,128)S(1)} %local_sums.1.refs_1_), channel_id=1, source_target_pairs={{0,2},{1,3},{2,0},{3,1},{4,6},{5,7},{6,4},{7,5},{8,10},{9,11},{10,... | collective-permute-start | bytes 12296 | tf_op jit(solution)/shard_map/ppermute | solution.py:445
  34.8 4.5 %collective-permute-start.6 = (f32[8,128]{1,0:T(8,128)S(1)}, f32[8,128]{1,0:T(8,128)S(1)}, u32[]{:S(2)}, u32[]{:S(2)}) collective-permute-start(f32[8,128]{1,0:T(8,128)S(1)} %local_sums.1.refs_1_), channel_id=1, source_target_pairs={{0,1},{1,0},{2,3},{3,2},{4,5},{5,4},{6,7},{7,6},{8,9},{9,8},{10,11... | collective-permute-start | bytes 12296 | tf_op jit(solution)/shard_map/ppermute | solution.py:445
  47.1 4.4 %collective-permute-start.10 = (f32[8,128]{1,0:T(8,128)S(1)}, f32[8,128]{1,0:T(8,128)S(1)}, u32[]{:S(2)}, u32[]{:S(2)}) collective-permute-start(f32[8,128]{1,0:T(8,128)S(1)} %get-tuple-element.35), channel_id=1, source_target_pairs={{0,1},{1,0},{2,3},{3,2},{4,5},{5,4},{6,7},{7,6},{8,9},{9,8},{10,11... | collective-permute-start | bytes 12296 | tf_op jit(solution)/shard_map/ppermute | solution.py:453
  51.5 4.6 %collective-permute-start.11 = (f32[8,128]{1,0:T(8,128)S(1)}, f32[8,128]{1,0:T(8,128)S(1)}, u32[]{:S(2)}, u32[]{:S(2)}) collective-permute-start(f32[8,128]{1,0:T(8,128)S(1)} %add.74), channel_id=1, source_target_pairs={{0,2},{1,3},{2,0},{3,1},{4,6},{5,7},{6,4},{7,5},{8,10},{9,11},{10,... | collective-permute-start | bytes 12296 | tf_op jit(solution)/shard_map/ppermute | solution.py:454
